TPU v7x, 32 devices: a whole 2x2x4 slice. The times are simulated.
32 devices in a mesh: dp: 16 (over z, x, core), seq: 2 (over y).
Axes of the slice: x: 2, y: 2, z: 4, core: 2. Of those that a mesh axis runs over, the one named last changes fastest.
Arguments:
- targets: bfloat16 [4, 16, 1024, 768], P(None, 'dp', 'seq'), may hold values from -6 to 6
- memory: bfloat16 [4, 16, 1024, 768], P(None, 'dp', 'seq'), may hold values from -6 to 6
- row_kind: int32 [4, 16], P(None, 'dp'), may hold values from 0 to 1
- loss_mask: int32 [4, 16, 1024], P(None, 'dp', 'seq'), may hold values 0 or 1
- cotangent: bfloat16 [4, 16, 1024, 768], P(None, 'dp', 'seq'), may hold values from -6 to 6
- norm_self_gain: float32 [768], replicated, may hold values from 0.5 to 1.5
- norm_self_bias: float32 [768], replicated, may hold values from -1.75 to 1.75
- self_input: bfloat16 [768, 2304], replicated, may hold values from -0.21875 to 0.21875
- self_query_bias: float32 [768], replicated, may hold values from -3 to 3
- self_value_bias: float32 [768], replicated, may hold values from -0.1875 to 0.1875
- self_output: bfloat16 [768, 768], replicated, may hold values from -3.5 to 3.5
- self_output_bias: float32 [768], replicated, may hold values from -1.75 to 1.75
- norm_cross_gain: float32 [768], replicated, may hold values from 0.5 to 1.5
- norm_cross_bias: float32 [768], replicated, may hold values from -1.75 to 1.75
- cross_query: bfloat16 [768, 768], replicated, may hold values from -0.21875 to 0.21875
- cross_query_bias: float32 [768], replicated, may hold values from -3 to 3
- cross_input: bfloat16 [768, 1536], replicated, may hold values from -0.21875 to 0.21875
- cross_value_bias: float32 [768], replicated, may hold values from -0.1875 to 0.1875
- cross_output: bfloat16 [768, 768], replicated, may hold values from -3.5 to 3.5
- cross_output_bias: float32 [768], replicated, may hold values from -1.75 to 1.75
- norm_feed_gain: float32 [768], replicated, may hold values from 0.5 to 1.5
- norm_feed_bias: float32 [768], replicated, may hold values from -1.75 to 1.75
- feed_in: bfloat16 [768, 3072], replicated, may hold values from -0.21875 to 0.21875
- feed_in_bias: float32 [3072], replicated, may hold values from -3 to 3
- feed_out: bfloat16 [3072, 768], replicated, may hold values from -0.109375 to 0.109375
- feed_out_bias: float32 [768], replicated, may hold values from -1.75 to 1.75
Outputs:
- layer_output: bfloat16 [4, 16, 1024, 768], P(None, 'dp', 'seq')
- targets_gradient: float32 [4, 16, 1024, 768], P(None, 'dp', 'seq')
- memory_gradient: float32 [4, 16, 1024, 768], P(None, 'dp', 'seq')
- norm_self_gain_gradient: float32 [768], P('dp')
- norm_self_bias_gradient: float32 [768], P('dp')
- self_input_gradient: float32 [768, 2304], P('dp')
- self_query_bias_gradient: float32 [768], P('dp')
- self_value_bias_gradient: float32 [768], P('dp')
- self_output_gradient: float32 [768, 768], P('dp')
- self_output_bias_gradient: float32 [768], P('dp')
- norm_cross_gain_gradient: float32 [768], P('dp')
- norm_cross_bias_gradient: float32 [768], P('dp')
- cross_query_gradient: float32 [768, 768], P('dp')
- cross_query_bias_gradient: float32 [768], P('dp')
- cross_input_gradient: float32 [768, 1536], P('dp')
- cross_value_bias_gradient: float32 [768], P('dp')
- cross_output_gradient: float32 [768, 768], P('dp')
- cross_output_bias_gradient: float32 [768], P('dp')
- norm_feed_gain_gradient: float32 [768], P('dp')
- norm_feed_bias_gradient: float32 [768], P('dp')
- feed_in_gradient: float32 [768, 3072], P('dp')
- feed_in_bias_gradient: float32 [3072], P('dp')
- feed_out_gradient: float32 [3072, 768], P('dp')
- feed_out_bias_gradient: float32 [768], P('dp')
Inputs may be any that keep to these rules, and one draw needn't show every extreme that they name: `row_kind`: 0 marks a gap-sentence row, whose self-attention is causal; 1 a masked-token row, which attends to all its positions.
All inputs are finite; a program needn't handle non-finite values. No bound on the sum of `loss_mask` on one device may be relied on, other than what follows from the above.
Results may differ from a plain program's by a relative error of at most 0.038.
Values may be sent and summed in bfloat16 or wider, within the bound.
A program may use at most 576 MiB of HBM per device.

v0:
```python
import jax
import jax.numpy as jnp
from jax import lax
from jax.sharding import PartitionSpec as P

HEADS = 12
HEAD = 64


epsilon = 1e-05
blocked_score = -1e30


def normed(values, norm_gain, norm_shift):
    center = values - jnp.mean(values, axis=-1, keepdims=True)
    spread = jnp.mean(center * center, axis=-1, keepdims=True)
    return center * lax.rsqrt(spread + epsilon) * norm_gain + norm_shift


def normed_back(values, norm_gain, norm_shift, upstream):
    unused, pullback = jax.vjp(normed, values, norm_gain, norm_shift)
    return pullback(upstream)


def gelu_exact(values):
    return jax.nn.gelu(values, approximate=False)


def project_rows(row_block, weight):
    return jnp.einsum("bpd,de->bpe", row_block, weight, preferred_element_type=jnp.float32)


def project_back(row_block, weight):
    return jnp.einsum("bpe,de->bpd", row_block, weight, preferred_element_type=jnp.float32)


def outer_sum(first_rows, second_rows):
    return jnp.einsum("bpd,bpe->de", first_rows, second_rows, preferred_element_type=jnp.float32)


def split_heads(row_block):
    return row_block.reshape(row_block.shape[0], row_block.shape[1], HEADS, HEAD)


def masked_scores(queries, key_rows, allowed):
    scores = jnp.einsum(
        "bphe,bshe->bhps",
        split_heads(queries),
        split_heads(key_rows),
        preferred_element_type=jnp.float32,
    )
    if allowed is None:
        return scores
    return jnp.where(allowed[:, None], scores, blocked_score)


def attend_forward(queries, key_rows, values, allowed):
    scores = masked_scores(queries, key_rows, allowed)
    highest_score = jnp.max(scores, axis=-1, keepdims=True)
    raised = jnp.exp(scores - highest_score)
    totals = jnp.sum(raised, axis=-1, keepdims=True)
    weights = (raised / totals).astype(jnp.bfloat16)
    mixed = jnp.einsum(
        "bhps,bshe->bphe", weights, split_heads(values), preferred_element_type=jnp.float32
    )
    return (mixed.reshape(queries.shape).astype(jnp.bfloat16), highest_score + jnp.log(totals))


def attend_backward(queries, key_rows, values, allowed, log_totals, upstream):
    weights = jnp.exp(masked_scores(queries, key_rows, allowed) - log_totals)
    upstream_heads = split_heads(upstream)
    value_grads = jnp.einsum(
        "bhps,bphe->bshe",
        weights.astype(jnp.bfloat16),
        upstream_heads,
        preferred_element_type=jnp.float32,
    )
    weight_grads = jnp.einsum(
        "bphe,bshe->bhps", upstream_heads, split_heads(values), preferred_element_type=jnp.float32
    )
    score_grads = weights * (weight_grads - jnp.sum(weight_grads * weights, axis=-1, keepdims=True))
    score_low = score_grads.astype(jnp.bfloat16)
    query_grads = jnp.einsum(
        "bhps,bshe->bphe", score_low, split_heads(key_rows), preferred_element_type=jnp.float32
    ).reshape(queries.shape)
    key_grads = jnp.einsum(
        "bhps,bphe->bshe", score_low, split_heads(queries), preferred_element_type=jnp.float32
    ).reshape(key_rows.shape)
    return (query_grads, jnp.concatenate([key_grads, value_grads.reshape(key_rows.shape)], axis=-1))


def on_device(
    targets,
    memory,
    row_kind,
    loss_mask,
    cotangent,
    norm_self_gain,
    norm_self_bias,
    self_input,
    self_query_bias,
    self_value_bias,
    self_output,
    self_output_bias,
    norm_cross_gain,
    norm_cross_bias,
    cross_query,
    cross_query_bias,
    cross_input,
    cross_value_bias,
    cross_output,
    cross_output_bias,
    norm_feed_gain,
    norm_feed_bias,
    feed_in,
    feed_in_bias,
    feed_out,
    feed_out_bias,
):
    model_width = targets.shape[3]
    part_rows = targets.shape[2]
    key_span = part_rows * lax.axis_size("seq")
    query_scale = HEAD ** (-0.5)
    places = lax.axis_index("seq") * part_rows + jnp.arange(part_rows)
    causal = jnp.arange(key_span)[None, :] <= places[:, None]
    results, input_grads, source_grads = ([], [], [])
    totals = None
    for micro_index in range(targets.shape[0]):
        inputs = targets[micro_index].astype(jnp.float32)
        memory_local = memory[micro_index]
        allowed = causal[None] | (row_kind[micro_index] == 1)[:, None, None]
        first_normed = normed(inputs, norm_self_gain, norm_self_bias).astype(jnp.bfloat16)
        self_joint = project_rows(first_normed, self_input)
        queries = ((self_joint[..., :model_width] + self_query_bias) * query_scale).astype(
            jnp.bfloat16
        )
        own_pairs = jnp.concatenate(
            [
                self_joint[..., model_width : 2 * model_width],
                self_joint[..., 2 * model_width :] + self_value_bias,
            ],
            axis=-1,
        ).astype(jnp.bfloat16)
        gathered_self = lax.all_gather(own_pairs, "seq", axis=1, tiled=True)
        key_rows = gathered_self[..., :model_width]
        value_rows = gathered_self[..., model_width:]
        self_mixed, self_totals = attend_forward(queries, key_rows, value_rows, allowed)
        after_self = inputs + project_rows(self_mixed, self_output) + self_output_bias
        second_normed = normed(after_self, norm_cross_gain, norm_cross_bias).astype(jnp.bfloat16)
        cross_queries = (
            (project_rows(second_normed, cross_query) + cross_query_bias) * query_scale
        ).astype(jnp.bfloat16)
        joined = project_rows(lax.all_gather(memory_local, "seq", axis=1, tiled=True), cross_input)
        gathered_cross = jnp.concatenate(
            [joined[..., :model_width], joined[..., model_width:] + cross_value_bias], axis=-1
        ).astype(jnp.bfloat16)
        cross_keys = gathered_cross[..., :model_width]
        cross_values = gathered_cross[..., model_width:]
        cross_mixed, cross_totals = attend_forward(cross_queries, cross_keys, cross_values, None)
        after_cross = after_self + project_rows(cross_mixed, cross_output) + cross_output_bias
        third_normed = normed(after_cross, norm_feed_gain, norm_feed_bias).astype(jnp.bfloat16)
        activated, gelu_pullback = jax.vjp(
            gelu_exact, project_rows(third_normed, feed_in) + feed_in_bias
        )
        activated_low = activated.astype(jnp.bfloat16)
        results.append(
            (after_cross + project_rows(activated_low, feed_out) + feed_out_bias).astype(
                jnp.bfloat16
            )
        )
        pieces = [None] * 21
        grad_output = (
            cotangent[micro_index].astype(jnp.float32)
            * loss_mask[micro_index].astype(jnp.float32)[..., None]
        )
        output_low = grad_output.astype(jnp.bfloat16)
        pieces[19] = outer_sum(activated_low, output_low)
        pieces[20] = jnp.sum(grad_output, axis=(0, 1))
        grad_hidden = gelu_pullback(project_back(output_low, feed_out))[0]
        hidden_low = grad_hidden.astype(jnp.bfloat16)
        pieces[17] = outer_sum(third_normed, hidden_low)
        pieces[18] = jnp.sum(grad_hidden, axis=(0, 1))
        through_feed, pieces[15], pieces[16] = normed_back(
            after_cross, norm_feed_gain, norm_feed_bias, project_back(hidden_low, feed_in)
        )
        grad_cross = grad_output + through_feed
        cross_low = grad_cross.astype(jnp.bfloat16)
        pieces[13] = outer_sum(cross_mixed, cross_low)
        pieces[14] = jnp.sum(grad_cross, axis=(0, 1))
        cross_upstream = project_back(cross_low, cross_output).astype(jnp.bfloat16)
        cross_query_grads, cross_pair_grads = attend_backward(
            cross_queries, cross_keys, cross_values, None, cross_totals, cross_upstream
        )
        own_cross = lax.psum_scatter(
            cross_pair_grads.astype(jnp.bfloat16), "seq", scatter_dimension=1, tiled=True
        ).astype(jnp.float32)
        pieces[12] = jnp.sum(own_cross[..., model_width:], axis=(0, 1))
        own_cross_low = own_cross.astype(jnp.bfloat16)
        pieces[11] = outer_sum(memory_local, own_cross_low)
        source_grads.append(project_back(own_cross_low, cross_input))
        scaled_cross = cross_query_grads * query_scale
        pieces[10] = jnp.sum(scaled_cross, axis=(0, 1))
        scaled_cross_low = scaled_cross.astype(jnp.bfloat16)
        pieces[9] = outer_sum(second_normed, scaled_cross_low)
        through_cross, pieces[7], pieces[8] = normed_back(
            after_self,
            norm_cross_gain,
            norm_cross_bias,
            project_back(scaled_cross_low, cross_query),
        )
        grad_self = grad_cross + through_cross
        self_low = grad_self.astype(jnp.bfloat16)
        pieces[5] = outer_sum(self_mixed, self_low)
        pieces[6] = jnp.sum(grad_self, axis=(0, 1))
        self_upstream = project_back(self_low, self_output).astype(jnp.bfloat16)
        self_query_grads, self_pair_grads = attend_backward(
            queries, key_rows, value_rows, allowed, self_totals, self_upstream
        )
        own_self = lax.psum_scatter(
            self_pair_grads.astype(jnp.bfloat16), "seq", scatter_dimension=1, tiled=True
        ).astype(jnp.float32)
        scaled_self = self_query_grads * query_scale
        pieces[3] = jnp.sum(scaled_self, axis=(0, 1))
        pieces[4] = jnp.sum(own_self[..., model_width:], axis=(0, 1))
        joint_low = jnp.concatenate([scaled_self, own_self], axis=-1).astype(jnp.bfloat16)
        pieces[2] = outer_sum(first_normed, joint_low)
        through_first, pieces[0], pieces[1] = normed_back(
            inputs, norm_self_gain, norm_self_bias, project_back(joint_low, self_input)
        )
        input_grads.append(grad_self + through_first)
        totals = (
            pieces
            if totals is None
            else [running + added for running, added in zip(totals, pieces)]
        )
    block_sums = (
        lax.psum_scatter(
            totals[0].astype(jnp.bfloat16), "dp", scatter_dimension=0, tiled=True
        ).astype(jnp.float32),
        lax.psum_scatter(
            totals[1].astype(jnp.bfloat16), "dp", scatter_dimension=0, tiled=True
        ).astype(jnp.float32),
        lax.psum_scatter(
            totals[2].astype(jnp.bfloat16), "dp", scatter_dimension=0, tiled=True
        ).astype(jnp.float32),
        lax.psum_scatter(
            totals[3].astype(jnp.bfloat16), "dp", scatter_dimension=0, tiled=True
        ).astype(jnp.float32),
        lax.psum_scatter(
            totals[4].astype(jnp.bfloat16), "dp", scatter_dimension=0, tiled=True
        ).astype(jnp.float32),
        lax.psum_scatter(
            totals[5].astype(jnp.bfloat16), "dp", scatter_dimension=0, tiled=True
        ).astype(jnp.float32),
        lax.psum_scatter(
            totals[6].astype(jnp.bfloat16), "dp", scatter_dimension=0, tiled=True
        ).astype(jnp.float32),
        lax.psum_scatter(
            totals[7].astype(jnp.bfloat16), "dp", scatter_dimension=0, tiled=True
        ).astype(jnp.float32),
        lax.psum_scatter(
            totals[8].astype(jnp.bfloat16), "dp", scatter_dimension=0, tiled=True
        ).astype(jnp.float32),
        lax.psum_scatter(
            totals[9].astype(jnp.bfloat16), "dp", scatter_dimension=0, tiled=True
        ).astype(jnp.float32),
        lax.psum_scatter(
            totals[10].astype(jnp.bfloat16), "dp", scatter_dimension=0, tiled=True
        ).astype(jnp.float32),
        lax.psum_scatter(
            totals[11].astype(jnp.bfloat16), "dp", scatter_dimension=0, tiled=True
        ).astype(jnp.float32),
        lax.psum_scatter(
            totals[12].astype(jnp.bfloat16), "dp", scatter_dimension=0, tiled=True
        ).astype(jnp.float32),
        lax.psum_scatter(
            totals[13].astype(jnp.bfloat16), "dp", scatter_dimension=0, tiled=True
        ).astype(jnp.float32),
        lax.psum_scatter(
            totals[14].astype(jnp.bfloat16), "dp", scatter_dimension=0, tiled=True
        ).astype(jnp.float32),
        lax.psum_scatter(
            totals[15].astype(jnp.bfloat16), "dp", scatter_dimension=0, tiled=True
        ).astype(jnp.float32),
        lax.psum_scatter(
            totals[16].astype(jnp.bfloat16), "dp", scatter_dimension=0, tiled=True
        ).astype(jnp.float32),
        lax.psum_scatter(
            totals[17].astype(jnp.bfloat16), "dp", scatter_dimension=0, tiled=True
        ).astype(jnp.float32),
        lax.psum_scatter(
            totals[18].astype(jnp.bfloat16), "dp", scatter_dimension=0, tiled=True
        ).astype(jnp.float32),
        lax.psum_scatter(
            totals[19].astype(jnp.bfloat16), "dp", scatter_dimension=0, tiled=True
        ).astype(jnp.float32),
        lax.psum_scatter(
            totals[20].astype(jnp.bfloat16), "dp", scatter_dimension=0, tiled=True
        ).astype(jnp.float32),
    )
    final = (
        lax.psum(block_sums[0].astype(jnp.bfloat16), "seq").astype(jnp.float32),
        lax.psum(block_sums[1].astype(jnp.bfloat16), "seq").astype(jnp.float32),
        lax.psum(block_sums[2].astype(jnp.bfloat16), "seq").astype(jnp.float32),
        lax.psum(block_sums[3].astype(jnp.bfloat16), "seq").astype(jnp.float32),
        lax.psum(block_sums[4].astype(jnp.bfloat16), "seq").astype(jnp.float32),
        lax.psum(block_sums[5].astype(jnp.bfloat16), "seq").astype(jnp.float32),
        lax.psum(block_sums[6].astype(jnp.bfloat16), "seq").astype(jnp.float32),
        lax.psum(block_sums[7].astype(jnp.bfloat16), "seq").astype(jnp.float32),
        lax.psum(block_sums[8].astype(jnp.bfloat16), "seq").astype(jnp.float32),
        lax.psum(block_sums[9].astype(jnp.bfloat16), "seq").astype(jnp.float32),
        lax.psum(block_sums[10].astype(jnp.bfloat16), "seq").astype(jnp.float32),
        lax.psum(block_sums[11].astype(jnp.bfloat16), "seq").astype(jnp.float32),
        lax.psum(block_sums[12].astype(jnp.bfloat16), "seq").astype(jnp.float32),
        lax.psum(block_sums[13].astype(jnp.bfloat16), "seq").astype(jnp.float32),
        lax.psum(block_sums[14].astype(jnp.bfloat16), "seq").astype(jnp.float32),
        lax.psum(block_sums[15].astype(jnp.bfloat16), "seq").astype(jnp.float32),
        lax.psum(block_sums[16].astype(jnp.bfloat16), "seq").astype(jnp.float32),
        lax.psum(block_sums[17].astype(jnp.bfloat16), "seq").astype(jnp.float32),
        lax.psum(block_sums[18].astype(jnp.bfloat16), "seq").astype(jnp.float32),
        lax.psum(block_sums[19].astype(jnp.bfloat16), "seq").astype(jnp.float32),
        lax.psum(block_sums[20].astype(jnp.bfloat16), "seq").astype(jnp.float32),
    )
    return (jnp.stack(results), jnp.stack(input_grads), jnp.stack(source_grads)) + tuple(final)


def solution(mesh):
    in_specs = (
        P(None, "dp", "seq", None),
        P(None, "dp", "seq", None),
        P(None, "dp"),
        P(None, "dp", "seq"),
        P(None, "dp", "seq", None),
        P(),
        P(),
        P(),
        P(),
        P(),
        P(),
        P(),
        P(),
        P(),
        P(),
        P(),
        P(),
        P(),
        P(),
        P(),
        P(),
        P(),
        P(),
        P(),
        P(),
        P(),
    )
    out_specs = (
        P(None, "dp", "seq", None),
        P(None, "dp", "seq", None),
        P(None, "dp", "seq", None),
        P("dp"),
        P("dp"),
        P("dp", None),
        P("dp"),
        P("dp"),
        P("dp", None),
        P("dp"),
        P("dp"),
        P("dp"),
        P("dp", None),
        P("dp"),
        P("dp", None),
        P("dp"),
        P("dp", None),
        P("dp"),
        P("dp"),
        P("dp"),
        P("dp", None),
        P("dp"),
        P("dp", None),
        P("dp"),
    )
    return jax.shard_map(
        on_device, mesh=mesh, in_specs=in_specs, out_specs=out_specs, check_vma=False
    )
```

profile of v0, /device:TPU:0, one launch (start us, length us, event | category | flops | bytes accessed | tf_op | source)
XLA Modules:
  0.0 2053.8 jit_solution(7402360659595983173)
XLA Ops:
  110.1 17.2 all-gather.21.cloned.1.call-done
  157.4 16.8 all-gather.19.cloned.1.call-done
  180.6 40.0 %all-gather.13.cloned.1.call-done = bf16[1,1024,1536]{2,1,0:T(8,128)(2,1)} async-done(((bf16[1,512,1536]{2,1,0:T(8,128)(2,1)}), bf16[1,1024,1536]{2,1,0:T(8,128)(2,1)}) %all-gather.13.cloned.1.call-update) | async-done | bytes 3145744 | tf_op jit(solution)/shard_map/all_gather | solution.py:144
  227.0 40.2 %all-gather.15.cloned.1.call-done = bf16[1,1024,1536]{2,1,0:T(8,128)(2,1)} async-done(((bf16[1,512,1536]{2,1,0:T(8,128)(2,1)}), bf16[1,1024,1536]{2,1,0:T(8,128)(2,1)}) %all-gather.15.cloned.1.call-update) | async-done | bytes 3145744 | tf_op jit(solution)/shard_map/all_gather | solution.py:144
  273.4 40.2 %all-gather.17.cloned.1.call-done = bf16[1,1024,1536]{2,1,0:T(8,128)(2,1)} async-done(((bf16[1,512,1536]{2,1,0:T(8,128)(2,1)}), bf16[1,1024,1536]{2,1,0:T(8,128)(2,1)}) %all-gather.17.cloned.1.call-update) | async-done | bytes 3145744 | tf_op jit(solution)/shard_map/all_gather | solution.py:144
  330.7 13.8 select_reduce_fusion.1
  344.5 11.6 fusion.4
  356.2 11.8 fusion.259
  376.3 13.4 fusion.415
  389.8 11.0 fusion.5
  401.4 10.9 fusion.263
  415.4 10.4 select_reduce_fusion.2
  425.8 11.8 fusion.2
  437.7 11.6 fusion.260
  457.6 13.4 fusion.418
  471.1 11.0 fusion.3
  482.7 11.3 fusion.264
  511.3 10.4 select_reduce_fusion.3
  521.8 11.6 fusion
  533.4 11.8 fusion.261
  553.6 13.4 fusion.409
  567.0 11.0 fusion.1
  578.1 10.9 fusion.265
  592.0 10.4 select_reduce_fusion
  602.5 11.8 fusion.6
  614.3 11.6 fusion.258
  634.3 13.4 fusion.412
  647.8 11.0 fusion.7
  659.4 11.3 fusion.262
  677.9 65.2 %multiply_convert_fusion.11 = (bf16[512,3072]{1,0:T(8,128)(2,1)}, f32[512,3072]{1,0:T(8,128)}, bf16[512,3072]{1,0:T(8,128)(2,1)}, f32[512,3072]{1,0:T(8,128)}, b...) fusion(f32[3072]{0:T(1024)S(1)} %copy-done.342, ...), kind=kOutput, calls=%fused_computation.148 | convolution fusion | flops 2833121280 | bytes 69228544 | tf_op jit(solution)/shard_map/bpd,de->bpe/dot_general | solution.py:30
  743.1 10.4 fusion.421
  758.2 10.5 fusion.423
  789.8 10.4 fusion.422
  818.4 11.8 fusion.123
  830.2 17.1 multiply_reduce_fusion.3
  847.3 16.9 multiply_convert_fusion.3
  901.1 17.1 multiply_reduce_fusion.1
  918.2 21.8 %multiply_convert_fusion.1 = bf16[12,512,1024]{2,1,0:T(8,128)(2,1)} fusion(f32[12,512,1024]{2,1,0:T(8,128)} %get-tuple-element.357, f32[12,512,1024]{2,1,0:T(8,128)} %get-tuple-element.331, f32[12,512]{1,0:T(8,128)} %get-tuple-element.356, f32[12,512]{1,0:T(8,128)} %log_add_fusion.1), kind=kLoop, calls=%fused_computation.3 | loop fusion | flops 25165824 | bytes 62963712 | tf_op jit(solution)/shard_map/convert_element_type | solution.py:82
  955.1 20.3 multiply_reduce_fusion.5
  980.9 21.9 %multiply_convert_fusion.5 = bf16[12,512,1024]{2,1,0:T(8,128)(2,1)} fusion(f32[12,512,1024]{2,1,0:T(8,128)} %get-tuple-element.364, f32[12,512,1024]{2,1,0:T(8,128)} %get-tuple-element.347, f32[12,512]{1,0:T(8,128)S(1)} %copy-done.167, f32[12,512]{1,0:T(8,128)S(1)} %copy-done.153), kind=kLoop, calls=%fused_computation.15 | loop fusion | flops 25165824 | bytes 62963712 | tf_op jit(solution)/shard_map/convert_element_type | solution.py:82
  1021.8 10.6 fusion.120
  1034.5 19.8 multiply_reduce_fusion.7
  1054.3 21.8 %multiply_convert_fusion.7 = bf16[12,512,1024]{2,1,0:T(8,128)(2,1)} fusion(f32[12,512,1024]{2,1,0:T(8,128)} %get-tuple-element.354, f32[12,512,1024]{2,1,0:T(8,128)} %get-tuple-element.323, f32[12,512]{1,0:T(8,128)} %get-tuple-element.353, f32[12,512]{1,0:T(8,128)} %log_add_fusion.7), kind=kLoop, calls=%fused_computation.21 | loop fusion | flops 25165824 | bytes 62963712 | tf_op jit(solution)/shard_map/convert_element_type | solution.py:82
  1076.2 10.7 bitcast_convert_fusion.3
  1100.8 10.8 fusion.117
  1162.9 10.5 fusion.126
  1175.4 19.4 multiply_reduce_fusion.2
  1194.9 17.5 multiply_convert_fusion.2
  1219.3 11.2 fusion.135
  1232.5 19.2 multiply_reduce_fusion
  1251.7 17.5 multiply_convert_fusion
  1276.1 11.2 fusion.138
  1289.4 19.2 multiply_reduce_fusion.4
  1308.6 17.5 multiply_convert_fusion.4
  1333.1 11.2 fusion.132
  1346.4 19.5 multiply_reduce_fusion.6
  1365.9 17.5 multiply_convert_fusion.6
  1390.3 11.2 fusion.129
  1528.2 16.7 add_convert_fusion.1
  1595.3 15.5 add_convert_fusion
  1712.6 63.5 %reduce-scatter.42.cloned.1.call-done = bf16[48,3072]{1,0:T(8,128)(2,1)} async-done(((bf16[768,3072]{1,0:T(8,128)(2,1)}), bf16[48,3072]{1,0:T(8,128)(2,1)}) %reduce-scatter.42.cloned.1.call-update) | async-done | bytes 294928 | tf_op jit(solution)/shard_map/reduce_scatter | solution.py:288
  1776.1 78.5 %reduce-scatter.44.cloned.1.call-done = bf16[192,768]{1,0:T(8,128)(2,1)} async-done(((bf16[3072,768]{1,0:T(8,128)(2,1)}), bf16[192,768]{1,0:T(8,128)(2,1)}) %reduce-scatter.44.cloned.1.call-update) | async-done | bytes 294928 | tf_op jit(solution)/shard_map/reduce_scatter | solution.py:294
  1854.6 71.5 %reduce-scatter.34.cloned.1.call-done = bf16[48,2304]{1,0:T(8,128)(2,1)} async-done(((bf16[768,2304]{1,0:T(8,128)(2,1)}), bf16[48,2304]{1,0:T(8,128)(2,1)}) %reduce-scatter.34.cloned.1.call-update) | async-done | bytes 221200 | tf_op jit(solution)/shard_map/reduce_scatter | solution.py:243
  1927.4 58.9 %all-reduce.14 = (bf16[768]{0:T(1024)(128)(2,1)}, bf16[768]{0:T(1024)(128)(2,1)}, bf16[768]{0:T(1024)(128)(2,1)}, bf16[768]{0:T(1024)(128)(2,1)}, bf16[768]{0:T(...) all-reduce(bf16[768]{0:T(1024)(128)(2,1)} %add_convert_fusion.32, ...), channel_id=14, replica_groups=mesh['dp'=16,'seq'=2] {'dp'}, use_global_device_ids=true, to_apply=%region_84.85.clone | all-reduce | flops 13056 | bytes 52224
  (1099 shorter events, 791.7 us)
Async XLA Ops:
  7.2 50.6 %all-gather.25.cloned.1.call-start = ((), (), s32[]{:S(2)}) async-start(), calls=%async_computation.35 | async-start | bytes 2359296 | tf_op jit(solution)/shard_map/all_gather | solution.py:153
  11.0 58.9 %all-gather.27.cloned.1.call-start = ((), (), s32[]{:S(2)}) async-start(), calls=%async_computation.36 | async-start | bytes 2359296 | tf_op jit(solution)/shard_map/all_gather | solution.py:153
  11.8 86.9 %all-gather.23.cloned.1.call-start = ((), (), s32[]{:S(2)}) async-start(), calls=%async_computation.34 | async-start | bytes 2359296 | tf_op jit(solution)/shard_map/all_gather | solution.py:153
  12.5 114.8 %all-gather.21.cloned.1.call-start = ((), (), s32[]{:S(2)}) async-start(), calls=%async_computation.33 | async-start | bytes 2359296 | tf_op jit(solution)/shard_map/all_gather | solution.py:153
  13.1 161.2 %all-gather.19.cloned.1.call-start = ((), (), s32[]{:S(2)}) async-start(), calls=%async_computation.18 | async-start | bytes 4718592 | tf_op jit(solution)/shard_map/all_gather | solution.py:144
  32.7 187.9 %all-gather.13.cloned.1.call-start = ((), (), s32[]{:S(2)}) async-start(), calls=%async_computation.15 | async-start | bytes 4718592 | tf_op jit(solution)/shard_map/all_gather | solution.py:144
  35.7 231.4 %all-gather.15.cloned.1.call-start = ((), (), s32[]{:S(2)}) async-start(), calls=%async_computation.16 | async-start | bytes 4718592 | tf_op jit(solution)/shard_map/all_gather | solution.py:144
  38.7 275.0 %all-gather.17.cloned.1.call-start = ((), (), s32[]{:S(2)}) async-start(), calls=%async_computation.17 | async-start | bytes 4718592 | tf_op jit(solution)/shard_map/all_gather | solution.py:144
  41.7 1376.0 %reduce-scatter.30.cloned.1.call-start = ((), (), s32[]{:S(2)}) async-start(), calls=%async_computation.25 | async-start | bytes 4718592 | tf_op jit(solution)/shard_map/reduce_scatter | solution.py:194
  330.7 13.8 copy-start.57
  344.5 11.6 copy-start.81
  356.1 11.8 copy-start.168
  356.1 11.8 copy-start.336
  356.2 11.8 copy-start.343
  389.8 11.6 copy-start.85
  413.3 12.5 copy-start.93
  413.3 82.1 %copy-start.235 = (f32[512]{0:T(512)}, f32[512]{0:T(512)S(1)}, u32[]{:S(2)}) copy-start(f32[512]{0:T(512)S(1)} %broadcast_multiply_fusion.3) | copy-start | bytes 6148
  413.6 12.1 copy-start.271
  413.7 81.7 %copy-start.296 = (f32[512]{0:T(512)}, f32[512]{0:T(512)S(1)}, u32[]{:S(2)}) copy-start(f32[512]{0:T(512)S(1)} %fusion.327) | copy-start | bytes 6148
  425.8 11.8 copy-start.158
  425.8 11.9 copy-start.79
  437.6 11.7 copy-start.169
  437.6 11.7 copy-start.337
  437.7 11.6 copy-start.344
  471.1 11.6 copy-start.83
  533.4 11.8 copy-start.170
  533.4 11.8 copy-start.338
  533.4 11.8 copy-start.345
  590.0 12.5 copy-start.99
  590.0 219.4 %copy-start.247 = (f32[512]{0:T(512)}, f32[512]{0:T(512)S(1)}, u32[]{:S(2)}) copy-start(f32[512]{0:T(512)S(1)} %broadcast_multiply_fusion.9) | copy-start | bytes 6148
  590.3 12.2 copy-start.275
  602.4 11.8 copy-start.160
  602.5 11.9 copy-start.80
  614.3 11.7 copy-start.171
  614.3 11.6 copy-start.339
  647.8 11.6 copy-start.84
  677.8 65.2 %copy-start.360 = (f32[512,3072]{1,0:T(8,128)}, f32[512,3072]{1,0:T(8,128)S(1)}, u32[]{:S(2)}) copy-start(f32[512,3072]{1,0:T(8,128)S(1)} %fusion.369) | copy-start | bytes 18874372
  677.9 65.2 %copy-start.6 = (bf16[4,1,512,768]{3,2,1,0:T(8,128)(2,1)S(1)}, bf16[4,1,512,768]{3,2,1,0:T(8,128)(2,1)}, u32[]{:S(2)}) copy-start(bf16[4,1,512,768]{3,2,1,0:T(8,128)(2,1)} %param.30) | copy-start | bytes 9437188
  677.9 65.2 %copy-start.184 = (f32[1,1,512]{2,1,0:T(1,128)S(1)}, f32[1,1,512]{2,1,0:T(1,128)}, u32[]{:S(2)}) copy-start(f32[1,1,512]{2,1,0:T(1,128)} %get-tuple-element.281) | copy-start | bytes 6148
  847.3 21.5 %copy-start.68 = (bf16[512,768]{0,1:T(8,128)(2,1)S(1)}, bf16[512,768]{0,1:T(8,128)(2,1)}, u32[]{:S(2)}) copy-start(bf16[512,768]{0,1:T(8,128)(2,1)} %copy.164) | copy-start | bytes 2359300
  918.2 21.8 %copy-start.33 = (bf16[1,1024,768]{1,2,0:T(8,128)(2,1)S(1)}, bf16[1,1024,768]{1,2,0:T(8,128)(2,1)}, u32[]{:S(2)}) copy-start(bf16[1,1024,768]{1,2,0:T(8,128)(2,1)} %copy.171) | copy-start | bytes 4718596
  955.1 467.8 %reduce-scatter.28.cloned.1.call-start = ((), (), s32[]{:S(2)}) async-start(), calls=%async_computation.24 | async-start | bytes 4718592 | tf_op jit(solution)/shard_map/reduce_scatter | solution.py:194
  955.1 20.3 copy-start.270
  980.9 21.9 %copy-start.32 = (bf16[1,1024,768]{1,2,0:T(8,128)(2,1)S(1)}, bf16[1,1024,768]{1,2,0:T(8,128)(2,1)}, u32[]{:S(2)}) copy-start(bf16[1,1024,768]{1,2,0:T(8,128)(2,1)} %copy.159) | copy-start | bytes 4718596
  1034.4 393.6 %reduce-scatter.26.cloned.1.call-start = ((), (), s32[]{:S(2)}) async-start(), calls=%async_computation.23 | async-start | bytes 4718592 | tf_op jit(solution)/shard_map/reduce_scatter | solution.py:194
  1076.1 21.1 %slice-start = ((s8[12582912]{0:T(1024)(128)(4,1)}), s8[4194304]{0:T(1024)(128)(4,1)S(1)}, s32[]{:S(2)}) async-start(s8[12582912]{0:T(1024)(128)(4,1)} %bitcast.793), calls=%async_computation.39 | async-start | bytes 8388608
  1076.2 21.0 %slice-start.1 = ((s8[12582912]{0:T(1024)(128)(4,1)}), s8[4194304]{0:T(1024)(128)(4,1)S(1)}, s32[]{:S(2)}) async-start(s8[12582912]{0:T(1024)(128)(4,1)} %bitcast.793), calls=%async_computation.40 | async-start | bytes 8388608
  1113.6 319.6 %reduce-scatter.32.cloned.1.call-start = ((), (), s32[]{:S(2)}) async-start(), calls=%async_computation.26 | async-start | bytes 4718592 | tf_op jit(solution)/shard_map/reduce_scatter | solution.py:194
  1175.4 458.4 %reduce-scatter.22.cloned.1.call-start = ((), (), s32[]{:S(2)}) async-start(), calls=%async_computation.21 | async-start | bytes 4718592 | tf_op jit(solution)/shard_map/reduce_scatter | solution.py:219
  1194.9 22.1 %copy-start.65 = (bf16[1,512,768]{1,2,0:T(8,128)(2,1)S(1)}, bf16[1,512,768]{1,2,0:T(8,128)(2,1)}, u32[]{:S(2)}) copy-start(bf16[1,512,768]{1,2,0:T(8,128)(2,1)} %copy.161) | copy-start | bytes 2359300
  1232.5 406.2 %reduce-scatter.24.cloned.1.call-start = ((), (), s32[]{:S(2)}) async-start(), calls=%async_computation.22 | async-start | bytes 4718592 | tf_op jit(solution)/shard_map/reduce_scatter | solution.py:219
  1251.7 22.0 %copy-start.64 = (bf16[1,512,768]{1,2,0:T(8,128)(2,1)S(1)}, bf16[1,512,768]{1,2,0:T(8,128)(2,1)}, u32[]{:S(2)}) copy-start(bf16[1,512,768]{1,2,0:T(8,128)(2,1)} %copy.167) | copy-start | bytes 2359300
  1289.3 354.3 %reduce-scatter.20.cloned.1.call-start = ((), (), s32[]{:S(2)}) async-start(), calls=%async_computation.20 | async-start | bytes 4718592 | tf_op jit(solution)/shard_map/reduce_scatter | solution.py:219
  1308.6 22.1 %copy-start.62 = (bf16[1,512,768]{1,2,0:T(8,128)(2,1)S(1)}, bf16[1,512,768]{1,2,0:T(8,128)(2,1)}, u32[]{:S(2)}) copy-start(bf16[1,512,768]{1,2,0:T(8,128)(2,1)} %copy.155) | copy-start | bytes 2359300
  1346.3 317.0 %reduce-scatter.18.cloned.1.call-start = ((), (), s32[]{:S(2)}) async-start(), calls=%async_computation.19 | async-start | bytes 4718592 | tf_op jit(solution)/shard_map/reduce_scatter | solution.py:219
  1365.9 22.1 %copy-start.60 = (bf16[1,512,768]{1,2,0:T(8,128)(2,1)S(1)}, bf16[1,512,768]{1,2,0:T(8,128)(2,1)}, u32[]{:S(2)}) copy-start(bf16[1,512,768]{1,2,0:T(8,128)(2,1)} %copy.149) | copy-start | bytes 2359300
  1403.6 307.2 %reduce-scatter.46.cloned.1.call-start = ((), (), s32[]{:S(2)}) async-start(), calls=%async_computation.37 | async-start | bytes 2506752
  1446.3 266.4 %reduce-scatter.40.cloned.1.call-start = ((), (), s32[]{:S(2)}) async-start(), calls=%async_computation.30 | async-start | bytes 1253376 | tf_op jit(solution)/shard_map/reduce_scatter | solution.py:276
  1475.7 236.9 %reduce-scatter.38.cloned.1.call-start = ((), (), s32[]{:S(2)}) async-start(), calls=%async_computation.29 | async-start | bytes 1253376 | tf_op jit(solution)/shard_map/reduce_scatter | solution.py:264
  1497.0 215.6 %reduce-scatter.36.cloned.1.call-start = ((), (), s32[]{:S(2)}) async-start(), calls=%async_computation.28 | async-start | bytes 1253376 | tf_op jit(solution)/shard_map/reduce_scatter | solution.py:252
  1525.3 250.8 %reduce-scatter.42.cloned.1.call-start = ((), (), s32[]{:S(2)}) async-start(), calls=%async_computation.31 | async-start | bytes 5013504 | tf_op jit(solution)/shard_map/reduce_scatter | solution.py:288
  1544.9 309.7 %reduce-scatter.44.cloned.1.call-start = ((), (), s32[]{:S(2)}) async-start(), calls=%async_computation.32 | async-start | bytes 5013504 | tf_op jit(solution)/shard_map/reduce_scatter | solution.py:294
  1610.8 315.3 %reduce-scatter.34.cloned.1.call-start = ((), (), s32[]{:S(2)}) async-start(), calls=%async_computation.27 | async-start | bytes 3760128 | tf_op jit(solution)/shard_map/reduce_scatter | solution.py:243
  1679.4 356.3 %all-reduce.19.cloned.1.call-start = ((), (), s32[]{:S(2)}) async-start(), calls=%async_computation.38 | async-start | bytes 2850816 | tf_op jit(solution)/shard_map/psum | solution.py:313
  (327 other events, 1697.9 us)
Sparse Core Ops, SparseCore 0:
  11.1 29.9 all-gather.24
  42.6 27.1 all-gather.26
  71.4 27.2 all-gather.22
  100.1 27.2 all-gather.20
  129.3 44.9 all-gather.18
  175.6 44.9 all-gather.12
  222.2 44.9 all-gather.14
  268.7 44.9 all-gather.16
  955.2 43.3 reduce-scatter.29
  1034.5 43.3 reduce-scatter.27
  1113.7 43.3 reduce-scatter.25
  1175.5 43.1 reduce-scatter.31
  1232.6 43.1 reduce-scatter.21
  1289.5 43.0 reduce-scatter.23
  1346.5 43.0 reduce-scatter.19
  1403.7 42.9 reduce-scatter.17
  1450.3 62.9 reduce-scatter.45
  1517.2 57.1 reduce-scatter.39
  1578.4 57.0 reduce-scatter.37
  1639.5 57.0 reduce-scatter.35
  1701.5 74.5 reduce-scatter.41
  1780.0 74.6 reduce-scatter.43
  1859.0 67.0 reduce-scatter.33
  1929.5 48.1 all-reduce.18
where the time goes:
time: 2070 us; the launch traced here: 2050 us
  matrix products  988 us (48%)
  other arithmetic  397 us (19%)
  waiting for transfers between devices  384 us (19%)
  local copies, waits for them, and re-layouts  196 us (9%)
  blocking collectives  64.6 us (3%)
  between operations  22.8 us (1%)
    dot_general x28, matrix products, project_rows(): jnp.einsum('bpd,de->bpe', row_block, weight, preferred_element_type=jnp.f...  156 us
    dot_general x28, matrix products, outer_sum(): jnp.einsum('bpd,bpe->de', first_rows, second_rows, preferred_element_type...  155 us
    convert_element_type x8, other arithmetic, attend_backward(): score_low = score_grads.astype(jnp.bfloat16)  152 us
    dot_general x8, matrix products, attend_backward(): jnp.einsum('bphe,bshe->bhps', upstream_heads, split_heads(values), prefer...  152 us
    all_gather x4, waiting for transfers between devices, on_device(): gathered_self = lax.all_gather(own_pairs, 'seq', axis=1, tiled=True)  137 us
    dot_general x28, matrix products, project_back(): jnp.einsum('bpe,de->bpd', row_block, weight, preferred_element_type=jnp.f...  135 us
    dot_general x8, matrix products, masked_scores(): jnp.einsum('bphe,bshe->bhps', split_heads(queries), split_heads(key_rows)...  98.7 us
    dot_general x8, matrix products, attend_forward(): jnp.einsum('bhps,bshe->bphe', weights, split_heads(values), preferred_ele...  91.1 us
  transfers between devices with their start and end apart: 24, of which 10 were waited for; matrix products, arithmetic and copies ran while one was open for 43% of the time, Pallas kernels for 0%

commit v1 on v0

--- a/solution.py
+++ b/solution.py
@@ -1,6 +1,10 @@
+import functools
+
 import jax
 import jax.numpy as jnp
 from jax import lax
+from jax.experimental import pallas as pl
+from jax.experimental.pallas import tpu as pltpu
 from jax.sharding import PartitionSpec as P
 
 HEADS = 12
@@ -89,7 +93,7 @@
     return (query_grads, jnp.concatenate([key_grads, value_grads.reshape(key_rows.shape)], axis=-1))
 
 
-def on_device(
+def split_sequences(
     targets,
     memory,
     row_kind,
@@ -233,95 +237,356 @@
             if totals is None
             else [running + added for running, added in zip(totals, pieces)]
         )
-    block_sums = (
-        lax.psum_scatter(
-            totals[0].astype(jnp.bfloat16), "dp", scatter_dimension=0, tiled=True
-        ).astype(jnp.float32),
-        lax.psum_scatter(
-            totals[1].astype(jnp.bfloat16), "dp", scatter_dimension=0, tiled=True
-        ).astype(jnp.float32),
-        lax.psum_scatter(
-            totals[2].astype(jnp.bfloat16), "dp", scatter_dimension=0, tiled=True
-        ).astype(jnp.float32),
-        lax.psum_scatter(
-            totals[3].astype(jnp.bfloat16), "dp", scatter_dimension=0, tiled=True
-        ).astype(jnp.float32),
-        lax.psum_scatter(
-            totals[4].astype(jnp.bfloat16), "dp", scatter_dimension=0, tiled=True
-        ).astype(jnp.float32),
-        lax.psum_scatter(
-            totals[5].astype(jnp.bfloat16), "dp", scatter_dimension=0, tiled=True
-        ).astype(jnp.float32),
-        lax.psum_scatter(
-            totals[6].astype(jnp.bfloat16), "dp", scatter_dimension=0, tiled=True
-        ).astype(jnp.float32),
-        lax.psum_scatter(
-            totals[7].astype(jnp.bfloat16), "dp", scatter_dimension=0, tiled=True
-        ).astype(jnp.float32),
-        lax.psum_scatter(
-            totals[8].astype(jnp.bfloat16), "dp", scatter_dimension=0, tiled=True
-        ).astype(jnp.float32),
-        lax.psum_scatter(
-            totals[9].astype(jnp.bfloat16), "dp", scatter_dimension=0, tiled=True
-        ).astype(jnp.float32),
-        lax.psum_scatter(
-            totals[10].astype(jnp.bfloat16), "dp", scatter_dimension=0, tiled=True
-        ).astype(jnp.float32),
-        lax.psum_scatter(
-            totals[11].astype(jnp.bfloat16), "dp", scatter_dimension=0, tiled=True
-        ).astype(jnp.float32),
-        lax.psum_scatter(
-            totals[12].astype(jnp.bfloat16), "dp", scatter_dimension=0, tiled=True
-        ).astype(jnp.float32),
-        lax.psum_scatter(
-            totals[13].astype(jnp.bfloat16), "dp", scatter_dimension=0, tiled=True
-        ).astype(jnp.float32),
-        lax.psum_scatter(
-            totals[14].astype(jnp.bfloat16), "dp", scatter_dimension=0, tiled=True
-        ).astype(jnp.float32),
-        lax.psum_scatter(
-            totals[15].astype(jnp.bfloat16), "dp", scatter_dimension=0, tiled=True
-        ).astype(jnp.float32),
-        lax.psum_scatter(
-            totals[16].astype(jnp.bfloat16), "dp", scatter_dimension=0, tiled=True
-        ).astype(jnp.float32),
-        lax.psum_scatter(
-            totals[17].astype(jnp.bfloat16), "dp", scatter_dimension=0, tiled=True
-        ).astype(jnp.float32),
-        lax.psum_scatter(
-            totals[18].astype(jnp.bfloat16), "dp", scatter_dimension=0, tiled=True
-        ).astype(jnp.float32),
-        lax.psum_scatter(
-            totals[19].astype(jnp.bfloat16), "dp", scatter_dimension=0, tiled=True
-        ).astype(jnp.float32),
-        lax.psum_scatter(
-            totals[20].astype(jnp.bfloat16), "dp", scatter_dimension=0, tiled=True
-        ).astype(jnp.float32),
-    )
-    final = (
-        lax.psum(block_sums[0].astype(jnp.bfloat16), "seq").astype(jnp.float32),
-        lax.psum(block_sums[1].astype(jnp.bfloat16), "seq").astype(jnp.float32),
-        lax.psum(block_sums[2].astype(jnp.bfloat16), "seq").astype(jnp.float32),
-        lax.psum(block_sums[3].astype(jnp.bfloat16), "seq").astype(jnp.float32),
-        lax.psum(block_sums[4].astype(jnp.bfloat16), "seq").astype(jnp.float32),
-        lax.psum(block_sums[5].astype(jnp.bfloat16), "seq").astype(jnp.float32),
-        lax.psum(block_sums[6].astype(jnp.bfloat16), "seq").astype(jnp.float32),
-        lax.psum(block_sums[7].astype(jnp.bfloat16), "seq").astype(jnp.float32),
-        lax.psum(block_sums[8].astype(jnp.bfloat16), "seq").astype(jnp.float32),
-        lax.psum(block_sums[9].astype(jnp.bfloat16), "seq").astype(jnp.float32),
-        lax.psum(block_sums[10].astype(jnp.bfloat16), "seq").astype(jnp.float32),
-        lax.psum(block_sums[11].astype(jnp.bfloat16), "seq").astype(jnp.float32),
-        lax.psum(block_sums[12].astype(jnp.bfloat16), "seq").astype(jnp.float32),
-        lax.psum(block_sums[13].astype(jnp.bfloat16), "seq").astype(jnp.float32),
-        lax.psum(block_sums[14].astype(jnp.bfloat16), "seq").astype(jnp.float32),
-        lax.psum(block_sums[15].astype(jnp.bfloat16), "seq").astype(jnp.float32),
-        lax.psum(block_sums[16].astype(jnp.bfloat16), "seq").astype(jnp.float32),
-        lax.psum(block_sums[17].astype(jnp.bfloat16), "seq").astype(jnp.float32),
-        lax.psum(block_sums[18].astype(jnp.bfloat16), "seq").astype(jnp.float32),
-        lax.psum(block_sums[19].astype(jnp.bfloat16), "seq").astype(jnp.float32),
-        lax.psum(block_sums[20].astype(jnp.bfloat16), "seq").astype(jnp.float32),
-    )
+    def reduced(total):
+        block = lax.psum_scatter(
+            total.astype(jnp.bfloat16), "dp", scatter_dimension=0, tiled=True
+        )
+        return lax.psum(block, "seq").astype(jnp.float32)
+
+    final = [reduced(total) for total in totals]
     return (jnp.stack(results), jnp.stack(input_grads), jnp.stack(source_grads)) + tuple(final)
+
+
+def contract(first, second, first_dim, second_dim):
+    return lax.dot_general(
+        first, second, (((first_dim,), (second_dim,)), ((), ())), preferred_element_type=jnp.float32
+    )
+
+
+def head_masks(pair):
+    lane = lax.broadcasted_iota(jnp.int32, (1, pair.shape[1]), 1)
+    zero = jnp.zeros((), pair.dtype)
+    return (jnp.where(lane < HEAD, pair, zero), jnp.where(lane < HEAD, zero, pair))
+
+
+def attend_kernel(info_ref, q_ref, k_ref, v_ref, o_ref, e_ref, r_ref, *, block, use_mask):
+    length = k_ref.shape[1]
+    values_turned = v_ref[0].T
+    ones = jnp.ones((16, length), jnp.bfloat16)
+    own = length // 2
+    causal = info_ref[1 + pl.program_id(0)] == 0 if use_mask else None
+
+    def allowed(start):
+        offset = info_ref[0] * own
+        key_place = lax.broadcasted_iota(jnp.int32, (length, 1), 0) + offset
+        key_place = jnp.where(key_place >= length, key_place - length, key_place)
+        query_place = lax.broadcasted_iota(jnp.int32, (1, block), 1) + start + offset
+        query_place = jnp.where(query_place >= length, query_place - length, query_place)
+        return key_place <= query_place
+
+    def run(masked, shifted):
+        lowest, highest = None, None
+        for start in range(0, length, block):
+            mixed = []
+            for head, queries in enumerate(head_masks(q_ref[0, start : start + block, :])):
+                scores = contract(k_ref[0], queries, 1, 1)
+                if masked and shifted:
+                    scores = jnp.where(allowed(start), scores, blocked_score)
+                if shifted:
+                    scores = scores - jnp.max(scores, axis=0, keepdims=True)
+                raised = jnp.exp(scores)
+                if masked:
+                    raised = jnp.where(allowed(start), raised, 0.0)
+                low = raised.astype(jnp.bfloat16)
+                e_ref[0, head, :, start : start + block] = low
+                turned = jnp.concatenate(
+                    [values_turned[head * HEAD : (head + 1) * HEAD], ones], axis=0
+                )
+                sums = contract(turned, low, 1, 0)
+                total = sums[HEAD : HEAD + 1]
+                if not shifted:
+                    lowest = total if lowest is None else jnp.minimum(lowest, total)
+                    highest = total if highest is None else jnp.maximum(highest, total)
+                inverse = 1.0 / total
+                r_ref[0, 0, head : head + 1, start : start + block] = inverse
+                mixed.append(sums[:HEAD] * inverse)
+            o_ref[0, start : start + block, :] = (
+                jnp.concatenate(mixed, axis=0).T.astype(jnp.bfloat16)
+            )
+        if not shifted:
+            in_range = (jnp.min(lowest) > 1e-20) & (jnp.max(highest) < 1e30)
+
+            @pl.when(jnp.logical_not(in_range))
+            def _():
+                run(masked, True)
+
+    if use_mask:
+
+        @pl.when(causal)
+        def _():
+            run(True, False)
+
+        @pl.when(jnp.logical_not(causal))
+        def _():
+            run(False, False)
+
+    else:
+        run(False, False)
+
+
+def attend(info, queries, keys, values, use_mask, offsets):
+    count, length = queries.shape[:2]
+    pairs = HEADS * HEAD // 128
+    width = HEADS * HEAD
+
+    def spec(offset):
+        return pl.BlockSpec((1, length, 128), lambda s, p, info: (s, 0, offset * pairs + p))
+
+    return pl.pallas_call(
+        functools.partial(attend_kernel, block=length // 2, use_mask=use_mask),
+        grid_spec=pltpu.PrefetchScalarGridSpec(
+            num_scalar_prefetch=1,
+            grid=(count, pairs),
+            in_specs=[spec(offset) for offset in offsets],
+            out_specs=[
+                spec(0),
+                pl.BlockSpec((1, 2, length, length), lambda s, p, info: (s, p, 0, 0)),
+                pl.BlockSpec((1, 1, 2, length), lambda s, p, info: (s, p, 0, 0)),
+            ],
+        ),
+        out_shape=[
+            jax.ShapeDtypeStruct((count, length, width), jnp.bfloat16),
+            jax.ShapeDtypeStruct((count, HEADS, length, length), jnp.bfloat16),
+            jax.ShapeDtypeStruct((count, pairs, 2, length), jnp.float32),
+        ],
+        compiler_params=pltpu.CompilerParams(vmem_limit_bytes=56 * 2**20),
+        cost_estimate=pl.CostEstimate(
+            flops=4 * count * HEADS * length * length * 256,
+            bytes_accessed=count * HEADS * length * length * 2,
+            transcendentals=count * HEADS * length * length,
+        ),
+        name="attend",
+    )(info, queries, keys, values)
+
+
+def attend_back_kernel(q_ref, k_ref, v_ref, o_ref, g_ref, e_ref, r_ref, dq_ref, dk_ref, dv_ref):
+    length = k_ref.shape[1]
+    keys_turned = k_ref[0].T
+    upstream = g_ref[0].astype(jnp.float32)
+    products = (o_ref[0].astype(jnp.float32) * upstream).T
+    upstream = upstream.T
+    parts, deltas = [], []
+    for head in range(2):
+        rows = slice(head * HEAD, (head + 1) * HEAD)
+        inverse = r_ref[0, 0, head : head + 1, :]
+        parts.append(upstream[rows] * inverse)
+        deltas.append(jnp.sum(products[rows], axis=0, keepdims=True) * inverse)
+    scaled = head_masks(jnp.concatenate(parts, axis=0).T.astype(jnp.bfloat16))
+    queries = head_masks(q_ref[0])
+    key_sum, value_sum, query_parts = 0.0, 0.0, []
+    for head in range(2):
+        rows = slice(head * HEAD, (head + 1) * HEAD)
+        low = e_ref[0, head]
+        grads = contract(v_ref[0], scaled[head], 1, 1)
+        score_low = (low.astype(jnp.float32) * (grads - deltas[head])).astype(jnp.bfloat16)
+        value_sum += contract(low, scaled[head], 1, 0)
+        key_sum += contract(score_low, queries[head], 1, 0)
+        query_parts.append(contract(keys_turned[rows], score_low, 1, 0))
+    turned = jnp.concatenate(query_parts, axis=0) * (HEAD**-0.5)
+    dq_ref[0] = turned.T.astype(jnp.bfloat16)
+    dk_ref[0] = key_sum.astype(jnp.bfloat16)
+    dv_ref[0] = value_sum.astype(jnp.bfloat16)
+
+
+def attend_back(queries, keys, values, offsets, mixed, upstream, raised, inverse):
+    count, length = queries.shape[:2]
+    pairs = HEADS * HEAD // 128
+    width = HEADS * HEAD
+
+    def spec(offset):
+        return pl.BlockSpec((1, length, 128), lambda s, p: (s, 0, offset * pairs + p))
+
+    return pl.pallas_call(
+        attend_back_kernel,
+        grid=(count, pairs),
+        in_specs=[spec(offset) for offset in offsets]
+        + [
+            spec(0),
+            spec(0),
+            pl.BlockSpec((1, 2, length, length), lambda s, p: (s, p, 0, 0)),
+            pl.BlockSpec((1, 1, 2, length), lambda s, p: (s, p, 0, 0)),
+        ],
+        out_specs=[spec(0)] * 3,
+        out_shape=[jax.ShapeDtypeStruct((count, length, width), jnp.bfloat16)] * 3,
+        compiler_params=pltpu.CompilerParams(vmem_limit_bytes=56 * 2**20),
+        cost_estimate=pl.CostEstimate(
+            flops=8 * count * HEADS * length * length * 256,
+            bytes_accessed=count * HEADS * length * length * 2,
+            transcendentals=0,
+        ),
+        name="attend_back",
+    )(queries, keys, values, mixed, upstream, raised, inverse)
+
+
+SWAP = ((0, 1), (1, 0))
+
+
+def tree_sum(blocks):
+    place = lax.axis_index("dp")
+    count = lax.axis_size("dp")
+    steps = count.bit_length() - 1
+    blocks = blocks.reshape((2,) * steps + blocks.shape[1:])
+    for step in range(steps):
+        bit = 1 << step
+        mine = (place // bit) % 2
+        axis = steps - 1 - step
+        kept = lax.dynamic_index_in_dim(blocks, mine, axis, keepdims=False)
+        sent = lax.dynamic_index_in_dim(blocks, 1 - mine, axis, keepdims=False)
+        got = lax.ppermute(sent, "dp", [(i, i ^ bit) for i in range(count)])
+        blocks = (kept.astype(jnp.float32) + got.astype(jnp.float32)).astype(jnp.bfloat16)
+    got = lax.ppermute(blocks, "seq", SWAP)
+    return blocks.astype(jnp.float32) + got.astype(jnp.float32)
+
+
+def whole_sequences(
+    targets,
+    memory,
+    row_kind,
+    loss_mask,
+    cotangent,
+    norm_self_gain,
+    norm_self_bias,
+    self_input,
+    self_query_bias,
+    self_value_bias,
+    self_output,
+    self_output_bias,
+    norm_cross_gain,
+    norm_cross_bias,
+    cross_query,
+    cross_query_bias,
+    cross_input,
+    cross_value_bias,
+    cross_output,
+    cross_output_bias,
+    norm_feed_gain,
+    norm_feed_bias,
+    feed_in,
+    feed_in_bias,
+    feed_out,
+    feed_out_bias,
+):
+    micros, _, own, width = targets.shape
+    held = micros // 2
+    side = lax.axis_index("seq")
+    query_scale = HEAD ** (-0.5)
+
+    def take(rows):
+        kept = lax.dynamic_slice_in_dim(rows, side * held, held, axis=0)
+        sent = lax.dynamic_slice_in_dim(rows, (1 - side) * held, held, axis=0)
+        got = lax.ppermute(sent, "seq", SWAP)
+        return jnp.concatenate([kept[:, 0], got[:, 0]], axis=1)
+
+    def give(rows, dtype):
+        got = lax.ppermute(rows[:, own:].astype(jnp.bfloat16), "seq", SWAP).astype(dtype)
+        kept = rows[:, :own].astype(dtype)
+        first = jnp.where(side == 0, kept, got)
+        second = jnp.where(side == 0, got, kept)
+        return jnp.concatenate([first, second], axis=0)[:, None]
+
+    inputs = take(targets).astype(jnp.float32)
+    sources = take(memory)
+    output_low = take(
+        (cotangent.astype(jnp.float32) * loss_mask.astype(jnp.float32)[..., None]).astype(
+            jnp.bfloat16
+        )
+    )
+    kinds = lax.dynamic_slice_in_dim(row_kind[:, 0], side * held, held, axis=0)
+    info = jnp.concatenate([side[None].astype(jnp.int32), kinds])
+
+    first_normed = normed(inputs, norm_self_gain, norm_self_bias).astype(jnp.bfloat16)
+    joint_bias = jnp.concatenate(
+        [self_query_bias, jnp.zeros_like(self_query_bias), self_value_bias]
+    )
+    joint_scale = jnp.where(jnp.arange(3 * width) < width, query_scale, 1.0)
+    joint = ((project_rows(first_normed, self_input) + joint_bias) * joint_scale).astype(
+        jnp.bfloat16
+    )
+    self_mixed, self_raised, self_inverse = attend(info, joint, joint, joint, True, (0, 1, 2))
+    after_self = inputs + project_rows(self_mixed, self_output) + self_output_bias
+    second_normed = normed(after_self, norm_cross_gain, norm_cross_bias).astype(jnp.bfloat16)
+    cross_queries = (
+        (project_rows(second_normed, cross_query) + cross_query_bias) * query_scale
+    ).astype(jnp.bfloat16)
+    pair_bias = jnp.concatenate([jnp.zeros_like(cross_value_bias), cross_value_bias])
+    cross_pairs = (project_rows(sources, cross_input) + pair_bias).astype(jnp.bfloat16)
+    cross_mixed, cross_raised, cross_inverse = attend(
+        info, cross_queries, cross_pairs, cross_pairs, False, (0, 0, 1)
+    )
+    after_cross = after_self + project_rows(cross_mixed, cross_output) + cross_output_bias
+    third_normed = normed(after_cross, norm_feed_gain, norm_feed_bias).astype(jnp.bfloat16)
+    activated, gelu_pullback = jax.vjp(
+        gelu_exact, project_rows(third_normed, feed_in) + feed_in_bias
+    )
+    activated_low = activated.astype(jnp.bfloat16)
+    result = (after_cross + project_rows(activated_low, feed_out) + feed_out_bias).astype(
+        jnp.bfloat16
+    )
+    pieces = [None] * 21
+    grad_output = output_low.astype(jnp.float32)
+    pieces[19] = outer_sum(activated_low, output_low)
+    pieces[20] = jnp.sum(grad_output, axis=(0, 1))
+    grad_hidden = gelu_pullback(project_back(output_low, feed_out))[0]
+    hidden_low = grad_hidden.astype(jnp.bfloat16)
+    pieces[17] = outer_sum(third_normed, hidden_low)
+    pieces[18] = jnp.sum(grad_hidden, axis=(0, 1))
+    through_feed, pieces[15], pieces[16] = normed_back(
+        after_cross, norm_feed_gain, norm_feed_bias, project_back(hidden_low, feed_in)
+    )
+    grad_cross = grad_output + through_feed
+    cross_low = grad_cross.astype(jnp.bfloat16)
+    pieces[13] = outer_sum(cross_mixed, cross_low)
+    pieces[14] = jnp.sum(grad_cross, axis=(0, 1))
+    cross_upstream = project_back(cross_low, cross_output).astype(jnp.bfloat16)
+    scaled_cross, cross_key_grads, cross_value_grads = attend_back(
+        cross_queries, cross_pairs, cross_pairs, (0, 0, 1), cross_mixed, cross_upstream,
+        cross_raised, cross_inverse,
+    )
+    pair_grads = jnp.concatenate([cross_key_grads, cross_value_grads], axis=-1)
+    pieces[12] = jnp.sum(cross_value_grads.astype(jnp.float32), axis=(0, 1))
+    pieces[11] = outer_sum(sources, pair_grads)
+    source_grad = project_back(pair_grads, cross_input)
+    pieces[10] = jnp.sum(scaled_cross.astype(jnp.float32), axis=(0, 1))
+    pieces[9] = outer_sum(second_normed, scaled_cross)
+    through_cross, pieces[7], pieces[8] = normed_back(
+        after_self, norm_cross_gain, norm_cross_bias, project_back(scaled_cross, cross_query)
+    )
+    grad_self = grad_cross + through_cross
+    self_low = grad_self.astype(jnp.bfloat16)
+    pieces[5] = outer_sum(self_mixed, self_low)
+    pieces[6] = jnp.sum(grad_self, axis=(0, 1))
+    self_upstream = project_back(self_low, self_output).astype(jnp.bfloat16)
+    joint_grads = attend_back(
+        joint, joint, joint, (0, 1, 2), self_mixed, self_upstream, self_raised, self_inverse
+    )
+    pieces[3] = jnp.sum(joint_grads[0].astype(jnp.float32), axis=(0, 1))
+    pieces[4] = jnp.sum(joint_grads[2].astype(jnp.float32), axis=(0, 1))
+    joint_low = jnp.concatenate(joint_grads, axis=-1)
+    pieces[2] = outer_sum(first_normed, joint_low)
+    through_first, pieces[0], pieces[1] = normed_back(
+        inputs, norm_self_gain, norm_self_bias, project_back(joint_low, self_input)
+    )
+    input_grad = grad_self + through_first
+
+    count = lax.axis_size("dp")
+    final = [None] * 21
+    small = []
+    for index, piece in enumerate(pieces):
+        if piece.ndim == 2:
+            blocks = piece.astype(jnp.bfloat16).reshape(count, piece.shape[0] // count, -1)
+            final[index] = tree_sum(blocks)
+        else:
+            small.append((index, piece.reshape(count, -1)))
+    joined = tree_sum(jnp.concatenate([part for _, part in small], axis=1).astype(jnp.bfloat16))
+    place = 0
+    for index, part in small:
+        final[index] = joined[place : place + part.shape[1]]
+        place += part.shape[1]
+    return (
+        give(result, jnp.bfloat16),
+        give(input_grad, jnp.float32),
+        give(source_grad, jnp.float32),
+    ) + tuple(final)
 
 
 def solution(mesh):
@@ -379,6 +644,14 @@
         P("dp", None),
         P("dp"),
     )
+
+    def on_device(*arguments):
+        micros = arguments[0].shape[0]
+        rows = lax.axis_size("dp")
+        pairs = lax.axis_size("seq") == 2 and micros % 2 == 0
+        whole = pairs and rows & (rows - 1) == 0
+        return (whole_sequences if whole else split_sequences)(*arguments)
+
     return jax.shard_map(
         on_device, mesh=mesh, in_specs=in_specs, out_specs=out_specs, check_vma=False
     )

time: 2070 us -> 944 us (0.46)
  matrix products: 988 us -> 223 us
  other arithmetic: 397 us -> 177 us
  waiting for transfers between devices: 384 us -> 172 us
  Pallas kernels: 0 us -> 189 us
  local copies, waits for them, and re-layouts: 196 us -> 116 us
  blocking collectives: 64.6 us -> 0 us
  starting transfers between devices: 2.17 us -> 55.5 us
    dot_general x48 -> x0, matrix products: 541 us -> none  [the longest x8 152 us: attend_backward(): jnp.einsum('bphe,bshe->bhps', upstream_heads, split_heads(values), prefer...]
    reduce_scatter x14 -> x0, waiting for transfers between devices: 214 us -> none  [the longest x1 78.5 us: on_device(): lax.psum_scatter(totals[19].astype(jnp.bfloat16), 'dp', scatter_dimension...]
    pallas_call x0 -> x4, Pallas kernels: none -> 189 us  [the longest x2 117 us: attend_back(): pl.pallas_call(attend_back_kernel, grid=(count, pairs), in_specs=[spec(of...]
    ppermute x0 -> x46, waiting for transfers between devices: none -> 172 us  [the longest x32 136 us: tree_sum(): got = lax.ppermute(sent, 'dp', [(i, i ^ bit) for i in range(count)])]
    all_gather x8 -> x0, waiting for transfers between devices: 169 us -> none  [the longest x4 137 us: on_device(): gathered_self = lax.all_gather(own_pairs, 'seq', axis=1, tiled=True)]
    convert_element_type x44 -> x37, other arithmetic: 195 us -> 78.1 us  [the longest x1 62.9 us: whole_sequences(): activated_low = activated.astype(jnp.bfloat16)]
    reduce_sum x24 -> x9, other arithmetic: 120 us -> 26.5 us  [the longest x1 7.47 us: whole_sequences(): pieces[6] = jnp.sum(grad_self, axis=(0, 1))]
    dot_general x28 -> x7, matrix products: 155 us -> 67.4 us  [outer_sum(): jnp.einsum('bpd,bpe->de', first_rows, second_rows, preferred_element_type...]
  transfers between devices with their start and end apart: 24 -> 46, of which waited for: 10 -> 26; matrix products, arithmetic and copies ran while one was open for 43% -> 29% of each run, Pallas kernels for 0% -> 8%
where the time goes in v1:
time: 944 us; the launch traced here: 935 us
  matrix products  223 us (24%)
  Pallas kernels  189 us (20%)
  other arithmetic  177 us (19%)
  waiting for transfers between devices  172 us (18%)
  local copies, waits for them, and re-layouts  116 us (12%)
  starting transfers between devices  55.5 us (6%)
    ppermute x32, waiting for transfers between devices, tree_sum(): got = lax.ppermute(sent, 'dp', [(i, i ^ bit) for i in range(count)])  136 us
    pallas_call x2, Pallas kernels, attend_back(): pl.pallas_call(attend_back_kernel, grid=(count, pairs), in_specs=[spec(of...  117 us
    dot_general x7, matrix products, project_rows(): jnp.einsum('bpd,de->bpe', row_block, weight, preferred_element_type=jnp.f...  83 us
    pallas_call x2, Pallas kernels, attend(): pl.pallas_call(functools.partial(attend_kernel, block=length // 2, use_ma...  72.3 us
    dot_general x7, matrix products, project_back(): jnp.einsum('bpe,de->bpd', row_block, weight, preferred_element_type=jnp.f...  72.2 us
    dot_general x7, matrix products, outer_sum(): jnp.einsum('bpd,bpe->de', first_rows, second_rows, preferred_element_type...  67.4 us
    convert_element_type x1, other arithmetic, whole_sequences(): activated_low = activated.astype(jnp.bfloat16)  62.9 us
    unnamed x189, local copies, waits for them, and re-layouts  36.8 us
  transfers between devices with their start and end apart: 46, of which 26 were waited for; matrix products, arithmetic and copies ran while one was open for 29% of the time, Pallas kernels for 8%

profile of v1, /device:TPU:0, one launch (start us, length us, event | category | flops | bytes accessed | tf_op | source)
XLA Modules:
  0.0 934.8 jit_solution(1340752229153679695)
XLA Ops:
  0.7 3.9 constant_dynamic-slice_fusion.25
  12.8 4.6 copy.149
  30.1 15.5 %collective-permute-done = bf16[2,1,512,768]{2,3,0,1:T(8,128)(2,1)} collective-permute-done((bf16[2,1,512,768]{2,3,0,1:T(8,128)(2,1)}, bf16[2,1,512,768]{2,3,0,1:T(8,128)(2,1)}, u32[]{:S(2)}, u32[]{:S(2)}) %collective-permute-start) | collective-permute-done | bytes 1572896 | tf_op jit(solution)/shard_map/ppermute | solution.py:477
  51.6 13.0 %multiply_convert_fusion.1.q_ref.k_ref.v_ref = bf16[2,1024,2304]{2,1,0:T(8,128)(2,1)} fusion(f32[2304]{0:T(1024)S(1)} %get-tuple-element.200, f32[2304]{0:T(1024)S(1)} %get-tuple-element.199, bf16[768,2304]{1,0:T(8,128)(2,1)S(1)} %copy-done, f32[768]{0:T(1024)S(1)} %copy-done.76, f32[768]{0:T(1024)S(1)} %copy-done.51, f32[2,1024]{1,0:T(2,128)S(1)} %fusion.86, ...), kind=kOutput, calls=%fused_computation.21 | convolution fusion | flops 7276068864 | bytes 16162816 | tf_op jit(solution)/shard_map/bpd,de->bpe/dot_general | solution.py:34
  64.6 40.7 %attend.2 = (bf16[2,1024,768]{2,1,0:T(8,128)(2,1)}, bf16[2,12,1024,1024]{3,2,1,0:T(8,128)(2,1)}, f32[2,6,2,1024]{3,2,1,0:T(2,128)}) custom-call(s32[3]{0:T(128)} %pad_add_fusion.info_ref, bf16[2,1024,2304]{2,1,0:T(8,128)(2,1)} %multiply_convert_fusion.1.q_ref.k_ref.v_ref, bf16[2,1024,2304]{2,1,0:T(8,128)(2,1)} %multiply_convert_fusion.1.q_ref.k_ref.v_ref, ...), custom_call_target="tpu_custom_call" | custom-call | flops 25769803776 | bytes 50331648 | tf_op jit(solution)/shard_map/attend/pallas_call | solution.py:335
  105.3 5.5 fusion.105
  114.3 4.1 multiply_convert_fusion.3.q_ref
  118.4 8.4 add_convert_fusion.k_ref.v_ref
  126.8 31.7 %attend.3 = (bf16[2,1024,768]{2,1,0:T(8,128)(2,1)}, bf16[2,12,1024,1024]{3,2,1,0:T(8,128)(2,1)}, f32[2,6,2,1024]{3,2,1,0:T(2,128)}) custom-call(s32[3]{0:T(128)} %pad_add_fusion.info_ref, bf16[2,1024,768]{2,1,0:T(8,128)(2,1)} %multiply_convert_fusion.3.q_ref, bf16[2,1024,1536]{2,1,0:T(8,128)(2,1)} %add_convert_fusion.k_ref.v_ref, ...), custom_call_target="tpu_custom_call" | custom-call | flops 25769803776 | bytes 50331648 | tf_op jit(solution)/shard_map/attend/pallas_call | solution.py:335
  158.5 6.1 fusion.106
  168.6 29.3 %fusion.23 = (u8[1024,3072]{1,0:T(8,128)(4,1)}, u8[1024,3072]{1,0:T(8,128)(4,1)}, f32[2,1024,3072]{2,1,0:T(8,128)}) fusion(f32[3072]{0:T(1024)} %param.49, bf16[768,3072]{1,0:T(8,128)(2,1)} %param.48, f32[2,1024,768]{1,2,0:T(8,128)} %copy-done.9, f32[768]{0:T(1024)} %param.47, f32[768]{0:T(1024)} %param.46, f32[2,1024]{1,0:T(2,128)S(1)} %fusion.88, ...), kind=kOutput, calls=%fused_computation.66 | convolution fusion | flops 9753329664 | bytes 42502144 | tf_op jit(solution)/shard_map/bpd,de->bpe/dot_general | solution.py:34
  197.9 62.9 %multiply_convert_fusion = (bf16[2,1024,3072]{2,1,0:T(8,128)(2,1)}, f32[2,1024,3072]{2,1,0:T(8,128)}) fusion(f32[2,1024,3072]{2,1,0:T(8,128)} %get-tuple-element.190, f32[3072]{0:T(1024)} %param.49, u8[1024,3072]{1,0:T(8,128)(4,1)} %get-tuple-element.121, u8[1024,3072]{1,0:T(8,128)(4,1)} %get-tuple-element.120), kind=kLoop, calls=%fused_computation.8 | loop fusion | flops 446693376 | bytes 69218304 | tf_op jit(solution)/shard_map/convert_element_type | solution.py:521
  260.8 29.3 %fusion.110 = (bf16[3072]{0:T(1024)(128)(2,1)}, bf16[2,1024,3072]{2,1,0:T(8,128)(2,1)}) fusion(f32[2,1024,3072]{2,1,0:T(8,128)} %get-tuple-element.133, bf16[3072,768]{1,0:T(8,128)(2,1)} %param.50, bf16[2,512,768]{1,2,0:T(8,128)(2,1)} %bitcast.16, bf16[2,512,768]{1,2,0:T(8,128)(2,1)} %get-tuple-element.150, f32[2,1024,3072]{2,1,0:T(8,128)} %get-tuple-element.190, ...), kind=kOutput, calls=%fused_computation.293 | convolution fusion | flops 9770628096 | bytes 70797312 | tf_op jit(solution)/shard_map/bpe,de->bpd/dot_general | solution.py:38
  290.2 16.4 %bitcast_convert_fusion.1 = bf16[768,3072]{1,0:T(8,128)(2,1)} fusion(bf16[2,1024,3072]{2,1,0:T(8,128)(2,1)} %get-tuple-element.198, f32[2,1024,768]{1,2,0:T(8,128)} %copy-done.9, f32[768]{0:T(1024)} %param.47, f32[768]{0:T(1024)} %param.46, f32[2,1024]{1,0:T(2,128)S(1)} %fusion.88, f32[2,1024]{1,0:T(2,128)S(1)} %broadcast_multiply_fusion), kind=kOutput, calls=%fused_computation.34 | convolution fusion | flops 9673900032 | bytes 23615488 | tf_op jit(solution)/shard_map/bpd,bpe->de/dot_general | solution.py:42
  306.6 12.4 %fusion.109 = (bf16[768]{0:T(1024)(128)(2,1)}, f32[2,1024,768]{2,1,0:T(8,128)}) fusion(bf16[768,3072]{1,0:T(8,128)(2,1)S(1)} %copy-done.64, bf16[2,1024,3072]{2,1,0:T(8,128)(2,1)S(1)} %copy-done.80), kind=kOutput, calls=%fused_computation.292 | convolution fusion | flops 9665248256 | bytes 23594496 | tf_op jit(solution)/shard_map/bpe,de->bpd/dot_general | solution.py:38
  319.0 6.6 copy.151
  325.6 6.9 multiply_reduce_fusion
  332.5 4.0 fusion.99
  336.6 3.9 fusion.47
  341.2 3.7 bitcast_convert_fusion.4
  344.9 4.1 convolution_convert_fusion.1.g_ref
  348.9 58.3 %attend_back.2 = (bf16[2,1024,768]{2,1,0:T(8,128)(2,1)}, bf16[2,1024,768]{2,1,0:T(8,128)(2,1)}, bf16[2,1024,768]{2,1,0:T(8,128)(2,1)}) custom-call(bf16[2,1024,768]{2,1,0:T(8,128)(2,1)} %multiply_convert_fusion.3.q_ref, bf16[2,1024,1536]{2,1,0:T(8,128)(2,1)} %add_convert_fusion.k_ref.v_ref, bf16[2,1024,1536]{2,1,0:T(8,128)(2,1)} %add_convert_fusion.k_ref.v_ref, ...), custom_call_target="tpu_custom_call" | custom-call | flops 51539607552 | bytes 50331648 | tf_op jit(solution)/shard_map/attend_back/pallas_call | solution.py:399
  407.3 5.7 bitcast_convert_fusion.5
  413.0 5.1 fusion.108
  418.1 6.6 copy.153
  424.7 5.7 multiply_reduce_fusion.2
  431.1 6.2 multiply_reduce_fusion.1
  437.4 7.5 fusion.98
  444.8 7.6 bitcast_convert_fusion.6
  452.4 4.3 convolution_convert_fusion.g_ref
  460.0 8.1 bitcast_convert_fusion.3
  468.1 7.0 fusion.41
  475.1 58.5 %attend_back.3 = (bf16[2,1024,768]{2,1,0:T(8,128)(2,1)}, bf16[2,1024,768]{2,1,0:T(8,128)(2,1)}, bf16[2,1024,768]{2,1,0:T(8,128)(2,1)}) custom-call(bf16[2,1024,2304]{2,1,0:T(8,128)(2,1)} %multiply_convert_fusion.1.q_ref.k_ref.v_ref, bf16[2,1024,2304]{2,1,0:T(8,128)(2,1)} %multiply_convert_fusion.1.q_ref.k_ref.v_ref, ...), custom_call_target="tpu_custom_call" | custom-call | flops 51539607552 | bytes 50331648 | tf_op jit(solution)/shard_map/attend_back/pallas_call | solution.py:399
  538.8 10.6 %bitcast_convert_fusion.2 = bf16[768,2304]{1,0:T(8,128)(2,1)} fusion(bf16[2,1024,2304]{2,1,0:T(8,128)(2,1)S(1)} %get-tuple-element.154, f32[768]{0:T(1024)S(1)} %copy-done.77, f32[768]{0:T(1024)S(1)} %copy-done.52, f32[2,1024]{1,0:T(2,128)S(1)} %copy-done.40, f32[2,1024]{1,0:T(2,128)S(1)} %copy-done.36, bf16[2,512,768]{1,2,0:T(8,128)(2,1)} %bitcast.1, ...), kind=kOutput, calls=%fused_computation.37 | convolution fusion | flops 7263682560 | bytes 16144384 | tf_op jit(solution)/shard_map/bpd,bpe->de/dot_general | solution.py:42
  549.3 10.0 %fusion.107 = (bf16[768]{0:T(1024)(128)(2,1)}, f32[2,1024,768]{2,1,0:T(8,128)}) fusion(bf16[2,1024,2304]{2,1,0:T(8,128)(2,1)S(1)} %get-tuple-element.154, bf16[768,2304]{1,0:T(8,128)(2,1)S(1)} %copy-done), kind=kOutput, calls=%fused_computation.290 | convolution fusion | flops 7249329152 | bytes 19269120 | tf_op jit(solution)/shard_map/bpe,de->bpd/dot_general | solution.py:38
  568.6 15.5 %bitcast_convert_fusion = bf16[3072,768]{1,0:T(8,128)(2,1)} fusion(bf16[2,1024,3072]{2,1,0:T(8,128)(2,1)} %get-tuple-element.132, bf16[2,512,768]{1,2,0:T(8,128)(2,1)} %bitcast.16, bf16[2,512,768]{1,2,0:T(8,128)(2,1)} %get-tuple-element.150), kind=kOutput, calls=%fused_computation.33 | convolution fusion | flops 9672327168 | bytes 20447232 | tf_op jit(solution)/shard_map/bpd,bpe->de/dot_general | solution.py:42
  584.1 16.5 %add_convert_fusion.1 = bf16[2,1024,768]{1,2,0:T(8,128)(2,1)} fusion(f32[2,1024,768]{1,2,0:T(8,128)} %copy-done.9, f32[768]{0:T(1024)S(1)} %copy-done.78, bf16[2,1024,3072]{2,1,0:T(8,128)(2,1)} %get-tuple-element.132, bf16[3072,768]{1,0:T(8,128)(2,1)} %param.50), kind=kOutput, calls=%fused_computation.58 | convolution fusion | flops 9668395008 | bytes 26741760 | tf_op jit(solution)/shard_map/bpd,de->bpe/dot_general | solution.py:34
  605.4 4.3 constant_dynamic-slice_fusion.1
  628.9 4.0 constant_dynamic-slice_fusion.13
  634.2 6.8 copy.155
  641.0 4.5 fusion.16
  647.0 5.0 fusion.14
  662.0 3.6 collective-permute-done.7
  665.8 6.3 add_add_fusion.3
  686.0 6.3 collective-permute-done.32
  694.2 4.4 collective-permute-done.22
  722.7 4.3 collective-permute-done.34
  728.2 5.6 collective-permute-done.24
  733.9 5.4 collective-permute-done.19
  758.7 3.6 convert_select_fusion.1
  764.3 4.6 copy.182
  768.9 6.2 maximum_bitcast_fusion.1
  775.1 6.8 copy.184
  781.9 8.2 collective-permute-done.4
  796.8 6.6 copy.183
  807.7 5.9 collective-permute-done.28
  816.9 5.3 collective-permute-done.29
  831.3 6.5 collective-permute-done.12
  840.6 5.8 collective-permute-done.13
  846.5 16.5 %collective-permute-done.42 = bf16[2,2,192,768]{3,2,0,1:T(8,128)(2,1)S(1)} collective-permute-done((bf16[2,2,192,768]{3,2,0,1:T(8,128)(2,1)S(1)}, bf16[2,2,192,768]{3,2,0,1:T(8,128)(2,1)S(1)}, u32[]{:S(2)}, u32[]{:S(2)}) %collective-permute-start.42) | collective-permute-done | bytes 1179680 | tf_op jit(solution)/shard_map/ppermute | solution.py:435
  865.2 21.0 %collective-permute-done.37 = bf16[2,2,48,3072]{3,2,0,1:T(8,128)(2,1)S(1)} collective-permute-done((bf16[2,2,48,3072]{3,2,0,1:T(8,128)(2,1)S(1)}, bf16[2,2,48,3072]{3,2,0,1:T(8,128)(2,1)S(1)}, u32[]{:S(2)}, u32[]{:S(2)}) %collective-permute-start.37) | collective-permute-done | bytes 1179680 | tf_op jit(solution)/shard_map/ppermute | solution.py:435
  891.4 19.6 %collective-permute-done.38 = bf16[2,48,3072]{2,1,0:T(8,128)(2,1)S(1)} collective-permute-done((bf16[2,48,3072]{2,1,0:T(8,128)(2,1)S(1)}, bf16[2,48,3072]{2,1,0:T(8,128)(2,1)S(1)}, u32[]{:S(2)}, u32[]{:S(2)}) %collective-permute-start.38) | collective-permute-done | bytes 589856 | tf_op jit(solution)/shard_map/ppermute | solution.py:435
  913.5 10.9 %collective-permute-done.39 = bf16[48,3072]{1,0:T(8,128)(2,1)S(1)} collective-permute-done((bf16[48,3072]{1,0:T(8,128)(2,1)S(1)}, bf16[48,3072]{1,0:T(8,128)(2,1)S(1)}, u32[]{:S(2)}, u32[]{:S(2)}) %collective-permute-start.39) | collective-permute-done | bytes 294944 | tf_op jit(solution)/shard_map/ppermute | solution.py:435
  928.0 5.5 collective-permute-done.40
  (400 shorter events, 192.7 us)
Async XLA Ops:
  0.7 50.9 %copy-start = (bf16[768,2304]{1,0:T(8,128)(2,1)S(1)}, bf16[768,2304]{1,0:T(8,128)(2,1)}, u32[]{:S(2)}) copy-start(bf16[768,2304]{1,0:T(8,128)(2,1)} %param.33) | copy-start | bytes 10616836
  7.2 38.5 %collective-permute-start = (bf16[2,1,512,768]{2,3,0,1:T(8,128)(2,1)}, bf16[2,1,512,768]{2,3,0,1:T(8,128)(2,1)}, u32[]{:S(2)}, u32[]{:S(2)}) collective-permute-start(bf16[2,1,512,768]{2,3,0,1:T(8,128)(2,1)} %copy.211), channel_id=1, source_target_pairs={{0,1},{1,0},{2,3},{3,2},{4,5},{5,4},{6,7},{7,6},{8,9},{9,8},{10,11... | collective-permute-start | bytes 4718600 | tf_op jit(solution)/shard_map/ppermute | solution.py:477
  12.8 105.6 %collective-permute-start.1 = (bf16[2,1,512,768]{3,2,0,1:T(8,128)(2,1)}, bf16[2,1,512,768]{3,2,0,1:T(8,128)(2,1)}, u32[]{:S(2)}, u32[]{:S(2)}) collective-permute-start(bf16[2,1,512,768]{3,2,0,1:T(8,128)(2,1)} %constant_dynamic-slice_fusion.22), channel_id=1, source_target_pairs={{0,1},{1,0},{2,3},{3,2},{4,5},{5,4},{6,7},{7,6},{8,9},{9,8},{10,11... | collective-permute-start | bytes 4718600 | tf_op jit(solution)/shard_map/ppermute | solution.py:477
  22.5 238.4 %collective-permute-start.3 = (bf16[2,1,512,768]{2,3,0,1:T(8,128)(2,1)}, bf16[2,1,512,768]{2,3,0,1:T(8,128)(2,1)}, u32[]{:S(2)}, u32[]{:S(2)}) collective-permute-start(bf16[2,1,512,768]{2,3,0,1:T(8,128)(2,1)} %get-tuple-element.149), channel_id=1, source_target_pairs={{0,1},{1,0},{2,3},{3,2},{4,5},{5,4},{6,7},{7,6},{8,9},{9,8},{10,11... | collective-permute-start | bytes 4718600 | tf_op jit(solution)/shard_map/ppermute | solution.py:477
  24.5 27.1 %copy-start.51 = (f32[768]{0:T(1024)S(1)}, f32[768]{0:T(1024)}, u32[]{:S(2)}) copy-start(f32[768]{0:T(1024)} %param.31) | copy-start | bytes 9220
  27.1 21.0 %copy-start.5 = (bf16[2,1,512,768]{2,3,0,1:T(8,128)(2,1)S(1)}, bf16[2,1,512,768]{2,3,0,1:T(8,128)(2,1)}, u32[]{:S(2)}) copy-start(bf16[2,1,512,768]{2,3,0,1:T(8,128)(2,1)} %copy.140) | copy-start | bytes 4718596
  27.1 24.4 %copy-start.76 = (f32[768]{0:T(1024)S(1)}, f32[768]{0:T(1024)}, u32[]{:S(2)}) copy-start(f32[768]{0:T(1024)} %param.32) | copy-start | bytes 9220
  30.1 88.3 %copy-start.30 = (bf16[2,512,768]{2,1,0:T(8,128)(2,1)}, bf16[2,512,768]{2,1,0:T(8,128)(2,1)S(1)}, u32[]{:S(2)}) copy-start(bf16[2,512,768]{2,1,0:T(8,128)(2,1)S(1)} %dynamic-slice_bitcast_fusion) | copy-start | bytes 4718596
  64.6 40.7 %copy-start.71 = (bf16[768,768]{1,0:T(8,128)(2,1)S(1)}, bf16[768,768]{1,0:T(8,128)(2,1)}, u32[]{:S(2)}) copy-start(bf16[768,768]{1,0:T(8,128)(2,1)} %param.36) | copy-start | bytes 3538948
  64.6 40.7 %copy-start.73 = (f32[768]{0:T(1024)S(1)}, f32[768]{0:T(1024)}, u32[]{:S(2)}) copy-start(f32[768]{0:T(1024)} %param.37) | copy-start | bytes 9220
  126.8 31.7 %copy-start.67 = (bf16[768,768]{1,0:T(8,128)(2,1)S(1)}, bf16[768,768]{1,0:T(8,128)(2,1)}, u32[]{:S(2)}) copy-start(bf16[768,768]{1,0:T(8,128)(2,1)} %param.44) | copy-start | bytes 3538948
  126.8 31.7 %copy-start.75 = (f32[768]{0:T(1024)S(1)}, f32[768]{0:T(1024)}, u32[]{:S(2)}) copy-start(f32[768]{0:T(1024)} %param.45) | copy-start | bytes 9220
  290.2 16.4 %copy-start.64 = (bf16[768,3072]{1,0:T(8,128)(2,1)S(1)}, bf16[768,3072]{1,0:T(8,128)(2,1)}, u32[]{:S(2)}) copy-start(bf16[768,3072]{1,0:T(8,128)(2,1)} %param.48) | copy-start | bytes 14155780
  290.2 16.4 %copy-start.80 = (bf16[2,1024,3072]{2,1,0:T(8,128)(2,1)S(1)}, bf16[2,1024,3072]{2,1,0:T(8,128)(2,1)}, u32[]{:S(2)}) copy-start(bf16[2,1024,3072]{2,1,0:T(8,128)(2,1)} %get-tuple-element.198) | copy-start | bytes 37748740
  348.9 58.3 %copy-start.26 = (bf16[2,1024,768]{1,2,0:T(8,128)(2,1)S(1)}, bf16[2,1024,768]{1,2,0:T(8,128)(2,1)}, u32[]{:S(2)}) copy-start(bf16[2,1024,768]{1,2,0:T(8,128)(2,1)} %copy-done.25) | copy-start | bytes 9437188
  424.7 12.6 %slice-start = ((s8[6291456]{0:T(1024)(128)(4,1)}), s8[2097152]{0:T(1024)(128)(4,1)S(1)}, s32[]{:S(2)}) async-start(s8[6291456]{0:T(1024)(128)(4,1)} %bitcast.295), calls=%async_computation | async-start | bytes 4194304
  549.3 15.2 %copy-start.57 = (bf16[768]{0:T(1024)(128)(2,1)S(1)}, bf16[768]{0:T(1024)(128)(2,1)}, u32[]{:S(2)}) copy-start(bf16[768]{0:T(1024)(128)(2,1)} %get-tuple-element.148) | copy-start | bytes 4612
  568.6 15.5 %copy-start.78 = (f32[768]{0:T(1024)S(1)}, f32[768]{0:T(1024)}, u32[]{:S(2)}) copy-start(f32[768]{0:T(1024)} %param.51) | copy-start | bytes 9220
  603.3 152.7 %collective-permute-start.2 = (bf16[2,512,768]{1,2,0:T(8,128)(2,1)}, bf16[2,512,768]{1,2,0:T(8,128)(2,1)}, u32[]{:S(2)}, u32[]{:S(2)}) collective-permute-start(bf16[2,512,768]{1,2,0:T(8,128)(2,1)} %slice.83), channel_id=1, source_target_pairs={{0,1},{1,0},{2,3},{3,2},{4,5},{5,4},{6,7},{7,6},{8,9},{9,8},{10,11... | collective-permute-start | bytes 4718600 | tf_op jit(solution)/shard_map/ppermute | solution.py:481
  611.2 212.8 %collective-permute-start.41 = (bf16[2,2,2,192,768]{4,3,0,1,2:T(8,128)(2,1)}, bf16[2,2,2,192,768]{4,3,0,1,2:T(8,128)(2,1)}, u32[]{:S(2)}, u32[]{:S(2)}) collective-permute-start(bf16[2,2,2,192,768]{4,3,0,1,2:T(8,128)(2,1)} %bitcast.284), channel_id=1, source_target_pairs={{0,2},{2,0},{4,6},{6,4},{8,10},{10,8},{12,14},{14,12},{16,18},{18,... | collective-permute-start | bytes 7077896 | tf_op jit(solution)/shard_map/ppermute | solution.py:435
  656.0 5.8 collective-permute-start.6
  661.2 20.4 %collective-permute-start.31 = (bf16[2,2,2,48,768]{4,3,0,1,2:T(8,128)(2,1)S(1)}, bf16[2,2,2,48,768]{4,3,0,1,2:T(8,128)(2,1)S(1)}, u32[]{:S(2)}, u32[]{:S(2)}) collective-permute-start(bf16[2,2,2,48,768]{4,3,0,1,2:T(8,128)(2,1)S(1)} %bitcast.321), channel_id=1, source_target_pairs={{0,2},{2,0},{4,6},{6,4},{8,10},{10,8},{12,14},{14,12},{16,18},{18,... | collective-permute-start | bytes 1769480 | tf_op jit(solution)/shard_map/ppermute | solution.py:435
  661.3 21.1 %collective-permute-start.21 = (bf16[2,2,2,48,768]{4,3,0,1,2:T(8,128)(2,1)S(1)}, bf16[2,2,2,48,768]{4,3,0,1,2:T(8,128)(2,1)S(1)}, u32[]{:S(2)}, u32[]{:S(2)}) collective-permute-start(bf16[2,2,2,48,768]{4,3,0,1,2:T(8,128)(2,1)S(1)} %bitcast.320), channel_id=1, source_target_pairs={{0,2},{2,0},{4,6},{6,4},{8,10},{10,8},{12,14},{14,12},{16,18},{18,... | collective-permute-start | bytes 1769480 | tf_op jit(solution)/shard_map/ppermute | solution.py:435
  661.9 3.7 collective-permute-start.7
  665.7 6.5 collective-permute-start.8
  672.2 4.5 collective-permute-start.9
  676.8 3.6 collective-permute-start.10
  680.3 72.6 %collective-permute-start.26 = (bf16[2,2,2,48,1536]{4,3,0,1,2:T(8,128)(2,1)S(1)}, bf16[2,2,2,48,1536]{4,3,0,1,2:T(8,128)(2,1)S(1)}, u32[]{:S(2)}, u32[]{:S(2)}) collective-permute-start(bf16[2,2,2,48,1536]{4,3,0,1,2:T(8,128)(2,1)S(1)} %bitcast.317), channel_id=1, source_target_pairs={{0,2},{2,0},{4,6},{6,4},{8,10},{10,8},{12,14},{14,12},{16,18},{18,... | collective-permute-start | bytes 3538952 | tf_op jit(solution)/shard_map/ppermute | solution.py:435
  681.6 2.8 collective-permute-start.16
  682.4 9.9 %collective-permute-start.32 = (bf16[2,2,48,768]{3,2,0,1:T(8,128)(2,1)S(1)}, bf16[2,2,48,768]{3,2,0,1:T(8,128)(2,1)S(1)}, u32[]{:S(2)}, u32[]{:S(2)}) collective-permute-start(bf16[2,2,48,768]{3,2,0,1:T(8,128)(2,1)S(1)} %dynamic-slice_bitcast_fusion.11), channel_id=1, source_target_pairs={{0,4},{2,6},{4,0},{6,2},{8,12},{10,14},{12,8},{14,10},{16,20},{18,... | collective-permute-start | bytes 884744 | tf_op jit(solution)/shard_map/ppermute | solution.py:435
  684.4 14.2 %collective-permute-start.22 = (bf16[2,2,48,768]{3,2,0,1:T(8,128)(2,1)S(1)}, bf16[2,2,48,768]{3,2,0,1:T(8,128)(2,1)S(1)}, u32[]{:S(2)}, u32[]{:S(2)}) collective-permute-start(bf16[2,2,48,768]{3,2,0,1:T(8,128)(2,1)S(1)} %dynamic-slice_bitcast_fusion.13), channel_id=1, source_target_pairs={{0,4},{2,6},{4,0},{6,2},{8,12},{10,14},{12,8},{14,10},{16,20},{18,... | collective-permute-start | bytes 884744 | tf_op jit(solution)/shard_map/ppermute | solution.py:435
  685.9 70.6 %copy-start.24 = (bf16[2,1024,768]{1,2,0:T(8,128)(2,1)S(1)}, bf16[2,1024,768]{1,2,0:T(8,128)(2,1)}, u32[]{:S(2)}) copy-start(bf16[2,1024,768]{1,2,0:T(8,128)(2,1)} %add_convert_fusion.1) | copy-start | bytes 9437188
  692.3 11.7 %collective-permute-start.17 = (bf16[2,2,48,768]{3,2,0,1:T(8,128)(2,1)S(1)}, bf16[2,2,48,768]{3,2,0,1:T(8,128)(2,1)S(1)}, u32[]{:S(2)}, u32[]{:S(2)}) collective-permute-start(bf16[2,2,48,768]{3,2,0,1:T(8,128)(2,1)S(1)} %dynamic-slice_bitcast_fusion.14), channel_id=1, source_target_pairs={{0,4},{2,6},{4,0},{6,2},{8,12},{10,14},{12,8},{14,10},{16,20},{18,... | collective-permute-start | bytes 884744 | tf_op jit(solution)/shard_map/ppermute | solution.py:435
  698.6 59.6 %collective-permute-start.5 = (bf16[2,512,768]{1,2,0:T(8,128)(2,1)S(1)}, bf16[2,512,768]{1,2,0:T(8,128)(2,1)S(1)}, u32[]{:S(2)}, u32[]{:S(2)}) collective-permute-start(bf16[2,512,768]{1,2,0:T(8,128)(2,1)S(1)} %slice.96), channel_id=1, source_target_pairs={{0,1},{1,0},{2,3},{3,2},{4,5},{5,4},{6,7},{7,6},{8,9},{9,8},{10,11... | collective-permute-start | bytes 4718600 | tf_op jit(solution)/shard_map/ppermute | solution.py:481
  704.1 5.1 collective-permute-start.33
  709.2 5.1 collective-permute-start.23
  714.3 5.1 collective-permute-start.18
  719.5 7.5 collective-permute-start.34
  727.0 6.8 collective-permute-start.24
  733.8 5.4 collective-permute-start.19
  739.2 4.4 collective-permute-start.35
  743.6 4.4 collective-permute-start.25
  747.9 4.4 collective-permute-start.20
  752.3 74.6 %collective-permute-start.36 = (bf16[2,2,2,48,3072]{4,3,0,1,2:T(8,128)(2,1)}, bf16[2,2,2,48,3072]{4,3,0,1,2:T(8,128)(2,1)}, u32[]{:S(2)}, u32[]{:S(2)}) collective-permute-start(bf16[2,2,2,48,3072]{4,3,0,1,2:T(8,128)(2,1)} %bitcast.285), channel_id=1, source_target_pairs={{0,2},{2,0},{4,6},{6,4},{8,10},{10,8},{12,14},{14,12},{16,18},{18,... | collective-permute-start | bytes 7077896 | tf_op jit(solution)/shard_map/ppermute | solution.py:435
  753.0 37.1 %collective-permute-start.4 = (bf16[2,512,768]{1,2,0:T(8,128)(2,1)}, bf16[2,512,768]{1,2,0:T(8,128)(2,1)}, u32[]{:S(2)}, u32[]{:S(2)}) collective-permute-start(bf16[2,512,768]{1,2,0:T(8,128)(2,1)} %slice.97), channel_id=1, source_target_pairs={{0,1},{1,0},{2,3},{3,2},{4,5},{5,4},{6,7},{7,6},{8,9},{9,8},{10,11... | collective-permute-start | bytes 4718600 | tf_op jit(solution)/shard_map/ppermute | solution.py:481
  756.3 49.0 %collective-permute-start.11 = (bf16[2,2,2,48,2304]{4,3,0,1,2:T(8,128)(2,1)}, bf16[2,2,2,48,2304]{4,3,0,1,2:T(8,128)(2,1)}, u32[]{:S(2)}, u32[]{:S(2)}) collective-permute-start(bf16[2,2,2,48,2304]{4,3,0,1,2:T(8,128)(2,1)} %bitcast.286), channel_id=1, source_target_pairs={{0,2},{2,0},{4,6},{6,4},{8,10},{10,8},{12,14},{14,12},{16,18},{18,... | collective-permute-start | bytes 5308424 | tf_op jit(solution)/shard_map/ppermute | solution.py:435
  758.3 45.1 %collective-permute-start.27 = (bf16[2,2,48,1536]{3,2,0,1:T(8,128)(2,1)}, bf16[2,2,48,1536]{3,2,0,1:T(8,128)(2,1)}, u32[]{:S(2)}, u32[]{:S(2)}) collective-permute-start(bf16[2,2,48,1536]{3,2,0,1:T(8,128)(2,1)} %dynamic-slice_bitcast_fusion.7), channel_id=1, source_target_pairs={{0,4},{2,6},{4,0},{6,2},{8,12},{10,14},{12,8},{14,10},{16,20},{18,... | collective-permute-start | bytes 1769480 | tf_op jit(solution)/shard_map/ppermute | solution.py:435
  803.4 20.7 %copy-start.16 = (bf16[2,2,2,1,192,768]{5,4,3,2,1,0:T(8,128)(2,1)S(1)}, bf16[2,2,2,1,192,768]{5,4,3,2,1,0:T(8,128)(2,1)}, u32[]{:S(2)}) copy-start(bf16[2,2,2,1,192,768]{5,4,3,2,1,0:T(8,128)(2,1)} %get-tuple-element.140) | copy-start | bytes 7077892
  805.0 8.7 collective-permute-start.28
  807.7 19.1 %copy-start.15 = (bf16[2,2,2,1,48,3072]{5,4,3,2,1,0:T(8,128)(2,1)S(1)}, bf16[2,2,2,1,48,3072]{5,4,3,2,1,0:T(8,128)(2,1)}, u32[]{:S(2)}) copy-start(bf16[2,2,2,1,48,3072]{5,4,3,2,1,0:T(8,128)(2,1)} %get-tuple-element.142) | copy-start | bytes 7077892
  813.8 8.4 collective-permute-start.29
  815.1 22.6 %collective-permute-start.12 = (bf16[2,2,48,2304]{3,2,0,1:T(8,128)(2,1)S(1)}, bf16[2,2,48,2304]{3,2,0,1:T(8,128)(2,1)S(1)}, u32[]{:S(2)}, u32[]{:S(2)}) collective-permute-start(bf16[2,2,48,2304]{3,2,0,1:T(8,128)(2,1)S(1)} %dynamic-slice_bitcast_fusion.4), channel_id=1, source_target_pairs={{0,4},{2,6},{4,0},{6,2},{8,12},{10,14},{12,8},{14,10},{16,20},{18,... | collective-permute-start | bytes 2654216 | tf_op jit(solution)/shard_map/ppermute | solution.py:435
  822.2 17.6 %collective-permute-start.30 = (bf16[48,1536]{1,0:T(8,128)(2,1)S(1)}, bf16[48,1536]{1,0:T(8,128)(2,1)S(1)}, u32[]{:S(2)}, u32[]{:S(2)}) collective-permute-start(bf16[48,1536]{1,0:T(8,128)(2,1)S(1)} %fusion.74), channel_id=1, source_target_pairs={{0,1},{1,0},{2,3},{3,2},{4,5},{5,4},{6,7},{7,6},{8,9},{9,8},{10,11... | collective-permute-start | bytes 442376 | tf_op jit(solution)/shard_map/ppermute | solution.py:437
  826.4 36.6 %collective-permute-start.42 = (bf16[2,2,192,768]{3,2,0,1:T(8,128)(2,1)S(1)}, bf16[2,2,192,768]{3,2,0,1:T(8,128)(2,1)S(1)}, u32[]{:S(2)}, u32[]{:S(2)}) collective-permute-start(bf16[2,2,192,768]{3,2,0,1:T(8,128)(2,1)S(1)} %dynamic-slice_bitcast_fusion.2), channel_id=1, source_target_pairs={{0,4},{2,6},{4,0},{6,2},{8,12},{10,14},{12,8},{14,10},{16,20},{18,... | collective-permute-start | bytes 3538952 | tf_op jit(solution)/shard_map/ppermute | solution.py:435
  829.6 56.6 %collective-permute-start.37 = (bf16[2,2,48,3072]{3,2,0,1:T(8,128)(2,1)S(1)}, bf16[2,2,48,3072]{3,2,0,1:T(8,128)(2,1)S(1)}, u32[]{:S(2)}, u32[]{:S(2)}) collective-permute-start(bf16[2,2,48,3072]{3,2,0,1:T(8,128)(2,1)S(1)} %dynamic-slice_bitcast_fusion.3), channel_id=1, source_target_pairs={{0,4},{2,6},{4,0},{6,2},{8,12},{10,14},{12,8},{14,10},{16,20},{18,... | collective-permute-start | bytes 3538952 | tf_op jit(solution)/shard_map/ppermute | solution.py:435
  838.0 8.4 collective-permute-start.13
  863.4 25.1 %collective-permute-start.43 = (bf16[2,192,768]{2,1,0:T(8,128)(2,1)S(1)}, bf16[2,192,768]{2,1,0:T(8,128)(2,1)S(1)}, u32[]{:S(2)}, u32[]{:S(2)}) collective-permute-start(bf16[2,192,768]{2,1,0:T(8,128)(2,1)S(1)} %dynamic-slice_bitcast_fusion.5), channel_id=1, source_target_pairs={{0,8},{2,10},{4,12},{6,14},{8,0},{10,2},{12,4},{14,6},{16,24},{18,... | collective-permute-start | bytes 1769480 | tf_op jit(solution)/shard_map/ppermute | solution.py:435
  886.6 24.3 %collective-permute-start.38 = (bf16[2,48,3072]{2,1,0:T(8,128)(2,1)S(1)}, bf16[2,48,3072]{2,1,0:T(8,128)(2,1)S(1)}, u32[]{:S(2)}, u32[]{:S(2)}) collective-permute-start(bf16[2,48,3072]{2,1,0:T(8,128)(2,1)S(1)} %dynamic-slice_bitcast_fusion.6), channel_id=1, source_target_pairs={{0,8},{2,10},{4,12},{6,14},{8,0},{10,2},{12,4},{14,6},{16,24},{18,... | collective-permute-start | bytes 1769480 | tf_op jit(solution)/shard_map/ppermute | solution.py:435
  888.1 23.1 %collective-permute-start.14 = (bf16[48,2304]{1,0:T(8,128)(2,1)S(1)}, bf16[48,2304]{1,0:T(8,128)(2,1)S(1)}, u32[]{:S(2)}, u32[]{:S(2)}) collective-permute-start(bf16[48,2304]{1,0:T(8,128)(2,1)S(1)} %dynamic-slice_bitcast_fusion.15), channel_id=1, source_target_pairs={{0,16},{2,18},{4,20},{6,22},{8,24},{10,26},{12,28},{14,30},{16,0},... | collective-permute-start | bytes 663560 | tf_op jit(solution)/shard_map/ppermute | solution.py:435
  888.7 24.4 %collective-permute-start.44 = (bf16[192,768]{1,0:T(8,128)(2,1)S(1)}, bf16[192,768]{1,0:T(8,128)(2,1)S(1)}, u32[]{:S(2)}, u32[]{:S(2)}) collective-permute-start(bf16[192,768]{1,0:T(8,128)(2,1)S(1)} %dynamic-slice_bitcast_fusion.9), channel_id=1, source_target_pairs={{0,16},{2,18},{4,20},{6,22},{8,24},{10,26},{12,28},{14,30},{16,0},... | collective-permute-start | bytes 884744 | tf_op jit(solution)/shard_map/ppermute | solution.py:435
  911.1 13.3 %collective-permute-start.39 = (bf16[48,3072]{1,0:T(8,128)(2,1)S(1)}, bf16[48,3072]{1,0:T(8,128)(2,1)S(1)}, u32[]{:S(2)}, u32[]{:S(2)}) collective-permute-start(bf16[48,3072]{1,0:T(8,128)(2,1)S(1)} %dynamic-slice_bitcast_fusion.10), channel_id=1, source_target_pairs={{0,16},{2,18},{4,20},{6,22},{8,24},{10,26},{12,28},{14,30},{16,0},... | collective-permute-start | bytes 884744 | tf_op jit(solution)/shard_map/ppermute | solution.py:435
  911.3 15.1 %collective-permute-start.15 = (bf16[48,2304]{1,0:T(8,128)(2,1)S(1)}, bf16[48,2304]{1,0:T(8,128)(2,1)S(1)}, u32[]{:S(2)}, u32[]{:S(2)}) collective-permute-start(bf16[48,2304]{1,0:T(8,128)(2,1)S(1)} %fusion.72), channel_id=1, source_target_pairs={{0,1},{1,0},{2,3},{3,2},{4,5},{5,4},{6,7},{7,6},{8,9},{9,8},{10,11... | collective-permute-start | bytes 663560 | tf_op jit(solution)/shard_map/ppermute | solution.py:437
  913.2 14.0 %collective-permute-start.45 = (bf16[192,768]{1,0:T(8,128)(2,1)S(1)}, bf16[192,768]{1,0:T(8,128)(2,1)S(1)}, u32[]{:S(2)}, u32[]{:S(2)}) collective-permute-start(bf16[192,768]{1,0:T(8,128)(2,1)S(1)} %fusion.66), channel_id=1, source_target_pairs={{0,1},{1,0},{2,3},{3,2},{4,5},{5,4},{6,7},{7,6},{8,9},{9,8},{10,11... | collective-permute-start | bytes 884744 | tf_op jit(solution)/shard_map/ppermute | solution.py:437
  924.5 9.0 collective-permute-start.40
  (71 other events, 381.4 us)

commit v2 on v1

--- a/solution.py
+++ b/solution.py
@@ -388,54 +388,279 @@
     dv_ref[0] = value_sum.astype(jnp.bfloat16)
 
 
-def attend_back(queries, keys, values, offsets, mixed, upstream, raised, inverse):
+def attend_back(first, pairs_now, previous, queries, keys, values, offsets, *rest):
     count, length = queries.shape[:2]
     pairs = HEADS * HEAD // 128
     width = HEADS * HEAD
 
     def spec(offset):
-        return pl.BlockSpec((1, length, 128), lambda s, p: (s, 0, offset * pairs + p))
-
+        return pl.BlockSpec((1, length, 128), lambda s, p: (s, 0, offset * pairs + first + p))
+
+    kernel = attend_back_kernel
+    aliases = {}
+    if previous:
+        kernel = lambda *refs: attend_back_kernel(*refs[3:])
+        aliases = {0: 0, 1: 1, 2: 2}
     return pl.pallas_call(
-        attend_back_kernel,
-        grid=(count, pairs),
-        in_specs=[spec(offset) for offset in offsets]
+        kernel,
+        grid=(count, pairs_now),
+        in_specs=[pl.BlockSpec(memory_space=pl.ANY)] * len(previous)
+        + [spec(offset) for offset in offsets]
         + [
             spec(0),
             spec(0),
-            pl.BlockSpec((1, 2, length, length), lambda s, p: (s, p, 0, 0)),
-            pl.BlockSpec((1, 1, 2, length), lambda s, p: (s, p, 0, 0)),
+            pl.BlockSpec((1, 2, length, length), lambda s, p: (s, first + p, 0, 0)),
+            pl.BlockSpec((1, 1, 2, length), lambda s, p: (s, first + p, 0, 0)),
         ],
         out_specs=[spec(0)] * 3,
         out_shape=[jax.ShapeDtypeStruct((count, length, width), jnp.bfloat16)] * 3,
+        input_output_aliases=aliases,
         compiler_params=pltpu.CompilerParams(vmem_limit_bytes=56 * 2**20),
         cost_estimate=pl.CostEstimate(
-            flops=8 * count * HEADS * length * length * 256,
-            bytes_accessed=count * HEADS * length * length * 2,
+            flops=16 * count * pairs_now * length * length * 256,
+            bytes_accessed=4 * count * pairs_now * length * length,
             transcendentals=0,
         ),
         name="attend_back",
-    )(queries, keys, values, mixed, upstream, raised, inverse)
-
+    )(*previous, queries, keys, values, *rest)
+
+
+def normal_parts(values):
+    center = values - jnp.mean(values, axis=-1, keepdims=True)
+    inverse = lax.rsqrt(jnp.mean(center * center, axis=-1, keepdims=True) + epsilon)
+    return center * inverse, inverse
+
+
+def normal_back(unit, inverse, norm_gain, upstream):
+    inner = upstream * norm_gain
+    shift = jnp.mean(inner, axis=-1, keepdims=True)
+    tilt = jnp.mean(inner * unit, axis=-1, keepdims=True)
+    return inverse * (inner - shift - unit * tilt)
+
+
+def gelu_parts(values):
+    size = jnp.abs(values)
+    ratio = 1.0 / (1.0 + 0.2316418882663604 * size)
+    series = 0.5307027145
+    for weight in (-0.7265760135, 0.7107068705, -0.142248368, 0.127414796):
+        series = series * ratio + weight
+    bell = jnp.exp(-0.5 * values * values)
+    upper = series * ratio * bell
+    chance = jnp.where(values < 0, upper, 1.0 - upper)
+    return values * chance, chance + values * (0.3989422804014327 * bell)
+
+
+def column_sum(values):
+    return jnp.sum(values, axis=0, keepdims=True)
+
+
+def split_rows(core, rows, kept_ref, sent_ref):
+    half = rows.shape[0] // 2
+    low = rows.astype(jnp.bfloat16)
+
+    @pl.when(core == 0)
+    def _():
+        kept_ref[0], sent_ref[0] = low[:half], low[half:]
+
+    @pl.when(core != 0)
+    def _():
+        kept_ref[0], sent_ref[0] = low[half:], low[:half]
+
+
+def feed_kernel(
+    info_ref, x_ref, mixed_ref, dy_ref, wc_ref, wi_ref, wo_ref, vec_ref, bi_ref,
+    out_ref, dx_ref, do_ref, vsum_ref, bsum_ref, ki_ref, si_ref, ko_ref, so_ref, kc_ref, sc_ref,
+    ai_ref, ao_ref, ac_ref, *, steps, chunk,
+):
+    step = pl.program_id(0)
+
+    @pl.when(step == 0)
+    def _():
+        for ref in (vsum_ref, bsum_ref, ai_ref, ao_ref, ac_ref):
+            ref[...] = jnp.zeros_like(ref)
+
+    @pl.when(step < steps)
+    def _():
+        cross_bias, gain, shift, out_bias = (vec_ref[i : i + 1, :] for i in range(4))
+        mixed = mixed_ref[...]
+        x2 = x_ref[...] + contract(mixed, wc_ref[...], 1, 0) + cross_bias
+        unit, inverse = normal_parts(x2)
+        normal = (unit * gain + shift).astype(jnp.bfloat16)
+        normal_turned = normal.T
+        dy = dy_ref[...]
+        dy_turned = dy.T
+        result, upstream = None, None
+        for start in range(0, wi_ref.shape[1], chunk):
+            part = slice(start, start + chunk)
+            hidden = contract(normal, wi_ref[:, part], 1, 0) + bi_ref[:, part]
+            active, slope = gelu_parts(hidden)
+            active = active.astype(jnp.bfloat16)
+            down = contract(active, wo_ref[part, :], 1, 0)
+            result = down if result is None else result + down
+            grads = contract(dy, wo_ref[part, :], 1, 1) * slope
+            bsum_ref[:, part] += column_sum(grads)
+            low = grads.astype(jnp.bfloat16)
+            up = contract(low, wi_ref[:, part], 1, 1)
+            upstream = up if upstream is None else upstream + up
+            ao_ref[:, part] += contract(dy_turned, active, 1, 0)
+            ai_ref[:, part] += contract(normal_turned, low, 1, 0)
+        out_ref[...] = (x2 + result + out_bias).astype(jnp.bfloat16)
+        wide = dy.astype(jnp.float32)
+        dx = wide + normal_back(unit, inverse, gain, upstream)
+        dx_ref[...] = dx
+        dx_low = dx.astype(jnp.bfloat16)
+        do_ref[...] = contract(dx_low, wc_ref[...], 1, 1).astype(jnp.bfloat16)
+        ac_ref[...] += contract(mixed.T, dx_low, 1, 0)
+        vsum_ref[0:1, :] += column_sum(dx)
+        vsum_ref[1:2, :] += column_sum(upstream * unit)
+        vsum_ref[2:3, :] += column_sum(upstream)
+        vsum_ref[3:4, :] += column_sum(wide)
+
+    @pl.when(step >= steps)
+    def _():
+        at = step - steps
+        core = info_ref[0]
+        rows = 2 * ki_ref.shape[1]
+        split_rows(core, ai_ref[pl.ds(pl.multiple_of(at * rows, 16), rows), :], ki_ref, si_ref)
+        split_rows(core, ac_ref[pl.ds(pl.multiple_of(at * rows, 16), rows), :], kc_ref, sc_ref)
+        rows = 2 * ko_ref.shape[1]
+        columns = ao_ref[:, pl.ds(pl.multiple_of(at * rows, 128), rows)]
+        split_rows(core, columns.astype(jnp.bfloat16).T, ko_ref, so_ref)
+
+
+def resident(array):
+    return pl.BlockSpec(array.shape, lambda *_: (0,) * array.ndim, pipeline_mode=pl.Buffered(1))
+
+
+def feed(info, x1, mixed, dy, wc, wi, wo, vectors, bi, parts, block=512, chunk=768):
+    rows, width = x1.shape
+    inner = wi.shape[1]
+    steps = rows // block
+    pairs = parts // 2
+    row = lambda g, info: (jnp.minimum(g, steps - 1), 0)
+    late = lambda g, info: (jnp.maximum(g - steps, 0), 0, 0)
+    row_spec = pl.BlockSpec((block, width), row)
+    fixed = lambda *_: (0, 0)
+
+    def piece(high, wide):
+        return (
+            [pl.BlockSpec((1, high // parts, wide), late)] * 2,
+            [jax.ShapeDtypeStruct((pairs, high // parts, wide), jnp.bfloat16)] * 2,
+        )
+
+    pieces = [piece(width, inner), piece(inner, width), piece(width, width)]
+    return pl.pallas_call(
+        functools.partial(feed_kernel, steps=steps, chunk=chunk),
+        grid_spec=pltpu.PrefetchScalarGridSpec(
+            num_scalar_prefetch=1,
+            grid=(steps + pairs,),
+            in_specs=[row_spec] * 3 + [resident(a) for a in (wc, wi, wo, vectors, bi)],
+            out_specs=[row_spec] * 3
+            + [pl.BlockSpec((8, width), fixed), pl.BlockSpec((1, inner), fixed)]
+            + sum([p[0] for p in pieces], []),
+            scratch_shapes=[
+                pltpu.VMEM((width, inner), jnp.float32),
+                pltpu.VMEM((width, inner), jnp.float32),
+                pltpu.VMEM((width, width), jnp.float32),
+            ],
+        ),
+        out_shape=[
+            jax.ShapeDtypeStruct((rows, width), jnp.bfloat16),
+            jax.ShapeDtypeStruct((rows, width), jnp.float32),
+            jax.ShapeDtypeStruct((rows, width), jnp.bfloat16),
+            jax.ShapeDtypeStruct((8, width), jnp.float32),
+            jax.ShapeDtypeStruct((1, inner), jnp.float32),
+        ]
+        + sum([p[1] for p in pieces], []),
+        compiler_params=pltpu.CompilerParams(vmem_limit_bytes=60 * 2**20),
+        cost_estimate=pl.CostEstimate(
+            flops=2 * rows * width * (6 * inner + 3 * width),
+            bytes_accessed=60 * 2**20,
+            transcendentals=rows * inner,
+        ),
+        name="feed",
+    )(info, x1, mixed, dy, wc, wi, wo, vectors, bi)
 
 SWAP = ((0, 1), (1, 0))
 
 
-def tree_sum(blocks):
-    place = lax.axis_index("dp")
+class Tree:
+    def __init__(self, kept, sent, order):
+        self.count = lax.axis_size("dp")
+        self.bits = [1 << i for i in reversed(range(1, self.count.bit_length() - 1))]
+        self.order = [bit for bit in order(self.bits)]
+        shape = (2,) * len(self.bits) + kept.shape[1:]
+        self.kept, self.sent, self.bit = kept.reshape(shape), sent.reshape(shape), 1
+        self.got, self.total = None, None
+
+    def exchange(self):
+        if self.total is not None or self.got is not None:
+            return
+        if self.bit:
+            pairs = [(i, i ^ self.bit) for i in range(self.count)]
+            self.got = lax.ppermute(self.sent, "dp", pairs)
+        else:
+            self.got = lax.ppermute(self.kept, "seq", SWAP)
+
+    def add(self):
+        if self.got is None:
+            return
+        total = self.kept.astype(jnp.float32) + self.got.astype(jnp.float32)
+        self.got = None
+        if not self.bit:
+            self.total = total
+            return
+        self.kept = total.astype(jnp.bfloat16)
+        if not self.order:
+            self.bit = 0
+            return
+        self.bit = self.order.pop(0)
+        axis = self.bits.index(self.bit)
+        self.bits.remove(self.bit)
+        mine = (lax.axis_index("dp") // self.bit) % 2
+        whole = self.kept
+        self.kept = lax.dynamic_index_in_dim(whole, mine, axis, keepdims=False)
+        self.sent = lax.dynamic_index_in_dim(whole, 1 - mine, axis, keepdims=False)
+
+
+def low_first(bits):
+    return bits[::-1]
+
+
+def second_first(bits):
+    turned = bits[::-1]
+    return turned[1:2] + turned[:1] + turned[2:]
+
+
+def tree_of(total, order):
     count = lax.axis_size("dp")
-    steps = count.bit_length() - 1
-    blocks = blocks.reshape((2,) * steps + blocks.shape[1:])
-    for step in range(steps):
-        bit = 1 << step
-        mine = (place // bit) % 2
-        axis = steps - 1 - step
-        kept = lax.dynamic_index_in_dim(blocks, mine, axis, keepdims=False)
-        sent = lax.dynamic_index_in_dim(blocks, 1 - mine, axis, keepdims=False)
-        got = lax.ppermute(sent, "dp", [(i, i ^ bit) for i in range(count)])
-        blocks = (kept.astype(jnp.float32) + got.astype(jnp.float32)).astype(jnp.bfloat16)
-    got = lax.ppermute(blocks, "seq", SWAP)
-    return blocks.astype(jnp.float32) + got.astype(jnp.float32)
+    blocks = total.astype(jnp.bfloat16).reshape((count // 2, 2, total.shape[0] // count, -1))
+    core = lax.axis_index("dp") % 2
+    return Tree(
+        lax.dynamic_index_in_dim(blocks, core, 1, keepdims=False),
+        lax.dynamic_index_in_dim(blocks, 1 - core, 1, keepdims=False),
+        order,
+    )
+
+
+def exchange(trees):
+    for tree in trees:
+        tree.exchange()
+
+
+def settle(trees, values):
+    trees = [tree for tree in trees if tree.got is not None]
+    gots, values = lax.optimization_barrier(([tree.got for tree in trees], values))
+    for tree, got in zip(trees, gots):
+        tree.got = got
+        tree.add()
+    return values
+
+
+def finish(trees):
+    while any(tree.total is None for tree in trees):
+        exchange(trees)
+        settle(trees, ())
 
 
 def whole_sequences(
@@ -513,35 +738,50 @@
     cross_mixed, cross_raised, cross_inverse = attend(
         info, cross_queries, cross_pairs, cross_pairs, False, (0, 0, 1)
     )
-    after_cross = after_self + project_rows(cross_mixed, cross_output) + cross_output_bias
-    third_normed = normed(after_cross, norm_feed_gain, norm_feed_bias).astype(jnp.bfloat16)
-    activated, gelu_pullback = jax.vjp(
-        gelu_exact, project_rows(third_normed, feed_in) + feed_in_bias
-    )
-    activated_low = activated.astype(jnp.bfloat16)
-    result = (after_cross + project_rows(activated_low, feed_out) + feed_out_bias).astype(
-        jnp.bfloat16
+    vectors = jnp.concatenate(
+        [
+            jnp.stack([cross_output_bias, norm_feed_gain, norm_feed_bias, feed_out_bias]),
+            jnp.zeros((4, width), jnp.float32),
+        ]
+    )
+    flat = lambda rows: rows.reshape(-1, width)
+    result, grad_cross, cross_upstream, vector_sums, hidden_sums, *feed_parts = feed(
+        (lax.axis_index("dp") % 2)[None].astype(jnp.int32),
+        flat(after_self),
+        flat(cross_mixed),
+        flat(output_low),
+        cross_output,
+        feed_in,
+        feed_out,
+        vectors,
+        feed_in_bias[None],
+        lax.axis_size("dp"),
+    )
+    result, grad_cross, cross_upstream = (
+        rows.reshape(inputs.shape) for rows in (result, grad_cross, cross_upstream)
     )
     pieces = [None] * 21
-    grad_output = output_low.astype(jnp.float32)
-    pieces[19] = outer_sum(activated_low, output_low)
-    pieces[20] = jnp.sum(grad_output, axis=(0, 1))
-    grad_hidden = gelu_pullback(project_back(output_low, feed_out))[0]
-    hidden_low = grad_hidden.astype(jnp.bfloat16)
-    pieces[17] = outer_sum(third_normed, hidden_low)
-    pieces[18] = jnp.sum(grad_hidden, axis=(0, 1))
-    through_feed, pieces[15], pieces[16] = normed_back(
-        after_cross, norm_feed_gain, norm_feed_bias, project_back(hidden_low, feed_in)
-    )
-    grad_cross = grad_output + through_feed
-    cross_low = grad_cross.astype(jnp.bfloat16)
-    pieces[13] = outer_sum(cross_mixed, cross_low)
-    pieces[14] = jnp.sum(grad_cross, axis=(0, 1))
-    cross_upstream = project_back(cross_low, cross_output).astype(jnp.bfloat16)
-    scaled_cross, cross_key_grads, cross_value_grads = attend_back(
+    pieces[14], pieces[15], pieces[16], pieces[20] = vector_sums[:4]
+    pieces[18] = hidden_sums[0]
+    feed_trees = [
+        Tree(*feed_parts[0:2], low_first),
+        Tree(*feed_parts[2:4], second_first),
+        Tree(*feed_parts[4:6], low_first),
+    ]
+    pairs = HEADS * HEAD // 128
+    first = pairs // 2
+    cross_inputs = (
         cross_queries, cross_pairs, cross_pairs, (0, 0, 1), cross_mixed, cross_upstream,
         cross_raised, cross_inverse,
     )
+    exchange(feed_trees)
+    half_grads = attend_back(0, first, (), *cross_inputs)
+    half_grads = settle(feed_trees, half_grads)
+    exchange(feed_trees)
+    scaled_cross, cross_key_grads, cross_value_grads = settle(
+        feed_trees, attend_back(first, pairs - first, half_grads, *cross_inputs)
+    )
+    exchange(feed_trees)
     pair_grads = jnp.concatenate([cross_key_grads, cross_value_grads], axis=-1)
     pieces[12] = jnp.sum(cross_value_grads.astype(jnp.float32), axis=(0, 1))
     pieces[11] = outer_sum(sources, pair_grads)
@@ -556,31 +796,55 @@
     pieces[5] = outer_sum(self_mixed, self_low)
     pieces[6] = jnp.sum(grad_self, axis=(0, 1))
     self_upstream = project_back(self_low, self_output).astype(jnp.bfloat16)
-    joint_grads = attend_back(
+    pieces[5], pieces[9], pieces[11], self_upstream, source_grad = settle(
+        feed_trees, (pieces[5], pieces[9], pieces[11], self_upstream, source_grad)
+    )
+    exchange(feed_trees)
+    mid_trees = [
+        tree_of(pieces[11], low_first),
+        tree_of(pieces[9], second_first),
+        tree_of(pieces[5], second_first),
+    ]
+    exchange(mid_trees)
+    self_inputs = (
         joint, joint, joint, (0, 1, 2), self_mixed, self_upstream, self_raised, self_inverse
     )
+    half_grads = settle(feed_trees + mid_trees, attend_back(0, first, (), *self_inputs))
+    exchange(feed_trees + mid_trees)
+    joint_grads = settle(
+        feed_trees + mid_trees, attend_back(first, pairs - first, half_grads, *self_inputs)
+    )
+    exchange(mid_trees)
     pieces[3] = jnp.sum(joint_grads[0].astype(jnp.float32), axis=(0, 1))
     pieces[4] = jnp.sum(joint_grads[2].astype(jnp.float32), axis=(0, 1))
     joint_low = jnp.concatenate(joint_grads, axis=-1)
     pieces[2] = outer_sum(first_normed, joint_low)
+    late_trees = [
+        tree_of(pieces[2][:, : 3 * width // 2], low_first),
+        tree_of(pieces[2][:, 3 * width // 2 :], second_first),
+    ]
+    exchange(late_trees)
     through_first, pieces[0], pieces[1] = normed_back(
         inputs, norm_self_gain, norm_self_bias, project_back(joint_low, self_input)
     )
     input_grad = grad_self + through_first
-
     count = lax.axis_size("dp")
-    final = [None] * 21
     small = []
     for index, piece in enumerate(pieces):
-        if piece.ndim == 2:
-            blocks = piece.astype(jnp.bfloat16).reshape(count, piece.shape[0] // count, -1)
-            final[index] = tree_sum(blocks)
-        else:
+        if piece is not None and piece.ndim == 1:
             small.append((index, piece.reshape(count, -1)))
-    joined = tree_sum(jnp.concatenate([part for _, part in small], axis=1).astype(jnp.bfloat16))
+    joined = jnp.concatenate([part for _, part in small], axis=1)
+    late_trees.append(tree_of(joined, low_first))
+    finish(feed_trees + mid_trees + late_trees[:2])
+    finish(late_trees[2:])
+    final = [None] * 21
+    for index, tree in zip((17, 19, 13, 11, 9, 5), feed_trees + mid_trees):
+        final[index] = tree.total
+    final[2] = jnp.concatenate([late_trees[0].total, late_trees[1].total], axis=1)
+    joined = late_trees[2].total
     place = 0
     for index, part in small:
-        final[index] = joined[place : place + part.shape[1]]
+        final[index] = joined[0, place : place + part.shape[1]]
         place += part.shape[1]
     return (
         give(result, jnp.bfloat16),

time: 944 us -> 699 us (0.74)
  matrix products: 223 us -> 93.6 us
  Pallas kernels: 189 us -> 284 us
  other arithmetic: 177 us -> 83.7 us
  waiting for transfers between devices: 172 us -> 94.8 us
  local copies, waits for them, and re-layouts: 116 us -> 69.1 us
    pallas_call x2 -> x5, Pallas kernels: 117 us -> 220 us  [the longest x4 123 us: attend_back(): pl.pallas_call(kernel, grid=(count, pairs_now), in_specs=[pl.BlockSpec(me...]
    ppermute x40 -> x45, waiting for transfers between devices: 148 us -> 51.7 us  [the longest x36 41.5 us: exchange(): self.got = lax.ppermute(self.sent, 'dp', pairs)]
    dot_general x7 -> x4, matrix products: 83 us -> 30 us  [project_rows(): jnp.einsum('bpd,de->bpe', row_block, weight, preferred_element_type=jnp.f...]
    convert_element_type x35 -> x36, other arithmetic: 75.6 us -> 24.5 us  [add(): self.kept = total.astype(jnp.bfloat16)]
    dot_general x7 -> x4, matrix products: 72.2 us -> 30.9 us  [project_back(): jnp.einsum('bpe,de->bpd', row_block, weight, preferred_element_type=jnp.f...]
    dot_general x7 -> x4, matrix products: 67.4 us -> 32.7 us  [outer_sum(): jnp.einsum('bpd,bpe->de', first_rows, second_rows, preferred_element_type...]
    dynamic_slice x17 -> x6, local copies, waits for them, and re-layouts: 27.6 us -> 4.3 us  [the longest x5 3.32 us: tree_of(): lax.dynamic_index_in_dim(blocks, core, 1, keepdims=False)]
    unnamed x189 -> x185, local copies, waits for them, and re-layouts: 36.8 us -> 16.3 us
  transfers between devices with their start and end apart: 46 -> 51, of which waited for: 26 -> 17; matrix products, arithmetic and copies ran while one was open for 29% -> 19% of each run, Pallas kernels for 8% -> 27%
where the time goes in v2:
time: 699 us; the launch traced here: 692 us
  Pallas kernels  284 us (41%)
  waiting for transfers between devices  94.8 us (14%)
  matrix products  93.6 us (13%)
  other arithmetic  83.7 us (12%)
  local copies, waits for them, and re-layouts  69.1 us (10%)
  starting transfers between devices  64.4 us (9%)
    pallas_call x4, Pallas kernels, attend_back(): pl.pallas_call(kernel, grid=(count, pairs_now), in_specs=[pl.BlockSpec(me...  123 us
    pallas_call x1, Pallas kernels, feed(): pl.pallas_call(functools.partial(feed_kernel, steps=steps, chunk=chunk),...  96.3 us
    pallas_call x2, Pallas kernels, attend(): pl.pallas_call(functools.partial(attend_kernel, block=length // 2, use_ma...  64.5 us
    ppermute x36, waiting for transfers between devices, exchange(): self.got = lax.ppermute(self.sent, 'dp', pairs)  41.5 us
    ppermute x36, starting transfers between devices, exchange(): self.got = lax.ppermute(self.sent, 'dp', pairs)  40.9 us
    dot_general x4, matrix products, outer_sum(): jnp.einsum('bpd,bpe->de', first_rows, second_rows, preferred_element_type...  32.7 us
    dot_general x4, matrix products, project_back(): jnp.einsum('bpe,de->bpd', row_block, weight, preferred_element_type=jnp.f...  30.9 us
    dot_general x4, matrix products, project_rows(): jnp.einsum('bpd,de->bpe', row_block, weight, preferred_element_type=jnp.f...  30 us
  transfers between devices with their start and end apart: 51, of which 17 were waited for; matrix products, arithmetic and copies ran while one was open for 19% of the time, Pallas kernels for 27%

profile of v2, /device:TPU:0, one launch (start us, length us, event | category | flops | bytes accessed | tf_op | source)
XLA Modules:
  0.0 692.2 jit_solution(1293737060712640290)
XLA Ops:
  0.7 2.8 constant_dynamic-slice_fusion.21
  3.5 3.0 collective-permute-start
  7.8 2.5 multiply_convert_fusion.1
  10.3 1.9 dynamic-slice_bitcast_fusion
  12.2 2.0 collective-permute-start.2
  23.2 18.8 %collective-permute-done = bf16[2,1,512,768]{3,2,0,1:T(8,128)(2,1)} collective-permute-done((bf16[2,1,512,768]{3,2,0,1:T(8,128)(2,1)}, bf16[2,1,512,768]{3,2,0,1:T(8,128)(2,1)}, u32[]{:S(2)}, u32[]{:S(2)}) %collective-permute-start) | collective-permute-done | bytes 1572896 | tf_op jit(solution)/shard_map/ppermute | solution.py:702
  42.0 1.9 convert_reduce_fusion
  44.0 2.4 fusion.9
  47.5 11.5 %multiply_convert_fusion.q_ref.k_ref.v_ref.refs_3_.refs_4_.refs_5_ = bf16[2,1024,2304]{2,1,0:T(8,128)(2,1)} fusion(f32[2304]{0:T(1024)S(1)} %get-tuple-element.304, f32[2304]{0:T(1024)S(1)} %get-tuple-element.303, bf16[768,2304]{1,0:T(8,128)(2,1)S(1)} %copy-done, f32[768]{0:T(1024)S(1)} %copy-done.82, f32[768]{0:T(1024)S(1)} %copy-done.61, ...), kind=kOutput, calls=%fused_computation | convolution fusion | flops 7276068864 | bytes 16162816 | tf_op jit(solution)/shard_map/bpd,de->bpe/dot_general | solution.py:34
  59.0 33.2 %attend.2 = (bf16[2,1024,768]{2,1,0:T(8,128)(2,1)}, bf16[2,12,1024,1024]{3,2,1,0:T(8,128)(2,1)}, f32[2,6,2,1024]{3,2,1,0:T(2,128)}) custom-call(s32[3]{0:T(128)} %pad_add_fusion.info_ref, bf16[2,1024,2304]{2,1,0:T(8,128)(2,1)} %multiply_convert_fusion.q_ref.k_ref.v_ref.refs_3_.refs_4_.refs_5_, ...), custom_call_target="tpu_custom_call" | custom-call | flops 25769803776 | bytes 50331648 | tf_op jit(solution)/shard_map/attend/pallas_call | solution.py:335
  92.3 5.5 fusion.90
  99.4 2.0 copy-done.73
  101.3 8.5 %add_convert_fusion.k_ref.v_ref.refs_4_.refs_5_ = bf16[2,1024,1536]{2,1,0:T(8,128)(2,1)} fusion(f32[1536]{0:T(1024)S(1)} %copy-done.69, bf16[768,1536]{1,0:T(8,128)(2,1)S(1)} %copy-done.73, bf16[2,512,768]{2,1,0:T(8,128)(2,1)} %bitcast.12, bf16[2,512,768]{2,1,0:T(8,128)(2,1)S(1)} %dynamic-slice_bitcast_fusion.1), kind=kOutput, calls=%fused_computation.1 | convolution fusion | flops 4844421120 | bytes 11802624 | tf_op jit(solution)/shard_map/bpd,de->bpe/dot_general | solution.py:34
  109.9 4.6 multiply_convert_fusion.2.q_ref.refs_3_
  114.4 31.2 %attend.3 = (bf16[2,1024,768]{2,1,0:T(8,128)(2,1)}, bf16[2,12,1024,1024]{3,2,1,0:T(8,128)(2,1)}, f32[2,6,2,1024]{3,2,1,0:T(2,128)}) custom-call(s32[3]{0:T(128)} %pad_add_fusion.info_ref, bf16[2,1024,768]{2,1,0:T(8,128)(2,1)} %multiply_convert_fusion.2.q_ref.refs_3_, bf16[2,1024,1536]{2,1,0:T(8,128)(2,1)} %add_convert_fusion.k_ref.v_ref.refs_4_.refs_5_, ...), custom_call_target="tpu_custom_call" | custom-call | flops 25769803776 | bytes 50331648 | tf_op jit(solution)/shard_map/attend/pallas_call | solution.py:335
  145.7 3.3 pad_maximum_fusion.2
  149.0 96.3 %feed.1 = (bf16[2048,768]{1,0:T(8,128)(2,1)}, f32[2048,768]{1,0:T(8,128)}, bf16[2048,768]{1,0:T(8,128)(2,1)}, f32[8,768]{1,0:T(8,128)}, f32[1,3072]{1,0:T(1,128)...) custom-call(s32[1]{0:T(128)} %bitcast.info_ref, ...), custom_call_target="tpu_custom_call" | custom-call | flops 65229815808 | bytes 62914560 | tf_op jit(solution)/shard_map/feed/pallas_call | solution.py:552
  245.3 2.8 slice.98
  248.1 5.9 collective-permute-start.3
  259.2 30.6 %attend_back.4 = (bf16[2,1024,768]{2,1,0:T(8,128)(2,1)}, bf16[2,1024,768]{2,1,0:T(8,128)(2,1)}, bf16[2,1024,768]{2,1,0:T(8,128)(2,1)}) custom-call(bf16[2,1024,768]{2,1,0:T(8,128)(2,1)} %multiply_convert_fusion.2.q_ref.refs_3_, bf16[2,1024,1536]{2,1,0:T(8,128)(2,1)} %add_convert_fusion.k_ref.v_ref.refs_4_.refs_5_, ...), custom_call_target="tpu_custom_call" | custom-call | flops 25769803776 | bytes 25165824 | tf_op jit(solution)/shard_map/attend_back/pallas_call | solution.py:404
  294.7 2.1 broadcast_select_fusion.1
  296.8 1.9 maximum_bitcast_fusion.2
  299.5 2.7 fusion.13
  304.2 2.3 fusion.12
  307.6 5.4 collective-permute-start.8
  315.8 30.8 %attend_back.5 = (bf16[2,1024,768]{2,1,0:T(8,128)(2,1)}, bf16[2,1024,768]{2,1,0:T(8,128)(2,1)}, bf16[2,1024,768]{2,1,0:T(8,128)(2,1)}) custom-call(bf16[2,1024,768]{2,1,0:T(8,128)(2,1)} %get-tuple-element.129.refs_0_, bf16[2,1024,768]{2,1,0:T(8,128)(2,1)} %get-tuple-element.130.refs_1_, ...), custom_call_target="tpu_custom_call", output_to_operand_aliasing={{0}: (0, {}), {1}: (1, {}), {2}: (2, {})} | custom-call | flops 25769803776 | bytes 25165824 | tf_op jit(solution)/shard_map/attend_back/pallas_call | solution.py:404
  346.7 7.6 %fusion.83 = (bf16[768]{0:T(1024)(128)(2,1)S(1)}, f32[2,1024]{1,0:T(2,128)S(1)}, f32[2,1024,768]{2,1,0:T(8,128)S(1)}) fusion(f32[768]{0:T(1024)S(1)} %copy-done.66, f32[2,1024,768]{2,1,0:T(8,128)} %copy-done.1, f32[2,1024]{1,0:T(2,128)S(1)} %copy-done.50, bf16[2,1024,768]{2,1,0:T(8,128)(2,1)} %get-tuple-element.135, bf16[768,768]{1,0:T(8,128)(2,1)} %param.40), kind=kOutput, calls=%fused_computation.242 | convolution fusion | flops 2423780608 | bytes 16929280 | tf_op jit(solution)/shard_map/bpe,de->bpd/dot_general | solution.py:38
  354.3 7.4 %convolution_bitcast_fusion.1 = bf16[768,768]{1,0:T(8,128)(2,1)} fusion(bf16[2,1024,768]{2,1,0:T(8,128)(2,1)S(1)} %copy-done.13, f32[2,1024,768]{2,1,0:T(8,128)} %copy-done.1, f32[768]{0:T(1024)S(1)} %copy-done.81, f32[768]{0:T(1024)S(1)} %copy-done.66, f32[2,1024]{1,0:T(2,128)S(1)} %copy-done.54, f32[2,1024]{1,0:T(2,128)S(1)} %copy-done.50), kind=kOutput, calls=%fused_computation.63 | convolution fusion | flops 2423783424 | bytes 10639360 | tf_op jit(solution)/shard_map/bpd,bpe->de/dot_general | solution.py:42
  365.0 8.0 %convolution_bitcast_fusion = bf16[768,1536]{1,0:T(8,128)(2,1)} fusion(bf16[2,1024,1536]{2,1,0:T(8,128)(2,1)S(1)} %get-tuple-element.267, bf16[2,512,768]{2,1,0:T(8,128)(2,1)} %bitcast.12, bf16[2,512,768]{2,1,0:T(8,128)(2,1)S(1)} %copy-done.29), kind=kOutput, calls=%fused_computation.38 | convolution fusion | flops 4838129664 | bytes 11796480 | tf_op jit(solution)/shard_map/bpd,bpe->de/dot_general | solution.py:42
  373.1 7.0 %fusion.21 = f32[2,1024,768]{2,1,0:T(8,128)} fusion(bf16[2,1024,1536]{2,1,0:T(8,128)(2,1)S(1)} %get-tuple-element.267, bf16[768,1536]{1,0:T(8,128)(2,1)S(1)} %copy-done.74), kind=kOutput, calls=%fused_computation.55 | convolution fusion | flops 4831838208 | bytes 14942208 | tf_op jit(solution)/shard_map/bpe,de->bpd/dot_general | solution.py:38
  380.1 3.1 multiply_reduce_fusion
  388.3 2.0 collective-permute-start.11
  392.1 2.0 collective-permute-start.12
  394.2 5.0 fusion.85
  399.2 3.8 convolution_bitcast_fusion.2
  403.0 4.0 convolution_convert_fusion.g_ref.refs_7_
  409.1 2.4 reduce.2
  415.2 2.6 collective-permute-start.13
  421.2 2.7 collective-permute-start.15
  427.4 18.1 %collective-permute-done.15 = bf16[48,768]{1,0:T(8,128)(2,1)} collective-permute-done((bf16[48,768]{1,0:T(8,128)(2,1)S(1)}, bf16[48,768]{1,0:T(8,128)(2,1)}, u32[]{:S(2)}, u32[]{:S(2)}) %collective-permute-start.15) | collective-permute-done | bytes 73760 | tf_op jit(solution)/shard_map/ppermute | solution.py:601
  445.6 31.1 %attend_back.6 = (bf16[2,1024,768]{2,1,0:T(8,128)(2,1)}, bf16[2,1024,768]{2,1,0:T(8,128)(2,1)}, bf16[2,1024,768]{2,1,0:T(8,128)(2,1)}) custom-call(bf16[2,1024,2304]{2,1,0:T(8,128)(2,1)} %multiply_convert_fusion.q_ref.k_ref.v_ref.refs_3_.refs_4_.refs_5_, bf16[2,1024,2304]{2,1,0:T(8,128)(2,1)} %multiply_convert_fusion.q_ref.k_ref.v_ref.refs_3_.refs_4_.refs_5_, ...), custom_call_target="tpu_custom_call" | custom-call | flops 25769803776 | bytes 25165824 | tf_op jit(solution)/shard_map/attend_back/pallas_call | solution.py:404
  476.7 3.2 slice.139
  492.9 30.9 %attend_back.7 = (bf16[2,1024,768]{2,1,0:T(8,128)(2,1)}, bf16[2,1024,768]{2,1,0:T(8,128)(2,1)}, bf16[2,1024,768]{2,1,0:T(8,128)(2,1)}) custom-call(bf16[2,1024,768]{2,1,0:T(8,128)(2,1)} %get-tuple-element.159.refs_0_, bf16[2,1024,768]{2,1,0:T(8,128)(2,1)} %get-tuple-element.160.refs_1_, ...), custom_call_target="tpu_custom_call", output_to_operand_aliasing={{0}: (0, {}), {1}: (1, {}), {2}: (2, {})} | custom-call | flops 25769803776 | bytes 25165824 | tf_op jit(solution)/shard_map/attend_back/pallas_call | solution.py:404
  523.8 7.4 %collective-permute-done.21 = bf16[48,768]{1,0:T(8,128)(2,1)} collective-permute-done((bf16[48,768]{1,0:T(8,128)(2,1)S(1)}, bf16[48,768]{1,0:T(8,128)(2,1)}, u32[]{:S(2)}, u32[]{:S(2)}) %collective-permute-start.21) | collective-permute-done | bytes 73760 | tf_op jit(solution)/shard_map/ppermute | solution.py:603
  531.3 2.0 collective-permute-start.24
  533.3 2.9 convert_select_fusion.1
  536.2 3.2 maximum_bitcast_fusion.1
  541.2 5.0 collective-permute-done.24
  551.7 3.7 copy-done.36
  555.4 12.2 %fusion.84 = (bf16[768]{0:T(1024)(128)(2,1)}, f32[2,1024]{1,0:T(2,128)S(1)}, f32[2,1024,768]{2,1,0:T(8,128)S(1)}) fusion(f32[768]{0:T(1024)S(1)} %copy-done.62, f32[2,1024]{1,0:T(2,128)S(1)} %copy-done.48, bf16[2,512,768]{2,1,0:T(8,128)(2,1)} %bitcast.3, bf16[2,512,768]{2,1,0:T(8,128)(2,1)S(1)} %copy-done.3, bf16[2,1024,2304]{2,1,0:T(8,128)(2,1)} %copy-done.36, ...), kind=kOutput, calls=%fused_computation.243 | convolution fusion | flops 7261910016 | bytes 22434304 | tf_op jit(solution)/shard_map/bpe,de->bpd/dot_general | solution.py:38
  567.6 13.5 %bitcast_convert_fusion = bf16[768,2304]{1,0:T(8,128)(2,1)} fusion(bf16[2,1024,2304]{2,1,0:T(8,128)(2,1)} %copy-done.36, f32[768]{0:T(1024)S(1)} %copy-done.83, f32[768]{0:T(1024)S(1)} %copy-done.62, f32[2,1024]{1,0:T(2,128)S(1)} %copy-done.52, f32[2,1024]{1,0:T(2,128)S(1)} %copy-done.48, bf16[2,512,768]{2,1,0:T(8,128)(2,1)} %bitcast.3, ...), kind=kOutput, calls=%fused_computation.13 | convolution fusion | flops 7263682560 | bytes 16144384 | tf_op jit(solution)/shard_map/bpd,bpe->de/dot_general | solution.py:42
  581.2 5.0 fusion.8
  586.2 5.5 add_add_fusion.2
  606.2 1.9 convert_add_fusion.19
  610.8 1.8 convert_add_fusion.18
  612.7 3.0 collective-permute-start.30
  623.5 2.6 collective-permute-done.34
  626.3 3.0 collective-permute-start.37
  631.0 1.8 collective-permute-start.41
  635.4 5.1 collective-permute-done.39
  640.4 2.7 collective-permute-done.41
  654.5 2.5 collective-permute-start.47
  659.8 24.2 %collective-permute-done.25 = bf16[2,512,768]{2,1,0:T(8,128)(2,1)S(1)} collective-permute-done((bf16[2,512,768]{2,1,0:T(8,128)(2,1)S(1)}, bf16[2,512,768]{2,1,0:T(8,128)(2,1)S(1)}, u32[]{:S(2)}, u32[]{:S(2)}) %collective-permute-start.25) | collective-permute-done | bytes 1572896 | tf_op jit(solution)/shard_map/ppermute | solution.py:706
  686.8 3.2 maximum_bitcast_fusion
  (396 shorter events, 120.6 us)
Async XLA Ops:
  0.7 46.9 %copy-start = (bf16[768,2304]{1,0:T(8,128)(2,1)S(1)}, bf16[768,2304]{1,0:T(8,128)(2,1)}, u32[]{:S(2)}) copy-start(bf16[768,2304]{1,0:T(8,128)(2,1)} %param.33) | copy-start | bytes 10616836
  3.5 38.5 %collective-permute-start = (bf16[2,1,512,768]{3,2,0,1:T(8,128)(2,1)}, bf16[2,1,512,768]{3,2,0,1:T(8,128)(2,1)}, u32[]{:S(2)}, u32[]{:S(2)}) collective-permute-start(bf16[2,1,512,768]{3,2,0,1:T(8,128)(2,1)} %constant_dynamic-slice_fusion.21), channel_id=1, source_target_pairs={{0,1},{1,0},{2,3},{3,2},{4,5},{5,4},{6,7},{7,6},{8,9},{9,8},{10,11... | collective-permute-start | bytes 4718600 | tf_op jit(solution)/shard_map/ppermute | solution.py:702
  7.7 91.6 %collective-permute-start.1 = (bf16[2,1,512,768]{3,2,0,1:T(8,128)(2,1)}, bf16[2,1,512,768]{3,2,0,1:T(8,128)(2,1)}, u32[]{:S(2)}, u32[]{:S(2)}) collective-permute-start(bf16[2,1,512,768]{3,2,0,1:T(8,128)(2,1)} %constant_dynamic-slice_fusion.19), channel_id=1, source_target_pairs={{0,1},{1,0},{2,3},{3,2},{4,5},{5,4},{6,7},{7,6},{8,9},{9,8},{10,11... | collective-permute-start | bytes 4718600 | tf_op jit(solution)/shard_map/ppermute | solution.py:702
  12.2 133.5 %collective-permute-start.2 = (bf16[2,1,512,768]{3,2,1,0:T(8,128)(2,1)}, bf16[2,1,512,768]{3,2,1,0:T(8,128)(2,1)}, u32[]{:S(2)}, u32[]{:S(2)}) collective-permute-start(bf16[2,1,512,768]{3,2,1,0:T(8,128)(2,1)} %get-tuple-element.273), channel_id=1, source_target_pairs={{0,1},{1,0},{2,3},{3,2},{4,5},{5,4},{6,7},{7,6},{8,9},{9,8},{10,11... | collective-permute-start | bytes 4718600 | tf_op jit(solution)/shard_map/ppermute | solution.py:702
  23.0 69.3 %copy-start.2 = (bf16[2,512,768]{2,1,0:T(8,128)(2,1)}, bf16[2,512,768]{2,1,0:T(8,128)(2,1)S(1)}, u32[]{:S(2)}) copy-start(bf16[2,512,768]{2,1,0:T(8,128)(2,1)S(1)} %dynamic-slice_bitcast_fusion.2) | copy-start | bytes 4718596
  23.2 76.2 %copy-start.28 = (bf16[2,512,768]{2,1,0:T(8,128)(2,1)}, bf16[2,512,768]{2,1,0:T(8,128)(2,1)S(1)}, u32[]{:S(2)}) copy-start(bf16[2,512,768]{2,1,0:T(8,128)(2,1)S(1)} %dynamic-slice_bitcast_fusion.1) | copy-start | bytes 4718596
  59.0 33.2 %copy-start.76 = (bf16[768,768]{1,0:T(8,128)(2,1)S(1)}, bf16[768,768]{1,0:T(8,128)(2,1)}, u32[]{:S(2)}) copy-start(bf16[768,768]{1,0:T(8,128)(2,1)} %param.36) | copy-start | bytes 3538948
  59.0 33.3 %copy-start.78 = (f32[768]{0:T(1024)S(1)}, f32[768]{0:T(1024)}, u32[]{:S(2)}) copy-start(f32[768]{0:T(1024)} %param.37) | copy-start | bytes 9220
  114.4 31.3 %copy-start.5 = (bf16[2,512,768]{2,1,0:T(8,128)(2,1)S(1)}, bf16[2,512,768]{2,1,0:T(8,128)(2,1)}, u32[]{:S(2)}) copy-start(bf16[2,512,768]{2,1,0:T(8,128)(2,1)} %get-tuple-element.272) | copy-start | bytes 4718596
  248.1 46.6 %collective-permute-start.3 = (bf16[2,512,768]{2,1,0:T(8,128)(2,1)}, bf16[2,512,768]{2,1,0:T(8,128)(2,1)}, u32[]{:S(2)}, u32[]{:S(2)}) collective-permute-start(bf16[2,512,768]{2,1,0:T(8,128)(2,1)} %slice.98), channel_id=1, source_target_pairs={{0,1},{1,0},{2,3},{3,2},{4,5},{5,4},{6,7},{7,6},{8,9},{9,8},{10,11... | collective-permute-start | bytes 4718600 | tf_op jit(solution)/shard_map/ppermute | solution.py:706
  255.6 43.1 %collective-permute-start.4 = (bf16[2,2,2,48,3072]{4,3,0,1,2:T(8,128)(2,1)}, bf16[2,2,2,48,3072]{4,3,0,1,2:T(8,128)(2,1)}, u32[]{:S(2)}, u32[]{:S(2)}) collective-permute-start(bf16[2,2,2,48,3072]{4,3,0,1,2:T(8,128)(2,1)} %copy.73), channel_id=1, source_target_pairs={{0,2},{2,0},{4,6},{6,4},{8,10},{10,8},{12,14},{14,12},{16,18},{18,... | collective-permute-start | bytes 7077896 | tf_op jit(solution)/shard_map/ppermute | solution.py:601
  257.2 41.5 %collective-permute-start.5 = (bf16[2,2,2,192,768]{4,3,0,2,1:T(8,128)(2,1)}, bf16[2,2,2,192,768]{4,3,0,2,1:T(8,128)(2,1)}, u32[]{:S(2)}, u32[]{:S(2)}) collective-permute-start(bf16[2,2,2,192,768]{4,3,0,2,1:T(8,128)(2,1)} %copy.74), channel_id=1, source_target_pairs={{0,2},{2,0},{4,6},{6,4},{8,10},{10,8},{12,14},{14,12},{16,18},{18,... | collective-permute-start | bytes 7077896 | tf_op jit(solution)/shard_map/ppermute | solution.py:601
  258.6 40.1 %collective-permute-start.6 = (bf16[2,2,2,48,768]{4,3,0,1,2:T(8,128)(2,1)}, bf16[2,2,2,48,768]{4,3,0,1,2:T(8,128)(2,1)}, u32[]{:S(2)}, u32[]{:S(2)}) collective-permute-start(bf16[2,2,2,48,768]{4,3,0,1,2:T(8,128)(2,1)} %copy.75), channel_id=1, source_target_pairs={{0,2},{2,0},{4,6},{6,4},{8,10},{10,8},{12,14},{14,12},{16,18},{18,... | collective-permute-start | bytes 1769480 | tf_op jit(solution)/shard_map/ppermute | solution.py:601
  259.2 30.6 %copy-start.67 = (f32[1,3072]{1,0:T(1,128)S(1)}, f32[1,3072]{1,0:T(1,128)}, u32[]{:S(2)}) copy-start(f32[1,3072]{1,0:T(1,128)} %get-tuple-element.170) | copy-start | bytes 36868
  303.4 43.3 %collective-permute-start.7 = (bf16[2,2,48,3072]{3,2,0,1:T(8,128)(2,1)}, bf16[2,2,48,3072]{3,2,0,1:T(8,128)(2,1)}, u32[]{:S(2)}, u32[]{:S(2)}) collective-permute-start(bf16[2,2,48,3072]{3,2,0,1:T(8,128)(2,1)} %dynamic-slice_bitcast_fusion.4), channel_id=1, source_target_pairs={{0,4},{2,6},{4,0},{6,2},{8,12},{10,14},{12,8},{14,10},{16,20},{18,... | collective-permute-start | bytes 3538952 | tf_op jit(solution)/shard_map/ppermute | solution.py:601
  307.6 39.0 %collective-permute-start.8 = (bf16[2,2,192,768]{3,2,0,1:T(8,128)(2,1)}, bf16[2,2,192,768]{3,2,0,1:T(8,128)(2,1)}, u32[]{:S(2)}, u32[]{:S(2)}) collective-permute-start(bf16[2,2,192,768]{3,2,0,1:T(8,128)(2,1)} %dynamic-slice_bitcast_fusion.3), channel_id=1, source_target_pairs={{0,8},{2,10},{4,12},{6,14},{8,0},{10,2},{12,4},{14,6},{16,24},{18,... | collective-permute-start | bytes 3538952 | tf_op jit(solution)/shard_map/ppermute | solution.py:601
  315.8 30.9 %copy-start.50 = (f32[2,1024]{1,0:T(2,128)S(1)}, f32[2,1024]{1,0:T(2,128)}, u32[]{:S(2)}) copy-start(f32[2,1024]{1,0:T(2,128)} %copy-done.49) | copy-start | bytes 24580
  315.8 30.9 %copy-start.66 = (f32[768]{0:T(1024)S(1)}, f32[768]{0:T(1024)}, u32[]{:S(2)}) copy-start(f32[768]{0:T(1024)} %param.38) | copy-start | bytes 9220
  315.8 30.9 %collective-permute-start.9 = (bf16[2,2,48,768]{3,2,0,1:T(8,128)(2,1)}, bf16[2,2,48,768]{3,2,0,1:T(8,128)(2,1)}, u32[]{:S(2)}, u32[]{:S(2)}) collective-permute-start(bf16[2,2,48,768]{3,2,0,1:T(8,128)(2,1)} %dynamic-slice_bitcast_fusion.15), channel_id=1, source_target_pairs={{0,4},{2,6},{4,0},{6,2},{8,12},{10,14},{12,8},{14,10},{16,20},{18,... | collective-permute-start | bytes 884744 | tf_op jit(solution)/shard_map/ppermute | solution.py:601
  385.8 27.0 %collective-permute-start.10 = (bf16[2,48,3072]{2,1,0:T(8,128)(2,1)}, bf16[2,48,3072]{2,1,0:T(8,128)(2,1)}, u32[]{:S(2)}, u32[]{:S(2)}) collective-permute-start(bf16[2,48,3072]{2,1,0:T(8,128)(2,1)} %dynamic-slice_bitcast_fusion.7), channel_id=1, source_target_pairs={{0,8},{2,10},{4,12},{6,14},{8,0},{10,2},{12,4},{14,6},{16,24},{18,... | collective-permute-start | bytes 1769480 | tf_op jit(solution)/shard_map/ppermute | solution.py:601
  388.3 24.5 %collective-permute-start.11 = (bf16[2,192,768]{2,1,0:T(8,128)(2,1)}, bf16[2,192,768]{2,1,0:T(8,128)(2,1)}, u32[]{:S(2)}, u32[]{:S(2)}) collective-permute-start(bf16[2,192,768]{2,1,0:T(8,128)(2,1)} %dynamic-slice_bitcast_fusion.6), channel_id=1, source_target_pairs={{0,4},{2,6},{4,0},{6,2},{8,12},{10,14},{12,8},{14,10},{16,20},{18,... | collective-permute-start | bytes 1769480 | tf_op jit(solution)/shard_map/ppermute | solution.py:601
  392.1 20.7 %collective-permute-start.12 = (bf16[2,48,768]{2,1,0:T(8,128)(2,1)}, bf16[2,48,768]{2,1,0:T(8,128)(2,1)}, u32[]{:S(2)}, u32[]{:S(2)}) collective-permute-start(bf16[2,48,768]{2,1,0:T(8,128)(2,1)} %dynamic-slice_bitcast_fusion.21), channel_id=1, source_target_pairs={{0,8},{2,10},{4,12},{6,14},{8,0},{10,2},{12,4},{14,6},{16,24},{18,... | collective-permute-start | bytes 442376 | tf_op jit(solution)/shard_map/ppermute | solution.py:601
  415.2 64.8 %collective-permute-start.13 = (bf16[48,3072]{1,0:T(8,128)(2,1)}, bf16[48,3072]{1,0:T(8,128)(2,1)}, u32[]{:S(2)}, u32[]{:S(2)}) collective-permute-start(bf16[48,3072]{1,0:T(8,128)(2,1)} %dynamic-slice_bitcast_fusion.14), channel_id=1, source_target_pairs={{0,16},{2,18},{4,20},{6,22},{8,24},{10,26},{12,28},{14,30},{16,0},... | collective-permute-start | bytes 884744 | tf_op jit(solution)/shard_map/ppermute | solution.py:601
  419.9 61.7 %collective-permute-start.14 = (bf16[192,768]{1,0:T(8,128)(2,1)}, bf16[192,768]{1,0:T(8,128)(2,1)}, u32[]{:S(2)}, u32[]{:S(2)}) collective-permute-start(bf16[192,768]{1,0:T(8,128)(2,1)} %dynamic-slice_bitcast_fusion.13), channel_id=1, source_target_pairs={{0,16},{2,18},{4,20},{6,22},{8,24},{10,26},{12,28},{14,30},{16,0},... | collective-permute-start | bytes 884744 | tf_op jit(solution)/shard_map/ppermute | solution.py:601
  421.2 24.3 %collective-permute-start.15 = (bf16[48,768]{1,0:T(8,128)(2,1)S(1)}, bf16[48,768]{1,0:T(8,128)(2,1)}, u32[]{:S(2)}, u32[]{:S(2)}) collective-permute-start(bf16[48,768]{1,0:T(8,128)(2,1)S(1)} %dynamic-slice_bitcast_fusion.26), channel_id=1, source_target_pairs={{0,16},{2,18},{4,20},{6,22},{8,24},{10,26},{12,28},{14,30},{16,0},... | collective-permute-start | bytes 221192 | tf_op jit(solution)/shard_map/ppermute | solution.py:601
  425.1 56.5 %collective-permute-start.16 = (bf16[2,2,2,48,1536]{4,3,2,1,0:T(8,128)(2,1)}, bf16[2,2,2,48,1536]{4,3,2,1,0:T(8,128)(2,1)S(1)}, u32[]{:S(2)}, u32[]{:S(2)}) collective-permute-start(bf16[2,2,2,48,1536]{4,3,2,1,0:T(8,128)(2,1)} %bitcast.50), channel_id=1, source_target_pairs={{0,2},{2,0},{4,6},{6,4},{8,10},{10,8},{12,14},{14,12},{16,18},{18,... | collective-permute-start | bytes 3538952 | tf_op jit(solution)/shard_map/ppermute | solution.py:601
  426.0 55.6 %collective-permute-start.17 = (bf16[2,2,2,48,768]{4,3,2,1,0:T(8,128)(2,1)}, bf16[2,2,2,48,768]{4,3,2,1,0:T(8,128)(2,1)}, u32[]{:S(2)}, u32[]{:S(2)}) collective-permute-start(bf16[2,2,2,48,768]{4,3,2,1,0:T(8,128)(2,1)} %bitcast.52), channel_id=1, source_target_pairs={{0,2},{2,0},{4,6},{6,4},{8,10},{10,8},{12,14},{14,12},{16,18},{18,... | collective-permute-start | bytes 1769480 | tf_op jit(solution)/shard_map/ppermute | solution.py:601
  445.6 36.0 %collective-permute-start.18 = (bf16[2,2,2,48,768]{4,3,2,1,0:T(8,128)(2,1)}, bf16[2,2,2,48,768]{4,3,2,1,0:T(8,128)(2,1)}, u32[]{:S(2)}, u32[]{:S(2)}) collective-permute-start(bf16[2,2,2,48,768]{4,3,2,1,0:T(8,128)(2,1)} %bitcast.54), channel_id=1, source_target_pairs={{0,2},{2,0},{4,6},{6,4},{8,10},{10,8},{12,14},{14,12},{16,18},{18,... | collective-permute-start | bytes 1769480 | tf_op jit(solution)/shard_map/ppermute | solution.py:601
  479.9 51.3 %collective-permute-start.26 = (bf16[2,512,768]{2,1,0:T(8,128)(2,1)}, bf16[2,512,768]{2,1,0:T(8,128)(2,1)}, u32[]{:S(2)}, u32[]{:S(2)}) collective-permute-start(bf16[2,512,768]{2,1,0:T(8,128)(2,1)} %slice.139), channel_id=1, source_target_pairs={{0,1},{1,0},{2,3},{3,2},{4,5},{5,4},{6,7},{7,6},{8,9},{9,8},{10,11... | collective-permute-start | bytes 4718600 | tf_op jit(solution)/shard_map/ppermute | solution.py:706
  483.4 56.1 %collective-permute-start.19 = (bf16[48,3072]{1,0:T(8,128)(2,1)}, bf16[48,3072]{1,0:T(8,128)(2,1)}, u32[]{:S(2)}, u32[]{:S(2)}) collective-permute-start(bf16[48,3072]{1,0:T(8,128)(2,1)} %fusion.48), channel_id=1, source_target_pairs={{0,1},{1,0},{2,3},{3,2},{4,5},{5,4},{6,7},{7,6},{8,9},{9,8},{10,11... | collective-permute-start | bytes 884744 | tf_op jit(solution)/shard_map/ppermute | solution.py:603
  484.8 54.7 %collective-permute-start.20 = (bf16[192,768]{1,0:T(8,128)(2,1)S(1)}, bf16[192,768]{1,0:T(8,128)(2,1)}, u32[]{:S(2)}, u32[]{:S(2)}) collective-permute-start(bf16[192,768]{1,0:T(8,128)(2,1)S(1)} %fusion.47), channel_id=1, source_target_pairs={{0,1},{1,0},{2,3},{3,2},{4,5},{5,4},{6,7},{7,6},{8,9},{9,8},{10,11... | collective-permute-start | bytes 884744 | tf_op jit(solution)/shard_map/ppermute | solution.py:603
  487.4 43.8 %collective-permute-start.21 = (bf16[48,768]{1,0:T(8,128)(2,1)S(1)}, bf16[48,768]{1,0:T(8,128)(2,1)}, u32[]{:S(2)}, u32[]{:S(2)}) collective-permute-start(bf16[48,768]{1,0:T(8,128)(2,1)S(1)} %fusion.60), channel_id=1, source_target_pairs={{0,1},{1,0},{2,3},{3,2},{4,5},{5,4},{6,7},{7,6},{8,9},{9,8},{10,11... | collective-permute-start | bytes 221192 | tf_op jit(solution)/shard_map/ppermute | solution.py:603
  489.3 56.9 %collective-permute-start.22 = (bf16[2,2,48,1536]{3,2,1,0:T(8,128)(2,1)S(1)}, bf16[2,2,48,1536]{3,2,1,0:T(8,128)(2,1)S(1)}, u32[]{:S(2)}, u32[]{:S(2)}) collective-permute-start(bf16[2,2,48,1536]{3,2,1,0:T(8,128)(2,1)S(1)} %dynamic-slice_bitcast_fusion.5), channel_id=1, source_target_pairs={{0,4},{2,6},{4,0},{6,2},{8,12},{10,14},{12,8},{14,10},{16,20},{18,... | collective-permute-start | bytes 1769480 | tf_op jit(solution)/shard_map/ppermute | solution.py:601
  492.9 30.9 %copy-start.21 = (bf16[2,2,2,48,768]{4,3,2,1,0:T(8,128)(2,1)}, bf16[2,2,2,48,768]{4,3,2,1,0:T(8,128)(2,1)S(1)}, u32[]{:S(2)}) copy-start(bf16[2,2,2,48,768]{4,3,2,1,0:T(8,128)(2,1)S(1)} %fusion.31) | copy-start | bytes 1769476
  531.3 9.9 %collective-permute-start.23 = (bf16[2,2,48,768]{3,2,1,0:T(8,128)(2,1)S(1)}, bf16[2,2,48,768]{3,2,1,0:T(8,128)(2,1)S(1)}, u32[]{:S(2)}, u32[]{:S(2)}) collective-permute-start(bf16[2,2,48,768]{3,2,1,0:T(8,128)(2,1)S(1)} %dynamic-slice_bitcast_fusion.12), channel_id=1, source_target_pairs={{0,8},{2,10},{4,12},{6,14},{8,0},{10,2},{12,4},{14,6},{16,24},{18,... | collective-permute-start | bytes 884744 | tf_op jit(solution)/shard_map/ppermute | solution.py:601
  531.3 14.9 %collective-permute-start.24 = (bf16[2,2,48,768]{3,2,1,0:T(8,128)(2,1)S(1)}, bf16[2,2,48,768]{3,2,1,0:T(8,128)(2,1)S(1)}, u32[]{:S(2)}, u32[]{:S(2)}) collective-permute-start(bf16[2,2,48,768]{3,2,1,0:T(8,128)(2,1)S(1)} %dynamic-slice_bitcast_fusion.11), channel_id=1, source_target_pairs={{0,8},{2,10},{4,12},{6,14},{8,0},{10,2},{12,4},{14,6},{16,24},{18,... | collective-permute-start | bytes 884744 | tf_op jit(solution)/shard_map/ppermute | solution.py:601
  550.3 35.8 %slice-start.2 = ((s8[6291456]{0:T(1024)(128)(4,1)}), s8[4194304]{0:T(1024)(128)(4,1)S(1)}, s32[]{:S(2)}) async-start(s8[6291456]{0:T(1024)(128)(4,1)} %bitcast.315), calls=%async_computation.2 | async-start | bytes 8388608
  555.4 30.7 %slice-start.3 = ((s8[6291456]{0:T(1024)(128)(4,1)}), s8[2097152]{0:T(1024)(128)(4,1)S(1)}, s32[]{:S(2)}) async-start(s8[6291456]{0:T(1024)(128)(4,1)} %bitcast.315), calls=%async_computation.3 | async-start | bytes 4194304
  599.6 4.7 collective-permute-start.27
  601.1 25.0 %collective-permute-start.32 = (bf16[2,48,1536]{2,1,0:T(8,128)(2,1)S(1)}, bf16[2,48,1536]{2,1,0:T(8,128)(2,1)S(1)}, u32[]{:S(2)}, u32[]{:S(2)}) collective-permute-start(bf16[2,48,1536]{2,1,0:T(8,128)(2,1)S(1)} %dynamic-slice_bitcast_fusion.10), channel_id=1, source_target_pairs={{0,8},{2,10},{4,12},{6,14},{8,0},{10,2},{12,4},{14,6},{16,24},{18,... | collective-permute-start | bytes 884744 | tf_op jit(solution)/shard_map/ppermute | solution.py:601
  602.6 20.9 %collective-permute-start.33 = (bf16[2,48,768]{2,1,0:T(8,128)(2,1)S(1)}, bf16[2,48,768]{2,1,0:T(8,128)(2,1)S(1)}, u32[]{:S(2)}, u32[]{:S(2)}) collective-permute-start(bf16[2,48,768]{2,1,0:T(8,128)(2,1)S(1)} %dynamic-slice_bitcast_fusion.20), channel_id=1, source_target_pairs={{0,4},{2,6},{4,0},{6,2},{8,12},{10,14},{12,8},{14,10},{16,20},{18,... | collective-permute-start | bytes 442376 | tf_op jit(solution)/shard_map/ppermute | solution.py:601
  603.4 22.7 %collective-permute-start.35 = (bf16[2,2,2,48,1152]{4,3,2,1,0:T(8,128)(2,1)S(1)}, bf16[2,2,2,48,1152]{4,3,2,1,0:T(8,128)(2,1)S(1)}, u32[]{:S(2)}, u32[]{:S(2)}) collective-permute-start(bf16[2,2,2,48,1152]{4,3,2,1,0:T(8,128)(2,1)S(1)} %bitcast.339), channel_id=1, source_target_pairs={{0,2},{2,0},{4,6},{6,4},{8,10},{10,8},{12,14},{14,12},{16,18},{18,... | collective-permute-start | bytes 2654216 | tf_op jit(solution)/shard_map/ppermute | solution.py:601
  603.8 22.3 %collective-permute-start.36 = (bf16[2,2,2,48,1152]{4,3,0,2,1:T(8,128)(2,1)S(1)}, bf16[2,2,2,48,1152]{4,3,0,2,1:T(8,128)(2,1)S(1)}, u32[]{:S(2)}, u32[]{:S(2)}) collective-permute-start(bf16[2,2,2,48,1152]{4,3,0,2,1:T(8,128)(2,1)S(1)} %copy.92), channel_id=1, source_target_pairs={{0,2},{2,0},{4,6},{6,4},{8,10},{10,8},{12,14},{14,12},{16,18},{18,... | collective-permute-start | bytes 2654216 | tf_op jit(solution)/shard_map/ppermute | solution.py:601
  604.4 17.6 %copy-start.46 = (bf16[48,768]{1,0:T(8,128)(2,1)S(1)}, bf16[48,768]{1,0:T(8,128)(2,1)}, u32[]{:S(2)}) copy-start(bf16[48,768]{1,0:T(8,128)(2,1)} %copy-done.45) | copy-start | bytes 221188
  604.4 4.5 collective-permute-start.28
  609.0 3.7 collective-permute-start.29
  612.7 4.6 collective-permute-start.30
  617.3 3.7 collective-permute-start.31
  621.0 5.1 collective-permute-start.34
  626.3 14.2 %collective-permute-start.37 = (bf16[48,1536]{1,0:T(8,128)(2,1)S(1)}, bf16[48,1536]{1,0:T(8,128)(2,1)S(1)}, u32[]{:S(2)}, u32[]{:S(2)}) collective-permute-start(bf16[48,1536]{1,0:T(8,128)(2,1)S(1)} %dynamic-slice_bitcast_fusion.18), channel_id=1, source_target_pairs={{0,16},{2,18},{4,20},{6,22},{8,24},{10,26},{12,28},{14,30},{16,0},... | collective-permute-start | bytes 442376 | tf_op jit(solution)/shard_map/ppermute | solution.py:601
  629.3 6.1 collective-permute-start.38
  629.6 10.8 %collective-permute-start.40 = (bf16[2,2,48,1152]{3,2,1,0:T(8,128)(2,1)S(1)}, bf16[2,2,48,1152]{3,2,1,0:T(8,128)(2,1)S(1)}, u32[]{:S(2)}, u32[]{:S(2)}) collective-permute-start(bf16[2,2,48,1152]{3,2,1,0:T(8,128)(2,1)S(1)} %dynamic-slice_bitcast_fusion.9), channel_id=1, source_target_pairs={{0,4},{2,6},{4,0},{6,2},{8,12},{10,14},{12,8},{14,10},{16,20},{18,... | collective-permute-start | bytes 1327112 | tf_op jit(solution)/shard_map/ppermute | solution.py:601
  631.0 12.2 %collective-permute-start.41 = (bf16[2,2,48,1152]{3,2,0,1:T(8,128)(2,1)S(1)}, bf16[2,2,48,1152]{3,2,0,1:T(8,128)(2,1)S(1)}, u32[]{:S(2)}, u32[]{:S(2)}) collective-permute-start(bf16[2,2,48,1152]{3,2,0,1:T(8,128)(2,1)S(1)} %dynamic-slice_bitcast_fusion.8), channel_id=1, source_target_pairs={{0,8},{2,10},{4,12},{6,14},{8,0},{10,2},{12,4},{14,6},{16,24},{18,... | collective-permute-start | bytes 1327112 | tf_op jit(solution)/shard_map/ppermute | solution.py:601
  632.8 7.6 %collective-permute-start.39 = (bf16[48,768]{1,0:T(8,128)(2,1)S(1)}, bf16[48,768]{1,0:T(8,128)(2,1)S(1)}, u32[]{:S(2)}, u32[]{:S(2)}) collective-permute-start(bf16[48,768]{1,0:T(8,128)(2,1)S(1)} %dynamic-slice_bitcast_fusion.24), channel_id=1, source_target_pairs={{0,16},{2,18},{4,20},{6,22},{8,24},{10,26},{12,28},{14,30},{16,0},... | collective-permute-start | bytes 221192 | tf_op jit(solution)/shard_map/ppermute | solution.py:601
  643.2 8.5 %collective-permute-start.42 = (bf16[48,1536]{1,0:T(8,128)(2,1)S(1)}, bf16[48,1536]{1,0:T(8,128)(2,1)S(1)}, u32[]{:S(2)}, u32[]{:S(2)}) collective-permute-start(bf16[48,1536]{1,0:T(8,128)(2,1)S(1)} %fusion.52), channel_id=1, source_target_pairs={{0,1},{1,0},{2,3},{3,2},{4,5},{5,4},{6,7},{7,6},{8,9},{9,8},{10,11... | collective-permute-start | bytes 442376 | tf_op jit(solution)/shard_map/ppermute | solution.py:603
  644.9 6.0 collective-permute-start.43
  645.4 6.3 collective-permute-start.44
  647.3 6.0 collective-permute-start.45
  648.5 6.0 collective-permute-start.46
  650.9 33.1 %collective-permute-start.25 = (bf16[2,512,768]{2,1,0:T(8,128)(2,1)S(1)}, bf16[2,512,768]{2,1,0:T(8,128)(2,1)S(1)}, u32[]{:S(2)}, u32[]{:S(2)}) collective-permute-start(bf16[2,512,768]{2,1,0:T(8,128)(2,1)S(1)} %slice.140), channel_id=1, source_target_pairs={{0,1},{1,0},{2,3},{3,2},{4,5},{5,4},{6,7},{7,6},{8,9},{9,8},{10,11... | collective-permute-start | bytes 4718600 | tf_op jit(solution)/shard_map/ppermute | solution.py:706
  654.5 30.0 %collective-permute-start.47 = (bf16[48,1152]{1,0:T(8,128)(2,1)S(1)}, bf16[48,1152]{1,0:T(8,128)(2,1)S(1)}, u32[]{:S(2)}, u32[]{:S(2)}) collective-permute-start(bf16[48,1152]{1,0:T(8,128)(2,1)S(1)} %dynamic-slice_bitcast_fusion.23), channel_id=1, source_target_pairs={{0,16},{2,18},{4,20},{6,22},{8,24},{10,26},{12,28},{14,30},{16,0},... | collective-permute-start | bytes 331784 | tf_op jit(solution)/shard_map/ppermute | solution.py:601
  657.1 27.5 %collective-permute-start.48 = (bf16[48,1152]{1,0:T(8,128)(2,1)S(1)}, bf16[48,1152]{1,0:T(8,128)(2,1)S(1)}, u32[]{:S(2)}, u32[]{:S(2)}) collective-permute-start(bf16[48,1152]{1,0:T(8,128)(2,1)S(1)} %dynamic-slice_bitcast_fusion.22), channel_id=1, source_target_pairs={{0,16},{2,18},{4,20},{6,22},{8,24},{10,26},{12,28},{14,30},{16,0},... | collective-permute-start | bytes 331784 | tf_op jit(solution)/shard_map/ppermute | solution.py:601
  684.6 5.4 collective-permute-start.49
  686.3 4.8 collective-permute-start.50
  (78 other events, 495.3 us)

commit v3 on v2

--- a/solution.py
+++ b/solution.py
@@ -259,68 +259,86 @@
     return (jnp.where(lane < HEAD, pair, zero), jnp.where(lane < HEAD, zero, pair))
 
 
-def attend_kernel(info_ref, q_ref, k_ref, v_ref, o_ref, e_ref, r_ref, *, block, use_mask):
+ATTEND_LIMIT = 40 * 2**20
+
+
+def attend_kernel(info_ref, q_ref, k_ref, v_ref, o_ref, e_ref, r_ref, *, use_mask):
     length = k_ref.shape[1]
+    half = length // 2
     values_turned = v_ref[0].T
     ones = jnp.ones((16, length), jnp.bfloat16)
-    own = length // 2
-    causal = info_ref[1 + pl.program_id(0)] == 0 if use_mask else None
-
-    def allowed(start):
-        offset = info_ref[0] * own
-        key_place = lax.broadcasted_iota(jnp.int32, (length, 1), 0) + offset
-        key_place = jnp.where(key_place >= length, key_place - length, key_place)
-        query_place = lax.broadcasted_iota(jnp.int32, (1, block), 1) + start + offset
-        query_place = jnp.where(query_place >= length, query_place - length, query_place)
-        return key_place <= query_place
-
-    def run(masked, shifted):
+    side = info_ref[0]
+
+    def run(masked, shifted, side_now=None):
         lowest, highest = None, None
-        for start in range(0, length, block):
+        below = (
+            lax.broadcasted_iota(jnp.int32, (half, 1), 0)
+            <= lax.broadcasted_iota(jnp.int32, (1, half), 1)
+            if masked
+            else None
+        )
+        for at in range(2):
+            queries_at = slice(at * half, (at + 1) * half)
+            if masked:
+                seen = [at] if at == side_now else [0, 1]
+            else:
+                seen = [None]
             mixed = []
-            for head, queries in enumerate(head_masks(q_ref[0, start : start + block, :])):
-                scores = contract(k_ref[0], queries, 1, 1)
-                if masked and shifted:
-                    scores = jnp.where(allowed(start), scores, blocked_score)
+            for head, queries in enumerate(head_masks(q_ref[0, queries_at, :])):
+                tiles = []
+                for key_at in seen:
+                    rows = slice(0, length)
+                    if key_at is not None:
+                        rows = slice(key_at * half, (key_at + 1) * half)
+                    scores = contract(k_ref[0, rows, :], queries, 1, 1)
+                    if key_at == at:
+                        scores = jnp.where(below, scores, blocked_score)
+                    tiles.append((rows, scores))
                 if shifted:
-                    scores = scores - jnp.max(scores, axis=0, keepdims=True)
-                raised = jnp.exp(scores)
-                if masked:
-                    raised = jnp.where(allowed(start), raised, 0.0)
-                low = raised.astype(jnp.bfloat16)
-                e_ref[0, head, :, start : start + block] = low
-                turned = jnp.concatenate(
-                    [values_turned[head * HEAD : (head + 1) * HEAD], ones], axis=0
-                )
-                sums = contract(turned, low, 1, 0)
+                    highest_score = functools.reduce(
+                        jnp.maximum,
+                        [jnp.max(scores, axis=0, keepdims=True) for _, scores in tiles],
+                    )
+                    tiles = [(rows, scores - highest_score) for rows, scores in tiles]
+                sums = None
+                for rows, scores in tiles:
+                    low = jnp.exp(scores).astype(jnp.bfloat16)
+                    e_ref[0, head, rows, queries_at] = low
+                    turned = jnp.concatenate(
+                        [values_turned[head * HEAD : (head + 1) * HEAD, rows], ones[:, rows]], axis=0
+                    )
+                    part = contract(turned, low, 1, 0)
+                    sums = part if sums is None else sums + part
+                if masked and len(seen) == 1:
+                    other = slice((1 - at) * half, (2 - at) * half)
+                    e_ref[0, head, other, queries_at] = jnp.zeros((half, half), jnp.bfloat16)
                 total = sums[HEAD : HEAD + 1]
                 if not shifted:
                     lowest = total if lowest is None else jnp.minimum(lowest, total)
                     highest = total if highest is None else jnp.maximum(highest, total)
                 inverse = 1.0 / total
-                r_ref[0, 0, head : head + 1, start : start + block] = inverse
+                r_ref[0, 0, head : head + 1, queries_at] = inverse
                 mixed.append(sums[:HEAD] * inverse)
-            o_ref[0, start : start + block, :] = (
-                jnp.concatenate(mixed, axis=0).T.astype(jnp.bfloat16)
-            )
+            o_ref[0, queries_at, :] = jnp.concatenate(mixed, axis=0).T.astype(jnp.bfloat16)
         if not shifted:
             in_range = (jnp.min(lowest) > 1e-20) & (jnp.max(highest) < 1e30)
 
             @pl.when(jnp.logical_not(in_range))
             def _():
-                run(masked, True)
-
-    if use_mask:
-
-        @pl.when(causal)
+                run(masked, True, side_now)
+
+    if not use_mask:
+        run(False, False)
+        return
+    causal = info_ref[2 + pl.program_id(0)] == 0
+    for side_now in range(2):
+
+        @pl.when(causal & (side == side_now))
         def _():
-            run(True, False)
-
-        @pl.when(jnp.logical_not(causal))
-        def _():
-            run(False, False)
-
-    else:
+            run(True, False, side_now)
+
+    @pl.when(jnp.logical_not(causal))
+    def _():
         run(False, False)
 
 
@@ -333,7 +351,7 @@
         return pl.BlockSpec((1, length, 128), lambda s, p, info: (s, 0, offset * pairs + p))
 
     return pl.pallas_call(
-        functools.partial(attend_kernel, block=length // 2, use_mask=use_mask),
+        functools.partial(attend_kernel, use_mask=use_mask),
         grid_spec=pltpu.PrefetchScalarGridSpec(
             num_scalar_prefetch=1,
             grid=(count, pairs),
@@ -349,7 +367,7 @@
             jax.ShapeDtypeStruct((count, HEADS, length, length), jnp.bfloat16),
             jax.ShapeDtypeStruct((count, pairs, 2, length), jnp.float32),
         ],
-        compiler_params=pltpu.CompilerParams(vmem_limit_bytes=56 * 2**20),
+        compiler_params=pltpu.CompilerParams(vmem_limit_bytes=ATTEND_LIMIT),
         cost_estimate=pl.CostEstimate(
             flops=4 * count * HEADS * length * length * 256,
             bytes_accessed=count * HEADS * length * length * 2,
@@ -388,13 +406,17 @@
     dv_ref[0] = value_sum.astype(jnp.bfloat16)
 
 
-def attend_back(first, pairs_now, previous, queries, keys, values, offsets, *rest):
+def attend_back(place, size, previous, queries, keys, values, offsets, *rest):
     count, length = queries.shape[:2]
     pairs = HEADS * HEAD // 128
     width = HEADS * HEAD
 
+    start, first = place
+
     def spec(offset):
-        return pl.BlockSpec((1, length, 128), lambda s, p: (s, 0, offset * pairs + first + p))
+        return pl.BlockSpec(
+            (1, length, 128), lambda s, p: (start + s, 0, offset * pairs + first + p)
+        )
 
     kernel = attend_back_kernel
     aliases = {}
@@ -403,22 +425,22 @@
         aliases = {0: 0, 1: 1, 2: 2}
     return pl.pallas_call(
         kernel,
-        grid=(count, pairs_now),
+        grid=size,
         in_specs=[pl.BlockSpec(memory_space=pl.ANY)] * len(previous)
         + [spec(offset) for offset in offsets]
         + [
             spec(0),
             spec(0),
-            pl.BlockSpec((1, 2, length, length), lambda s, p: (s, first + p, 0, 0)),
-            pl.BlockSpec((1, 1, 2, length), lambda s, p: (s, first + p, 0, 0)),
+            pl.BlockSpec((1, 2, length, length), lambda s, p: (start + s, first + p, 0, 0)),
+            pl.BlockSpec((1, 1, 2, length), lambda s, p: (start + s, first + p, 0, 0)),
         ],
         out_specs=[spec(0)] * 3,
         out_shape=[jax.ShapeDtypeStruct((count, length, width), jnp.bfloat16)] * 3,
         input_output_aliases=aliases,
-        compiler_params=pltpu.CompilerParams(vmem_limit_bytes=56 * 2**20),
+        compiler_params=pltpu.CompilerParams(vmem_limit_bytes=ATTEND_LIMIT),
         cost_estimate=pl.CostEstimate(
-            flops=16 * count * pairs_now * length * length * 256,
-            bytes_accessed=4 * count * pairs_now * length * length,
+            flops=16 * size[0] * size[1] * length * length * 256,
+            bytes_accessed=4 * size[0] * size[1] * length * length,
             transcendentals=0,
         ),
         name="attend_back",
@@ -454,23 +476,170 @@
     return jnp.sum(values, axis=0, keepdims=True)
 
 
-def split_rows(core, rows, kept_ref, sent_ref):
+def resident(array):
+    return pl.BlockSpec(array.shape, lambda *_: (0,) * array.ndim, pipeline_mode=pl.Buffered(1))
+
+
+def whole_block(array):
+    return pl.BlockSpec(array.shape, lambda *_: (0,) * len(array.shape))
+
+
+def like(shape, dtype=jnp.float32):
+    return jax.ShapeDtypeStruct(tuple(shape), dtype)
+
+
+def pick(take_first, first_ref, second_ref):
+    return lax.cond(take_first, lambda: first_ref[...], lambda: second_ref[...])
+
+
+ONCE = {"pipeline_mode": pl.Buffered(1)}
+
+
+def own_spec(own, width, held, last, **more):
+    def place(step, info):
+        return (info[0] * held + jnp.minimum(step, last) // 2, 0, 0)
+
+    return pl.BlockSpec((None, own, width), place, **more)
+
+
+def got_spec(own, width, last, **more):
+    return pl.BlockSpec(
+        (None, own, width), lambda step, info: (jnp.minimum(step, last) // 2, 0, 0), **more
+    )
+
+
+def row_spec(own, width, last, **more):
+    return pl.BlockSpec((own, width), lambda step, info: (jnp.minimum(step, last), 0), **more)
+
+
+def kernel_call(kernel, name, info, arrays, in_specs, outs, out_specs, grid, flops, moved, **more):
+    scratch = more.pop("scratch", [])
+    return pl.pallas_call(
+        kernel,
+        grid_spec=pltpu.PrefetchScalarGridSpec(
+            num_scalar_prefetch=1,
+            grid=(grid,),
+            in_specs=in_specs,
+            out_specs=out_specs,
+            scratch_shapes=scratch,
+        ),
+        out_shape=outs,
+        compiler_params=pltpu.CompilerParams(
+            vmem_limit_bytes=more.pop("limit", 48) * 2**20
+        ),
+        cost_estimate=pl.CostEstimate(flops=flops, bytes_accessed=moved, transcendentals=0),
+        name=name,
+        **more,
+    )(info, *arrays)
+
+
+def enter_kernel(info_ref, own_ref, got_ref, w_ref, vec_ref, bias_ref, x_ref, out_ref, *, norm):
+    x = pick(pl.program_id(0) % 2 == 0, own_ref, got_ref)
+    x_ref[...] = x
+    if norm:
+        unit, _ = normal_parts(x.astype(jnp.float32))
+        x = (unit * vec_ref[0:1, :] + vec_ref[1:2, :]).astype(jnp.bfloat16)
+    width = x.shape[1]
+    for start in range(0, w_ref.shape[1], width):
+        part = slice(start, start + width)
+        total = contract(x, w_ref[:, part], 1, 0) + bias_ref[:, part]
+        if norm and start == 0:
+            total = total * (HEAD**-0.5)
+        out_ref[:, part] = total.astype(jnp.bfloat16)
+
+
+def enter(info, owns, gots, weight, vectors, bias, norm):
+    held, own, width = gots.shape
+    rows = 2 * held * own
+    last = 2 * held - 1
+    wide = weight.shape[1]
+    return kernel_call(
+        functools.partial(enter_kernel, norm=norm),
+        "enter",
+        info,
+        (owns, gots, weight, vectors, bias),
+        [own_spec(own, width, held, last), got_spec(own, width, last)]
+        + [resident(a) for a in (weight, vectors, bias)],
+        [like((rows, width), jnp.bfloat16), like((rows, wide), jnp.bfloat16)],
+        [row_spec(own, width, last), row_spec(own, wide, last)],
+        2 * held,
+        2 * rows * width * wide,
+        2 * rows * (2 * width + wide),
+    )
+
+
+def middle_kernel(info_ref, x_ref, mixed_ref, wo_ref, wq_ref, vec_ref, after_ref, q_ref):
+    out_bias, gain, shift, query_bias = (vec_ref[i : i + 1, :] for i in range(4))
+    after = (
+        x_ref[...].astype(jnp.float32) + contract(mixed_ref[...], wo_ref[...], 1, 0) + out_bias
+    )
+    after_ref[...] = after
+    unit, _ = normal_parts(after)
+    normal = (unit * gain + shift).astype(jnp.bfloat16)
+    queries = (contract(normal, wq_ref[...], 1, 0) + query_bias) * (HEAD**-0.5)
+    q_ref[...] = queries.astype(jnp.bfloat16)
+
+
+def middle(info, x, mixed, wo, wq, vectors, own):
+    rows, width = x.shape
+    last = rows // own - 1
+    spec = row_spec(own, width, last)
+    return kernel_call(
+        middle_kernel,
+        "middle",
+        info,
+        (x, mixed, wo, wq, vectors),
+        [spec, spec] + [resident(a) for a in (wo, wq, vectors)],
+        [like((rows, width)), like((rows, width), jnp.bfloat16)],
+        [spec, spec],
+        rows // own,
+        4 * rows * width * width,
+        10 * rows * width,
+    )
+
+
+def write_split(core, rows, kept_ref, sent_ref, start):
     half = rows.shape[0] // 2
     low = rows.astype(jnp.bfloat16)
+    place = slice(start, start + half)
 
     @pl.when(core == 0)
     def _():
-        kept_ref[0], sent_ref[0] = low[:half], low[half:]
+        kept_ref[0, place, :] = low[:half]
+        sent_ref[0, place, :] = low[half:]
 
     @pl.when(core != 0)
     def _():
-        kept_ref[0], sent_ref[0] = low[half:], low[:half]
+        kept_ref[0, place, :] = low[half:]
+        sent_ref[0, place, :] = low[:half]
+
+
+def acc_rows(ref, at, rows):
+    return ref[pl.ds(pl.multiple_of(at * rows, 16), rows), :]
+
+
+def piece(parts, high, wide, steps):
+    late = lambda g, info: (jnp.maximum(g - steps, 0), 0, 0)
+    return (
+        [pl.BlockSpec((1, high, wide), late)] * 2,
+        [like((parts // 2, high, wide), jnp.bfloat16)] * 2,
+    )
+
+
+def put_rows(step, value, own_ref, got_ref):
+    @pl.when(step % 2 == 0)
+    def _():
+        own_ref[...] = value.astype(own_ref.dtype)
+
+    @pl.when(step % 2 != 0)
+    def _():
+        got_ref[...] = value.astype(got_ref.dtype)
 
 
 def feed_kernel(
-    info_ref, x_ref, mixed_ref, dy_ref, wc_ref, wi_ref, wo_ref, vec_ref, bi_ref,
-    out_ref, dx_ref, do_ref, vsum_ref, bsum_ref, ki_ref, si_ref, ko_ref, so_ref, kc_ref, sc_ref,
-    ai_ref, ao_ref, ac_ref, *, steps, chunk,
+    info_ref, x_ref, mixed_ref, dyo_ref, dyg_ref, wc_ref, wi_ref, wo_ref, vec_ref, bi_ref,
+    own_ref, got_ref, dx_ref, do_ref, vsum_ref, bsum_ref, ki_ref, si_ref, ko_ref, so_ref,
+    ai_ref, ao_ref, ac_ref, *, steps, chunk, parts,
 ):
     step = pl.program_id(0)
 
@@ -487,7 +656,7 @@
         unit, inverse = normal_parts(x2)
         normal = (unit * gain + shift).astype(jnp.bfloat16)
         normal_turned = normal.T
-        dy = dy_ref[...]
+        dy = pick(step % 2 == 0, dyo_ref, dyg_ref)
         dy_turned = dy.T
         result, upstream = None, None
         for start in range(0, wi_ref.shape[1], chunk):
@@ -504,7 +673,7 @@
             upstream = up if upstream is None else upstream + up
             ao_ref[:, part] += contract(dy_turned, active, 1, 0)
             ai_ref[:, part] += contract(normal_turned, low, 1, 0)
-        out_ref[...] = (x2 + result + out_bias).astype(jnp.bfloat16)
+        put_rows(step, x2 + result + out_bias, own_ref, got_ref)
         wide = dy.astype(jnp.float32)
         dx = wide + normal_back(unit, inverse, gain, upstream)
         dx_ref[...] = dx
@@ -519,67 +688,243 @@
     @pl.when(step >= steps)
     def _():
         at = step - steps
-        core = info_ref[0]
+        core = info_ref[1]
         rows = 2 * ki_ref.shape[1]
-        split_rows(core, ai_ref[pl.ds(pl.multiple_of(at * rows, 16), rows), :], ki_ref, si_ref)
-        split_rows(core, ac_ref[pl.ds(pl.multiple_of(at * rows, 16), rows), :], kc_ref, sc_ref)
-        rows = 2 * ko_ref.shape[1]
-        columns = ao_ref[:, pl.ds(pl.multiple_of(at * rows, 128), rows)]
-        split_rows(core, columns.astype(jnp.bfloat16).T, ko_ref, so_ref)
-
-
-def resident(array):
-    return pl.BlockSpec(array.shape, lambda *_: (0,) * array.ndim, pipeline_mode=pl.Buffered(1))
-
-
-def feed(info, x1, mixed, dy, wc, wi, wo, vectors, bi, parts, block=512, chunk=768):
+        inner = 2 * ai_ref.shape[1] // parts
+        write_split(core, acc_rows(ai_ref, at, rows), ki_ref, si_ref, 0)
+        columns = ao_ref[:, pl.ds(pl.multiple_of(at * inner, 128), inner)]
+        write_split(core, columns.astype(jnp.bfloat16).T, ko_ref, so_ref, 0)
+        write_split(core, acc_rows(ac_ref, at, rows), ko_ref, so_ref, inner // 2)
+
+
+def feed(info, x1, mixed, dys, dy_gots, wc, wi, wo, vectors, bi, parts, chunk=768):
     rows, width = x1.shape
+    held, own = dy_gots.shape[:2]
+    micros = dys.shape[0]
     inner = wi.shape[1]
-    steps = rows // block
-    pairs = parts // 2
-    row = lambda g, info: (jnp.minimum(g, steps - 1), 0)
-    late = lambda g, info: (jnp.maximum(g - steps, 0), 0, 0)
-    row_spec = pl.BlockSpec((block, width), row)
-    fixed = lambda *_: (0, 0)
-
-    def piece(high, wide):
-        return (
-            [pl.BlockSpec((1, high // parts, wide), late)] * 2,
-            [jax.ShapeDtypeStruct((pairs, high // parts, wide), jnp.bfloat16)] * 2,
-        )
-
-    pieces = [piece(width, inner), piece(inner, width), piece(width, width)]
-    return pl.pallas_call(
-        functools.partial(feed_kernel, steps=steps, chunk=chunk),
-        grid_spec=pltpu.PrefetchScalarGridSpec(
-            num_scalar_prefetch=1,
-            grid=(steps + pairs,),
-            in_specs=[row_spec] * 3 + [resident(a) for a in (wc, wi, wo, vectors, bi)],
-            out_specs=[row_spec] * 3
-            + [pl.BlockSpec((8, width), fixed), pl.BlockSpec((1, inner), fixed)]
-            + sum([p[0] for p in pieces], []),
-            scratch_shapes=[
-                pltpu.VMEM((width, inner), jnp.float32),
-                pltpu.VMEM((width, inner), jnp.float32),
-                pltpu.VMEM((width, width), jnp.float32),
-            ],
-        ),
-        out_shape=[
-            jax.ShapeDtypeStruct((rows, width), jnp.bfloat16),
-            jax.ShapeDtypeStruct((rows, width), jnp.float32),
-            jax.ShapeDtypeStruct((rows, width), jnp.bfloat16),
-            jax.ShapeDtypeStruct((8, width), jnp.float32),
-            jax.ShapeDtypeStruct((1, inner), jnp.float32),
+    steps = 2 * held
+    last = steps - 1
+    row = row_spec(own, width, last)
+    pieces = [
+        piece(parts, width // parts, inner, steps),
+        piece(parts, (inner + width) // parts, width, steps),
+    ]
+    sums = [like((8, width)), like((1, inner))]
+    return kernel_call(
+        functools.partial(feed_kernel, steps=steps, chunk=chunk, parts=parts),
+        "feed",
+        info,
+        (x1, mixed, dys, dy_gots, wc, wi, wo, vectors, bi),
+        [row_spec(own, width, last, **ONCE)] * 2
+        + [own_spec(own, width, held, last, **ONCE), got_spec(own, width, last, **ONCE)]
+        + [resident(a) for a in (wc, wi, wo, vectors, bi)],
+        [
+            like((micros, own, width), jnp.bfloat16),
+            like((held, own, width), jnp.bfloat16),
+            like((rows, width)),
+            like((rows, width), jnp.bfloat16),
+        ]
+        + sums
+        + sum([p[1] for p in pieces], []),
+        [own_spec(own, width, held, last), got_spec(own, width, last), row, row]
+        + [whole_block(a) for a in sums]
+        + sum([p[0] for p in pieces], []),
+        steps + parts // 2,
+        2 * rows * width * (6 * inner + 3 * width),
+        60 * 2**20,
+        scratch=[
+            pltpu.VMEM((width, inner), jnp.float32),
+            pltpu.VMEM((width, inner), jnp.float32),
+            pltpu.VMEM((width, width), jnp.float32),
+        ],
+        limit=62,
+    )
+
+
+def return_kernel(
+    info_ref, dq_ref, dk_ref, dv_ref, x_ref, dx_ref, mixed_ref, src_ref, wq_ref, wi_ref, wo_ref,
+    vec_ref, own_ref, got_ref, dxo_ref, do_ref, vsum_ref, ka_ref, sa_ref, kb_ref, sb_ref,
+    aq_ref, ao_ref, ai_ref, *, steps,
+):
+    step = pl.program_id(0)
+
+    @pl.when(step == 0)
+    def _():
+        for ref in (vsum_ref, aq_ref, ao_ref, ai_ref):
+            ref[...] = jnp.zeros_like(ref)
+
+    @pl.when(step < steps)
+    def _():
+        width = x_ref.shape[1]
+        gain, shift = vec_ref[0:1, :], vec_ref[1:2, :]
+        dq, dk, dv = dq_ref[...], dk_ref[...], dv_ref[...]
+        upstream = contract(dq, wq_ref[...], 1, 1)
+        unit, inverse = normal_parts(x_ref[...])
+        normal = (unit * gain + shift).astype(jnp.bfloat16)
+        dx = dx_ref[...] + normal_back(unit, inverse, gain, upstream)
+        dxo_ref[...] = dx
+        low = dx.astype(jnp.bfloat16)
+        do_ref[...] = contract(low, wo_ref[...], 1, 1).astype(jnp.bfloat16)
+        source = contract(dk, wi_ref[:, :width], 1, 1) + contract(dv, wi_ref[:, width:], 1, 1)
+        put_rows(step, source, own_ref, got_ref)
+        aq_ref[...] += contract(normal.T, dq, 1, 0)
+        ao_ref[...] += contract(mixed_ref[...].T, low, 1, 0)
+        turned = src_ref[...].T
+        ai_ref[:, :width] += contract(turned, dk, 1, 0)
+        ai_ref[:, width:] += contract(turned, dv, 1, 0)
+        vsum_ref[0:1, :] += column_sum(upstream * unit)
+        vsum_ref[1:2, :] += column_sum(upstream)
+        vsum_ref[2:3, :] += column_sum(dx)
+        vsum_ref[3:4, :] += column_sum(dq.astype(jnp.float32))
+        vsum_ref[4:5, :] += column_sum(dv.astype(jnp.float32))
+
+    @pl.when(step >= steps)
+    def _():
+        at = step - steps
+        core = info_ref[1]
+        rows = 2 * ka_ref.shape[1]
+        write_split(core, acc_rows(ai_ref, at, rows), ka_ref, sa_ref, 0)
+        write_split(core, acc_rows(aq_ref, at, rows), kb_ref, sb_ref, 0)
+        write_split(core, acc_rows(ao_ref, at, rows), kb_ref, sb_ref, rows // 2)
+
+
+def return_rows(info, grads, x1, dx2, mixed, sources, wq, wi, wo, vectors, own, micros, parts):
+    rows, width = x1.shape
+    held = rows // own // 2
+    steps = 2 * held
+    last = steps - 1
+    row = row_spec(own, width, last)
+    pieces = [
+        piece(parts, width // parts, 2 * width, steps),
+        piece(parts, 2 * width // parts, width, steps),
+    ]
+    sums = like((8, width))
+    return kernel_call(
+        functools.partial(return_kernel, steps=steps),
+        "return_rows",
+        info,
+        (*grads, x1, dx2, mixed, sources, wq, wi, wo, vectors),
+        [row] * 7 + [resident(a) for a in (wq, wi, wo, vectors)],
+        [
+            like((micros, own, width)),
+            like((held, own, width), jnp.bfloat16),
+            like((rows, width)),
+            like((rows, width), jnp.bfloat16),
+            sums,
         ]
         + sum([p[1] for p in pieces], []),
-        compiler_params=pltpu.CompilerParams(vmem_limit_bytes=60 * 2**20),
-        cost_estimate=pl.CostEstimate(
-            flops=2 * rows * width * (6 * inner + 3 * width),
-            bytes_accessed=60 * 2**20,
-            transcendentals=rows * inner,
-        ),
-        name="feed",
-    )(info, x1, mixed, dy, wc, wi, wo, vectors, bi)
+        [own_spec(own, width, held, last), got_spec(own, width, last), row, row, whole_block(sums)]
+        + sum([p[0] for p in pieces], []),
+        steps + parts // 2,
+        16 * rows * width * width,
+        40 * 2**20,
+        scratch=[
+            pltpu.VMEM((width, width), jnp.float32),
+            pltpu.VMEM((width, width), jnp.float32),
+            pltpu.VMEM((width, 2 * width), jnp.float32),
+        ],
+        limit=56,
+    )
+
+
+def last_weight_kernel(
+    info_ref, dq_ref, dk_ref, dv_ref, x_ref, vec_ref, ka_ref, sa_ref, kb_ref, sb_ref, acc_ref,
+    *, steps,
+):
+    step = pl.program_id(0)
+
+    @pl.when(step == 0)
+    def _():
+        acc_ref[...] = jnp.zeros_like(acc_ref)
+
+    @pl.when(step < steps)
+    def _():
+        unit, _ = normal_parts(x_ref[...].astype(jnp.float32))
+        turned = (unit * vec_ref[0:1, :] + vec_ref[1:2, :]).astype(jnp.bfloat16).T
+        width = x_ref.shape[1]
+        for at, ref in enumerate((dq_ref, dk_ref, dv_ref)):
+            acc_ref[:, at * width : (at + 1) * width] += contract(turned, ref[...], 1, 0)
+
+    @pl.when(step >= steps)
+    def _():
+        rows = acc_rows(acc_ref, step - steps, 2 * ka_ref.shape[1])
+        half = ka_ref.shape[2]
+        write_split(info_ref[1], rows[:, :half], ka_ref, sa_ref, 0)
+        write_split(info_ref[1], rows[:, half:], kb_ref, sb_ref, 0)
+
+
+def last_weight(info, grads, x, vectors, own, parts):
+    rows, width = x.shape
+    steps = rows // own
+    row = row_spec(own, width, steps - 1)
+    pieces = [piece(parts, width // parts, 3 * width // 2, steps)] * 2
+    return kernel_call(
+        functools.partial(last_weight_kernel, steps=steps),
+        "last_weight",
+        info,
+        (*grads, x, vectors),
+        [row] * 4 + [resident(vectors)],
+        sum([p[1] for p in pieces], []),
+        sum([p[0] for p in pieces], []),
+        steps + parts // 2,
+        6 * rows * width * width,
+        20 * 2**20,
+        scratch=[pltpu.VMEM((width, 3 * width), jnp.float32)],
+    )
+
+
+def leave_kernel(
+    info_ref, dq_ref, dk_ref, dv_ref, x_ref, dx_ref, w_ref, vec_ref, *refs
+):
+    own_ref, got_ref, vsum_ref = refs[-3:]
+    step = pl.program_id(0)
+
+    @pl.when(step == 0)
+    def _():
+        vsum_ref[...] = jnp.zeros_like(vsum_ref)
+
+    width = x_ref.shape[1]
+    dq, dk, dv = dq_ref[...], dk_ref[...], dv_ref[...]
+    upstream = (
+        contract(dq, w_ref[:, :width], 1, 1)
+        + contract(dk, w_ref[:, width : 2 * width], 1, 1)
+        + contract(dv, w_ref[:, 2 * width :], 1, 1)
+    )
+    unit, inverse = normal_parts(x_ref[...].astype(jnp.float32))
+    dx = dx_ref[...] + normal_back(unit, inverse, vec_ref[0:1, :], upstream)
+    put_rows(step, dx, own_ref, got_ref)
+    vsum_ref[0:1, :] += column_sum(upstream * unit)
+    vsum_ref[1:2, :] += column_sum(upstream)
+    vsum_ref[2:3, :] += column_sum(dq.astype(jnp.float32))
+    vsum_ref[3:4, :] += column_sum(dv.astype(jnp.float32))
+
+
+def leave(info, at, previous, grads, x, dx1, weight, vectors, own, micros):
+    rows, width = x.shape
+    held = rows // own // 2
+    row = pl.BlockSpec((own, width), lambda step, info: (2 * at + step, 0))
+    more = {"input_output_aliases": {8: 0}} if previous else {}
+    sums = like((8, width))
+    return kernel_call(
+        leave_kernel,
+        "leave",
+        info,
+        (*grads, x, dx1, weight, vectors, *previous),
+        [row] * 5
+        + [resident(a) for a in (weight, vectors)]
+        + [pl.BlockSpec(memory_space=pl.ANY)] * len(previous),
+        [like((micros, own, width)), like((own, width), jnp.bfloat16), sums],
+        [
+            pl.BlockSpec((None, own, width), lambda step, info: (info[0] * held + at, 0, 0)),
+            pl.BlockSpec((own, width), lambda step, info: (0, 0)),
+            whole_block(sums),
+        ],
+        2,
+        12 * own * width * width,
+        16 * 2**20,
+        **more,
+    )
+
 
 SWAP = ((0, 1), (1, 0))
 
@@ -630,17 +975,6 @@
 def second_first(bits):
     turned = bits[::-1]
     return turned[1:2] + turned[:1] + turned[2:]
-
-
-def tree_of(total, order):
-    count = lax.axis_size("dp")
-    blocks = total.astype(jnp.bfloat16).reshape((count // 2, 2, total.shape[0] // count, -1))
-    core = lax.axis_index("dp") % 2
-    return Tree(
-        lax.dynamic_index_in_dim(blocks, core, 1, keepdims=False),
-        lax.dynamic_index_in_dim(blocks, 1 - core, 1, keepdims=False),
-        order,
-    )
 
 
 def exchange(trees):
@@ -694,163 +1028,175 @@
     micros, _, own, width = targets.shape
     held = micros // 2
     side = lax.axis_index("seq")
-    query_scale = HEAD ** (-0.5)
-
-    def take(rows):
-        kept = lax.dynamic_slice_in_dim(rows, side * held, held, axis=0)
+    parts = lax.axis_size("dp")
+    place = lax.axis_index("dp")
+    length = 2 * own
+    pairs = HEADS * HEAD // 128
+
+    def swap(rows):
         sent = lax.dynamic_slice_in_dim(rows, (1 - side) * held, held, axis=0)
-        got = lax.ppermute(sent, "seq", SWAP)
-        return jnp.concatenate([kept[:, 0], got[:, 0]], axis=1)
-
-    def give(rows, dtype):
-        got = lax.ppermute(rows[:, own:].astype(jnp.bfloat16), "seq", SWAP).astype(dtype)
-        kept = rows[:, :own].astype(dtype)
-        first = jnp.where(side == 0, kept, got)
-        second = jnp.where(side == 0, got, kept)
-        return jnp.concatenate([first, second], axis=0)[:, None]
-
-    inputs = take(targets).astype(jnp.float32)
-    sources = take(memory)
-    output_low = take(
-        (cotangent.astype(jnp.float32) * loss_mask.astype(jnp.float32)[..., None]).astype(
-            jnp.bfloat16
-        )
-    )
+        return lax.ppermute(sent, "seq", SWAP)
+
+    def give(owns, got, at):
+        got = lax.ppermute(got, "seq", SWAP).astype(owns.dtype)
+        return lax.dynamic_update_slice_in_dim(owns, got, (1 - side) * held + at, axis=0)
+
+    def pack(*rows):
+        zero = jnp.zeros((8 - len(rows), width), jnp.float32)
+        return jnp.concatenate([jnp.stack(rows), zero])
+
+    def batch(rows):
+        return rows.reshape(held, length, -1)
+
+    def flat(rows):
+        return rows.reshape(held * length, -1)
+
+    targets, memory = targets[:, 0], memory[:, 0]
+    target_gots = swap(targets)
+    memory_gots = swap(memory)
+    upstreams = (
+        cotangent[:, 0].astype(jnp.float32) * loss_mask[:, 0].astype(jnp.float32)[..., None]
+    ).astype(jnp.bfloat16)
+    upstream_gots = swap(upstreams)
     kinds = lax.dynamic_slice_in_dim(row_kind[:, 0], side * held, held, axis=0)
-    info = jnp.concatenate([side[None].astype(jnp.int32), kinds])
-
-    first_normed = normed(inputs, norm_self_gain, norm_self_bias).astype(jnp.bfloat16)
-    joint_bias = jnp.concatenate(
-        [self_query_bias, jnp.zeros_like(self_query_bias), self_value_bias]
-    )
-    joint_scale = jnp.where(jnp.arange(3 * width) < width, query_scale, 1.0)
-    joint = ((project_rows(first_normed, self_input) + joint_bias) * joint_scale).astype(
-        jnp.bfloat16
-    )
+    info = jnp.concatenate([jnp.stack([side, place % 2]).astype(jnp.int32), kinds])
+
+    self_vectors = pack(norm_self_gain, norm_self_bias)
+    zero = jnp.zeros_like(self_query_bias)
+    joint_bias = jnp.concatenate([self_query_bias, zero, self_value_bias])[None]
+    inputs, joint = enter(
+        info, targets, target_gots, self_input, self_vectors, joint_bias, True
+    )
+    joint = batch(joint)
     self_mixed, self_raised, self_inverse = attend(info, joint, joint, joint, True, (0, 1, 2))
-    after_self = inputs + project_rows(self_mixed, self_output) + self_output_bias
-    second_normed = normed(after_self, norm_cross_gain, norm_cross_bias).astype(jnp.bfloat16)
-    cross_queries = (
-        (project_rows(second_normed, cross_query) + cross_query_bias) * query_scale
-    ).astype(jnp.bfloat16)
-    pair_bias = jnp.concatenate([jnp.zeros_like(cross_value_bias), cross_value_bias])
-    cross_pairs = (project_rows(sources, cross_input) + pair_bias).astype(jnp.bfloat16)
+    after_self, cross_queries = middle(
+        info,
+        inputs,
+        flat(self_mixed),
+        self_output,
+        cross_query,
+        pack(self_output_bias, norm_cross_gain, norm_cross_bias, cross_query_bias),
+        own,
+    )
+    pair_bias = jnp.concatenate([zero, cross_value_bias])[None]
+    sources, cross_pairs = enter(
+        info, memory, memory_gots, cross_input, self_vectors, pair_bias, False
+    )
+    cross_queries, cross_pairs = batch(cross_queries), batch(cross_pairs)
     cross_mixed, cross_raised, cross_inverse = attend(
         info, cross_queries, cross_pairs, cross_pairs, False, (0, 0, 1)
     )
-    vectors = jnp.concatenate(
-        [
-            jnp.stack([cross_output_bias, norm_feed_gain, norm_feed_bias, feed_out_bias]),
-            jnp.zeros((4, width), jnp.float32),
-        ]
-    )
-    flat = lambda rows: rows.reshape(-1, width)
-    result, grad_cross, cross_upstream, vector_sums, hidden_sums, *feed_parts = feed(
-        (lax.axis_index("dp") % 2)[None].astype(jnp.int32),
-        flat(after_self),
+    results, result_gots, grad_cross, cross_upstream, feed_sums, hidden_sums, *feed_parts = feed(
+        info,
+        after_self,
         flat(cross_mixed),
-        flat(output_low),
+        upstreams,
+        upstream_gots,
         cross_output,
         feed_in,
         feed_out,
-        vectors,
+        pack(cross_output_bias, norm_feed_gain, norm_feed_bias, feed_out_bias),
         feed_in_bias[None],
-        lax.axis_size("dp"),
-    )
-    result, grad_cross, cross_upstream = (
-        rows.reshape(inputs.shape) for rows in (result, grad_cross, cross_upstream)
-    )
-    pieces = [None] * 21
-    pieces[14], pieces[15], pieces[16], pieces[20] = vector_sums[:4]
-    pieces[18] = hidden_sums[0]
-    feed_trees = [
-        Tree(*feed_parts[0:2], low_first),
-        Tree(*feed_parts[2:4], second_first),
-        Tree(*feed_parts[4:6], low_first),
-    ]
-    pairs = HEADS * HEAD // 128
+        parts,
+    )
+    feed_trees = [Tree(*feed_parts[0:2], low_first), Tree(*feed_parts[2:4], second_first)]
     first = pairs // 2
     cross_inputs = (
-        cross_queries, cross_pairs, cross_pairs, (0, 0, 1), cross_mixed, cross_upstream,
+        cross_queries, cross_pairs, cross_pairs, (0, 0, 1), cross_mixed, batch(cross_upstream),
         cross_raised, cross_inverse,
     )
     exchange(feed_trees)
-    half_grads = attend_back(0, first, (), *cross_inputs)
-    half_grads = settle(feed_trees, half_grads)
+    half_grads = settle(feed_trees, attend_back((0, 0), (held, first), (), *cross_inputs))
     exchange(feed_trees)
-    scaled_cross, cross_key_grads, cross_value_grads = settle(
-        feed_trees, attend_back(first, pairs - first, half_grads, *cross_inputs)
+    cross_grads = settle(
+        feed_trees, attend_back((0, first), (held, pairs - first), half_grads, *cross_inputs)
     )
     exchange(feed_trees)
-    pair_grads = jnp.concatenate([cross_key_grads, cross_value_grads], axis=-1)
-    pieces[12] = jnp.sum(cross_value_grads.astype(jnp.float32), axis=(0, 1))
-    pieces[11] = outer_sum(sources, pair_grads)
-    source_grad = project_back(pair_grads, cross_input)
-    pieces[10] = jnp.sum(scaled_cross.astype(jnp.float32), axis=(0, 1))
-    pieces[9] = outer_sum(second_normed, scaled_cross)
-    through_cross, pieces[7], pieces[8] = normed_back(
-        after_self, norm_cross_gain, norm_cross_bias, project_back(scaled_cross, cross_query)
-    )
-    grad_self = grad_cross + through_cross
-    self_low = grad_self.astype(jnp.bfloat16)
-    pieces[5] = outer_sum(self_mixed, self_low)
-    pieces[6] = jnp.sum(grad_self, axis=(0, 1))
-    self_upstream = project_back(self_low, self_output).astype(jnp.bfloat16)
-    pieces[5], pieces[9], pieces[11], self_upstream, source_grad = settle(
-        feed_trees, (pieces[5], pieces[9], pieces[11], self_upstream, source_grad)
-    )
-    exchange(feed_trees)
-    mid_trees = [
-        tree_of(pieces[11], low_first),
-        tree_of(pieces[9], second_first),
-        tree_of(pieces[5], second_first),
+    source_grads, source_gots, grad_self, self_upstream, return_sums, *mid_parts = settle(
+        feed_trees,
+        return_rows(
+            info,
+            [flat(rows) for rows in cross_grads],
+            after_self,
+            grad_cross,
+            flat(self_mixed),
+            sources,
+            cross_query,
+            cross_input,
+            self_output,
+            pack(norm_cross_gain, norm_cross_bias),
+            own,
+            micros,
+            parts,
+        ),
+    )
+    mid_trees = [Tree(*mid_parts[0:2], low_first), Tree(*mid_parts[2:4], second_first)]
+    exchange(feed_trees + mid_trees)
+    self_inputs = (
+        joint, joint, joint, (0, 1, 2), self_mixed, batch(self_upstream), self_raised, self_inverse
+    )
+    grads = settle(feed_trees + mid_trees, attend_back((0, 0), (1, pairs), (), *self_inputs))
+    exchange(feed_trees + mid_trees)
+    input_grads, leave_sums, leave_gots = (), [], []
+
+    def leave_one(at, grads, input_grads):
+        input_grads, got, sums = leave(
+            info, at, input_grads, [flat(rows) for rows in grads], inputs, grad_self,
+            self_input, self_vectors, own, micros,
+        )
+        leave_sums.append(sums)
+        leave_gots.append(got[None])
+        return (input_grads,)
+
+    for at in range(held - 1):
+        input_grads = leave_one(at, grads, input_grads)
+        grads, input_grads = lax.optimization_barrier((grads, input_grads))
+        grads = settle(
+            feed_trees + mid_trees, attend_back((at + 1, 0), (1, pairs), grads, *self_inputs)
+        )
+        exchange(feed_trees + mid_trees)
+    late_parts = last_weight(
+        info, [flat(rows) for rows in grads], inputs, self_vectors, own, parts
+    )
+    late_trees = [Tree(*late_parts[0:2], low_first), Tree(*late_parts[2:4], second_first)]
+    exchange(late_trees)
+    grads, _ = lax.optimization_barrier((grads, late_parts[0]))
+    (input_grads,) = leave_one(held - 1, grads, input_grads)
+    leave_sums = sum(leave_sums)
+    small = [
+        (0, leave_sums[0]), (1, leave_sums[1]), (3, leave_sums[2]), (4, leave_sums[3]),
+        (6, return_sums[2]), (7, return_sums[0]), (8, return_sums[1]), (10, return_sums[3]),
+        (12, return_sums[4]), (14, feed_sums[0]), (15, feed_sums[1]), (16, feed_sums[2]),
+        (20, feed_sums[3]), (18, hidden_sums[0]),
     ]
-    exchange(mid_trees)
-    self_inputs = (
-        joint, joint, joint, (0, 1, 2), self_mixed, self_upstream, self_raised, self_inverse
-    )
-    half_grads = settle(feed_trees + mid_trees, attend_back(0, first, (), *self_inputs))
-    exchange(feed_trees + mid_trees)
-    joint_grads = settle(
-        feed_trees + mid_trees, attend_back(first, pairs - first, half_grads, *self_inputs)
-    )
-    exchange(mid_trees)
-    pieces[3] = jnp.sum(joint_grads[0].astype(jnp.float32), axis=(0, 1))
-    pieces[4] = jnp.sum(joint_grads[2].astype(jnp.float32), axis=(0, 1))
-    joint_low = jnp.concatenate(joint_grads, axis=-1)
-    pieces[2] = outer_sum(first_normed, joint_low)
-    late_trees = [
-        tree_of(pieces[2][:, : 3 * width // 2], low_first),
-        tree_of(pieces[2][:, 3 * width // 2 :], second_first),
-    ]
-    exchange(late_trees)
-    through_first, pieces[0], pieces[1] = normed_back(
-        inputs, norm_self_gain, norm_self_bias, project_back(joint_low, self_input)
-    )
-    input_grad = grad_self + through_first
-    count = lax.axis_size("dp")
-    small = []
-    for index, piece in enumerate(pieces):
-        if piece is not None and piece.ndim == 1:
-            small.append((index, piece.reshape(count, -1)))
-    joined = jnp.concatenate([part for _, part in small], axis=1)
-    late_trees.append(tree_of(joined, low_first))
-    finish(feed_trees + mid_trees + late_trees[:2])
-    finish(late_trees[2:])
+    joined = jnp.concatenate([row.reshape(parts, -1) for _, row in small], axis=1)
+    halves = joined.astype(jnp.bfloat16).reshape(parts // 2, 2, 1, -1)
+    small_tree = Tree(
+        lax.dynamic_index_in_dim(halves, place % 2, 1, keepdims=False),
+        lax.dynamic_index_in_dim(halves, 1 - place % 2, 1, keepdims=False),
+        low_first,
+    )
+    finish(feed_trees + mid_trees + late_trees)
+    finish([small_tree])
+    rows = width // parts
     final = [None] * 21
-    for index, tree in zip((17, 19, 13, 11, 9, 5), feed_trees + mid_trees):
-        final[index] = tree.total
-    final[2] = jnp.concatenate([late_trees[0].total, late_trees[1].total], axis=1)
-    joined = late_trees[2].total
-    place = 0
-    for index, part in small:
-        final[index] = joined[0, place : place + part.shape[1]]
-        place += part.shape[1]
-    return (
-        give(result, jnp.bfloat16),
-        give(input_grad, jnp.float32),
-        give(source_grad, jnp.float32),
-    ) + tuple(final)
+    for index, row in small:
+        size = row.shape[0] // parts
+        final[index] = small_tree.total[0, :size]
+        small_tree.total = small_tree.total[:, size:]
+    inner_rows = feed_in.shape[1] // parts
+    final[17] = feed_trees[0].total
+    final[19] = feed_trees[1].total[:inner_rows]
+    final[13] = feed_trees[1].total[inner_rows:]
+    final[11] = mid_trees[0].total
+    final[9] = mid_trees[1].total[:rows]
+    final[5] = mid_trees[1].total[rows:]
+    final[2] = jnp.concatenate([tree.total for tree in late_trees], axis=1)
+    results = give(results, result_gots, 0)
+    source_grads = give(source_grads, source_gots, 0)
+    for at in range(held):
+        input_grads = give(input_grads, leave_gots[at], at)
+    return (results[:, None], input_grads[:, None], source_grads[:, None]) + tuple(final)
 
 
 def solution(mesh):

time: 699 us -> 622 us (0.89)
  Pallas kernels: 284 us -> 412 us
  matrix products: 93.6 us -> 0 us
  other arithmetic: 83.7 us -> 30.5 us
  waiting for transfers between devices: 94.8 us -> 58.4 us
  starting transfers between devices: 64.4 us -> 46.3 us
    pallas_call x7 -> x14, Pallas kernels: 284 us -> 412 us  [the longest x8 224 us: kernel_call(): pl.pallas_call(kernel, grid_spec=pltpu.PrefetchScalarGridSpec(num_scalar_...]
    dot_general x12 -> x0, matrix products: 93.6 us -> none  [the longest x4 32.7 us: outer_sum(): jnp.einsum('bpd,bpe->de', first_rows, second_rows, preferred_element_type...]
    reduce_sum x10 -> x0, other arithmetic: 24.2 us -> none  [the longest x2 8.08 us: normed(): return center * lax.rsqrt(spread + epsilon) * norm_gain + norm_shift]
    ppermute x6 -> x7, waiting for transfers between devices: 43.1 us -> 26.6 us  [the longest x3 26.6 us: swap(): return lax.ppermute(sent, 'seq', SWAP)]
    ppermute x36 -> x28, waiting for transfers between devices: 41.5 us -> 27.8 us  [exchange(): self.got = lax.ppermute(self.sent, 'dp', pairs)]
    ppermute x36 -> x28, starting transfers between devices: 40.9 us -> 30.2 us  [exchange(): self.got = lax.ppermute(self.sent, 'dp', pairs)]
    unnamed x185 -> x149, local copies, waits for them, and re-layouts: 16.3 us -> 26.5 us
    unnamed x6 -> x0, other arithmetic: 8.41 us -> none
  transfers between devices with their start and end apart: 51 -> 42, of which waited for: 17 -> 15; matrix products, arithmetic and copies ran while one was open for 19% -> 9% of each run, Pallas kernels for 27% -> 49%
where the time goes in v3:
time: 622 us; the launch traced here: 616 us
  Pallas kernels  412 us (66%)
  local copies, waits for them, and re-layouts  67.4 us (11%)
  waiting for transfers between devices  58.4 us (9%)
  starting transfers between devices  46.3 us (7%)
  other arithmetic  30.5 us (5%)
    pallas_call x8, Pallas kernels, kernel_call(): pl.pallas_call(kernel, grid_spec=pltpu.PrefetchScalarGridSpec(num_scalar_...  224 us
    pallas_call x4, Pallas kernels, attend_back(): pl.pallas_call(kernel, grid=size, in_specs=[pl.BlockSpec(memory_space=pl....  124 us
    pallas_call x2, Pallas kernels, attend(): pl.pallas_call(functools.partial(attend_kernel, use_mask=use_mask), grid_...  63.6 us
    ppermute x28, starting transfers between devices, exchange(): self.got = lax.ppermute(self.sent, 'dp', pairs)  30.2 us
    ppermute x28, waiting for transfers between devices, exchange(): self.got = lax.ppermute(self.sent, 'dp', pairs)  27.8 us
    ppermute x3, waiting for transfers between devices, swap(): return lax.ppermute(sent, 'seq', SWAP)  26.6 us
    unnamed x149, local copies, waits for them, and re-layouts  26.5 us
    convert_element_type x28, other arithmetic, add(): self.kept = total.astype(jnp.bfloat16)  16.8 us
  transfers between devices with their start and end apart: 42, of which 15 were waited for; matrix products, arithmetic and copies ran while one was open for 9% of the time, Pallas kernels for 49%

profile of v3, /device:TPU:0, one launch (start us, length us, event | category | flops | bytes accessed | tf_op | source)
XLA Modules:
  0.0 616.4 jit_solution(425429327817497644)
XLA Ops:
  0.7 2.8 dynamic-slice_bitcast_fusion.1
  3.5 3.0 collective-permute-start
  8.4 1.7 copy-done.31
  11.4 2.0 collective-permute-start.2
  15.4 26.5 %collective-permute-done.got_ref = bf16[2,512,768]{2,1,0:T(8,128)(2,1)S(1)} collective-permute-done((bf16[2,512,768]{2,1,0:T(8,128)(2,1)}, bf16[2,512,768]{2,1,0:T(8,128)(2,1)S(1)}, u32[]{:S(2)}, u32[]{:S(2)}) %collective-permute-start) | collective-permute-done | bytes 1572896 | tf_op jit(solution)/shard_map/ppermute | solution.py:1038
  41.9 14.9 %enter.2 = (bf16[2048,768]{1,0:T(8,128)(2,1)S(1)}, bf16[2048,2304]{1,0:T(8,128)(2,1)}) custom-call(s32[4]{0:T(128)S(1)} %pad_add_fusion.info_ref, bf16[4,512,768]{2,1,0:T(8,128)(2,1)} %bitcast.273, bf16[2,512,768]{2,1,0:T(8,128)(2,1)S(1)} %collective-permute-done.got_ref, bf16[768,2304]{1,0:T(8,128)(2,1)} %w_ref.7, f32[8,768]{1,0:T(8,128)S(1)} %get-tuple-element.301.vec_ref, ...), custom_call_target="tpu_custom_call" | custom-call | flops 7247757312 | bytes 15728640 | tf_op jit(solution)/shard_map/enter/pallas_call | solution.py:517
  56.8 1.6 copy-done.2
  58.4 3.7 copy-done.20
  62.1 31.8 %attend.2 = (bf16[2,1024,768]{2,1,0:T(8,128)(2,1)S(1)}, bf16[2,12,1024,1024]{3,2,1,0:T(8,128)(2,1)}, f32[2,6,2,1024]{3,2,1,0:T(2,128)S(1)}) custom-call(s32[4]{0:T(128)S(1)} %pad_add_fusion.info_ref, bf16[2,1024,2304]{2,1,0:T(8,128)(2,1)S(1)} %bitcast.245, bf16[2,1024,2304]{2,1,0:T(8,128)(2,1)S(1)} %bitcast.246, bf16[2,1024,2304]{2,1,0:T(8,128)(2,1)S(1)} %bitcast.247), custom_call_target="tpu_custom_call" | custom-call | flops 25769803776 | bytes 50331648 | tf_op jit(solution)/shard_map/attend/pallas_call | solution.py:353
  93.9 1.6 copy-done.22
  95.5 10.8 %middle.1 = (f32[2048,768]{1,0:T(8,128)}, bf16[2048,768]{1,0:T(8,128)(2,1)S(1)}) custom-call(s32[4]{0:T(128)S(1)} %pad_add_fusion.info_ref, bf16[2048,768]{1,0:T(8,128)(2,1)} %copy-done.2, bf16[2048,768]{1,0:T(8,128)(2,1)} %bitcast.254, bf16[768,768]{1,0:T(8,128)(2,1)S(1)} %copy-done.16, bf16[768,768]{1,0:T(8,128)(2,1)S(1)} %copy-done.17, ...), custom_call_target="tpu_custom_call" | custom-call | flops 4831838208 | bytes 15728640 | tf_op jit(solution)/shard_map/middle/pallas_call | solution.py:517
  106.4 10.9 %enter.3 = (bf16[2048,768]{1,0:T(8,128)(2,1)}, bf16[2048,1536]{1,0:T(8,128)(2,1)}) custom-call(s32[4]{0:T(128)S(1)} %pad_add_fusion.info_ref, bf16[4,512,768]{2,1,0:T(8,128)(2,1)} %bitcast.274, bf16[2,512,768]{2,1,0:T(8,128)(2,1)} %collective-permute-done.1.got_ref, bf16[768,1536]{1,0:T(8,128)(2,1)S(1)} %copy-done.15, ...), custom_call_target="tpu_custom_call" | custom-call | flops 4831838208 | bytes 12582912 | tf_op jit(solution)/shard_map/enter/pallas_call | solution.py:517
  117.2 2.8 copy-done.21
  120.0 31.8 %attend.3 = (bf16[2,1024,768]{2,1,0:T(8,128)(2,1)S(1)}, bf16[2,12,1024,1024]{3,2,1,0:T(8,128)(2,1)}, f32[2,6,2,1024]{3,2,1,0:T(2,128)S(1)}) custom-call(s32[4]{0:T(128)S(1)} %pad_add_fusion.info_ref, bf16[2,1024,768]{2,1,0:T(8,128)(2,1)S(1)} %bitcast.256, bf16[2,1024,1536]{2,1,0:T(8,128)(2,1)S(1)} %bitcast.252, bf16[2,1024,1536]{2,1,0:T(8,128)(2,1)S(1)} %bitcast.253), custom_call_target="tpu_custom_call" | custom-call | flops 25769803776 | bytes 50331648 | tf_op jit(solution)/shard_map/attend/pallas_call | solution.py:353
  151.9 1.6 copy-done.27
  153.5 109.5 %feed.1 = (bf16[4,512,768]{2,1,0:T(8,128)(2,1)}, bf16[2,512,768]{2,1,0:T(8,128)(2,1)}, f32[2048,768]{1,0:T(8,128)}, bf16[2048,768]{1,0:T(8,128)(2,1)}, f32[8,768...) custom-call(s32[4]{0:T(128)} %copy-done.13, ...), custom_call_target="tpu_custom_call" | custom-call | flops 65229815808 | bytes 62914560 | tf_op jit(solution)/shard_map/feed/pallas_call | solution.py:517
  263.0 3.7 copy.59
  266.7 1.8 collective-permute-start.3
  268.5 3.4 copy.58
  275.6 31.0 %attend_back.4 = (bf16[2,1024,768]{2,1,0:T(8,128)(2,1)S(1)}, bf16[2,1024,768]{2,1,0:T(8,128)(2,1)S(1)}, bf16[2,1024,768]{2,1,0:T(8,128)(2,1)S(1)}) custom-call(bf16[2,1024,768]{2,1,0:T(8,128)(2,1)S(1)} %bitcast.257, bf16[2,1024,1536]{2,1,0:T(8,128)(2,1)} %bitcast.248, bf16[2,1024,1536]{2,1,0:T(8,128)(2,1)} %bitcast.249, bf16[2,1024,768]{2,1,0:T(8,128)(2,1)} %copy-done.27, ...), custom_call_target="tpu_custom_call" | custom-call | flops 25769803776 | bytes 25165824 | tf_op jit(solution)/shard_map/attend_back/pallas_call | solution.py:426
  306.6 1.7 bitcast_dynamic-update-slice_fusion
  308.4 1.6 copy-done.73
  310.0 2.8 fusion.2
  312.9 3.9 collective-permute-start.6
  316.8 2.5 fusion.1
  319.9 30.8 %attend_back.5 = (bf16[2,1024,768]{2,1,0:T(8,128)(2,1)S(1)}, bf16[2,1024,768]{2,1,0:T(8,128)(2,1)S(1)}, bf16[2,1024,768]{2,1,0:T(8,128)(2,1)S(1)}) custom-call(bf16[2,1024,768]{2,1,0:T(8,128)(2,1)S(1)} %get-tuple-element.156.refs_0_, ...), custom_call_target="tpu_custom_call", output_to_operand_aliasing={{0}: (0, {}), {1}: (1, {}), {2}: (2, {})} | custom-call | flops 25769803776 | bytes 25165824 | tf_op jit(solution)/shard_map/attend_back/pallas_call | solution.py:426
  350.7 1.6 copy-done.29
  352.4 1.7 copy-done.30
  354.0 2.6 fusion.4
  356.7 1.7 collective-permute-start.8
  359.0 41.0 %return_rows.1 = (f32[4,512,768]{2,1,0:T(8,128)}, bf16[2,512,768]{2,1,0:T(8,128)(2,1)}, f32[2048,768]{1,0:T(8,128)}, bf16[2048,768]{1,0:T(8,128)(2,1)}, f32[8,76...) custom-call(s32[4]{0:T(128)} %copy-done.13, ...), custom_call_target="tpu_custom_call" | custom-call | flops 19327352832 | bytes 41943040 | tf_op jit(solution)/shard_map/return_rows/pallas_call | solution.py:517
  401.1 3.0 collective-permute-start.10
  408.2 31.0 %attend_back.6 = (bf16[2,1024,768]{2,1,0:T(8,128)(2,1)S(1)}, bf16[2,1024,768]{2,1,0:T(8,128)(2,1)S(1)}, bf16[2,1024,768]{2,1,0:T(8,128)(2,1)S(1)}) custom-call(bf16[2,1024,2304]{2,1,0:T(8,128)(2,1)} %bitcast.239, bf16[2,1024,2304]{2,1,0:T(8,128)(2,1)} %bitcast.240, bf16[2,1024,2304]{2,1,0:T(8,128)(2,1)} %bitcast.241, bf16[2,1024,768]{2,1,0:T(8,128)(2,1)S(1)} %copy-done.23, ...), custom_call_target="tpu_custom_call" | custom-call | flops 25769803776 | bytes 25165824 | tf_op jit(solution)/shard_map/attend_back/pallas_call | solution.py:426
  439.3 1.7 copy-done.5
  441.0 1.7 copy-done.8
  449.2 1.7 collective-permute-start.14
  452.6 1.7 fusion.6
  455.2 2.0 collective-permute-start.16
  457.2 1.6 fusion.5
  458.9 1.7 collective-permute-start.17
  460.5 11.5 %leave.2 = (f32[4,512,768]{2,1,0:T(8,128)}, bf16[512,768]{1,0:T(8,128)(2,1)}, f32[8,768]{1,0:T(8,128)S(1)}) custom-call(s32[4]{0:T(128)S(1)} %copy-done.14, bf16[2048,768]{1,0:T(8,128)(2,1)S(1)} %bitcast.225, bf16[2048,768]{1,0:T(8,128)(2,1)} %bitcast.228, bf16[2048,768]{1,0:T(8,128)(2,1)} %bitcast.231, bf16[2048,768]{1,0:T(8,128)(2,1)} %copy-done.2, ...), custom_call_target="tpu_custom_call" | custom-call | flops 3623878656 | bytes 16777216 | tf_op jit(solution)/shard_map/leave/pallas_call | solution.py:517
  472.1 30.8 %attend_back.7 = (bf16[2,1024,768]{2,1,0:T(8,128)(2,1)S(1)}, bf16[2,1024,768]{2,1,0:T(8,128)(2,1)S(1)}, bf16[2,1024,768]{2,1,0:T(8,128)(2,1)S(1)}) custom-call(bf16[2,1024,768]{2,1,0:T(8,128)(2,1)S(1)} %get-tuple-element.199.refs_0_, bf16[2,1024,768]{2,1,0:T(8,128)(2,1)S(1)} %copy-done.6, ...), custom_call_target="tpu_custom_call", output_to_operand_aliasing={{0}: (0, {}), {1}: (1, {}), {2}: (2, {})} | custom-call | flops 25769803776 | bytes 25165824 | tf_op jit(solution)/shard_map/attend_back/pallas_call | solution.py:426
  502.9 1.6 copy-done.7
  504.6 1.7 copy-done.10
  506.6 4.1 convert_dynamic-update-slice_fusion
  510.7 14.6 %last_weight.1 = (bf16[8,48,1152]{2,1,0:T(8,128)(2,1)S(1)}, bf16[8,48,1152]{2,1,0:T(8,128)(2,1)S(1)}, bf16[8,48,1152]{2,1,0:T(8,128)(2,1)S(1)}, bf16[8,48,1152]{2,1,0:T(8,128)(2,1)S(1)}) custom-call(s32[4]{0:T(128)S(1)} %copy-done.14, bf16[2048,768]{1,0:T(8,128)(2,1)} %bitcast.226, bf16[2048,768]{1,0:T(8,128)(2,1)} %bitcast.229, ...), custom_call_target="tpu_custom_call" | custom-call | flops 7247757312 | bytes 20971520 | tf_op jit(solution)/shard_map/last_weight/pallas_call | solution.py:517
  525.3 11.2 %leave.3 = (f32[4,512,768]{2,1,0:T(8,128)}, bf16[512,768]{1,0:T(8,128)(2,1)S(1)}, f32[8,768]{1,0:T(8,128)S(1)}) custom-call(s32[4]{0:T(128)S(1)} %copy-done.14, bf16[2048,768]{1,0:T(8,128)(2,1)S(1)} %bitcast.227, bf16[2048,768]{1,0:T(8,128)(2,1)} %bitcast.230, bf16[2048,768]{1,0:T(8,128)(2,1)} %bitcast.233, ...), custom_call_target="tpu_custom_call", output_to_operand_aliasing={{0}: (8, {})} | custom-call | flops 3623878656 | bytes 16777216 | tf_op jit(solution)/shard_map/leave/pallas_call | solution.py:517
  543.5 1.6 concatenate.84
  546.8 1.9 convert_add_fusion.13
  552.4 1.7 collective-permute-done.22
  555.2 2.6 collective-permute-done.23
  557.9 1.7 collective-permute-start.24
  559.7 2.8 collective-permute-done.24
  568.4 3.4 collective-permute-done.26
  573.0 3.8 collective-permute-start.30
  578.9 2.4 convert_dynamic-update-slice_fusion.2
  581.2 1.9 collective-permute-done.30
  583.2 4.0 collective-permute-done.31
  587.2 2.0 collective-permute-done.33
  596.0 3.9 collective-permute-done.36
  600.0 2.0 collective-permute-start.38
  603.9 3.0 collective-permute-done.38
  606.9 2.4 collective-permute-done.39
  612.2 1.9 collective-permute-done.40
  (305 shorter events, 61.1 us)
Async XLA Ops:
  0.7 13.9 %copy-start = (s32[4,1]{0,1:T(1,128)S(1)}, s32[4,1]{0,1:T(1,128)}, u32[]{:S(2)}) copy-start(s32[4,1]{0,1:T(1,128)} %param.28) | copy-start | bytes 52
  3.5 38.4 %collective-permute-start = (bf16[2,512,768]{2,1,0:T(8,128)(2,1)}, bf16[2,512,768]{2,1,0:T(8,128)(2,1)S(1)}, u32[]{:S(2)}, u32[]{:S(2)}) collective-permute-start(bf16[2,512,768]{2,1,0:T(8,128)(2,1)} %dynamic-slice_bitcast_fusion.1), channel_id=1, source_target_pairs={{0,1},{1,0},{2,3},{3,2},{4,5},{5,4},{6,7},{7,6},{8,9},{9,8},{10,11... | collective-permute-start | bytes 4718600 | tf_op jit(solution)/shard_map/ppermute | solution.py:1038
  7.7 98.6 %collective-permute-start.1 = (bf16[2,512,768]{2,1,0:T(8,128)(2,1)}, bf16[2,512,768]{2,1,0:T(8,128)(2,1)}, u32[]{:S(2)}, u32[]{:S(2)}) collective-permute-start(bf16[2,512,768]{2,1,0:T(8,128)(2,1)} %dynamic-slice_bitcast_fusion), channel_id=1, source_target_pairs={{0,1},{1,0},{2,3},{3,2},{4,5},{5,4},{6,7},{7,6},{8,9},{9,8},{10,11... | collective-permute-start | bytes 4718600 | tf_op jit(solution)/shard_map/ppermute | solution.py:1038
  11.4 142.0 %collective-permute-start.2 = (bf16[2,512,768]{2,1,0:T(8,128)(2,1)}, bf16[2,512,768]{2,1,0:T(8,128)(2,1)}, u32[]{:S(2)}, u32[]{:S(2)}) collective-permute-start(bf16[2,512,768]{2,1,0:T(8,128)(2,1)} %constant_dynamic-slice_fusion.6), channel_id=1, source_target_pairs={{0,1},{1,0},{2,3},{3,2},{4,5},{5,4},{6,7},{7,6},{8,9},{9,8},{10,11... | collective-permute-start | bytes 4718600 | tf_op jit(solution)/shard_map/ppermute | solution.py:1038
  14.7 102.6 %copy-start.13 = (s32[4]{0:T(128)}, s32[4]{0:T(128)S(1)}, u32[]{:S(2)}) copy-start(s32[4]{0:T(128)S(1)} %pad_add_fusion.info_ref) | copy-start | bytes 52
  15.4 91.0 %copy-start.11 = (f32[8,768]{1,0:T(8,128)}, f32[8,768]{1,0:T(8,128)S(1)}, u32[]{:S(2)}) copy-start(f32[8,768]{1,0:T(8,128)S(1)} %get-tuple-element.301.vec_ref) | copy-start | bytes 73732
  62.1 33.4 %copy-start.16 = (bf16[768,768]{1,0:T(8,128)(2,1)S(1)}, bf16[768,768]{1,0:T(8,128)(2,1)}, u32[]{:S(2)}) copy-start(bf16[768,768]{1,0:T(8,128)(2,1)} %wo_ref.5) | copy-start | bytes 3538948
  62.1 33.4 %copy-start.17 = (bf16[768,768]{1,0:T(8,128)(2,1)S(1)}, bf16[768,768]{1,0:T(8,128)(2,1)}, u32[]{:S(2)}) copy-start(bf16[768,768]{1,0:T(8,128)(2,1)} %wq_ref.3) | copy-start | bytes 3538948
  95.5 10.8 %copy-start.15 = (bf16[768,1536]{1,0:T(8,128)(2,1)S(1)}, bf16[768,1536]{1,0:T(8,128)(2,1)}, u32[]{:S(2)}) copy-start(bf16[768,1536]{1,0:T(8,128)(2,1)} %wi_ref.3) | copy-start | bytes 7077892
  106.3 10.9 %copy-start.25 = (bf16[2048,768]{1,0:T(8,128)(2,1)}, bf16[2048,768]{1,0:T(8,128)(2,1)S(1)}, u32[]{:S(2)}) copy-start(bf16[2048,768]{1,0:T(8,128)(2,1)S(1)} %get-tuple-element.139) | copy-start | bytes 9437188
  266.7 41.7 %collective-permute-start.5 = (bf16[2,2,2,240,768]{4,3,0,2,1:T(8,128)(2,1)}, bf16[2,2,2,240,768]{4,3,0,2,1:T(8,128)(2,1)}, u32[]{:S(2)}, u32[]{:S(2)}) collective-permute-start(bf16[2,2,2,240,768]{4,3,0,2,1:T(8,128)(2,1)} %copy.59), channel_id=1, source_target_pairs={{0,2},{2,0},{4,6},{6,4},{8,10},{10,8},{12,14},{14,12},{16,18},{18,... | collective-permute-start | bytes 8847368 | tf_op jit(solution)/shard_map/ppermute | solution.py:946
  266.7 39.9 %collective-permute-start.3 = (bf16[2,512,768]{2,1,0:T(8,128)(2,1)}, bf16[2,512,768]{2,1,0:T(8,128)(2,1)}, u32[]{:S(2)}, u32[]{:S(2)}) collective-permute-start(bf16[2,512,768]{2,1,0:T(8,128)(2,1)} %get-tuple-element.143), channel_id=1, source_target_pairs={{0,1},{1,0},{2,3},{3,2},{4,5},{5,4},{6,7},{7,6},{8,9},{9,8},{10,11... | collective-permute-start | bytes 4718600 | tf_op jit(solution)/shard_map/ppermute | solution.py:1041
  268.5 7.1 %copy-start.26 = (bf16[2048,768]{1,0:T(8,128)(2,1)S(1)}, bf16[2048,768]{1,0:T(8,128)(2,1)}, u32[]{:S(2)}) copy-start(bf16[2048,768]{1,0:T(8,128)(2,1)} %copy-done.25) | copy-start | bytes 9437188
  271.9 36.5 %collective-permute-start.4 = (bf16[2,2,2,48,3072]{4,3,0,1,2:T(8,128)(2,1)}, bf16[2,2,2,48,3072]{4,3,0,1,2:T(8,128)(2,1)}, u32[]{:S(2)}, u32[]{:S(2)}) collective-permute-start(bf16[2,2,2,48,3072]{4,3,0,1,2:T(8,128)(2,1)} %copy.58), channel_id=1, source_target_pairs={{0,2},{2,0},{4,6},{6,4},{8,10},{10,8},{12,14},{14,12},{16,18},{18,... | collective-permute-start | bytes 7077896 | tf_op jit(solution)/shard_map/ppermute | solution.py:946
  275.6 31.0 %copy-start.72 = (bf16[4,512,768]{2,1,0:T(8,128)(2,1)S(1)}, bf16[4,512,768]{2,1,0:T(8,128)(2,1)}, u32[]{:S(2)}) copy-start(bf16[4,512,768]{2,1,0:T(8,128)(2,1)} %get-tuple-element.142) | copy-start | bytes 9437188
  312.9 41.1 %collective-permute-start.6 = (bf16[2,2,48,3072]{3,2,0,1:T(8,128)(2,1)S(1)}, bf16[2,2,48,3072]{3,2,0,1:T(8,128)(2,1)}, u32[]{:S(2)}, u32[]{:S(2)}) collective-permute-start(bf16[2,2,48,3072]{3,2,0,1:T(8,128)(2,1)S(1)} %dynamic-slice_bitcast_fusion.3), channel_id=1, source_target_pairs={{0,4},{2,6},{4,0},{6,2},{8,12},{10,14},{12,8},{14,10},{16,20},{18,... | collective-permute-start | bytes 3538952 | tf_op jit(solution)/shard_map/ppermute | solution.py:946
  319.4 34.6 %collective-permute-start.7 = (bf16[2,2,240,768]{3,2,0,1:T(8,128)(2,1)S(1)}, bf16[2,2,240,768]{3,2,0,1:T(8,128)(2,1)S(1)}, u32[]{:S(2)}, u32[]{:S(2)}) collective-permute-start(bf16[2,2,240,768]{3,2,0,1:T(8,128)(2,1)S(1)} %dynamic-slice_bitcast_fusion.2), channel_id=1, source_target_pairs={{0,8},{2,10},{4,12},{6,14},{8,0},{10,2},{12,4},{14,6},{16,24},{18,... | collective-permute-start | bytes 4423688 | tf_op jit(solution)/shard_map/ppermute | solution.py:946
  356.7 43.3 %collective-permute-start.8 = (bf16[2,48,3072]{2,1,0:T(8,128)(2,1)S(1)}, bf16[2,48,3072]{2,1,0:T(8,128)(2,1)S(1)}, u32[]{:S(2)}, u32[]{:S(2)}) collective-permute-start(bf16[2,48,3072]{2,1,0:T(8,128)(2,1)S(1)} %dynamic-slice_bitcast_fusion.7), channel_id=1, source_target_pairs={{0,8},{2,10},{4,12},{6,14},{8,0},{10,2},{12,4},{14,6},{16,24},{18,... | collective-permute-start | bytes 1769480 | tf_op jit(solution)/shard_map/ppermute | solution.py:946
  358.8 41.2 %collective-permute-start.9 = (bf16[2,240,768]{2,1,0:T(8,128)(2,1)S(1)}, bf16[2,240,768]{2,1,0:T(8,128)(2,1)S(1)}, u32[]{:S(2)}, u32[]{:S(2)}) collective-permute-start(bf16[2,240,768]{2,1,0:T(8,128)(2,1)S(1)} %dynamic-slice_bitcast_fusion.4), channel_id=1, source_target_pairs={{0,4},{2,6},{4,0},{6,2},{8,12},{10,14},{12,8},{14,10},{16,20},{18,... | collective-permute-start | bytes 2211848 | tf_op jit(solution)/shard_map/ppermute | solution.py:946
  401.1 46.3 %collective-permute-start.10 = (bf16[48,3072]{1,0:T(8,128)(2,1)}, bf16[48,3072]{1,0:T(8,128)(2,1)S(1)}, u32[]{:S(2)}, u32[]{:S(2)}) collective-permute-start(bf16[48,3072]{1,0:T(8,128)(2,1)} %dynamic-slice_bitcast_fusion.13), channel_id=1, source_target_pairs={{0,16},{2,18},{4,20},{6,22},{8,24},{10,26},{12,28},{14,30},{16,0},... | collective-permute-start | bytes 884744 | tf_op jit(solution)/shard_map/ppermute | solution.py:946
  404.3 35.0 %copy-start.37 = (bf16[2,240,768]{2,1,0:T(8,128)(2,1)}, bf16[2,240,768]{2,1,0:T(8,128)(2,1)S(1)}, u32[]{:S(2)}) copy-start(bf16[2,240,768]{2,1,0:T(8,128)(2,1)S(1)} %fusion.9) | copy-start | bytes 2211844
  405.1 42.2 %collective-permute-start.11 = (bf16[240,768]{1,0:T(8,128)(2,1)}, bf16[240,768]{1,0:T(8,128)(2,1)}, u32[]{:S(2)}, u32[]{:S(2)}) collective-permute-start(bf16[240,768]{1,0:T(8,128)(2,1)} %dynamic-slice_bitcast_fusion.10), channel_id=1, source_target_pairs={{0,16},{2,18},{4,20},{6,22},{8,24},{10,26},{12,28},{14,30},{16,0},... | collective-permute-start | bytes 1105928 | tf_op jit(solution)/shard_map/ppermute | solution.py:946
  406.3 41.1 %collective-permute-start.12 = (bf16[2,2,2,48,1536]{4,3,0,1,2:T(8,128)(2,1)}, bf16[2,2,2,48,1536]{4,3,0,1,2:T(8,128)(2,1)}, u32[]{:S(2)}, u32[]{:S(2)}) collective-permute-start(bf16[2,2,2,48,1536]{4,3,0,1,2:T(8,128)(2,1)} %copy.62), channel_id=1, source_target_pairs={{0,2},{2,0},{4,6},{6,4},{8,10},{10,8},{12,14},{14,12},{16,18},{18,... | collective-permute-start | bytes 3538952 | tf_op jit(solution)/shard_map/ppermute | solution.py:946
  407.4 40.0 %collective-permute-start.13 = (bf16[2,2,2,96,768]{4,3,0,2,1:T(8,128)(2,1)}, bf16[2,2,2,96,768]{4,3,0,2,1:T(8,128)(2,1)}, u32[]{:S(2)}, u32[]{:S(2)}) collective-permute-start(bf16[2,2,2,96,768]{4,3,0,2,1:T(8,128)(2,1)} %copy.63), channel_id=1, source_target_pairs={{0,2},{2,0},{4,6},{6,4},{8,10},{10,8},{12,14},{14,12},{16,18},{18,... | collective-permute-start | bytes 3538952 | tf_op jit(solution)/shard_map/ppermute | solution.py:946
  407.9 98.4 %collective-permute-start.20 = (bf16[2,512,768]{2,1,0:T(8,128)(2,1)}, bf16[2,512,768]{2,1,0:T(8,128)(2,1)}, u32[]{:S(2)}, u32[]{:S(2)}) collective-permute-start(bf16[2,512,768]{2,1,0:T(8,128)(2,1)} %get-tuple-element.217), channel_id=1, source_target_pairs={{0,1},{1,0},{2,3},{3,2},{4,5},{5,4},{6,7},{7,6},{8,9},{9,8},{10,11... | collective-permute-start | bytes 4718600 | tf_op jit(solution)/shard_map/ppermute | solution.py:1041
  408.2 34.4 %copy-start.54 = (f32[8,768]{1,0:T(8,128)S(1)}, f32[8,768]{1,0:T(8,128)}, u32[]{:S(2)}) copy-start(f32[8,768]{1,0:T(8,128)} %get-tuple-element.220) | copy-start | bytes 73732
  449.2 61.4 %collective-permute-start.14 = (bf16[48,3072]{1,0:T(8,128)(2,1)S(1)}, bf16[48,3072]{1,0:T(8,128)(2,1)}, u32[]{:S(2)}, u32[]{:S(2)}) collective-permute-start(bf16[48,3072]{1,0:T(8,128)(2,1)S(1)} %fusion.18), channel_id=1, source_target_pairs={{0,1},{1,0},{2,3},{3,2},{4,5},{5,4},{6,7},{7,6},{8,9},{9,8},{10,11... | collective-permute-start | bytes 884744 | tf_op jit(solution)/shard_map/ppermute | solution.py:948
  452.2 58.5 %collective-permute-start.15 = (bf16[240,768]{1,0:T(8,128)(2,1)S(1)}, bf16[240,768]{1,0:T(8,128)(2,1)}, u32[]{:S(2)}, u32[]{:S(2)}) collective-permute-start(bf16[240,768]{1,0:T(8,128)(2,1)S(1)} %fusion.15), channel_id=1, source_target_pairs={{0,1},{1,0},{2,3},{3,2},{4,5},{5,4},{6,7},{7,6},{8,9},{9,8},{10,11... | collective-permute-start | bytes 1105928 | tf_op jit(solution)/shard_map/ppermute | solution.py:948
  455.2 55.5 %collective-permute-start.16 = (bf16[2,2,48,1536]{3,2,0,1:T(8,128)(2,1)}, bf16[2,2,48,1536]{3,2,0,1:T(8,128)(2,1)}, u32[]{:S(2)}, u32[]{:S(2)}) collective-permute-start(bf16[2,2,48,1536]{3,2,0,1:T(8,128)(2,1)} %dynamic-slice_bitcast_fusion.6), channel_id=1, source_target_pairs={{0,4},{2,6},{4,0},{6,2},{8,12},{10,14},{12,8},{14,10},{16,20},{18,... | collective-permute-start | bytes 1769480 | tf_op jit(solution)/shard_map/ppermute | solution.py:946
  458.8 13.3 %copy-start.32 = (bf16[2,2,2,96,768]{4,3,0,2,1:T(8,128)(2,1)}, bf16[2,2,2,96,768]{4,3,0,2,1:T(8,128)(2,1)S(1)}, u32[]{:S(2)}) copy-start(bf16[2,2,2,96,768]{4,3,0,2,1:T(8,128)(2,1)S(1)} %fusion.5) | copy-start | bytes 3538948
  458.9 51.8 %collective-permute-start.17 = (bf16[2,2,96,768]{3,2,0,1:T(8,128)(2,1)S(1)}, bf16[2,2,96,768]{3,2,0,1:T(8,128)(2,1)S(1)}, u32[]{:S(2)}, u32[]{:S(2)}) collective-permute-start(bf16[2,2,96,768]{3,2,0,1:T(8,128)(2,1)S(1)} %dynamic-slice_bitcast_fusion.5), channel_id=1, source_target_pairs={{0,8},{2,10},{4,12},{6,14},{8,0},{10,2},{12,4},{14,6},{16,24},{18,... | collective-permute-start | bytes 1769480 | tf_op jit(solution)/shard_map/ppermute | solution.py:946
  460.5 11.5 %copy-start.6 = (bf16[2,1024,768]{2,1,0:T(8,128)(2,1)S(1)}, bf16[2,1024,768]{2,1,0:T(8,128)(2,1)}, u32[]{:S(2)}) copy-start(bf16[2,1024,768]{2,1,0:T(8,128)(2,1)} %copy-done.5) | copy-start | bytes 9437188
  460.5 11.5 %copy-start.9 = (bf16[2,1024,768]{2,1,0:T(8,128)(2,1)S(1)}, bf16[2,1024,768]{2,1,0:T(8,128)(2,1)}, u32[]{:S(2)}) copy-start(bf16[2,1024,768]{2,1,0:T(8,128)(2,1)} %copy-done.8) | copy-start | bytes 9437188
  460.5 11.5 %copy-start.24 = (bf16[2,1024,768]{2,1,0:T(8,128)(2,1)S(1)}, bf16[2,1024,768]{2,1,0:T(8,128)(2,1)}, u32[]{:S(2)}) copy-start(bf16[2,1024,768]{2,1,0:T(8,128)(2,1)} %copy-done.22) | copy-start | bytes 9437188
  506.2 72.5 %collective-permute-start.18 = (bf16[1,512,768]{2,1,0:T(8,128)(2,1)}, bf16[1,512,768]{2,1,0:T(8,128)(2,1)}, u32[]{:S(2)}, u32[]{:S(2)}) collective-permute-start(bf16[1,512,768]{2,1,0:T(8,128)(2,1)} %bitcast.55), channel_id=1, source_target_pairs={{0,1},{1,0},{2,3},{3,2},{4,5},{5,4},{6,7},{7,6},{8,9},{9,8},{10,11... | collective-permute-start | bytes 2359304 | tf_op jit(solution)/shard_map/ppermute | solution.py:1041
  510.7 14.6 %copy-start.49 = (bf16[2,2,96,768]{3,2,0,1:T(8,128)(2,1)}, bf16[2,2,96,768]{3,2,0,1:T(8,128)(2,1)S(1)}, u32[]{:S(2)}) copy-start(bf16[2,2,96,768]{3,2,0,1:T(8,128)(2,1)S(1)} %collective-permute-done.17) | copy-start | bytes 1769476
  510.7 14.6 %copy-start.4 = (bf16[2,1024,768]{2,1,0:T(8,128)(2,1)S(1)}, bf16[2,1024,768]{2,1,0:T(8,128)(2,1)}, u32[]{:S(2)}) copy-start(bf16[2,1024,768]{2,1,0:T(8,128)(2,1)} %copy-done.3) | copy-start | bytes 9437188
  525.3 18.2 %copy-start.52 = (bf16[8,2,1,192]{3,1,0,2:T(2,128)(2,1)S(1)}, bf16[8,2,1,192]{3,1,0,2:T(2,128)(2,1)}, u32[]{:S(2)}) copy-start(bf16[8,2,1,192]{3,1,0,2:T(2,128)(2,1)} %concatenate.83) | copy-start | bytes 18436
  525.3 18.2 %copy-start.55 = (bf16[8,2,1,48]{3,1,0,2:T(2,128)(2,1)S(1)}, bf16[8,2,1,48]{3,1,0,2:T(2,128)(2,1)}, u32[]{:S(2)}) copy-start(bf16[8,2,1,48]{3,1,0,2:T(2,128)(2,1)} %concatenate.79) | copy-start | bytes 4612
  525.3 18.2 %copy-start.56 = (bf16[8,2,1,48]{3,1,0,2:T(2,128)(2,1)S(1)}, bf16[8,2,1,48]{3,1,0,2:T(2,128)(2,1)}, u32[]{:S(2)}) copy-start(bf16[8,2,1,48]{3,1,0,2:T(2,128)(2,1)} %concatenate.80) | copy-start | bytes 4612
  546.1 4.2 collective-permute-start.21
  546.2 26.7 %collective-permute-start.29 = (bf16[2,2,2,48,1152]{4,3,0,2,1:T(8,128)(2,1)S(1)}, bf16[2,2,2,48,1152]{4,3,0,2,1:T(8,128)(2,1)S(1)}, u32[]{:S(2)}, u32[]{:S(2)}) collective-permute-start(bf16[2,2,2,48,1152]{4,3,0,2,1:T(8,128)(2,1)S(1)} %copy.68), channel_id=1, source_target_pairs={{0,2},{2,0},{4,6},{6,4},{8,10},{10,8},{12,14},{14,12},{16,18},{18,... | collective-permute-start | bytes 2654216 | tf_op jit(solution)/shard_map/ppermute | solution.py:946
  550.1 22.8 %collective-permute-start.28 = (bf16[2,2,2,48,1152]{4,3,0,1,2:T(8,128)(2,1)S(1)}, bf16[2,2,2,48,1152]{4,3,0,1,2:T(8,128)(2,1)S(1)}, u32[]{:S(2)}, u32[]{:S(2)}) collective-permute-start(bf16[2,2,2,48,1152]{4,3,0,1,2:T(8,128)(2,1)S(1)} %copy.67), channel_id=1, source_target_pairs={{0,2},{2,0},{4,6},{6,4},{8,10},{10,8},{12,14},{14,12},{16,18},{18,... | collective-permute-start | bytes 2654216 | tf_op jit(solution)/shard_map/ppermute | solution.py:946
  550.3 3.8 collective-permute-start.22
  552.4 19.4 %copy-start.19 = (bf16[512,768]{1,0:T(8,128)(2,1)S(1)}, bf16[512,768]{1,0:T(8,128)(2,1)}, u32[]{:S(2)}) copy-start(bf16[512,768]{1,0:T(8,128)(2,1)} %copy-done.18) | copy-start | bytes 2359300
  554.2 3.7 collective-permute-start.23
  557.9 4.6 collective-permute-start.24
  562.5 3.7 collective-permute-start.25
  565.0 6.7 %collective-permute-start.26 = (bf16[2,48,1536]{2,1,0:T(8,128)(2,1)S(1)}, bf16[2,48,1536]{2,1,0:T(8,128)(2,1)S(1)}, u32[]{:S(2)}, u32[]{:S(2)}) collective-permute-start(bf16[2,48,1536]{2,1,0:T(8,128)(2,1)S(1)} %dynamic-slice_bitcast_fusion.12), channel_id=1, source_target_pairs={{0,8},{2,10},{4,12},{6,14},{8,0},{10,2},{12,4},{14,6},{16,24},{18,... | collective-permute-start | bytes 884744 | tf_op jit(solution)/shard_map/ppermute | solution.py:946
  566.2 6.7 %collective-permute-start.27 = (bf16[2,96,768]{2,1,0:T(8,128)(2,1)S(1)}, bf16[2,96,768]{2,1,0:T(8,128)(2,1)S(1)}, u32[]{:S(2)}, u32[]{:S(2)}) collective-permute-start(bf16[2,96,768]{2,1,0:T(8,128)(2,1)S(1)} %dynamic-slice_bitcast_fusion.11), channel_id=1, source_target_pairs={{0,4},{2,6},{4,0},{6,2},{8,12},{10,14},{12,8},{14,10},{16,20},{18,... | collective-permute-start | bytes 884744 | tf_op jit(solution)/shard_map/ppermute | solution.py:946
  571.7 22.0 %collective-permute-start.19 = (bf16[1,512,768]{2,1,0:T(8,128)(2,1)S(1)}, bf16[1,512,768]{2,1,0:T(8,128)(2,1)S(1)}, u32[]{:S(2)}, u32[]{:S(2)}) collective-permute-start(bf16[1,512,768]{2,1,0:T(8,128)(2,1)S(1)} %bitcast.238), channel_id=1, source_target_pairs={{0,1},{1,0},{2,3},{3,2},{4,5},{5,4},{6,7},{7,6},{8,9},{9,8},{10,11... | collective-permute-start | bytes 2359304 | tf_op jit(solution)/shard_map/ppermute | solution.py:1041
  573.0 10.2 %collective-permute-start.30 = (bf16[48,1536]{1,0:T(8,128)(2,1)S(1)}, bf16[48,1536]{1,0:T(8,128)(2,1)S(1)}, u32[]{:S(2)}, u32[]{:S(2)}) collective-permute-start(bf16[48,1536]{1,0:T(8,128)(2,1)S(1)} %dynamic-slice_bitcast_fusion.17), channel_id=1, source_target_pairs={{0,16},{2,18},{4,20},{6,22},{8,24},{10,26},{12,28},{14,30},{16,0},... | collective-permute-start | bytes 442376 | tf_op jit(solution)/shard_map/ppermute | solution.py:946
  577.1 10.1 %collective-permute-start.32 = (bf16[2,2,48,1152]{3,2,0,1:T(8,128)(2,1)S(1)}, bf16[2,2,48,1152]{3,2,0,1:T(8,128)(2,1)S(1)}, u32[]{:S(2)}, u32[]{:S(2)}) collective-permute-start(bf16[2,2,48,1152]{3,2,0,1:T(8,128)(2,1)S(1)} %dynamic-slice_bitcast_fusion.9), channel_id=1, source_target_pairs={{0,4},{2,6},{4,0},{6,2},{8,12},{10,14},{12,8},{14,10},{16,20},{18,... | collective-permute-start | bytes 1327112 | tf_op jit(solution)/shard_map/ppermute | solution.py:946
  577.7 11.4 %collective-permute-start.33 = (bf16[2,2,48,1152]{3,2,0,1:T(8,128)(2,1)S(1)}, bf16[2,2,48,1152]{3,2,0,1:T(8,128)(2,1)S(1)}, u32[]{:S(2)}, u32[]{:S(2)}) collective-permute-start(bf16[2,2,48,1152]{3,2,0,1:T(8,128)(2,1)S(1)} %dynamic-slice_bitcast_fusion.8), channel_id=1, source_target_pairs={{0,8},{2,10},{4,12},{6,14},{8,0},{10,2},{12,4},{14,6},{16,24},{18,... | collective-permute-start | bytes 1327112 | tf_op jit(solution)/shard_map/ppermute | solution.py:946
  578.7 8.4 %collective-permute-start.31 = (bf16[96,768]{1,0:T(8,128)(2,1)S(1)}, bf16[96,768]{1,0:T(8,128)(2,1)S(1)}, u32[]{:S(2)}, u32[]{:S(2)}) collective-permute-start(bf16[96,768]{1,0:T(8,128)(2,1)S(1)} %dynamic-slice_bitcast_fusion.16), channel_id=1, source_target_pairs={{0,16},{2,18},{4,20},{6,22},{8,24},{10,26},{12,28},{14,30},{16,0},... | collective-permute-start | bytes 442376 | tf_op jit(solution)/shard_map/ppermute | solution.py:946
  589.2 5.9 collective-permute-start.34
  590.1 5.8 collective-permute-start.35
  591.5 8.4 %collective-permute-start.36 = (bf16[2,48,1152]{2,1,0:T(8,128)(2,1)S(1)}, bf16[2,48,1152]{2,1,0:T(8,128)(2,1)S(1)}, u32[]{:S(2)}, u32[]{:S(2)}) collective-permute-start(bf16[2,48,1152]{2,1,0:T(8,128)(2,1)S(1)} %dynamic-slice_bitcast_fusion.15), channel_id=1, source_target_pairs={{0,8},{2,10},{4,12},{6,14},{8,0},{10,2},{12,4},{14,6},{16,24},{18,... | collective-permute-start | bytes 663560 | tf_op jit(solution)/shard_map/ppermute | solution.py:946
  592.9 7.0 %collective-permute-start.37 = (bf16[2,48,1152]{2,1,0:T(8,128)(2,1)S(1)}, bf16[2,48,1152]{2,1,0:T(8,128)(2,1)S(1)}, u32[]{:S(2)}, u32[]{:S(2)}) collective-permute-start(bf16[2,48,1152]{2,1,0:T(8,128)(2,1)S(1)} %dynamic-slice_bitcast_fusion.14), channel_id=1, source_target_pairs={{0,4},{2,6},{4,0},{6,2},{8,12},{10,14},{12,8},{14,10},{16,20},{18,... | collective-permute-start | bytes 663560 | tf_op jit(solution)/shard_map/ppermute | solution.py:946
  600.0 6.9 %collective-permute-start.38 = (bf16[48,1152]{1,0:T(8,128)(2,1)S(1)}, bf16[48,1152]{1,0:T(8,128)(2,1)S(1)}, u32[]{:S(2)}, u32[]{:S(2)}) collective-permute-start(bf16[48,1152]{1,0:T(8,128)(2,1)S(1)} %dynamic-slice_bitcast_fusion.19), channel_id=1, source_target_pairs={{0,16},{2,18},{4,20},{6,22},{8,24},{10,26},{12,28},{14,30},{16,0},... | collective-permute-start | bytes 331784 | tf_op jit(solution)/shard_map/ppermute | solution.py:946
  602.0 14.2 %copy-start.1 = (s32[4,1]{0,1:T(1,128)S(1)}, s32[4,1]{0,1:T(1,128)}, u32[]{:S(2)}) copy-start(s32[4,1]{0,1:T(1,128)} %param.28) | copy-start | bytes 52
  602.1 7.2 %collective-permute-start.39 = (bf16[48,1152]{1,0:T(8,128)(2,1)S(1)}, bf16[48,1152]{1,0:T(8,128)(2,1)S(1)}, u32[]{:S(2)}, u32[]{:S(2)}) collective-permute-start(bf16[48,1152]{1,0:T(8,128)(2,1)S(1)} %dynamic-slice_bitcast_fusion.18), channel_id=1, source_target_pairs={{0,16},{2,18},{4,20},{6,22},{8,24},{10,26},{12,28},{14,30},{16,0},... | collective-permute-start | bytes 331784 | tf_op jit(solution)/shard_map/ppermute | solution.py:946
  609.3 4.8 collective-permute-start.40
  610.3 4.9 collective-permute-start.41
  (52 other events, 182.1 us)

commit v4 on v3

--- a/solution.py
+++ b/solution.py
@@ -259,10 +259,11 @@
     return (jnp.where(lane < HEAD, pair, zero), jnp.where(lane < HEAD, zero, pair))
 
 
-ATTEND_LIMIT = 40 * 2**20
-
-
-def attend_kernel(info_ref, q_ref, k_ref, v_ref, o_ref, e_ref, r_ref, *, use_mask):
+LIMIT = 62 * 2**20
+
+
+def attend_kernel(info_ref, q_ref, k_ref, v_ref, *refs, use_mask, start):
+    o_ref, e_ref, r_ref = refs[-3:]
     length = k_ref.shape[1]
     half = length // 2
     values_turned = v_ref[0].T
@@ -330,7 +331,7 @@
     if not use_mask:
         run(False, False)
         return
-    causal = info_ref[2 + pl.program_id(0)] == 0
+    causal = info_ref[2 + start + pl.program_id(0)] == 0
     for side_now in range(2):
 
         @pl.when(causal & (side == side_now))
@@ -342,24 +343,26 @@
         run(False, False)
 
 
-def attend(info, queries, keys, values, use_mask, offsets):
+def attend(info, start, count_now, previous, queries, keys, values, use_mask, offsets):
     count, length = queries.shape[:2]
     pairs = HEADS * HEAD // 128
     width = HEADS * HEAD
 
     def spec(offset):
-        return pl.BlockSpec((1, length, 128), lambda s, p, info: (s, 0, offset * pairs + p))
-
+        return pl.BlockSpec((1, length, 128), lambda s, p, info: (start + s, 0, offset * pairs + p))
+
+    place = lambda s, p, info: (start + s, p, 0, 0)
     return pl.pallas_call(
-        functools.partial(attend_kernel, use_mask=use_mask),
+        functools.partial(attend_kernel, use_mask=use_mask, start=start),
         grid_spec=pltpu.PrefetchScalarGridSpec(
             num_scalar_prefetch=1,
-            grid=(count, pairs),
-            in_specs=[spec(offset) for offset in offsets],
+            grid=(count_now, pairs),
+            in_specs=[spec(offset) for offset in offsets]
+            + [pl.BlockSpec(memory_space=pl.ANY)] * len(previous),
             out_specs=[
                 spec(0),
-                pl.BlockSpec((1, 2, length, length), lambda s, p, info: (s, p, 0, 0)),
-                pl.BlockSpec((1, 1, 2, length), lambda s, p, info: (s, p, 0, 0)),
+                pl.BlockSpec((1, 2, length, length), place),
+                pl.BlockSpec((1, 1, 2, length), place),
             ],
         ),
         out_shape=[
@@ -367,14 +370,15 @@
             jax.ShapeDtypeStruct((count, HEADS, length, length), jnp.bfloat16),
             jax.ShapeDtypeStruct((count, pairs, 2, length), jnp.float32),
         ],
-        compiler_params=pltpu.CompilerParams(vmem_limit_bytes=ATTEND_LIMIT),
+        input_output_aliases={4: 0, 5: 1, 6: 2} if previous else {},
+        compiler_params=pltpu.CompilerParams(vmem_limit_bytes=LIMIT),
         cost_estimate=pl.CostEstimate(
-            flops=4 * count * HEADS * length * length * 256,
-            bytes_accessed=count * HEADS * length * length * 2,
-            transcendentals=count * HEADS * length * length,
+            flops=4 * count_now * HEADS * length * length * 256,
+            bytes_accessed=count_now * HEADS * length * length * 2,
+            transcendentals=count_now * HEADS * length * length,
         ),
         name="attend",
-    )(info, queries, keys, values)
+    )(info, queries, keys, values, *previous)
 
 
 def attend_back_kernel(q_ref, k_ref, v_ref, o_ref, g_ref, e_ref, r_ref, dq_ref, dk_ref, dv_ref):
@@ -437,7 +441,7 @@
         out_specs=[spec(0)] * 3,
         out_shape=[jax.ShapeDtypeStruct((count, length, width), jnp.bfloat16)] * 3,
         input_output_aliases=aliases,
-        compiler_params=pltpu.CompilerParams(vmem_limit_bytes=ATTEND_LIMIT),
+        compiler_params=pltpu.CompilerParams(vmem_limit_bytes=LIMIT),
         cost_estimate=pl.CostEstimate(
             flops=16 * size[0] * size[1] * length * length * 256,
             bytes_accessed=4 * size[0] * size[1] * length * length,
@@ -489,7 +493,7 @@
 
 
 def pick(take_first, first_ref, second_ref):
-    return lax.cond(take_first, lambda: first_ref[...], lambda: second_ref[...])
+    return jnp.where(take_first, first_ref[...], second_ref[...])
 
 
 ONCE = {"pipeline_mode": pl.Buffered(1)}
@@ -525,7 +529,7 @@
         ),
         out_shape=outs,
         compiler_params=pltpu.CompilerParams(
-            vmem_limit_bytes=more.pop("limit", 48) * 2**20
+            vmem_limit_bytes=more.pop("limit", LIMIT)
         ),
         cost_estimate=pl.CostEstimate(flops=flops, bytes_accessed=moved, transcendentals=0),
         name=name,
@@ -533,7 +537,8 @@
     )(info, *arrays)
 
 
-def enter_kernel(info_ref, own_ref, got_ref, w_ref, vec_ref, bias_ref, x_ref, out_ref, *, norm):
+def enter_kernel(info_ref, own_ref, got_ref, w_ref, vec_ref, bias_ref, *refs, norm):
+    x_ref, out_ref = refs[-2:]
     x = pick(pl.program_id(0) % 2 == 0, own_ref, got_ref)
     x_ref[...] = x
     if norm:
@@ -548,23 +553,28 @@
         out_ref[:, part] = total.astype(jnp.bfloat16)
 
 
-def enter(info, owns, gots, weight, vectors, bias, norm):
-    held, own, width = gots.shape
+def enter(info, at, previous, held, owns, gots, weight, vectors, bias, norm):
+    count, own, width = gots.shape
     rows = 2 * held * own
-    last = 2 * held - 1
     wide = weight.shape[1]
+    own_rows = pl.BlockSpec(
+        (None, own, width), lambda step, info: (info[0] * held + at + step // 2, 0, 0)
+    )
+    row = lambda step, info: (2 * at + step, 0)
     return kernel_call(
         functools.partial(enter_kernel, norm=norm),
         "enter",
         info,
-        (owns, gots, weight, vectors, bias),
-        [own_spec(own, width, held, last), got_spec(own, width, last)]
-        + [resident(a) for a in (weight, vectors, bias)],
+        (owns, gots, weight, vectors, bias, *previous),
+        [own_rows, got_spec(own, width, 2 * count - 1)]
+        + [resident(a) for a in (weight, vectors, bias)]
+        + [pl.BlockSpec(memory_space=pl.ANY)] * len(previous),
         [like((rows, width), jnp.bfloat16), like((rows, wide), jnp.bfloat16)],
-        [row_spec(own, width, last), row_spec(own, wide, last)],
-        2 * held,
-        2 * rows * width * wide,
-        2 * rows * (2 * width + wide),
+        [pl.BlockSpec((own, width), row), pl.BlockSpec((own, wide), row)],
+        2 * count,
+        4 * count * own * width * wide,
+        4 * count * own * (2 * width + wide),
+        input_output_aliases={6: 0, 7: 1} if previous else {},
     )
 
 
@@ -614,18 +624,41 @@
         sent_ref[0, place, :] = low[:half]
 
 
+def write_wide(core, rows, kept_ref, sent_ref, start):
+    half, width = rows.shape[0] // 2, kept_ref.shape[2]
+    for at in range(rows.shape[1] // width):
+        part = rows[:, at * width : (at + 1) * width]
+        write_split(core, part, kept_ref, sent_ref, start + at * half)
+
+
 def acc_rows(ref, at, rows):
     return ref[pl.ds(pl.multiple_of(at * rows, 16), rows), :]
 
 
-def piece(parts, high, wide, steps):
-    late = lambda g, info: (jnp.maximum(g - steps, 0), 0, 0)
+def piece(parts, high, wide, steps, order):
+    bits = parts.bit_length() - 2
+
+    def late(step, info):
+        at = jnp.maximum(step - steps, 0)
+        place = 0
+        for bit in order(bits):
+            place = 2 * place + (at // 2**bit) % 2
+        return (place, 0, 0)
+
     return (
         [pl.BlockSpec((1, high, wide), late)] * 2,
         [like((parts // 2, high, wide), jnp.bfloat16)] * 2,
     )
 
 
+def low_first(bits):
+    return list(range(bits))
+
+
+def second_first(bits):
+    return list(range(bits))[1:2] + [0] + list(range(2, bits))
+
+
 def put_rows(step, value, own_ref, got_ref):
     @pl.when(step % 2 == 0)
     def _():
@@ -638,8 +671,8 @@
 
 def feed_kernel(
     info_ref, x_ref, mixed_ref, dyo_ref, dyg_ref, wc_ref, wi_ref, wo_ref, vec_ref, bi_ref,
-    own_ref, got_ref, dx_ref, do_ref, vsum_ref, bsum_ref, ki_ref, si_ref, ko_ref, so_ref,
-    ai_ref, ao_ref, ac_ref, *, steps, chunk, parts,
+    own_ref, got_ref, dx_ref, do_ref, vsum_ref, bsum_ref, kept_ref, sent_ref, ai_ref, ao_ref,
+    ac_ref, *, steps, chunk, parts,
 ):
     step = pl.program_id(0)
 
@@ -689,12 +722,13 @@
     def _():
         at = step - steps
         core = info_ref[1]
-        rows = 2 * ki_ref.shape[1]
-        inner = 2 * ai_ref.shape[1] // parts
-        write_split(core, acc_rows(ai_ref, at, rows), ki_ref, si_ref, 0)
+        width, wide = ai_ref.shape
+        rows = 2 * width // parts
+        inner = 2 * wide // parts
         columns = ao_ref[:, pl.ds(pl.multiple_of(at * inner, 128), inner)]
-        write_split(core, columns.astype(jnp.bfloat16).T, ko_ref, so_ref, 0)
-        write_split(core, acc_rows(ac_ref, at, rows), ko_ref, so_ref, inner // 2)
+        write_split(core, columns.astype(jnp.bfloat16).T, kept_ref, sent_ref, 0)
+        write_split(core, acc_rows(ac_ref, at, rows), kept_ref, sent_ref, inner // 2)
+        write_wide(core, acc_rows(ai_ref, at, rows), kept_ref, sent_ref, (inner + rows) // 2)
 
 
 def feed(info, x1, mixed, dys, dy_gots, wc, wi, wo, vectors, bi, parts, chunk=768):
@@ -705,10 +739,7 @@
     steps = 2 * held
     last = steps - 1
     row = row_spec(own, width, last)
-    pieces = [
-        piece(parts, width // parts, inner, steps),
-        piece(parts, (inner + width) // parts, width, steps),
-    ]
+    pieces = [piece(parts, (2 * inner + width) // parts, width, steps, low_first)]
     sums = [like((8, width)), like((1, inner))]
     return kernel_call(
         functools.partial(feed_kernel, steps=steps, chunk=chunk, parts=parts),
@@ -737,14 +768,14 @@
             pltpu.VMEM((width, inner), jnp.float32),
             pltpu.VMEM((width, width), jnp.float32),
         ],
-        limit=62,
+        limit=LIMIT,
     )
 
 
 def return_kernel(
     info_ref, dq_ref, dk_ref, dv_ref, x_ref, dx_ref, mixed_ref, src_ref, wq_ref, wi_ref, wo_ref,
-    vec_ref, own_ref, got_ref, dxo_ref, do_ref, vsum_ref, ka_ref, sa_ref, kb_ref, sb_ref,
-    aq_ref, ao_ref, ai_ref, *, steps,
+    vec_ref, own_ref, got_ref, dxo_ref, do_ref, vsum_ref, kept_ref, sent_ref, aq_ref, ao_ref,
+    ai_ref, *, steps, parts,
 ):
     step = pl.program_id(0)
 
@@ -782,10 +813,10 @@
     def _():
         at = step - steps
         core = info_ref[1]
-        rows = 2 * ka_ref.shape[1]
-        write_split(core, acc_rows(ai_ref, at, rows), ka_ref, sa_ref, 0)
-        write_split(core, acc_rows(aq_ref, at, rows), kb_ref, sb_ref, 0)
-        write_split(core, acc_rows(ao_ref, at, rows), kb_ref, sb_ref, rows // 2)
+        rows = 2 * aq_ref.shape[0] // parts
+        write_split(core, acc_rows(aq_ref, at, rows), kept_ref, sent_ref, 0)
+        write_split(core, acc_rows(ao_ref, at, rows), kept_ref, sent_ref, rows // 2)
+        write_wide(core, acc_rows(ai_ref, at, rows), kept_ref, sent_ref, rows)
 
 
 def return_rows(info, grads, x1, dx2, mixed, sources, wq, wi, wo, vectors, own, micros, parts):
@@ -794,13 +825,10 @@
     steps = 2 * held
     last = steps - 1
     row = row_spec(own, width, last)
-    pieces = [
-        piece(parts, width // parts, 2 * width, steps),
-        piece(parts, 2 * width // parts, width, steps),
-    ]
+    pieces = [piece(parts, 4 * width // parts, width, steps, low_first)]
     sums = like((8, width))
     return kernel_call(
-        functools.partial(return_kernel, steps=steps),
+        functools.partial(return_kernel, steps=steps, parts=parts),
         "return_rows",
         info,
         (*grads, x1, dx2, mixed, sources, wq, wi, wo, vectors),
@@ -823,7 +851,6 @@
             pltpu.VMEM((width, width), jnp.float32),
             pltpu.VMEM((width, 2 * width), jnp.float32),
         ],
-        limit=56,
     )
 
 
@@ -857,7 +884,10 @@
     rows, width = x.shape
     steps = rows // own
     row = row_spec(own, width, steps - 1)
-    pieces = [piece(parts, width // parts, 3 * width // 2, steps)] * 2
+    pieces = [
+        piece(parts, width // parts, 3 * width // 2, steps, order)
+        for order in (low_first, second_first)
+    ]
     return kernel_call(
         functools.partial(last_weight_kernel, steps=steps),
         "last_weight",
@@ -932,9 +962,9 @@
 class Tree:
     def __init__(self, kept, sent, order):
         self.count = lax.axis_size("dp")
-        self.bits = [1 << i for i in reversed(range(1, self.count.bit_length() - 1))]
-        self.order = [bit for bit in order(self.bits)]
-        shape = (2,) * len(self.bits) + kept.shape[1:]
+        bits = self.count.bit_length() - 2
+        shape = (2,) * bits + kept.shape[1:]
+        self.order = [2 << bit for bit in order(bits)]
         self.kept, self.sent, self.bit = kept.reshape(shape), sent.reshape(shape), 1
         self.got, self.total = None, None
 
@@ -955,26 +985,38 @@
         if not self.bit:
             self.total = total
             return
-        self.kept = total.astype(jnp.bfloat16)
+        total = total.astype(jnp.bfloat16)
         if not self.order:
-            self.bit = 0
+            self.bit, self.kept = 0, total
             return
         self.bit = self.order.pop(0)
-        axis = self.bits.index(self.bit)
-        self.bits.remove(self.bit)
         mine = (lax.axis_index("dp") // self.bit) % 2
-        whole = self.kept
-        self.kept = lax.dynamic_index_in_dim(whole, mine, axis, keepdims=False)
-        self.sent = lax.dynamic_index_in_dim(whole, 1 - mine, axis, keepdims=False)
-
-
-def low_first(bits):
-    return bits[::-1]
-
-
-def second_first(bits):
-    turned = bits[::-1]
-    return turned[1:2] + turned[:1] + turned[2:]
+        self.kept = lax.dynamic_index_in_dim(total, mine, 0, keepdims=False)
+        self.sent = lax.dynamic_index_in_dim(total, 1 - mine, 0, keepdims=False)
+
+
+class Whole:
+    def __init__(self, rows):
+        self.count = lax.axis_size("dp")
+        self.rows, self.bit, self.got, self.total = rows, 1, None, None
+
+    def exchange(self):
+        if self.total is not None or self.got is not None:
+            return
+        if self.bit < self.count:
+            pairs = [(i, i ^ self.bit) for i in range(self.count)]
+            self.got = lax.ppermute(self.rows, "dp", pairs)
+        else:
+            self.got = lax.ppermute(self.rows, "seq", SWAP)
+
+    def add(self):
+        if self.got is None:
+            return
+        self.rows = self.rows + self.got
+        self.got = None
+        if self.bit == self.count:
+            self.total = self.rows
+        self.bit *= 2
 
 
 def exchange(trees):
@@ -1033,12 +1075,12 @@
     length = 2 * own
     pairs = HEADS * HEAD // 128
 
-    def swap(rows):
-        sent = lax.dynamic_slice_in_dim(rows, (1 - side) * held, held, axis=0)
+    def swap(rows, at, count):
+        sent = lax.dynamic_slice_in_dim(rows, (1 - side) * held + at, count, axis=0)
         return lax.ppermute(sent, "seq", SWAP)
 
     def give(owns, got, at):
-        got = lax.ppermute(got, "seq", SWAP).astype(owns.dtype)
+        got = got.astype(owns.dtype)
         return lax.dynamic_update_slice_in_dim(owns, got, (1 - side) * held + at, axis=0)
 
     def pack(*rows):
@@ -1052,23 +1094,29 @@
         return rows.reshape(held * length, -1)
 
     targets, memory = targets[:, 0], memory[:, 0]
-    target_gots = swap(targets)
-    memory_gots = swap(memory)
+    target_gots = [swap(targets, at, 1) for at in range(held)]
+    memory_gots = swap(memory, 0, held)
     upstreams = (
         cotangent[:, 0].astype(jnp.float32) * loss_mask[:, 0].astype(jnp.float32)[..., None]
     ).astype(jnp.bfloat16)
-    upstream_gots = swap(upstreams)
+    upstream_gots = swap(upstreams, 0, held)
     kinds = lax.dynamic_slice_in_dim(row_kind[:, 0], side * held, held, axis=0)
     info = jnp.concatenate([jnp.stack([side, place % 2]).astype(jnp.int32), kinds])
 
     self_vectors = pack(norm_self_gain, norm_self_bias)
     zero = jnp.zeros_like(self_query_bias)
     joint_bias = jnp.concatenate([self_query_bias, zero, self_value_bias])[None]
-    inputs, joint = enter(
-        info, targets, target_gots, self_input, self_vectors, joint_bias, True
-    )
-    joint = batch(joint)
-    self_mixed, self_raised, self_inverse = attend(info, joint, joint, joint, True, (0, 1, 2))
+    entered, attended = (), ()
+    for at in range(held):
+        entered = enter(
+            info, at, entered, held, targets, target_gots[at], self_input, self_vectors,
+            joint_bias, True,
+        )
+        joint = batch(entered[1])
+        attended = attend(info, at, 1, attended, joint, joint, joint, True, (0, 1, 2))
+        entered, attended = lax.optimization_barrier((entered, attended))
+    inputs, joint = entered[0], batch(entered[1])
+    self_mixed, self_raised, self_inverse = attended
     after_self, cross_queries = middle(
         info,
         inputs,
@@ -1080,11 +1128,11 @@
     )
     pair_bias = jnp.concatenate([zero, cross_value_bias])[None]
     sources, cross_pairs = enter(
-        info, memory, memory_gots, cross_input, self_vectors, pair_bias, False
+        info, 0, (), held, memory, memory_gots, cross_input, self_vectors, pair_bias, False
     )
     cross_queries, cross_pairs = batch(cross_queries), batch(cross_pairs)
     cross_mixed, cross_raised, cross_inverse = attend(
-        info, cross_queries, cross_pairs, cross_pairs, False, (0, 0, 1)
+        info, 0, held, (), cross_queries, cross_pairs, cross_pairs, False, (0, 0, 1)
     )
     results, result_gots, grad_cross, cross_upstream, feed_sums, hidden_sums, *feed_parts = feed(
         info,
@@ -1099,19 +1147,19 @@
         feed_in_bias[None],
         parts,
     )
-    feed_trees = [Tree(*feed_parts[0:2], low_first), Tree(*feed_parts[2:4], second_first)]
+    feed_trees = [Tree(*feed_parts, low_first)]
     first = pairs // 2
     cross_inputs = (
         cross_queries, cross_pairs, cross_pairs, (0, 0, 1), cross_mixed, batch(cross_upstream),
         cross_raised, cross_inverse,
     )
     exchange(feed_trees)
-    half_grads = settle(feed_trees, attend_back((0, 0), (held, first), (), *cross_inputs))
+    result_gots = lax.ppermute(result_gots, "seq", SWAP)
+    half_grads, result_gots = settle(
+        feed_trees, (attend_back((0, 0), (held, first), (), *cross_inputs), result_gots)
+    )
     exchange(feed_trees)
-    cross_grads = settle(
-        feed_trees, attend_back((0, first), (held, pairs - first), half_grads, *cross_inputs)
-    )
-    exchange(feed_trees)
+    cross_grads = attend_back((0, first), (held, pairs - first), half_grads, *cross_inputs)
     source_grads, source_gots, grad_self, self_upstream, return_sums, *mid_parts = settle(
         feed_trees,
         return_rows(
@@ -1130,72 +1178,87 @@
             parts,
         ),
     )
-    mid_trees = [Tree(*mid_parts[0:2], low_first), Tree(*mid_parts[2:4], second_first)]
+    early_sums = Whole(
+        jnp.concatenate([feed_sums, return_sums, hidden_sums.reshape(-1, width)], axis=0)
+    )
+    mid_trees = [Tree(*mid_parts, low_first), early_sums]
     exchange(feed_trees + mid_trees)
     self_inputs = (
         joint, joint, joint, (0, 1, 2), self_mixed, batch(self_upstream), self_raised, self_inverse
     )
-    grads = settle(feed_trees + mid_trees, attend_back((0, 0), (1, pairs), (), *self_inputs))
+    source_gots = lax.ppermute(source_gots, "seq", SWAP)
+    grads, source_gots = settle(
+        feed_trees + mid_trees,
+        (attend_back((0, 0), (1, pairs), (), *self_inputs), source_gots),
+    )
     exchange(feed_trees + mid_trees)
-    input_grads, leave_sums, leave_gots = (), [], []
-
-    def leave_one(at, grads, input_grads):
-        input_grads, got, sums = leave(
-            info, at, input_grads, [flat(rows) for rows in grads], inputs, grad_self,
+    kept, leave_sums = (), []
+    trees = feed_trees + mid_trees
+    for at in range(held):
+        if at == held - 1:
+            late_parts = last_weight(
+                info, [flat(rows) for rows in grads], inputs, self_vectors, own, parts
+            )
+            late_trees = [
+                Tree(*late_parts[0:2], low_first),
+                Tree(*late_parts[2:4], second_first),
+            ]
+            trees = trees + late_trees
+            exchange(trees)
+            grads, _ = lax.optimization_barrier((grads, late_parts[0]))
+        kept, got, sums = leave(
+            info, at, kept, [flat(rows) for rows in grads], inputs, grad_self,
             self_input, self_vectors, own, micros,
         )
         leave_sums.append(sums)
-        leave_gots.append(got[None])
-        return (input_grads,)
-
-    for at in range(held - 1):
-        input_grads = leave_one(at, grads, input_grads)
-        grads, input_grads = lax.optimization_barrier((grads, input_grads))
-        grads = settle(
-            feed_trees + mid_trees, attend_back((at + 1, 0), (1, pairs), grads, *self_inputs)
-        )
-        exchange(feed_trees + mid_trees)
-    late_parts = last_weight(
-        info, [flat(rows) for rows in grads], inputs, self_vectors, own, parts
-    )
-    late_trees = [Tree(*late_parts[0:2], low_first), Tree(*late_parts[2:4], second_first)]
-    exchange(late_trees)
-    grads, _ = lax.optimization_barrier((grads, late_parts[0]))
-    (input_grads,) = leave_one(held - 1, grads, input_grads)
-    leave_sums = sum(leave_sums)
-    small = [
-        (0, leave_sums[0]), (1, leave_sums[1]), (3, leave_sums[2]), (4, leave_sums[3]),
-        (6, return_sums[2]), (7, return_sums[0]), (8, return_sums[1]), (10, return_sums[3]),
-        (12, return_sums[4]), (14, feed_sums[0]), (15, feed_sums[1]), (16, feed_sums[2]),
-        (20, feed_sums[3]), (18, hidden_sums[0]),
-    ]
-    joined = jnp.concatenate([row.reshape(parts, -1) for _, row in small], axis=1)
-    halves = joined.astype(jnp.bfloat16).reshape(parts // 2, 2, 1, -1)
-    small_tree = Tree(
-        lax.dynamic_index_in_dim(halves, place % 2, 1, keepdims=False),
-        lax.dynamic_index_in_dim(halves, 1 - place % 2, 1, keepdims=False),
-        low_first,
-    )
-    finish(feed_trees + mid_trees + late_trees)
-    finish([small_tree])
+        if at < held - 1:
+            grads, kept = lax.optimization_barrier((grads, kept))
+            back = lax.ppermute(got, "seq", SWAP)
+            grads, back = settle(
+                trees,
+                (attend_back((at + 1, 0), (1, pairs), grads, *self_inputs), back),
+            )
+            exchange(trees)
+            back = back.astype(kept.dtype)[None]
+            kept = (
+                lax.dynamic_update_slice_in_dim(kept, back, (1 - side) * held + at, axis=0),
+            )
+    input_grads, got, sums = settle(trees, (kept, got, sum(leave_sums)))
+    late_sums = Whole(sums)
+    trees = trees + [late_sums]
+    exchange(trees)
+    back = lax.ppermute(got, "seq", SWAP)
+    settle(trees, ())
+    exchange(trees)
+    back = settle(trees, back)
+    exchange(trees)
+    input_grads = give(input_grads, back[None], held - 1)
+    finish(trees)
     rows = width // parts
+    inner_rows = feed_in.shape[1] // parts
     final = [None] * 21
-    for index, row in small:
-        size = row.shape[0] // parts
-        final[index] = small_tree.total[0, :size]
-        small_tree.total = small_tree.total[:, size:]
-    inner_rows = feed_in.shape[1] // parts
-    final[17] = feed_trees[0].total
-    final[19] = feed_trees[1].total[:inner_rows]
-    final[13] = feed_trees[1].total[inner_rows:]
-    final[11] = mid_trees[0].total
-    final[9] = mid_trees[1].total[:rows]
-    final[5] = mid_trees[1].total[rows:]
+
+    def mine(row):
+        return lax.dynamic_slice_in_dim(row, place * (row.shape[0] // parts), row.shape[0] // parts)
+
+    def widen(block):
+        return jnp.concatenate([block[i : i + rows] for i in range(0, len(block), rows)], axis=1)
+
+    for index, at in ((14, 0), (15, 1), (16, 2), (20, 3), (7, 8), (8, 9), (6, 10), (10, 11), (12, 12)):
+        final[index] = mine(early_sums.total[at])
+    final[18] = mine(early_sums.total[16:].reshape(-1))
+    for index, at in ((0, 0), (1, 1), (3, 2), (4, 3)):
+        final[index] = mine(late_sums.total[at])
+    feed_total, mid_total = feed_trees[0].total, mid_trees[0].total
+    final[19] = feed_total[:inner_rows]
+    final[13] = feed_total[inner_rows : inner_rows + rows]
+    final[17] = widen(feed_total[inner_rows + rows :])
+    final[9] = mid_total[:rows]
+    final[5] = mid_total[rows : 2 * rows]
+    final[11] = widen(mid_total[2 * rows :])
     final[2] = jnp.concatenate([tree.total for tree in late_trees], axis=1)
     results = give(results, result_gots, 0)
     source_grads = give(source_grads, source_gots, 0)
-    for at in range(held):
-        input_grads = give(input_grads, leave_gots[at], at)
     return (results[:, None], input_grads[:, None], source_grads[:, None]) + tuple(final)
 
 

time: 622 us -> 598 us (0.961)
  local copies, waits for them, and re-layouts: 67.4 us -> 29.4 us
  Pallas kernels: 412 us -> 422 us
  starting transfers between devices: 46.3 us -> 39.7 us
    ppermute x4 -> x14, waiting for transfers between devices: 0.01 us -> 29.4 us  [the longest x8 16.3 us: exchange(): self.got = lax.ppermute(self.rows, 'dp', pairs)]
    ppermute x28 -> x16, waiting for transfers between devices: 27.8 us -> 3.96 us  [exchange(): self.got = lax.ppermute(self.sent, 'dp', pairs)]
    unnamed x149 -> x71, local copies, waits for them, and re-layouts: 26.5 us -> 9.3 us
    ppermute x28 -> x16, starting transfers between devices: 30.2 us -> 13.4 us  [exchange(): self.got = lax.ppermute(self.sent, 'dp', pairs)]
    concatenate x15 -> x1, local copies, waits for them, and re-layouts: 14.5 us -> 0.01 us  [whole_sequences(): jnp.concatenate([feed_sums, return_sums, hidden_sums.reshape(-1, width)],...]
    ppermute x4 -> x14, starting transfers between devices: 3.61 us -> 16.7 us  [the longest x8 9.65 us: exchange(): self.got = lax.ppermute(self.rows, 'dp', pairs)]
    reshape x6 -> x2, local copies, waits for them, and re-layouts: 9.44 us -> 0.02 us  [the longest x1 0.01 us: whole_sequences(): final[18] = mine(early_sums.total[16:].reshape(-1))]
    pallas_call x8 -> x9, Pallas kernels: 224 us -> 232 us  [kernel_call(): pl.pallas_call(kernel, grid_spec=pltpu.PrefetchScalarGridSpec(num_scalar_...]
  transfers between devices with their start and end apart: 42 -> 38, of which waited for: 15 -> 11; matrix products, arithmetic and copies ran while one was open for 9% -> 6% of each run, Pallas kernels for 49% -> 53%
where the time goes in v4:
time: 598 us; the launch traced here: 589 us
  Pallas kernels  422 us (71%)
  waiting for transfers between devices  58.5 us (10%)
  starting transfers between devices  39.7 us (7%)
  other arithmetic  36.7 us (6%)
  local copies, waits for them, and re-layouts  29.4 us (5%)
    pallas_call x9, Pallas kernels, kernel_call(): pl.pallas_call(kernel, grid_spec=pltpu.PrefetchScalarGridSpec(num_scalar_...  232 us
    pallas_call x4, Pallas kernels, attend_back(): pl.pallas_call(kernel, grid=size, in_specs=[pl.BlockSpec(memory_space=pl....  123 us
    pallas_call x3, Pallas kernels, attend(): pl.pallas_call(functools.partial(attend_kernel, use_mask=use_mask, start=...  67.2 us
    ppermute x4, waiting for transfers between devices, swap(): return lax.ppermute(sent, 'seq', SWAP)  25.1 us
    convert_element_type x16, other arithmetic, add(): total = total.astype(jnp.bfloat16)  20.8 us
    ppermute x8, waiting for transfers between devices, exchange(): self.got = lax.ppermute(self.rows, 'dp', pairs)  16.3 us
    ppermute x16, starting transfers between devices, exchange(): self.got = lax.ppermute(self.sent, 'dp', pairs)  13.4 us
  transfers between devices with their start and end apart: 38, of which 11 were waited for; matrix products, arithmetic and copies ran while one was open for 6% of the time, Pallas kernels for 53%

profile of v4, /device:TPU:0, one launch (start us, length us, event | category | flops | bytes accessed | tf_op | source)
XLA Modules:
  0.0 588.5 jit_solution(4946756521688003422)
XLA Ops:
  0.7 2.8 dynamic-slice_bitcast_fusion.4
  3.5 3.0 collective-permute-start
  6.5 1.2 dynamic-slice_bitcast_fusion.1
  7.7 2.0 collective-permute-start.2
  10.3 1.7 copy-done.5
  16.9 25.1 %collective-permute-done.1.got_ref = bf16[1,512,768]{2,1,0:T(8,128)(2,1)} collective-permute-done((bf16[1,512,768]{2,1,0:T(8,128)(2,1)}, bf16[1,512,768]{2,1,0:T(8,128)(2,1)}, u32[]{:S(2)}, u32[]{:S(2)}) %collective-permute-start.1) | collective-permute-done | bytes 786464 | tf_op jit(solution)/shard_map/ppermute | solution.py:1080
  42.0 9.4 %enter.3 = (bf16[2048,768]{1,0:T(8,128)(2,1)}, bf16[2048,2304]{1,0:T(8,128)(2,1)}) custom-call(s32[4]{0:T(128)} %pad_add_fusion.info_ref, bf16[4,512,768]{2,1,0:T(8,128)(2,1)} %bitcast.181, bf16[1,512,768]{2,1,0:T(8,128)(2,1)} %collective-permute-done.1.got_ref, bf16[768,2304]{1,0:T(8,128)(2,1)} %w_ref.9, f32[8,768]{1,0:T(8,128)} %get-tuple-element.319.vec_ref, ...), custom_call_target="tpu_custom_call" | custom-call | flops 3623878656 | bytes 7864320 | tf_op jit(solution)/shard_map/enter/pallas_call | solution.py:521
  51.4 18.4 %attend.3 = (bf16[2,1024,768]{2,1,0:T(8,128)(2,1)}, bf16[2,12,1024,1024]{3,2,1,0:T(8,128)(2,1)}, f32[2,6,2,1024]{3,2,1,0:T(2,128)}) custom-call(s32[4]{0:T(128)} %pad_add_fusion.info_ref, bf16[2,1024,2304]{2,1,0:T(8,128)(2,1)} %bitcast.160, bf16[2,1024,2304]{2,1,0:T(8,128)(2,1)} %bitcast.161, bf16[2,1024,2304]{2,1,0:T(8,128)(2,1)} %bitcast.162), custom_call_target="tpu_custom_call" | custom-call | flops 12884901888 | bytes 25165824 | tf_op jit(solution)/shard_map/attend/pallas_call | solution.py:355
  69.8 9.5 %enter.4 = (bf16[2048,768]{1,0:T(8,128)(2,1)}, bf16[2048,2304]{1,0:T(8,128)(2,1)}) custom-call(s32[4]{0:T(128)} %pad_add_fusion.info_ref, bf16[4,512,768]{2,1,0:T(8,128)(2,1)} %bitcast.182, bf16[1,512,768]{2,1,0:T(8,128)(2,1)} %collective-permute-done.got_ref, bf16[768,2304]{1,0:T(8,128)(2,1)} %w_ref.9, ...), custom_call_target="tpu_custom_call", output_to_operand_aliasing={{0}: (6, {}), {1}: (7, {})} | custom-call | flops 3623878656 | bytes 7864320 | tf_op jit(solution)/shard_map/enter/pallas_call | solution.py:521
  79.3 17.7 %attend.4 = (bf16[2,1024,768]{2,1,0:T(8,128)(2,1)}, bf16[2,12,1024,1024]{3,2,1,0:T(8,128)(2,1)}, f32[2,6,2,1024]{3,2,1,0:T(2,128)}) custom-call(s32[4]{0:T(128)} %pad_add_fusion.info_ref, bf16[2,1024,2304]{2,1,0:T(8,128)(2,1)} %bitcast.163, bf16[2,1024,2304]{2,1,0:T(8,128)(2,1)} %bitcast.164, ...), custom_call_target="tpu_custom_call", output_to_operand_aliasing={{0}: (4, {}), {1}: (5, {}), {2}: (6, {})} | custom-call | flops 12884901888 | bytes 25165824 | tf_op jit(solution)/shard_map/attend/pallas_call | solution.py:355
  97.0 12.4 %middle.1 = (f32[2048,768]{1,0:T(8,128)}, bf16[2048,768]{1,0:T(8,128)(2,1)}) custom-call(s32[4]{0:T(128)} %pad_add_fusion.info_ref, bf16[2048,768]{1,0:T(8,128)(2,1)} %get-tuple-element.162.x_ref, bf16[2048,768]{1,0:T(8,128)(2,1)} %bitcast.184, bf16[768,768]{1,0:T(8,128)(2,1)} %wo_ref.5, bf16[768,768]{1,0:T(8,128)(2,1)} %wq_ref.3, f32[8,768]{1,0:T(8,128)} %concatenate.36.vec_ref), custom_call_target="tpu_custom_call" | custom-call | flops 4831838208 | bytes 15728640 | tf_op jit(solution)/shard_map/middle/pallas_call | solution.py:521
  109.4 10.5 %enter.5 = (bf16[2048,768]{1,0:T(8,128)(2,1)}, bf16[2048,1536]{1,0:T(8,128)(2,1)}) custom-call(s32[4]{0:T(128)} %pad_add_fusion.info_ref, bf16[4,512,768]{2,1,0:T(8,128)(2,1)} %bitcast.189, bf16[2,512,768]{2,1,0:T(8,128)(2,1)} %collective-permute-done.2.got_ref, bf16[768,1536]{1,0:T(8,128)(2,1)} %wi_ref.3, f32[8,768]{1,0:T(8,128)} %get-tuple-element.319.vec_ref, ...), custom_call_target="tpu_custom_call" | custom-call | flops 4831838208 | bytes 12582912 | tf_op jit(solution)/shard_map/enter/pallas_call | solution.py:521
  119.9 31.1 %attend.5 = (bf16[2,1024,768]{2,1,0:T(8,128)(2,1)}, bf16[2,12,1024,1024]{3,2,1,0:T(8,128)(2,1)}, f32[2,6,2,1024]{3,2,1,0:T(2,128)}) custom-call(s32[4]{0:T(128)} %pad_add_fusion.info_ref, bf16[2,1024,768]{2,1,0:T(8,128)(2,1)} %bitcast.205, bf16[2,1024,1536]{2,1,0:T(8,128)(2,1)} %bitcast.199, bf16[2,1024,1536]{2,1,0:T(8,128)(2,1)} %bitcast.200), custom_call_target="tpu_custom_call" | custom-call | flops 25769803776 | bytes 50331648 | tf_op jit(solution)/shard_map/attend/pallas_call | solution.py:355
  151.0 108.1 %feed.1 = (bf16[4,512,768]{2,1,0:T(8,128)(2,1)}, bf16[2,512,768]{2,1,0:T(8,128)(2,1)}, f32[2048,768]{1,0:T(8,128)}, bf16[2048,768]{1,0:T(8,128)(2,1)}, f32[8,768...) custom-call(s32[4]{0:T(128)} %pad_add_fusion.info_ref, ...), custom_call_target="tpu_custom_call" | custom-call | flops 65229815808 | bytes 62914560 | tf_op jit(solution)/shard_map/feed/pallas_call | solution.py:521
  259.2 3.1 collective-permute-start.5
  262.9 1.4 reduce.3
  265.0 30.7 %attend_back.4 = (bf16[2,1024,768]{2,1,0:T(8,128)(2,1)}, bf16[2,1024,768]{2,1,0:T(8,128)(2,1)}, bf16[2,1024,768]{2,1,0:T(8,128)(2,1)}) custom-call(bf16[2,1024,768]{2,1,0:T(8,128)(2,1)} %bitcast.206, bf16[2,1024,1536]{2,1,0:T(8,128)(2,1)} %bitcast.201, bf16[2,1024,1536]{2,1,0:T(8,128)(2,1)} %bitcast.202, ...), custom_call_target="tpu_custom_call" | custom-call | flops 25769803776 | bytes 25165824 | tf_op jit(solution)/shard_map/attend_back/pallas_call | solution.py:430
  295.7 1.8 collective-permute-done.5
  297.5 5.3 fusion
  302.8 2.3 copy-done.2
  305.1 1.7 dynamic-slice_bitcast_fusion
  306.8 1.5 collective-permute-start.6
  308.2 30.6 %attend_back.5 = (bf16[2,1024,768]{2,1,0:T(8,128)(2,1)}, bf16[2,1024,768]{2,1,0:T(8,128)(2,1)}, bf16[2,1024,768]{2,1,0:T(8,128)(2,1)}) custom-call(bf16[2,1024,768]{2,1,0:T(8,128)(2,1)} %get-tuple-element.180.refs_0_, bf16[2,1024,768]{2,1,0:T(8,128)(2,1)} %get-tuple-element.181.refs_1_, ...), custom_call_target="tpu_custom_call", output_to_operand_aliasing={{0}: (0, {}), {1}: (1, {}), {2}: (2, {})} | custom-call | flops 25769803776 | bytes 25165824 | tf_op jit(solution)/shard_map/attend_back/pallas_call | solution.py:430
  338.9 1.2 bitcast_dynamic-update-slice_fusion
  340.1 41.2 %return_rows.1 = (f32[4,512,768]{2,1,0:T(8,128)}, bf16[2,512,768]{2,1,0:T(8,128)(2,1)}, f32[2048,768]{1,0:T(8,128)}, bf16[2048,768]{1,0:T(8,128)(2,1)}, f32[8,76...) custom-call(s32[4]{0:T(128)} %pad_add_fusion.info_ref, bf16[2048,768]{1,0:T(8,128)(2,1)} %bitcast.213, ...), custom_call_target="tpu_custom_call" | custom-call | flops 19327352832 | bytes 41943040 | tf_op jit(solution)/shard_map/return_rows/pallas_call | solution.py:521
  381.3 3.2 fusion.2
  384.5 1.5 copy-done.3
  387.2 1.8 collective-permute-start.7
  389.9 31.0 %attend_back.6 = (bf16[2,1024,768]{2,1,0:T(8,128)(2,1)}, bf16[2,1024,768]{2,1,0:T(8,128)(2,1)}, bf16[2,1024,768]{2,1,0:T(8,128)(2,1)}) custom-call(bf16[2,1024,2304]{2,1,0:T(8,128)(2,1)} %bitcast.166, bf16[2,1024,2304]{2,1,0:T(8,128)(2,1)} %bitcast.167, bf16[2,1024,2304]{2,1,0:T(8,128)(2,1)} %bitcast.168, ...), custom_call_target="tpu_custom_call" | custom-call | flops 25769803776 | bytes 25165824 | tf_op jit(solution)/shard_map/attend_back/pallas_call | solution.py:430
  420.9 5.2 collective-permute-done.10
  427.3 2.0 fusion.4
  429.4 2.6 collective-permute-start.11
  432.1 2.3 fusion.3
  434.4 1.4 copy-done.4
  437.6 2.0 collective-permute-start.13
  439.6 11.8 %leave.2 = (f32[4,512,768]{2,1,0:T(8,128)}, bf16[512,768]{1,0:T(8,128)(2,1)}, f32[8,768]{1,0:T(8,128)}) custom-call(s32[4]{0:T(128)} %pad_add_fusion.info_ref, bf16[2048,768]{1,0:T(8,128)(2,1)} %bitcast.172, bf16[2048,768]{1,0:T(8,128)(2,1)} %bitcast.175, bf16[2048,768]{1,0:T(8,128)(2,1)} %bitcast.178, bf16[2048,768]{1,0:T(8,128)(2,1)} %get-tuple-element.162.x_ref, ...), custom_call_target="tpu_custom_call" | custom-call | flops 3623878656 | bytes 16777216 | tf_op jit(solution)/shard_map/leave/pallas_call | solution.py:521
  451.9 30.6 %attend_back.7 = (bf16[2,1024,768]{2,1,0:T(8,128)(2,1)}, bf16[2,1024,768]{2,1,0:T(8,128)(2,1)}, bf16[2,1024,768]{2,1,0:T(8,128)(2,1)}) custom-call(bf16[2,1024,768]{2,1,0:T(8,128)(2,1)} %get-tuple-element.217.refs_0_, bf16[2,1024,768]{2,1,0:T(8,128)(2,1)} %get-tuple-element.218.refs_1_, ...), custom_call_target="tpu_custom_call", output_to_operand_aliasing={{0}: (0, {}), {1}: (1, {}), {2}: (2, {})} | custom-call | flops 25769803776 | bytes 25165824 | tf_op jit(solution)/shard_map/attend_back/pallas_call | solution.py:430
  482.5 1.2 fusion.8
  483.8 1.6 collective-permute-start.15
  485.4 17.4 %last_weight.1 = (bf16[8,48,1152]{2,1,0:T(8,128)(2,1)}, bf16[8,48,1152]{2,1,0:T(8,128)(2,1)}, bf16[8,48,1152]{2,1,0:T(8,128)(2,1)}, bf16[8,48,1152]{2,1,0:T(8,128)(2,1)}) custom-call(s32[4]{0:T(128)} %pad_add_fusion.info_ref, bf16[2048,768]{1,0:T(8,128)(2,1)} %bitcast.173, bf16[2048,768]{1,0:T(8,128)(2,1)} %bitcast.176, bf16[2048,768]{1,0:T(8,128)(2,1)} %bitcast.179, ...), custom_call_target="tpu_custom_call" | custom-call | flops 7247757312 | bytes 20971520 | tf_op jit(solution)/shard_map/last_weight/pallas_call | solution.py:521
  503.4 1.9 fusion.5
  507.6 1.6 collective-permute-start.17
  509.2 2.4 convert_dynamic-update-slice_fusion.2.refs_0_
  511.6 12.1 %leave.3 = (f32[4,512,768]{2,1,0:T(8,128)}, bf16[512,768]{1,0:T(8,128)(2,1)}, f32[8,768]{1,0:T(8,128)}) custom-call(s32[4]{0:T(128)} %pad_add_fusion.info_ref, bf16[2048,768]{1,0:T(8,128)(2,1)} %bitcast.174, bf16[2048,768]{1,0:T(8,128)(2,1)} %bitcast.177, bf16[2048,768]{1,0:T(8,128)(2,1)} %bitcast.180, ...), custom_call_target="tpu_custom_call", output_to_operand_aliasing={{0}: (8, {})} | custom-call | flops 3623878656 | bytes 16777216 | tf_op jit(solution)/shard_map/leave/pallas_call | solution.py:521
  524.5 1.2 fusion.9
  525.8 1.6 fusion.7
  527.6 1.5 fusion.6
  531.2 2.4 collective-permute-start.21
  533.6 1.9 convert_dynamic-update-slice_fusion
  536.4 10.3 %collective-permute-done.21 = f32[20,768]{1,0:T(8,128)S(1)} collective-permute-done((f32[20,768]{1,0:T(8,128)S(1)}, f32[20,768]{1,0:T(8,128)S(1)}, u32[]{:S(2)}, u32[]{:S(2)}) %collective-permute-start.21) | collective-permute-done | bytes 61472 | tf_op jit(solution)/shard_map/ppermute | solution.py:1008
  546.6 2.0 collective-permute-done.23
  549.5 1.4 collective-permute-start.26
  551.7 1.4 collective-permute-start.29
  553.3 2.5 collective-permute-done.29
  555.8 1.4 collective-permute-start.28
  557.2 1.2 convert_add_fusion.8
  559.3 4.1 collective-permute-done.26
  564.2 2.4 collective-permute-start.32
  566.6 1.6 collective-permute-start.33
  569.2 1.3 convert_dynamic-update-slice_fusion.1
  575.0 1.2 collective-permute-done.32
  577.3 1.2 collective-permute-start.35
  579.7 3.5 collective-permute-done.36
  585.0 2.1 collective-permute-done.37
  (194 shorter events, 33.0 us)
Async XLA Ops:
  0.7 14.9 %copy-start = (s32[4,1]{0,1:T(1,128)S(1)}, s32[4,1]{0,1:T(1,128)}, u32[]{:S(2)}) copy-start(s32[4,1]{0,1:T(1,128)} %param.28) | copy-start | bytes 52
  0.7 5.8 copy-start.11
  0.7 9.0 %copy-start.19 = (s32[4,1,512]{2,1,0:T(1,128)S(1)}, s32[4,1,512]{2,1,0:T(1,128)}, u32[]{:S(2)}) copy-start(s32[4,1,512]{2,1,0:T(1,128)} %param.29) | copy-start | bytes 24580
  0.7 9.0 %copy-start.6 = (bf16[4,1,512,768]{3,2,1,0:T(8,128)(2,1)S(1)}, bf16[4,1,512,768]{3,2,1,0:T(8,128)(2,1)}, u32[]{:S(2)}) copy-start(bf16[4,1,512,768]{3,2,1,0:T(8,128)(2,1)} %param.30) | copy-start | bytes 9437188
  3.5 66.3 %collective-permute-start = (bf16[1,512,768]{2,1,0:T(8,128)(2,1)}, bf16[1,512,768]{2,1,0:T(8,128)(2,1)}, u32[]{:S(2)}, u32[]{:S(2)}) collective-permute-start(bf16[1,512,768]{2,1,0:T(8,128)(2,1)} %get-tuple-element.295), channel_id=1, source_target_pairs={{0,1},{1,0},{2,3},{3,2},{4,5},{5,4},{6,7},{7,6},{8,9},{9,8},{10,11... | collective-permute-start | bytes 2359304 | tf_op jit(solution)/shard_map/ppermute | solution.py:1080
  6.4 35.5 %collective-permute-start.1 = (bf16[1,512,768]{2,1,0:T(8,128)(2,1)}, bf16[1,512,768]{2,1,0:T(8,128)(2,1)}, u32[]{:S(2)}, u32[]{:S(2)}) collective-permute-start(bf16[1,512,768]{2,1,0:T(8,128)(2,1)} %get-tuple-element.294), channel_id=1, source_target_pairs={{0,1},{1,0},{2,3},{3,2},{4,5},{5,4},{6,7},{7,6},{8,9},{9,8},{10,11... | collective-permute-start | bytes 2359304 | tf_op jit(solution)/shard_map/ppermute | solution.py:1080
  7.7 101.7 %collective-permute-start.2 = (bf16[2,512,768]{2,1,0:T(8,128)(2,1)}, bf16[2,512,768]{2,1,0:T(8,128)(2,1)}, u32[]{:S(2)}, u32[]{:S(2)}) collective-permute-start(bf16[2,512,768]{2,1,0:T(8,128)(2,1)} %dynamic-slice_bitcast_fusion.1), channel_id=1, source_target_pairs={{0,1},{1,0},{2,3},{3,2},{4,5},{5,4},{6,7},{7,6},{8,9},{9,8},{10,11... | collective-permute-start | bytes 4718600 | tf_op jit(solution)/shard_map/ppermute | solution.py:1080
  10.3 1.7 copy-start.5
  12.1 1.4 copy-start.25
  12.1 1.4 copy-start.20
  12.1 2.0 copy-start.27
  12.1 2.0 copy-start.28
  12.1 2.0 copy-start.29
  12.1 2.0 copy-start.30
  12.3 138.7 %collective-permute-start.3 = (bf16[2,512,768]{2,1,0:T(8,128)(2,1)S(1)}, bf16[2,512,768]{2,1,0:T(8,128)(2,1)}, u32[]{:S(2)}, u32[]{:S(2)}) collective-permute-start(bf16[2,512,768]{2,1,0:T(8,128)(2,1)S(1)} %constant_dynamic-slice_fusion.13), channel_id=1, source_target_pairs={{0,1},{1,0},{2,3},{3,2},{4,5},{5,4},{6,7},{7,6},{8,9},{9,8},{10,11... | collective-permute-start | bytes 4718600 | tf_op jit(solution)/shard_map/ppermute | solution.py:1080
  259.1 38.4 %collective-permute-start.4 = (bf16[2,2,2,432,768]{4,3,2,1,0:T(8,128)(2,1)}, bf16[2,2,2,432,768]{4,3,2,1,0:T(8,128)(2,1)}, u32[]{:S(2)}, u32[]{:S(2)}) collective-permute-start(bf16[2,2,2,432,768]{4,3,2,1,0:T(8,128)(2,1)} %bitcast.193), channel_id=1, source_target_pairs={{0,2},{2,0},{4,6},{6,4},{8,10},{10,8},{12,14},{14,12},{16,18},{18,... | collective-permute-start | bytes 15925256 | tf_op jit(solution)/shard_map/ppermute | solution.py:976
  259.2 38.2 %collective-permute-start.5 = (bf16[2,512,768]{2,1,0:T(8,128)(2,1)}, bf16[2,512,768]{2,1,0:T(8,128)(2,1)S(1)}, u32[]{:S(2)}, u32[]{:S(2)}) collective-permute-start(bf16[2,512,768]{2,1,0:T(8,128)(2,1)} %get-tuple-element.176), channel_id=1, source_target_pairs={{0,1},{1,0},{2,3},{3,2},{4,5},{5,4},{6,7},{7,6},{8,9},{9,8},{10,11... | collective-permute-start | bytes 4718600 | tf_op jit(solution)/shard_map/ppermute | solution.py:1157
  302.8 2.3 copy-start.2
  306.8 74.5 %collective-permute-start.6 = (bf16[2,2,432,768]{3,2,1,0:T(8,128)(2,1)}, bf16[2,2,432,768]{3,2,1,0:T(8,128)(2,1)}, u32[]{:S(2)}, u32[]{:S(2)}) collective-permute-start(bf16[2,2,432,768]{3,2,1,0:T(8,128)(2,1)} %dynamic-slice_bitcast_fusion), channel_id=1, source_target_pairs={{0,4},{2,6},{4,0},{6,2},{8,12},{10,14},{12,8},{14,10},{16,20},{18,... | collective-permute-start | bytes 7962632 | tf_op jit(solution)/shard_map/ppermute | solution.py:976
  381.3 7.7 %copy-start.17 = (f32[8,768]{1,0:T(8,128)S(1)}, f32[8,768]{1,0:T(8,128)}, u32[]{:S(2)}) copy-start(f32[8,768]{1,0:T(8,128)} %get-tuple-element.198) | copy-start | bytes 73732
  384.5 1.5 copy-start.3
  387.2 33.8 %collective-permute-start.7 = (bf16[2,432,768]{2,1,0:T(8,128)(2,1)}, bf16[2,432,768]{2,1,0:T(8,128)(2,1)}, u32[]{:S(2)}, u32[]{:S(2)}) collective-permute-start(bf16[2,432,768]{2,1,0:T(8,128)(2,1)} %dynamic-slice_bitcast_fusion.2), channel_id=1, source_target_pairs={{0,8},{2,10},{4,12},{6,14},{8,0},{10,2},{12,4},{14,6},{16,24},{18,... | collective-permute-start | bytes 3981320 | tf_op jit(solution)/shard_map/ppermute | solution.py:976
  389.0 37.2 %collective-permute-start.8 = (bf16[2,2,2,192,768]{4,3,2,1,0:T(8,128)(2,1)}, bf16[2,2,2,192,768]{4,3,2,1,0:T(8,128)(2,1)}, u32[]{:S(2)}, u32[]{:S(2)}) collective-permute-start(bf16[2,2,2,192,768]{4,3,2,1,0:T(8,128)(2,1)} %bitcast.30), channel_id=1, source_target_pairs={{0,2},{2,0},{4,6},{6,4},{8,10},{10,8},{12,14},{14,12},{16,18},{18,... | collective-permute-start | bytes 7077896 | tf_op jit(solution)/shard_map/ppermute | solution.py:976
  389.0 31.9 %copy-start.12 = (f32[20,768]{1,0:T(8,128)}, f32[20,768]{1,0:T(8,128)S(1)}, u32[]{:S(2)}) copy-start(f32[20,768]{1,0:T(8,128)S(1)} %constant_dynamic-update-slice_fusion) | copy-start | bytes 184324
  389.0 31.9 %collective-permute-start.9 = (f32[20,768]{1,0:T(8,128)S(1)}, f32[20,768]{1,0:T(8,128)S(1)}, u32[]{:S(2)}, u32[]{:S(2)}) collective-permute-start(f32[20,768]{1,0:T(8,128)S(1)} %constant_dynamic-update-slice_fusion), channel_id=1, source_target_pairs={{0,2},{2,0},{4,6},{6,4},{8,10},{10,8},{12,14},{14,12},{16,18},{18,... | collective-permute-start | bytes 184328 | tf_op jit(solution)/shard_map/ppermute | solution.py:1008
  389.6 36.6 %collective-permute-start.10 = (bf16[2,512,768]{2,1,0:T(8,128)(2,1)}, bf16[2,512,768]{2,1,0:T(8,128)(2,1)S(1)}, u32[]{:S(2)}, u32[]{:S(2)}) collective-permute-start(bf16[2,512,768]{2,1,0:T(8,128)(2,1)} %get-tuple-element.207), channel_id=1, source_target_pairs={{0,1},{1,0},{2,3},{3,2},{4,5},{5,4},{6,7},{7,6},{8,9},{9,8},{10,11... | collective-permute-start | bytes 4718600 | tf_op jit(solution)/shard_map/ppermute | solution.py:1189
  420.9 11.2 %copy-start.7 = (bf16[8,192,768]{2,1,0:T(8,128)(2,1)S(1)}, bf16[8,192,768]{2,1,0:T(8,128)(2,1)}, u32[]{:S(2)}) copy-start(bf16[8,192,768]{2,1,0:T(8,128)(2,1)} %get-tuple-element.209) | copy-start | bytes 7077892
  420.9 6.4 %copy-start.15 = (f32[20,768]{1,0:T(8,128)}, f32[20,768]{1,0:T(8,128)S(1)}, u32[]{:S(2)}) copy-start(f32[20,768]{1,0:T(8,128)S(1)} %collective-permute-done.9) | copy-start | bytes 184324
  429.4 53.1 %collective-permute-start.11 = (bf16[432,768]{1,0:T(8,128)(2,1)S(1)}, bf16[432,768]{1,0:T(8,128)(2,1)}, u32[]{:S(2)}, u32[]{:S(2)}) collective-permute-start(bf16[432,768]{1,0:T(8,128)(2,1)S(1)} %dynamic-slice_bitcast_fusion.6), channel_id=1, source_target_pairs={{0,16},{2,18},{4,20},{6,22},{8,24},{10,26},{12,28},{14,30},{16,0},... | collective-permute-start | bytes 1990664 | tf_op jit(solution)/shard_map/ppermute | solution.py:976
  432.1 4.9 copy-start.13
  432.1 4.9 copy-start.16
  434.4 1.4 copy-start.4
  436.9 45.6 %collective-permute-start.12 = (bf16[2,2,192,768]{3,2,1,0:T(8,128)(2,1)}, bf16[2,2,192,768]{3,2,1,0:T(8,128)(2,1)}, u32[]{:S(2)}, u32[]{:S(2)}) collective-permute-start(bf16[2,2,192,768]{3,2,1,0:T(8,128)(2,1)} %dynamic-slice_bitcast_fusion.3), channel_id=1, source_target_pairs={{0,4},{2,6},{4,0},{6,2},{8,12},{10,14},{12,8},{14,10},{16,20},{18,... | collective-permute-start | bytes 3538952 | tf_op jit(solution)/shard_map/ppermute | solution.py:976
  437.6 44.9 %collective-permute-start.13 = (f32[20,768]{1,0:T(8,128)}, f32[20,768]{1,0:T(8,128)}, u32[]{:S(2)}, u32[]{:S(2)}) collective-permute-start(f32[20,768]{1,0:T(8,128)} %add.225), channel_id=1, source_target_pairs={{0,4},{2,6},{4,0},{6,2},{8,12},{10,14},{12,8},{14,10},{16,20},{18,... | collective-permute-start | bytes 184328 | tf_op jit(solution)/shard_map/ppermute | solution.py:1008
  451.4 31.1 %collective-permute-start.14 = (bf16[512,768]{1,0:T(8,128)(2,1)}, bf16[512,768]{1,0:T(8,128)(2,1)}, u32[]{:S(2)}, u32[]{:S(2)}) collective-permute-start(bf16[512,768]{1,0:T(8,128)(2,1)} %get-tuple-element.223), channel_id=1, source_target_pairs={{0,1},{1,0},{2,3},{3,2},{4,5},{5,4},{6,7},{7,6},{8,9},{9,8},{10,11... | collective-permute-start | bytes 2359304 | tf_op jit(solution)/shard_map/ppermute | solution.py:1216
  483.8 40.7 %collective-permute-start.15 = (bf16[432,768]{1,0:T(8,128)(2,1)S(1)}, bf16[432,768]{1,0:T(8,128)(2,1)}, u32[]{:S(2)}, u32[]{:S(2)}) collective-permute-start(bf16[432,768]{1,0:T(8,128)(2,1)S(1)} %fusion.8), channel_id=1, source_target_pairs={{0,1},{1,0},{2,3},{3,2},{4,5},{5,4},{6,7},{7,6},{8,9},{9,8},{10,11... | collective-permute-start | bytes 1990664 | tf_op jit(solution)/shard_map/ppermute | solution.py:978
  502.8 21.7 %collective-permute-start.18 = (bf16[2,2,2,48,1152]{4,3,2,1,0:T(8,128)(2,1)}, bf16[2,2,2,48,1152]{4,3,2,1,0:T(8,128)(2,1)}, u32[]{:S(2)}, u32[]{:S(2)}) collective-permute-start(bf16[2,2,2,48,1152]{4,3,2,1,0:T(8,128)(2,1)} %bitcast.197), channel_id=1, source_target_pairs={{0,2},{2,0},{4,6},{6,4},{8,10},{10,8},{12,14},{14,12},{16,18},{18,... | collective-permute-start | bytes 2654216 | tf_op jit(solution)/shard_map/ppermute | solution.py:976
  502.9 21.6 %collective-permute-start.19 = (bf16[2,2,2,48,1152]{4,3,2,1,0:T(8,128)(2,1)}, bf16[2,2,2,48,1152]{4,3,2,1,0:T(8,128)(2,1)}, u32[]{:S(2)}, u32[]{:S(2)}) collective-permute-start(bf16[2,2,2,48,1152]{4,3,2,1,0:T(8,128)(2,1)} %bitcast.196), channel_id=1, source_target_pairs={{0,2},{2,0},{4,6},{6,4},{8,10},{10,8},{12,14},{14,12},{16,18},{18,... | collective-permute-start | bytes 2654216 | tf_op jit(solution)/shard_map/ppermute | solution.py:976
  506.2 18.3 %collective-permute-start.16 = (bf16[2,192,768]{2,1,0:T(8,128)(2,1)}, bf16[2,192,768]{2,1,0:T(8,128)(2,1)}, u32[]{:S(2)}, u32[]{:S(2)}) collective-permute-start(bf16[2,192,768]{2,1,0:T(8,128)(2,1)} %dynamic-slice_bitcast_fusion.7), channel_id=1, source_target_pairs={{0,8},{2,10},{4,12},{6,14},{8,0},{10,2},{12,4},{14,6},{16,24},{18,... | collective-permute-start | bytes 1769480 | tf_op jit(solution)/shard_map/ppermute | solution.py:976
  507.6 16.9 %collective-permute-start.17 = (f32[20,768]{1,0:T(8,128)S(1)}, f32[20,768]{1,0:T(8,128)S(1)}, u32[]{:S(2)}, u32[]{:S(2)}) collective-permute-start(f32[20,768]{1,0:T(8,128)S(1)} %add.228), channel_id=1, source_target_pairs={{0,8},{2,10},{4,12},{6,14},{8,0},{10,2},{12,4},{14,6},{16,24},{18,... | collective-permute-start | bytes 184328 | tf_op jit(solution)/shard_map/ppermute | solution.py:1008
  511.6 12.1 %copy-start.18 = (f32[8,768]{1,0:T(8,128)S(1)}, f32[8,768]{1,0:T(8,128)}, u32[]{:S(2)}) copy-start(f32[8,768]{1,0:T(8,128)} %get-tuple-element.240) | copy-start | bytes 73732
  523.7 3.9 copy-start.10
  524.5 4.5 copy-start.14
  527.4 6.2 %copy-start.9 = (bf16[2,512,768]{2,1,0:T(8,128)(2,1)S(1)}, bf16[2,512,768]{2,1,0:T(8,128)(2,1)}, u32[]{:S(2)}) copy-start(bf16[2,512,768]{2,1,0:T(8,128)(2,1)} %copy-done.8) | copy-start | bytes 4718596
  527.5 19.2 %collective-permute-start.22 = (bf16[2,2,48,1152]{3,2,1,0:T(8,128)(2,1)S(1)}, bf16[2,2,48,1152]{3,2,1,0:T(8,128)(2,1)S(1)}, u32[]{:S(2)}, u32[]{:S(2)}) collective-permute-start(bf16[2,2,48,1152]{3,2,1,0:T(8,128)(2,1)S(1)} %dynamic-slice_bitcast_fusion.9), channel_id=1, source_target_pairs={{0,4},{2,6},{4,0},{6,2},{8,12},{10,14},{12,8},{14,10},{16,20},{18,... | collective-permute-start | bytes 1327112 | tf_op jit(solution)/shard_map/ppermute | solution.py:976
  529.0 6.5 %copy-start.33 = (bf16[512,768]{1,0:T(8,128)(2,1)S(1)}, bf16[512,768]{1,0:T(8,128)(2,1)}, u32[]{:S(2)}) copy-start(bf16[512,768]{1,0:T(8,128)(2,1)} %get-tuple-element.254) | copy-start | bytes 2359300
  529.1 19.6 %collective-permute-start.23 = (bf16[2,2,48,1152]{3,2,1,0:T(8,128)(2,1)S(1)}, bf16[2,2,48,1152]{3,2,1,0:T(8,128)(2,1)S(1)}, u32[]{:S(2)}, u32[]{:S(2)}) collective-permute-start(bf16[2,2,48,1152]{3,2,1,0:T(8,128)(2,1)S(1)} %dynamic-slice_bitcast_fusion.8), channel_id=1, source_target_pairs={{0,8},{2,10},{4,12},{6,14},{8,0},{10,2},{12,4},{14,6},{16,24},{18,... | collective-permute-start | bytes 1327112 | tf_op jit(solution)/shard_map/ppermute | solution.py:976
  529.6 17.0 %collective-permute-start.20 = (bf16[192,768]{1,0:T(8,128)(2,1)S(1)}, bf16[192,768]{1,0:T(8,128)(2,1)S(1)}, u32[]{:S(2)}, u32[]{:S(2)}) collective-permute-start(bf16[192,768]{1,0:T(8,128)(2,1)S(1)} %dynamic-slice_bitcast_fusion.10), channel_id=1, source_target_pairs={{0,16},{2,18},{4,20},{6,22},{8,24},{10,26},{12,28},{14,30},{16,0},... | collective-permute-start | bytes 884744 | tf_op jit(solution)/shard_map/ppermute | solution.py:976
  531.2 15.5 %collective-permute-start.21 = (f32[20,768]{1,0:T(8,128)S(1)}, f32[20,768]{1,0:T(8,128)S(1)}, u32[]{:S(2)}, u32[]{:S(2)}) collective-permute-start(f32[20,768]{1,0:T(8,128)S(1)} %add.231), channel_id=1, source_target_pairs={{0,16},{2,18},{4,20},{6,22},{8,24},{10,26},{12,28},{14,30},{16,0},... | collective-permute-start | bytes 184328 | tf_op jit(solution)/shard_map/ppermute | solution.py:1008
  533.6 1.9 collective-permute-start.24
  535.5 27.9 %collective-permute-start.30 = (bf16[512,768]{1,0:T(8,128)(2,1)S(1)}, bf16[512,768]{1,0:T(8,128)(2,1)S(1)}, u32[]{:S(2)}, u32[]{:S(2)}) collective-permute-start(bf16[512,768]{1,0:T(8,128)(2,1)S(1)} %copy-done.33), channel_id=1, source_target_pairs={{0,1},{1,0},{2,3},{3,2},{4,5},{5,4},{6,7},{7,6},{8,9},{9,8},{10,11... | collective-permute-start | bytes 2359304 | tf_op jit(solution)/shard_map/ppermute | solution.py:1230
  548.8 14.6 %collective-permute-start.25 = (bf16[192,768]{1,0:T(8,128)(2,1)S(1)}, bf16[192,768]{1,0:T(8,128)(2,1)S(1)}, u32[]{:S(2)}, u32[]{:S(2)}) collective-permute-start(bf16[192,768]{1,0:T(8,128)(2,1)S(1)} %fusion.12), channel_id=1, source_target_pairs={{0,1},{1,0},{2,3},{3,2},{4,5},{5,4},{6,7},{7,6},{8,9},{9,8},{10,11... | collective-permute-start | bytes 884744 | tf_op jit(solution)/shard_map/ppermute | solution.py:978
  549.5 13.8 %collective-permute-start.26 = (f32[20,768]{1,0:T(8,128)S(1)}, f32[20,768]{1,0:T(8,128)S(1)}, u32[]{:S(2)}, u32[]{:S(2)}) collective-permute-start(f32[20,768]{1,0:T(8,128)S(1)} %add.235), channel_id=1, source_target_pairs={{0,1},{1,0},{2,3},{3,2},{4,5},{5,4},{6,7},{7,6},{8,9},{9,8},{10,11... | collective-permute-start | bytes 184328 | tf_op jit(solution)/shard_map/ppermute | solution.py:1010
  551.1 12.3 %collective-permute-start.27 = (bf16[2,48,1152]{2,1,0:T(8,128)(2,1)S(1)}, bf16[2,48,1152]{2,1,0:T(8,128)(2,1)S(1)}, u32[]{:S(2)}, u32[]{:S(2)}) collective-permute-start(bf16[2,48,1152]{2,1,0:T(8,128)(2,1)S(1)} %dynamic-slice_bitcast_fusion.12), channel_id=1, source_target_pairs={{0,8},{2,10},{4,12},{6,14},{8,0},{10,2},{12,4},{14,6},{16,24},{18,... | collective-permute-start | bytes 663560 | tf_op jit(solution)/shard_map/ppermute | solution.py:976
  551.7 4.1 collective-permute-start.29
  555.8 7.5 %collective-permute-start.28 = (bf16[2,48,1152]{2,1,0:T(8,128)(2,1)S(1)}, bf16[2,48,1152]{2,1,0:T(8,128)(2,1)S(1)}, u32[]{:S(2)}, u32[]{:S(2)}) collective-permute-start(bf16[2,48,1152]{2,1,0:T(8,128)(2,1)S(1)} %dynamic-slice_bitcast_fusion.11), channel_id=1, source_target_pairs={{0,4},{2,6},{4,0},{6,2},{8,12},{10,14},{12,8},{14,10},{16,20},{18,... | collective-permute-start | bytes 663560 | tf_op jit(solution)/shard_map/ppermute | solution.py:976
  563.5 11.5 %collective-permute-start.31 = (bf16[48,1152]{1,0:T(8,128)(2,1)S(1)}, bf16[48,1152]{1,0:T(8,128)(2,1)S(1)}, u32[]{:S(2)}, u32[]{:S(2)}) collective-permute-start(bf16[48,1152]{1,0:T(8,128)(2,1)S(1)} %dynamic-slice_bitcast_fusion.14), channel_id=1, source_target_pairs={{0,16},{2,18},{4,20},{6,22},{8,24},{10,26},{12,28},{14,30},{16,0},... | collective-permute-start | bytes 331784 | tf_op jit(solution)/shard_map/ppermute | solution.py:976
  564.2 12.1 %collective-permute-start.32 = (bf16[48,1152]{1,0:T(8,128)(2,1)S(1)}, bf16[48,1152]{1,0:T(8,128)(2,1)S(1)}, u32[]{:S(2)}, u32[]{:S(2)}) collective-permute-start(bf16[48,1152]{1,0:T(8,128)(2,1)S(1)} %dynamic-slice_bitcast_fusion.13), channel_id=1, source_target_pairs={{0,16},{2,18},{4,20},{6,22},{8,24},{10,26},{12,28},{14,30},{16,0},... | collective-permute-start | bytes 331784 | tf_op jit(solution)/shard_map/ppermute | solution.py:976
  566.6 7.7 %collective-permute-start.33 = (f32[8,768]{1,0:T(8,128)S(1)}, f32[8,768]{1,0:T(8,128)S(1)}, u32[]{:S(2)}, u32[]{:S(2)}) collective-permute-start(f32[8,768]{1,0:T(8,128)S(1)} %add.239), channel_id=1, source_target_pairs={{0,8},{2,10},{4,12},{6,14},{8,0},{10,2},{12,4},{14,6},{16,24},{18,... | collective-permute-start | bytes 73736 | tf_op jit(solution)/shard_map/ppermute | solution.py:1008
  569.1 19.2 %copy-start.1 = (s32[4,1]{0,1:T(1,128)S(1)}, s32[4,1]{0,1:T(1,128)}, u32[]{:S(2)}) copy-start(s32[4,1]{0,1:T(1,128)} %param.28) | copy-start | bytes 52
  576.3 6.9 %collective-permute-start.34 = (bf16[48,1152]{1,0:T(8,128)(2,1)S(1)}, bf16[48,1152]{1,0:T(8,128)(2,1)S(1)}, u32[]{:S(2)}, u32[]{:S(2)}) collective-permute-start(bf16[48,1152]{1,0:T(8,128)(2,1)S(1)} %fusion.16), channel_id=1, source_target_pairs={{0,1},{1,0},{2,3},{3,2},{4,5},{5,4},{6,7},{7,6},{8,9},{9,8},{10,11... | collective-permute-start | bytes 331784 | tf_op jit(solution)/shard_map/ppermute | solution.py:978
  577.3 6.0 %collective-permute-start.35 = (bf16[48,1152]{1,0:T(8,128)(2,1)S(1)}, bf16[48,1152]{1,0:T(8,128)(2,1)S(1)}, u32[]{:S(2)}, u32[]{:S(2)}) collective-permute-start(bf16[48,1152]{1,0:T(8,128)(2,1)S(1)} %fusion.15), channel_id=1, source_target_pairs={{0,1},{1,0},{2,3},{3,2},{4,5},{5,4},{6,7},{7,6},{8,9},{9,8},{10,11... | collective-permute-start | bytes 331784 | tf_op jit(solution)/shard_map/ppermute | solution.py:978
  578.5 4.7 collective-permute-start.36
  583.2 3.9 collective-permute-start.37
  (8 other events, 6.8 us)

commit v5 on v4

--- a/solution.py
+++ b/solution.py
@@ -263,56 +263,32 @@
 
 
 def attend_kernel(info_ref, q_ref, k_ref, v_ref, *refs, use_mask, start):
-    o_ref, e_ref, r_ref = refs[-3:]
+    o_ref, e_ref, r_ref, mask_ref = refs[-4:]
     length = k_ref.shape[1]
     half = length // 2
     values_turned = v_ref[0].T
     ones = jnp.ones((16, length), jnp.bfloat16)
-    side = info_ref[0]
-
-    def run(masked, shifted, side_now=None):
+
+    def run(masked, shifted):
         lowest, highest = None, None
-        below = (
-            lax.broadcasted_iota(jnp.int32, (half, 1), 0)
-            <= lax.broadcasted_iota(jnp.int32, (1, half), 1)
-            if masked
-            else None
-        )
         for at in range(2):
             queries_at = slice(at * half, (at + 1) * half)
-            if masked:
-                seen = [at] if at == side_now else [0, 1]
-            else:
-                seen = [None]
             mixed = []
             for head, queries in enumerate(head_masks(q_ref[0, queries_at, :])):
-                tiles = []
-                for key_at in seen:
-                    rows = slice(0, length)
-                    if key_at is not None:
-                        rows = slice(key_at * half, (key_at + 1) * half)
-                    scores = contract(k_ref[0, rows, :], queries, 1, 1)
-                    if key_at == at:
-                        scores = jnp.where(below, scores, blocked_score)
-                    tiles.append((rows, scores))
+                scores = contract(k_ref[0], queries, 1, 1)
                 if shifted:
-                    highest_score = functools.reduce(
-                        jnp.maximum,
-                        [jnp.max(scores, axis=0, keepdims=True) for _, scores in tiles],
-                    )
-                    tiles = [(rows, scores - highest_score) for rows, scores in tiles]
-                sums = None
-                for rows, scores in tiles:
-                    low = jnp.exp(scores).astype(jnp.bfloat16)
-                    e_ref[0, head, rows, queries_at] = low
-                    turned = jnp.concatenate(
-                        [values_turned[head * HEAD : (head + 1) * HEAD, rows], ones[:, rows]], axis=0
-                    )
-                    part = contract(turned, low, 1, 0)
-                    sums = part if sums is None else sums + part
-                if masked and len(seen) == 1:
-                    other = slice((1 - at) * half, (2 - at) * half)
-                    e_ref[0, head, other, queries_at] = jnp.zeros((half, half), jnp.bfloat16)
+                    if masked:
+                        seen = mask_ref[:, queries_at].astype(jnp.float32) > 0
+                        scores = jnp.where(seen, scores, blocked_score)
+                    scores = scores - jnp.max(scores, axis=0, keepdims=True)
+                low = jnp.exp(scores).astype(jnp.bfloat16)
+                if masked:
+                    low = low * mask_ref[:, queries_at]
+                e_ref[0, head, :, queries_at] = low
+                turned = jnp.concatenate(
+                    [values_turned[head * HEAD : (head + 1) * HEAD], ones], axis=0
+                )
+                sums = contract(turned, low, 1, 0)
                 total = sums[HEAD : HEAD + 1]
                 if not shifted:
                     lowest = total if lowest is None else jnp.minimum(lowest, total)
@@ -326,17 +302,29 @@
 
             @pl.when(jnp.logical_not(in_range))
             def _():
-                run(masked, True, side_now)
+                run(masked, True)
 
     if not use_mask:
         run(False, False)
         return
     causal = info_ref[2 + start + pl.program_id(0)] == 0
-    for side_now in range(2):
-
-        @pl.when(causal & (side == side_now))
-        def _():
-            run(True, False, side_now)
+
+    @pl.when(causal & (pl.program_id(1) == 0))
+    def _():
+        later = info_ref[0] * half
+        query = lax.broadcasted_iota(jnp.int32, (1, length), 1)
+        query = jnp.where(query < half, query + later, query - later)
+
+        @pl.loop(0, length, step=64)
+        def _(row):
+            key = lax.broadcasted_iota(jnp.int32, (64, 1), 0) + row
+            key = jnp.where(key < half, key + later, key - later)
+            seen = jnp.where(key <= query, 1.0, 0.0)
+            mask_ref[pl.ds(pl.multiple_of(row, 64), 64), :] = seen.astype(jnp.bfloat16)
+
+    @pl.when(causal)
+    def _():
+        run(True, False)
 
     @pl.when(jnp.logical_not(causal))
     def _():
@@ -364,6 +352,7 @@
                 pl.BlockSpec((1, 2, length, length), place),
                 pl.BlockSpec((1, 1, 2, length), place),
             ],
+            scratch_shapes=[pltpu.VMEM((length, length), jnp.bfloat16)],
         ),
         out_shape=[
             jax.ShapeDtypeStruct((count, length, width), jnp.bfloat16),
@@ -537,14 +526,44 @@
     )(info, *arrays)
 
 
+GROUP = 32
+
+
+def sweep(rows, width, sums, body):
+    def step(index, totals):
+        parts = body(pl.ds(pl.multiple_of(index * GROUP, GROUP), GROUP))
+        return tuple(
+            total + jnp.sum(part.reshape(GROUP // 8, 8, width), axis=0)
+            for total, part in zip(totals, parts or ())
+        )
+
+    zeros = tuple(jnp.zeros((8, width), jnp.float32) for _ in range(sums))
+    totals = lax.fori_loop(0, rows // GROUP, step, zeros)
+    return [column_sum(total) for total in totals]
+
+
+def add_sums(ref, sums):
+    for at, row in enumerate(sums):
+        ref[at : at + 1, :] += row
+
+
 def enter_kernel(info_ref, own_ref, got_ref, w_ref, vec_ref, bias_ref, *refs, norm):
-    x_ref, out_ref = refs[-2:]
-    x = pick(pl.program_id(0) % 2 == 0, own_ref, got_ref)
-    x_ref[...] = x
+    x_ref, out_ref, normal_ref = refs[-3:]
+    first = pl.program_id(0) % 2 == 0
+    rows, width = x_ref.shape
+
+    def normalise(place):
+        x = jnp.where(first, own_ref[place, :], got_ref[place, :])
+        x_ref[place, :] = x
+        unit, _ = normal_parts(x.astype(jnp.float32))
+        normal_ref[place, :] = (unit * vec_ref[0:1, :] + vec_ref[1:2, :]).astype(jnp.bfloat16)
+
     if norm:
-        unit, _ = normal_parts(x.astype(jnp.float32))
-        x = (unit * vec_ref[0:1, :] + vec_ref[1:2, :]).astype(jnp.bfloat16)
-    width = x.shape[1]
+        sweep(rows, width, 0, normalise)
+        x = normal_ref[...]
+    else:
+        x = pick(first, own_ref, got_ref)
+        x_ref[...] = x
     for start in range(0, w_ref.shape[1], width):
         part = slice(start, start + width)
         total = contract(x, w_ref[:, part], 1, 0) + bias_ref[:, part]
@@ -574,19 +593,23 @@
         2 * count,
         4 * count * own * width * wide,
         4 * count * own * (2 * width + wide),
+        scratch=[pltpu.VMEM((own, width), jnp.bfloat16)],
         input_output_aliases={6: 0, 7: 1} if previous else {},
     )
 
 
-def middle_kernel(info_ref, x_ref, mixed_ref, wo_ref, wq_ref, vec_ref, after_ref, q_ref):
+def middle_kernel(info_ref, x_ref, mixed_ref, wo_ref, wq_ref, vec_ref, after_ref, q_ref, normal_ref):
     out_bias, gain, shift, query_bias = (vec_ref[i : i + 1, :] for i in range(4))
-    after = (
-        x_ref[...].astype(jnp.float32) + contract(mixed_ref[...], wo_ref[...], 1, 0) + out_bias
-    )
-    after_ref[...] = after
-    unit, _ = normal_parts(after)
-    normal = (unit * gain + shift).astype(jnp.bfloat16)
-    queries = (contract(normal, wq_ref[...], 1, 0) + query_bias) * (HEAD**-0.5)
+    after_ref[...] = contract(mixed_ref[...], wo_ref[...], 1, 0)
+
+    def normalise(place):
+        after = after_ref[place, :] + x_ref[place, :].astype(jnp.float32) + out_bias
+        after_ref[place, :] = after
+        unit, _ = normal_parts(after)
+        normal_ref[place, :] = (unit * gain + shift).astype(jnp.bfloat16)
+
+    sweep(*x_ref.shape, 0, normalise)
+    queries = (contract(normal_ref[...], wq_ref[...], 1, 0) + query_bias) * (HEAD**-0.5)
     q_ref[...] = queries.astype(jnp.bfloat16)
 
 
@@ -605,6 +628,7 @@
         rows // own,
         4 * rows * width * width,
         10 * rows * width,
+        scratch=[pltpu.VMEM((own, width), jnp.bfloat16)],
     )
 
 
@@ -672,7 +696,7 @@
 def feed_kernel(
     info_ref, x_ref, mixed_ref, dyo_ref, dyg_ref, wc_ref, wi_ref, wo_ref, vec_ref, bi_ref,
     own_ref, got_ref, dx_ref, do_ref, vsum_ref, bsum_ref, kept_ref, sent_ref, ai_ref, ao_ref,
-    ac_ref, *, steps, chunk, parts,
+    ac_ref, normal_ref, x2_ref, up_ref, *, steps, chunk, parts,
 ):
     step = pl.program_id(0)
 
@@ -685,9 +709,17 @@
     def _():
         cross_bias, gain, shift, out_bias = (vec_ref[i : i + 1, :] for i in range(4))
         mixed = mixed_ref[...]
-        x2 = x_ref[...] + contract(mixed, wc_ref[...], 1, 0) + cross_bias
-        unit, inverse = normal_parts(x2)
-        normal = (unit * gain + shift).astype(jnp.bfloat16)
+        rows, width = x_ref.shape
+        up_ref[...] = contract(mixed, wc_ref[...], 1, 0)
+
+        def normalise(place):
+            x2 = up_ref[place, :] + x_ref[place, :] + cross_bias
+            x2_ref[place, :] = x2
+            unit, _ = normal_parts(x2)
+            normal_ref[place, :] = (unit * gain + shift).astype(jnp.bfloat16)
+
+        sweep(rows, width, 0, normalise)
+        normal = normal_ref[...]
         normal_turned = normal.T
         dy = pick(step % 2 == 0, dyo_ref, dyg_ref)
         dy_turned = dy.T
@@ -706,17 +738,23 @@
             upstream = up if upstream is None else upstream + up
             ao_ref[:, part] += contract(dy_turned, active, 1, 0)
             ai_ref[:, part] += contract(normal_turned, low, 1, 0)
-        put_rows(step, x2 + result + out_bias, own_ref, got_ref)
-        wide = dy.astype(jnp.float32)
-        dx = wide + normal_back(unit, inverse, gain, upstream)
-        dx_ref[...] = dx
-        dx_low = dx.astype(jnp.bfloat16)
+        put_rows(step, x2_ref[...] + result + out_bias, own_ref, got_ref)
+        up_ref[...] = upstream
+
+        def back(place):
+            unit, inverse = normal_parts(x2_ref[place, :])
+            upstream = up_ref[place, :]
+            wide = jnp.where(step % 2 == 0, dyo_ref[place, :], dyg_ref[place, :])
+            wide = wide.astype(jnp.float32)
+            dx = wide + normal_back(unit, inverse, gain, upstream)
+            dx_ref[place, :] = dx
+            normal_ref[place, :] = dx.astype(jnp.bfloat16)
+            return dx, upstream * unit, upstream, wide
+
+        add_sums(vsum_ref, sweep(rows, width, 4, back))
+        dx_low = normal_ref[...]
         do_ref[...] = contract(dx_low, wc_ref[...], 1, 1).astype(jnp.bfloat16)
         ac_ref[...] += contract(mixed.T, dx_low, 1, 0)
-        vsum_ref[0:1, :] += column_sum(dx)
-        vsum_ref[1:2, :] += column_sum(upstream * unit)
-        vsum_ref[2:3, :] += column_sum(upstream)
-        vsum_ref[3:4, :] += column_sum(wide)
 
     @pl.when(step >= steps)
     def _():
@@ -767,15 +805,17 @@
             pltpu.VMEM((width, inner), jnp.float32),
             pltpu.VMEM((width, inner), jnp.float32),
             pltpu.VMEM((width, width), jnp.float32),
+            pltpu.VMEM((own, width), jnp.bfloat16),
+            pltpu.VMEM((own, width), jnp.float32),
+            pltpu.VMEM((own, width), jnp.float32),
         ],
-        limit=LIMIT,
     )
 
 
 def return_kernel(
     info_ref, dq_ref, dk_ref, dv_ref, x_ref, dx_ref, mixed_ref, src_ref, wq_ref, wi_ref, wo_ref,
     vec_ref, own_ref, got_ref, dxo_ref, do_ref, vsum_ref, kept_ref, sent_ref, aq_ref, ao_ref,
-    ai_ref, *, steps, parts,
+    ai_ref, normal_ref, low_ref, up_ref, *, steps, parts,
 ):
     step = pl.program_id(0)
 
@@ -786,28 +826,33 @@
 
     @pl.when(step < steps)
     def _():
-        width = x_ref.shape[1]
+        rows, width = x_ref.shape
         gain, shift = vec_ref[0:1, :], vec_ref[1:2, :]
-        dq, dk, dv = dq_ref[...], dk_ref[...], dv_ref[...]
-        upstream = contract(dq, wq_ref[...], 1, 1)
-        unit, inverse = normal_parts(x_ref[...])
-        normal = (unit * gain + shift).astype(jnp.bfloat16)
-        dx = dx_ref[...] + normal_back(unit, inverse, gain, upstream)
-        dxo_ref[...] = dx
-        low = dx.astype(jnp.bfloat16)
-        do_ref[...] = contract(low, wo_ref[...], 1, 1).astype(jnp.bfloat16)
+        up_ref[...] = contract(dq_ref[...], wq_ref[...], 1, 1)
+
+        def back(place):
+            unit, inverse = normal_parts(x_ref[place, :])
+            upstream = up_ref[place, :]
+            normal_ref[place, :] = (unit * gain + shift).astype(jnp.bfloat16)
+            dx = dx_ref[place, :] + normal_back(unit, inverse, gain, upstream)
+            dxo_ref[place, :] = dx
+            low_ref[place, :] = dx.astype(jnp.bfloat16)
+            dq, dv = dq_ref[place, :], dv_ref[place, :]
+            return (
+                upstream * unit, upstream, dx, dq.astype(jnp.float32), dv.astype(jnp.float32)
+            )
+
+        add_sums(vsum_ref, sweep(rows, width, 5, back))
+        dk, dv = dk_ref[...], dv_ref[...]
         source = contract(dk, wi_ref[:, :width], 1, 1) + contract(dv, wi_ref[:, width:], 1, 1)
         put_rows(step, source, own_ref, got_ref)
-        aq_ref[...] += contract(normal.T, dq, 1, 0)
-        ao_ref[...] += contract(mixed_ref[...].T, low, 1, 0)
         turned = src_ref[...].T
         ai_ref[:, :width] += contract(turned, dk, 1, 0)
         ai_ref[:, width:] += contract(turned, dv, 1, 0)
-        vsum_ref[0:1, :] += column_sum(upstream * unit)
-        vsum_ref[1:2, :] += column_sum(upstream)
-        vsum_ref[2:3, :] += column_sum(dx)
-        vsum_ref[3:4, :] += column_sum(dq.astype(jnp.float32))
-        vsum_ref[4:5, :] += column_sum(dv.astype(jnp.float32))
+        low = low_ref[...]
+        do_ref[...] = contract(low, wo_ref[...], 1, 1).astype(jnp.bfloat16)
+        aq_ref[...] += contract(normal_ref[...].T, dq_ref[...], 1, 0)
+        ao_ref[...] += contract(mixed_ref[...].T, low, 1, 0)
 
     @pl.when(step >= steps)
     def _():
@@ -850,13 +895,16 @@
             pltpu.VMEM((width, width), jnp.float32),
             pltpu.VMEM((width, width), jnp.float32),
             pltpu.VMEM((width, 2 * width), jnp.float32),
+            pltpu.VMEM((own, width), jnp.bfloat16),
+            pltpu.VMEM((own, width), jnp.bfloat16),
+            pltpu.VMEM((own, width), jnp.float32),
         ],
     )
 
 
 def last_weight_kernel(
     info_ref, dq_ref, dk_ref, dv_ref, x_ref, vec_ref, ka_ref, sa_ref, kb_ref, sb_ref, acc_ref,
-    *, steps,
+    normal_ref, *, steps,
 ):
     step = pl.program_id(0)
 
@@ -866,9 +914,15 @@
 
     @pl.when(step < steps)
     def _():
-        unit, _ = normal_parts(x_ref[...].astype(jnp.float32))
-        turned = (unit * vec_ref[0:1, :] + vec_ref[1:2, :]).astype(jnp.bfloat16).T
-        width = x_ref.shape[1]
+        rows, width = x_ref.shape
+
+        def normalise(place):
+            unit, _ = normal_parts(x_ref[place, :].astype(jnp.float32))
+            normal = unit * vec_ref[0:1, :] + vec_ref[1:2, :]
+            normal_ref[place, :] = normal.astype(jnp.bfloat16)
+
+        sweep(rows, width, 0, normalise)
+        turned = normal_ref[...].T
         for at, ref in enumerate((dq_ref, dk_ref, dv_ref)):
             acc_ref[:, at * width : (at + 1) * width] += contract(turned, ref[...], 1, 0)
 
@@ -899,34 +953,48 @@
         steps + parts // 2,
         6 * rows * width * width,
         20 * 2**20,
-        scratch=[pltpu.VMEM((width, 3 * width), jnp.float32)],
+        scratch=[
+            pltpu.VMEM((width, 3 * width), jnp.float32),
+            pltpu.VMEM((own, width), jnp.bfloat16),
+        ],
     )
 
 
 def leave_kernel(
     info_ref, dq_ref, dk_ref, dv_ref, x_ref, dx_ref, w_ref, vec_ref, *refs
 ):
-    own_ref, got_ref, vsum_ref = refs[-3:]
+    own_ref, got_ref, vsum_ref, up_ref = refs[-4:]
     step = pl.program_id(0)
 
     @pl.when(step == 0)
     def _():
         vsum_ref[...] = jnp.zeros_like(vsum_ref)
 
-    width = x_ref.shape[1]
-    dq, dk, dv = dq_ref[...], dk_ref[...], dv_ref[...]
-    upstream = (
-        contract(dq, w_ref[:, :width], 1, 1)
-        + contract(dk, w_ref[:, width : 2 * width], 1, 1)
-        + contract(dv, w_ref[:, 2 * width :], 1, 1)
-    )
-    unit, inverse = normal_parts(x_ref[...].astype(jnp.float32))
-    dx = dx_ref[...] + normal_back(unit, inverse, vec_ref[0:1, :], upstream)
-    put_rows(step, dx, own_ref, got_ref)
-    vsum_ref[0:1, :] += column_sum(upstream * unit)
-    vsum_ref[1:2, :] += column_sum(upstream)
-    vsum_ref[2:3, :] += column_sum(dq.astype(jnp.float32))
-    vsum_ref[3:4, :] += column_sum(dv.astype(jnp.float32))
+    rows, width = x_ref.shape
+    up_ref[...] = (
+        contract(dq_ref[...], w_ref[:, :width], 1, 1)
+        + contract(dk_ref[...], w_ref[:, width : 2 * width], 1, 1)
+        + contract(dv_ref[...], w_ref[:, 2 * width :], 1, 1)
+    )
+
+    def finish_rows(out_ref):
+        def back(place):
+            unit, inverse = normal_parts(x_ref[place, :].astype(jnp.float32))
+            upstream = up_ref[place, :]
+            dx = dx_ref[place, :] + normal_back(unit, inverse, vec_ref[0:1, :], upstream)
+            out_ref[place, :] = dx.astype(out_ref.dtype)
+            dq, dv = dq_ref[place, :], dv_ref[place, :]
+            return upstream * unit, upstream, dq.astype(jnp.float32), dv.astype(jnp.float32)
+
+        add_sums(vsum_ref, sweep(rows, width, 4, back))
+
+    @pl.when(step == 0)
+    def _():
+        finish_rows(own_ref)
+
+    @pl.when(step != 0)
+    def _():
+        finish_rows(got_ref)
 
 
 def leave(info, at, previous, grads, x, dx1, weight, vectors, own, micros):
@@ -952,6 +1020,7 @@
         2,
         12 * own * width * width,
         16 * 2**20,
+        scratch=[pltpu.VMEM((own, width), jnp.float32)],
         **more,
     )
 
@@ -1075,9 +1144,10 @@
     length = 2 * own
     pairs = HEADS * HEAD // 128
 
-    def swap(rows, at, count):
+    def swap(rows, at, count, after=()):
         sent = lax.dynamic_slice_in_dim(rows, (1 - side) * held + at, count, axis=0)
-        return lax.ppermute(sent, "seq", SWAP)
+        sent, after = lax.optimization_barrier((sent, after))
+        return lax.ppermute(sent, "seq", SWAP), after
 
     def give(owns, got, at):
         got = got.astype(owns.dtype)
@@ -1094,12 +1164,18 @@
         return rows.reshape(held * length, -1)
 
     targets, memory = targets[:, 0], memory[:, 0]
-    target_gots = [swap(targets, at, 1) for at in range(held)]
-    memory_gots = swap(memory, 0, held)
     upstreams = (
         cotangent[:, 0].astype(jnp.float32) * loss_mask[:, 0].astype(jnp.float32)[..., None]
     ).astype(jnp.bfloat16)
-    upstream_gots = swap(upstreams, 0, held)
+    target_gots, last_got = [], ()
+    for at in range(held):
+        got, last_got = swap(targets, at, 1, last_got)
+        target_gots.append(got)
+        if at:
+            target_gots[at - 1] = last_got
+        last_got = got
+    memory_gots, target_gots[-1] = swap(memory, 0, held, last_got)
+    upstream_gots, memory_gots = swap(upstreams, 0, held, memory_gots)
     kinds = lax.dynamic_slice_in_dim(row_kind[:, 0], side * held, held, axis=0)
     info = jnp.concatenate([jnp.stack([side, place % 2]).astype(jnp.int32), kinds])
 

time: 598 us -> 673 us (1.13)
  Pallas kernels: 422 us -> 516 us
  waiting for transfers between devices: 58.5 us -> 42.7 us
    pallas_call x9, Pallas kernels: 232 us -> 325 us  [kernel_call(): pl.pallas_call(kernel, grid_spec=pltpu.PrefetchScalarGridSpec(num_scalar_...]
    ppermute x4, waiting for transfers between devices: 25.1 us -> 7.54 us  [swap(): return (lax.ppermute(sent, 'seq', SWAP), after)]
  transfers between devices with their start and end apart: 38 -> 38, of which waited for: 11 -> 11; matrix products, arithmetic and copies ran while one was open for 6% -> 6% of each run, Pallas kernels for 53% -> 57%
where the time goes in v5:
time: 673 us; the launch traced here: 669 us
  Pallas kernels  516 us (77%)
  waiting for transfers between devices  42.7 us (6%)
  starting transfers between devices  39.1 us (6%)
  other arithmetic  36.6 us (5%)
  local copies, waits for them, and re-layouts  32.6 us (5%)
    pallas_call x9, Pallas kernels, kernel_call(): pl.pallas_call(kernel, grid_spec=pltpu.PrefetchScalarGridSpec(num_scalar_...  325 us
    pallas_call x4, Pallas kernels, attend_back(): pl.pallas_call(kernel, grid=size, in_specs=[pl.BlockSpec(memory_space=pl....  123 us
    pallas_call x3, Pallas kernels, attend(): pl.pallas_call(functools.partial(attend_kernel, use_mask=use_mask, start=...  68.2 us
    convert_element_type x16, other arithmetic, add(): total = total.astype(jnp.bfloat16)  20.7 us
    ppermute x8, waiting for transfers between devices, exchange(): self.got = lax.ppermute(self.rows, 'dp', pairs)  16.1 us
    ppermute x16, starting transfers between devices, exchange(): self.got = lax.ppermute(self.sent, 'dp', pairs)  14.1 us
  transfers between devices with their start and end apart: 38, of which 11 were waited for; matrix products, arithmetic and copies ran while one was open for 6% of the time, Pallas kernels for 57%

profile of v5, /device:TPU:0, one launch (start us, length us, event | category | flops | bytes accessed | tf_op | source)
XLA Modules:
  0.0 668.8 jit_solution(11676055826430566519)
XLA Ops:
  0.8 2.8 dynamic-slice_bitcast_fusion.4
  3.6 3.0 collective-permute-start
  6.6 2.7 dynamic-slice_bitcast_fusion.1
  13.3 1.7 copy-done.5
  15.0 1.2 constant_dynamic-slice_fusion.13
  16.9 7.5 %collective-permute-done.got_ref = bf16[1,512,768]{2,1,0:T(8,128)(2,1)} collective-permute-done((bf16[1,512,768]{2,1,0:T(8,128)(2,1)}, bf16[1,512,768]{2,1,0:T(8,128)(2,1)}, u32[]{:S(2)}, u32[]{:S(2)}) %collective-permute-start) | collective-permute-done | bytes 786464 | tf_op jit(solution)/shard_map/ppermute | solution.py:1150
  24.4 1.7 collective-permute-start.1
  26.2 14.7 %enter.3 = (bf16[2048,768]{1,0:T(8,128)(2,1)}, bf16[2048,2304]{1,0:T(8,128)(2,1)}) custom-call(s32[4]{0:T(128)} %pad_add_fusion.info_ref, bf16[4,512,768]{2,1,0:T(8,128)(2,1)} %bitcast.181, bf16[1,512,768]{2,1,0:T(8,128)(2,1)} %collective-permute-done.got_ref, bf16[768,2304]{1,0:T(8,128)(2,1)} %w_ref.9, f32[8,768]{1,0:T(8,128)} %get-tuple-element.331.vec_ref, ...), custom_call_target="tpu_custom_call" | custom-call | flops 3623878656 | bytes 7864320 | tf_op jit(solution)/shard_map/enter/pallas_call | solution.py:510
  40.9 18.4 %attend.3 = (bf16[2,1024,768]{2,1,0:T(8,128)(2,1)}, bf16[2,12,1024,1024]{3,2,1,0:T(8,128)(2,1)}, f32[2,6,2,1024]{3,2,1,0:T(2,128)}) custom-call(s32[4]{0:T(128)} %pad_add_fusion.info_ref, bf16[2,1024,2304]{2,1,0:T(8,128)(2,1)} %bitcast.160, bf16[2,1024,2304]{2,1,0:T(8,128)(2,1)} %bitcast.161, bf16[2,1024,2304]{2,1,0:T(8,128)(2,1)} %bitcast.162), custom_call_target="tpu_custom_call" | custom-call | flops 12884901888 | bytes 25165824 | tf_op jit(solution)/shard_map/attend/pallas_call | solution.py:343
  59.7 15.0 %enter.4 = (bf16[2048,768]{1,0:T(8,128)(2,1)}, bf16[2048,2304]{1,0:T(8,128)(2,1)}) custom-call(s32[4]{0:T(128)} %pad_add_fusion.info_ref, bf16[4,512,768]{2,1,0:T(8,128)(2,1)} %bitcast.182, bf16[1,512,768]{2,1,0:T(8,128)(2,1)} %collective-permute-done.1.got_ref, bf16[768,2304]{1,0:T(8,128)(2,1)} %w_ref.9, ...), custom_call_target="tpu_custom_call", output_to_operand_aliasing={{0}: (6, {}), {1}: (7, {})} | custom-call | flops 3623878656 | bytes 7864320 | tf_op jit(solution)/shard_map/enter/pallas_call | solution.py:510
  74.7 18.6 %attend.4 = (bf16[2,1024,768]{2,1,0:T(8,128)(2,1)}, bf16[2,12,1024,1024]{3,2,1,0:T(8,128)(2,1)}, f32[2,6,2,1024]{3,2,1,0:T(2,128)}) custom-call(s32[4]{0:T(128)} %pad_add_fusion.info_ref, bf16[2,1024,2304]{2,1,0:T(8,128)(2,1)} %bitcast.163, bf16[2,1024,2304]{2,1,0:T(8,128)(2,1)} %bitcast.164, ...), custom_call_target="tpu_custom_call", output_to_operand_aliasing={{0}: (4, {}), {1}: (5, {}), {2}: (6, {})} | custom-call | flops 12884901888 | bytes 25165824 | tf_op jit(solution)/shard_map/attend/pallas_call | solution.py:343
  93.3 24.5 %middle.1 = (f32[2048,768]{1,0:T(8,128)}, bf16[2048,768]{1,0:T(8,128)(2,1)}) custom-call(s32[4]{0:T(128)} %pad_add_fusion.info_ref, bf16[2048,768]{1,0:T(8,128)(2,1)} %get-tuple-element.171.x_ref, bf16[2048,768]{1,0:T(8,128)(2,1)} %bitcast.184, bf16[768,768]{1,0:T(8,128)(2,1)} %wo_ref.5, bf16[768,768]{1,0:T(8,128)(2,1)} %wq_ref.3, f32[8,768]{1,0:T(8,128)} %concatenate.36.vec_ref), custom_call_target="tpu_custom_call" | custom-call | flops 4831838208 | bytes 15728640 | tf_op jit(solution)/shard_map/middle/pallas_call | solution.py:510
  117.8 1.3 collective-permute-start.3
  119.1 10.5 %enter.5 = (bf16[2048,768]{1,0:T(8,128)(2,1)}, bf16[2048,1536]{1,0:T(8,128)(2,1)}) custom-call(s32[4]{0:T(128)} %pad_add_fusion.info_ref, bf16[4,512,768]{2,1,0:T(8,128)(2,1)} %bitcast.189, bf16[2,512,768]{2,1,0:T(8,128)(2,1)} %collective-permute-done.2.got_ref, bf16[768,1536]{1,0:T(8,128)(2,1)} %wi_ref.3, f32[8,768]{1,0:T(8,128)} %get-tuple-element.331.vec_ref, ...), custom_call_target="tpu_custom_call" | custom-call | flops 4831838208 | bytes 12582912 | tf_op jit(solution)/shard_map/enter/pallas_call | solution.py:510
  129.6 31.1 %attend.5 = (bf16[2,1024,768]{2,1,0:T(8,128)(2,1)}, bf16[2,12,1024,1024]{3,2,1,0:T(8,128)(2,1)}, f32[2,6,2,1024]{3,2,1,0:T(2,128)}) custom-call(s32[4]{0:T(128)} %pad_add_fusion.info_ref, bf16[2,1024,768]{2,1,0:T(8,128)(2,1)} %bitcast.205, bf16[2,1024,1536]{2,1,0:T(8,128)(2,1)} %bitcast.199, bf16[2,1024,1536]{2,1,0:T(8,128)(2,1)} %bitcast.200), custom_call_target="tpu_custom_call" | custom-call | flops 25769803776 | bytes 50331648 | tf_op jit(solution)/shard_map/attend/pallas_call | solution.py:343
  161.9 136.1 %feed.1 = (bf16[4,512,768]{2,1,0:T(8,128)(2,1)}, bf16[2,512,768]{2,1,0:T(8,128)(2,1)}, f32[2048,768]{1,0:T(8,128)}, bf16[2048,768]{1,0:T(8,128)(2,1)}, f32[8,768...) custom-call(s32[4]{0:T(128)} %pad_add_fusion.info_ref, ...), custom_call_target="tpu_custom_call" | custom-call | flops 65229815808 | bytes 62914560 | tf_op jit(solution)/shard_map/feed/pallas_call | solution.py:510
  299.5 1.4 reduce.3
  301.6 30.7 %attend_back.4 = (bf16[2,1024,768]{2,1,0:T(8,128)(2,1)}, bf16[2,1024,768]{2,1,0:T(8,128)(2,1)}, bf16[2,1024,768]{2,1,0:T(8,128)(2,1)}) custom-call(bf16[2,1024,768]{2,1,0:T(8,128)(2,1)} %bitcast.206, bf16[2,1024,1536]{2,1,0:T(8,128)(2,1)} %bitcast.201, bf16[2,1024,1536]{2,1,0:T(8,128)(2,1)} %bitcast.202, ...), custom_call_target="tpu_custom_call" | custom-call | flops 25769803776 | bytes 25165824 | tf_op jit(solution)/shard_map/attend_back/pallas_call | solution.py:419
  332.3 2.8 collective-permute-done.5
  335.1 5.3 fusion
  340.4 2.3 copy-done.2
  342.7 1.7 dynamic-slice_bitcast_fusion
  344.3 2.0 collective-permute-start.6
  346.3 30.6 %attend_back.5 = (bf16[2,1024,768]{2,1,0:T(8,128)(2,1)}, bf16[2,1024,768]{2,1,0:T(8,128)(2,1)}, bf16[2,1024,768]{2,1,0:T(8,128)(2,1)}) custom-call(bf16[2,1024,768]{2,1,0:T(8,128)(2,1)} %get-tuple-element.192.refs_0_, bf16[2,1024,768]{2,1,0:T(8,128)(2,1)} %get-tuple-element.193.refs_1_, ...), custom_call_target="tpu_custom_call", output_to_operand_aliasing={{0}: (0, {}), {1}: (1, {}), {2}: (2, {})} | custom-call | flops 25769803776 | bytes 25165824 | tf_op jit(solution)/shard_map/attend_back/pallas_call | solution.py:419
  376.9 1.2 bitcast_dynamic-update-slice_fusion
  378.2 57.1 %return_rows.1 = (f32[4,512,768]{2,1,0:T(8,128)}, bf16[2,512,768]{2,1,0:T(8,128)(2,1)}, f32[2048,768]{1,0:T(8,128)}, bf16[2048,768]{1,0:T(8,128)(2,1)}, f32[8,76...) custom-call(s32[4]{0:T(128)} %pad_add_fusion.info_ref, bf16[2048,768]{1,0:T(8,128)(2,1)} %bitcast.213, ...), custom_call_target="tpu_custom_call" | custom-call | flops 19327352832 | bytes 41943040 | tf_op jit(solution)/shard_map/return_rows/pallas_call | solution.py:510
  435.3 3.2 fusion.2
  438.5 1.5 copy-done.3
  441.1 1.6 collective-permute-start.7
  443.8 30.6 %attend_back.6 = (bf16[2,1024,768]{2,1,0:T(8,128)(2,1)}, bf16[2,1024,768]{2,1,0:T(8,128)(2,1)}, bf16[2,1024,768]{2,1,0:T(8,128)(2,1)}) custom-call(bf16[2,1024,2304]{2,1,0:T(8,128)(2,1)} %bitcast.166, bf16[2,1024,2304]{2,1,0:T(8,128)(2,1)} %bitcast.167, bf16[2,1024,2304]{2,1,0:T(8,128)(2,1)} %bitcast.168, ...), custom_call_target="tpu_custom_call" | custom-call | flops 25769803776 | bytes 25165824 | tf_op jit(solution)/shard_map/attend_back/pallas_call | solution.py:419
  474.5 5.4 collective-permute-done.10
  481.0 2.0 fusion.4
  483.1 2.7 collective-permute-start.11
  485.8 2.3 fusion.3
  488.1 1.4 copy-done.4
  491.8 1.5 collective-permute-start.13
  493.3 19.8 %leave.2 = (f32[4,512,768]{2,1,0:T(8,128)}, bf16[512,768]{1,0:T(8,128)(2,1)}, f32[8,768]{1,0:T(8,128)}) custom-call(s32[4]{0:T(128)} %pad_add_fusion.info_ref, bf16[2048,768]{1,0:T(8,128)(2,1)} %bitcast.172, bf16[2048,768]{1,0:T(8,128)(2,1)} %bitcast.175, bf16[2048,768]{1,0:T(8,128)(2,1)} %bitcast.178, bf16[2048,768]{1,0:T(8,128)(2,1)} %get-tuple-element.171.x_ref, ...), custom_call_target="tpu_custom_call" | custom-call | flops 3623878656 | bytes 16777216 | tf_op jit(solution)/shard_map/leave/pallas_call | solution.py:510
  514.1 30.6 %attend_back.7 = (bf16[2,1024,768]{2,1,0:T(8,128)(2,1)}, bf16[2,1024,768]{2,1,0:T(8,128)(2,1)}, bf16[2,1024,768]{2,1,0:T(8,128)(2,1)}) custom-call(bf16[2,1024,768]{2,1,0:T(8,128)(2,1)} %get-tuple-element.229.refs_0_, bf16[2,1024,768]{2,1,0:T(8,128)(2,1)} %get-tuple-element.230.refs_1_, ...), custom_call_target="tpu_custom_call", output_to_operand_aliasing={{0}: (0, {}), {1}: (1, {}), {2}: (2, {})} | custom-call | flops 25769803776 | bytes 25165824 | tf_op jit(solution)/shard_map/attend_back/pallas_call | solution.py:419
  544.8 1.2 fusion.8
  547.1 27.6 %last_weight.1 = (bf16[8,48,1152]{2,1,0:T(8,128)(2,1)}, bf16[8,48,1152]{2,1,0:T(8,128)(2,1)}, bf16[8,48,1152]{2,1,0:T(8,128)(2,1)}, bf16[8,48,1152]{2,1,0:T(8,128)(2,1)}) custom-call(s32[4]{0:T(128)} %pad_add_fusion.info_ref, bf16[2048,768]{1,0:T(8,128)(2,1)} %bitcast.173, bf16[2048,768]{1,0:T(8,128)(2,1)} %bitcast.176, bf16[2048,768]{1,0:T(8,128)(2,1)} %bitcast.179, ...), custom_call_target="tpu_custom_call" | custom-call | flops 7247757312 | bytes 20971520 | tf_op jit(solution)/shard_map/last_weight/pallas_call | solution.py:510
  575.3 1.9 fusion.5
  579.4 1.6 collective-permute-start.17
  581.0 2.4 convert_dynamic-update-slice_fusion.2.refs_0_
  583.4 20.0 %leave.3 = (f32[4,512,768]{2,1,0:T(8,128)}, bf16[512,768]{1,0:T(8,128)(2,1)}, f32[8,768]{1,0:T(8,128)}) custom-call(s32[4]{0:T(128)} %pad_add_fusion.info_ref, bf16[2048,768]{1,0:T(8,128)(2,1)} %bitcast.174, bf16[2048,768]{1,0:T(8,128)(2,1)} %bitcast.177, bf16[2048,768]{1,0:T(8,128)(2,1)} %bitcast.180, ...), custom_call_target="tpu_custom_call", output_to_operand_aliasing={{0}: (8, {})} | custom-call | flops 3623878656 | bytes 16777216 | tf_op jit(solution)/shard_map/leave/pallas_call | solution.py:510
  604.4 1.2 fusion.9
  605.6 1.6 fusion.7
  607.9 1.4 fusion.6
  611.0 2.9 collective-permute-start.21
  613.8 1.9 convert_dynamic-update-slice_fusion
  616.3 10.3 %collective-permute-done.21 = f32[20,768]{1,0:T(8,128)S(1)} collective-permute-done((f32[20,768]{1,0:T(8,128)S(1)}, f32[20,768]{1,0:T(8,128)S(1)}, u32[]{:S(2)}, u32[]{:S(2)}) %collective-permute-start.21) | collective-permute-done | bytes 61472 | tf_op jit(solution)/shard_map/ppermute | solution.py:1077
  626.7 2.0 collective-permute-done.23
  629.6 1.3 collective-permute-start.26
  631.4 1.5 collective-permute-start.29
  633.1 2.3 collective-permute-done.29
  635.3 1.7 collective-permute-start.28
  637.0 1.2 convert_add_fusion.8
  639.1 4.5 collective-permute-done.26
  644.0 2.9 collective-permute-start.32
  646.9 1.6 collective-permute-start.33
  649.4 1.3 convert_dynamic-update-slice_fusion.1
  655.3 1.2 collective-permute-done.32
  657.2 1.5 collective-permute-start.35
  660.0 3.5 collective-permute-done.36
  665.0 2.4 collective-permute-done.37
  (196 shorter events, 35.6 us)
Async XLA Ops:
  0.7 8.6 %copy-start = (s32[4,1]{0,1:T(1,128)S(1)}, s32[4,1]{0,1:T(1,128)}, u32[]{:S(2)}) copy-start(s32[4,1]{0,1:T(1,128)} %param.28) | copy-start | bytes 52
  0.7 8.6 %copy-start.31 = (f32[768]{0:T(1024)S(1)}, f32[768]{0:T(1024)}, u32[]{:S(2)}) copy-start(f32[768]{0:T(1024)} %param.35) | copy-start | bytes 9220
  0.7 8.6 %copy-start.32 = (f32[768]{0:T(1024)S(1)}, f32[768]{0:T(1024)}, u32[]{:S(2)}) copy-start(f32[768]{0:T(1024)} %param.34) | copy-start | bytes 9220
  0.7 9.2 %copy-start.21 = (f32[768]{0:T(1024)S(1)}, f32[768]{0:T(1024)}, u32[]{:S(2)}) copy-start(f32[768]{0:T(1024)} %param.39) | copy-start | bytes 9220
  0.7 9.2 %copy-start.22 = (f32[768]{0:T(1024)S(1)}, f32[768]{0:T(1024)}, u32[]{:S(2)}) copy-start(f32[768]{0:T(1024)} %param.38) | copy-start | bytes 9220
  0.7 9.2 %copy-start.23 = (f32[768]{0:T(1024)S(1)}, f32[768]{0:T(1024)}, u32[]{:S(2)}) copy-start(f32[768]{0:T(1024)} %param.32) | copy-start | bytes 9220
  0.7 9.2 %copy-start.24 = (f32[768]{0:T(1024)S(1)}, f32[768]{0:T(1024)}, u32[]{:S(2)}) copy-start(f32[768]{0:T(1024)} %param.31) | copy-start | bytes 9220
  0.7 9.8 %copy-start.25 = (f32[768]{0:T(1024)S(1)}, f32[768]{0:T(1024)}, u32[]{:S(2)}) copy-start(f32[768]{0:T(1024)} %param.37) | copy-start | bytes 9220
  0.8 9.8 %copy-start.26 = (f32[768]{0:T(1024)S(1)}, f32[768]{0:T(1024)}, u32[]{:S(2)}) copy-start(f32[768]{0:T(1024)} %param.41) | copy-start | bytes 9220
  0.8 9.8 %copy-start.19 = (s32[4,1,512]{2,1,0:T(1,128)S(1)}, s32[4,1,512]{2,1,0:T(1,128)}, u32[]{:S(2)}) copy-start(s32[4,1,512]{2,1,0:T(1,128)} %param.29) | copy-start | bytes 24580
  0.8 9.9 %copy-start.20 = (f32[768]{0:T(1024)S(1)}, f32[768]{0:T(1024)}, u32[]{:S(2)}) copy-start(f32[768]{0:T(1024)} %param.43) | copy-start | bytes 9220
  0.8 10.5 %copy-start.27 = (f32[768]{0:T(1024)S(1)}, f32[768]{0:T(1024)}, u32[]{:S(2)}) copy-start(f32[768]{0:T(1024)} %param.45) | copy-start | bytes 9220
  0.8 10.5 %copy-start.28 = (f32[768]{0:T(1024)S(1)}, f32[768]{0:T(1024)}, u32[]{:S(2)}) copy-start(f32[768]{0:T(1024)} %param.46) | copy-start | bytes 9220
  0.8 10.5 %copy-start.29 = (f32[768]{0:T(1024)S(1)}, f32[768]{0:T(1024)}, u32[]{:S(2)}) copy-start(f32[768]{0:T(1024)} %param.47) | copy-start | bytes 9220
  0.8 10.5 %copy-start.30 = (f32[768]{0:T(1024)S(1)}, f32[768]{0:T(1024)}, u32[]{:S(2)}) copy-start(f32[768]{0:T(1024)} %param.51) | copy-start | bytes 9220
  0.8 11.9 %copy-start.6 = (bf16[4,1,512,768]{3,2,1,0:T(8,128)(2,1)S(1)}, bf16[4,1,512,768]{3,2,1,0:T(8,128)(2,1)}, u32[]{:S(2)}) copy-start(bf16[4,1,512,768]{3,2,1,0:T(8,128)(2,1)} %param.30) | copy-start | bytes 9437188
  3.6 20.8 %collective-permute-start = (bf16[1,512,768]{2,1,0:T(8,128)(2,1)}, bf16[1,512,768]{2,1,0:T(8,128)(2,1)}, u32[]{:S(2)}, u32[]{:S(2)}) collective-permute-start(bf16[1,512,768]{2,1,0:T(8,128)(2,1)} %get-tuple-element.306), channel_id=1, source_target_pairs={{0,1},{1,0},{2,3},{3,2},{4,5},{5,4},{6,7},{7,6},{8,9},{9,8},{10,11... | collective-permute-start | bytes 2359304 | tf_op jit(solution)/shard_map/ppermute | solution.py:1150
  24.4 34.9 %collective-permute-start.1 = (bf16[1,512,768]{2,1,0:T(8,128)(2,1)}, bf16[1,512,768]{2,1,0:T(8,128)(2,1)}, u32[]{:S(2)}, u32[]{:S(2)}) collective-permute-start(bf16[1,512,768]{2,1,0:T(8,128)(2,1)} %get-tuple-element.153), channel_id=1, source_target_pairs={{0,1},{1,0},{2,3},{3,2},{4,5},{5,4},{6,7},{7,6},{8,9},{9,8},{10,11... | collective-permute-start | bytes 2359304 | tf_op jit(solution)/shard_map/ppermute | solution.py:1150
  40.9 18.4 %copy-start.10 = (bf16[2,512,768]{2,1,0:T(8,128)(2,1)S(1)}, bf16[2,512,768]{2,1,0:T(8,128)(2,1)}, u32[]{:S(2)}) copy-start(bf16[2,512,768]{2,1,0:T(8,128)(2,1)} %dynamic-slice_bitcast_fusion.1) | copy-start | bytes 4718596
  59.3 58.5 %collective-permute-start.2 = (bf16[2,512,768]{2,1,0:T(8,128)(2,1)S(1)}, bf16[2,512,768]{2,1,0:T(8,128)(2,1)}, u32[]{:S(2)}, u32[]{:S(2)}) collective-permute-start(bf16[2,512,768]{2,1,0:T(8,128)(2,1)S(1)} %copy-done.10), channel_id=1, source_target_pairs={{0,1},{1,0},{2,3},{3,2},{4,5},{5,4},{6,7},{7,6},{8,9},{9,8},{10,11... | collective-permute-start | bytes 4718600 | tf_op jit(solution)/shard_map/ppermute | solution.py:1150
  117.8 42.9 %collective-permute-start.3 = (bf16[2,512,768]{2,1,0:T(8,128)(2,1)}, bf16[2,512,768]{2,1,0:T(8,128)(2,1)S(1)}, u32[]{:S(2)}, u32[]{:S(2)}) collective-permute-start(bf16[2,512,768]{2,1,0:T(8,128)(2,1)} %constant_dynamic-slice_fusion.13), channel_id=1, source_target_pairs={{0,1},{1,0},{2,3},{3,2},{4,5},{5,4},{6,7},{7,6},{8,9},{9,8},{10,11... | collective-permute-start | bytes 4718600 | tf_op jit(solution)/shard_map/ppermute | solution.py:1150
  298.0 37.1 %collective-permute-start.4 = (bf16[2,2,2,432,768]{4,3,2,1,0:T(8,128)(2,1)}, bf16[2,2,2,432,768]{4,3,2,1,0:T(8,128)(2,1)}, u32[]{:S(2)}, u32[]{:S(2)}) collective-permute-start(bf16[2,2,2,432,768]{4,3,2,1,0:T(8,128)(2,1)} %bitcast.193), channel_id=1, source_target_pairs={{0,2},{2,0},{4,6},{6,4},{8,10},{10,8},{12,14},{14,12},{16,18},{18,... | collective-permute-start | bytes 15925256 | tf_op jit(solution)/shard_map/ppermute | solution.py:1045
  298.2 36.9 %collective-permute-start.5 = (bf16[2,512,768]{2,1,0:T(8,128)(2,1)}, bf16[2,512,768]{2,1,0:T(8,128)(2,1)S(1)}, u32[]{:S(2)}, u32[]{:S(2)}) collective-permute-start(bf16[2,512,768]{2,1,0:T(8,128)(2,1)} %get-tuple-element.188), channel_id=1, source_target_pairs={{0,1},{1,0},{2,3},{3,2},{4,5},{5,4},{6,7},{7,6},{8,9},{9,8},{10,11... | collective-permute-start | bytes 4718600 | tf_op jit(solution)/shard_map/ppermute | solution.py:1233
  344.3 90.9 %collective-permute-start.6 = (bf16[2,2,432,768]{3,2,1,0:T(8,128)(2,1)}, bf16[2,2,432,768]{3,2,1,0:T(8,128)(2,1)}, u32[]{:S(2)}, u32[]{:S(2)}) collective-permute-start(bf16[2,2,432,768]{3,2,1,0:T(8,128)(2,1)} %dynamic-slice_bitcast_fusion), channel_id=1, source_target_pairs={{0,4},{2,6},{4,0},{6,2},{8,12},{10,14},{12,8},{14,10},{16,20},{18,... | collective-permute-start | bytes 7962632 | tf_op jit(solution)/shard_map/ppermute | solution.py:1045
  435.2 7.4 %copy-start.17 = (f32[8,768]{1,0:T(8,128)S(1)}, f32[8,768]{1,0:T(8,128)}, u32[]{:S(2)}) copy-start(f32[8,768]{1,0:T(8,128)} %get-tuple-element.210) | copy-start | bytes 73732
  441.1 33.4 %collective-permute-start.7 = (bf16[2,432,768]{2,1,0:T(8,128)(2,1)}, bf16[2,432,768]{2,1,0:T(8,128)(2,1)}, u32[]{:S(2)}, u32[]{:S(2)}) collective-permute-start(bf16[2,432,768]{2,1,0:T(8,128)(2,1)} %dynamic-slice_bitcast_fusion.2), channel_id=1, source_target_pairs={{0,8},{2,10},{4,12},{6,14},{8,0},{10,2},{12,4},{14,6},{16,24},{18,... | collective-permute-start | bytes 3981320 | tf_op jit(solution)/shard_map/ppermute | solution.py:1045
  442.7 37.2 %collective-permute-start.8 = (bf16[2,2,2,192,768]{4,3,2,1,0:T(8,128)(2,1)}, bf16[2,2,2,192,768]{4,3,2,1,0:T(8,128)(2,1)}, u32[]{:S(2)}, u32[]{:S(2)}) collective-permute-start(bf16[2,2,2,192,768]{4,3,2,1,0:T(8,128)(2,1)} %bitcast.30), channel_id=1, source_target_pairs={{0,2},{2,0},{4,6},{6,4},{8,10},{10,8},{12,14},{14,12},{16,18},{18,... | collective-permute-start | bytes 7077896 | tf_op jit(solution)/shard_map/ppermute | solution.py:1045
  442.7 31.7 %copy-start.12 = (f32[20,768]{1,0:T(8,128)}, f32[20,768]{1,0:T(8,128)S(1)}, u32[]{:S(2)}) copy-start(f32[20,768]{1,0:T(8,128)S(1)} %constant_dynamic-update-slice_fusion) | copy-start | bytes 184324
  442.7 31.7 %collective-permute-start.9 = (f32[20,768]{1,0:T(8,128)S(1)}, f32[20,768]{1,0:T(8,128)S(1)}, u32[]{:S(2)}, u32[]{:S(2)}) collective-permute-start(f32[20,768]{1,0:T(8,128)S(1)} %constant_dynamic-update-slice_fusion), channel_id=1, source_target_pairs={{0,2},{2,0},{4,6},{6,4},{8,10},{10,8},{12,14},{14,12},{16,18},{18,... | collective-permute-start | bytes 184328 | tf_op jit(solution)/shard_map/ppermute | solution.py:1077
  443.3 36.6 %collective-permute-start.10 = (bf16[2,512,768]{2,1,0:T(8,128)(2,1)}, bf16[2,512,768]{2,1,0:T(8,128)(2,1)S(1)}, u32[]{:S(2)}, u32[]{:S(2)}) collective-permute-start(bf16[2,512,768]{2,1,0:T(8,128)(2,1)} %get-tuple-element.219), channel_id=1, source_target_pairs={{0,1},{1,0},{2,3},{3,2},{4,5},{5,4},{6,7},{7,6},{8,9},{9,8},{10,11... | collective-permute-start | bytes 4718600 | tf_op jit(solution)/shard_map/ppermute | solution.py:1265
  474.4 11.4 %copy-start.7 = (bf16[8,192,768]{2,1,0:T(8,128)(2,1)S(1)}, bf16[8,192,768]{2,1,0:T(8,128)(2,1)}, u32[]{:S(2)}) copy-start(bf16[8,192,768]{2,1,0:T(8,128)(2,1)} %get-tuple-element.221) | copy-start | bytes 7077892
  474.5 6.6 copy-start.15
  483.1 61.6 %collective-permute-start.11 = (bf16[432,768]{1,0:T(8,128)(2,1)S(1)}, bf16[432,768]{1,0:T(8,128)(2,1)}, u32[]{:S(2)}, u32[]{:S(2)}) collective-permute-start(bf16[432,768]{1,0:T(8,128)(2,1)S(1)} %dynamic-slice_bitcast_fusion.6), channel_id=1, source_target_pairs={{0,16},{2,18},{4,20},{6,22},{8,24},{10,26},{12,28},{14,30},{16,0},... | collective-permute-start | bytes 1990664 | tf_op jit(solution)/shard_map/ppermute | solution.py:1045
  485.8 5.4 copy-start.16
  490.6 54.1 %collective-permute-start.12 = (bf16[2,2,192,768]{3,2,1,0:T(8,128)(2,1)}, bf16[2,2,192,768]{3,2,1,0:T(8,128)(2,1)}, u32[]{:S(2)}, u32[]{:S(2)}) collective-permute-start(bf16[2,2,192,768]{3,2,1,0:T(8,128)(2,1)} %dynamic-slice_bitcast_fusion.3), channel_id=1, source_target_pairs={{0,4},{2,6},{4,0},{6,2},{8,12},{10,14},{12,8},{14,10},{16,20},{18,... | collective-permute-start | bytes 3538952 | tf_op jit(solution)/shard_map/ppermute | solution.py:1045
  491.8 52.9 %collective-permute-start.13 = (f32[20,768]{1,0:T(8,128)}, f32[20,768]{1,0:T(8,128)}, u32[]{:S(2)}, u32[]{:S(2)}) collective-permute-start(f32[20,768]{1,0:T(8,128)} %add.225), channel_id=1, source_target_pairs={{0,4},{2,6},{4,0},{6,2},{8,12},{10,14},{12,8},{14,10},{16,20},{18,... | collective-permute-start | bytes 184328 | tf_op jit(solution)/shard_map/ppermute | solution.py:1077
  513.1 31.7 %collective-permute-start.14 = (bf16[512,768]{1,0:T(8,128)(2,1)}, bf16[512,768]{1,0:T(8,128)(2,1)}, u32[]{:S(2)}, u32[]{:S(2)}) collective-permute-start(bf16[512,768]{1,0:T(8,128)(2,1)} %get-tuple-element.235), channel_id=1, source_target_pairs={{0,1},{1,0},{2,3},{3,2},{4,5},{5,4},{6,7},{7,6},{8,9},{9,8},{10,11... | collective-permute-start | bytes 2359304 | tf_op jit(solution)/shard_map/ppermute | solution.py:1292
  546.0 58.3 %collective-permute-start.15 = (bf16[432,768]{1,0:T(8,128)(2,1)S(1)}, bf16[432,768]{1,0:T(8,128)(2,1)}, u32[]{:S(2)}, u32[]{:S(2)}) collective-permute-start(bf16[432,768]{1,0:T(8,128)(2,1)S(1)} %fusion.8), channel_id=1, source_target_pairs={{0,1},{1,0},{2,3},{3,2},{4,5},{5,4},{6,7},{7,6},{8,9},{9,8},{10,11... | collective-permute-start | bytes 1990664 | tf_op jit(solution)/shard_map/ppermute | solution.py:1047
  574.7 29.6 %collective-permute-start.18 = (bf16[2,2,2,48,1152]{4,3,2,1,0:T(8,128)(2,1)}, bf16[2,2,2,48,1152]{4,3,2,1,0:T(8,128)(2,1)}, u32[]{:S(2)}, u32[]{:S(2)}) collective-permute-start(bf16[2,2,2,48,1152]{4,3,2,1,0:T(8,128)(2,1)} %bitcast.197), channel_id=1, source_target_pairs={{0,2},{2,0},{4,6},{6,4},{8,10},{10,8},{12,14},{14,12},{16,18},{18,... | collective-permute-start | bytes 2654216 | tf_op jit(solution)/shard_map/ppermute | solution.py:1045
  574.8 29.6 %collective-permute-start.19 = (bf16[2,2,2,48,1152]{4,3,2,1,0:T(8,128)(2,1)}, bf16[2,2,2,48,1152]{4,3,2,1,0:T(8,128)(2,1)}, u32[]{:S(2)}, u32[]{:S(2)}) collective-permute-start(bf16[2,2,2,48,1152]{4,3,2,1,0:T(8,128)(2,1)} %bitcast.196), channel_id=1, source_target_pairs={{0,2},{2,0},{4,6},{6,4},{8,10},{10,8},{12,14},{14,12},{16,18},{18,... | collective-permute-start | bytes 2654216 | tf_op jit(solution)/shard_map/ppermute | solution.py:1045
  578.0 26.3 %collective-permute-start.16 = (bf16[2,192,768]{2,1,0:T(8,128)(2,1)}, bf16[2,192,768]{2,1,0:T(8,128)(2,1)}, u32[]{:S(2)}, u32[]{:S(2)}) collective-permute-start(bf16[2,192,768]{2,1,0:T(8,128)(2,1)} %dynamic-slice_bitcast_fusion.7), channel_id=1, source_target_pairs={{0,8},{2,10},{4,12},{6,14},{8,0},{10,2},{12,4},{14,6},{16,24},{18,... | collective-permute-start | bytes 1769480 | tf_op jit(solution)/shard_map/ppermute | solution.py:1045
  579.4 24.9 %collective-permute-start.17 = (f32[20,768]{1,0:T(8,128)S(1)}, f32[20,768]{1,0:T(8,128)S(1)}, u32[]{:S(2)}, u32[]{:S(2)}) collective-permute-start(f32[20,768]{1,0:T(8,128)S(1)} %add.228), channel_id=1, source_target_pairs={{0,8},{2,10},{4,12},{6,14},{8,0},{10,2},{12,4},{14,6},{16,24},{18,... | collective-permute-start | bytes 184328 | tf_op jit(solution)/shard_map/ppermute | solution.py:1077
  583.4 20.1 %copy-start.18 = (f32[8,768]{1,0:T(8,128)S(1)}, f32[8,768]{1,0:T(8,128)}, u32[]{:S(2)}) copy-start(f32[8,768]{1,0:T(8,128)} %get-tuple-element.252) | copy-start | bytes 73732
  607.2 6.6 copy-start.9
  607.3 19.4 %collective-permute-start.22 = (bf16[2,2,48,1152]{3,2,1,0:T(8,128)(2,1)S(1)}, bf16[2,2,48,1152]{3,2,1,0:T(8,128)(2,1)S(1)}, u32[]{:S(2)}, u32[]{:S(2)}) collective-permute-start(bf16[2,2,48,1152]{3,2,1,0:T(8,128)(2,1)S(1)} %dynamic-slice_bitcast_fusion.9), channel_id=1, source_target_pairs={{0,4},{2,6},{4,0},{6,2},{8,12},{10,14},{12,8},{14,10},{16,20},{18,... | collective-permute-start | bytes 1327112 | tf_op jit(solution)/shard_map/ppermute | solution.py:1045
  609.3 6.5 copy-start.34
  609.3 19.4 %collective-permute-start.23 = (bf16[2,2,48,1152]{3,2,1,0:T(8,128)(2,1)S(1)}, bf16[2,2,48,1152]{3,2,1,0:T(8,128)(2,1)S(1)}, u32[]{:S(2)}, u32[]{:S(2)}) collective-permute-start(bf16[2,2,48,1152]{3,2,1,0:T(8,128)(2,1)S(1)} %dynamic-slice_bitcast_fusion.8), channel_id=1, source_target_pairs={{0,8},{2,10},{4,12},{6,14},{8,0},{10,2},{12,4},{14,6},{16,24},{18,... | collective-permute-start | bytes 1327112 | tf_op jit(solution)/shard_map/ppermute | solution.py:1045
  609.9 16.8 %collective-permute-start.20 = (bf16[192,768]{1,0:T(8,128)(2,1)S(1)}, bf16[192,768]{1,0:T(8,128)(2,1)S(1)}, u32[]{:S(2)}, u32[]{:S(2)}) collective-permute-start(bf16[192,768]{1,0:T(8,128)(2,1)S(1)} %dynamic-slice_bitcast_fusion.10), channel_id=1, source_target_pairs={{0,16},{2,18},{4,20},{6,22},{8,24},{10,26},{12,28},{14,30},{16,0},... | collective-permute-start | bytes 884744 | tf_op jit(solution)/shard_map/ppermute | solution.py:1045
  611.0 15.7 %collective-permute-start.21 = (f32[20,768]{1,0:T(8,128)S(1)}, f32[20,768]{1,0:T(8,128)S(1)}, u32[]{:S(2)}, u32[]{:S(2)}) collective-permute-start(f32[20,768]{1,0:T(8,128)S(1)} %add.231), channel_id=1, source_target_pairs={{0,16},{2,18},{4,20},{6,22},{8,24},{10,26},{12,28},{14,30},{16,0},... | collective-permute-start | bytes 184328 | tf_op jit(solution)/shard_map/ppermute | solution.py:1077
  613.8 1.9 collective-permute-start.24
  615.7 27.9 %collective-permute-start.30 = (bf16[512,768]{1,0:T(8,128)(2,1)S(1)}, bf16[512,768]{1,0:T(8,128)(2,1)S(1)}, u32[]{:S(2)}, u32[]{:S(2)}) collective-permute-start(bf16[512,768]{1,0:T(8,128)(2,1)S(1)} %copy-done.34), channel_id=1, source_target_pairs={{0,1},{1,0},{2,3},{3,2},{4,5},{5,4},{6,7},{7,6},{8,9},{9,8},{10,11... | collective-permute-start | bytes 2359304 | tf_op jit(solution)/shard_map/ppermute | solution.py:1306
  628.8 14.8 %collective-permute-start.25 = (bf16[192,768]{1,0:T(8,128)(2,1)S(1)}, bf16[192,768]{1,0:T(8,128)(2,1)S(1)}, u32[]{:S(2)}, u32[]{:S(2)}) collective-permute-start(bf16[192,768]{1,0:T(8,128)(2,1)S(1)} %fusion.12), channel_id=1, source_target_pairs={{0,1},{1,0},{2,3},{3,2},{4,5},{5,4},{6,7},{7,6},{8,9},{9,8},{10,11... | collective-permute-start | bytes 884744 | tf_op jit(solution)/shard_map/ppermute | solution.py:1047
  629.6 13.9 %collective-permute-start.26 = (f32[20,768]{1,0:T(8,128)S(1)}, f32[20,768]{1,0:T(8,128)S(1)}, u32[]{:S(2)}, u32[]{:S(2)}) collective-permute-start(f32[20,768]{1,0:T(8,128)S(1)} %add.235), channel_id=1, source_target_pairs={{0,1},{1,0},{2,3},{3,2},{4,5},{5,4},{6,7},{7,6},{8,9},{9,8},{10,11... | collective-permute-start | bytes 184328 | tf_op jit(solution)/shard_map/ppermute | solution.py:1079
  631.1 12.5 %collective-permute-start.27 = (bf16[2,48,1152]{2,1,0:T(8,128)(2,1)S(1)}, bf16[2,48,1152]{2,1,0:T(8,128)(2,1)S(1)}, u32[]{:S(2)}, u32[]{:S(2)}) collective-permute-start(bf16[2,48,1152]{2,1,0:T(8,128)(2,1)S(1)} %dynamic-slice_bitcast_fusion.12), channel_id=1, source_target_pairs={{0,8},{2,10},{4,12},{6,14},{8,0},{10,2},{12,4},{14,6},{16,24},{18,... | collective-permute-start | bytes 663560 | tf_op jit(solution)/shard_map/ppermute | solution.py:1045
  631.4 4.0 collective-permute-start.29
  635.3 8.2 %collective-permute-start.28 = (bf16[2,48,1152]{2,1,0:T(8,128)(2,1)S(1)}, bf16[2,48,1152]{2,1,0:T(8,128)(2,1)S(1)}, u32[]{:S(2)}, u32[]{:S(2)}) collective-permute-start(bf16[2,48,1152]{2,1,0:T(8,128)(2,1)S(1)} %dynamic-slice_bitcast_fusion.11), channel_id=1, source_target_pairs={{0,4},{2,6},{4,0},{6,2},{8,12},{10,14},{12,8},{14,10},{16,20},{18,... | collective-permute-start | bytes 663560 | tf_op jit(solution)/shard_map/ppermute | solution.py:1045
  643.7 11.5 %collective-permute-start.31 = (bf16[48,1152]{1,0:T(8,128)(2,1)S(1)}, bf16[48,1152]{1,0:T(8,128)(2,1)S(1)}, u32[]{:S(2)}, u32[]{:S(2)}) collective-permute-start(bf16[48,1152]{1,0:T(8,128)(2,1)S(1)} %dynamic-slice_bitcast_fusion.14), channel_id=1, source_target_pairs={{0,16},{2,18},{4,20},{6,22},{8,24},{10,26},{12,28},{14,30},{16,0},... | collective-permute-start | bytes 331784 | tf_op jit(solution)/shard_map/ppermute | solution.py:1045
  644.0 12.5 %collective-permute-start.32 = (bf16[48,1152]{1,0:T(8,128)(2,1)S(1)}, bf16[48,1152]{1,0:T(8,128)(2,1)S(1)}, u32[]{:S(2)}, u32[]{:S(2)}) collective-permute-start(bf16[48,1152]{1,0:T(8,128)(2,1)S(1)} %dynamic-slice_bitcast_fusion.13), channel_id=1, source_target_pairs={{0,16},{2,18},{4,20},{6,22},{8,24},{10,26},{12,28},{14,30},{16,0},... | collective-permute-start | bytes 331784 | tf_op jit(solution)/shard_map/ppermute | solution.py:1045
  646.9 7.7 %collective-permute-start.33 = (f32[8,768]{1,0:T(8,128)S(1)}, f32[8,768]{1,0:T(8,128)S(1)}, u32[]{:S(2)}, u32[]{:S(2)}) collective-permute-start(f32[8,768]{1,0:T(8,128)S(1)} %add.239), channel_id=1, source_target_pairs={{0,8},{2,10},{4,12},{6,14},{8,0},{10,2},{12,4},{14,6},{16,24},{18,... | collective-permute-start | bytes 73736 | tf_op jit(solution)/shard_map/ppermute | solution.py:1077
  649.4 19.2 %copy-start.1 = (s32[4,1]{0,1:T(1,128)S(1)}, s32[4,1]{0,1:T(1,128)}, u32[]{:S(2)}) copy-start(s32[4,1]{0,1:T(1,128)} %param.28) | copy-start | bytes 52
  656.5 6.9 %collective-permute-start.34 = (bf16[48,1152]{1,0:T(8,128)(2,1)S(1)}, bf16[48,1152]{1,0:T(8,128)(2,1)S(1)}, u32[]{:S(2)}, u32[]{:S(2)}) collective-permute-start(bf16[48,1152]{1,0:T(8,128)(2,1)S(1)} %fusion.16), channel_id=1, source_target_pairs={{0,1},{1,0},{2,3},{3,2},{4,5},{5,4},{6,7},{7,6},{8,9},{9,8},{10,11... | collective-permute-start | bytes 331784 | tf_op jit(solution)/shard_map/ppermute | solution.py:1047
  657.2 6.2 collective-permute-start.35
  658.7 4.7 collective-permute-start.36
  663.5 3.9 collective-permute-start.37
  (9 other events, 24.0 us)

commit v6 on v4

--- a/solution.py
+++ b/solution.py
@@ -263,56 +263,32 @@
 
 
 def attend_kernel(info_ref, q_ref, k_ref, v_ref, *refs, use_mask, start):
-    o_ref, e_ref, r_ref = refs[-3:]
+    o_ref, e_ref, r_ref, mask_ref = refs[-4:]
     length = k_ref.shape[1]
     half = length // 2
     values_turned = v_ref[0].T
     ones = jnp.ones((16, length), jnp.bfloat16)
-    side = info_ref[0]
-
-    def run(masked, shifted, side_now=None):
+
+    def run(masked, shifted):
         lowest, highest = None, None
-        below = (
-            lax.broadcasted_iota(jnp.int32, (half, 1), 0)
-            <= lax.broadcasted_iota(jnp.int32, (1, half), 1)
-            if masked
-            else None
-        )
         for at in range(2):
             queries_at = slice(at * half, (at + 1) * half)
-            if masked:
-                seen = [at] if at == side_now else [0, 1]
-            else:
-                seen = [None]
             mixed = []
             for head, queries in enumerate(head_masks(q_ref[0, queries_at, :])):
-                tiles = []
-                for key_at in seen:
-                    rows = slice(0, length)
-                    if key_at is not None:
-                        rows = slice(key_at * half, (key_at + 1) * half)
-                    scores = contract(k_ref[0, rows, :], queries, 1, 1)
-                    if key_at == at:
-                        scores = jnp.where(below, scores, blocked_score)
-                    tiles.append((rows, scores))
+                scores = contract(k_ref[0], queries, 1, 1)
                 if shifted:
-                    highest_score = functools.reduce(
-                        jnp.maximum,
-                        [jnp.max(scores, axis=0, keepdims=True) for _, scores in tiles],
-                    )
-                    tiles = [(rows, scores - highest_score) for rows, scores in tiles]
-                sums = None
-                for rows, scores in tiles:
-                    low = jnp.exp(scores).astype(jnp.bfloat16)
-                    e_ref[0, head, rows, queries_at] = low
-                    turned = jnp.concatenate(
-                        [values_turned[head * HEAD : (head + 1) * HEAD, rows], ones[:, rows]], axis=0
-                    )
-                    part = contract(turned, low, 1, 0)
-                    sums = part if sums is None else sums + part
-                if masked and len(seen) == 1:
-                    other = slice((1 - at) * half, (2 - at) * half)
-                    e_ref[0, head, other, queries_at] = jnp.zeros((half, half), jnp.bfloat16)
+                    if masked:
+                        seen = mask_ref[:, queries_at].astype(jnp.float32) > 0
+                        scores = jnp.where(seen, scores, blocked_score)
+                    scores = scores - jnp.max(scores, axis=0, keepdims=True)
+                low = jnp.exp(scores).astype(jnp.bfloat16)
+                if masked:
+                    low = low * mask_ref[:, queries_at]
+                e_ref[0, head, :, queries_at] = low
+                turned = jnp.concatenate(
+                    [values_turned[head * HEAD : (head + 1) * HEAD], ones], axis=0
+                )
+                sums = contract(turned, low, 1, 0)
                 total = sums[HEAD : HEAD + 1]
                 if not shifted:
                     lowest = total if lowest is None else jnp.minimum(lowest, total)
@@ -326,17 +302,29 @@
 
             @pl.when(jnp.logical_not(in_range))
             def _():
-                run(masked, True, side_now)
+                run(masked, True)
 
     if not use_mask:
         run(False, False)
         return
     causal = info_ref[2 + start + pl.program_id(0)] == 0
-    for side_now in range(2):
-
-        @pl.when(causal & (side == side_now))
-        def _():
-            run(True, False, side_now)
+
+    @pl.when(causal & (pl.program_id(1) == 0))
+    def _():
+        later = info_ref[0] * half
+        query = lax.broadcasted_iota(jnp.int32, (1, length), 1)
+        query = jnp.where(query < half, query + later, query - later)
+
+        @pl.loop(0, length, step=64)
+        def _(row):
+            key = lax.broadcasted_iota(jnp.int32, (64, 1), 0) + row
+            key = jnp.where(key < half, key + later, key - later)
+            seen = jnp.where(key <= query, 1.0, 0.0)
+            mask_ref[pl.ds(pl.multiple_of(row, 64), 64), :] = seen.astype(jnp.bfloat16)
+
+    @pl.when(causal)
+    def _():
+        run(True, False)
 
     @pl.when(jnp.logical_not(causal))
     def _():
@@ -364,6 +352,7 @@
                 pl.BlockSpec((1, 2, length, length), place),
                 pl.BlockSpec((1, 1, 2, length), place),
             ],
+            scratch_shapes=[pltpu.VMEM((length, length), jnp.bfloat16)],
         ),
         out_shape=[
             jax.ShapeDtypeStruct((count, length, width), jnp.bfloat16),
@@ -1004,19 +993,22 @@
         if self.total is not None or self.got is not None:
             return
         if self.bit < self.count:
-            pairs = [(i, i ^ self.bit) for i in range(self.count)]
-            self.got = lax.ppermute(self.rows, "dp", pairs)
+            steps = [step * self.bit for step in (1, 2, 3) if step * self.bit < self.count]
+            self.got = [
+                lax.ppermute(self.rows, "dp", [(i, i ^ step) for i in range(self.count)])
+                for step in steps
+            ]
         else:
-            self.got = lax.ppermute(self.rows, "seq", SWAP)
+            self.got = [lax.ppermute(self.rows, "seq", SWAP)]
 
     def add(self):
         if self.got is None:
             return
-        self.rows = self.rows + self.got
+        self.rows = sum(self.got, self.rows)
         self.got = None
-        if self.bit == self.count:
+        if self.bit >= self.count:
             self.total = self.rows
-        self.bit *= 2
+        self.bit *= 4
 
 
 def exchange(trees):
@@ -1075,9 +1067,10 @@
     length = 2 * own
     pairs = HEADS * HEAD // 128
 
-    def swap(rows, at, count):
+    def swap(rows, at, count, after=()):
         sent = lax.dynamic_slice_in_dim(rows, (1 - side) * held + at, count, axis=0)
-        return lax.ppermute(sent, "seq", SWAP)
+        sent, after = lax.optimization_barrier((sent, after))
+        return lax.ppermute(sent, "seq", SWAP), after
 
     def give(owns, got, at):
         got = got.astype(owns.dtype)
@@ -1094,12 +1087,18 @@
         return rows.reshape(held * length, -1)
 
     targets, memory = targets[:, 0], memory[:, 0]
-    target_gots = [swap(targets, at, 1) for at in range(held)]
-    memory_gots = swap(memory, 0, held)
     upstreams = (
         cotangent[:, 0].astype(jnp.float32) * loss_mask[:, 0].astype(jnp.float32)[..., None]
     ).astype(jnp.bfloat16)
-    upstream_gots = swap(upstreams, 0, held)
+    target_gots, last_got = [], ()
+    for at in range(held):
+        got, last_got = swap(targets, at, 1, last_got)
+        target_gots.append(got)
+        if at:
+            target_gots[at - 1] = last_got
+        last_got = got
+    memory_gots, target_gots[-1] = swap(memory, 0, held, last_got)
+    upstream_gots, memory_gots = swap(upstreams, 0, held, memory_gots)
     kinds = lax.dynamic_slice_in_dim(row_kind[:, 0], side * held, held, axis=0)
     info = jnp.concatenate([jnp.stack([side, place % 2]).astype(jnp.int32), kinds])
 
@@ -1203,9 +1202,11 @@
                 Tree(*late_parts[0:2], low_first),
                 Tree(*late_parts[2:4], second_first),
             ]
+            grads = settle(trees, lax.optimization_barrier((grads, late_parts[0]))[0])
             trees = trees + late_trees
             exchange(trees)
-            grads, _ = lax.optimization_barrier((grads, late_parts[0]))
+            grads = settle(late_trees, grads)
+            exchange(trees)
         kept, got, sums = leave(
             info, at, kept, [flat(rows) for rows in grads], inputs, grad_self,
             self_input, self_vectors, own, micros,

time: 598 us -> 581 us (0.972)
  waiting for transfers between devices: 58.5 us -> 26.8 us
  local copies, waits for them, and re-layouts: 29.4 us -> 37.7 us
  starting transfers between devices: 39.7 us -> 46.7 us
    ppermute x14 -> x18, waiting for transfers between devices: 47.6 us -> 12 us  [the longest x4 7.52 us: swap(): return (lax.ppermute(sent, 'seq', SWAP), after)]
    ppermute x14 -> x18, starting transfers between devices: 17.1 us -> 24.6 us  [the longest x12 15.9 us: exchange(): lax.ppermute(self.rows, 'dp', [(i, i ^ step) for i in range(self.count)])]
  transfers between devices with their start and end apart: 38 -> 42, of which waited for: 11 -> 9; matrix products, arithmetic and copies ran while one was open for 6% -> 9% of each run, Pallas kernels for 53% -> 55%
where the time goes in v6:
time: 581 us; the launch traced here: 576 us
  Pallas kernels  424 us (73%)
  starting transfers between devices  46.7 us (8%)
  other arithmetic  39.4 us (7%)
  local copies, waits for them, and re-layouts  37.7 us (6%)
  waiting for transfers between devices  26.8 us (5%)
    pallas_call x9, Pallas kernels, kernel_call(): pl.pallas_call(kernel, grid_spec=pltpu.PrefetchScalarGridSpec(num_scalar_...  233 us
    pallas_call x4, Pallas kernels, attend_back(): pl.pallas_call(kernel, grid=size, in_specs=[pl.BlockSpec(memory_space=pl....  123 us
    pallas_call x3, Pallas kernels, attend(): pl.pallas_call(functools.partial(attend_kernel, use_mask=use_mask, start=...  67.7 us
    convert_element_type x16, other arithmetic, add(): total = total.astype(jnp.bfloat16)  22 us
    ppermute x12, starting transfers between devices, exchange(): lax.ppermute(self.rows, 'dp', [(i, i ^ step) for i in range(self.count)])  15.9 us
    ppermute x16, starting transfers between devices, exchange(): self.got = lax.ppermute(self.sent, 'dp', pairs)  13.8 us
  transfers between devices with their start and end apart: 42, of which 9 were waited for; matrix products, arithmetic and copies ran while one was open for 9% of the time, Pallas kernels for 55%

profile of v6, /device:TPU:0, one launch (start us, length us, event | category | flops | bytes accessed | tf_op | source)
XLA Modules:
  0.0 576.1 jit_solution(9987848045573613719)
XLA Ops:
  0.8 2.8 dynamic-slice_bitcast_fusion.4
  3.6 3.0 collective-permute-start
  6.6 2.7 dynamic-slice_bitcast_fusion.1
  13.3 1.7 copy-done.6
  15.0 1.2 constant_dynamic-slice_fusion.13
  16.9 7.5 %collective-permute-done.got_ref = bf16[1,512,768]{2,1,0:T(8,128)(2,1)} collective-permute-done((bf16[1,512,768]{2,1,0:T(8,128)(2,1)}, bf16[1,512,768]{2,1,0:T(8,128)(2,1)}, u32[]{:S(2)}, u32[]{:S(2)}) %collective-permute-start) | collective-permute-done | bytes 786464 | tf_op jit(solution)/shard_map/ppermute | solution.py:1073
  24.4 1.7 collective-permute-start.1
  26.2 9.5 %enter.3 = (bf16[2048,768]{1,0:T(8,128)(2,1)}, bf16[2048,2304]{1,0:T(8,128)(2,1)}) custom-call(s32[4]{0:T(128)} %pad_add_fusion.info_ref, bf16[4,512,768]{2,1,0:T(8,128)(2,1)} %bitcast.181, bf16[1,512,768]{2,1,0:T(8,128)(2,1)} %collective-permute-done.got_ref, bf16[768,2304]{1,0:T(8,128)(2,1)} %w_ref.9, f32[8,768]{1,0:T(8,128)} %get-tuple-element.353.vec_ref, ...), custom_call_target="tpu_custom_call" | custom-call | flops 3623878656 | bytes 7864320 | tf_op jit(solution)/shard_map/enter/pallas_call | solution.py:510
  35.7 18.5 %attend.3 = (bf16[2,1024,768]{2,1,0:T(8,128)(2,1)}, bf16[2,12,1024,1024]{3,2,1,0:T(8,128)(2,1)}, f32[2,6,2,1024]{3,2,1,0:T(2,128)}) custom-call(s32[4]{0:T(128)} %pad_add_fusion.info_ref, bf16[2,1024,2304]{2,1,0:T(8,128)(2,1)} %bitcast.160, bf16[2,1024,2304]{2,1,0:T(8,128)(2,1)} %bitcast.161, bf16[2,1024,2304]{2,1,0:T(8,128)(2,1)} %bitcast.162), custom_call_target="tpu_custom_call" | custom-call | flops 12884901888 | bytes 25165824 | tf_op jit(solution)/shard_map/attend/pallas_call | solution.py:343
  54.5 9.7 %enter.4 = (bf16[2048,768]{1,0:T(8,128)(2,1)}, bf16[2048,2304]{1,0:T(8,128)(2,1)}) custom-call(s32[4]{0:T(128)} %pad_add_fusion.info_ref, bf16[4,512,768]{2,1,0:T(8,128)(2,1)} %bitcast.182, bf16[1,512,768]{2,1,0:T(8,128)(2,1)} %collective-permute-done.1.got_ref, bf16[768,2304]{1,0:T(8,128)(2,1)} %w_ref.9, ...), custom_call_target="tpu_custom_call", output_to_operand_aliasing={{0}: (6, {}), {1}: (7, {})} | custom-call | flops 3623878656 | bytes 7864320 | tf_op jit(solution)/shard_map/enter/pallas_call | solution.py:510
  64.2 18.1 %attend.4 = (bf16[2,1024,768]{2,1,0:T(8,128)(2,1)}, bf16[2,12,1024,1024]{3,2,1,0:T(8,128)(2,1)}, f32[2,6,2,1024]{3,2,1,0:T(2,128)}) custom-call(s32[4]{0:T(128)} %pad_add_fusion.info_ref, bf16[2,1024,2304]{2,1,0:T(8,128)(2,1)} %bitcast.163, bf16[2,1024,2304]{2,1,0:T(8,128)(2,1)} %bitcast.164, ...), custom_call_target="tpu_custom_call", output_to_operand_aliasing={{0}: (4, {}), {1}: (5, {}), {2}: (6, {})} | custom-call | flops 12884901888 | bytes 25165824 | tf_op jit(solution)/shard_map/attend/pallas_call | solution.py:343
  82.3 12.9 %middle.1 = (f32[2048,768]{1,0:T(8,128)}, bf16[2048,768]{1,0:T(8,128)(2,1)}) custom-call(s32[4]{0:T(128)} %pad_add_fusion.info_ref, bf16[2048,768]{1,0:T(8,128)(2,1)} %get-tuple-element.182.x_ref, bf16[2048,768]{1,0:T(8,128)(2,1)} %bitcast.186, bf16[768,768]{1,0:T(8,128)(2,1)} %wo_ref.5, bf16[768,768]{1,0:T(8,128)(2,1)} %wq_ref.3, f32[8,768]{1,0:T(8,128)} %concatenate.36.vec_ref), custom_call_target="tpu_custom_call" | custom-call | flops 4831838208 | bytes 15728640 | tf_op jit(solution)/shard_map/middle/pallas_call | solution.py:510
  95.2 1.8 collective-permute-start.3
  97.0 10.5 %enter.5 = (bf16[2048,768]{1,0:T(8,128)(2,1)}, bf16[2048,1536]{1,0:T(8,128)(2,1)}) custom-call(s32[4]{0:T(128)} %pad_add_fusion.info_ref, bf16[4,512,768]{2,1,0:T(8,128)(2,1)} %bitcast.191, bf16[2,512,768]{2,1,0:T(8,128)(2,1)} %collective-permute-done.2.got_ref, bf16[768,1536]{1,0:T(8,128)(2,1)} %wi_ref.3, f32[8,768]{1,0:T(8,128)} %get-tuple-element.353.vec_ref, ...), custom_call_target="tpu_custom_call" | custom-call | flops 4831838208 | bytes 12582912 | tf_op jit(solution)/shard_map/enter/pallas_call | solution.py:510
  107.4 31.1 %attend.5 = (bf16[2,1024,768]{2,1,0:T(8,128)(2,1)}, bf16[2,12,1024,1024]{3,2,1,0:T(8,128)(2,1)}, f32[2,6,2,1024]{3,2,1,0:T(2,128)}) custom-call(s32[4]{0:T(128)} %pad_add_fusion.info_ref, bf16[2,1024,768]{2,1,0:T(8,128)(2,1)} %bitcast.207, bf16[2,1024,1536]{2,1,0:T(8,128)(2,1)} %bitcast.201, bf16[2,1024,1536]{2,1,0:T(8,128)(2,1)} %bitcast.202), custom_call_target="tpu_custom_call" | custom-call | flops 25769803776 | bytes 50331648 | tf_op jit(solution)/shard_map/attend/pallas_call | solution.py:343
  139.7 108.1 %feed.1 = (bf16[4,512,768]{2,1,0:T(8,128)(2,1)}, bf16[2,512,768]{2,1,0:T(8,128)(2,1)}, f32[2048,768]{1,0:T(8,128)}, bf16[2048,768]{1,0:T(8,128)(2,1)}, f32[8,768...) custom-call(s32[4]{0:T(128)} %pad_add_fusion.info_ref, ...), custom_call_target="tpu_custom_call" | custom-call | flops 65229815808 | bytes 62914560 | tf_op jit(solution)/shard_map/feed/pallas_call | solution.py:510
  248.8 1.4 reduce.3
  251.0 30.7 %attend_back.4 = (bf16[2,1024,768]{2,1,0:T(8,128)(2,1)}, bf16[2,1024,768]{2,1,0:T(8,128)(2,1)}, bf16[2,1024,768]{2,1,0:T(8,128)(2,1)}) custom-call(bf16[2,1024,768]{2,1,0:T(8,128)(2,1)} %bitcast.208, bf16[2,1024,1536]{2,1,0:T(8,128)(2,1)} %bitcast.203, bf16[2,1024,1536]{2,1,0:T(8,128)(2,1)} %bitcast.204, ...), custom_call_target="tpu_custom_call" | custom-call | flops 25769803776 | bytes 25165824 | tf_op jit(solution)/shard_map/attend_back/pallas_call | solution.py:419
  281.6 3.2 collective-permute-done.5
  284.9 5.3 fusion
  290.2 2.3 copy-done.2
  292.5 1.7 dynamic-slice_bitcast_fusion
  294.2 1.5 collective-permute-start.6
  295.6 30.6 %attend_back.5 = (bf16[2,1024,768]{2,1,0:T(8,128)(2,1)}, bf16[2,1024,768]{2,1,0:T(8,128)(2,1)}, bf16[2,1024,768]{2,1,0:T(8,128)(2,1)}) custom-call(bf16[2,1024,768]{2,1,0:T(8,128)(2,1)} %get-tuple-element.203.refs_0_, bf16[2,1024,768]{2,1,0:T(8,128)(2,1)} %get-tuple-element.204.refs_1_, ...), custom_call_target="tpu_custom_call", output_to_operand_aliasing={{0}: (0, {}), {1}: (1, {}), {2}: (2, {})} | custom-call | flops 25769803776 | bytes 25165824 | tf_op jit(solution)/shard_map/attend_back/pallas_call | solution.py:419
  326.3 1.2 bitcast_dynamic-update-slice_fusion
  327.5 41.2 %return_rows.1 = (f32[4,512,768]{2,1,0:T(8,128)}, bf16[2,512,768]{2,1,0:T(8,128)(2,1)}, f32[2048,768]{1,0:T(8,128)}, bf16[2048,768]{1,0:T(8,128)(2,1)}, f32[8,76...) custom-call(s32[4]{0:T(128)} %pad_add_fusion.info_ref, bf16[2048,768]{1,0:T(8,128)(2,1)} %bitcast.215, ...), custom_call_target="tpu_custom_call" | custom-call | flops 19327352832 | bytes 41943040 | tf_op jit(solution)/shard_map/return_rows/pallas_call | solution.py:510
  370.1 1.2 collective-permute-start.11
  371.3 3.2 fusion.2
  374.5 1.5 copy-done.3
  377.1 1.6 collective-permute-start.7
  378.8 1.5 collective-permute-start.12
  380.3 30.8 %attend_back.6 = (bf16[2,1024,768]{2,1,0:T(8,128)(2,1)}, bf16[2,1024,768]{2,1,0:T(8,128)(2,1)}, bf16[2,1024,768]{2,1,0:T(8,128)(2,1)}) custom-call(bf16[2,1024,2304]{2,1,0:T(8,128)(2,1)} %bitcast.166, bf16[2,1024,2304]{2,1,0:T(8,128)(2,1)} %bitcast.167, bf16[2,1024,2304]{2,1,0:T(8,128)(2,1)} %bitcast.168, ...), custom_call_target="tpu_custom_call" | custom-call | flops 25769803776 | bytes 25165824 | tf_op jit(solution)/shard_map/attend_back/pallas_call | solution.py:419
  411.2 4.6 collective-permute-done.12
  416.9 3.6 collective-permute-start.16
  420.5 2.0 fusion.4
  422.7 2.3 fusion.3
  425.0 1.4 copy-done.4
  427.8 11.8 %leave.2 = (f32[4,512,768]{2,1,0:T(8,128)}, bf16[512,768]{1,0:T(8,128)(2,1)}, f32[8,768]{1,0:T(8,128)}) custom-call(s32[4]{0:T(128)} %pad_add_fusion.info_ref, bf16[2048,768]{1,0:T(8,128)(2,1)} %bitcast.172, bf16[2048,768]{1,0:T(8,128)(2,1)} %bitcast.175, bf16[2048,768]{1,0:T(8,128)(2,1)} %bitcast.178, bf16[2048,768]{1,0:T(8,128)(2,1)} %get-tuple-element.182.x_ref, ...), custom_call_target="tpu_custom_call" | custom-call | flops 3623878656 | bytes 16777216 | tf_op jit(solution)/shard_map/leave/pallas_call | solution.py:510
  440.5 30.7 %attend_back.7 = (bf16[2,1024,768]{2,1,0:T(8,128)(2,1)}, bf16[2,1024,768]{2,1,0:T(8,128)(2,1)}, bf16[2,1024,768]{2,1,0:T(8,128)(2,1)}) custom-call(bf16[2,1024,768]{2,1,0:T(8,128)(2,1)} %get-tuple-element.242.refs_0_, bf16[2,1024,768]{2,1,0:T(8,128)(2,1)} %get-tuple-element.243.refs_1_, ...), custom_call_target="tpu_custom_call", output_to_operand_aliasing={{0}: (0, {}), {1}: (1, {}), {2}: (2, {})} | custom-call | flops 25769803776 | bytes 25165824 | tf_op jit(solution)/shard_map/attend_back/pallas_call | solution.py:419
  471.1 3.7 collective-permute-start.17
  474.8 3.5 convert_dynamic-update-slice_fusion
  478.3 1.2 fusion.8
  479.6 1.3 collective-permute-start.19
  480.8 1.5 fusion.5
  485.1 17.5 %last_weight.1 = (bf16[8,48,1152]{2,1,0:T(8,128)(2,1)}, bf16[8,48,1152]{2,1,0:T(8,128)(2,1)}, bf16[8,48,1152]{2,1,0:T(8,128)(2,1)}, bf16[8,48,1152]{2,1,0:T(8,128)(2,1)}) custom-call(s32[4]{0:T(128)} %pad_add_fusion.info_ref, bf16[2048,768]{1,0:T(8,128)(2,1)} %bitcast.173, bf16[2048,768]{1,0:T(8,128)(2,1)} %bitcast.176, bf16[2048,768]{1,0:T(8,128)(2,1)} %bitcast.179, ...), custom_call_target="tpu_custom_call" | custom-call | flops 7247757312 | bytes 20971520 | tf_op jit(solution)/shard_map/last_weight/pallas_call | solution.py:510
  503.1 2.4 convert_dynamic-update-slice_fusion.2.refs_0_
  505.5 1.3 fusion.9
  507.7 3.4 collective-permute-start.22
  513.2 1.2 convert_add_fusion.8
  516.4 1.7 collective-permute-start.25
  520.7 12.0 %leave.3 = (f32[4,512,768]{2,1,0:T(8,128)}, bf16[512,768]{1,0:T(8,128)(2,1)}, f32[8,768]{1,0:T(8,128)}) custom-call(s32[4]{0:T(128)} %pad_add_fusion.info_ref, bf16[2048,768]{1,0:T(8,128)(2,1)} %bitcast.174, bf16[2048,768]{1,0:T(8,128)(2,1)} %bitcast.177, bf16[2048,768]{1,0:T(8,128)(2,1)} %bitcast.180, ...), custom_call_target="tpu_custom_call", output_to_operand_aliasing={{0}: (8, {})} | custom-call | flops 3623878656 | bytes 16777216 | tf_op jit(solution)/shard_map/leave/pallas_call | solution.py:510
  535.5 1.3 collective-permute-start.27
  536.8 1.3 fusion.11
  539.6 1.3 fusion.10
  542.8 1.4 collective-permute-start.31
  546.8 2.0 collective-permute-done.31
  549.7 1.8 collective-permute-start.35
  552.4 1.8 collective-permute-start.37
  554.2 1.5 collective-permute-start.33
  558.5 1.5 collective-permute-start.34
  560.8 2.8 collective-permute-done.33
  563.5 2.8 collective-permute-done.34
  570.0 1.3 convert_dynamic-update-slice_fusion.1
  571.3 2.5 collective-permute-done.41
  (203 shorter events, 44.3 us)
Async XLA Ops:
  0.7 8.6 %copy-start.33 = (f32[768]{0:T(1024)S(1)}, f32[768]{0:T(1024)}, u32[]{:S(2)}) copy-start(f32[768]{0:T(1024)} %param.35) | copy-start | bytes 9220
  0.7 8.6 %copy-start.34 = (f32[768]{0:T(1024)S(1)}, f32[768]{0:T(1024)}, u32[]{:S(2)}) copy-start(f32[768]{0:T(1024)} %param.34) | copy-start | bytes 9220
  0.7 9.2 %copy-start.23 = (f32[768]{0:T(1024)S(1)}, f32[768]{0:T(1024)}, u32[]{:S(2)}) copy-start(f32[768]{0:T(1024)} %param.39) | copy-start | bytes 9220
  0.7 9.2 %copy-start.24 = (f32[768]{0:T(1024)S(1)}, f32[768]{0:T(1024)}, u32[]{:S(2)}) copy-start(f32[768]{0:T(1024)} %param.38) | copy-start | bytes 9220
  0.7 9.2 %copy-start.25 = (f32[768]{0:T(1024)S(1)}, f32[768]{0:T(1024)}, u32[]{:S(2)}) copy-start(f32[768]{0:T(1024)} %param.32) | copy-start | bytes 9220
  0.7 9.2 %copy-start.26 = (f32[768]{0:T(1024)S(1)}, f32[768]{0:T(1024)}, u32[]{:S(2)}) copy-start(f32[768]{0:T(1024)} %param.31) | copy-start | bytes 9220
  0.7 9.8 %copy-start.27 = (f32[768]{0:T(1024)S(1)}, f32[768]{0:T(1024)}, u32[]{:S(2)}) copy-start(f32[768]{0:T(1024)} %param.37) | copy-start | bytes 9220
  0.8 9.8 %copy-start.28 = (f32[768]{0:T(1024)S(1)}, f32[768]{0:T(1024)}, u32[]{:S(2)}) copy-start(f32[768]{0:T(1024)} %param.41) | copy-start | bytes 9220
  0.8 9.8 %copy-start.21 = (s32[4,1,512]{2,1,0:T(1,128)S(1)}, s32[4,1,512]{2,1,0:T(1,128)}, u32[]{:S(2)}) copy-start(s32[4,1,512]{2,1,0:T(1,128)} %param.29) | copy-start | bytes 24580
  0.8 9.9 %copy-start.22 = (f32[768]{0:T(1024)S(1)}, f32[768]{0:T(1024)}, u32[]{:S(2)}) copy-start(f32[768]{0:T(1024)} %param.43) | copy-start | bytes 9220
  0.8 10.5 %copy-start.29 = (f32[768]{0:T(1024)S(1)}, f32[768]{0:T(1024)}, u32[]{:S(2)}) copy-start(f32[768]{0:T(1024)} %param.45) | copy-start | bytes 9220
  0.8 10.5 %copy-start.30 = (f32[768]{0:T(1024)S(1)}, f32[768]{0:T(1024)}, u32[]{:S(2)}) copy-start(f32[768]{0:T(1024)} %param.46) | copy-start | bytes 9220
  0.8 10.5 %copy-start.31 = (f32[768]{0:T(1024)S(1)}, f32[768]{0:T(1024)}, u32[]{:S(2)}) copy-start(f32[768]{0:T(1024)} %param.47) | copy-start | bytes 9220
  0.8 10.5 %copy-start.32 = (f32[768]{0:T(1024)S(1)}, f32[768]{0:T(1024)}, u32[]{:S(2)}) copy-start(f32[768]{0:T(1024)} %param.51) | copy-start | bytes 9220
  0.8 11.9 %copy-start.9 = (bf16[4,1,512,768]{3,2,1,0:T(8,128)(2,1)S(1)}, bf16[4,1,512,768]{3,2,1,0:T(8,128)(2,1)}, u32[]{:S(2)}) copy-start(bf16[4,1,512,768]{3,2,1,0:T(8,128)(2,1)} %param.30) | copy-start | bytes 9437188
  3.6 20.8 %collective-permute-start = (bf16[1,512,768]{2,1,0:T(8,128)(2,1)}, bf16[1,512,768]{2,1,0:T(8,128)(2,1)}, u32[]{:S(2)}, u32[]{:S(2)}) collective-permute-start(bf16[1,512,768]{2,1,0:T(8,128)(2,1)} %get-tuple-element.328), channel_id=1, source_target_pairs={{0,1},{1,0},{2,3},{3,2},{4,5},{5,4},{6,7},{7,6},{8,9},{9,8},{10,11... | collective-permute-start | bytes 2359304 | tf_op jit(solution)/shard_map/ppermute | solution.py:1073
  24.4 29.7 %collective-permute-start.1 = (bf16[1,512,768]{2,1,0:T(8,128)(2,1)}, bf16[1,512,768]{2,1,0:T(8,128)(2,1)}, u32[]{:S(2)}, u32[]{:S(2)}) collective-permute-start(bf16[1,512,768]{2,1,0:T(8,128)(2,1)} %get-tuple-element.164), channel_id=1, source_target_pairs={{0,1},{1,0},{2,3},{3,2},{4,5},{5,4},{6,7},{7,6},{8,9},{9,8},{10,11... | collective-permute-start | bytes 2359304 | tf_op jit(solution)/shard_map/ppermute | solution.py:1073
  35.7 18.5 %copy-start.14 = (bf16[2,512,768]{2,1,0:T(8,128)(2,1)S(1)}, bf16[2,512,768]{2,1,0:T(8,128)(2,1)}, u32[]{:S(2)}) copy-start(bf16[2,512,768]{2,1,0:T(8,128)(2,1)} %dynamic-slice_bitcast_fusion.1) | copy-start | bytes 4718596
  54.1 41.0 %collective-permute-start.2 = (bf16[2,512,768]{2,1,0:T(8,128)(2,1)S(1)}, bf16[2,512,768]{2,1,0:T(8,128)(2,1)}, u32[]{:S(2)}, u32[]{:S(2)}) collective-permute-start(bf16[2,512,768]{2,1,0:T(8,128)(2,1)S(1)} %copy-done.14), channel_id=1, source_target_pairs={{0,1},{1,0},{2,3},{3,2},{4,5},{5,4},{6,7},{7,6},{8,9},{9,8},{10,11... | collective-permute-start | bytes 4718600 | tf_op jit(solution)/shard_map/ppermute | solution.py:1073
  95.2 43.4 %collective-permute-start.3 = (bf16[2,512,768]{2,1,0:T(8,128)(2,1)}, bf16[2,512,768]{2,1,0:T(8,128)(2,1)S(1)}, u32[]{:S(2)}, u32[]{:S(2)}) collective-permute-start(bf16[2,512,768]{2,1,0:T(8,128)(2,1)} %constant_dynamic-slice_fusion.13), channel_id=1, source_target_pairs={{0,1},{1,0},{2,3},{3,2},{4,5},{5,4},{6,7},{7,6},{8,9},{9,8},{10,11... | collective-permute-start | bytes 4718600 | tf_op jit(solution)/shard_map/ppermute | solution.py:1073
  247.8 37.1 %collective-permute-start.4 = (bf16[2,2,2,432,768]{4,3,2,1,0:T(8,128)(2,1)}, bf16[2,2,2,432,768]{4,3,2,1,0:T(8,128)(2,1)}, u32[]{:S(2)}, u32[]{:S(2)}) collective-permute-start(bf16[2,2,2,432,768]{4,3,2,1,0:T(8,128)(2,1)} %bitcast.195), channel_id=1, source_target_pairs={{0,2},{2,0},{4,6},{6,4},{8,10},{10,8},{12,14},{14,12},{16,18},{18,... | collective-permute-start | bytes 15925256 | tf_op jit(solution)/shard_map/ppermute | solution.py:965
  248.0 36.9 %collective-permute-start.5 = (bf16[2,512,768]{2,1,0:T(8,128)(2,1)}, bf16[2,512,768]{2,1,0:T(8,128)(2,1)S(1)}, u32[]{:S(2)}, u32[]{:S(2)}) collective-permute-start(bf16[2,512,768]{2,1,0:T(8,128)(2,1)} %get-tuple-element.199), channel_id=1, source_target_pairs={{0,1},{1,0},{2,3},{3,2},{4,5},{5,4},{6,7},{7,6},{8,9},{9,8},{10,11... | collective-permute-start | bytes 4718600 | tf_op jit(solution)/shard_map/ppermute | solution.py:1156
  294.2 74.5 %collective-permute-start.6 = (bf16[2,2,432,768]{3,2,1,0:T(8,128)(2,1)}, bf16[2,2,432,768]{3,2,1,0:T(8,128)(2,1)}, u32[]{:S(2)}, u32[]{:S(2)}) collective-permute-start(bf16[2,2,432,768]{3,2,1,0:T(8,128)(2,1)} %dynamic-slice_bitcast_fusion), channel_id=1, source_target_pairs={{0,4},{2,6},{4,0},{6,2},{8,12},{10,14},{12,8},{14,10},{16,20},{18,... | collective-permute-start | bytes 7962632 | tf_op jit(solution)/shard_map/ppermute | solution.py:965
  369.5 9.4 %collective-permute-start.9 = (f32[20,768]{1,0:T(8,128)S(1)}, f32[20,768]{1,0:T(8,128)S(1)}, u32[]{:S(2)}, u32[]{:S(2)}) collective-permute-start(f32[20,768]{1,0:T(8,128)S(1)} %constant_dynamic-update-slice_fusion), channel_id=1, source_target_pairs={{0,2},{2,0},{4,6},{6,4},{8,10},{10,8},{12,14},{14,12},{16,18},{18,... | collective-permute-start | bytes 184328 | tf_op jit(solution)/shard_map/ppermute | solution.py:998
  369.5 41.7 %collective-permute-start.10 = (f32[20,768]{1,0:T(8,128)S(1)}, f32[20,768]{1,0:T(8,128)S(1)}, u32[]{:S(2)}, u32[]{:S(2)}) collective-permute-start(f32[20,768]{1,0:T(8,128)S(1)} %constant_dynamic-update-slice_fusion), channel_id=1, source_target_pairs={{0,4},{2,6},{4,0},{6,2},{8,12},{10,14},{12,8},{14,10},{16,20},{18,... | collective-permute-start | bytes 184328 | tf_op jit(solution)/shard_map/ppermute | solution.py:998
  370.1 41.1 %collective-permute-start.11 = (f32[20,768]{1,0:T(8,128)S(1)}, f32[20,768]{1,0:T(8,128)S(1)}, u32[]{:S(2)}, u32[]{:S(2)}) collective-permute-start(f32[20,768]{1,0:T(8,128)S(1)} %constant_dynamic-update-slice_fusion), channel_id=1, source_target_pairs={{0,6},{2,4},{4,2},{6,0},{8,14},{10,12},{12,10},{14,8},{16,22},{18,... | collective-permute-start | bytes 184328 | tf_op jit(solution)/shard_map/ppermute | solution.py:998
  377.1 34.0 %collective-permute-start.7 = (bf16[2,432,768]{2,1,0:T(8,128)(2,1)}, bf16[2,432,768]{2,1,0:T(8,128)(2,1)}, u32[]{:S(2)}, u32[]{:S(2)}) collective-permute-start(bf16[2,432,768]{2,1,0:T(8,128)(2,1)} %dynamic-slice_bitcast_fusion.2), channel_id=1, source_target_pairs={{0,8},{2,10},{4,12},{6,14},{8,0},{10,2},{12,4},{14,6},{16,24},{18,... | collective-permute-start | bytes 3981320 | tf_op jit(solution)/shard_map/ppermute | solution.py:965
  378.7 37.0 %collective-permute-start.8 = (bf16[2,2,2,192,768]{4,3,2,1,0:T(8,128)(2,1)}, bf16[2,2,2,192,768]{4,3,2,1,0:T(8,128)(2,1)}, u32[]{:S(2)}, u32[]{:S(2)}) collective-permute-start(bf16[2,2,2,192,768]{4,3,2,1,0:T(8,128)(2,1)} %bitcast.30), channel_id=1, source_target_pairs={{0,2},{2,0},{4,6},{6,4},{8,10},{10,8},{12,14},{14,12},{16,18},{18,... | collective-permute-start | bytes 7077896 | tf_op jit(solution)/shard_map/ppermute | solution.py:965
  378.8 37.0 %collective-permute-start.12 = (bf16[2,512,768]{2,1,0:T(8,128)(2,1)}, bf16[2,512,768]{2,1,0:T(8,128)(2,1)S(1)}, u32[]{:S(2)}, u32[]{:S(2)}) collective-permute-start(bf16[2,512,768]{2,1,0:T(8,128)(2,1)} %get-tuple-element.231), channel_id=1, source_target_pairs={{0,1},{1,0},{2,3},{3,2},{4,5},{5,4},{6,7},{7,6},{8,9},{9,8},{10,11... | collective-permute-start | bytes 4718600 | tf_op jit(solution)/shard_map/ppermute | solution.py:1188
  411.2 11.5 %copy-start.10 = (bf16[8,192,768]{2,1,0:T(8,128)(2,1)S(1)}, bf16[8,192,768]{2,1,0:T(8,128)(2,1)}, u32[]{:S(2)}) copy-start(bf16[8,192,768]{2,1,0:T(8,128)(2,1)} %get-tuple-element.218) | copy-start | bytes 7077892
  416.5 54.7 %collective-permute-start.15 = (f32[20,768]{1,0:T(8,128)}, f32[20,768]{1,0:T(8,128)}, u32[]{:S(2)}, u32[]{:S(2)}) collective-permute-start(f32[20,768]{1,0:T(8,128)} %add_add_fusion.1), channel_id=1, source_target_pairs={{0,8},{2,10},{4,12},{6,14},{8,0},{10,2},{12,4},{14,6},{16,24},{18,... | collective-permute-start | bytes 184328 | tf_op jit(solution)/shard_map/ppermute | solution.py:998
  416.9 61.3 %collective-permute-start.16 = (f32[20,768]{1,0:T(8,128)}, f32[20,768]{1,0:T(8,128)}, u32[]{:S(2)}, u32[]{:S(2)}) collective-permute-start(f32[20,768]{1,0:T(8,128)} %add_add_fusion.1), channel_id=1, source_target_pairs={{0,16},{2,18},{4,20},{6,22},{8,24},{10,26},{12,28},{14,30},{16,0},... | collective-permute-start | bytes 184328 | tf_op jit(solution)/shard_map/ppermute | solution.py:998
  422.6 55.7 %collective-permute-start.13 = (bf16[432,768]{1,0:T(8,128)(2,1)S(1)}, bf16[432,768]{1,0:T(8,128)(2,1)}, u32[]{:S(2)}, u32[]{:S(2)}) collective-permute-start(bf16[432,768]{1,0:T(8,128)(2,1)S(1)} %dynamic-slice_bitcast_fusion.6), channel_id=1, source_target_pairs={{0,16},{2,18},{4,20},{6,22},{8,24},{10,26},{12,28},{14,30},{16,0},... | collective-permute-start | bytes 1990664 | tf_op jit(solution)/shard_map/ppermute | solution.py:965
  427.5 50.8 %collective-permute-start.14 = (bf16[2,2,192,768]{3,2,1,0:T(8,128)(2,1)}, bf16[2,2,192,768]{3,2,1,0:T(8,128)(2,1)}, u32[]{:S(2)}, u32[]{:S(2)}) collective-permute-start(bf16[2,2,192,768]{3,2,1,0:T(8,128)(2,1)} %dynamic-slice_bitcast_fusion.3), channel_id=1, source_target_pairs={{0,4},{2,6},{4,0},{6,2},{8,12},{10,14},{12,8},{14,10},{16,20},{18,... | collective-permute-start | bytes 3538952 | tf_op jit(solution)/shard_map/ppermute | solution.py:965
  439.6 38.6 %collective-permute-start.18 = (bf16[512,768]{1,0:T(8,128)(2,1)}, bf16[512,768]{1,0:T(8,128)(2,1)}, u32[]{:S(2)}, u32[]{:S(2)}) collective-permute-start(bf16[512,768]{1,0:T(8,128)(2,1)} %get-tuple-element.248), channel_id=1, source_target_pairs={{0,1},{1,0},{2,3},{3,2},{4,5},{5,4},{6,7},{7,6},{8,9},{9,8},{10,11... | collective-permute-start | bytes 2359304 | tf_op jit(solution)/shard_map/ppermute | solution.py:1217
  471.1 7.1 %collective-permute-start.17 = (f32[20,768]{1,0:T(8,128)}, f32[20,768]{1,0:T(8,128)S(1)}, u32[]{:S(2)}, u32[]{:S(2)}) collective-permute-start(f32[20,768]{1,0:T(8,128)} %add_add_fusion.1), channel_id=1, source_target_pairs={{0,24},{2,26},{4,28},{6,30},{8,16},{10,18},{12,20},{14,22},{16,8},... | collective-permute-start | bytes 184328 | tf_op jit(solution)/shard_map/ppermute | solution.py:998
  479.6 26.0 %collective-permute-start.19 = (bf16[432,768]{1,0:T(8,128)(2,1)S(1)}, bf16[432,768]{1,0:T(8,128)(2,1)}, u32[]{:S(2)}, u32[]{:S(2)}) collective-permute-start(bf16[432,768]{1,0:T(8,128)(2,1)S(1)} %fusion.8), channel_id=1, source_target_pairs={{0,1},{1,0},{2,3},{3,2},{4,5},{5,4},{6,7},{7,6},{8,9},{9,8},{10,11... | collective-permute-start | bytes 1990664 | tf_op jit(solution)/shard_map/ppermute | solution.py:967
  483.3 22.3 %collective-permute-start.20 = (bf16[2,192,768]{2,1,0:T(8,128)(2,1)}, bf16[2,192,768]{2,1,0:T(8,128)(2,1)}, u32[]{:S(2)}, u32[]{:S(2)}) collective-permute-start(bf16[2,192,768]{2,1,0:T(8,128)(2,1)} %dynamic-slice_bitcast_fusion.7), channel_id=1, source_target_pairs={{0,8},{2,10},{4,12},{6,14},{8,0},{10,2},{12,4},{14,6},{16,24},{18,... | collective-permute-start | bytes 1769480 | tf_op jit(solution)/shard_map/ppermute | solution.py:965
  484.2 21.3 %collective-permute-start.21 = (f32[20,768]{1,0:T(8,128)S(1)}, f32[20,768]{1,0:T(8,128)S(1)}, u32[]{:S(2)}, u32[]{:S(2)}) collective-permute-start(f32[20,768]{1,0:T(8,128)S(1)} %add_add_fusion), channel_id=1, source_target_pairs={{0,1},{1,0},{2,3},{3,2},{4,5},{5,4},{6,7},{7,6},{8,9},{9,8},{10,11... | collective-permute-start | bytes 184328 | tf_op jit(solution)/shard_map/ppermute | solution.py:1002
  502.6 11.8 %collective-permute-start.23 = (bf16[2,2,2,48,1152]{4,3,2,1,0:T(8,128)(2,1)}, bf16[2,2,2,48,1152]{4,3,2,1,0:T(8,128)(2,1)S(1)}, u32[]{:S(2)}, u32[]{:S(2)}) collective-permute-start(bf16[2,2,2,48,1152]{4,3,2,1,0:T(8,128)(2,1)} %bitcast.199), channel_id=1, source_target_pairs={{0,2},{2,0},{4,6},{6,4},{8,10},{10,8},{12,14},{14,12},{16,18},{18,... | collective-permute-start | bytes 2654216 | tf_op jit(solution)/shard_map/ppermute | solution.py:965
  502.6 11.8 %collective-permute-start.24 = (bf16[2,2,2,48,1152]{4,3,2,1,0:T(8,128)(2,1)}, bf16[2,2,2,48,1152]{4,3,2,1,0:T(8,128)(2,1)S(1)}, u32[]{:S(2)}, u32[]{:S(2)}) collective-permute-start(bf16[2,2,2,48,1152]{4,3,2,1,0:T(8,128)(2,1)} %bitcast.198), channel_id=1, source_target_pairs={{0,2},{2,0},{4,6},{6,4},{8,10},{10,8},{12,14},{14,12},{16,18},{18,... | collective-permute-start | bytes 2654216 | tf_op jit(solution)/shard_map/ppermute | solution.py:965
  505.5 9.0 %copy-start.16 = (bf16[8,48,1152]{2,1,0:T(8,128)(2,1)S(1)}, bf16[8,48,1152]{2,1,0:T(8,128)(2,1)}, u32[]{:S(2)}) copy-start(bf16[8,48,1152]{2,1,0:T(8,128)(2,1)} %get-tuple-element.257) | copy-start | bytes 2654212
  507.7 25.8 %collective-permute-start.22 = (bf16[192,768]{1,0:T(8,128)(2,1)}, bf16[192,768]{1,0:T(8,128)(2,1)}, u32[]{:S(2)}, u32[]{:S(2)}) collective-permute-start(bf16[192,768]{1,0:T(8,128)(2,1)} %dynamic-slice_bitcast_fusion.10), channel_id=1, source_target_pairs={{0,16},{2,18},{4,20},{6,22},{8,24},{10,26},{12,28},{14,30},{16,0},... | collective-permute-start | bytes 884744 | tf_op jit(solution)/shard_map/ppermute | solution.py:965
  516.4 17.1 %collective-permute-start.25 = (bf16[2,2,48,1152]{3,2,1,0:T(8,128)(2,1)}, bf16[2,2,48,1152]{3,2,1,0:T(8,128)(2,1)}, u32[]{:S(2)}, u32[]{:S(2)}) collective-permute-start(bf16[2,2,48,1152]{3,2,1,0:T(8,128)(2,1)} %dynamic-slice_bitcast_fusion.9), channel_id=1, source_target_pairs={{0,4},{2,6},{4,0},{6,2},{8,12},{10,14},{12,8},{14,10},{16,20},{18,... | collective-permute-start | bytes 1327112 | tf_op jit(solution)/shard_map/ppermute | solution.py:965
  520.1 14.4 %collective-permute-start.26 = (bf16[2,2,48,1152]{3,2,1,0:T(8,128)(2,1)}, bf16[2,2,48,1152]{3,2,1,0:T(8,128)(2,1)}, u32[]{:S(2)}, u32[]{:S(2)}) collective-permute-start(bf16[2,2,48,1152]{3,2,1,0:T(8,128)(2,1)} %dynamic-slice_bitcast_fusion.8), channel_id=1, source_target_pairs={{0,8},{2,10},{4,12},{6,14},{8,0},{10,2},{12,4},{14,6},{16,24},{18,... | collective-permute-start | bytes 1327112 | tf_op jit(solution)/shard_map/ppermute | solution.py:965
  520.7 12.1 %copy-start.20 = (f32[8,768]{1,0:T(8,128)S(1)}, f32[8,768]{1,0:T(8,128)}, u32[]{:S(2)}) copy-start(f32[8,768]{1,0:T(8,128)} %get-tuple-element.277) | copy-start | bytes 73732
  520.7 13.8 %copy-start.12 = (bf16[2,192,768]{2,1,0:T(8,128)(2,1)S(1)}, bf16[2,192,768]{2,1,0:T(8,128)(2,1)}, u32[]{:S(2)}) copy-start(bf16[2,192,768]{2,1,0:T(8,128)(2,1)} %copy-done.11) | copy-start | bytes 1769476
  532.7 12.6 %slice-start = ((f32[20,768]{1,0:T(8,128)}), f32[4,768]{1,0:T(4,128)S(1)}, s32[]{:S(2)}) async-start(f32[20,768]{1,0:T(8,128)} %copy-done.18), calls=%async_computation | async-start | bytes 24576 | tf_op jit(solution)/shard_map/slice | solution.py:1250
  535.5 14.1 %collective-permute-start.27 = (bf16[192,768]{1,0:T(8,128)(2,1)S(1)}, bf16[192,768]{1,0:T(8,128)(2,1)S(1)}, u32[]{:S(2)}, u32[]{:S(2)}) collective-permute-start(bf16[192,768]{1,0:T(8,128)(2,1)S(1)} %fusion.12), channel_id=1, source_target_pairs={{0,1},{1,0},{2,3},{3,2},{4,5},{5,4},{6,7},{7,6},{8,9},{9,8},{10,11... | collective-permute-start | bytes 884744 | tf_op jit(solution)/shard_map/ppermute | solution.py:967
  538.8 10.9 %collective-permute-start.28 = (bf16[2,48,1152]{2,1,0:T(8,128)(2,1)}, bf16[2,48,1152]{2,1,0:T(8,128)(2,1)S(1)}, u32[]{:S(2)}, u32[]{:S(2)}) collective-permute-start(bf16[2,48,1152]{2,1,0:T(8,128)(2,1)} %dynamic-slice_bitcast_fusion.12), channel_id=1, source_target_pairs={{0,8},{2,10},{4,12},{6,14},{8,0},{10,2},{12,4},{14,6},{16,24},{18,... | collective-permute-start | bytes 663560 | tf_op jit(solution)/shard_map/ppermute | solution.py:965
  541.6 8.0 %collective-permute-start.29 = (bf16[2,48,1152]{2,1,0:T(8,128)(2,1)}, bf16[2,48,1152]{2,1,0:T(8,128)(2,1)S(1)}, u32[]{:S(2)}, u32[]{:S(2)}) collective-permute-start(bf16[2,48,1152]{2,1,0:T(8,128)(2,1)} %dynamic-slice_bitcast_fusion.11), channel_id=1, source_target_pairs={{0,4},{2,6},{4,0},{6,2},{8,12},{10,14},{12,8},{14,10},{16,20},{18,... | collective-permute-start | bytes 663560 | tf_op jit(solution)/shard_map/ppermute | solution.py:965
  542.2 2.0 collective-permute-start.30
  542.8 6.0 %collective-permute-start.31 = (f32[8,768]{1,0:T(8,128)S(1)}, f32[8,768]{1,0:T(8,128)S(1)}, u32[]{:S(2)}, u32[]{:S(2)}) collective-permute-start(f32[8,768]{1,0:T(8,128)S(1)} %add.248), channel_id=1, source_target_pairs={{0,4},{2,6},{4,0},{6,2},{8,12},{10,14},{12,8},{14,10},{16,20},{18,... | collective-permute-start | bytes 73736 | tf_op jit(solution)/shard_map/ppermute | solution.py:998
  544.2 5.4 collective-permute-start.32
  548.8 17.9 %collective-permute-start.38 = (bf16[512,768]{1,0:T(8,128)(2,1)}, bf16[512,768]{1,0:T(8,128)(2,1)S(1)}, u32[]{:S(2)}, u32[]{:S(2)}) collective-permute-start(bf16[512,768]{1,0:T(8,128)(2,1)} %get-tuple-element.289), channel_id=1, source_target_pairs={{0,1},{1,0},{2,3},{3,2},{4,5},{5,4},{6,7},{7,6},{8,9},{9,8},{10,11... | collective-permute-start | bytes 2359304 | tf_op jit(solution)/shard_map/ppermute | solution.py:1231
  549.7 8.8 %collective-permute-start.35 = (f32[8,768]{1,0:T(8,128)S(1)}, f32[8,768]{1,0:T(8,128)S(1)}, u32[]{:S(2)}, u32[]{:S(2)}) collective-permute-start(f32[8,768]{1,0:T(8,128)S(1)} %add_add_fusion.3), channel_id=1, source_target_pairs={{0,8},{2,10},{4,12},{6,14},{8,0},{10,2},{12,4},{14,6},{16,24},{18,... | collective-permute-start | bytes 73736 | tf_op jit(solution)/shard_map/ppermute | solution.py:998
  551.5 9.3 %collective-permute-start.36 = (f32[8,768]{1,0:T(8,128)S(1)}, f32[8,768]{1,0:T(8,128)S(1)}, u32[]{:S(2)}, u32[]{:S(2)}) collective-permute-start(f32[8,768]{1,0:T(8,128)S(1)} %add_add_fusion.3), channel_id=1, source_target_pairs={{0,16},{2,18},{4,20},{6,22},{8,24},{10,26},{12,28},{14,30},{16,0},... | collective-permute-start | bytes 73736 | tf_op jit(solution)/shard_map/ppermute | solution.py:998
  552.4 8.4 %collective-permute-start.37 = (f32[8,768]{1,0:T(8,128)S(1)}, f32[8,768]{1,0:T(8,128)S(1)}, u32[]{:S(2)}, u32[]{:S(2)}) collective-permute-start(f32[8,768]{1,0:T(8,128)S(1)} %add_add_fusion.3), channel_id=1, source_target_pairs={{0,24},{2,26},{4,28},{6,30},{8,16},{10,18},{12,20},{14,22},{16,8},... | collective-permute-start | bytes 73736 | tf_op jit(solution)/shard_map/ppermute | solution.py:998
  554.2 9.3 %collective-permute-start.33 = (bf16[48,1152]{1,0:T(8,128)(2,1)S(1)}, bf16[48,1152]{1,0:T(8,128)(2,1)S(1)}, u32[]{:S(2)}, u32[]{:S(2)}) collective-permute-start(bf16[48,1152]{1,0:T(8,128)(2,1)S(1)} %dynamic-slice_bitcast_fusion.14), channel_id=1, source_target_pairs={{0,16},{2,18},{4,20},{6,22},{8,24},{10,26},{12,28},{14,30},{16,0},... | collective-permute-start | bytes 331784 | tf_op jit(solution)/shard_map/ppermute | solution.py:965
  557.6 18.2 %copy-start.1 = (s32[4,1]{0,1:T(1,128)S(1)}, s32[4,1]{0,1:T(1,128)}, u32[]{:S(2)}) copy-start(s32[4,1]{0,1:T(1,128)} %param.28) | copy-start | bytes 52
  558.5 7.9 %collective-permute-start.34 = (bf16[48,1152]{1,0:T(8,128)(2,1)S(1)}, bf16[48,1152]{1,0:T(8,128)(2,1)S(1)}, u32[]{:S(2)}, u32[]{:S(2)}) collective-permute-start(bf16[48,1152]{1,0:T(8,128)(2,1)S(1)} %dynamic-slice_bitcast_fusion.13), channel_id=1, source_target_pairs={{0,16},{2,18},{4,20},{6,22},{8,24},{10,26},{12,28},{14,30},{16,0},... | collective-permute-start | bytes 331784 | tf_op jit(solution)/shard_map/ppermute | solution.py:965
  566.8 7.0 %collective-permute-start.39 = (bf16[48,1152]{1,0:T(8,128)(2,1)S(1)}, bf16[48,1152]{1,0:T(8,128)(2,1)S(1)}, u32[]{:S(2)}, u32[]{:S(2)}) collective-permute-start(bf16[48,1152]{1,0:T(8,128)(2,1)S(1)} %fusion.16), channel_id=1, source_target_pairs={{0,1},{1,0},{2,3},{3,2},{4,5},{5,4},{6,7},{7,6},{8,9},{9,8},{10,11... | collective-permute-start | bytes 331784 | tf_op jit(solution)/shard_map/ppermute | solution.py:967
  567.9 5.9 %collective-permute-start.40 = (bf16[48,1152]{1,0:T(8,128)(2,1)S(1)}, bf16[48,1152]{1,0:T(8,128)(2,1)S(1)}, u32[]{:S(2)}, u32[]{:S(2)}) collective-permute-start(bf16[48,1152]{1,0:T(8,128)(2,1)S(1)} %fusion.15), channel_id=1, source_target_pairs={{0,1},{1,0},{2,3},{3,2},{4,5},{5,4},{6,7},{7,6},{8,9},{9,8},{10,11... | collective-permute-start | bytes 331784 | tf_op jit(solution)/shard_map/ppermute | solution.py:967
  569.0 4.8 collective-permute-start.41
  (15 other events, 43.1 us)

commit v7 on v6

--- a/solution.py
+++ b/solution.py
@@ -526,9 +526,9 @@
     )(info, *arrays)
 
 
-def enter_kernel(info_ref, own_ref, got_ref, w_ref, vec_ref, bias_ref, *refs, norm):
+def enter_kernel(info_ref, source_ref, w_ref, vec_ref, bias_ref, *refs, norm):
     x_ref, out_ref = refs[-2:]
-    x = pick(pl.program_id(0) % 2 == 0, own_ref, got_ref)
+    x = source_ref[...]
     x_ref[...] = x
     if norm:
         unit, _ = normal_parts(x.astype(jnp.float32))
@@ -542,28 +542,30 @@
         out_ref[:, part] = total.astype(jnp.bfloat16)
 
 
-def enter(info, at, previous, held, owns, gots, weight, vectors, bias, norm):
-    count, own, width = gots.shape
+def enter(info, first, count, previous, held, rows_in, weight, vectors, bias, norm):
+    own, width = rows_in.shape[1:]
     rows = 2 * held * own
     wide = weight.shape[1]
-    own_rows = pl.BlockSpec(
-        (None, own, width), lambda step, info: (info[0] * held + at + step // 2, 0, 0)
-    )
-    row = lambda step, info: (2 * at + step, 0)
+    if first is None:
+        place = lambda step, info: (info[0] * held + step, 0, 0)
+        row = lambda step, info: (2 * step, 0)
+    else:
+        place = lambda step, info: (step, 0, 0)
+        row = lambda step, info: (2 * (first + step) + 1, 0)
     return kernel_call(
         functools.partial(enter_kernel, norm=norm),
         "enter",
         info,
-        (owns, gots, weight, vectors, bias, *previous),
-        [own_rows, got_spec(own, width, 2 * count - 1)]
+        (rows_in, weight, vectors, bias, *previous),
+        [pl.BlockSpec((None, own, width), place)]
         + [resident(a) for a in (weight, vectors, bias)]
         + [pl.BlockSpec(memory_space=pl.ANY)] * len(previous),
         [like((rows, width), jnp.bfloat16), like((rows, wide), jnp.bfloat16)],
         [pl.BlockSpec((own, width), row), pl.BlockSpec((own, wide), row)],
-        2 * count,
-        4 * count * own * width * wide,
-        4 * count * own * (2 * width + wide),
-        input_output_aliases={6: 0, 7: 1} if previous else {},
+        count,
+        2 * count * own * width * wide,
+        2 * count * own * (2 * width + wide),
+        input_output_aliases={5: 0, 6: 1} if previous else {},
     )
 
 
@@ -1090,30 +1092,34 @@
     upstreams = (
         cotangent[:, 0].astype(jnp.float32) * loss_mask[:, 0].astype(jnp.float32)[..., None]
     ).astype(jnp.bfloat16)
-    target_gots, last_got = [], ()
-    for at in range(held):
-        got, last_got = swap(targets, at, 1, last_got)
-        target_gots.append(got)
-        if at:
-            target_gots[at - 1] = last_got
-        last_got = got
-    memory_gots, target_gots[-1] = swap(memory, 0, held, last_got)
-    upstream_gots, memory_gots = swap(upstreams, 0, held, memory_gots)
     kinds = lax.dynamic_slice_in_dim(row_kind[:, 0], side * held, held, axis=0)
     info = jnp.concatenate([jnp.stack([side, place % 2]).astype(jnp.int32), kinds])
 
     self_vectors = pack(norm_self_gain, norm_self_bias)
     zero = jnp.zeros_like(self_query_bias)
     joint_bias = jnp.concatenate([self_query_bias, zero, self_value_bias])[None]
-    entered, attended = (), ()
+    pair_bias = jnp.concatenate([zero, cross_value_bias])[None]
+    got, _ = swap(targets, 0, 1)
+    entered = enter(
+        info, None, held, (), held, targets, self_input, self_vectors, joint_bias, True
+    )
+    source_parts = enter(
+        info, None, held, (), held, memory, cross_input, self_vectors, pair_bias, False
+    )
+    got, entered, source_parts = lax.optimization_barrier((got, entered, source_parts))
+    attended = ()
     for at in range(held):
+        if at + 1 < held:
+            later, got = swap(targets, at + 1, 1, got)
         entered = enter(
-            info, at, entered, held, targets, target_gots[at], self_input, self_vectors,
-            joint_bias, True,
+            info, at, 1, entered, held, got, self_input, self_vectors, joint_bias, True
         )
         joint = batch(entered[1])
         attended = attend(info, at, 1, attended, joint, joint, joint, True, (0, 1, 2))
-        entered, attended = lax.optimization_barrier((entered, attended))
+        if at + 1 < held:
+            entered, attended, got = lax.optimization_barrier((entered, attended, later))
+        if at + 2 == held:
+            memory_gots, got = swap(memory, 0, held, got)
     inputs, joint = entered[0], batch(entered[1])
     self_mixed, self_raised, self_inverse = attended
     after_self, cross_queries = middle(
@@ -1125,9 +1131,12 @@
         pack(self_output_bias, norm_cross_gain, norm_cross_bias, cross_query_bias),
         own,
     )
-    pair_bias = jnp.concatenate([zero, cross_value_bias])[None]
+    cross_queries, source_parts, memory_gots = lax.optimization_barrier(
+        (cross_queries, source_parts, memory_gots)
+    )
+    upstream_gots, memory_gots = swap(upstreams, 0, held, memory_gots)
     sources, cross_pairs = enter(
-        info, 0, (), held, memory, memory_gots, cross_input, self_vectors, pair_bias, False
+        info, 0, held, source_parts, held, memory_gots, cross_input, self_vectors, pair_bias, False
     )
     cross_queries, cross_pairs = batch(cross_queries), batch(cross_pairs)
     cross_mixed, cross_raised, cross_inverse = attend(
@@ -1154,14 +1163,12 @@
     )
     exchange(feed_trees)
     result_gots = lax.ppermute(result_gots, "seq", SWAP)
-    half_grads, result_gots = settle(
-        feed_trees, (attend_back((0, 0), (held, first), (), *cross_inputs), result_gots)
-    )
+    half_grads = settle(feed_trees, attend_back((0, 0), (held, first), (), *cross_inputs))
     exchange(feed_trees)
     cross_grads = attend_back((0, first), (held, pairs - first), half_grads, *cross_inputs)
-    source_grads, source_gots, grad_self, self_upstream, return_sums, *mid_parts = settle(
+    (source_grads, source_gots, grad_self, self_upstream, return_sums, *mid_parts), back = settle(
         feed_trees,
-        return_rows(
+        (return_rows(
             info,
             [flat(rows) for rows in cross_grads],
             after_self,
@@ -1175,21 +1182,16 @@
             own,
             micros,
             parts,
-        ),
-    )
-    early_sums = Whole(
-        jnp.concatenate([feed_sums, return_sums, hidden_sums.reshape(-1, width)], axis=0)
-    )
-    mid_trees = [Tree(*mid_parts, low_first), early_sums]
+        ), result_gots),
+    )
+    results = give(results, back, 0)
+    mid_trees = [Tree(*mid_parts, low_first)]
     exchange(feed_trees + mid_trees)
     self_inputs = (
         joint, joint, joint, (0, 1, 2), self_mixed, batch(self_upstream), self_raised, self_inverse
     )
     source_gots = lax.ppermute(source_gots, "seq", SWAP)
-    grads, source_gots = settle(
-        feed_trees + mid_trees,
-        (attend_back((0, 0), (1, pairs), (), *self_inputs), source_gots),
-    )
+    grads = settle(feed_trees + mid_trees, attend_back((0, 0), (1, pairs), (), *self_inputs))
     exchange(feed_trees + mid_trees)
     kept, leave_sums = (), []
     trees = feed_trees + mid_trees
@@ -1215,9 +1217,9 @@
         if at < held - 1:
             grads, kept = lax.optimization_barrier((grads, kept))
             back = lax.ppermute(got, "seq", SWAP)
-            grads, back = settle(
+            grads, back, source_gots = settle(
                 trees,
-                (attend_back((at + 1, 0), (1, pairs), grads, *self_inputs), back),
+                (attend_back((at + 1, 0), (1, pairs), grads, *self_inputs), back, source_gots),
             )
             exchange(trees)
             back = back.astype(kept.dtype)[None]
@@ -1225,7 +1227,9 @@
                 lax.dynamic_update_slice_in_dim(kept, back, (1 - side) * held + at, axis=0),
             )
     input_grads, got, sums = settle(trees, (kept, got, sum(leave_sums)))
-    late_sums = Whole(sums)
+    late_sums = Whole(
+        jnp.concatenate([sums, feed_sums, return_sums, hidden_sums.reshape(-1, width)], axis=0)
+    )
     trees = trees + [late_sums]
     exchange(trees)
     back = lax.ppermute(got, "seq", SWAP)
@@ -1245,11 +1249,10 @@
     def widen(block):
         return jnp.concatenate([block[i : i + rows] for i in range(0, len(block), rows)], axis=1)
 
-    for index, at in ((14, 0), (15, 1), (16, 2), (20, 3), (7, 8), (8, 9), (6, 10), (10, 11), (12, 12)):
-        final[index] = mine(early_sums.total[at])
-    final[18] = mine(early_sums.total[16:].reshape(-1))
-    for index, at in ((0, 0), (1, 1), (3, 2), (4, 3)):
-        final[index] = mine(late_sums.total[at])
+    for at, index in enumerate((0, 1, 3, 4, 14, 15, 16, 20, 7, 8, 6, 10, 12)):
+        row = at if at < 4 else at + 4 if at < 8 else at + 8
+        final[index] = mine(late_sums.total[row])
+    final[18] = mine(late_sums.total[24:].reshape(-1))
     feed_total, mid_total = feed_trees[0].total, mid_trees[0].total
     final[19] = feed_total[:inner_rows]
     final[13] = feed_total[inner_rows : inner_rows + rows]
@@ -1258,7 +1261,6 @@
     final[5] = mid_total[rows : 2 * rows]
     final[11] = widen(mid_total[2 * rows :])
     final[2] = jnp.concatenate([tree.total for tree in late_trees], axis=1)
-    results = give(results, result_gots, 0)
     source_grads = give(source_grads, source_gots, 0)
     return (results[:, None], input_grads[:, None], source_grads[:, None]) + tuple(final)
 

time: 581 us -> 574 us (0.988)
  starting transfers between devices: 46.7 us -> 34.8 us
  Pallas kernels: 424 us -> 430 us
    ppermute x16, waiting for transfers between devices: 6.61 us -> 21.9 us  [exchange(): self.got = lax.ppermute(self.sent, 'dp', pairs)]
    ppermute x12 -> x6, starting transfers between devices: 15.9 us -> 6.38 us  [exchange(): lax.ppermute(self.rows, 'dp', [(i, i ^ step) for i in range(self.count)])]
    ppermute x4, waiting for transfers between devices: 7.52 us -> 0.01 us  [swap(): return (lax.ppermute(sent, 'seq', SWAP), after)]
    pallas_call x9 -> x11, Pallas kernels: 233 us -> 239 us  [kernel_call(): pl.pallas_call(kernel, grid_spec=pltpu.PrefetchScalarGridSpec(num_scalar_...]
  transfers between devices with their start and end apart: 42 -> 35, of which waited for: 9 -> 9; matrix products, arithmetic and copies ran while one was open for 9% -> 8% of each run, Pallas kernels for 55% -> 57%
where the time goes in v7:
time: 574 us; the launch traced here: 568 us
  Pallas kernels  430 us (75%)
  starting transfers between devices  34.8 us (6%)
  local copies, waits for them, and re-layouts  34.7 us (6%)
  other arithmetic  34.7 us (6%)
  waiting for transfers between devices  31.7 us (6%)
    pallas_call x11, Pallas kernels, kernel_call(): pl.pallas_call(kernel, grid_spec=pltpu.PrefetchScalarGridSpec(num_scalar_...  239 us
    pallas_call x4, Pallas kernels, attend_back(): pl.pallas_call(kernel, grid=size, in_specs=[pl.BlockSpec(memory_space=pl....  123 us
    pallas_call x3, Pallas kernels, attend(): pl.pallas_call(functools.partial(attend_kernel, use_mask=use_mask, start=...  68.5 us
    ppermute x16, waiting for transfers between devices, exchange(): self.got = lax.ppermute(self.sent, 'dp', pairs)  21.9 us
    convert_element_type x16, other arithmetic, add(): total = total.astype(jnp.bfloat16)  19.9 us
    ppermute x16, starting transfers between devices, exchange(): self.got = lax.ppermute(self.sent, 'dp', pairs)  13.7 us
  transfers between devices with their start and end apart: 35, of which 9 were waited for; matrix products, arithmetic and copies ran while one was open for 8% of the time, Pallas kernels for 57%

profile of v7, /device:TPU:0, one launch (start us, length us, event | category | flops | bytes accessed | tf_op | source)
XLA Modules:
  0.0 567.9 jit_solution(11745520883922495535)
XLA Ops:
  0.8 2.8 dynamic-slice_bitcast_fusion.4
  3.6 3.0 collective-permute-start
  6.5 2.7 dynamic-slice_bitcast_fusion.1
  11.2 1.7 copy-done.6
  12.9 1.2 constant_dynamic-slice_fusion.13
  16.9 6.6 %enter.6 = (bf16[2048,768]{1,0:T(8,128)(2,1)}, bf16[2048,1536]{1,0:T(8,128)(2,1)}) custom-call(s32[4]{0:T(128)} %pad_add_fusion.info_ref, bf16[4,512,768]{2,1,0:T(8,128)(2,1)} %bitcast.193, bf16[768,1536]{1,0:T(8,128)(2,1)} %wi_ref.3, f32[8,768]{1,0:T(8,128)} %get-tuple-element.357.vec_ref, f32[1,1536]{1,0:T(1,128)} %broadcast_in_dim.41.bias_ref), custom_call_target="tpu_custom_call" | custom-call | flops 2415919104 | bytes 6291456 | tf_op jit(solution)/shard_map/enter/pallas_call | solution.py:510
  23.5 9.3 %enter.5 = (bf16[2048,768]{1,0:T(8,128)(2,1)}, bf16[2048,2304]{1,0:T(8,128)(2,1)}) custom-call(s32[4]{0:T(128)} %pad_add_fusion.info_ref, bf16[4,512,768]{2,1,0:T(8,128)(2,1)} %bitcast.192, bf16[768,2304]{1,0:T(8,128)(2,1)} %w_ref.13, f32[8,768]{1,0:T(8,128)} %get-tuple-element.357.vec_ref, f32[1,2304]{1,0:T(1,128)} %broadcast_in_dim.40.bias_ref), custom_call_target="tpu_custom_call" | custom-call | flops 3623878656 | bytes 7864320 | tf_op jit(solution)/shard_map/enter/pallas_call | solution.py:510
  32.8 6.6 %enter.7 = (bf16[2048,768]{1,0:T(8,128)(2,1)}, bf16[2048,2304]{1,0:T(8,128)(2,1)}) custom-call(s32[4]{0:T(128)} %pad_add_fusion.info_ref, bf16[1,512,768]{2,1,0:T(8,128)(2,1)} %collective-permute-done.source_ref, bf16[768,2304]{1,0:T(8,128)(2,1)} %w_ref.13, f32[8,768]{1,0:T(8,128)} %get-tuple-element.357.vec_ref, ...), custom_call_target="tpu_custom_call", output_to_operand_aliasing={{0}: (5, {}), {1}: (6, {})} | custom-call | flops 1811939328 | bytes 3932160 | tf_op jit(solution)/shard_map/enter/pallas_call | solution.py:510
  39.5 18.9 %attend.3 = (bf16[2,1024,768]{2,1,0:T(8,128)(2,1)}, bf16[2,12,1024,1024]{3,2,1,0:T(8,128)(2,1)}, f32[2,6,2,1024]{3,2,1,0:T(2,128)}) custom-call(s32[4]{0:T(128)} %pad_add_fusion.info_ref, bf16[2,1024,2304]{2,1,0:T(8,128)(2,1)} %bitcast.159, bf16[2,1024,2304]{2,1,0:T(8,128)(2,1)} %bitcast.160, bf16[2,1024,2304]{2,1,0:T(8,128)(2,1)} %bitcast.161), custom_call_target="tpu_custom_call" | custom-call | flops 12884901888 | bytes 25165824 | tf_op jit(solution)/shard_map/attend/pallas_call | solution.py:343
  59.3 2.0 collective-permute-start.2
  61.3 6.6 %enter.8 = (bf16[2048,768]{1,0:T(8,128)(2,1)}, bf16[2048,2304]{1,0:T(8,128)(2,1)}) custom-call(s32[4]{0:T(128)} %pad_add_fusion.info_ref, bf16[1,512,768]{2,1,0:T(8,128)(2,1)} %copy-done.15, bf16[768,2304]{1,0:T(8,128)(2,1)} %w_ref.13, f32[8,768]{1,0:T(8,128)} %get-tuple-element.357.vec_ref, ...), custom_call_target="tpu_custom_call", output_to_operand_aliasing={{0}: (5, {}), {1}: (6, {})} | custom-call | flops 1811939328 | bytes 3932160 | tf_op jit(solution)/shard_map/enter/pallas_call | solution.py:510
  67.9 18.5 %attend.4 = (bf16[2,1024,768]{2,1,0:T(8,128)(2,1)}, bf16[2,12,1024,1024]{3,2,1,0:T(8,128)(2,1)}, f32[2,6,2,1024]{3,2,1,0:T(2,128)}) custom-call(s32[4]{0:T(128)} %pad_add_fusion.info_ref, bf16[2,1024,2304]{2,1,0:T(8,128)(2,1)} %bitcast.162, bf16[2,1024,2304]{2,1,0:T(8,128)(2,1)} %bitcast.163, ...), custom_call_target="tpu_custom_call", output_to_operand_aliasing={{0}: (4, {}), {1}: (5, {}), {2}: (6, {})} | custom-call | flops 12884901888 | bytes 25165824 | tf_op jit(solution)/shard_map/attend/pallas_call | solution.py:343
  86.4 12.5 %middle.1 = (f32[2048,768]{1,0:T(8,128)}, bf16[2048,768]{1,0:T(8,128)(2,1)}) custom-call(s32[4]{0:T(128)} %pad_add_fusion.info_ref, bf16[2048,768]{1,0:T(8,128)(2,1)} %get-tuple-element.184.x_ref, bf16[2048,768]{1,0:T(8,128)(2,1)} %bitcast.187, bf16[768,768]{1,0:T(8,128)(2,1)} %wo_ref.5, bf16[768,768]{1,0:T(8,128)(2,1)} %wq_ref.3, f32[8,768]{1,0:T(8,128)} %concatenate.37.vec_ref), custom_call_target="tpu_custom_call" | custom-call | flops 4831838208 | bytes 15728640 | tf_op jit(solution)/shard_map/middle/pallas_call | solution.py:510
  100.1 6.6 %enter.9 = (bf16[2048,768]{1,0:T(8,128)(2,1)}, bf16[2048,1536]{1,0:T(8,128)(2,1)}) custom-call(s32[4]{0:T(128)} %pad_add_fusion.info_ref, bf16[2,512,768]{2,1,0:T(8,128)(2,1)} %copy-done.12, bf16[768,1536]{1,0:T(8,128)(2,1)} %wi_ref.3, f32[8,768]{1,0:T(8,128)} %get-tuple-element.357.vec_ref, ...), custom_call_target="tpu_custom_call", output_to_operand_aliasing={{0}: (5, {}), {1}: (6, {})} | custom-call | flops 2415919104 | bytes 6291456 | tf_op jit(solution)/shard_map/enter/pallas_call | solution.py:510
  106.7 31.1 %attend.5 = (bf16[2,1024,768]{2,1,0:T(8,128)(2,1)}, bf16[2,12,1024,1024]{3,2,1,0:T(8,128)(2,1)}, f32[2,6,2,1024]{3,2,1,0:T(2,128)}) custom-call(s32[4]{0:T(128)} %pad_add_fusion.info_ref, bf16[2,1024,768]{2,1,0:T(8,128)(2,1)} %bitcast.203, bf16[2,1024,1536]{2,1,0:T(8,128)(2,1)} %bitcast.180, bf16[2,1024,1536]{2,1,0:T(8,128)(2,1)} %bitcast.181), custom_call_target="tpu_custom_call" | custom-call | flops 25769803776 | bytes 50331648 | tf_op jit(solution)/shard_map/attend/pallas_call | solution.py:343
  137.8 108.1 %feed.1 = (bf16[4,512,768]{2,1,0:T(8,128)(2,1)}, bf16[2,512,768]{2,1,0:T(8,128)(2,1)}, f32[2048,768]{1,0:T(8,128)}, bf16[2048,768]{1,0:T(8,128)(2,1)}, f32[8,768...) custom-call(s32[4]{0:T(128)} %pad_add_fusion.info_ref, ...), custom_call_target="tpu_custom_call" | custom-call | flops 65229815808 | bytes 62914560 | tf_op jit(solution)/shard_map/feed/pallas_call | solution.py:510
  247.6 1.4 reduce.3
  249.6 30.6 %attend_back.4 = (bf16[2,1024,768]{2,1,0:T(8,128)(2,1)}, bf16[2,1024,768]{2,1,0:T(8,128)(2,1)}, bf16[2,1024,768]{2,1,0:T(8,128)(2,1)}) custom-call(bf16[2,1024,768]{2,1,0:T(8,128)(2,1)} %bitcast.204, bf16[2,1024,1536]{2,1,0:T(8,128)(2,1)} %bitcast.182, bf16[2,1024,1536]{2,1,0:T(8,128)(2,1)} %bitcast.183, ...), custom_call_target="tpu_custom_call" | custom-call | flops 25769803776 | bytes 25165824 | tf_op jit(solution)/shard_map/attend_back/pallas_call | solution.py:419
  280.2 5.3 fusion
  285.6 2.3 copy-done.2
  287.8 1.7 dynamic-slice_bitcast_fusion
  289.5 2.0 collective-permute-start.5
  291.5 30.6 %attend_back.5 = (bf16[2,1024,768]{2,1,0:T(8,128)(2,1)}, bf16[2,1024,768]{2,1,0:T(8,128)(2,1)}, bf16[2,1024,768]{2,1,0:T(8,128)(2,1)}) custom-call(bf16[2,1024,768]{2,1,0:T(8,128)(2,1)} %get-tuple-element.213.refs_0_, bf16[2,1024,768]{2,1,0:T(8,128)(2,1)} %get-tuple-element.214.refs_1_, ...), custom_call_target="tpu_custom_call", output_to_operand_aliasing={{0}: (0, {}), {1}: (1, {}), {2}: (2, {})} | custom-call | flops 25769803776 | bytes 25165824 | tf_op jit(solution)/shard_map/attend_back/pallas_call | solution.py:419
  322.2 41.3 %return_rows.1 = (f32[4,512,768]{2,1,0:T(8,128)}, bf16[2,512,768]{2,1,0:T(8,128)(2,1)}, f32[2048,768]{1,0:T(8,128)}, bf16[2048,768]{1,0:T(8,128)(2,1)}, f32[8,76...) custom-call(s32[4]{0:T(128)} %pad_add_fusion.info_ref, bf16[2048,768]{1,0:T(8,128)(2,1)} %bitcast.211, ...), custom_call_target="tpu_custom_call" | custom-call | flops 19327352832 | bytes 41943040 | tf_op jit(solution)/shard_map/return_rows/pallas_call | solution.py:510
  363.4 3.2 fusion.2
  366.6 1.5 copy-done.3
  368.1 1.1 dynamic-slice_bitcast_fusion.2
  371.4 31.0 %attend_back.6 = (bf16[2,1024,768]{2,1,0:T(8,128)(2,1)}, bf16[2,1024,768]{2,1,0:T(8,128)(2,1)}, bf16[2,1024,768]{2,1,0:T(8,128)(2,1)}) custom-call(bf16[2,1024,2304]{2,1,0:T(8,128)(2,1)} %bitcast.165, bf16[2,1024,2304]{2,1,0:T(8,128)(2,1)} %bitcast.166, bf16[2,1024,2304]{2,1,0:T(8,128)(2,1)} %bitcast.167, ...), custom_call_target="tpu_custom_call" | custom-call | flops 25769803776 | bytes 25165824 | tf_op jit(solution)/shard_map/attend_back/pallas_call | solution.py:419
  402.5 1.2 bitcast_dynamic-update-slice_fusion
  404.8 1.7 fusion.4
  406.6 3.2 collective-permute-start.9
  409.7 2.3 fusion.3
  412.0 1.4 copy-done.5
  413.5 1.1 dynamic-slice_bitcast_fusion.3
  414.6 11.8 %leave.2 = (f32[4,512,768]{2,1,0:T(8,128)}, bf16[512,768]{1,0:T(8,128)(2,1)}, f32[8,768]{1,0:T(8,128)}) custom-call(s32[4]{0:T(128)} %pad_add_fusion.info_ref, bf16[2048,768]{1,0:T(8,128)(2,1)} %bitcast.171, bf16[2048,768]{1,0:T(8,128)(2,1)} %bitcast.174, bf16[2048,768]{1,0:T(8,128)(2,1)} %bitcast.177, bf16[2048,768]{1,0:T(8,128)(2,1)} %get-tuple-element.184.x_ref, ...), custom_call_target="tpu_custom_call" | custom-call | flops 3623878656 | bytes 16777216 | tf_op jit(solution)/shard_map/leave/pallas_call | solution.py:510
  427.4 30.7 %attend_back.7 = (bf16[2,1024,768]{2,1,0:T(8,128)(2,1)}, bf16[2,1024,768]{2,1,0:T(8,128)(2,1)}, bf16[2,1024,768]{2,1,0:T(8,128)(2,1)}) custom-call(bf16[2,1024,768]{2,1,0:T(8,128)(2,1)} %get-tuple-element.246.refs_0_, bf16[2,1024,768]{2,1,0:T(8,128)(2,1)} %get-tuple-element.247.refs_1_, ...), custom_call_target="tpu_custom_call", output_to_operand_aliasing={{0}: (0, {}), {1}: (1, {}), {2}: (2, {})} | custom-call | flops 25769803776 | bytes 25165824 | tf_op jit(solution)/shard_map/attend_back/pallas_call | solution.py:419
  458.1 1.2 fusion.8
  460.5 1.9 fusion.5
  462.4 17.4 %last_weight.1 = (bf16[8,48,1152]{2,1,0:T(8,128)(2,1)}, bf16[8,48,1152]{2,1,0:T(8,128)(2,1)}, bf16[8,48,1152]{2,1,0:T(8,128)(2,1)}, bf16[8,48,1152]{2,1,0:T(8,128)(2,1)}) custom-call(s32[4]{0:T(128)} %pad_add_fusion.info_ref, bf16[2048,768]{1,0:T(8,128)(2,1)} %bitcast.172, bf16[2048,768]{1,0:T(8,128)(2,1)} %bitcast.175, bf16[2048,768]{1,0:T(8,128)(2,1)} %bitcast.178, ...), custom_call_target="tpu_custom_call" | custom-call | flops 7247757312 | bytes 20971520 | tf_op jit(solution)/shard_map/last_weight/pallas_call | solution.py:510
  481.0 2.4 convert_dynamic-update-slice_fusion.2.refs_0_
  483.3 3.4 convert_dynamic-update-slice_fusion
  486.7 9.1 %collective-permute-done.14 = bf16[2,192,768]{2,1,0:T(8,128)(2,1)S(1)} collective-permute-done((bf16[2,192,768]{2,1,0:T(8,128)(2,1)S(1)}, bf16[2,192,768]{2,1,0:T(8,128)(2,1)S(1)}, u32[]{:S(2)}, u32[]{:S(2)}) %collective-permute-start.14) | collective-permute-done | bytes 589856 | tf_op jit(solution)/shard_map/ppermute | solution.py:967
  497.1 2.0 collective-permute-start.18
  501.6 12.0 %leave.3 = (f32[4,512,768]{2,1,0:T(8,128)}, bf16[512,768]{1,0:T(8,128)(2,1)}, f32[8,768]{1,0:T(8,128)}) custom-call(s32[4]{0:T(128)} %pad_add_fusion.info_ref, bf16[2048,768]{1,0:T(8,128)(2,1)} %bitcast.173, bf16[2048,768]{1,0:T(8,128)(2,1)} %bitcast.176, bf16[2048,768]{1,0:T(8,128)(2,1)} %bitcast.179, ...), custom_call_target="tpu_custom_call", output_to_operand_aliasing={{0}: (8, {})} | custom-call | flops 3623878656 | bytes 16777216 | tf_op jit(solution)/shard_map/leave/pallas_call | solution.py:510
  514.4 1.5 collective-permute-done.15
  515.9 1.9 collective-permute-done.19
  518.2 1.5 collective-permute-start.25
  519.7 1.1 fusion.12
  521.9 1.1 fusion.11
  523.2 1.2 fusion.10
  524.8 1.2 convert_add_fusion.8
  528.0 2.6 collective-permute-done.21
  530.5 1.3 collective-permute-done.22
  531.9 1.7 collective-permute-start.28
  533.6 1.5 collective-permute-start.29
  535.2 1.2 collective-permute-start.30
  539.0 2.4 collective-permute-start.27
  542.1 6.0 %collective-permute-done.29 = f32[28,768]{1,0:T(8,128)S(1)} collective-permute-done((f32[28,768]{1,0:T(8,128)S(1)}, f32[28,768]{1,0:T(8,128)S(1)}, u32[]{:S(2)}, u32[]{:S(2)}) %collective-permute-start.29) | collective-permute-done | bytes 86048 | tf_op jit(solution)/shard_map/ppermute | solution.py:1000
  548.1 4.4 collective-permute-done.26
  552.5 1.2 collective-permute-done.27
  553.7 1.1 collective-permute-start.32
  555.9 1.1 collective-permute-start.34
  557.0 1.3 convert_dynamic-update-slice_fusion.1
  558.3 3.7 collective-permute-done.34
  (187 shorter events, 34.0 us)
Async XLA Ops:
  0.7 13.5 %copy-start = (s32[4,1]{0,1:T(1,128)S(1)}, s32[4,1]{0,1:T(1,128)}, u32[]{:S(2)}) copy-start(s32[4,1]{0,1:T(1,128)} %param.28) | copy-start | bytes 52
  0.7 8.5 %copy-start.23 = (f32[768]{0:T(1024)S(1)}, f32[768]{0:T(1024)}, u32[]{:S(2)}) copy-start(f32[768]{0:T(1024)} %param.39) | copy-start | bytes 9220
  0.7 8.5 %copy-start.24 = (f32[768]{0:T(1024)S(1)}, f32[768]{0:T(1024)}, u32[]{:S(2)}) copy-start(f32[768]{0:T(1024)} %param.38) | copy-start | bytes 9220
  0.7 8.5 %copy-start.25 = (f32[768]{0:T(1024)S(1)}, f32[768]{0:T(1024)}, u32[]{:S(2)}) copy-start(f32[768]{0:T(1024)} %param.32) | copy-start | bytes 9220
  0.7 8.5 %copy-start.26 = (f32[768]{0:T(1024)S(1)}, f32[768]{0:T(1024)}, u32[]{:S(2)}) copy-start(f32[768]{0:T(1024)} %param.31) | copy-start | bytes 9220
  0.7 8.5 %copy-start.33 = (f32[768]{0:T(1024)S(1)}, f32[768]{0:T(1024)}, u32[]{:S(2)}) copy-start(f32[768]{0:T(1024)} %param.35) | copy-start | bytes 9220
  0.7 8.5 %copy-start.34 = (f32[768]{0:T(1024)S(1)}, f32[768]{0:T(1024)}, u32[]{:S(2)}) copy-start(f32[768]{0:T(1024)} %param.34) | copy-start | bytes 9220
  0.7 9.2 %copy-start.22 = (f32[768]{0:T(1024)S(1)}, f32[768]{0:T(1024)}, u32[]{:S(2)}) copy-start(f32[768]{0:T(1024)} %param.43) | copy-start | bytes 9220
  0.8 9.8 %copy-start.27 = (f32[768]{0:T(1024)S(1)}, f32[768]{0:T(1024)}, u32[]{:S(2)}) copy-start(f32[768]{0:T(1024)} %param.37) | copy-start | bytes 9220
  0.8 9.8 %copy-start.28 = (f32[768]{0:T(1024)S(1)}, f32[768]{0:T(1024)}, u32[]{:S(2)}) copy-start(f32[768]{0:T(1024)} %param.41) | copy-start | bytes 9220
  0.8 9.8 %copy-start.21 = (s32[4,1,512]{2,1,0:T(1,128)S(1)}, s32[4,1,512]{2,1,0:T(1,128)}, u32[]{:S(2)}) copy-start(s32[4,1,512]{2,1,0:T(1,128)} %param.29) | copy-start | bytes 24580
  0.8 9.8 %copy-start.7 = (bf16[4,1,512,768]{3,2,1,0:T(8,128)(2,1)S(1)}, bf16[4,1,512,768]{3,2,1,0:T(8,128)(2,1)}, u32[]{:S(2)}) copy-start(bf16[4,1,512,768]{3,2,1,0:T(8,128)(2,1)} %param.30) | copy-start | bytes 9437188
  3.6 29.2 %collective-permute-start = (bf16[1,512,768]{2,1,0:T(8,128)(2,1)}, bf16[1,512,768]{2,1,0:T(8,128)(2,1)}, u32[]{:S(2)}, u32[]{:S(2)}) collective-permute-start(bf16[1,512,768]{2,1,0:T(8,128)(2,1)} %get-tuple-element.332), channel_id=1, source_target_pairs={{0,1},{1,0},{2,3},{3,2},{4,5},{5,4},{6,7},{7,6},{8,9},{9,8},{10,11... | collective-permute-start | bytes 2359304 | tf_op jit(solution)/shard_map/ppermute | solution.py:1075
  11.2 1.7 copy-start.6
  23.5 9.3 %copy-start.16 = (bf16[1,512,768]{2,1,0:T(8,128)(2,1)S(1)}, bf16[1,512,768]{2,1,0:T(8,128)(2,1)}, u32[]{:S(2)}) copy-start(bf16[1,512,768]{2,1,0:T(8,128)(2,1)} %get-tuple-element.179) | copy-start | bytes 2359300
  32.8 25.6 %collective-permute-start.1 = (bf16[1,512,768]{2,1,0:T(8,128)(2,1)S(1)}, bf16[1,512,768]{2,1,0:T(8,128)(2,1)S(1)}, u32[]{:S(2)}, u32[]{:S(2)}) collective-permute-start(bf16[1,512,768]{2,1,0:T(8,128)(2,1)S(1)} %copy-done.16), channel_id=1, source_target_pairs={{0,1},{1,0},{2,3},{3,2},{4,5},{5,4},{6,7},{7,6},{8,9},{9,8},{10,11... | collective-permute-start | bytes 2359304 | tf_op jit(solution)/shard_map/ppermute | solution.py:1075
  59.3 39.7 %collective-permute-start.2 = (bf16[2,512,768]{2,1,0:T(8,128)(2,1)}, bf16[2,512,768]{2,1,0:T(8,128)(2,1)S(1)}, u32[]{:S(2)}, u32[]{:S(2)}) collective-permute-start(bf16[2,512,768]{2,1,0:T(8,128)(2,1)} %dynamic-slice_bitcast_fusion.1), channel_id=1, source_target_pairs={{0,1},{1,0},{2,3},{3,2},{4,5},{5,4},{6,7},{7,6},{8,9},{9,8},{10,11... | collective-permute-start | bytes 4718600 | tf_op jit(solution)/shard_map/ppermute | solution.py:1075
  99.0 38.8 %collective-permute-start.3 = (bf16[2,512,768]{2,1,0:T(8,128)(2,1)}, bf16[2,512,768]{2,1,0:T(8,128)(2,1)}, u32[]{:S(2)}, u32[]{:S(2)}) collective-permute-start(bf16[2,512,768]{2,1,0:T(8,128)(2,1)} %constant_dynamic-slice_fusion.13), channel_id=1, source_target_pairs={{0,1},{1,0},{2,3},{3,2},{4,5},{5,4},{6,7},{7,6},{8,9},{9,8},{10,11... | collective-permute-start | bytes 4718600 | tf_op jit(solution)/shard_map/ppermute | solution.py:1075
  245.9 34.4 %collective-permute-start.4 = (bf16[2,2,2,432,768]{4,3,2,1,0:T(8,128)(2,1)}, bf16[2,2,2,432,768]{4,3,2,1,0:T(8,128)(2,1)}, u32[]{:S(2)}, u32[]{:S(2)}) collective-permute-start(bf16[2,2,2,432,768]{4,3,2,1,0:T(8,128)(2,1)} %bitcast.197), channel_id=1, source_target_pairs={{0,2},{2,0},{4,6},{6,4},{8,10},{10,8},{12,14},{14,12},{16,18},{18,... | collective-permute-start | bytes 15925256 | tf_op jit(solution)/shard_map/ppermute | solution.py:967
  246.0 117.4 %collective-permute-start.6 = (bf16[2,512,768]{2,1,0:T(8,128)(2,1)}, bf16[2,512,768]{2,1,0:T(8,128)(2,1)S(1)}, u32[]{:S(2)}, u32[]{:S(2)}) collective-permute-start(bf16[2,512,768]{2,1,0:T(8,128)(2,1)} %get-tuple-element.228), channel_id=1, source_target_pairs={{0,1},{1,0},{2,3},{3,2},{4,5},{5,4},{6,7},{7,6},{8,9},{9,8},{10,11... | collective-permute-start | bytes 4718600 | tf_op jit(solution)/shard_map/ppermute | solution.py:1165
  285.6 2.3 copy-start.2
  289.5 73.9 %collective-permute-start.5 = (bf16[2,2,432,768]{3,2,1,0:T(8,128)(2,1)}, bf16[2,2,432,768]{3,2,1,0:T(8,128)(2,1)}, u32[]{:S(2)}, u32[]{:S(2)}) collective-permute-start(bf16[2,2,432,768]{3,2,1,0:T(8,128)(2,1)} %dynamic-slice_bitcast_fusion), channel_id=1, source_target_pairs={{0,4},{2,6},{4,0},{6,2},{8,12},{10,14},{12,8},{14,10},{16,20},{18,... | collective-permute-start | bytes 7962632 | tf_op jit(solution)/shard_map/ppermute | solution.py:967
  366.6 1.5 copy-start.3
  369.3 34.4 %collective-permute-start.7 = (bf16[2,432,768]{2,1,0:T(8,128)(2,1)}, bf16[2,432,768]{2,1,0:T(8,128)(2,1)}, u32[]{:S(2)}, u32[]{:S(2)}) collective-permute-start(bf16[2,432,768]{2,1,0:T(8,128)(2,1)} %dynamic-slice_bitcast_fusion.2), channel_id=1, source_target_pairs={{0,8},{2,10},{4,12},{6,14},{8,0},{10,2},{12,4},{14,6},{16,24},{18,... | collective-permute-start | bytes 3981320 | tf_op jit(solution)/shard_map/ppermute | solution.py:967
  370.4 33.4 %collective-permute-start.8 = (bf16[2,2,2,192,768]{4,3,2,1,0:T(8,128)(2,1)}, bf16[2,2,2,192,768]{4,3,2,1,0:T(8,128)(2,1)}, u32[]{:S(2)}, u32[]{:S(2)}) collective-permute-start(bf16[2,2,2,192,768]{4,3,2,1,0:T(8,128)(2,1)} %bitcast.30), channel_id=1, source_target_pairs={{0,2},{2,0},{4,6},{6,4},{8,10},{10,8},{12,14},{14,12},{16,18},{18,... | collective-permute-start | bytes 7077896 | tf_op jit(solution)/shard_map/ppermute | solution.py:967
  370.4 87.7 %collective-permute-start.12 = (bf16[2,512,768]{2,1,0:T(8,128)(2,1)}, bf16[2,512,768]{2,1,0:T(8,128)(2,1)}, u32[]{:S(2)}, u32[]{:S(2)}) collective-permute-start(bf16[2,512,768]{2,1,0:T(8,128)(2,1)} %get-tuple-element.253), channel_id=1, source_target_pairs={{0,1},{1,0},{2,3},{3,2},{4,5},{5,4},{6,7},{7,6},{8,9},{9,8},{10,11... | collective-permute-start | bytes 4718600 | tf_op jit(solution)/shard_map/ppermute | solution.py:1193
  402.5 2.3 copy-start.4
  403.7 6.0 %copy-start.10 = (bf16[8,192,768]{2,1,0:T(8,128)(2,1)S(1)}, bf16[8,192,768]{2,1,0:T(8,128)(2,1)}, u32[]{:S(2)}) copy-start(bf16[8,192,768]{2,1,0:T(8,128)(2,1)} %get-tuple-element.230) | copy-start | bytes 7077892
  406.6 51.5 %collective-permute-start.9 = (bf16[432,768]{1,0:T(8,128)(2,1)S(1)}, bf16[432,768]{1,0:T(8,128)(2,1)}, u32[]{:S(2)}, u32[]{:S(2)}) collective-permute-start(bf16[432,768]{1,0:T(8,128)(2,1)S(1)} %dynamic-slice_bitcast_fusion.6), channel_id=1, source_target_pairs={{0,16},{2,18},{4,20},{6,22},{8,24},{10,26},{12,28},{14,30},{16,0},... | collective-permute-start | bytes 1990664 | tf_op jit(solution)/shard_map/ppermute | solution.py:967
  414.5 43.6 %collective-permute-start.10 = (bf16[2,2,192,768]{3,2,1,0:T(8,128)(2,1)}, bf16[2,2,192,768]{3,2,1,0:T(8,128)(2,1)}, u32[]{:S(2)}, u32[]{:S(2)}) collective-permute-start(bf16[2,2,192,768]{3,2,1,0:T(8,128)(2,1)} %dynamic-slice_bitcast_fusion.3), channel_id=1, source_target_pairs={{0,4},{2,6},{4,0},{6,2},{8,12},{10,14},{12,8},{14,10},{16,20},{18,... | collective-permute-start | bytes 3538952 | tf_op jit(solution)/shard_map/ppermute | solution.py:967
  426.4 31.7 %collective-permute-start.11 = (bf16[512,768]{1,0:T(8,128)(2,1)}, bf16[512,768]{1,0:T(8,128)(2,1)}, u32[]{:S(2)}, u32[]{:S(2)}) collective-permute-start(bf16[512,768]{1,0:T(8,128)(2,1)} %get-tuple-element.252), channel_id=1, source_target_pairs={{0,1},{1,0},{2,3},{3,2},{4,5},{5,4},{6,7},{7,6},{8,9},{9,8},{10,11... | collective-permute-start | bytes 2359304 | tf_op jit(solution)/shard_map/ppermute | solution.py:1219
  459.4 20.4 %copy-start.8 = (bf16[432,768]{1,0:T(8,128)(2,1)}, bf16[432,768]{1,0:T(8,128)(2,1)S(1)}, u32[]{:S(2)}) copy-start(bf16[432,768]{1,0:T(8,128)(2,1)S(1)} %fusion.8) | copy-start | bytes 1990660
  459.4 36.4 %collective-permute-start.13 = (bf16[432,768]{1,0:T(8,128)(2,1)S(1)}, bf16[432,768]{1,0:T(8,128)(2,1)}, u32[]{:S(2)}, u32[]{:S(2)}) collective-permute-start(bf16[432,768]{1,0:T(8,128)(2,1)S(1)} %fusion.8), channel_id=1, source_target_pairs={{0,1},{1,0},{2,3},{3,2},{4,5},{5,4},{6,7},{7,6},{8,9},{9,8},{10,11... | collective-permute-start | bytes 1990664 | tf_op jit(solution)/shard_map/ppermute | solution.py:969
  479.8 16.2 %collective-permute-start.16 = (bf16[2,2,2,48,1152]{4,3,2,1,0:T(8,128)(2,1)}, bf16[2,2,2,48,1152]{4,3,2,1,0:T(8,128)(2,1)S(1)}, u32[]{:S(2)}, u32[]{:S(2)}) collective-permute-start(bf16[2,2,2,48,1152]{4,3,2,1,0:T(8,128)(2,1)} %bitcast.201), channel_id=1, source_target_pairs={{0,2},{2,0},{4,6},{6,4},{8,10},{10,8},{12,14},{14,12},{16,18},{18,... | collective-permute-start | bytes 2654216 | tf_op jit(solution)/shard_map/ppermute | solution.py:967
  479.9 16.1 %collective-permute-start.17 = (bf16[2,2,2,48,1152]{4,3,2,1,0:T(8,128)(2,1)}, bf16[2,2,2,48,1152]{4,3,2,1,0:T(8,128)(2,1)S(1)}, u32[]{:S(2)}, u32[]{:S(2)}) collective-permute-start(bf16[2,2,2,48,1152]{4,3,2,1,0:T(8,128)(2,1)} %bitcast.200), channel_id=1, source_target_pairs={{0,2},{2,0},{4,6},{6,4},{8,10},{10,8},{12,14},{14,12},{16,18},{18,... | collective-permute-start | bytes 2654216 | tf_op jit(solution)/shard_map/ppermute | solution.py:967
  480.5 15.4 %collective-permute-start.14 = (bf16[2,192,768]{2,1,0:T(8,128)(2,1)S(1)}, bf16[2,192,768]{2,1,0:T(8,128)(2,1)S(1)}, u32[]{:S(2)}, u32[]{:S(2)}) collective-permute-start(bf16[2,192,768]{2,1,0:T(8,128)(2,1)S(1)} %dynamic-slice_bitcast_fusion.7), channel_id=1, source_target_pairs={{0,8},{2,10},{4,12},{6,14},{8,0},{10,2},{12,4},{14,6},{16,24},{18,... | collective-permute-start | bytes 1769480 | tf_op jit(solution)/shard_map/ppermute | solution.py:967
  483.3 12.7 %copy-start.14 = (bf16[8,48,1152]{2,1,0:T(8,128)(2,1)S(1)}, bf16[8,48,1152]{2,1,0:T(8,128)(2,1)}, u32[]{:S(2)}) copy-start(bf16[8,48,1152]{2,1,0:T(8,128)(2,1)} %get-tuple-element.259) | copy-start | bytes 2654212
  486.7 12.3 %copy-start.13 = (bf16[8,48,1152]{2,1,0:T(8,128)(2,1)S(1)}, bf16[8,48,1152]{2,1,0:T(8,128)(2,1)}, u32[]{:S(2)}) copy-start(bf16[8,48,1152]{2,1,0:T(8,128)(2,1)} %get-tuple-element.270) | copy-start | bytes 2654212
  496.0 4.4 copy-start.11
  497.1 18.8 %collective-permute-start.18 = (bf16[2,2,48,1152]{3,2,1,0:T(8,128)(2,1)}, bf16[2,2,48,1152]{3,2,1,0:T(8,128)(2,1)}, u32[]{:S(2)}, u32[]{:S(2)}) collective-permute-start(bf16[2,2,48,1152]{3,2,1,0:T(8,128)(2,1)} %dynamic-slice_bitcast_fusion.9), channel_id=1, source_target_pairs={{0,4},{2,6},{4,0},{6,2},{8,12},{10,14},{12,8},{14,10},{16,20},{18,... | collective-permute-start | bytes 1327112 | tf_op jit(solution)/shard_map/ppermute | solution.py:967
  500.1 17.7 %collective-permute-start.19 = (bf16[2,2,48,1152]{3,2,1,0:T(8,128)(2,1)}, bf16[2,2,48,1152]{3,2,1,0:T(8,128)(2,1)}, u32[]{:S(2)}, u32[]{:S(2)}) collective-permute-start(bf16[2,2,48,1152]{3,2,1,0:T(8,128)(2,1)} %dynamic-slice_bitcast_fusion.8), channel_id=1, source_target_pairs={{0,8},{2,10},{4,12},{6,14},{8,0},{10,2},{12,4},{14,6},{16,24},{18,... | collective-permute-start | bytes 1327112 | tf_op jit(solution)/shard_map/ppermute | solution.py:967
  501.1 14.8 %collective-permute-start.15 = (bf16[192,768]{1,0:T(8,128)(2,1)}, bf16[192,768]{1,0:T(8,128)(2,1)}, u32[]{:S(2)}, u32[]{:S(2)}) collective-permute-start(bf16[192,768]{1,0:T(8,128)(2,1)} %dynamic-slice_bitcast_fusion.10), channel_id=1, source_target_pairs={{0,16},{2,18},{4,20},{6,22},{8,24},{10,26},{12,28},{14,30},{16,0},... | collective-permute-start | bytes 884744 | tf_op jit(solution)/shard_map/ppermute | solution.py:967
  501.6 12.0 %copy-start.20 = (f32[8,768]{1,0:T(8,128)S(1)}, f32[8,768]{1,0:T(8,128)}, u32[]{:S(2)}) copy-start(f32[8,768]{1,0:T(8,128)} %get-tuple-element.279) | copy-start | bytes 73732
  501.6 16.2 %copy-start.18 = (f32[8,768]{1,0:T(8,128)S(1)}, f32[8,768]{1,0:T(8,128)}, u32[]{:S(2)}) copy-start(f32[8,768]{1,0:T(8,128)} %get-tuple-element.286) | copy-start | bytes 73732
  501.6 16.2 %copy-start.19 = (f32[8,768]{1,0:T(8,128)S(1)}, f32[8,768]{1,0:T(8,128)}, u32[]{:S(2)}) copy-start(f32[8,768]{1,0:T(8,128)} %get-tuple-element.287) | copy-start | bytes 73732
  501.6 16.2 %copy-start.17 = (f32[4,768]{1,0:T(4,128)S(1)}, f32[4,768]{1,0:T(4,128)}, u32[]{:S(2)}) copy-start(f32[4,768]{1,0:T(4,128)} %reshape.223) | copy-start | bytes 36868
  513.6 11.3 %copy-start.9 = (bf16[432,768]{1,0:T(8,128)(2,1)S(1)}, bf16[432,768]{1,0:T(8,128)(2,1)}, u32[]{:S(2)}) copy-start(bf16[432,768]{1,0:T(8,128)(2,1)} %copy-done.8) | copy-start | bytes 1990660
  517.8 6.6 %collective-permute-start.23 = (f32[28,768]{1,0:T(8,128)S(1)}, f32[28,768]{1,0:T(8,128)S(1)}, u32[]{:S(2)}, u32[]{:S(2)}) collective-permute-start(f32[28,768]{1,0:T(8,128)S(1)} %constant_dynamic-update-slice_fusion), channel_id=1, source_target_pairs={{0,2},{2,0},{4,6},{6,4},{8,10},{10,8},{12,14},{14,12},{16,18},{18,... | collective-permute-start | bytes 258056 | tf_op jit(solution)/shard_map/ppermute | solution.py:1000
  517.9 9.0 %collective-permute-start.24 = (f32[28,768]{1,0:T(8,128)S(1)}, f32[28,768]{1,0:T(8,128)S(1)}, u32[]{:S(2)}, u32[]{:S(2)}) collective-permute-start(f32[28,768]{1,0:T(8,128)S(1)} %constant_dynamic-update-slice_fusion), channel_id=1, source_target_pairs={{0,4},{2,6},{4,0},{6,2},{8,12},{10,14},{12,8},{14,10},{16,20},{18,... | collective-permute-start | bytes 258056 | tf_op jit(solution)/shard_map/ppermute | solution.py:1000
  518.2 9.7 %collective-permute-start.25 = (f32[28,768]{1,0:T(8,128)S(1)}, f32[28,768]{1,0:T(8,128)S(1)}, u32[]{:S(2)}, u32[]{:S(2)}) collective-permute-start(f32[28,768]{1,0:T(8,128)S(1)} %constant_dynamic-update-slice_fusion), channel_id=1, source_target_pairs={{0,6},{2,4},{4,2},{6,0},{8,14},{10,12},{12,10},{14,8},{16,22},{18,... | collective-permute-start | bytes 258056 | tf_op jit(solution)/shard_map/ppermute | solution.py:1000
  520.9 11.0 %collective-permute-start.20 = (bf16[192,768]{1,0:T(8,128)(2,1)S(1)}, bf16[192,768]{1,0:T(8,128)(2,1)S(1)}, u32[]{:S(2)}, u32[]{:S(2)}) collective-permute-start(bf16[192,768]{1,0:T(8,128)(2,1)S(1)} %fusion.12), channel_id=1, source_target_pairs={{0,1},{1,0},{2,3},{3,2},{4,5},{5,4},{6,7},{7,6},{8,9},{9,8},{10,11... | collective-permute-start | bytes 884744 | tf_op jit(solution)/shard_map/ppermute | solution.py:969
  523.0 3.9 copy-start.35
  523.1 7.5 %collective-permute-start.21 = (bf16[2,48,1152]{2,1,0:T(8,128)(2,1)S(1)}, bf16[2,48,1152]{2,1,0:T(8,128)(2,1)S(1)}, u32[]{:S(2)}, u32[]{:S(2)}) collective-permute-start(bf16[2,48,1152]{2,1,0:T(8,128)(2,1)S(1)} %dynamic-slice_bitcast_fusion.12), channel_id=1, source_target_pairs={{0,8},{2,10},{4,12},{6,14},{8,0},{10,2},{12,4},{14,6},{16,24},{18,... | collective-permute-start | bytes 663560 | tf_op jit(solution)/shard_map/ppermute | solution.py:967
  524.5 7.4 %collective-permute-start.22 = (bf16[2,48,1152]{2,1,0:T(8,128)(2,1)S(1)}, bf16[2,48,1152]{2,1,0:T(8,128)(2,1)S(1)}, u32[]{:S(2)}, u32[]{:S(2)}) collective-permute-start(bf16[2,48,1152]{2,1,0:T(8,128)(2,1)S(1)} %dynamic-slice_bitcast_fusion.11), channel_id=1, source_target_pairs={{0,4},{2,6},{4,0},{6,2},{8,12},{10,14},{12,8},{14,10},{16,20},{18,... | collective-permute-start | bytes 663560 | tf_op jit(solution)/shard_map/ppermute | solution.py:967
  526.9 26.7 %collective-permute-start.31 = (bf16[512,768]{1,0:T(8,128)(2,1)S(1)}, bf16[512,768]{1,0:T(8,128)(2,1)S(1)}, u32[]{:S(2)}, u32[]{:S(2)}) collective-permute-start(bf16[512,768]{1,0:T(8,128)(2,1)S(1)} %copy-done.35), channel_id=1, source_target_pairs={{0,1},{1,0},{2,3},{3,2},{4,5},{5,4},{6,7},{7,6},{8,9},{9,8},{10,11... | collective-permute-start | bytes 2359304 | tf_op jit(solution)/shard_map/ppermute | solution.py:1235
  531.9 7.1 %collective-permute-start.28 = (f32[28,768]{1,0:T(8,128)S(1)}, f32[28,768]{1,0:T(8,128)S(1)}, u32[]{:S(2)}, u32[]{:S(2)}) collective-permute-start(f32[28,768]{1,0:T(8,128)S(1)} %add_add_fusion.1), channel_id=1, source_target_pairs={{0,8},{2,10},{4,12},{6,14},{8,0},{10,2},{12,4},{14,6},{16,24},{18,... | collective-permute-start | bytes 258056 | tf_op jit(solution)/shard_map/ppermute | solution.py:1000
  533.6 14.5 %collective-permute-start.29 = (f32[28,768]{1,0:T(8,128)S(1)}, f32[28,768]{1,0:T(8,128)S(1)}, u32[]{:S(2)}, u32[]{:S(2)}) collective-permute-start(f32[28,768]{1,0:T(8,128)S(1)} %add_add_fusion.1), channel_id=1, source_target_pairs={{0,16},{2,18},{4,20},{6,22},{8,24},{10,26},{12,28},{14,30},{16,0},... | collective-permute-start | bytes 258056 | tf_op jit(solution)/shard_map/ppermute | solution.py:1000
  535.2 12.9 %collective-permute-start.30 = (f32[28,768]{1,0:T(8,128)S(1)}, f32[28,768]{1,0:T(8,128)S(1)}, u32[]{:S(2)}, u32[]{:S(2)}) collective-permute-start(f32[28,768]{1,0:T(8,128)S(1)} %add_add_fusion.1), channel_id=1, source_target_pairs={{0,24},{2,26},{4,28},{6,30},{8,16},{10,18},{12,20},{14,22},{16,8},... | collective-permute-start | bytes 258056 | tf_op jit(solution)/shard_map/ppermute | solution.py:1000
  536.5 16.0 %collective-permute-start.26 = (bf16[48,1152]{1,0:T(8,128)(2,1)S(1)}, bf16[48,1152]{1,0:T(8,128)(2,1)S(1)}, u32[]{:S(2)}, u32[]{:S(2)}) collective-permute-start(bf16[48,1152]{1,0:T(8,128)(2,1)S(1)} %dynamic-slice_bitcast_fusion.14), channel_id=1, source_target_pairs={{0,16},{2,18},{4,20},{6,22},{8,24},{10,26},{12,28},{14,30},{16,0},... | collective-permute-start | bytes 331784 | tf_op jit(solution)/shard_map/ppermute | solution.py:967
  539.0 14.7 %collective-permute-start.27 = (bf16[48,1152]{1,0:T(8,128)(2,1)S(1)}, bf16[48,1152]{1,0:T(8,128)(2,1)S(1)}, u32[]{:S(2)}, u32[]{:S(2)}) collective-permute-start(bf16[48,1152]{1,0:T(8,128)(2,1)S(1)} %dynamic-slice_bitcast_fusion.13), channel_id=1, source_target_pairs={{0,16},{2,18},{4,20},{6,22},{8,24},{10,26},{12,28},{14,30},{16,0},... | collective-permute-start | bytes 331784 | tf_op jit(solution)/shard_map/ppermute | solution.py:967
  541.3 26.4 %copy-start.1 = (s32[4,1]{0,1:T(1,128)S(1)}, s32[4,1]{0,1:T(1,128)}, u32[]{:S(2)}) copy-start(s32[4,1]{0,1:T(1,128)} %param.28) | copy-start | bytes 52
  553.7 8.3 %collective-permute-start.32 = (bf16[48,1152]{1,0:T(8,128)(2,1)S(1)}, bf16[48,1152]{1,0:T(8,128)(2,1)S(1)}, u32[]{:S(2)}, u32[]{:S(2)}) collective-permute-start(bf16[48,1152]{1,0:T(8,128)(2,1)S(1)} %fusion.16), channel_id=1, source_target_pairs={{0,1},{1,0},{2,3},{3,2},{4,5},{5,4},{6,7},{7,6},{8,9},{9,8},{10,11... | collective-permute-start | bytes 331784 | tf_op jit(solution)/shard_map/ppermute | solution.py:969
  554.9 7.2 %collective-permute-start.33 = (bf16[48,1152]{1,0:T(8,128)(2,1)S(1)}, bf16[48,1152]{1,0:T(8,128)(2,1)S(1)}, u32[]{:S(2)}, u32[]{:S(2)}) collective-permute-start(bf16[48,1152]{1,0:T(8,128)(2,1)S(1)} %fusion.15), channel_id=1, source_target_pairs={{0,1},{1,0},{2,3},{3,2},{4,5},{5,4},{6,7},{7,6},{8,9},{9,8},{10,11... | collective-permute-start | bytes 331784 | tf_op jit(solution)/shard_map/ppermute | solution.py:969
  555.9 6.1 %collective-permute-start.34 = (f32[28,768]{1,0:T(8,128)S(1)}, f32[28,768]{1,0:T(8,128)S(1)}, u32[]{:S(2)}, u32[]{:S(2)}) collective-permute-start(f32[28,768]{1,0:T(8,128)S(1)} %add_add_fusion), channel_id=1, source_target_pairs={{0,1},{1,0},{2,3},{3,2},{4,5},{5,4},{6,7},{7,6},{8,9},{9,8},{10,11... | collective-permute-start | bytes 258056 | tf_op jit(solution)/shard_map/ppermute | solution.py:1004
  (7 other events, 8.5 us)

commit v8 on v7

--- a/solution.py
+++ b/solution.py
@@ -986,33 +986,6 @@
         self.sent = lax.dynamic_index_in_dim(total, 1 - mine, 0, keepdims=False)
 
 
-class Whole:
-    def __init__(self, rows):
-        self.count = lax.axis_size("dp")
-        self.rows, self.bit, self.got, self.total = rows, 1, None, None
-
-    def exchange(self):
-        if self.total is not None or self.got is not None:
-            return
-        if self.bit < self.count:
-            steps = [step * self.bit for step in (1, 2, 3) if step * self.bit < self.count]
-            self.got = [
-                lax.ppermute(self.rows, "dp", [(i, i ^ step) for i in range(self.count)])
-                for step in steps
-            ]
-        else:
-            self.got = [lax.ppermute(self.rows, "seq", SWAP)]
-
-    def add(self):
-        if self.got is None:
-            return
-        self.rows = sum(self.got, self.rows)
-        self.got = None
-        if self.bit >= self.count:
-            self.total = self.rows
-        self.bit *= 4
-
-
 def exchange(trees):
     for tree in trees:
         tree.exchange()
@@ -1027,10 +1000,155 @@
     return values
 
 
+def receive(trees, values):
+    gots, values = lax.optimization_barrier(([tree.got for tree in trees], values))
+    for tree, got in zip(trees, gots):
+        tree.got = got
+    return values
+
+
 def finish(trees):
     while any(tree.total is None for tree in trees):
         exchange(trees)
         settle(trees, ())
+
+
+MESH = pl.DeviceIdType.MESH
+
+
+def partner(place, offset):
+    bit = 1
+    while bit <= offset:
+        if offset & bit:
+            place = place + bit * (1 - 2 * ((place // bit) % 2))
+        bit *= 2
+    return place
+
+
+def tail_kernel(*refs, orders, groups):
+    trees = len(orders)
+    ins, refs = refs[: 2 * trees + 2], refs[2 * trees + 2 :]
+    outs, refs = refs[: trees + 2], refs[trees + 2 :]
+    send_sems, recv_sems = refs[-2:]
+    scratch = list(refs[:-2])
+    place = lax.axis_index("dp")
+    side = lax.axis_index("seq")
+    offsets = sorted({bit for order in orders for bit in order} | {o for g in groups for o in g})
+    peers = [{"dp": partner(place, offset)} for offset in offsets] + [{"seq": 1 - side}]
+    barrier = pltpu.get_barrier_semaphore()
+    for peer in peers:
+        pl.semaphore_signal(barrier, inc=1, device_id=peer, device_id_type=MESH)
+    pl.semaphore_wait(barrier, len(peers))
+    used = []
+
+    def send(source, target, peer):
+        at = len(used)
+        copy = pltpu.make_async_remote_copy(
+            src_ref=source,
+            dst_ref=target,
+            send_sem=send_sems.at[at],
+            recv_sem=recv_sems.at[at],
+            device_id=peer,
+            device_id_type=MESH,
+        )
+        used.append(copy)
+        copy.start()
+        return copy
+
+    other = {"seq": 1 - side}
+    rows_copy = send(ins[-1], outs[-1], other)
+    totals = []
+    for at in range(trees):
+        total = scratch.pop(0)
+        total[...] = (
+            ins[2 * at][...].astype(jnp.float32) + ins[2 * at + 1][...].astype(jnp.float32)
+        ).astype(jnp.bfloat16)
+        totals.append(total)
+    sums = scratch.pop(0)
+    sums[...] = ins[2 * trees][...]
+    rounds = max(max(len(order) for order in orders) + 1, len(groups) + 1)
+    for step in range(rounds):
+        copies = []
+        for at, order in enumerate(orders):
+            if step < len(order):
+                mine = (place // order[step]) % 2
+                got = scratch.pop(0)
+                peer = {"dp": partner(place, order[step])}
+                copy = send(totals[at].at[1 - mine], got, peer)
+                copies.append((copy, at, mine, got, scratch.pop(0)))
+            elif step == len(order):
+                got = scratch.pop(0)
+                copies.append((send(totals[at], got, other), at, None, got, outs[at]))
+        summed = []
+        if step < len(groups):
+            for offset in groups[step]:
+                got = scratch.pop(0)
+                summed.append((send(sums, got, {"dp": partner(place, offset)}), got))
+        elif step == len(groups):
+            got = scratch.pop(0)
+            summed.append((send(sums, got, other), got))
+        for copy, at, mine, got, target in copies:
+            copy.wait()
+            held = totals[at][...] if mine is None else totals[at][mine]
+            total = held.astype(jnp.float32) + got[...].astype(jnp.float32)
+            target[...] = total.astype(target.dtype)
+            totals[at] = target
+        if summed:
+            target = scratch.pop(0) if step < len(groups) else outs[trees]
+            total = sums[...]
+            for copy, got in summed:
+                copy.wait()
+                total = total + got[...]
+            target[...] = total
+            sums = target
+    rows_copy.wait()
+
+
+def tail(trees, sums, rows, parts):
+    orders = [tuple(tree.order) for tree in trees]
+    groups, bit = [], 1
+    while bit < parts:
+        groups.append(tuple(step * bit for step in (1, 2, 3) if step * bit < parts))
+        bit *= 4
+    arrays = []
+    for tree in trees:
+        arrays += [tree.kept, tree.got]
+    arrays += [sums, rows]
+    totals = [pltpu.VMEM(tree.kept.shape, jnp.bfloat16) for tree in trees]
+    scratch = totals + [pltpu.VMEM(sums.shape, jnp.float32)]
+    shapes = [tree.kept.shape for tree in trees]
+    copies = 1
+    for step in range(max(max(len(order) for order in orders) + 1, len(groups) + 1)):
+        for at, order in enumerate(orders):
+            if step < len(order):
+                shapes[at] = shapes[at][1:]
+                scratch += [pltpu.VMEM(shapes[at], jnp.bfloat16)] * 2
+                copies += 1
+            elif step == len(order):
+                scratch += [pltpu.VMEM(shapes[at], jnp.bfloat16)]
+                copies += 1
+        if step < len(groups):
+            scratch += [pltpu.VMEM(sums.shape, jnp.float32)] * (len(groups[step]) + 1)
+            copies += len(groups[step])
+        elif step == len(groups):
+            scratch += [pltpu.VMEM(sums.shape, jnp.float32)]
+            copies += 1
+    outs = [like(shape) for shape in shapes] + [like(sums.shape), like(rows.shape, rows.dtype)]
+    vmem = pl.BlockSpec(memory_space=pltpu.VMEM)
+    return pl.pallas_call(
+        functools.partial(tail_kernel, orders=orders, groups=groups),
+        in_specs=[vmem] * len(arrays),
+        out_specs=[vmem] * len(outs),
+        out_shape=outs,
+        scratch_shapes=scratch + [pltpu.SemaphoreType.DMA((copies,))] * 2,
+        compiler_params=pltpu.CompilerParams(
+            collective_id=0, has_side_effects=True, vmem_limit_bytes=LIMIT
+        ),
+        cost_estimate=pl.CostEstimate(
+            flops=2 * 10**10, bytes_accessed=10**7, transcendentals=0
+        ),
+        name="tail",
+    )(*arrays)
 
 
 def whole_sequences(
@@ -1204,11 +1322,10 @@
                 Tree(*late_parts[0:2], low_first),
                 Tree(*late_parts[2:4], second_first),
             ]
-            grads = settle(trees, lax.optimization_barrier((grads, late_parts[0]))[0])
-            trees = trees + late_trees
-            exchange(trees)
+            exchange(late_trees)
+            grads, _ = lax.optimization_barrier((grads, late_parts[0]))
             grads = settle(late_trees, grads)
-            exchange(trees)
+            exchange(late_trees)
         kept, got, sums = leave(
             info, at, kept, [flat(rows) for rows in grads], inputs, grad_self,
             self_input, self_vectors, own, micros,
@@ -1226,19 +1343,13 @@
             kept = (
                 lax.dynamic_update_slice_in_dim(kept, back, (1 - side) * held + at, axis=0),
             )
-    input_grads, got, sums = settle(trees, (kept, got, sum(leave_sums)))
-    late_sums = Whole(
-        jnp.concatenate([sums, feed_sums, return_sums, hidden_sums.reshape(-1, width)], axis=0)
-    )
-    trees = trees + [late_sums]
-    exchange(trees)
-    back = lax.ppermute(got, "seq", SWAP)
-    settle(trees, ())
-    exchange(trees)
-    back = settle(trees, back)
-    exchange(trees)
+    input_grads, got, sums = settle(
+        feed_trees, receive(mid_trees + late_trees, (kept, got, sum(leave_sums)))
+    )
+    finish(feed_trees)
+    sums = jnp.concatenate([sums, feed_sums, return_sums, hidden_sums.reshape(-1, width)], axis=0)
+    mid_total, *late_totals, sums, back = tail(mid_trees + late_trees, sums, got, parts)
     input_grads = give(input_grads, back[None], held - 1)
-    finish(trees)
     rows = width // parts
     inner_rows = feed_in.shape[1] // parts
     final = [None] * 21
@@ -1251,16 +1362,16 @@
 
     for at, index in enumerate((0, 1, 3, 4, 14, 15, 16, 20, 7, 8, 6, 10, 12)):
         row = at if at < 4 else at + 4 if at < 8 else at + 8
-        final[index] = mine(late_sums.total[row])
-    final[18] = mine(late_sums.total[24:].reshape(-1))
-    feed_total, mid_total = feed_trees[0].total, mid_trees[0].total
+        final[index] = mine(sums[row])
+    final[18] = mine(sums[24:].reshape(-1))
+    feed_total = feed_trees[0].total
     final[19] = feed_total[:inner_rows]
     final[13] = feed_total[inner_rows : inner_rows + rows]
     final[17] = widen(feed_total[inner_rows + rows :])
     final[9] = mid_total[:rows]
     final[5] = mid_total[rows : 2 * rows]
     final[11] = widen(mid_total[2 * rows :])
-    final[2] = jnp.concatenate([tree.total for tree in late_trees], axis=1)
+    final[2] = jnp.concatenate(late_totals, axis=1)
     source_grads = give(source_grads, source_gots, 0)
     return (results[:, None], input_grads[:, None], source_grads[:, None]) + tuple(final)
 
@@ -1325,7 +1436,7 @@
         micros = arguments[0].shape[0]
         rows = lax.axis_size("dp")
         pairs = lax.axis_size("seq") == 2 and micros % 2 == 0
-        whole = pairs and rows & (rows - 1) == 0
+        whole = pairs and rows == 16
         return (whole_sequences if whole else split_sequences)(*arguments)
 
     return jax.shard_map(

time: 574 us -> 574 us (level)
  Pallas kernels: 430 us -> 475 us
  waiting for transfers between devices: 31.7 us -> 0.16 us
  starting transfers between devices: 34.8 us -> 19.8 us
  local copies, waits for them, and re-layouts: 34.7 us -> 41.1 us
    pallas_call x0 -> x1, Pallas kernels: none -> 44.6 us  [tail(): pl.pallas_call(functools.partial(tail_kernel, orders=orders, groups=group...]
    ppermute x16 -> x11, waiting for transfers between devices: 21.9 us -> 0.14 us  [exchange(): self.got = lax.ppermute(self.sent, 'dp', pairs)]
    ppermute x7 -> x0, waiting for transfers between devices: 9.77 us -> none  [the longest x6 6.05 us: exchange(): lax.ppermute(self.rows, 'dp', [(i, i ^ step) for i in range(self.count)])]
    ppermute x7 -> x0, starting transfers between devices: 7.52 us -> none  [the longest x6 6.38 us: exchange(): lax.ppermute(self.rows, 'dp', [(i, i ^ step) for i in range(self.count)])]
    convert_element_type x16 -> x7, other arithmetic: 19.9 us -> 16.1 us  [add(): total = total.astype(jnp.bfloat16)]
    ppermute x16 -> x11, starting transfers between devices: 13.7 us -> 10.4 us  [exchange(): self.got = lax.ppermute(self.sent, 'dp', pairs)]
  transfers between devices with their start and end apart: 35 -> 19, of which waited for: 9 -> 1; matrix products, arithmetic and copies ran while one was open for 8% -> 7% of each run, Pallas kernels for 57% -> 54%
where the time goes in v8:
time: 574 us; the launch traced here: 568 us
  Pallas kernels  475 us (83%)
  local copies, waits for them, and re-layouts  41.1 us (7%)
  other arithmetic  30.2 us (5%)
  starting transfers between devices  19.8 us (3%)
    pallas_call x11, Pallas kernels, kernel_call(): pl.pallas_call(kernel, grid_spec=pltpu.PrefetchScalarGridSpec(num_scalar_...  239 us
    pallas_call x4, Pallas kernels, attend_back(): pl.pallas_call(kernel, grid=size, in_specs=[pl.BlockSpec(memory_space=pl....  123 us
    pallas_call x3, Pallas kernels, attend(): pl.pallas_call(functools.partial(attend_kernel, use_mask=use_mask, start=...  68.4 us
    pallas_call x1, Pallas kernels, tail(): pl.pallas_call(functools.partial(tail_kernel, orders=orders, groups=group...  44.6 us
    convert_element_type x7, other arithmetic, add(): total = total.astype(jnp.bfloat16)  16.1 us
  transfers between devices with their start and end apart: 19, of which 1 were waited for; matrix products, arithmetic and copies ran while one was open for 7% of the time, Pallas kernels for 54%

profile of v8, /device:TPU:0, one launch (start us, length us, event | category | flops | bytes accessed | tf_op | source)
XLA Modules:
  0.0 567.6 jit_solution(4293145916436498369)
XLA Ops:
  0.8 2.8 dynamic-slice_bitcast_fusion.4
  3.6 3.0 collective-permute-start
  6.5 2.7 dynamic-slice_bitcast_fusion.1
  11.2 1.7 copy-done.6
  12.9 1.3 constant_dynamic-slice_fusion.13
  16.9 6.6 %enter.6 = (bf16[2048,768]{1,0:T(8,128)(2,1)}, bf16[2048,1536]{1,0:T(8,128)(2,1)}) custom-call(s32[4]{0:T(128)} %pad_add_fusion.info_ref, bf16[4,512,768]{2,1,0:T(8,128)(2,1)} %bitcast.165, bf16[768,1536]{1,0:T(8,128)(2,1)} %wi_ref.3, f32[8,768]{1,0:T(8,128)} %get-tuple-element.341.vec_ref, f32[1,1536]{1,0:T(1,128)} %broadcast_in_dim.41.bias_ref), custom_call_target="tpu_custom_call" | custom-call | flops 2415919104 | bytes 6291456 | tf_op jit(solution)/shard_map/enter/pallas_call | solution.py:510
  23.5 9.3 %enter.5 = (bf16[2048,768]{1,0:T(8,128)(2,1)}, bf16[2048,2304]{1,0:T(8,128)(2,1)}) custom-call(s32[4]{0:T(128)} %pad_add_fusion.info_ref, bf16[4,512,768]{2,1,0:T(8,128)(2,1)} %bitcast.164, bf16[768,2304]{1,0:T(8,128)(2,1)} %w_ref.13, f32[8,768]{1,0:T(8,128)} %get-tuple-element.341.vec_ref, f32[1,2304]{1,0:T(1,128)} %broadcast_in_dim.40.bias_ref), custom_call_target="tpu_custom_call" | custom-call | flops 3623878656 | bytes 7864320 | tf_op jit(solution)/shard_map/enter/pallas_call | solution.py:510
  32.9 6.6 %enter.7 = (bf16[2048,768]{1,0:T(8,128)(2,1)}, bf16[2048,2304]{1,0:T(8,128)(2,1)}) custom-call(s32[4]{0:T(128)} %pad_add_fusion.info_ref, bf16[1,512,768]{2,1,0:T(8,128)(2,1)} %collective-permute-done.source_ref, bf16[768,2304]{1,0:T(8,128)(2,1)} %w_ref.13, f32[8,768]{1,0:T(8,128)} %get-tuple-element.341.vec_ref, ...), custom_call_target="tpu_custom_call", output_to_operand_aliasing={{0}: (5, {}), {1}: (6, {})} | custom-call | flops 1811939328 | bytes 3932160 | tf_op jit(solution)/shard_map/enter/pallas_call | solution.py:510
  39.5 18.8 %attend.3 = (bf16[2,1024,768]{2,1,0:T(8,128)(2,1)}, bf16[2,12,1024,1024]{3,2,1,0:T(8,128)(2,1)}, f32[2,6,2,1024]{3,2,1,0:T(2,128)}) custom-call(s32[4]{0:T(128)} %pad_add_fusion.info_ref, bf16[2,1024,2304]{2,1,0:T(8,128)(2,1)} %bitcast.131, bf16[2,1024,2304]{2,1,0:T(8,128)(2,1)} %bitcast.132, bf16[2,1024,2304]{2,1,0:T(8,128)(2,1)} %bitcast.133), custom_call_target="tpu_custom_call" | custom-call | flops 12884901888 | bytes 25165824 | tf_op jit(solution)/shard_map/attend/pallas_call | solution.py:343
  58.3 0.9 copy-done.12
  59.2 2.0 collective-permute-start.2
  61.2 6.7 %enter.8 = (bf16[2048,768]{1,0:T(8,128)(2,1)}, bf16[2048,2304]{1,0:T(8,128)(2,1)}) custom-call(s32[4]{0:T(128)} %pad_add_fusion.info_ref, bf16[1,512,768]{2,1,0:T(8,128)(2,1)} %copy-done.12, bf16[768,2304]{1,0:T(8,128)(2,1)} %w_ref.13, f32[8,768]{1,0:T(8,128)} %get-tuple-element.341.vec_ref, ...), custom_call_target="tpu_custom_call", output_to_operand_aliasing={{0}: (5, {}), {1}: (6, {})} | custom-call | flops 1811939328 | bytes 3932160 | tf_op jit(solution)/shard_map/enter/pallas_call | solution.py:510
  67.8 18.5 %attend.4 = (bf16[2,1024,768]{2,1,0:T(8,128)(2,1)}, bf16[2,12,1024,1024]{3,2,1,0:T(8,128)(2,1)}, f32[2,6,2,1024]{3,2,1,0:T(2,128)}) custom-call(s32[4]{0:T(128)} %pad_add_fusion.info_ref, bf16[2,1024,2304]{2,1,0:T(8,128)(2,1)} %bitcast.134, bf16[2,1024,2304]{2,1,0:T(8,128)(2,1)} %bitcast.135, ...), custom_call_target="tpu_custom_call", output_to_operand_aliasing={{0}: (4, {}), {1}: (5, {}), {2}: (6, {})} | custom-call | flops 12884901888 | bytes 25165824 | tf_op jit(solution)/shard_map/attend/pallas_call | solution.py:343
  86.3 12.5 %middle.1 = (f32[2048,768]{1,0:T(8,128)}, bf16[2048,768]{1,0:T(8,128)(2,1)}) custom-call(s32[4]{0:T(128)} %pad_add_fusion.info_ref, bf16[2048,768]{1,0:T(8,128)(2,1)} %get-tuple-element.173.x_ref, bf16[2048,768]{1,0:T(8,128)(2,1)} %bitcast.159, bf16[768,768]{1,0:T(8,128)(2,1)} %wo_ref.5, bf16[768,768]{1,0:T(8,128)(2,1)} %wq_ref.3, f32[8,768]{1,0:T(8,128)} %concatenate.37.vec_ref), custom_call_target="tpu_custom_call" | custom-call | flops 4831838208 | bytes 15728640 | tf_op jit(solution)/shard_map/middle/pallas_call | solution.py:510
  99.0 1.0 copy-done.9
  100.0 6.6 %enter.9 = (bf16[2048,768]{1,0:T(8,128)(2,1)}, bf16[2048,1536]{1,0:T(8,128)(2,1)}) custom-call(s32[4]{0:T(128)} %pad_add_fusion.info_ref, bf16[2,512,768]{2,1,0:T(8,128)(2,1)} %copy-done.9, bf16[768,1536]{1,0:T(8,128)(2,1)} %wi_ref.3, f32[8,768]{1,0:T(8,128)} %get-tuple-element.341.vec_ref, ...), custom_call_target="tpu_custom_call", output_to_operand_aliasing={{0}: (5, {}), {1}: (6, {})} | custom-call | flops 2415919104 | bytes 6291456 | tf_op jit(solution)/shard_map/enter/pallas_call | solution.py:510
  106.6 31.1 %attend.5 = (bf16[2,1024,768]{2,1,0:T(8,128)(2,1)}, bf16[2,12,1024,1024]{3,2,1,0:T(8,128)(2,1)}, f32[2,6,2,1024]{3,2,1,0:T(2,128)}) custom-call(s32[4]{0:T(128)} %pad_add_fusion.info_ref, bf16[2,1024,768]{2,1,0:T(8,128)(2,1)} %bitcast.175, bf16[2,1024,1536]{2,1,0:T(8,128)(2,1)} %bitcast.152, bf16[2,1024,1536]{2,1,0:T(8,128)(2,1)} %bitcast.153), custom_call_target="tpu_custom_call" | custom-call | flops 25769803776 | bytes 50331648 | tf_op jit(solution)/shard_map/attend/pallas_call | solution.py:343
  137.7 108.1 %feed.1 = (bf16[4,512,768]{2,1,0:T(8,128)(2,1)}, bf16[2,512,768]{2,1,0:T(8,128)(2,1)}, f32[2048,768]{1,0:T(8,128)}, bf16[2048,768]{1,0:T(8,128)(2,1)}, f32[8,768...) custom-call(s32[4]{0:T(128)} %pad_add_fusion.info_ref, ...), custom_call_target="tpu_custom_call" | custom-call | flops 65229815808 | bytes 62914560 | tf_op jit(solution)/shard_map/feed/pallas_call | solution.py:510
  246.0 1.0 collective-permute-start.6
  247.5 1.4 reduce.3
  249.5 30.6 %attend_back.4 = (bf16[2,1024,768]{2,1,0:T(8,128)(2,1)}, bf16[2,1024,768]{2,1,0:T(8,128)(2,1)}, bf16[2,1024,768]{2,1,0:T(8,128)(2,1)}) custom-call(bf16[2,1024,768]{2,1,0:T(8,128)(2,1)} %bitcast.176, bf16[2,1024,1536]{2,1,0:T(8,128)(2,1)} %bitcast.154, bf16[2,1024,1536]{2,1,0:T(8,128)(2,1)} %bitcast.155, ...), custom_call_target="tpu_custom_call" | custom-call | flops 25769803776 | bytes 25165824 | tf_op jit(solution)/shard_map/attend_back/pallas_call | solution.py:419
  280.1 5.3 fusion
  285.5 2.3 copy-done.2
  287.8 1.7 dynamic-slice_bitcast_fusion
  289.5 1.0 collective-permute-start.5
  290.5 30.6 %attend_back.5 = (bf16[2,1024,768]{2,1,0:T(8,128)(2,1)}, bf16[2,1024,768]{2,1,0:T(8,128)(2,1)}, bf16[2,1024,768]{2,1,0:T(8,128)(2,1)}) custom-call(bf16[2,1024,768]{2,1,0:T(8,128)(2,1)} %get-tuple-element.202.refs_0_, bf16[2,1024,768]{2,1,0:T(8,128)(2,1)} %get-tuple-element.203.refs_1_, ...), custom_call_target="tpu_custom_call", output_to_operand_aliasing={{0}: (0, {}), {1}: (1, {}), {2}: (2, {})} | custom-call | flops 25769803776 | bytes 25165824 | tf_op jit(solution)/shard_map/attend_back/pallas_call | solution.py:419
  321.1 41.4 %return_rows.1 = (f32[4,512,768]{2,1,0:T(8,128)}, bf16[2,512,768]{2,1,0:T(8,128)(2,1)}, f32[2048,768]{1,0:T(8,128)}, bf16[2048,768]{1,0:T(8,128)(2,1)}, f32[8,76...) custom-call(s32[4]{0:T(128)} %pad_add_fusion.info_ref, bf16[2048,768]{1,0:T(8,128)(2,1)} %bitcast.183, ...), custom_call_target="tpu_custom_call" | custom-call | flops 19327352832 | bytes 41943040 | tf_op jit(solution)/shard_map/return_rows/pallas_call | solution.py:510
  362.6 3.2 fusion.2
  365.8 1.5 copy-done.3
  367.3 1.2 dynamic-slice_bitcast_fusion.2
  368.4 2.6 collective-permute-start.7
  371.0 1.1 collective-permute-start.12
  372.1 31.0 %attend_back.6 = (bf16[2,1024,768]{2,1,0:T(8,128)(2,1)}, bf16[2,1024,768]{2,1,0:T(8,128)(2,1)}, bf16[2,1024,768]{2,1,0:T(8,128)(2,1)}) custom-call(bf16[2,1024,2304]{2,1,0:T(8,128)(2,1)} %bitcast.137, bf16[2,1024,2304]{2,1,0:T(8,128)(2,1)} %bitcast.138, bf16[2,1024,2304]{2,1,0:T(8,128)(2,1)} %bitcast.139, ...), custom_call_target="tpu_custom_call" | custom-call | flops 25769803776 | bytes 25165824 | tf_op jit(solution)/shard_map/attend_back/pallas_call | solution.py:419
  403.1 1.2 bitcast_dynamic-update-slice_fusion
  404.3 1.0 copy-done.4
  405.4 1.7 fusion.4
  407.2 2.2 collective-permute-start.9
  409.3 2.3 fusion.3
  411.6 1.5 copy-done.5
  413.1 1.1 dynamic-slice_bitcast_fusion.3
  414.6 11.8 %leave.2 = (f32[4,512,768]{2,1,0:T(8,128)}, bf16[512,768]{1,0:T(8,128)(2,1)}, f32[8,768]{1,0:T(8,128)}) custom-call(s32[4]{0:T(128)} %pad_add_fusion.info_ref, bf16[2048,768]{1,0:T(8,128)(2,1)} %bitcast.143, bf16[2048,768]{1,0:T(8,128)(2,1)} %bitcast.146, bf16[2048,768]{1,0:T(8,128)(2,1)} %bitcast.149, bf16[2048,768]{1,0:T(8,128)(2,1)} %get-tuple-element.173.x_ref, ...), custom_call_target="tpu_custom_call" | custom-call | flops 3623878656 | bytes 16777216 | tf_op jit(solution)/shard_map/leave/pallas_call | solution.py:510
  426.5 1.1 collective-permute-start.11
  427.5 30.6 %attend_back.7 = (bf16[2,1024,768]{2,1,0:T(8,128)(2,1)}, bf16[2,1024,768]{2,1,0:T(8,128)(2,1)}, bf16[2,1024,768]{2,1,0:T(8,128)(2,1)}) custom-call(bf16[2,1024,768]{2,1,0:T(8,128)(2,1)} %get-tuple-element.235.refs_0_, bf16[2,1024,768]{2,1,0:T(8,128)(2,1)} %get-tuple-element.236.refs_1_, ...), custom_call_target="tpu_custom_call", output_to_operand_aliasing={{0}: (0, {}), {1}: (1, {}), {2}: (2, {})} | custom-call | flops 25769803776 | bytes 25165824 | tf_op jit(solution)/shard_map/attend_back/pallas_call | solution.py:419
  458.2 17.4 %last_weight.1 = (bf16[8,48,1152]{2,1,0:T(8,128)(2,1)}, bf16[8,48,1152]{2,1,0:T(8,128)(2,1)}, bf16[8,48,1152]{2,1,0:T(8,128)(2,1)}, bf16[8,48,1152]{2,1,0:T(8,128)(2,1)}) custom-call(s32[4]{0:T(128)} %pad_add_fusion.info_ref, bf16[2048,768]{1,0:T(8,128)(2,1)} %bitcast.144, bf16[2048,768]{1,0:T(8,128)(2,1)} %bitcast.147, bf16[2048,768]{1,0:T(8,128)(2,1)} %bitcast.150, ...), custom_call_target="tpu_custom_call" | custom-call | flops 7247757312 | bytes 20971520 | tf_op jit(solution)/shard_map/last_weight/pallas_call | solution.py:510
  476.2 1.2 fusion.8
  477.4 1.0 collective-permute-start.13
  478.5 1.9 fusion.5
  480.4 0.9 dynamic-slice_bitcast_fusion.7
  481.8 3.3 convert_dynamic-update-slice_fusion
  485.6 1.0 dynamic-slice_bitcast_fusion.10
  486.6 1.5 collective-permute-start.17
  488.1 1.0 dynamic-slice_bitcast_fusion.9
  489.1 1.6 collective-permute-start.18
  490.7 2.4 convert_dynamic-update-slice_fusion.2.refs_0_
  493.1 12.0 %leave.3 = (f32[4,512,768]{2,1,0:T(8,128)}, bf16[512,768]{1,0:T(8,128)(2,1)}, f32[8,768]{1,0:T(8,128)}) custom-call(s32[4]{0:T(128)} %pad_add_fusion.info_ref, bf16[2048,768]{1,0:T(8,128)(2,1)} %bitcast.145, bf16[2048,768]{1,0:T(8,128)(2,1)} %bitcast.148, bf16[2048,768]{1,0:T(8,128)(2,1)} %bitcast.151, ...), custom_call_target="tpu_custom_call", output_to_operand_aliasing={{0}: (8, {})} | custom-call | flops 3623878656 | bytes 16777216 | tf_op jit(solution)/shard_map/leave/pallas_call | solution.py:510
  505.0 0.7 add.148
  506.6 44.6 %tail.1 = (f32[192,768]{1,0:T(8,128)}, f32[48,1152]{1,0:T(8,128)}, f32[48,1152]{1,0:T(8,128)}, f32[28,768]{1,0:T(8,128)}, bf16[512,768]{1,0:T(8,128)(2,1)}) custom-call(bf16[2,192,768]{2,1,0:T(8,128)(2,1)} %get-tuple-element.317.refs_0_, bf16[2,192,768]{2,1,0:T(8,128)(2,1)} %collective-permute-done.14.refs_1_, ...), custom_call_target="tpu_custom_call" | custom-call | flops 20000000000 | bytes 10000000 | tf_op jit(solution)/shard_map/tail/pallas_call | solution.py:1138
  551.2 1.2 fusion.25
  552.3 0.7 slice.101
  554.0 0.9 slice.109
  557.2 0.7 fusion.24
  563.2 1.3 convert_dynamic-update-slice_fusion.1
  564.4 0.8 pad_maximum_fusion.1
  566.6 0.9 pad_maximum_fusion
  (141 shorter events, 18.7 us)
Async XLA Ops:
  0.7 13.6 %copy-start = (s32[4,1]{0,1:T(1,128)S(1)}, s32[4,1]{0,1:T(1,128)}, u32[]{:S(2)}) copy-start(s32[4,1]{0,1:T(1,128)} %param.28) | copy-start | bytes 52
  0.7 8.5 %copy-start.24 = (f32[768]{0:T(1024)S(1)}, f32[768]{0:T(1024)}, u32[]{:S(2)}) copy-start(f32[768]{0:T(1024)} %param.39) | copy-start | bytes 9220
  0.7 8.5 %copy-start.25 = (f32[768]{0:T(1024)S(1)}, f32[768]{0:T(1024)}, u32[]{:S(2)}) copy-start(f32[768]{0:T(1024)} %param.38) | copy-start | bytes 9220
  0.7 8.5 %copy-start.26 = (f32[768]{0:T(1024)S(1)}, f32[768]{0:T(1024)}, u32[]{:S(2)}) copy-start(f32[768]{0:T(1024)} %param.32) | copy-start | bytes 9220
  0.7 8.5 %copy-start.27 = (f32[768]{0:T(1024)S(1)}, f32[768]{0:T(1024)}, u32[]{:S(2)}) copy-start(f32[768]{0:T(1024)} %param.31) | copy-start | bytes 9220
  0.7 8.5 %copy-start.34 = (f32[768]{0:T(1024)S(1)}, f32[768]{0:T(1024)}, u32[]{:S(2)}) copy-start(f32[768]{0:T(1024)} %param.35) | copy-start | bytes 9220
  0.7 8.5 %copy-start.35 = (f32[768]{0:T(1024)S(1)}, f32[768]{0:T(1024)}, u32[]{:S(2)}) copy-start(f32[768]{0:T(1024)} %param.34) | copy-start | bytes 9220
  0.7 9.1 %copy-start.23 = (f32[768]{0:T(1024)S(1)}, f32[768]{0:T(1024)}, u32[]{:S(2)}) copy-start(f32[768]{0:T(1024)} %param.43) | copy-start | bytes 9220
  0.8 9.7 %copy-start.28 = (f32[768]{0:T(1024)S(1)}, f32[768]{0:T(1024)}, u32[]{:S(2)}) copy-start(f32[768]{0:T(1024)} %param.37) | copy-start | bytes 9220
  0.8 9.7 %copy-start.29 = (f32[768]{0:T(1024)S(1)}, f32[768]{0:T(1024)}, u32[]{:S(2)}) copy-start(f32[768]{0:T(1024)} %param.41) | copy-start | bytes 9220
  0.8 9.7 %copy-start.22 = (s32[4,1,512]{2,1,0:T(1,128)S(1)}, s32[4,1,512]{2,1,0:T(1,128)}, u32[]{:S(2)}) copy-start(s32[4,1,512]{2,1,0:T(1,128)} %param.29) | copy-start | bytes 24580
  0.8 9.8 %copy-start.7 = (bf16[4,1,512,768]{3,2,1,0:T(8,128)(2,1)S(1)}, bf16[4,1,512,768]{3,2,1,0:T(8,128)(2,1)}, u32[]{:S(2)}) copy-start(bf16[4,1,512,768]{3,2,1,0:T(8,128)(2,1)} %param.30) | copy-start | bytes 9437188
  3.6 29.2 %collective-permute-start = (bf16[1,512,768]{2,1,0:T(8,128)(2,1)}, bf16[1,512,768]{2,1,0:T(8,128)(2,1)}, u32[]{:S(2)}, u32[]{:S(2)}) collective-permute-start(bf16[1,512,768]{2,1,0:T(8,128)(2,1)} %get-tuple-element.310), channel_id=1, source_target_pairs={{0,1},{1,0},{2,3},{3,2},{4,5},{5,4},{6,7},{7,6},{8,9},{9,8},{10,11... | collective-permute-start | bytes 2359304 | tf_op jit(solution)/shard_map/ppermute | solution.py:1193
  11.2 1.7 copy-start.6
  12.9 1.3 copy-start.30
  12.9 1.3 copy-start.31
  12.9 1.3 copy-start.32
  12.9 1.3 copy-start.33
  23.5 9.3 %copy-start.14 = (bf16[1,512,768]{2,1,0:T(8,128)(2,1)S(1)}, bf16[1,512,768]{2,1,0:T(8,128)(2,1)}, u32[]{:S(2)}) copy-start(bf16[1,512,768]{2,1,0:T(8,128)(2,1)} %get-tuple-element.168) | copy-start | bytes 2359300
  32.8 25.5 %collective-permute-start.1 = (bf16[1,512,768]{2,1,0:T(8,128)(2,1)S(1)}, bf16[1,512,768]{2,1,0:T(8,128)(2,1)S(1)}, u32[]{:S(2)}, u32[]{:S(2)}) collective-permute-start(bf16[1,512,768]{2,1,0:T(8,128)(2,1)S(1)} %copy-done.14), channel_id=1, source_target_pairs={{0,1},{1,0},{2,3},{3,2},{4,5},{5,4},{6,7},{7,6},{8,9},{9,8},{10,11... | collective-permute-start | bytes 2359304 | tf_op jit(solution)/shard_map/ppermute | solution.py:1193
  58.3 0.9 copy-start.12
  59.2 39.7 %collective-permute-start.2 = (bf16[2,512,768]{2,1,0:T(8,128)(2,1)}, bf16[2,512,768]{2,1,0:T(8,128)(2,1)S(1)}, u32[]{:S(2)}, u32[]{:S(2)}) collective-permute-start(bf16[2,512,768]{2,1,0:T(8,128)(2,1)} %dynamic-slice_bitcast_fusion.1), channel_id=1, source_target_pairs={{0,1},{1,0},{2,3},{3,2},{4,5},{5,4},{6,7},{7,6},{8,9},{9,8},{10,11... | collective-permute-start | bytes 4718600 | tf_op jit(solution)/shard_map/ppermute | solution.py:1193
  98.9 1.1 copy-start.9
  98.9 38.8 %collective-permute-start.3 = (bf16[2,512,768]{2,1,0:T(8,128)(2,1)}, bf16[2,512,768]{2,1,0:T(8,128)(2,1)}, u32[]{:S(2)}, u32[]{:S(2)}) collective-permute-start(bf16[2,512,768]{2,1,0:T(8,128)(2,1)} %constant_dynamic-slice_fusion.13), channel_id=1, source_target_pairs={{0,1},{1,0},{2,3},{3,2},{4,5},{5,4},{6,7},{7,6},{8,9},{9,8},{10,11... | collective-permute-start | bytes 4718600 | tf_op jit(solution)/shard_map/ppermute | solution.py:1193
  245.8 34.4 %collective-permute-start.4 = (bf16[2,2,2,432,768]{4,3,2,1,0:T(8,128)(2,1)}, bf16[2,2,2,432,768]{4,3,2,1,0:T(8,128)(2,1)}, u32[]{:S(2)}, u32[]{:S(2)}) collective-permute-start(bf16[2,2,2,432,768]{4,3,2,1,0:T(8,128)(2,1)} %bitcast.169), channel_id=1, source_target_pairs={{0,2},{2,0},{4,6},{6,4},{8,10},{10,8},{12,14},{14,12},{16,18},{18,... | collective-permute-start | bytes 15925256 | tf_op jit(solution)/shard_map/ppermute | solution.py:967
  246.0 116.6 %collective-permute-start.6 = (bf16[2,512,768]{2,1,0:T(8,128)(2,1)}, bf16[2,512,768]{2,1,0:T(8,128)(2,1)S(1)}, u32[]{:S(2)}, u32[]{:S(2)}) collective-permute-start(bf16[2,512,768]{2,1,0:T(8,128)(2,1)} %get-tuple-element.217), channel_id=1, source_target_pairs={{0,1},{1,0},{2,3},{3,2},{4,5},{5,4},{6,7},{7,6},{8,9},{9,8},{10,11... | collective-permute-start | bytes 4718600 | tf_op jit(solution)/shard_map/ppermute | solution.py:1283
  285.5 2.3 copy-start.2
  289.5 73.1 %collective-permute-start.5 = (bf16[2,2,432,768]{3,2,1,0:T(8,128)(2,1)}, bf16[2,2,432,768]{3,2,1,0:T(8,128)(2,1)}, u32[]{:S(2)}, u32[]{:S(2)}) collective-permute-start(bf16[2,2,432,768]{3,2,1,0:T(8,128)(2,1)} %dynamic-slice_bitcast_fusion), channel_id=1, source_target_pairs={{0,4},{2,6},{4,0},{6,2},{8,12},{10,14},{12,8},{14,10},{16,20},{18,... | collective-permute-start | bytes 7962632 | tf_op jit(solution)/shard_map/ppermute | solution.py:967
  365.8 1.5 copy-start.3
  368.4 35.9 %collective-permute-start.7 = (bf16[2,432,768]{2,1,0:T(8,128)(2,1)}, bf16[2,432,768]{2,1,0:T(8,128)(2,1)}, u32[]{:S(2)}, u32[]{:S(2)}) collective-permute-start(bf16[2,432,768]{2,1,0:T(8,128)(2,1)} %dynamic-slice_bitcast_fusion.2), channel_id=1, source_target_pairs={{0,8},{2,10},{4,12},{6,14},{8,0},{10,2},{12,4},{14,6},{16,24},{18,... | collective-permute-start | bytes 3981320 | tf_op jit(solution)/shard_map/ppermute | solution.py:967
  371.0 33.3 %collective-permute-start.8 = (bf16[2,2,2,192,768]{4,3,2,1,0:T(8,128)(2,1)}, bf16[2,2,2,192,768]{4,3,2,1,0:T(8,128)(2,1)}, u32[]{:S(2)}, u32[]{:S(2)}) collective-permute-start(bf16[2,2,2,192,768]{4,3,2,1,0:T(8,128)(2,1)} %bitcast.30), channel_id=1, source_target_pairs={{0,2},{2,0},{4,6},{6,4},{8,10},{10,8},{12,14},{14,12},{16,18},{18,... | collective-permute-start | bytes 7077896 | tf_op jit(solution)/shard_map/ppermute | solution.py:967
  371.0 87.2 %collective-permute-start.12 = (bf16[2,512,768]{2,1,0:T(8,128)(2,1)}, bf16[2,512,768]{2,1,0:T(8,128)(2,1)}, u32[]{:S(2)}, u32[]{:S(2)}) collective-permute-start(bf16[2,512,768]{2,1,0:T(8,128)(2,1)} %get-tuple-element.242), channel_id=1, source_target_pairs={{0,1},{1,0},{2,3},{3,2},{4,5},{5,4},{6,7},{7,6},{8,9},{9,8},{10,11... | collective-permute-start | bytes 4718600 | tf_op jit(solution)/shard_map/ppermute | solution.py:1311
  403.1 2.3 copy-start.4
  404.3 5.0 copy-start.8
  407.2 51.0 %collective-permute-start.9 = (bf16[432,768]{1,0:T(8,128)(2,1)S(1)}, bf16[432,768]{1,0:T(8,128)(2,1)}, u32[]{:S(2)}, u32[]{:S(2)}) collective-permute-start(bf16[432,768]{1,0:T(8,128)(2,1)S(1)} %dynamic-slice_bitcast_fusion.6), channel_id=1, source_target_pairs={{0,16},{2,18},{4,20},{6,22},{8,24},{10,26},{12,28},{14,30},{16,0},... | collective-permute-start | bytes 1990664 | tf_op jit(solution)/shard_map/ppermute | solution.py:967
  411.6 1.5 copy-start.5
  414.2 44.0 %collective-permute-start.10 = (bf16[2,2,192,768]{3,2,1,0:T(8,128)(2,1)}, bf16[2,2,192,768]{3,2,1,0:T(8,128)(2,1)}, u32[]{:S(2)}, u32[]{:S(2)}) collective-permute-start(bf16[2,2,192,768]{3,2,1,0:T(8,128)(2,1)} %dynamic-slice_bitcast_fusion.3), channel_id=1, source_target_pairs={{0,4},{2,6},{4,0},{6,2},{8,12},{10,14},{12,8},{14,10},{16,20},{18,... | collective-permute-start | bytes 3538952 | tf_op jit(solution)/shard_map/ppermute | solution.py:967
  426.5 31.7 %collective-permute-start.11 = (bf16[512,768]{1,0:T(8,128)(2,1)}, bf16[512,768]{1,0:T(8,128)(2,1)}, u32[]{:S(2)}, u32[]{:S(2)}) collective-permute-start(bf16[512,768]{1,0:T(8,128)(2,1)} %get-tuple-element.241), channel_id=1, source_target_pairs={{0,1},{1,0},{2,3},{3,2},{4,5},{5,4},{6,7},{7,6},{8,9},{9,8},{10,11... | collective-permute-start | bytes 2359304 | tf_op jit(solution)/shard_map/ppermute | solution.py:1336
  475.6 9.5 %collective-permute-start.15 = (bf16[2,2,2,48,1152]{4,3,2,1,0:T(8,128)(2,1)}, bf16[2,2,2,48,1152]{4,3,2,1,0:T(8,128)(2,1)S(1)}, u32[]{:S(2)}, u32[]{:S(2)}) collective-permute-start(bf16[2,2,2,48,1152]{4,3,2,1,0:T(8,128)(2,1)} %bitcast.173), channel_id=1, source_target_pairs={{0,2},{2,0},{4,6},{6,4},{8,10},{10,8},{12,14},{14,12},{16,18},{18,... | collective-permute-start | bytes 2654216 | tf_op jit(solution)/shard_map/ppermute | solution.py:967
  475.7 9.4 %collective-permute-start.16 = (bf16[2,2,2,48,1152]{4,3,2,1,0:T(8,128)(2,1)}, bf16[2,2,2,48,1152]{4,3,2,1,0:T(8,128)(2,1)S(1)}, u32[]{:S(2)}, u32[]{:S(2)}) collective-permute-start(bf16[2,2,2,48,1152]{4,3,2,1,0:T(8,128)(2,1)} %bitcast.172), channel_id=1, source_target_pairs={{0,2},{2,0},{4,6},{6,4},{8,10},{10,8},{12,14},{14,12},{16,18},{18,... | collective-permute-start | bytes 2654216 | tf_op jit(solution)/shard_map/ppermute | solution.py:967
  477.4 28.5 %collective-permute-start.13 = (bf16[432,768]{1,0:T(8,128)(2,1)S(1)}, bf16[432,768]{1,0:T(8,128)(2,1)S(1)}, u32[]{:S(2)}, u32[]{:S(2)}) collective-permute-start(bf16[432,768]{1,0:T(8,128)(2,1)S(1)} %fusion.8), channel_id=1, source_target_pairs={{0,1},{1,0},{2,3},{3,2},{4,5},{5,4},{6,7},{7,6},{8,9},{9,8},{10,11... | collective-permute-start | bytes 1990664 | tf_op jit(solution)/shard_map/ppermute | solution.py:969
  480.4 4.7 copy-start.10
  480.4 4.7 copy-start.11
  481.3 24.5 %collective-permute-start.14 = (bf16[2,192,768]{2,1,0:T(8,128)(2,1)S(1)}, bf16[2,192,768]{2,1,0:T(8,128)(2,1)}, u32[]{:S(2)}, u32[]{:S(2)}) collective-permute-start(bf16[2,192,768]{2,1,0:T(8,128)(2,1)S(1)} %get-tuple-element.318), channel_id=1, source_target_pairs={{0,8},{2,10},{4,12},{6,14},{8,0},{10,2},{12,4},{14,6},{16,24},{18,... | collective-permute-start | bytes 1769480 | tf_op jit(solution)/shard_map/ppermute | solution.py:967
  486.6 19.2 %collective-permute-start.17 = (bf16[2,2,48,1152]{3,2,1,0:T(8,128)(2,1)}, bf16[2,2,48,1152]{3,2,1,0:T(8,128)(2,1)}, u32[]{:S(2)}, u32[]{:S(2)}) collective-permute-start(bf16[2,2,48,1152]{3,2,1,0:T(8,128)(2,1)} %get-tuple-element.322), channel_id=1, source_target_pairs={{0,4},{2,6},{4,0},{6,2},{8,12},{10,14},{12,8},{14,10},{16,20},{18,... | collective-permute-start | bytes 1327112 | tf_op jit(solution)/shard_map/ppermute | solution.py:967
  489.1 16.8 %collective-permute-start.18 = (bf16[2,2,48,1152]{3,2,1,0:T(8,128)(2,1)}, bf16[2,2,48,1152]{3,2,1,0:T(8,128)(2,1)}, u32[]{:S(2)}, u32[]{:S(2)}) collective-permute-start(bf16[2,2,48,1152]{3,2,1,0:T(8,128)(2,1)} %get-tuple-element.320), channel_id=1, source_target_pairs={{0,8},{2,10},{4,12},{6,14},{8,0},{10,2},{12,4},{14,6},{16,24},{18,... | collective-permute-start | bytes 1327112 | tf_op jit(solution)/shard_map/ppermute | solution.py:967
  493.1 12.0 %copy-start.19 = (f32[8,768]{1,0:T(8,128)S(1)}, f32[8,768]{1,0:T(8,128)}, u32[]{:S(2)}) copy-start(f32[8,768]{1,0:T(8,128)} %get-tuple-element.264) | copy-start | bytes 73732
  493.1 12.8 %copy-start.18 = (f32[4,768]{1,0:T(4,128)S(1)}, f32[4,768]{1,0:T(4,128)}, u32[]{:S(2)}) copy-start(f32[4,768]{1,0:T(4,128)} %reshape.207) | copy-start | bytes 36868
  493.1 12.9 %copy-start.20 = (f32[8,768]{1,0:T(8,128)S(1)}, f32[8,768]{1,0:T(8,128)}, u32[]{:S(2)}) copy-start(f32[8,768]{1,0:T(8,128)} %get-tuple-element.274) | copy-start | bytes 73732
  493.1 12.9 %copy-start.21 = (f32[8,768]{1,0:T(8,128)S(1)}, f32[8,768]{1,0:T(8,128)}, u32[]{:S(2)}) copy-start(f32[8,768]{1,0:T(8,128)} %get-tuple-element.275) | copy-start | bytes 73732
  551.2 6.0 %copy-start.15 = (f32[192,768]{1,0:T(8,128)S(1)}, f32[192,768]{1,0:T(8,128)}, u32[]{:S(2)}) copy-start(f32[192,768]{1,0:T(8,128)} %get-tuple-element.284) | copy-start | bytes 1769476
  553.1 10.1 %copy-start.13 = (bf16[512,768]{1,0:T(8,128)(2,1)S(1)}, bf16[512,768]{1,0:T(8,128)(2,1)}, u32[]{:S(2)}) copy-start(bf16[512,768]{1,0:T(8,128)(2,1)} %get-tuple-element.278) | copy-start | bytes 2359300
  553.3 11.2 %copy-start.16 = (f32[48,1152]{1,0:T(8,128)S(1)}, f32[48,1152]{1,0:T(8,128)}, u32[]{:S(2)}) copy-start(f32[48,1152]{1,0:T(8,128)} %get-tuple-element.282) | copy-start | bytes 663556
  553.3 11.2 %copy-start.17 = (f32[48,1152]{1,0:T(8,128)S(1)}, f32[48,1152]{1,0:T(8,128)}, u32[]{:S(2)}) copy-start(f32[48,1152]{1,0:T(8,128)} %get-tuple-element.283) | copy-start | bytes 663556
  556.6 10.9 %copy-start.1 = (s32[4,1]{0,1:T(1,128)S(1)}, s32[4,1]{0,1:T(1,128)}, u32[]{:S(2)}) copy-start(s32[4,1]{0,1:T(1,128)} %param.28) | copy-start | bytes 52

commit v9 on v8

--- a/solution.py
+++ b/solution.py
@@ -888,16 +888,19 @@
         sum([p[1] for p in pieces], []),
         sum([p[0] for p in pieces], []),
         steps + parts // 2,
-        6 * rows * width * width,
+        24 * rows * width * width,
         20 * 2**20,
         scratch=[pltpu.VMEM((width, 3 * width), jnp.float32)],
     )
 
 
 def leave_kernel(
-    info_ref, dq_ref, dk_ref, dv_ref, x_ref, dx_ref, w_ref, vec_ref, *refs
+    info_ref, dq_ref, dk_ref, dv_ref, x_ref, dx_ref, w_ref, vec_ref, *refs, halves
 ):
-    own_ref, got_ref, vsum_ref = refs[-3:]
+    refs = list(refs)
+    up_ref, vsum_ref = refs.pop(), refs.pop()
+    got_ref = refs.pop() if 1 in halves else None
+    own_ref = refs.pop() if 0 in halves else None
     step = pl.program_id(0)
 
     @pl.when(step == 0)
@@ -913,36 +916,46 @@
     )
     unit, inverse = normal_parts(x_ref[...].astype(jnp.float32))
     dx = dx_ref[...] + normal_back(unit, inverse, vec_ref[0:1, :], upstream)
-    put_rows(step, dx, own_ref, got_ref)
+    if len(halves) == 2:
+        put_rows(step, dx, own_ref, got_ref)
+    else:
+        out_ref = got_ref if own_ref is None else own_ref
+        out_ref[...] = dx.astype(out_ref.dtype)
     vsum_ref[0:1, :] += column_sum(upstream * unit)
     vsum_ref[1:2, :] += column_sum(upstream)
     vsum_ref[2:3, :] += column_sum(dq.astype(jnp.float32))
     vsum_ref[3:4, :] += column_sum(dv.astype(jnp.float32))
 
 
-def leave(info, at, previous, grads, x, dx1, weight, vectors, own, micros):
+def leave(info, at, halves, previous, grads, x, dx1, weight, vectors, own, micros):
     rows, width = x.shape
     held = rows // own // 2
-    row = pl.BlockSpec((own, width), lambda step, info: (2 * at + step, 0))
+    row = pl.BlockSpec((own, width), lambda step, info: (2 * at + halves[0] + step, 0))
     more = {"input_output_aliases": {8: 0}} if previous else {}
     sums = like((8, width))
+    outs, out_specs = [], []
+    if 0 in halves:
+        outs.append(like((micros, own, width)))
+        out_specs.append(
+            pl.BlockSpec((None, own, width), lambda step, info: (info[0] * held + at, 0, 0))
+        )
+    if 1 in halves:
+        outs.append(like((own, width), jnp.bfloat16))
+        out_specs.append(pl.BlockSpec((own, width), lambda step, info: (0, 0)))
     return kernel_call(
-        leave_kernel,
+        functools.partial(leave_kernel, halves=halves),
         "leave",
         info,
         (*grads, x, dx1, weight, vectors, *previous),
         [row] * 5
         + [resident(a) for a in (weight, vectors)]
         + [pl.BlockSpec(memory_space=pl.ANY)] * len(previous),
-        [like((micros, own, width)), like((own, width), jnp.bfloat16), sums],
-        [
-            pl.BlockSpec((None, own, width), lambda step, info: (info[0] * held + at, 0, 0)),
-            pl.BlockSpec((own, width), lambda step, info: (0, 0)),
-            whole_block(sums),
-        ],
-        2,
-        12 * own * width * width,
-        16 * 2**20,
+        outs + [sums],
+        out_specs + [whole_block(sums)],
+        len(halves),
+        12 * len(halves) * own * width * width,
+        8 * len(halves) * 2**20,
+        scratch=[pltpu.VMEM((8, 128), jnp.float32)],
         **more,
     )
 
@@ -1027,8 +1040,8 @@
 
 def tail_kernel(*refs, orders, groups):
     trees = len(orders)
-    ins, refs = refs[: 2 * trees + 2], refs[2 * trees + 2 :]
-    outs, refs = refs[: trees + 2], refs[trees + 2 :]
+    ins, refs = refs[: 2 * trees + 1], refs[2 * trees + 1 :]
+    outs, refs = refs[: trees + 1], refs[trees + 1 :]
     send_sems, recv_sems = refs[-2:]
     scratch = list(refs[:-2])
     place = lax.axis_index("dp")
@@ -1056,7 +1069,6 @@
         return copy
 
     other = {"seq": 1 - side}
-    rows_copy = send(ins[-1], outs[-1], other)
     totals = []
     for at in range(trees):
         total = scratch.pop(0)
@@ -1101,10 +1113,9 @@
                 total = total + got[...]
             target[...] = total
             sums = target
-    rows_copy.wait()
-
-
-def tail(trees, sums, rows, parts):
+
+
+def tail(trees, sums, parts):
     orders = [tuple(tree.order) for tree in trees]
     groups, bit = [], 1
     while bit < parts:
@@ -1113,11 +1124,11 @@
     arrays = []
     for tree in trees:
         arrays += [tree.kept, tree.got]
-    arrays += [sums, rows]
+    arrays += [sums]
     totals = [pltpu.VMEM(tree.kept.shape, jnp.bfloat16) for tree in trees]
     scratch = totals + [pltpu.VMEM(sums.shape, jnp.float32)]
     shapes = [tree.kept.shape for tree in trees]
-    copies = 1
+    copies = 0
     for step in range(max(max(len(order) for order in orders) + 1, len(groups) + 1)):
         for at, order in enumerate(orders):
             if step < len(order):
@@ -1133,7 +1144,7 @@
         elif step == len(groups):
             scratch += [pltpu.VMEM(sums.shape, jnp.float32)]
             copies += 1
-    outs = [like(shape) for shape in shapes] + [like(sums.shape), like(rows.shape, rows.dtype)]
+    outs = [like(shape) for shape in shapes] + [like(sums.shape)]
     vmem = pl.BlockSpec(memory_space=pltpu.VMEM)
     return pl.pallas_call(
         functools.partial(tail_kernel, orders=orders, groups=groups),
@@ -1149,6 +1160,73 @@
         ),
         name="tail",
     )(*arrays)
+
+
+def final_kernel(info_ref, kept_ref, got_ref, mid_ref, first_ref, second_ref, sums_ref, *outs, rows, vectors):
+    place = info_ref[info_ref.shape[0] - 1]
+    width = mid_ref.shape[1]
+    high = kept_ref.shape[0]
+
+    def feed_rows(start, count):
+        at = slice(start, start + count)
+        return kept_ref[at, :].astype(jnp.float32) + got_ref[at, :].astype(jnp.float32)
+
+    wide = outs[17].shape[1] // width
+    inner = high - (wide + 1) * rows
+    outs[19][...] = feed_rows(0, inner)
+    outs[13][...] = feed_rows(inner, rows)
+    for at in range(wide):
+        outs[17][:, at * width : (at + 1) * width] = feed_rows(inner + (at + 1) * rows, rows)
+    outs[9][...] = mid_ref[:rows, :]
+    outs[5][...] = mid_ref[rows : 2 * rows, :]
+    for at in range(2):
+        outs[11][:, at * width : (at + 1) * width] = mid_ref[(2 + at) * rows : (3 + at) * rows, :]
+    half = first_ref.shape[1]
+    outs[2][:, :half] = first_ref[...]
+    outs[2][:, half:] = second_ref[...]
+    turn = lax.rem(width - place * rows, width)
+    for group in range(3):
+        turned = pltpu.roll(sums_ref[8 * group : 8 * group + 8, :], turn, 1)
+        for index, row in vectors:
+            if row // 8 == group:
+                outs[index][...] = turned[row % 8 : row % 8 + 1, :rows]
+    each = width // inner
+    hidden = sums_ref[24 : 24 + wide, :]
+    turned = pltpu.roll(
+        jnp.concatenate([hidden] * (8 // wide), axis=0),
+        lax.rem(width - lax.rem(place, each) * inner, width),
+        1,
+    )[:, :inner]
+    mine = lax.broadcasted_iota(jnp.int32, turned.shape, 0) == place // each
+    outs[18][...] = jnp.sum(jnp.where(mine, turned, 0.0), axis=0, keepdims=True)
+
+
+def final_outputs(info, kept, got, mid, first, second, sums, inner, rows):
+    width = mid.shape[1]
+    block = inner * rows // width
+    vectors = tuple(
+        (index, at if at < 4 else at + 4 if at < 8 else at + 8)
+        for at, index in enumerate((0, 1, 3, 4, 14, 15, 16, 20, 7, 8, 6, 10, 12))
+    )
+    shapes = [(1, rows)] * 21
+    shapes[18] = (1, block)
+    shapes[2], shapes[5], shapes[9], shapes[13] = (rows, 3 * width), *[(rows, width)] * 3
+    shapes[11], shapes[17], shapes[19] = (rows, 2 * width), (rows, inner), (block, width)
+    arrays = (kept, got, mid, first, second, sums)
+    outs = [like(shape) for shape in shapes]
+    results = kernel_call(
+        functools.partial(final_kernel, rows=rows, vectors=vectors),
+        "final",
+        info,
+        arrays,
+        [whole_block(a) for a in arrays],
+        outs,
+        [whole_block(a) for a in outs],
+        1,
+        10**6,
+        10**7,
+    )
+    return [out[0] if out.shape[0] == 1 else out for out in results]
 
 
 def whole_sequences(
@@ -1211,7 +1289,9 @@
         cotangent[:, 0].astype(jnp.float32) * loss_mask[:, 0].astype(jnp.float32)[..., None]
     ).astype(jnp.bfloat16)
     kinds = lax.dynamic_slice_in_dim(row_kind[:, 0], side * held, held, axis=0)
-    info = jnp.concatenate([jnp.stack([side, place % 2]).astype(jnp.int32), kinds])
+    info = jnp.concatenate(
+        [jnp.stack([side, place % 2]), kinds, place[None]], dtype=jnp.int32
+    )
 
     self_vectors = pack(norm_self_gain, norm_self_bias)
     zero = jnp.zeros_like(self_query_bias)
@@ -1311,67 +1391,47 @@
     source_gots = lax.ppermute(source_gots, "seq", SWAP)
     grads = settle(feed_trees + mid_trees, attend_back((0, 0), (1, pairs), (), *self_inputs))
     exchange(feed_trees + mid_trees)
-    kept, leave_sums = (), []
+    kept, sums = (), 0.0
     trees = feed_trees + mid_trees
-    for at in range(held):
-        if at == held - 1:
-            late_parts = last_weight(
-                info, [flat(rows) for rows in grads], inputs, self_vectors, own, parts
-            )
-            late_trees = [
-                Tree(*late_parts[0:2], low_first),
-                Tree(*late_parts[2:4], second_first),
-            ]
-            exchange(late_trees)
-            grads, _ = lax.optimization_barrier((grads, late_parts[0]))
-            grads = settle(late_trees, grads)
-            exchange(late_trees)
-        kept, got, sums = leave(
-            info, at, kept, [flat(rows) for rows in grads], inputs, grad_self,
+
+    def leave_now(at, halves, kept, grads):
+        return leave(
+            info, at, halves, kept, [flat(rows) for rows in grads], inputs, grad_self,
             self_input, self_vectors, own, micros,
         )
-        leave_sums.append(sums)
-        if at < held - 1:
-            grads, kept = lax.optimization_barrier((grads, kept))
-            back = lax.ppermute(got, "seq", SWAP)
-            grads, back, source_gots = settle(
-                trees,
-                (attend_back((at + 1, 0), (1, pairs), grads, *self_inputs), back, source_gots),
-            )
-            exchange(trees)
-            back = back.astype(kept.dtype)[None]
-            kept = (
-                lax.dynamic_update_slice_in_dim(kept, back, (1 - side) * held + at, axis=0),
-            )
-    input_grads, got, sums = settle(
-        feed_trees, receive(mid_trees + late_trees, (kept, got, sum(leave_sums)))
-    )
-    finish(feed_trees)
-    sums = jnp.concatenate([sums, feed_sums, return_sums, hidden_sums.reshape(-1, width)], axis=0)
-    mid_total, *late_totals, sums, back = tail(mid_trees + late_trees, sums, got, parts)
+
+    for at in range(held - 1):
+        kept, got, new_sums = leave_now(at, (0, 1), kept, grads)
+        sums = sums + new_sums
+        grads, kept = lax.optimization_barrier((grads, kept))
+        back = lax.ppermute(got, "seq", SWAP)
+        grads, back, source_gots = settle(
+            trees, (attend_back((at + 1, 0), (1, pairs), grads, *self_inputs), back, source_gots)
+        )
+        exchange(trees)
+        back = back.astype(kept.dtype)[None]
+        kept = (lax.dynamic_update_slice_in_dim(kept, back, (1 - side) * held + at, axis=0),)
+    got, new_sums = leave_now(held - 1, (1,), (), grads)
+    sums = sums + new_sums
+    back = lax.ppermute(got, "seq", SWAP)
+    grads, _ = lax.optimization_barrier((grads, got))
+    late_parts = last_weight(info, [flat(rows) for rows in grads], inputs, self_vectors, own, parts)
+    late_trees = [Tree(*late_parts[0:2], low_first), Tree(*late_parts[2:4], second_first)]
+    exchange(late_trees)
+    (grads, _), back = lax.optimization_barrier(((grads, late_parts[0]), back))
+    grads = settle(late_trees, grads)
+    exchange(late_trees)
+    input_grads, new_sums = leave_now(held - 1, (0,), kept, grads)
+    input_grads, new_sums = receive(trees + late_trees, (input_grads, new_sums))
+    sums = jnp.concatenate(
+        [sums + new_sums, feed_sums, return_sums, hidden_sums.reshape(-1, width)], axis=0
+    )
+    mid_total, *late_totals, sums = tail(mid_trees + late_trees, sums, parts)
     input_grads = give(input_grads, back[None], held - 1)
-    rows = width // parts
-    inner_rows = feed_in.shape[1] // parts
-    final = [None] * 21
-
-    def mine(row):
-        return lax.dynamic_slice_in_dim(row, place * (row.shape[0] // parts), row.shape[0] // parts)
-
-    def widen(block):
-        return jnp.concatenate([block[i : i + rows] for i in range(0, len(block), rows)], axis=1)
-
-    for at, index in enumerate((0, 1, 3, 4, 14, 15, 16, 20, 7, 8, 6, 10, 12)):
-        row = at if at < 4 else at + 4 if at < 8 else at + 8
-        final[index] = mine(sums[row])
-    final[18] = mine(sums[24:].reshape(-1))
-    feed_total = feed_trees[0].total
-    final[19] = feed_total[:inner_rows]
-    final[13] = feed_total[inner_rows : inner_rows + rows]
-    final[17] = widen(feed_total[inner_rows + rows :])
-    final[9] = mid_total[:rows]
-    final[5] = mid_total[rows : 2 * rows]
-    final[11] = widen(mid_total[2 * rows :])
-    final[2] = jnp.concatenate(late_totals, axis=1)
+    final = final_outputs(
+        info, feed_trees[0].kept, feed_trees[0].got, mid_total, *late_totals, sums,
+        feed_in.shape[1], width // parts,
+    )
     source_grads = give(source_grads, source_gots, 0)
     return (results[:, None], input_grads[:, None], source_grads[:, None]) + tuple(final)
 

time: 574 us -> 573 us (level)
  local copies, waits for them, and re-layouts: 41.1 us -> 28.2 us
    dynamic_slice x14 -> x0, local copies, waits for them, and re-layouts: 8.19 us -> none  [mine(): lax.dynamic_slice_in_dim(row, place * (row.shape[0] // parts), row.shape[...]
    pallas_call x11 -> x13, Pallas kernels: 239 us -> 246 us  [kernel_call(): pl.pallas_call(kernel, grid_spec=pltpu.PrefetchScalarGridSpec(num_scalar_...]
  transfers between devices with their start and end apart: 19 -> 20, of which waited for: 1 -> 1; matrix products, arithmetic and copies ran while one was open for 7% -> 6% of each run, Pallas kernels for 54% -> 56%
where the time goes in v9:
time: 573 us; the launch traced here: 566 us
  Pallas kernels  480 us (84%)
  other arithmetic  29.6 us (5%)
  local copies, waits for them, and re-layouts  28.2 us (5%)
  starting transfers between devices  21.2 us (4%)
    pallas_call x13, Pallas kernels, kernel_call(): pl.pallas_call(kernel, grid_spec=pltpu.PrefetchScalarGridSpec(num_scalar_...  246 us
    pallas_call x4, Pallas kernels, attend_back(): pl.pallas_call(kernel, grid=size, in_specs=[pl.BlockSpec(memory_space=pl....  123 us
    pallas_call x3, Pallas kernels, attend(): pl.pallas_call(functools.partial(attend_kernel, use_mask=use_mask, start=...  68.5 us
    pallas_call x1, Pallas kernels, tail(): pl.pallas_call(functools.partial(tail_kernel, orders=orders, groups=group...  42.4 us
    convert_element_type x7, other arithmetic, add(): total = total.astype(jnp.bfloat16)  16.1 us
  transfers between devices with their start and end apart: 20, of which 1 were waited for; matrix products, arithmetic and copies ran while one was open for 6% of the time, Pallas kernels for 56%

profile of v9, /device:TPU:0, one launch (start us, length us, event | category | flops | bytes accessed | tf_op | source)
XLA Modules:
  0.0 565.8 jit_solution(1645668539195214016)
XLA Ops:
  0.8 2.8 dynamic-slice_bitcast_fusion.4
  3.6 3.0 collective-permute-start
  6.5 2.7 dynamic-slice_bitcast_fusion.1
  11.2 1.7 copy-done.6
  12.9 1.3 constant_dynamic-slice_fusion
  14.4 0.6 pad_add_fusion.info_ref
  16.3 0.7 maximum_maximum_fusion.1
  17.0 6.6 %enter.6 = (bf16[2048,768]{1,0:T(8,128)(2,1)}, bf16[2048,1536]{1,0:T(8,128)(2,1)}) custom-call(s32[5]{0:T(128)} %pad_add_fusion.info_ref, bf16[4,512,768]{2,1,0:T(8,128)(2,1)} %bitcast.157, bf16[768,1536]{1,0:T(8,128)(2,1)} %wi_ref.3, f32[8,768]{1,0:T(8,128)} %get-tuple-element.361.vec_ref, f32[1,1536]{1,0:T(1,128)} %broadcast_in_dim.45.bias_ref), custom_call_target="tpu_custom_call" | custom-call | flops 2415919104 | bytes 6291456 | tf_op jit(solution)/shard_map/enter/pallas_call | solution.py:510
  23.5 9.3 %enter.5 = (bf16[2048,768]{1,0:T(8,128)(2,1)}, bf16[2048,2304]{1,0:T(8,128)(2,1)}) custom-call(s32[5]{0:T(128)} %pad_add_fusion.info_ref, bf16[4,512,768]{2,1,0:T(8,128)(2,1)} %bitcast.156, bf16[768,2304]{1,0:T(8,128)(2,1)} %w_ref.15, f32[8,768]{1,0:T(8,128)} %get-tuple-element.361.vec_ref, f32[1,2304]{1,0:T(1,128)} %broadcast_in_dim.44.bias_ref), custom_call_target="tpu_custom_call" | custom-call | flops 3623878656 | bytes 7864320 | tf_op jit(solution)/shard_map/enter/pallas_call | solution.py:510
  32.9 6.6 %enter.7 = (bf16[2048,768]{1,0:T(8,128)(2,1)}, bf16[2048,2304]{1,0:T(8,128)(2,1)}) custom-call(s32[5]{0:T(128)} %pad_add_fusion.info_ref, bf16[1,512,768]{2,1,0:T(8,128)(2,1)} %collective-permute-done.source_ref, bf16[768,2304]{1,0:T(8,128)(2,1)} %w_ref.15, f32[8,768]{1,0:T(8,128)} %get-tuple-element.361.vec_ref, ...), custom_call_target="tpu_custom_call", output_to_operand_aliasing={{0}: (5, {}), {1}: (6, {})} | custom-call | flops 1811939328 | bytes 3932160 | tf_op jit(solution)/shard_map/enter/pallas_call | solution.py:510
  39.5 18.9 %attend.3 = (bf16[2,1024,768]{2,1,0:T(8,128)(2,1)}, bf16[2,12,1024,1024]{3,2,1,0:T(8,128)(2,1)}, f32[2,6,2,1024]{3,2,1,0:T(2,128)}) custom-call(s32[5]{0:T(128)} %pad_add_fusion.info_ref, bf16[2,1024,2304]{2,1,0:T(8,128)(2,1)} %bitcast.120, bf16[2,1024,2304]{2,1,0:T(8,128)(2,1)} %bitcast.121, bf16[2,1024,2304]{2,1,0:T(8,128)(2,1)} %bitcast.122), custom_call_target="tpu_custom_call" | custom-call | flops 12884901888 | bytes 25165824 | tf_op jit(solution)/shard_map/attend/pallas_call | solution.py:343
  58.3 0.9 copy-done.13
  59.2 2.0 collective-permute-start.2
  61.2 6.7 %enter.8 = (bf16[2048,768]{1,0:T(8,128)(2,1)}, bf16[2048,2304]{1,0:T(8,128)(2,1)}) custom-call(s32[5]{0:T(128)} %pad_add_fusion.info_ref, bf16[1,512,768]{2,1,0:T(8,128)(2,1)} %copy-done.13, bf16[768,2304]{1,0:T(8,128)(2,1)} %w_ref.15, f32[8,768]{1,0:T(8,128)} %get-tuple-element.361.vec_ref, ...), custom_call_target="tpu_custom_call", output_to_operand_aliasing={{0}: (5, {}), {1}: (6, {})} | custom-call | flops 1811939328 | bytes 3932160 | tf_op jit(solution)/shard_map/enter/pallas_call | solution.py:510
  67.9 18.5 %attend.4 = (bf16[2,1024,768]{2,1,0:T(8,128)(2,1)}, bf16[2,12,1024,1024]{3,2,1,0:T(8,128)(2,1)}, f32[2,6,2,1024]{3,2,1,0:T(2,128)}) custom-call(s32[5]{0:T(128)} %pad_add_fusion.info_ref, bf16[2,1024,2304]{2,1,0:T(8,128)(2,1)} %bitcast.123, bf16[2,1024,2304]{2,1,0:T(8,128)(2,1)} %bitcast.124, ...), custom_call_target="tpu_custom_call", output_to_operand_aliasing={{0}: (4, {}), {1}: (5, {}), {2}: (6, {})} | custom-call | flops 12884901888 | bytes 25165824 | tf_op jit(solution)/shard_map/attend/pallas_call | solution.py:343
  86.4 12.5 %middle.1 = (f32[2048,768]{1,0:T(8,128)}, bf16[2048,768]{1,0:T(8,128)(2,1)}) custom-call(s32[5]{0:T(128)} %pad_add_fusion.info_ref, bf16[2048,768]{1,0:T(8,128)(2,1)} %get-tuple-element.194.x_ref, bf16[2048,768]{1,0:T(8,128)(2,1)} %bitcast.151, bf16[768,768]{1,0:T(8,128)(2,1)} %wo_ref.5, bf16[768,768]{1,0:T(8,128)(2,1)} %wq_ref.3, f32[8,768]{1,0:T(8,128)} %concatenate.28.vec_ref), custom_call_target="tpu_custom_call" | custom-call | flops 4831838208 | bytes 15728640 | tf_op jit(solution)/shard_map/middle/pallas_call | solution.py:510
  100.1 6.6 %enter.9 = (bf16[2048,768]{1,0:T(8,128)(2,1)}, bf16[2048,1536]{1,0:T(8,128)(2,1)}) custom-call(s32[5]{0:T(128)} %pad_add_fusion.info_ref, bf16[2,512,768]{2,1,0:T(8,128)(2,1)} %copy-done.10, bf16[768,1536]{1,0:T(8,128)(2,1)} %wi_ref.3, f32[8,768]{1,0:T(8,128)} %get-tuple-element.361.vec_ref, ...), custom_call_target="tpu_custom_call", output_to_operand_aliasing={{0}: (5, {}), {1}: (6, {})} | custom-call | flops 2415919104 | bytes 6291456 | tf_op jit(solution)/shard_map/enter/pallas_call | solution.py:510
  106.6 31.1 %attend.5 = (bf16[2,1024,768]{2,1,0:T(8,128)(2,1)}, bf16[2,12,1024,1024]{3,2,1,0:T(8,128)(2,1)}, f32[2,6,2,1024]{3,2,1,0:T(2,128)}) custom-call(s32[5]{0:T(128)} %pad_add_fusion.info_ref, bf16[2,1024,768]{2,1,0:T(8,128)(2,1)} %bitcast.181, bf16[2,1024,1536]{2,1,0:T(8,128)(2,1)} %bitcast.144, bf16[2,1024,1536]{2,1,0:T(8,128)(2,1)} %bitcast.145), custom_call_target="tpu_custom_call" | custom-call | flops 25769803776 | bytes 50331648 | tf_op jit(solution)/shard_map/attend/pallas_call | solution.py:343
  137.8 108.1 %feed.1 = (bf16[4,512,768]{2,1,0:T(8,128)(2,1)}, bf16[2,512,768]{2,1,0:T(8,128)(2,1)}, f32[2048,768]{1,0:T(8,128)}, bf16[2048,768]{1,0:T(8,128)(2,1)}, f32[8,768...) custom-call(s32[5]{0:T(128)} %pad_add_fusion.info_ref, ...), custom_call_target="tpu_custom_call" | custom-call | flops 65229815808 | bytes 62914560 | tf_op jit(solution)/shard_map/feed/pallas_call | solution.py:510
  246.1 1.0 collective-permute-start.6
  247.6 1.4 reduce.3
  249.6 30.6 %attend_back.4 = (bf16[2,1024,768]{2,1,0:T(8,128)(2,1)}, bf16[2,1024,768]{2,1,0:T(8,128)(2,1)}, bf16[2,1024,768]{2,1,0:T(8,128)(2,1)}) custom-call(bf16[2,1024,768]{2,1,0:T(8,128)(2,1)} %bitcast.182, bf16[2,1024,1536]{2,1,0:T(8,128)(2,1)} %bitcast.146, bf16[2,1024,1536]{2,1,0:T(8,128)(2,1)} %bitcast.147, ...), custom_call_target="tpu_custom_call" | custom-call | flops 25769803776 | bytes 25165824 | tf_op jit(solution)/shard_map/attend_back/pallas_call | solution.py:419
  280.2 5.3 fusion
  285.6 2.3 copy-done.2
  287.9 1.7 dynamic-slice_bitcast_fusion
  289.6 1.5 collective-permute-start.5
  291.1 30.7 %attend_back.5 = (bf16[2,1024,768]{2,1,0:T(8,128)(2,1)}, bf16[2,1024,768]{2,1,0:T(8,128)(2,1)}, bf16[2,1024,768]{2,1,0:T(8,128)(2,1)}) custom-call(bf16[2,1024,768]{2,1,0:T(8,128)(2,1)} %get-tuple-element.223.refs_0_, bf16[2,1024,768]{2,1,0:T(8,128)(2,1)} %get-tuple-element.224.refs_1_, ...), custom_call_target="tpu_custom_call", output_to_operand_aliasing={{0}: (0, {}), {1}: (1, {}), {2}: (2, {})} | custom-call | flops 25769803776 | bytes 25165824 | tf_op jit(solution)/shard_map/attend_back/pallas_call | solution.py:419
  321.8 41.4 %return_rows.1 = (f32[4,512,768]{2,1,0:T(8,128)}, bf16[2,512,768]{2,1,0:T(8,128)(2,1)}, f32[2048,768]{1,0:T(8,128)}, bf16[2048,768]{1,0:T(8,128)(2,1)}, f32[8,76...) custom-call(s32[5]{0:T(128)} %pad_add_fusion.info_ref, bf16[2048,768]{1,0:T(8,128)(2,1)} %bitcast.189, ...), custom_call_target="tpu_custom_call" | custom-call | flops 19327352832 | bytes 41943040 | tf_op jit(solution)/shard_map/return_rows/pallas_call | solution.py:510
  363.2 3.2 fusion.2
  366.4 1.5 copy-done.3
  367.9 1.2 dynamic-slice_bitcast_fusion.2
  369.1 1.6 collective-permute-start.7
  370.7 1.1 collective-permute-start.12
  371.7 31.0 %attend_back.6 = (bf16[2,1024,768]{2,1,0:T(8,128)(2,1)}, bf16[2,1024,768]{2,1,0:T(8,128)(2,1)}, bf16[2,1024,768]{2,1,0:T(8,128)(2,1)}) custom-call(bf16[2,1024,2304]{2,1,0:T(8,128)(2,1)} %bitcast.126, bf16[2,1024,2304]{2,1,0:T(8,128)(2,1)} %bitcast.127, bf16[2,1024,2304]{2,1,0:T(8,128)(2,1)} %bitcast.128, ...), custom_call_target="tpu_custom_call" | custom-call | flops 25769803776 | bytes 25165824 | tf_op jit(solution)/shard_map/attend_back/pallas_call | solution.py:419
  402.7 1.2 bitcast_dynamic-update-slice_fusion
  404.0 1.0 copy-done.4
  405.0 1.7 fusion.4
  406.8 2.7 collective-permute-start.9
  409.5 2.3 fusion.3
  411.8 1.5 copy-done.5
  413.2 1.1 dynamic-slice_bitcast_fusion.3
  414.9 11.8 %leave.3 = (f32[4,512,768]{2,1,0:T(8,128)}, bf16[512,768]{1,0:T(8,128)(2,1)}, f32[8,768]{1,0:T(8,128)}) custom-call(s32[5]{0:T(128)} %pad_add_fusion.info_ref, bf16[2048,768]{1,0:T(8,128)(2,1)} %bitcast.132, bf16[2048,768]{1,0:T(8,128)(2,1)} %bitcast.136, bf16[2048,768]{1,0:T(8,128)(2,1)} %bitcast.140, bf16[2048,768]{1,0:T(8,128)(2,1)} %get-tuple-element.194.x_ref, ...), custom_call_target="tpu_custom_call" | custom-call | flops 7247757312 | bytes 16777216 | tf_op jit(solution)/shard_map/leave/pallas_call | solution.py:510
  426.7 1.0 collective-permute-start.11
  427.7 30.7 %attend_back.7 = (bf16[2,1024,768]{2,1,0:T(8,128)(2,1)}, bf16[2,1024,768]{2,1,0:T(8,128)(2,1)}, bf16[2,1024,768]{2,1,0:T(8,128)(2,1)}) custom-call(bf16[2,1024,768]{2,1,0:T(8,128)(2,1)} %get-tuple-element.256.refs_0_, bf16[2,1024,768]{2,1,0:T(8,128)(2,1)} %get-tuple-element.257.refs_1_, ...), custom_call_target="tpu_custom_call", output_to_operand_aliasing={{0}: (0, {}), {1}: (1, {}), {2}: (2, {})} | custom-call | flops 25769803776 | bytes 25165824 | tf_op jit(solution)/shard_map/attend_back/pallas_call | solution.py:419
  458.5 7.6 %leave.4 = (bf16[512,768]{1,0:T(8,128)(2,1)}, f32[8,768]{1,0:T(8,128)}) custom-call(s32[5]{0:T(128)} %pad_add_fusion.info_ref, bf16[2048,768]{1,0:T(8,128)(2,1)} %bitcast.133, bf16[2048,768]{1,0:T(8,128)(2,1)} %bitcast.137, bf16[2048,768]{1,0:T(8,128)(2,1)} %bitcast.141, bf16[2048,768]{1,0:T(8,128)(2,1)} %get-tuple-element.194.x_ref, ...), custom_call_target="tpu_custom_call" | custom-call | flops 3623878656 | bytes 8388608 | tf_op jit(solution)/shard_map/leave/pallas_call | solution.py:510
  466.1 1.0 collective-permute-start.17
  467.1 17.4 %last_weight.1 = (bf16[8,48,1152]{2,1,0:T(8,128)(2,1)}, bf16[8,48,1152]{2,1,0:T(8,128)(2,1)}, bf16[8,48,1152]{2,1,0:T(8,128)(2,1)}, bf16[8,48,1152]{2,1,0:T(8,128)(2,1)}) custom-call(s32[5]{0:T(128)} %pad_add_fusion.info_ref, bf16[2048,768]{1,0:T(8,128)(2,1)} %bitcast.134, bf16[2048,768]{1,0:T(8,128)(2,1)} %bitcast.138, bf16[2048,768]{1,0:T(8,128)(2,1)} %bitcast.142, ...), custom_call_target="tpu_custom_call" | custom-call | flops 28991029248 | bytes 20971520 | tf_op jit(solution)/shard_map/last_weight/pallas_call | solution.py:510
  485.1 1.2 fusion.8.kept_ref
  486.3 1.1 collective-permute-start.13
  487.4 1.9 fusion.5
  489.3 0.9 dynamic-slice_bitcast_fusion.7
  490.6 3.3 convert_dynamic-update-slice_fusion
  494.4 1.0 dynamic-slice_bitcast_fusion.10
  495.4 1.1 collective-permute-start.18
  496.5 1.0 dynamic-slice_bitcast_fusion.9
  497.5 2.0 collective-permute-start.19
  499.5 2.4 convert_dynamic-update-slice_fusion.2.refs_0_
  501.9 8.0 %leave.5 = (f32[4,512,768]{2,1,0:T(8,128)}, f32[8,768]{1,0:T(8,128)}) custom-call(s32[5]{0:T(128)} %pad_add_fusion.info_ref, bf16[2048,768]{1,0:T(8,128)(2,1)} %bitcast.135, bf16[2048,768]{1,0:T(8,128)(2,1)} %bitcast.139, bf16[2048,768]{1,0:T(8,128)(2,1)} %bitcast.143, bf16[2048,768]{1,0:T(8,128)(2,1)} %get-tuple-element.194.x_ref, ...), custom_call_target="tpu_custom_call", output_to_operand_aliasing={{0}: (8, {})} | custom-call | flops 3623878656 | bytes 8388608 | tf_op jit(solution)/shard_map/leave/pallas_call | solution.py:510
  509.9 4.9 collective-permute-done.19.refs_5_
  514.8 2.4 convert_dynamic-update-slice_fusion.1
  517.2 0.7 add_add_fusion
  518.0 1.4 pad_maximum_fusion.refs_6_
  519.4 42.4 %tail.1 = (f32[192,768]{1,0:T(8,128)}, f32[48,1152]{1,0:T(8,128)}, f32[48,1152]{1,0:T(8,128)}, f32[28,768]{1,0:T(8,128)}) custom-call(bf16[2,192,768]{2,1,0:T(8,128)(2,1)} %get-tuple-element.354.refs_0_, bf16[2,192,768]{2,1,0:T(8,128)(2,1)} %collective-permute-done.14.refs_1_, bf16[2,2,48,1152]{3,2,1,0:T(8,128)(2,1)} %get-tuple-element.358.refs_2_, ...), custom_call_target="tpu_custom_call" | custom-call | flops 20000000000 | bytes 10000000 | tf_op jit(solution)/shard_map/tail/pallas_call | solution.py:1149
  561.8 3.8 final.1
  (117 shorter events, 7.8 us)
Async XLA Ops:
  0.7 13.5 %copy-start = (s32[4,1]{0,1:T(1,128)S(1)}, s32[4,1]{0,1:T(1,128)}, u32[]{:S(2)}) copy-start(s32[4,1]{0,1:T(1,128)} %param.28) | copy-start | bytes 52
  0.7 8.5 %copy-start.22 = (f32[768]{0:T(1024)S(1)}, f32[768]{0:T(1024)}, u32[]{:S(2)}) copy-start(f32[768]{0:T(1024)} %param.39) | copy-start | bytes 9220
  0.7 8.5 %copy-start.23 = (f32[768]{0:T(1024)S(1)}, f32[768]{0:T(1024)}, u32[]{:S(2)}) copy-start(f32[768]{0:T(1024)} %param.38) | copy-start | bytes 9220
  0.7 8.5 %copy-start.24 = (f32[768]{0:T(1024)S(1)}, f32[768]{0:T(1024)}, u32[]{:S(2)}) copy-start(f32[768]{0:T(1024)} %param.32) | copy-start | bytes 9220
  0.7 8.5 %copy-start.25 = (f32[768]{0:T(1024)S(1)}, f32[768]{0:T(1024)}, u32[]{:S(2)}) copy-start(f32[768]{0:T(1024)} %param.31) | copy-start | bytes 9220
  0.7 8.5 %copy-start.32 = (f32[768]{0:T(1024)S(1)}, f32[768]{0:T(1024)}, u32[]{:S(2)}) copy-start(f32[768]{0:T(1024)} %param.35) | copy-start | bytes 9220
  0.7 8.5 %copy-start.33 = (f32[768]{0:T(1024)S(1)}, f32[768]{0:T(1024)}, u32[]{:S(2)}) copy-start(f32[768]{0:T(1024)} %param.34) | copy-start | bytes 9220
  0.7 9.1 %copy-start.21 = (f32[768]{0:T(1024)S(1)}, f32[768]{0:T(1024)}, u32[]{:S(2)}) copy-start(f32[768]{0:T(1024)} %param.43) | copy-start | bytes 9220
  0.8 9.7 %copy-start.26 = (f32[768]{0:T(1024)S(1)}, f32[768]{0:T(1024)}, u32[]{:S(2)}) copy-start(f32[768]{0:T(1024)} %param.37) | copy-start | bytes 9220
  0.8 9.7 %copy-start.27 = (f32[768]{0:T(1024)S(1)}, f32[768]{0:T(1024)}, u32[]{:S(2)}) copy-start(f32[768]{0:T(1024)} %param.41) | copy-start | bytes 9220
  0.8 9.7 %copy-start.20 = (s32[4,1,512]{2,1,0:T(1,128)S(1)}, s32[4,1,512]{2,1,0:T(1,128)}, u32[]{:S(2)}) copy-start(s32[4,1,512]{2,1,0:T(1,128)} %param.29) | copy-start | bytes 24580
  0.8 9.8 %copy-start.7 = (bf16[4,1,512,768]{3,2,1,0:T(8,128)(2,1)S(1)}, bf16[4,1,512,768]{3,2,1,0:T(8,128)(2,1)}, u32[]{:S(2)}) copy-start(bf16[4,1,512,768]{3,2,1,0:T(8,128)(2,1)} %param.30) | copy-start | bytes 9437188
  3.6 29.2 %collective-permute-start = (bf16[1,512,768]{2,1,0:T(8,128)(2,1)}, bf16[1,512,768]{2,1,0:T(8,128)(2,1)}, u32[]{:S(2)}, u32[]{:S(2)}) collective-permute-start(bf16[1,512,768]{2,1,0:T(8,128)(2,1)} %get-tuple-element.352), channel_id=1, source_target_pairs={{0,1},{1,0},{2,3},{3,2},{4,5},{5,4},{6,7},{7,6},{8,9},{9,8},{10,11... | collective-permute-start | bytes 2359304 | tf_op jit(solution)/shard_map/ppermute | solution.py:1271
  11.2 1.7 copy-start.6
  12.9 1.3 copy-start.28
  12.9 1.3 copy-start.29
  12.9 1.3 copy-start.30
  12.9 1.3 copy-start.31
  23.5 9.3 %copy-start.14 = (bf16[1,512,768]{2,1,0:T(8,128)(2,1)S(1)}, bf16[1,512,768]{2,1,0:T(8,128)(2,1)}, u32[]{:S(2)}) copy-start(bf16[1,512,768]{2,1,0:T(8,128)(2,1)} %get-tuple-element.189) | copy-start | bytes 2359300
  32.8 25.5 %collective-permute-start.1 = (bf16[1,512,768]{2,1,0:T(8,128)(2,1)S(1)}, bf16[1,512,768]{2,1,0:T(8,128)(2,1)S(1)}, u32[]{:S(2)}, u32[]{:S(2)}) collective-permute-start(bf16[1,512,768]{2,1,0:T(8,128)(2,1)S(1)} %copy-done.14), channel_id=1, source_target_pairs={{0,1},{1,0},{2,3},{3,2},{4,5},{5,4},{6,7},{7,6},{8,9},{9,8},{10,11... | collective-permute-start | bytes 2359304 | tf_op jit(solution)/shard_map/ppermute | solution.py:1271
  58.3 0.9 copy-start.13
  59.2 39.7 %collective-permute-start.2 = (bf16[2,512,768]{2,1,0:T(8,128)(2,1)}, bf16[2,512,768]{2,1,0:T(8,128)(2,1)S(1)}, u32[]{:S(2)}, u32[]{:S(2)}) collective-permute-start(bf16[2,512,768]{2,1,0:T(8,128)(2,1)} %dynamic-slice_bitcast_fusion.1), channel_id=1, source_target_pairs={{0,1},{1,0},{2,3},{3,2},{4,5},{5,4},{6,7},{7,6},{8,9},{9,8},{10,11... | collective-permute-start | bytes 4718600 | tf_op jit(solution)/shard_map/ppermute | solution.py:1271
  98.9 1.1 copy-start.10
  98.9 38.8 %collective-permute-start.3 = (bf16[2,512,768]{2,1,0:T(8,128)(2,1)}, bf16[2,512,768]{2,1,0:T(8,128)(2,1)}, u32[]{:S(2)}, u32[]{:S(2)}) collective-permute-start(bf16[2,512,768]{2,1,0:T(8,128)(2,1)} %constant_dynamic-slice_fusion), channel_id=1, source_target_pairs={{0,1},{1,0},{2,3},{3,2},{4,5},{5,4},{6,7},{7,6},{8,9},{9,8},{10,11... | collective-permute-start | bytes 4718600 | tf_op jit(solution)/shard_map/ppermute | solution.py:1271
  245.9 34.3 %collective-permute-start.4 = (bf16[2,2,2,432,768]{4,3,2,1,0:T(8,128)(2,1)}, bf16[2,2,2,432,768]{4,3,2,1,0:T(8,128)(2,1)}, u32[]{:S(2)}, u32[]{:S(2)}) collective-permute-start(bf16[2,2,2,432,768]{4,3,2,1,0:T(8,128)(2,1)} %bitcast.161), channel_id=1, source_target_pairs={{0,2},{2,0},{4,6},{6,4},{8,10},{10,8},{12,14},{14,12},{16,18},{18,... | collective-permute-start | bytes 15925256 | tf_op jit(solution)/shard_map/ppermute | solution.py:980
  246.1 117.1 %collective-permute-start.6 = (bf16[2,512,768]{2,1,0:T(8,128)(2,1)}, bf16[2,512,768]{2,1,0:T(8,128)(2,1)S(1)}, u32[]{:S(2)}, u32[]{:S(2)}) collective-permute-start(bf16[2,512,768]{2,1,0:T(8,128)(2,1)} %get-tuple-element.238), channel_id=1, source_target_pairs={{0,1},{1,0},{2,3},{3,2},{4,5},{5,4},{6,7},{7,6},{8,9},{9,8},{10,11... | collective-permute-start | bytes 4718600 | tf_op jit(solution)/shard_map/ppermute | solution.py:1363
  285.6 2.3 copy-start.2
  289.6 73.6 %collective-permute-start.5 = (bf16[2,2,432,768]{3,2,1,0:T(8,128)(2,1)}, bf16[2,2,432,768]{3,2,1,0:T(8,128)(2,1)}, u32[]{:S(2)}, u32[]{:S(2)}) collective-permute-start(bf16[2,2,432,768]{3,2,1,0:T(8,128)(2,1)} %dynamic-slice_bitcast_fusion), channel_id=1, source_target_pairs={{0,4},{2,6},{4,0},{6,2},{8,12},{10,14},{12,8},{14,10},{16,20},{18,... | collective-permute-start | bytes 7962632 | tf_op jit(solution)/shard_map/ppermute | solution.py:980
  366.4 1.5 copy-start.3
  369.1 34.9 %collective-permute-start.7 = (bf16[2,432,768]{2,1,0:T(8,128)(2,1)}, bf16[2,432,768]{2,1,0:T(8,128)(2,1)}, u32[]{:S(2)}, u32[]{:S(2)}) collective-permute-start(bf16[2,432,768]{2,1,0:T(8,128)(2,1)} %dynamic-slice_bitcast_fusion.2), channel_id=1, source_target_pairs={{0,8},{2,10},{4,12},{6,14},{8,0},{10,2},{12,4},{14,6},{16,24},{18,... | collective-permute-start | bytes 3981320 | tf_op jit(solution)/shard_map/ppermute | solution.py:980
  370.7 33.3 %collective-permute-start.8 = (bf16[2,2,2,192,768]{4,3,2,1,0:T(8,128)(2,1)}, bf16[2,2,2,192,768]{4,3,2,1,0:T(8,128)(2,1)}, u32[]{:S(2)}, u32[]{:S(2)}) collective-permute-start(bf16[2,2,2,192,768]{4,3,2,1,0:T(8,128)(2,1)} %bitcast.31), channel_id=1, source_target_pairs={{0,2},{2,0},{4,6},{6,4},{8,10},{10,8},{12,14},{14,12},{16,18},{18,... | collective-permute-start | bytes 7077896 | tf_op jit(solution)/shard_map/ppermute | solution.py:980
  370.7 87.8 %collective-permute-start.12 = (bf16[2,512,768]{2,1,0:T(8,128)(2,1)}, bf16[2,512,768]{2,1,0:T(8,128)(2,1)}, u32[]{:S(2)}, u32[]{:S(2)}) collective-permute-start(bf16[2,512,768]{2,1,0:T(8,128)(2,1)} %get-tuple-element.263), channel_id=1, source_target_pairs={{0,1},{1,0},{2,3},{3,2},{4,5},{5,4},{6,7},{7,6},{8,9},{9,8},{10,11... | collective-permute-start | bytes 4718600 | tf_op jit(solution)/shard_map/ppermute | solution.py:1391
  402.7 2.3 copy-start.4
  404.0 5.5 copy-start.9
  406.8 51.6 %collective-permute-start.9 = (bf16[432,768]{1,0:T(8,128)(2,1)S(1)}, bf16[432,768]{1,0:T(8,128)(2,1)}, u32[]{:S(2)}, u32[]{:S(2)}) collective-permute-start(bf16[432,768]{1,0:T(8,128)(2,1)S(1)} %dynamic-slice_bitcast_fusion.6), channel_id=1, source_target_pairs={{0,16},{2,18},{4,20},{6,22},{8,24},{10,26},{12,28},{14,30},{16,0},... | collective-permute-start | bytes 1990664 | tf_op jit(solution)/shard_map/ppermute | solution.py:980
  411.8 1.5 copy-start.5
  414.3 44.1 %collective-permute-start.10 = (bf16[2,2,192,768]{3,2,1,0:T(8,128)(2,1)}, bf16[2,2,192,768]{3,2,1,0:T(8,128)(2,1)}, u32[]{:S(2)}, u32[]{:S(2)}) collective-permute-start(bf16[2,2,192,768]{3,2,1,0:T(8,128)(2,1)} %dynamic-slice_bitcast_fusion.3), channel_id=1, source_target_pairs={{0,4},{2,6},{4,0},{6,2},{8,12},{10,14},{12,8},{14,10},{16,20},{18,... | collective-permute-start | bytes 3538952 | tf_op jit(solution)/shard_map/ppermute | solution.py:980
  426.7 31.8 %collective-permute-start.11 = (bf16[512,768]{1,0:T(8,128)(2,1)}, bf16[512,768]{1,0:T(8,128)(2,1)}, u32[]{:S(2)}, u32[]{:S(2)}) collective-permute-start(bf16[512,768]{1,0:T(8,128)(2,1)} %get-tuple-element.262), channel_id=1, source_target_pairs={{0,1},{1,0},{2,3},{3,2},{4,5},{5,4},{6,7},{7,6},{8,9},{9,8},{10,11... | collective-permute-start | bytes 2359304 | tf_op jit(solution)/shard_map/ppermute | solution.py:1407
  466.1 27.8 %collective-permute-start.17 = (bf16[512,768]{1,0:T(8,128)(2,1)}, bf16[512,768]{1,0:T(8,128)(2,1)}, u32[]{:S(2)}, u32[]{:S(2)}) collective-permute-start(bf16[512,768]{1,0:T(8,128)(2,1)} %get-tuple-element.269), channel_id=1, source_target_pairs={{0,1},{1,0},{2,3},{3,2},{4,5},{5,4},{6,7},{7,6},{8,9},{9,8},{10,11... | collective-permute-start | bytes 2359304 | tf_op jit(solution)/shard_map/ppermute | solution.py:1416
  484.5 9.4 %collective-permute-start.15 = (bf16[2,2,2,48,1152]{4,3,2,1,0:T(8,128)(2,1)}, bf16[2,2,2,48,1152]{4,3,2,1,0:T(8,128)(2,1)S(1)}, u32[]{:S(2)}, u32[]{:S(2)}) collective-permute-start(bf16[2,2,2,48,1152]{4,3,2,1,0:T(8,128)(2,1)} %bitcast.165), channel_id=1, source_target_pairs={{0,2},{2,0},{4,6},{6,4},{8,10},{10,8},{12,14},{14,12},{16,18},{18,... | collective-permute-start | bytes 2654216 | tf_op jit(solution)/shard_map/ppermute | solution.py:980
  484.6 9.4 %collective-permute-start.16 = (bf16[2,2,2,48,1152]{4,3,2,1,0:T(8,128)(2,1)}, bf16[2,2,2,48,1152]{4,3,2,1,0:T(8,128)(2,1)S(1)}, u32[]{:S(2)}, u32[]{:S(2)}) collective-permute-start(bf16[2,2,2,48,1152]{4,3,2,1,0:T(8,128)(2,1)} %bitcast.164), channel_id=1, source_target_pairs={{0,2},{2,0},{4,6},{6,4},{8,10},{10,8},{12,14},{14,12},{16,18},{18,... | collective-permute-start | bytes 2654216 | tf_op jit(solution)/shard_map/ppermute | solution.py:980
  486.3 7.6 %copy-start.8 = (bf16[432,768]{1,0:T(8,128)(2,1)}, bf16[432,768]{1,0:T(8,128)(2,1)S(1)}, u32[]{:S(2)}) copy-start(bf16[432,768]{1,0:T(8,128)(2,1)S(1)} %fusion.8.kept_ref) | copy-start | bytes 1990660
  486.3 23.6 %collective-permute-start.13 = (bf16[432,768]{1,0:T(8,128)(2,1)S(1)}, bf16[432,768]{1,0:T(8,128)(2,1)S(1)}, u32[]{:S(2)}, u32[]{:S(2)}) collective-permute-start(bf16[432,768]{1,0:T(8,128)(2,1)S(1)} %fusion.8.kept_ref), channel_id=1, source_target_pairs={{0,1},{1,0},{2,3},{3,2},{4,5},{5,4},{6,7},{7,6},{8,9},{9,8},{10,11... | collective-permute-start | bytes 1990664 | tf_op jit(solution)/shard_map/ppermute | solution.py:982
  489.3 4.7 copy-start.11
  489.3 4.7 copy-start.12
  490.2 19.7 %collective-permute-start.14 = (bf16[2,192,768]{2,1,0:T(8,128)(2,1)S(1)}, bf16[2,192,768]{2,1,0:T(8,128)(2,1)}, u32[]{:S(2)}, u32[]{:S(2)}) collective-permute-start(bf16[2,192,768]{2,1,0:T(8,128)(2,1)S(1)} %get-tuple-element.355), channel_id=1, source_target_pairs={{0,8},{2,10},{4,12},{6,14},{8,0},{10,2},{12,4},{14,6},{16,24},{18,... | collective-permute-start | bytes 1769480 | tf_op jit(solution)/shard_map/ppermute | solution.py:980
  495.4 14.5 %collective-permute-start.18 = (bf16[2,2,48,1152]{3,2,1,0:T(8,128)(2,1)}, bf16[2,2,48,1152]{3,2,1,0:T(8,128)(2,1)}, u32[]{:S(2)}, u32[]{:S(2)}) collective-permute-start(bf16[2,2,48,1152]{3,2,1,0:T(8,128)(2,1)} %get-tuple-element.359), channel_id=1, source_target_pairs={{0,4},{2,6},{4,0},{6,2},{8,12},{10,14},{12,8},{14,10},{16,20},{18,... | collective-permute-start | bytes 1327112 | tf_op jit(solution)/shard_map/ppermute | solution.py:980
  497.5 17.3 %collective-permute-start.19 = (bf16[2,2,48,1152]{3,2,1,0:T(8,128)(2,1)}, bf16[2,2,48,1152]{3,2,1,0:T(8,128)(2,1)}, u32[]{:S(2)}, u32[]{:S(2)}) collective-permute-start(bf16[2,2,48,1152]{3,2,1,0:T(8,128)(2,1)} %get-tuple-element.357), channel_id=1, source_target_pairs={{0,8},{2,10},{4,12},{6,14},{8,0},{10,2},{12,4},{14,6},{16,24},{18,... | collective-permute-start | bytes 1327112 | tf_op jit(solution)/shard_map/ppermute | solution.py:980
  501.9 15.3 %copy-start.17 = (f32[8,768]{1,0:T(8,128)S(1)}, f32[8,768]{1,0:T(8,128)}, u32[]{:S(2)}) copy-start(f32[8,768]{1,0:T(8,128)} %get-tuple-element.297) | copy-start | bytes 73732
  501.9 15.3 %copy-start.18 = (f32[8,768]{1,0:T(8,128)S(1)}, f32[8,768]{1,0:T(8,128)}, u32[]{:S(2)}) copy-start(f32[8,768]{1,0:T(8,128)} %get-tuple-element.298) | copy-start | bytes 73732
  501.9 16.0 %copy-start.16 = (f32[4,768]{1,0:T(4,128)S(1)}, f32[4,768]{1,0:T(4,128)}, u32[]{:S(2)}) copy-start(f32[4,768]{1,0:T(4,128)} %reshape.203) | copy-start | bytes 36868
  501.9 16.0 %copy-start.19 = (f32[8,768]{1,0:T(8,128)S(1)}, f32[8,768]{1,0:T(8,128)}, u32[]{:S(2)}) copy-start(f32[8,768]{1,0:T(8,128)} %get-tuple-element.300) | copy-start | bytes 73732
  509.9 51.8 %copy-start.15 = (bf16[432,768]{1,0:T(8,128)(2,1)}, bf16[432,768]{1,0:T(8,128)(2,1)S(1)}, u32[]{:S(2)}) copy-start(bf16[432,768]{1,0:T(8,128)(2,1)S(1)} %collective-permute-done.13.got_ref) | copy-start | bytes 1990660
  519.4 46.2 %copy-start.1 = (s32[4,1]{0,1:T(1,128)S(1)}, s32[4,1]{0,1:T(1,128)}, u32[]{:S(2)}) copy-start(s32[4,1]{0,1:T(1,128)} %param.28) | copy-start | bytes 52

commit v10 on v9

--- a/solution.py
+++ b/solution.py
@@ -1076,8 +1076,7 @@
             ins[2 * at][...].astype(jnp.float32) + ins[2 * at + 1][...].astype(jnp.float32)
         ).astype(jnp.bfloat16)
         totals.append(total)
-    sums = scratch.pop(0)
-    sums[...] = ins[2 * trees][...]
+    sums = ins[2 * trees][...]
     rounds = max(max(len(order) for order in orders) + 1, len(groups) + 1)
     for step in range(rounds):
         copies = []
@@ -1092,27 +1091,25 @@
                 got = scratch.pop(0)
                 copies.append((send(totals[at], got, other), at, None, got, outs[at]))
         summed = []
-        if step < len(groups):
-            for offset in groups[step]:
+        if step <= len(groups):
+            low = scratch.pop(0)
+            low[...] = sums.astype(jnp.bfloat16)
+            goals = [other]
+            if step < len(groups):
+                goals = [{"dp": partner(place, offset)} for offset in groups[step]]
+            for goal in goals:
                 got = scratch.pop(0)
-                summed.append((send(sums, got, {"dp": partner(place, offset)}), got))
-        elif step == len(groups):
-            got = scratch.pop(0)
-            summed.append((send(sums, got, other), got))
+                summed.append((send(low, got, goal), got))
         for copy, at, mine, got, target in copies:
             copy.wait()
             held = totals[at][...] if mine is None else totals[at][mine]
             total = held.astype(jnp.float32) + got[...].astype(jnp.float32)
             target[...] = total.astype(target.dtype)
             totals[at] = target
-        if summed:
-            target = scratch.pop(0) if step < len(groups) else outs[trees]
-            total = sums[...]
-            for copy, got in summed:
-                copy.wait()
-                total = total + got[...]
-            target[...] = total
-            sums = target
+        for copy, got in summed:
+            copy.wait()
+            sums = sums + got[...].astype(jnp.float32)
+    outs[trees][...] = sums
 
 
 def tail(trees, sums, parts):
@@ -1126,7 +1123,7 @@
         arrays += [tree.kept, tree.got]
     arrays += [sums]
     totals = [pltpu.VMEM(tree.kept.shape, jnp.bfloat16) for tree in trees]
-    scratch = totals + [pltpu.VMEM(sums.shape, jnp.float32)]
+    scratch = totals
     shapes = [tree.kept.shape for tree in trees]
     copies = 0
     for step in range(max(max(len(order) for order in orders) + 1, len(groups) + 1)):
@@ -1138,12 +1135,10 @@
             elif step == len(order):
                 scratch += [pltpu.VMEM(shapes[at], jnp.bfloat16)]
                 copies += 1
-        if step < len(groups):
-            scratch += [pltpu.VMEM(sums.shape, jnp.float32)] * (len(groups[step]) + 1)
-            copies += len(groups[step])
-        elif step == len(groups):
-            scratch += [pltpu.VMEM(sums.shape, jnp.float32)]
-            copies += 1
+        if step <= len(groups):
+            each = len(groups[step]) if step < len(groups) else 1
+            scratch += [pltpu.VMEM(sums.shape, jnp.bfloat16)] * (each + 1)
+            copies += each
     outs = [like(shape) for shape in shapes] + [like(sums.shape)]
     vmem = pl.BlockSpec(memory_space=pltpu.VMEM)
     return pl.pallas_call(
@@ -1419,12 +1414,13 @@
     late_trees = [Tree(*late_parts[0:2], low_first), Tree(*late_parts[2:4], second_first)]
     exchange(late_trees)
     (grads, _), back = lax.optimization_barrier(((grads, late_parts[0]), back))
-    grads = settle(late_trees, grads)
-    exchange(late_trees)
+    grads = settle(mid_trees + late_trees, grads)
+    exchange(mid_trees + late_trees)
     input_grads, new_sums = leave_now(held - 1, (0,), kept, grads)
     input_grads, new_sums = receive(trees + late_trees, (input_grads, new_sums))
     sums = jnp.concatenate(
-        [sums + new_sums, feed_sums, return_sums, hidden_sums.reshape(-1, width)], axis=0
+        [sums + new_sums, feed_sums, return_sums, hidden_sums.reshape(-1, width), jnp.zeros((4, width))],
+        axis=0,
     )
     mid_total, *late_totals, sums = tail(mid_trees + late_trees, sums, parts)
     input_grads = give(input_grads, back[None], held - 1)

time: 573 us -> 577 us (level)
  waiting for transfers between devices: 4.92 us -> 17.8 us
  Pallas kernels: 480 us -> 472 us
    ppermute x11 -> x12, waiting for transfers between devices: 4.9 us -> 17.8 us  [exchange(): self.got = lax.ppermute(self.sent, 'dp', pairs)]
    pallas_call x1, Pallas kernels: 42.4 us -> 34.2 us  [tail(): pl.pallas_call(functools.partial(tail_kernel, orders=orders, groups=group...]
    convert_element_type x7 -> x8, other arithmetic: 16.1 us -> 16.3 us  [add(): total = total.astype(jnp.bfloat16)]
  transfers between devices with their start and end apart: 20 -> 21, of which waited for: 1 -> 3; matrix products, arithmetic and copies ran while one was open for 6% -> 6% of each run, Pallas kernels for 56% -> 56%
where the time goes in v10:
time: 577 us; the launch traced here: 571 us
  Pallas kernels  472 us (82%)
  local copies, waits for them, and re-layouts  31 us (5%)
  other arithmetic  28.5 us (5%)
  starting transfers between devices  19.6 us (3%)
  waiting for transfers between devices  17.8 us (3%)
    pallas_call x13, Pallas kernels, kernel_call(): pl.pallas_call(kernel, grid_spec=pltpu.PrefetchScalarGridSpec(num_scalar_...  246 us
    pallas_call x4, Pallas kernels, attend_back(): pl.pallas_call(kernel, grid=size, in_specs=[pl.BlockSpec(memory_space=pl....  123 us
    pallas_call x3, Pallas kernels, attend(): pl.pallas_call(functools.partial(attend_kernel, use_mask=use_mask, start=...  68.5 us
    pallas_call x1, Pallas kernels, tail(): pl.pallas_call(functools.partial(tail_kernel, orders=orders, groups=group...  34.2 us
    ppermute x12, waiting for transfers between devices, exchange(): self.got = lax.ppermute(self.sent, 'dp', pairs)  17.8 us
    convert_element_type x8, other arithmetic, add(): total = total.astype(jnp.bfloat16)  16.3 us
  transfers between devices with their start and end apart: 21, of which 3 were waited for; matrix products, arithmetic and copies ran while one was open for 6% of the time, Pallas kernels for 56%

profile of v10, /device:TPU:0, one launch (start us, length us, event | category | flops | bytes accessed | tf_op | source)
XLA Modules:
  0.0 570.5 jit_solution(3258834937841979387)
XLA Ops:
  0.8 2.8 dynamic-slice_bitcast_fusion.4
  3.6 3.0 collective-permute-start
  6.5 2.7 dynamic-slice_bitcast_fusion.1
  11.2 1.7 copy-done.6
  12.9 1.3 constant_dynamic-slice_fusion
  17.0 6.6 %enter.6 = (bf16[2048,768]{1,0:T(8,128)(2,1)}, bf16[2048,1536]{1,0:T(8,128)(2,1)}) custom-call(s32[5]{0:T(128)} %pad_add_fusion.info_ref, bf16[4,512,768]{2,1,0:T(8,128)(2,1)} %bitcast.164, bf16[768,1536]{1,0:T(8,128)(2,1)} %wi_ref.3, f32[8,768]{1,0:T(8,128)} %get-tuple-element.363.vec_ref, f32[1,1536]{1,0:T(1,128)} %broadcast_in_dim.45.bias_ref), custom_call_target="tpu_custom_call" | custom-call | flops 2415919104 | bytes 6291456 | tf_op jit(solution)/shard_map/enter/pallas_call | solution.py:510
  23.6 9.3 %enter.5 = (bf16[2048,768]{1,0:T(8,128)(2,1)}, bf16[2048,2304]{1,0:T(8,128)(2,1)}) custom-call(s32[5]{0:T(128)} %pad_add_fusion.info_ref, bf16[4,512,768]{2,1,0:T(8,128)(2,1)} %bitcast.163, bf16[768,2304]{1,0:T(8,128)(2,1)} %w_ref.15, f32[8,768]{1,0:T(8,128)} %get-tuple-element.363.vec_ref, f32[1,2304]{1,0:T(1,128)} %broadcast_in_dim.44.bias_ref), custom_call_target="tpu_custom_call" | custom-call | flops 3623878656 | bytes 7864320 | tf_op jit(solution)/shard_map/enter/pallas_call | solution.py:510
  32.9 6.6 %enter.7 = (bf16[2048,768]{1,0:T(8,128)(2,1)}, bf16[2048,2304]{1,0:T(8,128)(2,1)}) custom-call(s32[5]{0:T(128)} %pad_add_fusion.info_ref, bf16[1,512,768]{2,1,0:T(8,128)(2,1)} %collective-permute-done.source_ref, bf16[768,2304]{1,0:T(8,128)(2,1)} %w_ref.15, f32[8,768]{1,0:T(8,128)} %get-tuple-element.363.vec_ref, ...), custom_call_target="tpu_custom_call", output_to_operand_aliasing={{0}: (5, {}), {1}: (6, {})} | custom-call | flops 1811939328 | bytes 3932160 | tf_op jit(solution)/shard_map/enter/pallas_call | solution.py:510
  39.5 18.4 %attend.3 = (bf16[2,1024,768]{2,1,0:T(8,128)(2,1)}, bf16[2,12,1024,1024]{3,2,1,0:T(8,128)(2,1)}, f32[2,6,2,1024]{3,2,1,0:T(2,128)}) custom-call(s32[5]{0:T(128)} %pad_add_fusion.info_ref, bf16[2,1024,2304]{2,1,0:T(8,128)(2,1)} %bitcast.125, bf16[2,1024,2304]{2,1,0:T(8,128)(2,1)} %bitcast.126, bf16[2,1024,2304]{2,1,0:T(8,128)(2,1)} %bitcast.127), custom_call_target="tpu_custom_call" | custom-call | flops 12884901888 | bytes 25165824 | tf_op jit(solution)/shard_map/attend/pallas_call | solution.py:343
  58.0 0.9 copy-done.13
  58.8 2.0 collective-permute-start.2
  60.8 6.7 %enter.8 = (bf16[2048,768]{1,0:T(8,128)(2,1)}, bf16[2048,2304]{1,0:T(8,128)(2,1)}) custom-call(s32[5]{0:T(128)} %pad_add_fusion.info_ref, bf16[1,512,768]{2,1,0:T(8,128)(2,1)} %copy-done.13, bf16[768,2304]{1,0:T(8,128)(2,1)} %w_ref.15, f32[8,768]{1,0:T(8,128)} %get-tuple-element.363.vec_ref, ...), custom_call_target="tpu_custom_call", output_to_operand_aliasing={{0}: (5, {}), {1}: (6, {})} | custom-call | flops 1811939328 | bytes 3932160 | tf_op jit(solution)/shard_map/enter/pallas_call | solution.py:510
  67.5 19.0 %attend.4 = (bf16[2,1024,768]{2,1,0:T(8,128)(2,1)}, bf16[2,12,1024,1024]{3,2,1,0:T(8,128)(2,1)}, f32[2,6,2,1024]{3,2,1,0:T(2,128)}) custom-call(s32[5]{0:T(128)} %pad_add_fusion.info_ref, bf16[2,1024,2304]{2,1,0:T(8,128)(2,1)} %bitcast.128, bf16[2,1024,2304]{2,1,0:T(8,128)(2,1)} %bitcast.129, ...), custom_call_target="tpu_custom_call", output_to_operand_aliasing={{0}: (4, {}), {1}: (5, {}), {2}: (6, {})} | custom-call | flops 12884901888 | bytes 25165824 | tf_op jit(solution)/shard_map/attend/pallas_call | solution.py:343
  86.5 12.5 %middle.1 = (f32[2048,768]{1,0:T(8,128)}, bf16[2048,768]{1,0:T(8,128)(2,1)}) custom-call(s32[5]{0:T(128)} %pad_add_fusion.info_ref, bf16[2048,768]{1,0:T(8,128)(2,1)} %get-tuple-element.195.x_ref, bf16[2048,768]{1,0:T(8,128)(2,1)} %bitcast.158, bf16[768,768]{1,0:T(8,128)(2,1)} %wo_ref.5, bf16[768,768]{1,0:T(8,128)(2,1)} %wq_ref.3, f32[8,768]{1,0:T(8,128)} %concatenate.28.vec_ref), custom_call_target="tpu_custom_call" | custom-call | flops 4831838208 | bytes 15728640 | tf_op jit(solution)/shard_map/middle/pallas_call | solution.py:510
  99.1 1.1 copy-done.10
  100.2 6.6 %enter.9 = (bf16[2048,768]{1,0:T(8,128)(2,1)}, bf16[2048,1536]{1,0:T(8,128)(2,1)}) custom-call(s32[5]{0:T(128)} %pad_add_fusion.info_ref, bf16[2,512,768]{2,1,0:T(8,128)(2,1)} %copy-done.10, bf16[768,1536]{1,0:T(8,128)(2,1)} %wi_ref.3, f32[8,768]{1,0:T(8,128)} %get-tuple-element.363.vec_ref, ...), custom_call_target="tpu_custom_call", output_to_operand_aliasing={{0}: (5, {}), {1}: (6, {})} | custom-call | flops 2415919104 | bytes 6291456 | tf_op jit(solution)/shard_map/enter/pallas_call | solution.py:510
  106.8 31.1 %attend.5 = (bf16[2,1024,768]{2,1,0:T(8,128)(2,1)}, bf16[2,12,1024,1024]{3,2,1,0:T(8,128)(2,1)}, f32[2,6,2,1024]{3,2,1,0:T(2,128)}) custom-call(s32[5]{0:T(128)} %pad_add_fusion.info_ref, bf16[2,1024,768]{2,1,0:T(8,128)(2,1)} %bitcast.188, bf16[2,1024,1536]{2,1,0:T(8,128)(2,1)} %bitcast.149, bf16[2,1024,1536]{2,1,0:T(8,128)(2,1)} %bitcast.150), custom_call_target="tpu_custom_call" | custom-call | flops 25769803776 | bytes 50331648 | tf_op jit(solution)/shard_map/attend/pallas_call | solution.py:343
  137.9 108.1 %feed.1 = (bf16[4,512,768]{2,1,0:T(8,128)(2,1)}, bf16[2,512,768]{2,1,0:T(8,128)(2,1)}, f32[2048,768]{1,0:T(8,128)}, bf16[2048,768]{1,0:T(8,128)(2,1)}, f32[8,768...) custom-call(s32[5]{0:T(128)} %pad_add_fusion.info_ref, ...), custom_call_target="tpu_custom_call" | custom-call | flops 65229815808 | bytes 62914560 | tf_op jit(solution)/shard_map/feed/pallas_call | solution.py:510
  246.2 1.0 collective-permute-start.6
  247.7 1.4 reduce.3
  249.7 30.6 %attend_back.4 = (bf16[2,1024,768]{2,1,0:T(8,128)(2,1)}, bf16[2,1024,768]{2,1,0:T(8,128)(2,1)}, bf16[2,1024,768]{2,1,0:T(8,128)(2,1)}) custom-call(bf16[2,1024,768]{2,1,0:T(8,128)(2,1)} %bitcast.189, bf16[2,1024,1536]{2,1,0:T(8,128)(2,1)} %bitcast.151, bf16[2,1024,1536]{2,1,0:T(8,128)(2,1)} %bitcast.152, ...), custom_call_target="tpu_custom_call" | custom-call | flops 25769803776 | bytes 25165824 | tf_op jit(solution)/shard_map/attend_back/pallas_call | solution.py:419
  280.3 5.3 fusion
  285.7 2.3 copy-done.2
  288.0 1.7 dynamic-slice_bitcast_fusion
  289.7 1.5 collective-permute-start.5
  291.2 30.6 %attend_back.5 = (bf16[2,1024,768]{2,1,0:T(8,128)(2,1)}, bf16[2,1024,768]{2,1,0:T(8,128)(2,1)}, bf16[2,1024,768]{2,1,0:T(8,128)(2,1)}) custom-call(bf16[2,1024,768]{2,1,0:T(8,128)(2,1)} %get-tuple-element.224.refs_0_, bf16[2,1024,768]{2,1,0:T(8,128)(2,1)} %get-tuple-element.225.refs_1_, ...), custom_call_target="tpu_custom_call", output_to_operand_aliasing={{0}: (0, {}), {1}: (1, {}), {2}: (2, {})} | custom-call | flops 25769803776 | bytes 25165824 | tf_op jit(solution)/shard_map/attend_back/pallas_call | solution.py:419
  321.8 41.4 %return_rows.1 = (f32[4,512,768]{2,1,0:T(8,128)}, bf16[2,512,768]{2,1,0:T(8,128)(2,1)}, f32[2048,768]{1,0:T(8,128)}, bf16[2048,768]{1,0:T(8,128)(2,1)}, f32[8,76...) custom-call(s32[5]{0:T(128)} %pad_add_fusion.info_ref, bf16[2048,768]{1,0:T(8,128)(2,1)} %bitcast.196, ...), custom_call_target="tpu_custom_call" | custom-call | flops 19327352832 | bytes 41943040 | tf_op jit(solution)/shard_map/return_rows/pallas_call | solution.py:510
  363.3 3.2 fusion.2
  366.5 1.5 copy-done.3
  368.0 1.2 dynamic-slice_bitcast_fusion.2
  369.1 1.6 collective-permute-start.7
  370.7 1.0 collective-permute-start.12
  371.7 31.0 %attend_back.6 = (bf16[2,1024,768]{2,1,0:T(8,128)(2,1)}, bf16[2,1024,768]{2,1,0:T(8,128)(2,1)}, bf16[2,1024,768]{2,1,0:T(8,128)(2,1)}) custom-call(bf16[2,1024,2304]{2,1,0:T(8,128)(2,1)} %bitcast.131, bf16[2,1024,2304]{2,1,0:T(8,128)(2,1)} %bitcast.132, bf16[2,1024,2304]{2,1,0:T(8,128)(2,1)} %bitcast.133, ...), custom_call_target="tpu_custom_call" | custom-call | flops 25769803776 | bytes 25165824 | tf_op jit(solution)/shard_map/attend_back/pallas_call | solution.py:419
  402.8 1.2 bitcast_dynamic-update-slice_fusion
  404.0 1.0 copy-done.4
  405.1 1.7 fusion.4
  406.9 3.2 collective-permute-start.9
  410.0 2.3 fusion.3
  412.3 1.4 copy-done.5
  413.8 1.1 dynamic-slice_bitcast_fusion.3
  414.9 11.8 %leave.3 = (f32[4,512,768]{2,1,0:T(8,128)}, bf16[512,768]{1,0:T(8,128)(2,1)}, f32[8,768]{1,0:T(8,128)}) custom-call(s32[5]{0:T(128)} %pad_add_fusion.info_ref, bf16[2048,768]{1,0:T(8,128)(2,1)} %bitcast.137, bf16[2048,768]{1,0:T(8,128)(2,1)} %bitcast.141, bf16[2048,768]{1,0:T(8,128)(2,1)} %bitcast.145, bf16[2048,768]{1,0:T(8,128)(2,1)} %get-tuple-element.195.x_ref, ...), custom_call_target="tpu_custom_call" | custom-call | flops 7247757312 | bytes 16777216 | tf_op jit(solution)/shard_map/leave/pallas_call | solution.py:510
  426.7 1.0 collective-permute-start.11
  427.7 30.7 %attend_back.7 = (bf16[2,1024,768]{2,1,0:T(8,128)(2,1)}, bf16[2,1024,768]{2,1,0:T(8,128)(2,1)}, bf16[2,1024,768]{2,1,0:T(8,128)(2,1)}) custom-call(bf16[2,1024,768]{2,1,0:T(8,128)(2,1)} %get-tuple-element.257.refs_0_, bf16[2,1024,768]{2,1,0:T(8,128)(2,1)} %get-tuple-element.258.refs_1_, ...), custom_call_target="tpu_custom_call", output_to_operand_aliasing={{0}: (0, {}), {1}: (1, {}), {2}: (2, {})} | custom-call | flops 25769803776 | bytes 25165824 | tf_op jit(solution)/shard_map/attend_back/pallas_call | solution.py:419
  458.4 7.6 %leave.4 = (bf16[512,768]{1,0:T(8,128)(2,1)}, f32[8,768]{1,0:T(8,128)}) custom-call(s32[5]{0:T(128)} %pad_add_fusion.info_ref, bf16[2048,768]{1,0:T(8,128)(2,1)} %bitcast.138, bf16[2048,768]{1,0:T(8,128)(2,1)} %bitcast.142, bf16[2048,768]{1,0:T(8,128)(2,1)} %bitcast.146, bf16[2048,768]{1,0:T(8,128)(2,1)} %get-tuple-element.195.x_ref, ...), custom_call_target="tpu_custom_call" | custom-call | flops 3623878656 | bytes 8388608 | tf_op jit(solution)/shard_map/leave/pallas_call | solution.py:510
  466.1 1.0 collective-permute-start.17
  467.1 1.2 fusion.8.kept_ref
  468.3 1.1 collective-permute-start.13
  469.4 17.4 %last_weight.1 = (bf16[8,48,1152]{2,1,0:T(8,128)(2,1)}, bf16[8,48,1152]{2,1,0:T(8,128)(2,1)}, bf16[8,48,1152]{2,1,0:T(8,128)(2,1)}, bf16[8,48,1152]{2,1,0:T(8,128)(2,1)}) custom-call(s32[5]{0:T(128)} %pad_add_fusion.info_ref, bf16[2048,768]{1,0:T(8,128)(2,1)} %bitcast.139, bf16[2048,768]{1,0:T(8,128)(2,1)} %bitcast.143, bf16[2048,768]{1,0:T(8,128)(2,1)} %bitcast.147, ...), custom_call_target="tpu_custom_call" | custom-call | flops 28991029248 | bytes 20971520 | tf_op jit(solution)/shard_map/last_weight/pallas_call | solution.py:510
  487.4 1.9 fusion.5
  489.5 2.5 convert_dynamic-update-slice_fusion.2.refs_0_
  492.0 3.3 convert_dynamic-update-slice_fusion
  495.3 9.5 %collective-permute-done.14 = bf16[2,192,768]{2,1,0:T(8,128)(2,1)S(1)} collective-permute-done((bf16[2,192,768]{2,1,0:T(8,128)(2,1)S(1)}, bf16[2,192,768]{2,1,0:T(8,128)(2,1)S(1)}, u32[]{:S(2)}, u32[]{:S(2)}) %collective-permute-start.14) | collective-permute-done | bytes 589856 | tf_op jit(solution)/shard_map/ppermute | solution.py:980
  505.3 0.8 dynamic-slice_bitcast_fusion.9
  506.1 1.9 collective-permute-start.19
  508.0 1.0 dynamic-slice_bitcast_fusion.8
  509.5 0.9 dynamic-slice_bitcast_fusion.12
  510.4 8.0 %leave.5 = (f32[4,512,768]{2,1,0:T(8,128)}, f32[8,768]{1,0:T(8,128)}) custom-call(s32[5]{0:T(128)} %pad_add_fusion.info_ref, bf16[2048,768]{1,0:T(8,128)(2,1)} %bitcast.140, bf16[2048,768]{1,0:T(8,128)(2,1)} %bitcast.144, bf16[2048,768]{1,0:T(8,128)(2,1)} %bitcast.148, bf16[2048,768]{1,0:T(8,128)(2,1)} %get-tuple-element.195.x_ref, ...), custom_call_target="tpu_custom_call", output_to_operand_aliasing={{0}: (8, {})} | custom-call | flops 3623878656 | bytes 8388608 | tf_op jit(solution)/shard_map/leave/pallas_call | solution.py:510
  518.4 6.4 %collective-permute-done.18.refs_1_ = bf16[192,768]{1,0:T(8,128)(2,1)} collective-permute-done((bf16[192,768]{1,0:T(8,128)(2,1)}, bf16[192,768]{1,0:T(8,128)(2,1)}, u32[]{:S(2)}, u32[]{:S(2)}) %collective-permute-start.18) | collective-permute-done | bytes 294944 | tf_op jit(solution)/shard_map/ppermute | solution.py:980
  524.8 1.9 collective-permute-done.20.refs_5_
  526.7 2.4 convert_dynamic-update-slice_fusion.1
  529.1 0.7 add_add_fusion
  529.8 2.5 concatenate.31.refs_6_
  532.3 34.2 %tail.1 = (f32[192,768]{1,0:T(8,128)}, f32[48,1152]{1,0:T(8,128)}, f32[48,1152]{1,0:T(8,128)}, f32[32,768]{1,0:T(8,128)}) custom-call(bf16[192,768]{1,0:T(8,128)(2,1)} %get-tuple-element.360.refs_0_, bf16[192,768]{1,0:T(8,128)(2,1)} %collective-permute-done.18.refs_1_, bf16[2,2,48,1152]{3,2,1,0:T(8,128)(2,1)} %get-tuple-element.358.refs_2_, ...), custom_call_target="tpu_custom_call" | custom-call | flops 20000000000 | bytes 10000000 | tf_op jit(solution)/shard_map/tail/pallas_call | solution.py:1144
  566.6 3.8 final.1
  (127 shorter events, 7.9 us)
Async XLA Ops:
  0.7 13.6 %copy-start = (s32[4,1]{0,1:T(1,128)S(1)}, s32[4,1]{0,1:T(1,128)}, u32[]{:S(2)}) copy-start(s32[4,1]{0,1:T(1,128)} %param.28) | copy-start | bytes 52
  0.7 8.5 %copy-start.25 = (f32[768]{0:T(1024)S(1)}, f32[768]{0:T(1024)}, u32[]{:S(2)}) copy-start(f32[768]{0:T(1024)} %param.39) | copy-start | bytes 9220
  0.7 8.5 %copy-start.26 = (f32[768]{0:T(1024)S(1)}, f32[768]{0:T(1024)}, u32[]{:S(2)}) copy-start(f32[768]{0:T(1024)} %param.38) | copy-start | bytes 9220
  0.7 8.5 %copy-start.27 = (f32[768]{0:T(1024)S(1)}, f32[768]{0:T(1024)}, u32[]{:S(2)}) copy-start(f32[768]{0:T(1024)} %param.32) | copy-start | bytes 9220
  0.7 8.5 %copy-start.28 = (f32[768]{0:T(1024)S(1)}, f32[768]{0:T(1024)}, u32[]{:S(2)}) copy-start(f32[768]{0:T(1024)} %param.31) | copy-start | bytes 9220
  0.7 8.5 %copy-start.35 = (f32[768]{0:T(1024)S(1)}, f32[768]{0:T(1024)}, u32[]{:S(2)}) copy-start(f32[768]{0:T(1024)} %param.35) | copy-start | bytes 9220
  0.7 8.5 %copy-start.36 = (f32[768]{0:T(1024)S(1)}, f32[768]{0:T(1024)}, u32[]{:S(2)}) copy-start(f32[768]{0:T(1024)} %param.34) | copy-start | bytes 9220
  0.7 9.1 %copy-start.24 = (f32[768]{0:T(1024)S(1)}, f32[768]{0:T(1024)}, u32[]{:S(2)}) copy-start(f32[768]{0:T(1024)} %param.43) | copy-start | bytes 9220
  0.8 9.7 %copy-start.29 = (f32[768]{0:T(1024)S(1)}, f32[768]{0:T(1024)}, u32[]{:S(2)}) copy-start(f32[768]{0:T(1024)} %param.37) | copy-start | bytes 9220
  0.8 9.7 %copy-start.30 = (f32[768]{0:T(1024)S(1)}, f32[768]{0:T(1024)}, u32[]{:S(2)}) copy-start(f32[768]{0:T(1024)} %param.41) | copy-start | bytes 9220
  0.8 9.7 %copy-start.23 = (s32[4,1,512]{2,1,0:T(1,128)S(1)}, s32[4,1,512]{2,1,0:T(1,128)}, u32[]{:S(2)}) copy-start(s32[4,1,512]{2,1,0:T(1,128)} %param.29) | copy-start | bytes 24580
  0.8 9.8 %copy-start.7 = (bf16[4,1,512,768]{3,2,1,0:T(8,128)(2,1)S(1)}, bf16[4,1,512,768]{3,2,1,0:T(8,128)(2,1)}, u32[]{:S(2)}) copy-start(bf16[4,1,512,768]{3,2,1,0:T(8,128)(2,1)} %param.30) | copy-start | bytes 9437188
  3.6 29.3 %collective-permute-start = (bf16[1,512,768]{2,1,0:T(8,128)(2,1)}, bf16[1,512,768]{2,1,0:T(8,128)(2,1)}, u32[]{:S(2)}, u32[]{:S(2)}) collective-permute-start(bf16[1,512,768]{2,1,0:T(8,128)(2,1)} %get-tuple-element.354), channel_id=1, source_target_pairs={{0,1},{1,0},{2,3},{3,2},{4,5},{5,4},{6,7},{7,6},{8,9},{9,8},{10,11... | collective-permute-start | bytes 2359304 | tf_op jit(solution)/shard_map/ppermute | solution.py:1266
  11.2 1.7 copy-start.6
  12.9 1.3 copy-start.31
  12.9 1.3 copy-start.32
  12.9 1.3 copy-start.33
  12.9 1.3 copy-start.34
  15.0 0.6 copy-start.16
  23.6 9.3 %copy-start.14 = (bf16[1,512,768]{2,1,0:T(8,128)(2,1)S(1)}, bf16[1,512,768]{2,1,0:T(8,128)(2,1)}, u32[]{:S(2)}) copy-start(bf16[1,512,768]{2,1,0:T(8,128)(2,1)} %get-tuple-element.190) | copy-start | bytes 2359300
  32.8 25.1 %collective-permute-start.1 = (bf16[1,512,768]{2,1,0:T(8,128)(2,1)S(1)}, bf16[1,512,768]{2,1,0:T(8,128)(2,1)S(1)}, u32[]{:S(2)}, u32[]{:S(2)}) collective-permute-start(bf16[1,512,768]{2,1,0:T(8,128)(2,1)S(1)} %copy-done.14), channel_id=1, source_target_pairs={{0,1},{1,0},{2,3},{3,2},{4,5},{5,4},{6,7},{7,6},{8,9},{9,8},{10,11... | collective-permute-start | bytes 2359304 | tf_op jit(solution)/shard_map/ppermute | solution.py:1266
  57.9 0.9 copy-start.13
  58.8 40.2 %collective-permute-start.2 = (bf16[2,512,768]{2,1,0:T(8,128)(2,1)}, bf16[2,512,768]{2,1,0:T(8,128)(2,1)S(1)}, u32[]{:S(2)}, u32[]{:S(2)}) collective-permute-start(bf16[2,512,768]{2,1,0:T(8,128)(2,1)} %dynamic-slice_bitcast_fusion.1), channel_id=1, source_target_pairs={{0,1},{1,0},{2,3},{3,2},{4,5},{5,4},{6,7},{7,6},{8,9},{9,8},{10,11... | collective-permute-start | bytes 4718600 | tf_op jit(solution)/shard_map/ppermute | solution.py:1266
  99.0 1.1 copy-start.10
  99.1 38.8 %collective-permute-start.3 = (bf16[2,512,768]{2,1,0:T(8,128)(2,1)}, bf16[2,512,768]{2,1,0:T(8,128)(2,1)}, u32[]{:S(2)}, u32[]{:S(2)}) collective-permute-start(bf16[2,512,768]{2,1,0:T(8,128)(2,1)} %constant_dynamic-slice_fusion), channel_id=1, source_target_pairs={{0,1},{1,0},{2,3},{3,2},{4,5},{5,4},{6,7},{7,6},{8,9},{9,8},{10,11... | collective-permute-start | bytes 4718600 | tf_op jit(solution)/shard_map/ppermute | solution.py:1266
  246.0 34.4 %collective-permute-start.4 = (bf16[2,2,2,432,768]{4,3,2,1,0:T(8,128)(2,1)}, bf16[2,2,2,432,768]{4,3,2,1,0:T(8,128)(2,1)}, u32[]{:S(2)}, u32[]{:S(2)}) collective-permute-start(bf16[2,2,2,432,768]{4,3,2,1,0:T(8,128)(2,1)} %bitcast.168), channel_id=1, source_target_pairs={{0,2},{2,0},{4,6},{6,4},{8,10},{10,8},{12,14},{14,12},{16,18},{18,... | collective-permute-start | bytes 15925256 | tf_op jit(solution)/shard_map/ppermute | solution.py:980
  246.2 117.1 %collective-permute-start.6 = (bf16[2,512,768]{2,1,0:T(8,128)(2,1)}, bf16[2,512,768]{2,1,0:T(8,128)(2,1)S(1)}, u32[]{:S(2)}, u32[]{:S(2)}) collective-permute-start(bf16[2,512,768]{2,1,0:T(8,128)(2,1)} %get-tuple-element.239), channel_id=1, source_target_pairs={{0,1},{1,0},{2,3},{3,2},{4,5},{5,4},{6,7},{7,6},{8,9},{9,8},{10,11... | collective-permute-start | bytes 4718600 | tf_op jit(solution)/shard_map/ppermute | solution.py:1358
  285.7 2.3 copy-start.2
  289.7 73.6 %collective-permute-start.5 = (bf16[2,2,432,768]{3,2,1,0:T(8,128)(2,1)}, bf16[2,2,432,768]{3,2,1,0:T(8,128)(2,1)}, u32[]{:S(2)}, u32[]{:S(2)}) collective-permute-start(bf16[2,2,432,768]{3,2,1,0:T(8,128)(2,1)} %dynamic-slice_bitcast_fusion), channel_id=1, source_target_pairs={{0,4},{2,6},{4,0},{6,2},{8,12},{10,14},{12,8},{14,10},{16,20},{18,... | collective-permute-start | bytes 7962632 | tf_op jit(solution)/shard_map/ppermute | solution.py:980
  366.5 1.5 copy-start.3
  369.1 34.9 %collective-permute-start.7 = (bf16[2,432,768]{2,1,0:T(8,128)(2,1)}, bf16[2,432,768]{2,1,0:T(8,128)(2,1)}, u32[]{:S(2)}, u32[]{:S(2)}) collective-permute-start(bf16[2,432,768]{2,1,0:T(8,128)(2,1)} %dynamic-slice_bitcast_fusion.2), channel_id=1, source_target_pairs={{0,8},{2,10},{4,12},{6,14},{8,0},{10,2},{12,4},{14,6},{16,24},{18,... | collective-permute-start | bytes 3981320 | tf_op jit(solution)/shard_map/ppermute | solution.py:980
  370.7 33.3 %collective-permute-start.8 = (bf16[2,2,2,192,768]{4,3,2,1,0:T(8,128)(2,1)}, bf16[2,2,2,192,768]{4,3,2,1,0:T(8,128)(2,1)}, u32[]{:S(2)}, u32[]{:S(2)}) collective-permute-start(bf16[2,2,2,192,768]{4,3,2,1,0:T(8,128)(2,1)} %bitcast.31), channel_id=1, source_target_pairs={{0,2},{2,0},{4,6},{6,4},{8,10},{10,8},{12,14},{14,12},{16,18},{18,... | collective-permute-start | bytes 7077896 | tf_op jit(solution)/shard_map/ppermute | solution.py:980
  370.7 87.7 %collective-permute-start.12 = (bf16[2,512,768]{2,1,0:T(8,128)(2,1)}, bf16[2,512,768]{2,1,0:T(8,128)(2,1)}, u32[]{:S(2)}, u32[]{:S(2)}) collective-permute-start(bf16[2,512,768]{2,1,0:T(8,128)(2,1)} %get-tuple-element.264), channel_id=1, source_target_pairs={{0,1},{1,0},{2,3},{3,2},{4,5},{5,4},{6,7},{7,6},{8,9},{9,8},{10,11... | collective-permute-start | bytes 4718600 | tf_op jit(solution)/shard_map/ppermute | solution.py:1386
  402.8 2.3 copy-start.4
  404.0 6.0 %copy-start.9 = (bf16[8,192,768]{2,1,0:T(8,128)(2,1)S(1)}, bf16[8,192,768]{2,1,0:T(8,128)(2,1)}, u32[]{:S(2)}) copy-start(bf16[8,192,768]{2,1,0:T(8,128)(2,1)} %get-tuple-element.250) | copy-start | bytes 7077892
  406.9 51.5 %collective-permute-start.9 = (bf16[432,768]{1,0:T(8,128)(2,1)S(1)}, bf16[432,768]{1,0:T(8,128)(2,1)}, u32[]{:S(2)}, u32[]{:S(2)}) collective-permute-start(bf16[432,768]{1,0:T(8,128)(2,1)S(1)} %dynamic-slice_bitcast_fusion.6), channel_id=1, source_target_pairs={{0,16},{2,18},{4,20},{6,22},{8,24},{10,26},{12,28},{14,30},{16,0},... | collective-permute-start | bytes 1990664 | tf_op jit(solution)/shard_map/ppermute | solution.py:980
  412.3 1.5 copy-start.5
  414.9 43.6 %collective-permute-start.10 = (bf16[2,2,192,768]{3,2,1,0:T(8,128)(2,1)}, bf16[2,2,192,768]{3,2,1,0:T(8,128)(2,1)}, u32[]{:S(2)}, u32[]{:S(2)}) collective-permute-start(bf16[2,2,192,768]{3,2,1,0:T(8,128)(2,1)} %dynamic-slice_bitcast_fusion.3), channel_id=1, source_target_pairs={{0,4},{2,6},{4,0},{6,2},{8,12},{10,14},{12,8},{14,10},{16,20},{18,... | collective-permute-start | bytes 3538952 | tf_op jit(solution)/shard_map/ppermute | solution.py:980
  426.7 31.7 %collective-permute-start.11 = (bf16[512,768]{1,0:T(8,128)(2,1)}, bf16[512,768]{1,0:T(8,128)(2,1)}, u32[]{:S(2)}, u32[]{:S(2)}) collective-permute-start(bf16[512,768]{1,0:T(8,128)(2,1)} %get-tuple-element.263), channel_id=1, source_target_pairs={{0,1},{1,0},{2,3},{3,2},{4,5},{5,4},{6,7},{7,6},{8,9},{9,8},{10,11... | collective-permute-start | bytes 2359304 | tf_op jit(solution)/shard_map/ppermute | solution.py:1402
  466.1 29.2 %collective-permute-start.17 = (bf16[512,768]{1,0:T(8,128)(2,1)}, bf16[512,768]{1,0:T(8,128)(2,1)}, u32[]{:S(2)}, u32[]{:S(2)}) collective-permute-start(bf16[512,768]{1,0:T(8,128)(2,1)} %get-tuple-element.270), channel_id=1, source_target_pairs={{0,1},{1,0},{2,3},{3,2},{4,5},{5,4},{6,7},{7,6},{8,9},{9,8},{10,11... | collective-permute-start | bytes 2359304 | tf_op jit(solution)/shard_map/ppermute | solution.py:1411
  468.3 18.5 %copy-start.8 = (bf16[432,768]{1,0:T(8,128)(2,1)}, bf16[432,768]{1,0:T(8,128)(2,1)S(1)}, u32[]{:S(2)}) copy-start(bf16[432,768]{1,0:T(8,128)(2,1)S(1)} %fusion.8.kept_ref) | copy-start | bytes 1990660
  468.3 50.1 %collective-permute-start.13 = (bf16[432,768]{1,0:T(8,128)(2,1)S(1)}, bf16[432,768]{1,0:T(8,128)(2,1)S(1)}, u32[]{:S(2)}, u32[]{:S(2)}) collective-permute-start(bf16[432,768]{1,0:T(8,128)(2,1)S(1)} %fusion.8.kept_ref), channel_id=1, source_target_pairs={{0,1},{1,0},{2,3},{3,2},{4,5},{5,4},{6,7},{7,6},{8,9},{9,8},{10,11... | collective-permute-start | bytes 1990664 | tf_op jit(solution)/shard_map/ppermute | solution.py:982
  486.8 17.9 %collective-permute-start.15 = (bf16[2,2,2,48,1152]{4,3,2,1,0:T(8,128)(2,1)}, bf16[2,2,2,48,1152]{4,3,2,1,0:T(8,128)(2,1)S(1)}, u32[]{:S(2)}, u32[]{:S(2)}) collective-permute-start(bf16[2,2,2,48,1152]{4,3,2,1,0:T(8,128)(2,1)} %bitcast.172), channel_id=1, source_target_pairs={{0,2},{2,0},{4,6},{6,4},{8,10},{10,8},{12,14},{14,12},{16,18},{18,... | collective-permute-start | bytes 2654216 | tf_op jit(solution)/shard_map/ppermute | solution.py:980
  486.9 17.9 %collective-permute-start.16 = (bf16[2,2,2,48,1152]{4,3,2,1,0:T(8,128)(2,1)}, bf16[2,2,2,48,1152]{4,3,2,1,0:T(8,128)(2,1)S(1)}, u32[]{:S(2)}, u32[]{:S(2)}) collective-permute-start(bf16[2,2,2,48,1152]{4,3,2,1,0:T(8,128)(2,1)} %bitcast.171), channel_id=1, source_target_pairs={{0,2},{2,0},{4,6},{6,4},{8,10},{10,8},{12,14},{14,12},{16,18},{18,... | collective-permute-start | bytes 2654216 | tf_op jit(solution)/shard_map/ppermute | solution.py:980
  489.4 15.4 %copy-start.11 = (bf16[8,48,1152]{2,1,0:T(8,128)(2,1)S(1)}, bf16[8,48,1152]{2,1,0:T(8,128)(2,1)}, u32[]{:S(2)}) copy-start(bf16[8,48,1152]{2,1,0:T(8,128)(2,1)} %get-tuple-element.276) | copy-start | bytes 2654212
  489.4 15.4 %copy-start.12 = (bf16[8,48,1152]{2,1,0:T(8,128)(2,1)S(1)}, bf16[8,48,1152]{2,1,0:T(8,128)(2,1)}, u32[]{:S(2)}) copy-start(bf16[8,48,1152]{2,1,0:T(8,128)(2,1)} %get-tuple-element.282) | copy-start | bytes 2654212
  489.4 15.4 %collective-permute-start.14 = (bf16[2,192,768]{2,1,0:T(8,128)(2,1)S(1)}, bf16[2,192,768]{2,1,0:T(8,128)(2,1)S(1)}, u32[]{:S(2)}, u32[]{:S(2)}) collective-permute-start(bf16[2,192,768]{2,1,0:T(8,128)(2,1)S(1)} %dynamic-slice_bitcast_fusion.7), channel_id=1, source_target_pairs={{0,8},{2,10},{4,12},{6,14},{8,0},{10,2},{12,4},{14,6},{16,24},{18,... | collective-permute-start | bytes 1769480 | tf_op jit(solution)/shard_map/ppermute | solution.py:980
  506.1 18.7 %collective-permute-start.19 = (bf16[2,2,48,1152]{3,2,1,0:T(8,128)(2,1)S(1)}, bf16[2,2,48,1152]{3,2,1,0:T(8,128)(2,1)}, u32[]{:S(2)}, u32[]{:S(2)}) collective-permute-start(bf16[2,2,48,1152]{3,2,1,0:T(8,128)(2,1)S(1)} %get-tuple-element.359), channel_id=1, source_target_pairs={{0,4},{2,6},{4,0},{6,2},{8,12},{10,14},{12,8},{14,10},{16,20},{18,... | collective-permute-start | bytes 1327112 | tf_op jit(solution)/shard_map/ppermute | solution.py:980
  509.0 17.7 %collective-permute-start.20 = (bf16[2,2,48,1152]{3,2,1,0:T(8,128)(2,1)}, bf16[2,2,48,1152]{3,2,1,0:T(8,128)(2,1)}, u32[]{:S(2)}, u32[]{:S(2)}) collective-permute-start(bf16[2,2,48,1152]{3,2,1,0:T(8,128)(2,1)} %get-tuple-element.357), channel_id=1, source_target_pairs={{0,8},{2,10},{4,12},{6,14},{8,0},{10,2},{12,4},{14,6},{16,24},{18,... | collective-permute-start | bytes 1327112 | tf_op jit(solution)/shard_map/ppermute | solution.py:980
  510.3 14.5 %collective-permute-start.18 = (bf16[192,768]{1,0:T(8,128)(2,1)}, bf16[192,768]{1,0:T(8,128)(2,1)}, u32[]{:S(2)}, u32[]{:S(2)}) collective-permute-start(bf16[192,768]{1,0:T(8,128)(2,1)} %get-tuple-element.361), channel_id=1, source_target_pairs={{0,16},{2,18},{4,20},{6,22},{8,24},{10,26},{12,28},{14,30},{16,0},... | collective-permute-start | bytes 884744 | tf_op jit(solution)/shard_map/ppermute | solution.py:980
  510.4 18.7 %copy-start.21 = (f32[8,768]{1,0:T(8,128)S(1)}, f32[8,768]{1,0:T(8,128)}, u32[]{:S(2)}) copy-start(f32[8,768]{1,0:T(8,128)} %get-tuple-element.299) | copy-start | bytes 73732
  510.4 18.7 %copy-start.22 = (f32[8,768]{1,0:T(8,128)S(1)}, f32[8,768]{1,0:T(8,128)}, u32[]{:S(2)}) copy-start(f32[8,768]{1,0:T(8,128)} %get-tuple-element.300) | copy-start | bytes 73732
  510.4 19.4 %copy-start.17 = (f32[4,768]{1,0:T(4,128)S(1)}, f32[4,768]{1,0:T(4,128)}, u32[]{:S(2)}) copy-start(f32[4,768]{1,0:T(4,128)} %copy-done.16) | copy-start | bytes 36868
  510.4 19.4 %copy-start.18 = (f32[4,768]{1,0:T(4,128)S(1)}, f32[4,768]{1,0:T(4,128)}, u32[]{:S(2)}) copy-start(f32[4,768]{1,0:T(4,128)} %reshape.205) | copy-start | bytes 36868
  510.4 19.4 %copy-start.19 = (f32[8,768]{1,0:T(8,128)S(1)}, f32[8,768]{1,0:T(8,128)}, u32[]{:S(2)}) copy-start(f32[8,768]{1,0:T(8,128)} %get-tuple-element.302) | copy-start | bytes 73732
  510.4 19.4 %copy-start.20 = (f32[8,768]{1,0:T(8,128)S(1)}, f32[8,768]{1,0:T(8,128)}, u32[]{:S(2)}) copy-start(f32[8,768]{1,0:T(8,128)} %get-tuple-element.303) | copy-start | bytes 73732
  518.4 48.1 %copy-start.15 = (bf16[432,768]{1,0:T(8,128)(2,1)}, bf16[432,768]{1,0:T(8,128)(2,1)S(1)}, u32[]{:S(2)}) copy-start(bf16[432,768]{1,0:T(8,128)(2,1)S(1)} %collective-permute-done.13.got_ref) | copy-start | bytes 1990660
  532.3 38.0 %copy-start.1 = (s32[4,1]{0,1:T(1,128)S(1)}, s32[4,1]{0,1:T(1,128)}, u32[]{:S(2)}) copy-start(s32[4,1]{0,1:T(1,128)} %param.28) | copy-start | bytes 52

commit v11 on v10

--- a/solution.py
+++ b/solution.py
@@ -1040,7 +1040,7 @@
 
 def tail_kernel(*refs, orders, groups):
     trees = len(orders)
-    ins, refs = refs[: 2 * trees + 1], refs[2 * trees + 1 :]
+    ins, refs = refs[: 2 * trees + 4], refs[2 * trees + 4 :]
     outs, refs = refs[: trees + 1], refs[trees + 1 :]
     send_sems, recv_sems = refs[-2:]
     scratch = list(refs[:-2])
@@ -1076,7 +1076,11 @@
             ins[2 * at][...].astype(jnp.float32) + ins[2 * at + 1][...].astype(jnp.float32)
         ).astype(jnp.bfloat16)
         totals.append(total)
-    sums = ins[2 * trees][...]
+    sums = [ref[...] for ref in ins[2 * trees : 2 * trees + 3]]
+    hidden, width = ins[-1][...], sums[0].shape[1]
+    sums += [hidden[:, at : at + width] for at in range(0, hidden.shape[1], width)]
+    spare = outs[trees].shape[0] - sum(rows.shape[0] for rows in sums)
+    sums = jnp.concatenate(sums + [jnp.zeros((spare, width), jnp.float32)], axis=0)
     rounds = max(max(len(order) for order in orders) + 1, len(groups) + 1)
     for step in range(rounds):
         copies = []
@@ -1121,7 +1125,8 @@
     arrays = []
     for tree in trees:
         arrays += [tree.kept, tree.got]
-    arrays += [sums]
+    arrays += sums
+    sums = like((32, sums[0].shape[1]))
     totals = [pltpu.VMEM(tree.kept.shape, jnp.bfloat16) for tree in trees]
     scratch = totals
     shapes = [tree.kept.shape for tree in trees]
@@ -1403,6 +1408,8 @@
         grads, back, source_gots = settle(
             trees, (attend_back((at + 1, 0), (1, pairs), grads, *self_inputs), back, source_gots)
         )
+        for tree in mid_trees:
+            tree.kept, tree.sent, grads = lax.optimization_barrier((tree.kept, tree.sent, grads))
         exchange(trees)
         back = back.astype(kept.dtype)[None]
         kept = (lax.dynamic_update_slice_in_dim(kept, back, (1 - side) * held + at, axis=0),)
@@ -1411,17 +1418,15 @@
     back = lax.ppermute(got, "seq", SWAP)
     grads, _ = lax.optimization_barrier((grads, got))
     late_parts = last_weight(info, [flat(rows) for rows in grads], inputs, self_vectors, own, parts)
+    late_parts = settle(mid_trees, late_parts)
     late_trees = [Tree(*late_parts[0:2], low_first), Tree(*late_parts[2:4], second_first)]
+    exchange(mid_trees + late_trees)
+    (grads, _), back = lax.optimization_barrier(((grads, late_parts[0]), back))
+    grads = settle(late_trees, grads)
     exchange(late_trees)
-    (grads, _), back = lax.optimization_barrier(((grads, late_parts[0]), back))
-    grads = settle(mid_trees + late_trees, grads)
-    exchange(mid_trees + late_trees)
     input_grads, new_sums = leave_now(held - 1, (0,), kept, grads)
     input_grads, new_sums = receive(trees + late_trees, (input_grads, new_sums))
-    sums = jnp.concatenate(
-        [sums + new_sums, feed_sums, return_sums, hidden_sums.reshape(-1, width), jnp.zeros((4, width))],
-        axis=0,
-    )
+    sums = [sums + new_sums, feed_sums, return_sums, hidden_sums]
     mid_total, *late_totals, sums = tail(mid_trees + late_trees, sums, parts)
     input_grads = give(input_grads, back[None], held - 1)
     final = final_outputs(

time: 577 us -> 566 us (0.981)
  waiting for transfers between devices: 17.8 us -> 7.84 us
    ppermute x12, waiting for transfers between devices: 17.8 us -> 7.82 us  [exchange(): self.got = lax.ppermute(self.sent, 'dp', pairs)]
  transfers between devices with their start and end apart: 21 -> 21, of which waited for: 3 -> 2; matrix products, arithmetic and copies ran while one was open for 6% -> 6% of each run, Pallas kernels for 56% -> 57%
where the time goes in v11:
time: 566 us; the launch traced here: 560 us
  Pallas kernels  473 us (84%)
  local copies, waits for them, and re-layouts  28.4 us (5%)
  other arithmetic  27.7 us (5%)
  starting transfers between devices  21.5 us (4%)
  waiting for transfers between devices  7.84 us (1%)
    pallas_call x13, Pallas kernels, kernel_call(): pl.pallas_call(kernel, grid_spec=pltpu.PrefetchScalarGridSpec(num_scalar_...  246 us
    pallas_call x4, Pallas kernels, attend_back(): pl.pallas_call(kernel, grid=size, in_specs=[pl.BlockSpec(memory_space=pl....  123 us
    pallas_call x3, Pallas kernels, attend(): pl.pallas_call(functools.partial(attend_kernel, use_mask=use_mask, start=...  68.5 us
    pallas_call x1, Pallas kernels, tail(): pl.pallas_call(functools.partial(tail_kernel, orders=orders, groups=group...  35.5 us
    convert_element_type x8, other arithmetic, add(): total = total.astype(jnp.bfloat16)  16.3 us
  transfers between devices with their start and end apart: 21, of which 2 were waited for; matrix products, arithmetic and copies ran while one was open for 6% of the time, Pallas kernels for 57%

profile of v11, /device:TPU:0, one launch (start us, length us, event | category | flops | bytes accessed | tf_op | source)
XLA Modules:
  0.0 560.4 jit_solution(1065622094940361357)
XLA Ops:
  0.8 2.8 dynamic-slice_bitcast_fusion.4
  3.6 3.0 collective-permute-start
  6.5 2.7 dynamic-slice_bitcast_fusion.1
  11.2 1.7 copy-done.6
  12.9 1.3 constant_dynamic-slice_fusion
  17.0 6.6 %enter.6 = (bf16[2048,768]{1,0:T(8,128)(2,1)}, bf16[2048,1536]{1,0:T(8,128)(2,1)}) custom-call(s32[5]{0:T(128)} %pad_add_fusion.info_ref, bf16[4,512,768]{2,1,0:T(8,128)(2,1)} %bitcast.163, bf16[768,1536]{1,0:T(8,128)(2,1)} %wi_ref.3, f32[8,768]{1,0:T(8,128)} %get-tuple-element.383.vec_ref, f32[1,1536]{1,0:T(1,128)} %broadcast_in_dim.45.bias_ref), custom_call_target="tpu_custom_call" | custom-call | flops 2415919104 | bytes 6291456 | tf_op jit(solution)/shard_map/enter/pallas_call | solution.py:510
  23.5 9.3 %enter.5 = (bf16[2048,768]{1,0:T(8,128)(2,1)}, bf16[2048,2304]{1,0:T(8,128)(2,1)}) custom-call(s32[5]{0:T(128)} %pad_add_fusion.info_ref, bf16[4,512,768]{2,1,0:T(8,128)(2,1)} %bitcast.162, bf16[768,2304]{1,0:T(8,128)(2,1)} %w_ref.15, f32[8,768]{1,0:T(8,128)} %get-tuple-element.383.vec_ref, f32[1,2304]{1,0:T(1,128)} %broadcast_in_dim.44.bias_ref), custom_call_target="tpu_custom_call" | custom-call | flops 3623878656 | bytes 7864320 | tf_op jit(solution)/shard_map/enter/pallas_call | solution.py:510
  32.9 6.6 %enter.7 = (bf16[2048,768]{1,0:T(8,128)(2,1)}, bf16[2048,2304]{1,0:T(8,128)(2,1)}) custom-call(s32[5]{0:T(128)} %pad_add_fusion.info_ref, bf16[1,512,768]{2,1,0:T(8,128)(2,1)} %collective-permute-done.source_ref, bf16[768,2304]{1,0:T(8,128)(2,1)} %w_ref.15, f32[8,768]{1,0:T(8,128)} %get-tuple-element.383.vec_ref, ...), custom_call_target="tpu_custom_call", output_to_operand_aliasing={{0}: (5, {}), {1}: (6, {})} | custom-call | flops 1811939328 | bytes 3932160 | tf_op jit(solution)/shard_map/enter/pallas_call | solution.py:510
  39.5 18.4 %attend.3 = (bf16[2,1024,768]{2,1,0:T(8,128)(2,1)}, bf16[2,12,1024,1024]{3,2,1,0:T(8,128)(2,1)}, f32[2,6,2,1024]{3,2,1,0:T(2,128)}) custom-call(s32[5]{0:T(128)} %pad_add_fusion.info_ref, bf16[2,1024,2304]{2,1,0:T(8,128)(2,1)} %bitcast.124, bf16[2,1024,2304]{2,1,0:T(8,128)(2,1)} %bitcast.125, bf16[2,1024,2304]{2,1,0:T(8,128)(2,1)} %bitcast.126), custom_call_target="tpu_custom_call" | custom-call | flops 12884901888 | bytes 25165824 | tf_op jit(solution)/shard_map/attend/pallas_call | solution.py:343
  57.9 0.9 copy-done.14
  58.7 2.0 collective-permute-start.2
  60.7 6.7 %enter.8 = (bf16[2048,768]{1,0:T(8,128)(2,1)}, bf16[2048,2304]{1,0:T(8,128)(2,1)}) custom-call(s32[5]{0:T(128)} %pad_add_fusion.info_ref, bf16[1,512,768]{2,1,0:T(8,128)(2,1)} %copy-done.14, bf16[768,2304]{1,0:T(8,128)(2,1)} %w_ref.15, f32[8,768]{1,0:T(8,128)} %get-tuple-element.383.vec_ref, ...), custom_call_target="tpu_custom_call", output_to_operand_aliasing={{0}: (5, {}), {1}: (6, {})} | custom-call | flops 1811939328 | bytes 3932160 | tf_op jit(solution)/shard_map/enter/pallas_call | solution.py:510
  67.4 19.0 %attend.4 = (bf16[2,1024,768]{2,1,0:T(8,128)(2,1)}, bf16[2,12,1024,1024]{3,2,1,0:T(8,128)(2,1)}, f32[2,6,2,1024]{3,2,1,0:T(2,128)}) custom-call(s32[5]{0:T(128)} %pad_add_fusion.info_ref, bf16[2,1024,2304]{2,1,0:T(8,128)(2,1)} %bitcast.127, bf16[2,1024,2304]{2,1,0:T(8,128)(2,1)} %bitcast.128, ...), custom_call_target="tpu_custom_call", output_to_operand_aliasing={{0}: (4, {}), {1}: (5, {}), {2}: (6, {})} | custom-call | flops 12884901888 | bytes 25165824 | tf_op jit(solution)/shard_map/attend/pallas_call | solution.py:343
  86.4 12.5 %middle.1 = (f32[2048,768]{1,0:T(8,128)}, bf16[2048,768]{1,0:T(8,128)(2,1)}) custom-call(s32[5]{0:T(128)} %pad_add_fusion.info_ref, bf16[2048,768]{1,0:T(8,128)(2,1)} %get-tuple-element.204.x_ref, bf16[2048,768]{1,0:T(8,128)(2,1)} %bitcast.157, bf16[768,768]{1,0:T(8,128)(2,1)} %wo_ref.5, bf16[768,768]{1,0:T(8,128)(2,1)} %wq_ref.3, f32[8,768]{1,0:T(8,128)} %concatenate.25.vec_ref), custom_call_target="tpu_custom_call" | custom-call | flops 4831838208 | bytes 15728640 | tf_op jit(solution)/shard_map/middle/pallas_call | solution.py:510
  99.0 1.1 copy-done.11
  100.1 6.6 %enter.9 = (bf16[2048,768]{1,0:T(8,128)(2,1)}, bf16[2048,1536]{1,0:T(8,128)(2,1)}) custom-call(s32[5]{0:T(128)} %pad_add_fusion.info_ref, bf16[2,512,768]{2,1,0:T(8,128)(2,1)} %copy-done.11, bf16[768,1536]{1,0:T(8,128)(2,1)} %wi_ref.3, f32[8,768]{1,0:T(8,128)} %get-tuple-element.383.vec_ref, ...), custom_call_target="tpu_custom_call", output_to_operand_aliasing={{0}: (5, {}), {1}: (6, {})} | custom-call | flops 2415919104 | bytes 6291456 | tf_op jit(solution)/shard_map/enter/pallas_call | solution.py:510
  106.6 31.1 %attend.5 = (bf16[2,1024,768]{2,1,0:T(8,128)(2,1)}, bf16[2,12,1024,1024]{3,2,1,0:T(8,128)(2,1)}, f32[2,6,2,1024]{3,2,1,0:T(2,128)}) custom-call(s32[5]{0:T(128)} %pad_add_fusion.info_ref, bf16[2,1024,768]{2,1,0:T(8,128)(2,1)} %bitcast.187, bf16[2,1024,1536]{2,1,0:T(8,128)(2,1)} %bitcast.148, bf16[2,1024,1536]{2,1,0:T(8,128)(2,1)} %bitcast.149), custom_call_target="tpu_custom_call" | custom-call | flops 25769803776 | bytes 50331648 | tf_op jit(solution)/shard_map/attend/pallas_call | solution.py:343
  137.8 108.1 %feed.1 = (bf16[4,512,768]{2,1,0:T(8,128)(2,1)}, bf16[2,512,768]{2,1,0:T(8,128)(2,1)}, f32[2048,768]{1,0:T(8,128)}, bf16[2048,768]{1,0:T(8,128)(2,1)}, f32[8,768...) custom-call(s32[5]{0:T(128)} %pad_add_fusion.info_ref, ...), custom_call_target="tpu_custom_call" | custom-call | flops 65229815808 | bytes 62914560 | tf_op jit(solution)/shard_map/feed/pallas_call | solution.py:510
  246.1 1.0 collective-permute-start.6
  247.1 30.6 %attend_back.4 = (bf16[2,1024,768]{2,1,0:T(8,128)(2,1)}, bf16[2,1024,768]{2,1,0:T(8,128)(2,1)}, bf16[2,1024,768]{2,1,0:T(8,128)(2,1)}) custom-call(bf16[2,1024,768]{2,1,0:T(8,128)(2,1)} %bitcast.188, bf16[2,1024,1536]{2,1,0:T(8,128)(2,1)} %bitcast.150, bf16[2,1024,1536]{2,1,0:T(8,128)(2,1)} %bitcast.151, ...), custom_call_target="tpu_custom_call" | custom-call | flops 25769803776 | bytes 25165824 | tf_op jit(solution)/shard_map/attend_back/pallas_call | solution.py:419
  277.7 5.3 fusion
  283.1 2.3 copy-done.2
  285.4 1.7 dynamic-slice_bitcast_fusion
  287.0 1.5 collective-permute-start.5
  288.5 30.7 %attend_back.5 = (bf16[2,1024,768]{2,1,0:T(8,128)(2,1)}, bf16[2,1024,768]{2,1,0:T(8,128)(2,1)}, bf16[2,1024,768]{2,1,0:T(8,128)(2,1)}) custom-call(bf16[2,1024,768]{2,1,0:T(8,128)(2,1)} %get-tuple-element.233.refs_0_, bf16[2,1024,768]{2,1,0:T(8,128)(2,1)} %get-tuple-element.234.refs_1_, ...), custom_call_target="tpu_custom_call", output_to_operand_aliasing={{0}: (0, {}), {1}: (1, {}), {2}: (2, {})} | custom-call | flops 25769803776 | bytes 25165824 | tf_op jit(solution)/shard_map/attend_back/pallas_call | solution.py:419
  319.2 41.5 %return_rows.1 = (f32[4,512,768]{2,1,0:T(8,128)}, bf16[2,512,768]{2,1,0:T(8,128)(2,1)}, f32[2048,768]{1,0:T(8,128)}, bf16[2048,768]{1,0:T(8,128)(2,1)}, f32[8,76...) custom-call(s32[5]{0:T(128)} %pad_add_fusion.info_ref, bf16[2048,768]{1,0:T(8,128)(2,1)} %bitcast.195, ...), custom_call_target="tpu_custom_call" | custom-call | flops 19327352832 | bytes 41943040 | tf_op jit(solution)/shard_map/return_rows/pallas_call | solution.py:510
  360.6 3.2 fusion.2
  363.8 1.5 copy-done.3
  365.3 1.2 dynamic-slice_bitcast_fusion.2
  366.5 2.1 collective-permute-start.7
  368.6 1.1 collective-permute-start.12
  369.7 31.0 %attend_back.6 = (bf16[2,1024,768]{2,1,0:T(8,128)(2,1)}, bf16[2,1024,768]{2,1,0:T(8,128)(2,1)}, bf16[2,1024,768]{2,1,0:T(8,128)(2,1)}) custom-call(bf16[2,1024,2304]{2,1,0:T(8,128)(2,1)} %bitcast.130, bf16[2,1024,2304]{2,1,0:T(8,128)(2,1)} %bitcast.131, bf16[2,1024,2304]{2,1,0:T(8,128)(2,1)} %bitcast.132, ...), custom_call_target="tpu_custom_call" | custom-call | flops 25769803776 | bytes 25165824 | tf_op jit(solution)/shard_map/attend_back/pallas_call | solution.py:419
  400.7 1.2 bitcast_dynamic-update-slice_fusion
  401.9 1.0 copy-done.4
  403.0 1.7 fusion.4
  404.8 2.2 collective-permute-start.9
  406.9 2.3 fusion.3
  409.2 1.5 copy-done.5
  410.7 1.1 dynamic-slice_bitcast_fusion.3
  411.8 11.8 %leave.3 = (f32[4,512,768]{2,1,0:T(8,128)}, bf16[512,768]{1,0:T(8,128)(2,1)}, f32[8,768]{1,0:T(8,128)}) custom-call(s32[5]{0:T(128)} %pad_add_fusion.info_ref, bf16[2048,768]{1,0:T(8,128)(2,1)} %bitcast.136, bf16[2048,768]{1,0:T(8,128)(2,1)} %bitcast.140, bf16[2048,768]{1,0:T(8,128)(2,1)} %bitcast.144, bf16[2048,768]{1,0:T(8,128)(2,1)} %get-tuple-element.204.x_ref, ...), custom_call_target="tpu_custom_call" | custom-call | flops 7247757312 | bytes 16777216 | tf_op jit(solution)/shard_map/leave/pallas_call | solution.py:510
  423.6 1.0 collective-permute-start.11
  424.6 30.7 %attend_back.7 = (bf16[2,1024,768]{2,1,0:T(8,128)(2,1)}, bf16[2,1024,768]{2,1,0:T(8,128)(2,1)}, bf16[2,1024,768]{2,1,0:T(8,128)(2,1)}) custom-call(bf16[2,1024,768]{2,1,0:T(8,128)(2,1)} %get-tuple-element.266.refs_0_, bf16[2,1024,768]{2,1,0:T(8,128)(2,1)} %get-tuple-element.267.refs_1_, ...), custom_call_target="tpu_custom_call", output_to_operand_aliasing={{0}: (0, {}), {1}: (1, {}), {2}: (2, {})} | custom-call | flops 25769803776 | bytes 25165824 | tf_op jit(solution)/shard_map/attend_back/pallas_call | solution.py:419
  455.3 1.9 fusion.5
  457.2 1.1 dynamic-slice_bitcast_fusion.7
  458.3 7.6 %leave.4 = (bf16[512,768]{1,0:T(8,128)(2,1)}, f32[8,768]{1,0:T(8,128)}) custom-call(s32[5]{0:T(128)} %pad_add_fusion.info_ref, bf16[2048,768]{1,0:T(8,128)(2,1)} %bitcast.137, bf16[2048,768]{1,0:T(8,128)(2,1)} %bitcast.141, bf16[2048,768]{1,0:T(8,128)(2,1)} %bitcast.145, bf16[2048,768]{1,0:T(8,128)(2,1)} %get-tuple-element.204.x_ref, ...), custom_call_target="tpu_custom_call" | custom-call | flops 3623878656 | bytes 8388608 | tf_op jit(solution)/shard_map/leave/pallas_call | solution.py:510
  466.0 1.1 collective-permute-start.18
  467.0 1.2 fusion.8.kept_ref
  468.3 1.0 collective-permute-start.13
  469.3 1.4 collective-permute-start.14
  470.8 17.5 %last_weight.1 = (bf16[8,48,1152]{2,1,0:T(8,128)(2,1)}, bf16[8,48,1152]{2,1,0:T(8,128)(2,1)}, bf16[8,48,1152]{2,1,0:T(8,128)(2,1)}, bf16[8,48,1152]{2,1,0:T(8,128)(2,1)}) custom-call(s32[5]{0:T(128)} %pad_add_fusion.info_ref, bf16[2048,768]{1,0:T(8,128)(2,1)} %bitcast.138, bf16[2048,768]{1,0:T(8,128)(2,1)} %bitcast.142, bf16[2048,768]{1,0:T(8,128)(2,1)} %bitcast.146, ...), custom_call_target="tpu_custom_call" | custom-call | flops 28991029248 | bytes 20971520 | tf_op jit(solution)/shard_map/last_weight/pallas_call | solution.py:510
  488.8 2.4 convert_dynamic-update-slice_fusion.2.refs_0_
  491.2 3.4 convert_dynamic-update-slice_fusion
  495.3 0.8 dynamic-slice_bitcast_fusion.10
  496.2 1.5 collective-permute-start.19
  497.7 1.0 dynamic-slice_bitcast_fusion.9
  498.6 1.1 collective-permute-start.20
  499.7 0.8 dynamic-slice_bitcast_fusion.13
  501.4 8.0 %leave.5 = (f32[4,512,768]{2,1,0:T(8,128)}, f32[8,768]{1,0:T(8,128)}) custom-call(s32[5]{0:T(128)} %pad_add_fusion.info_ref, bf16[2048,768]{1,0:T(8,128)(2,1)} %bitcast.139, bf16[2048,768]{1,0:T(8,128)(2,1)} %bitcast.143, bf16[2048,768]{1,0:T(8,128)(2,1)} %bitcast.147, bf16[2048,768]{1,0:T(8,128)(2,1)} %get-tuple-element.204.x_ref, ...), custom_call_target="tpu_custom_call", output_to_operand_aliasing={{0}: (8, {})} | custom-call | flops 3623878656 | bytes 8388608 | tf_op jit(solution)/shard_map/leave/pallas_call | solution.py:510
  509.4 6.4 %collective-permute-done.15.refs_1_ = bf16[192,768]{1,0:T(8,128)(2,1)} collective-permute-done((bf16[192,768]{1,0:T(8,128)(2,1)}, bf16[192,768]{1,0:T(8,128)(2,1)}, u32[]{:S(2)}, u32[]{:S(2)}) %collective-permute-start.15) | collective-permute-done | bytes 294944 | tf_op jit(solution)/shard_map/ppermute | solution.py:980
  515.8 1.4 collective-permute-done.20.refs_5_
  517.2 2.4 convert_dynamic-update-slice_fusion.1
  519.6 1.4 add_add_fusion.refs_6_
  520.9 35.5 %tail.1 = (f32[192,768]{1,0:T(8,128)}, f32[48,1152]{1,0:T(8,128)}, f32[48,1152]{1,0:T(8,128)}, f32[32,768]{1,0:T(8,128)}) custom-call(bf16[192,768]{1,0:T(8,128)(2,1)} %get-tuple-element.380.refs_0_, bf16[192,768]{1,0:T(8,128)(2,1)} %collective-permute-done.15.refs_1_, bf16[2,2,48,1152]{3,2,1,0:T(8,128)(2,1)} %get-tuple-element.378.refs_2_, ...), custom_call_target="tpu_custom_call" | custom-call | flops 20000000000 | bytes 10000000 | tf_op jit(solution)/shard_map/tail/pallas_call | solution.py:1149
  556.5 3.8 final.1
  (115 shorter events, 7.0 us)
Async XLA Ops:
  0.7 13.6 %copy-start = (s32[4,1]{0,1:T(1,128)S(1)}, s32[4,1]{0,1:T(1,128)}, u32[]{:S(2)}) copy-start(s32[4,1]{0,1:T(1,128)} %param.28) | copy-start | bytes 52
  0.7 8.5 %copy-start.21 = (f32[768]{0:T(1024)S(1)}, f32[768]{0:T(1024)}, u32[]{:S(2)}) copy-start(f32[768]{0:T(1024)} %param.39) | copy-start | bytes 9220
  0.7 8.5 %copy-start.22 = (f32[768]{0:T(1024)S(1)}, f32[768]{0:T(1024)}, u32[]{:S(2)}) copy-start(f32[768]{0:T(1024)} %param.38) | copy-start | bytes 9220
  0.7 8.5 %copy-start.23 = (f32[768]{0:T(1024)S(1)}, f32[768]{0:T(1024)}, u32[]{:S(2)}) copy-start(f32[768]{0:T(1024)} %param.32) | copy-start | bytes 9220
  0.7 8.5 %copy-start.24 = (f32[768]{0:T(1024)S(1)}, f32[768]{0:T(1024)}, u32[]{:S(2)}) copy-start(f32[768]{0:T(1024)} %param.31) | copy-start | bytes 9220
  0.7 8.5 %copy-start.31 = (f32[768]{0:T(1024)S(1)}, f32[768]{0:T(1024)}, u32[]{:S(2)}) copy-start(f32[768]{0:T(1024)} %param.35) | copy-start | bytes 9220
  0.7 8.5 %copy-start.32 = (f32[768]{0:T(1024)S(1)}, f32[768]{0:T(1024)}, u32[]{:S(2)}) copy-start(f32[768]{0:T(1024)} %param.34) | copy-start | bytes 9220
  0.7 9.1 %copy-start.20 = (f32[768]{0:T(1024)S(1)}, f32[768]{0:T(1024)}, u32[]{:S(2)}) copy-start(f32[768]{0:T(1024)} %param.43) | copy-start | bytes 9220
  0.8 9.7 %copy-start.25 = (f32[768]{0:T(1024)S(1)}, f32[768]{0:T(1024)}, u32[]{:S(2)}) copy-start(f32[768]{0:T(1024)} %param.37) | copy-start | bytes 9220
  0.8 9.7 %copy-start.26 = (f32[768]{0:T(1024)S(1)}, f32[768]{0:T(1024)}, u32[]{:S(2)}) copy-start(f32[768]{0:T(1024)} %param.41) | copy-start | bytes 9220
  0.8 9.7 %copy-start.19 = (s32[4,1,512]{2,1,0:T(1,128)S(1)}, s32[4,1,512]{2,1,0:T(1,128)}, u32[]{:S(2)}) copy-start(s32[4,1,512]{2,1,0:T(1,128)} %param.29) | copy-start | bytes 24580
  0.8 9.8 %copy-start.7 = (bf16[4,1,512,768]{3,2,1,0:T(8,128)(2,1)S(1)}, bf16[4,1,512,768]{3,2,1,0:T(8,128)(2,1)}, u32[]{:S(2)}) copy-start(bf16[4,1,512,768]{3,2,1,0:T(8,128)(2,1)} %param.30) | copy-start | bytes 9437188
  3.6 29.2 %collective-permute-start = (bf16[1,512,768]{2,1,0:T(8,128)(2,1)}, bf16[1,512,768]{2,1,0:T(8,128)(2,1)}, u32[]{:S(2)}, u32[]{:S(2)}) collective-permute-start(bf16[1,512,768]{2,1,0:T(8,128)(2,1)} %get-tuple-element.372), channel_id=1, source_target_pairs={{0,1},{1,0},{2,3},{3,2},{4,5},{5,4},{6,7},{7,6},{8,9},{9,8},{10,11... | collective-permute-start | bytes 2359304 | tf_op jit(solution)/shard_map/ppermute | solution.py:1271
  11.2 1.7 copy-start.6
  12.9 1.3 copy-start.27
  12.9 1.3 copy-start.28
  12.9 1.3 copy-start.29
  12.9 1.3 copy-start.30
  23.5 9.3 %copy-start.15 = (bf16[1,512,768]{2,1,0:T(8,128)(2,1)S(1)}, bf16[1,512,768]{2,1,0:T(8,128)(2,1)}, u32[]{:S(2)}) copy-start(bf16[1,512,768]{2,1,0:T(8,128)(2,1)} %get-tuple-element.199) | copy-start | bytes 2359300
  32.8 25.0 %collective-permute-start.1 = (bf16[1,512,768]{2,1,0:T(8,128)(2,1)S(1)}, bf16[1,512,768]{2,1,0:T(8,128)(2,1)S(1)}, u32[]{:S(2)}, u32[]{:S(2)}) collective-permute-start(bf16[1,512,768]{2,1,0:T(8,128)(2,1)S(1)} %copy-done.15), channel_id=1, source_target_pairs={{0,1},{1,0},{2,3},{3,2},{4,5},{5,4},{6,7},{7,6},{8,9},{9,8},{10,11... | collective-permute-start | bytes 2359304 | tf_op jit(solution)/shard_map/ppermute | solution.py:1271
  57.8 0.9 copy-start.14
  58.7 40.2 %collective-permute-start.2 = (bf16[2,512,768]{2,1,0:T(8,128)(2,1)}, bf16[2,512,768]{2,1,0:T(8,128)(2,1)S(1)}, u32[]{:S(2)}, u32[]{:S(2)}) collective-permute-start(bf16[2,512,768]{2,1,0:T(8,128)(2,1)} %dynamic-slice_bitcast_fusion.1), channel_id=1, source_target_pairs={{0,1},{1,0},{2,3},{3,2},{4,5},{5,4},{6,7},{7,6},{8,9},{9,8},{10,11... | collective-permute-start | bytes 4718600 | tf_op jit(solution)/shard_map/ppermute | solution.py:1271
  98.9 1.1 copy-start.11
  98.9 38.8 %collective-permute-start.3 = (bf16[2,512,768]{2,1,0:T(8,128)(2,1)}, bf16[2,512,768]{2,1,0:T(8,128)(2,1)}, u32[]{:S(2)}, u32[]{:S(2)}) collective-permute-start(bf16[2,512,768]{2,1,0:T(8,128)(2,1)} %constant_dynamic-slice_fusion), channel_id=1, source_target_pairs={{0,1},{1,0},{2,3},{3,2},{4,5},{5,4},{6,7},{7,6},{8,9},{9,8},{10,11... | collective-permute-start | bytes 4718600 | tf_op jit(solution)/shard_map/ppermute | solution.py:1271
  245.9 31.8 %collective-permute-start.4 = (bf16[2,2,2,432,768]{4,3,2,1,0:T(8,128)(2,1)}, bf16[2,2,2,432,768]{4,3,2,1,0:T(8,128)(2,1)}, u32[]{:S(2)}, u32[]{:S(2)}) collective-permute-start(bf16[2,2,2,432,768]{4,3,2,1,0:T(8,128)(2,1)} %bitcast.167), channel_id=1, source_target_pairs={{0,2},{2,0},{4,6},{6,4},{8,10},{10,8},{12,14},{14,12},{16,18},{18,... | collective-permute-start | bytes 15925256 | tf_op jit(solution)/shard_map/ppermute | solution.py:980
  246.1 114.6 %collective-permute-start.6 = (bf16[2,512,768]{2,1,0:T(8,128)(2,1)}, bf16[2,512,768]{2,1,0:T(8,128)(2,1)S(1)}, u32[]{:S(2)}, u32[]{:S(2)}) collective-permute-start(bf16[2,512,768]{2,1,0:T(8,128)(2,1)} %get-tuple-element.248), channel_id=1, source_target_pairs={{0,1},{1,0},{2,3},{3,2},{4,5},{5,4},{6,7},{7,6},{8,9},{9,8},{10,11... | collective-permute-start | bytes 4718600 | tf_op jit(solution)/shard_map/ppermute | solution.py:1363
  283.1 2.3 copy-start.2
  287.0 73.6 %collective-permute-start.5 = (bf16[2,2,432,768]{3,2,1,0:T(8,128)(2,1)}, bf16[2,2,432,768]{3,2,1,0:T(8,128)(2,1)}, u32[]{:S(2)}, u32[]{:S(2)}) collective-permute-start(bf16[2,2,432,768]{3,2,1,0:T(8,128)(2,1)} %dynamic-slice_bitcast_fusion), channel_id=1, source_target_pairs={{0,4},{2,6},{4,0},{6,2},{8,12},{10,14},{12,8},{14,10},{16,20},{18,... | collective-permute-start | bytes 7962632 | tf_op jit(solution)/shard_map/ppermute | solution.py:980
  363.8 1.5 copy-start.3
  366.5 35.4 %collective-permute-start.7 = (bf16[2,432,768]{2,1,0:T(8,128)(2,1)}, bf16[2,432,768]{2,1,0:T(8,128)(2,1)}, u32[]{:S(2)}, u32[]{:S(2)}) collective-permute-start(bf16[2,432,768]{2,1,0:T(8,128)(2,1)} %dynamic-slice_bitcast_fusion.2), channel_id=1, source_target_pairs={{0,8},{2,10},{4,12},{6,14},{8,0},{10,2},{12,4},{14,6},{16,24},{18,... | collective-permute-start | bytes 3981320 | tf_op jit(solution)/shard_map/ppermute | solution.py:980
  368.6 33.3 %collective-permute-start.8 = (bf16[2,2,2,192,768]{4,3,2,1,0:T(8,128)(2,1)}, bf16[2,2,2,192,768]{4,3,2,1,0:T(8,128)(2,1)}, u32[]{:S(2)}, u32[]{:S(2)}) collective-permute-start(bf16[2,2,2,192,768]{4,3,2,1,0:T(8,128)(2,1)} %bitcast.31), channel_id=1, source_target_pairs={{0,2},{2,0},{4,6},{6,4},{8,10},{10,8},{12,14},{14,12},{16,18},{18,... | collective-permute-start | bytes 7077896 | tf_op jit(solution)/shard_map/ppermute | solution.py:980
  368.6 86.7 %collective-permute-start.12 = (bf16[2,512,768]{2,1,0:T(8,128)(2,1)}, bf16[2,512,768]{2,1,0:T(8,128)(2,1)}, u32[]{:S(2)}, u32[]{:S(2)}) collective-permute-start(bf16[2,512,768]{2,1,0:T(8,128)(2,1)} %get-tuple-element.273), channel_id=1, source_target_pairs={{0,1},{1,0},{2,3},{3,2},{4,5},{5,4},{6,7},{7,6},{8,9},{9,8},{10,11... | collective-permute-start | bytes 4718600 | tf_op jit(solution)/shard_map/ppermute | solution.py:1391
  400.7 2.3 copy-start.4
  401.9 5.0 copy-start.9
  404.8 50.5 %collective-permute-start.9 = (bf16[432,768]{1,0:T(8,128)(2,1)S(1)}, bf16[432,768]{1,0:T(8,128)(2,1)}, u32[]{:S(2)}, u32[]{:S(2)}) collective-permute-start(bf16[432,768]{1,0:T(8,128)(2,1)S(1)} %dynamic-slice_bitcast_fusion.6), channel_id=1, source_target_pairs={{0,16},{2,18},{4,20},{6,22},{8,24},{10,26},{12,28},{14,30},{16,0},... | collective-permute-start | bytes 1990664 | tf_op jit(solution)/shard_map/ppermute | solution.py:980
  409.2 1.5 copy-start.5
  411.8 43.5 %collective-permute-start.10 = (bf16[2,2,192,768]{3,2,1,0:T(8,128)(2,1)}, bf16[2,2,192,768]{3,2,1,0:T(8,128)(2,1)}, u32[]{:S(2)}, u32[]{:S(2)}) collective-permute-start(bf16[2,2,192,768]{3,2,1,0:T(8,128)(2,1)} %dynamic-slice_bitcast_fusion.3), channel_id=1, source_target_pairs={{0,4},{2,6},{4,0},{6,2},{8,12},{10,14},{12,8},{14,10},{16,20},{18,... | collective-permute-start | bytes 3538952 | tf_op jit(solution)/shard_map/ppermute | solution.py:980
  423.6 31.7 %collective-permute-start.11 = (bf16[512,768]{1,0:T(8,128)(2,1)}, bf16[512,768]{1,0:T(8,128)(2,1)}, u32[]{:S(2)}, u32[]{:S(2)}) collective-permute-start(bf16[512,768]{1,0:T(8,128)(2,1)} %get-tuple-element.272), channel_id=1, source_target_pairs={{0,1},{1,0},{2,3},{3,2},{4,5},{5,4},{6,7},{7,6},{8,9},{9,8},{10,11... | collective-permute-start | bytes 2359304 | tf_op jit(solution)/shard_map/ppermute | solution.py:1407
  466.0 28.8 %collective-permute-start.18 = (bf16[512,768]{1,0:T(8,128)(2,1)}, bf16[512,768]{1,0:T(8,128)(2,1)}, u32[]{:S(2)}, u32[]{:S(2)}) collective-permute-start(bf16[512,768]{1,0:T(8,128)(2,1)} %get-tuple-element.284), channel_id=1, source_target_pairs={{0,1},{1,0},{2,3},{3,2},{4,5},{5,4},{6,7},{7,6},{8,9},{9,8},{10,11... | collective-permute-start | bytes 2359304 | tf_op jit(solution)/shard_map/ppermute | solution.py:1418
  468.3 19.9 %copy-start.8 = (bf16[432,768]{1,0:T(8,128)(2,1)}, bf16[432,768]{1,0:T(8,128)(2,1)S(1)}, u32[]{:S(2)}) copy-start(bf16[432,768]{1,0:T(8,128)(2,1)S(1)} %fusion.8.kept_ref) | copy-start | bytes 1990660
  468.3 41.1 %collective-permute-start.13 = (bf16[432,768]{1,0:T(8,128)(2,1)S(1)}, bf16[432,768]{1,0:T(8,128)(2,1)S(1)}, u32[]{:S(2)}, u32[]{:S(2)}) collective-permute-start(bf16[432,768]{1,0:T(8,128)(2,1)S(1)} %fusion.8.kept_ref), channel_id=1, source_target_pairs={{0,1},{1,0},{2,3},{3,2},{4,5},{5,4},{6,7},{7,6},{8,9},{9,8},{10,11... | collective-permute-start | bytes 1990664 | tf_op jit(solution)/shard_map/ppermute | solution.py:982
  469.3 18.9 %collective-permute-start.14 = (bf16[2,192,768]{2,1,0:T(8,128)(2,1)}, bf16[2,192,768]{2,1,0:T(8,128)(2,1)S(1)}, u32[]{:S(2)}, u32[]{:S(2)}) collective-permute-start(bf16[2,192,768]{2,1,0:T(8,128)(2,1)} %get-tuple-element.280), channel_id=1, source_target_pairs={{0,8},{2,10},{4,12},{6,14},{8,0},{10,2},{12,4},{14,6},{16,24},{18,... | collective-permute-start | bytes 1769480 | tf_op jit(solution)/shard_map/ppermute | solution.py:980
  488.2 6.6 %collective-permute-start.16 = (bf16[2,2,2,48,1152]{4,3,2,1,0:T(8,128)(2,1)}, bf16[2,2,2,48,1152]{4,3,2,1,0:T(8,128)(2,1)S(1)}, u32[]{:S(2)}, u32[]{:S(2)}) collective-permute-start(bf16[2,2,2,48,1152]{4,3,2,1,0:T(8,128)(2,1)} %bitcast.171), channel_id=1, source_target_pairs={{0,2},{2,0},{4,6},{6,4},{8,10},{10,8},{12,14},{14,12},{16,18},{18,... | collective-permute-start | bytes 2654216 | tf_op jit(solution)/shard_map/ppermute | solution.py:980
  488.3 6.3 %copy-start.10 = (bf16[2,192,768]{2,1,0:T(8,128)(2,1)S(1)}, bf16[2,192,768]{2,1,0:T(8,128)(2,1)}, u32[]{:S(2)}) copy-start(bf16[2,192,768]{2,1,0:T(8,128)(2,1)} %get-tuple-element.279) | copy-start | bytes 1769476
  488.3 6.5 %collective-permute-start.17 = (bf16[2,2,2,48,1152]{4,3,2,1,0:T(8,128)(2,1)}, bf16[2,2,2,48,1152]{4,3,2,1,0:T(8,128)(2,1)S(1)}, u32[]{:S(2)}, u32[]{:S(2)}) collective-permute-start(bf16[2,2,2,48,1152]{4,3,2,1,0:T(8,128)(2,1)} %bitcast.170), channel_id=1, source_target_pairs={{0,2},{2,0},{4,6},{6,4},{8,10},{10,8},{12,14},{14,12},{16,18},{18,... | collective-permute-start | bytes 2654216 | tf_op jit(solution)/shard_map/ppermute | solution.py:980
  491.2 3.6 copy-start.12
  491.2 3.6 copy-start.13
  496.2 19.6 %collective-permute-start.19 = (bf16[2,2,48,1152]{3,2,1,0:T(8,128)(2,1)S(1)}, bf16[2,2,48,1152]{3,2,1,0:T(8,128)(2,1)}, u32[]{:S(2)}, u32[]{:S(2)}) collective-permute-start(bf16[2,2,48,1152]{3,2,1,0:T(8,128)(2,1)S(1)} %get-tuple-element.379), channel_id=1, source_target_pairs={{0,4},{2,6},{4,0},{6,2},{8,12},{10,14},{12,8},{14,10},{16,20},{18,... | collective-permute-start | bytes 1327112 | tf_op jit(solution)/shard_map/ppermute | solution.py:980
  498.6 18.6 %collective-permute-start.20 = (bf16[2,2,48,1152]{3,2,1,0:T(8,128)(2,1)}, bf16[2,2,48,1152]{3,2,1,0:T(8,128)(2,1)}, u32[]{:S(2)}, u32[]{:S(2)}) collective-permute-start(bf16[2,2,48,1152]{3,2,1,0:T(8,128)(2,1)} %get-tuple-element.377), channel_id=1, source_target_pairs={{0,8},{2,10},{4,12},{6,14},{8,0},{10,2},{12,4},{14,6},{16,24},{18,... | collective-permute-start | bytes 1327112 | tf_op jit(solution)/shard_map/ppermute | solution.py:980
  500.6 15.2 %collective-permute-start.15 = (bf16[192,768]{1,0:T(8,128)(2,1)}, bf16[192,768]{1,0:T(8,128)(2,1)}, u32[]{:S(2)}, u32[]{:S(2)}) collective-permute-start(bf16[192,768]{1,0:T(8,128)(2,1)} %get-tuple-element.381), channel_id=1, source_target_pairs={{0,16},{2,18},{4,20},{6,22},{8,24},{10,26},{12,28},{14,30},{16,0},... | collective-permute-start | bytes 884744 | tf_op jit(solution)/shard_map/ppermute | solution.py:980
  501.4 18.2 %copy-start.17 = (f32[8,768]{1,0:T(8,128)S(1)}, f32[8,768]{1,0:T(8,128)}, u32[]{:S(2)}) copy-start(f32[8,768]{1,0:T(8,128)} %get-tuple-element.317) | copy-start | bytes 73732
  501.4 18.2 %copy-start.18 = (f32[8,768]{1,0:T(8,128)S(1)}, f32[8,768]{1,0:T(8,128)}, u32[]{:S(2)}) copy-start(f32[8,768]{1,0:T(8,128)} %get-tuple-element.318) | copy-start | bytes 73732
  509.4 47.1 %copy-start.16 = (bf16[432,768]{1,0:T(8,128)(2,1)}, bf16[432,768]{1,0:T(8,128)(2,1)S(1)}, u32[]{:S(2)}) copy-start(bf16[432,768]{1,0:T(8,128)(2,1)S(1)} %collective-permute-done.13.got_ref) | copy-start | bytes 1990660
  520.9 39.3 %copy-start.1 = (s32[4,1]{0,1:T(1,128)S(1)}, s32[4,1]{0,1:T(1,128)}, u32[]{:S(2)}) copy-start(s32[4,1]{0,1:T(1,128)} %param.28) | copy-start | bytes 52

commit v12 on v11

--- a/solution.py
+++ b/solution.py
@@ -697,7 +697,7 @@
             upstream = up if upstream is None else upstream + up
             ao_ref[:, part] += contract(dy_turned, active, 1, 0)
             ai_ref[:, part] += contract(normal_turned, low, 1, 0)
-        put_rows(step, x2 + result + out_bias, own_ref, got_ref)
+        result = (x2 + result + out_bias).astype(jnp.bfloat16)
         wide = dy.astype(jnp.float32)
         dx = wide + normal_back(unit, inverse, gain, upstream)
         dx_ref[...] = dx
@@ -708,6 +708,7 @@
         vsum_ref[1:2, :] += column_sum(upstream * unit)
         vsum_ref[2:3, :] += column_sum(upstream)
         vsum_ref[3:4, :] += column_sum(wide)
+        put_rows(step, result, own_ref, got_ref)
 
     @pl.when(step >= steps)
     def _():
@@ -781,24 +782,24 @@
         gain, shift = vec_ref[0:1, :], vec_ref[1:2, :]
         dq, dk, dv = dq_ref[...], dk_ref[...], dv_ref[...]
         upstream = contract(dq, wq_ref[...], 1, 1)
+        turned = src_ref[...].T
+        ai_ref[:, :width] += contract(turned, dk, 1, 0)
         unit, inverse = normal_parts(x_ref[...])
         normal = (unit * gain + shift).astype(jnp.bfloat16)
+        ai_ref[:, width:] += contract(turned, dv, 1, 0)
         dx = dx_ref[...] + normal_back(unit, inverse, gain, upstream)
+        source = contract(dk, wi_ref[:, :width], 1, 1) + contract(dv, wi_ref[:, width:], 1, 1)
         dxo_ref[...] = dx
         low = dx.astype(jnp.bfloat16)
+        aq_ref[...] += contract(normal.T, dq, 1, 0)
         do_ref[...] = contract(low, wo_ref[...], 1, 1).astype(jnp.bfloat16)
-        source = contract(dk, wi_ref[:, :width], 1, 1) + contract(dv, wi_ref[:, width:], 1, 1)
-        put_rows(step, source, own_ref, got_ref)
-        aq_ref[...] += contract(normal.T, dq, 1, 0)
         ao_ref[...] += contract(mixed_ref[...].T, low, 1, 0)
-        turned = src_ref[...].T
-        ai_ref[:, :width] += contract(turned, dk, 1, 0)
-        ai_ref[:, width:] += contract(turned, dv, 1, 0)
         vsum_ref[0:1, :] += column_sum(upstream * unit)
         vsum_ref[1:2, :] += column_sum(upstream)
         vsum_ref[2:3, :] += column_sum(dx)
         vsum_ref[3:4, :] += column_sum(dq.astype(jnp.float32))
         vsum_ref[4:5, :] += column_sum(dv.astype(jnp.float32))
+        put_rows(step, source, own_ref, got_ref)
 
     @pl.when(step >= steps)
     def _():

time: 566 us -> 559 us (0.988)
  Pallas kernels: 473 us -> 466 us
    pallas_call x13, Pallas kernels: 246 us -> 239 us  [kernel_call(): pl.pallas_call(kernel, grid_spec=pltpu.PrefetchScalarGridSpec(num_scalar_...]
  transfers between devices with their start and end apart: 21 -> 21, of which waited for: 2 -> 1; matrix products, arithmetic and copies ran while one was open for 6% -> 6% of each run, Pallas kernels for 57% -> 57%
where the time goes in v12:
time: 559 us; the launch traced here: 553 us
  Pallas kernels  466 us (83%)
  local copies, waits for them, and re-layouts  28.4 us (5%)
  other arithmetic  27.7 us (5%)
  starting transfers between devices  20.7 us (4%)
  waiting for transfers between devices  8.1 us (1%)
    pallas_call x13, Pallas kernels, kernel_call(): pl.pallas_call(kernel, grid_spec=pltpu.PrefetchScalarGridSpec(num_scalar_...  239 us
    pallas_call x4, Pallas kernels, attend_back(): pl.pallas_call(kernel, grid=size, in_specs=[pl.BlockSpec(memory_space=pl....  123 us
    pallas_call x3, Pallas kernels, attend(): pl.pallas_call(functools.partial(attend_kernel, use_mask=use_mask, start=...  68.5 us
    pallas_call x1, Pallas kernels, tail(): pl.pallas_call(functools.partial(tail_kernel, orders=orders, groups=group...  35.7 us
    convert_element_type x8, other arithmetic, add(): total = total.astype(jnp.bfloat16)  16.3 us
  transfers between devices with their start and end apart: 21, of which 1 were waited for; matrix products, arithmetic and copies ran while one was open for 6% of the time, Pallas kernels for 57%

profile of v12, /device:TPU:0, one launch (start us, length us, event | category | flops | bytes accessed | tf_op | source)
XLA Modules:
  0.0 552.9 jit_solution(13639689805105750530)
XLA Ops:
  0.8 2.8 dynamic-slice_bitcast_fusion.4
  3.6 3.0 collective-permute-start
  6.5 2.7 dynamic-slice_bitcast_fusion.1
  11.2 1.7 copy-done.6
  12.9 1.3 constant_dynamic-slice_fusion
  16.3 0.7 maximum_maximum_fusion.1
  17.0 6.6 %enter.6 = (bf16[2048,768]{1,0:T(8,128)(2,1)}, bf16[2048,1536]{1,0:T(8,128)(2,1)}) custom-call(s32[5]{0:T(128)} %pad_add_fusion.info_ref, bf16[4,512,768]{2,1,0:T(8,128)(2,1)} %bitcast.163, bf16[768,1536]{1,0:T(8,128)(2,1)} %wi_ref.3, f32[8,768]{1,0:T(8,128)} %get-tuple-element.383.vec_ref, f32[1,1536]{1,0:T(1,128)} %broadcast_in_dim.45.bias_ref), custom_call_target="tpu_custom_call" | custom-call | flops 2415919104 | bytes 6291456 | tf_op jit(solution)/shard_map/enter/pallas_call | solution.py:510
  23.5 9.3 %enter.5 = (bf16[2048,768]{1,0:T(8,128)(2,1)}, bf16[2048,2304]{1,0:T(8,128)(2,1)}) custom-call(s32[5]{0:T(128)} %pad_add_fusion.info_ref, bf16[4,512,768]{2,1,0:T(8,128)(2,1)} %bitcast.162, bf16[768,2304]{1,0:T(8,128)(2,1)} %w_ref.15, f32[8,768]{1,0:T(8,128)} %get-tuple-element.383.vec_ref, f32[1,2304]{1,0:T(1,128)} %broadcast_in_dim.44.bias_ref), custom_call_target="tpu_custom_call" | custom-call | flops 3623878656 | bytes 7864320 | tf_op jit(solution)/shard_map/enter/pallas_call | solution.py:510
  32.9 6.6 %enter.7 = (bf16[2048,768]{1,0:T(8,128)(2,1)}, bf16[2048,2304]{1,0:T(8,128)(2,1)}) custom-call(s32[5]{0:T(128)} %pad_add_fusion.info_ref, bf16[1,512,768]{2,1,0:T(8,128)(2,1)} %collective-permute-done.source_ref, bf16[768,2304]{1,0:T(8,128)(2,1)} %w_ref.15, f32[8,768]{1,0:T(8,128)} %get-tuple-element.383.vec_ref, ...), custom_call_target="tpu_custom_call", output_to_operand_aliasing={{0}: (5, {}), {1}: (6, {})} | custom-call | flops 1811939328 | bytes 3932160 | tf_op jit(solution)/shard_map/enter/pallas_call | solution.py:510
  39.5 18.4 %attend.3 = (bf16[2,1024,768]{2,1,0:T(8,128)(2,1)}, bf16[2,12,1024,1024]{3,2,1,0:T(8,128)(2,1)}, f32[2,6,2,1024]{3,2,1,0:T(2,128)}) custom-call(s32[5]{0:T(128)} %pad_add_fusion.info_ref, bf16[2,1024,2304]{2,1,0:T(8,128)(2,1)} %bitcast.124, bf16[2,1024,2304]{2,1,0:T(8,128)(2,1)} %bitcast.125, bf16[2,1024,2304]{2,1,0:T(8,128)(2,1)} %bitcast.126), custom_call_target="tpu_custom_call" | custom-call | flops 12884901888 | bytes 25165824 | tf_op jit(solution)/shard_map/attend/pallas_call | solution.py:343
  57.9 0.9 copy-done.14
  58.7 2.5 collective-permute-start.2
  61.2 6.7 %enter.8 = (bf16[2048,768]{1,0:T(8,128)(2,1)}, bf16[2048,2304]{1,0:T(8,128)(2,1)}) custom-call(s32[5]{0:T(128)} %pad_add_fusion.info_ref, bf16[1,512,768]{2,1,0:T(8,128)(2,1)} %copy-done.14, bf16[768,2304]{1,0:T(8,128)(2,1)} %w_ref.15, f32[8,768]{1,0:T(8,128)} %get-tuple-element.383.vec_ref, ...), custom_call_target="tpu_custom_call", output_to_operand_aliasing={{0}: (5, {}), {1}: (6, {})} | custom-call | flops 1811939328 | bytes 3932160 | tf_op jit(solution)/shard_map/enter/pallas_call | solution.py:510
  67.9 19.0 %attend.4 = (bf16[2,1024,768]{2,1,0:T(8,128)(2,1)}, bf16[2,12,1024,1024]{3,2,1,0:T(8,128)(2,1)}, f32[2,6,2,1024]{3,2,1,0:T(2,128)}) custom-call(s32[5]{0:T(128)} %pad_add_fusion.info_ref, bf16[2,1024,2304]{2,1,0:T(8,128)(2,1)} %bitcast.127, bf16[2,1024,2304]{2,1,0:T(8,128)(2,1)} %bitcast.128, ...), custom_call_target="tpu_custom_call", output_to_operand_aliasing={{0}: (4, {}), {1}: (5, {}), {2}: (6, {})} | custom-call | flops 12884901888 | bytes 25165824 | tf_op jit(solution)/shard_map/attend/pallas_call | solution.py:343
  86.9 12.5 %middle.1 = (f32[2048,768]{1,0:T(8,128)}, bf16[2048,768]{1,0:T(8,128)(2,1)}) custom-call(s32[5]{0:T(128)} %pad_add_fusion.info_ref, bf16[2048,768]{1,0:T(8,128)(2,1)} %get-tuple-element.204.x_ref, bf16[2048,768]{1,0:T(8,128)(2,1)} %bitcast.157, bf16[768,768]{1,0:T(8,128)(2,1)} %wo_ref.5, bf16[768,768]{1,0:T(8,128)(2,1)} %wq_ref.3, f32[8,768]{1,0:T(8,128)} %concatenate.25.vec_ref), custom_call_target="tpu_custom_call" | custom-call | flops 4831838208 | bytes 15728640 | tf_op jit(solution)/shard_map/middle/pallas_call | solution.py:510
  99.5 1.1 copy-done.11
  100.6 6.6 %enter.9 = (bf16[2048,768]{1,0:T(8,128)(2,1)}, bf16[2048,1536]{1,0:T(8,128)(2,1)}) custom-call(s32[5]{0:T(128)} %pad_add_fusion.info_ref, bf16[2,512,768]{2,1,0:T(8,128)(2,1)} %copy-done.11, bf16[768,1536]{1,0:T(8,128)(2,1)} %wi_ref.3, f32[8,768]{1,0:T(8,128)} %get-tuple-element.383.vec_ref, ...), custom_call_target="tpu_custom_call", output_to_operand_aliasing={{0}: (5, {}), {1}: (6, {})} | custom-call | flops 2415919104 | bytes 6291456 | tf_op jit(solution)/shard_map/enter/pallas_call | solution.py:510
  107.1 31.1 %attend.5 = (bf16[2,1024,768]{2,1,0:T(8,128)(2,1)}, bf16[2,12,1024,1024]{3,2,1,0:T(8,128)(2,1)}, f32[2,6,2,1024]{3,2,1,0:T(2,128)}) custom-call(s32[5]{0:T(128)} %pad_add_fusion.info_ref, bf16[2,1024,768]{2,1,0:T(8,128)(2,1)} %bitcast.187, bf16[2,1024,1536]{2,1,0:T(8,128)(2,1)} %bitcast.148, bf16[2,1024,1536]{2,1,0:T(8,128)(2,1)} %bitcast.149), custom_call_target="tpu_custom_call" | custom-call | flops 25769803776 | bytes 50331648 | tf_op jit(solution)/shard_map/attend/pallas_call | solution.py:343
  138.2 106.4 %feed.1 = (bf16[4,512,768]{2,1,0:T(8,128)(2,1)}, bf16[2,512,768]{2,1,0:T(8,128)(2,1)}, f32[2048,768]{1,0:T(8,128)}, bf16[2048,768]{1,0:T(8,128)(2,1)}, f32[8,768...) custom-call(s32[5]{0:T(128)} %pad_add_fusion.info_ref, ...), custom_call_target="tpu_custom_call" | custom-call | flops 65229815808 | bytes 62914560 | tf_op jit(solution)/shard_map/feed/pallas_call | solution.py:510
  244.9 1.0 collective-permute-start.6
  245.9 30.6 %attend_back.4 = (bf16[2,1024,768]{2,1,0:T(8,128)(2,1)}, bf16[2,1024,768]{2,1,0:T(8,128)(2,1)}, bf16[2,1024,768]{2,1,0:T(8,128)(2,1)}) custom-call(bf16[2,1024,768]{2,1,0:T(8,128)(2,1)} %bitcast.188, bf16[2,1024,1536]{2,1,0:T(8,128)(2,1)} %bitcast.150, bf16[2,1024,1536]{2,1,0:T(8,128)(2,1)} %bitcast.151, ...), custom_call_target="tpu_custom_call" | custom-call | flops 25769803776 | bytes 25165824 | tf_op jit(solution)/shard_map/attend_back/pallas_call | solution.py:419
  276.5 5.3 fusion
  281.9 2.3 copy-done.2
  284.2 1.7 dynamic-slice_bitcast_fusion
  285.9 1.0 collective-permute-start.5
  286.9 30.7 %attend_back.5 = (bf16[2,1024,768]{2,1,0:T(8,128)(2,1)}, bf16[2,1024,768]{2,1,0:T(8,128)(2,1)}, bf16[2,1024,768]{2,1,0:T(8,128)(2,1)}) custom-call(bf16[2,1024,768]{2,1,0:T(8,128)(2,1)} %get-tuple-element.233.refs_0_, bf16[2,1024,768]{2,1,0:T(8,128)(2,1)} %get-tuple-element.234.refs_1_, ...), custom_call_target="tpu_custom_call", output_to_operand_aliasing={{0}: (0, {}), {1}: (1, {}), {2}: (2, {})} | custom-call | flops 25769803776 | bytes 25165824 | tf_op jit(solution)/shard_map/attend_back/pallas_call | solution.py:419
  317.5 35.9 %return_rows.1 = (f32[4,512,768]{2,1,0:T(8,128)}, bf16[2,512,768]{2,1,0:T(8,128)(2,1)}, f32[2048,768]{1,0:T(8,128)}, bf16[2048,768]{1,0:T(8,128)(2,1)}, f32[8,76...) custom-call(s32[5]{0:T(128)} %pad_add_fusion.info_ref, bf16[2048,768]{1,0:T(8,128)(2,1)} %bitcast.195, ...), custom_call_target="tpu_custom_call" | custom-call | flops 19327352832 | bytes 41943040 | tf_op jit(solution)/shard_map/return_rows/pallas_call | solution.py:510
  353.5 3.2 fusion.2
  356.7 1.5 copy-done.3
  358.2 1.2 dynamic-slice_bitcast_fusion.2
  359.3 1.1 collective-permute-start.7
  360.5 1.0 collective-permute-start.12
  361.5 31.0 %attend_back.6 = (bf16[2,1024,768]{2,1,0:T(8,128)(2,1)}, bf16[2,1024,768]{2,1,0:T(8,128)(2,1)}, bf16[2,1024,768]{2,1,0:T(8,128)(2,1)}) custom-call(bf16[2,1024,2304]{2,1,0:T(8,128)(2,1)} %bitcast.130, bf16[2,1024,2304]{2,1,0:T(8,128)(2,1)} %bitcast.131, bf16[2,1024,2304]{2,1,0:T(8,128)(2,1)} %bitcast.132, ...), custom_call_target="tpu_custom_call" | custom-call | flops 25769803776 | bytes 25165824 | tf_op jit(solution)/shard_map/attend_back/pallas_call | solution.py:419
  392.5 1.2 bitcast_dynamic-update-slice_fusion
  393.7 1.0 copy-done.4
  394.8 1.7 fusion.4
  396.6 3.1 collective-permute-start.9
  399.7 2.3 fusion.3
  402.0 1.5 copy-done.5
  403.5 1.1 dynamic-slice_bitcast_fusion.3
  404.6 1.1 collective-permute-start.10
  405.6 11.8 %leave.3 = (f32[4,512,768]{2,1,0:T(8,128)}, bf16[512,768]{1,0:T(8,128)(2,1)}, f32[8,768]{1,0:T(8,128)}) custom-call(s32[5]{0:T(128)} %pad_add_fusion.info_ref, bf16[2048,768]{1,0:T(8,128)(2,1)} %bitcast.136, bf16[2048,768]{1,0:T(8,128)(2,1)} %bitcast.140, bf16[2048,768]{1,0:T(8,128)(2,1)} %bitcast.144, bf16[2048,768]{1,0:T(8,128)(2,1)} %get-tuple-element.204.x_ref, ...), custom_call_target="tpu_custom_call" | custom-call | flops 7247757312 | bytes 16777216 | tf_op jit(solution)/shard_map/leave/pallas_call | solution.py:510
  417.4 1.0 collective-permute-start.11
  418.4 30.7 %attend_back.7 = (bf16[2,1024,768]{2,1,0:T(8,128)(2,1)}, bf16[2,1024,768]{2,1,0:T(8,128)(2,1)}, bf16[2,1024,768]{2,1,0:T(8,128)(2,1)}) custom-call(bf16[2,1024,768]{2,1,0:T(8,128)(2,1)} %get-tuple-element.266.refs_0_, bf16[2,1024,768]{2,1,0:T(8,128)(2,1)} %get-tuple-element.267.refs_1_, ...), custom_call_target="tpu_custom_call", output_to_operand_aliasing={{0}: (0, {}), {1}: (1, {}), {2}: (2, {})} | custom-call | flops 25769803776 | bytes 25165824 | tf_op jit(solution)/shard_map/attend_back/pallas_call | solution.py:419
  449.1 1.9 fusion.5
  451.0 1.1 dynamic-slice_bitcast_fusion.7
  452.1 7.6 %leave.4 = (bf16[512,768]{1,0:T(8,128)(2,1)}, f32[8,768]{1,0:T(8,128)}) custom-call(s32[5]{0:T(128)} %pad_add_fusion.info_ref, bf16[2048,768]{1,0:T(8,128)(2,1)} %bitcast.137, bf16[2048,768]{1,0:T(8,128)(2,1)} %bitcast.141, bf16[2048,768]{1,0:T(8,128)(2,1)} %bitcast.145, bf16[2048,768]{1,0:T(8,128)(2,1)} %get-tuple-element.204.x_ref, ...), custom_call_target="tpu_custom_call" | custom-call | flops 3623878656 | bytes 8388608 | tf_op jit(solution)/shard_map/leave/pallas_call | solution.py:510
  459.8 1.1 collective-permute-start.18
  460.8 1.2 fusion.8.kept_ref
  462.1 1.0 collective-permute-start.13
  463.1 17.5 %last_weight.1 = (bf16[8,48,1152]{2,1,0:T(8,128)(2,1)}, bf16[8,48,1152]{2,1,0:T(8,128)(2,1)}, bf16[8,48,1152]{2,1,0:T(8,128)(2,1)}, bf16[8,48,1152]{2,1,0:T(8,128)(2,1)}) custom-call(s32[5]{0:T(128)} %pad_add_fusion.info_ref, bf16[2048,768]{1,0:T(8,128)(2,1)} %bitcast.138, bf16[2048,768]{1,0:T(8,128)(2,1)} %bitcast.142, bf16[2048,768]{1,0:T(8,128)(2,1)} %bitcast.146, ...), custom_call_target="tpu_custom_call" | custom-call | flops 28991029248 | bytes 20971520 | tf_op jit(solution)/shard_map/last_weight/pallas_call | solution.py:510
  481.2 2.4 convert_dynamic-update-slice_fusion.2.refs_0_
  483.6 3.4 convert_dynamic-update-slice_fusion
  487.7 0.8 dynamic-slice_bitcast_fusion.10
  488.5 1.0 collective-permute-start.19
  489.5 1.0 dynamic-slice_bitcast_fusion.9
  490.5 2.0 collective-permute-start.20
  492.5 0.8 dynamic-slice_bitcast_fusion.13
  493.4 8.0 %leave.5 = (f32[4,512,768]{2,1,0:T(8,128)}, f32[8,768]{1,0:T(8,128)}) custom-call(s32[5]{0:T(128)} %pad_add_fusion.info_ref, bf16[2048,768]{1,0:T(8,128)(2,1)} %bitcast.139, bf16[2048,768]{1,0:T(8,128)(2,1)} %bitcast.143, bf16[2048,768]{1,0:T(8,128)(2,1)} %bitcast.147, bf16[2048,768]{1,0:T(8,128)(2,1)} %get-tuple-element.204.x_ref, ...), custom_call_target="tpu_custom_call", output_to_operand_aliasing={{0}: (8, {})} | custom-call | flops 3623878656 | bytes 8388608 | tf_op jit(solution)/shard_map/leave/pallas_call | solution.py:510
  501.4 8.0 %collective-permute-done.15.refs_1_ = bf16[192,768]{1,0:T(8,128)(2,1)} collective-permute-done((bf16[192,768]{1,0:T(8,128)(2,1)}, bf16[192,768]{1,0:T(8,128)(2,1)}, u32[]{:S(2)}, u32[]{:S(2)}) %collective-permute-start.15) | collective-permute-done | bytes 294944 | tf_op jit(solution)/shard_map/ppermute | solution.py:981
  509.4 2.4 convert_dynamic-update-slice_fusion.1
  511.8 1.4 add_add_fusion.refs_6_
  513.2 35.7 %tail.1 = (f32[192,768]{1,0:T(8,128)}, f32[48,1152]{1,0:T(8,128)}, f32[48,1152]{1,0:T(8,128)}, f32[32,768]{1,0:T(8,128)}) custom-call(bf16[192,768]{1,0:T(8,128)(2,1)} %get-tuple-element.380.refs_0_, bf16[192,768]{1,0:T(8,128)(2,1)} %collective-permute-done.15.refs_1_, bf16[2,2,48,1152]{3,2,1,0:T(8,128)(2,1)} %get-tuple-element.378.refs_2_, ...), custom_call_target="tpu_custom_call" | custom-call | flops 20000000000 | bytes 10000000 | tf_op jit(solution)/shard_map/tail/pallas_call | solution.py:1150
  548.9 3.8 final.1
  (115 shorter events, 5.5 us)
Async XLA Ops:
  0.7 13.6 %copy-start = (s32[4,1]{0,1:T(1,128)S(1)}, s32[4,1]{0,1:T(1,128)}, u32[]{:S(2)}) copy-start(s32[4,1]{0,1:T(1,128)} %param.28) | copy-start | bytes 52
  0.7 8.5 %copy-start.21 = (f32[768]{0:T(1024)S(1)}, f32[768]{0:T(1024)}, u32[]{:S(2)}) copy-start(f32[768]{0:T(1024)} %param.39) | copy-start | bytes 9220
  0.7 8.5 %copy-start.22 = (f32[768]{0:T(1024)S(1)}, f32[768]{0:T(1024)}, u32[]{:S(2)}) copy-start(f32[768]{0:T(1024)} %param.38) | copy-start | bytes 9220
  0.7 8.5 %copy-start.23 = (f32[768]{0:T(1024)S(1)}, f32[768]{0:T(1024)}, u32[]{:S(2)}) copy-start(f32[768]{0:T(1024)} %param.32) | copy-start | bytes 9220
  0.7 8.5 %copy-start.24 = (f32[768]{0:T(1024)S(1)}, f32[768]{0:T(1024)}, u32[]{:S(2)}) copy-start(f32[768]{0:T(1024)} %param.31) | copy-start | bytes 9220
  0.7 8.5 %copy-start.31 = (f32[768]{0:T(1024)S(1)}, f32[768]{0:T(1024)}, u32[]{:S(2)}) copy-start(f32[768]{0:T(1024)} %param.35) | copy-start | bytes 9220
  0.7 8.5 %copy-start.32 = (f32[768]{0:T(1024)S(1)}, f32[768]{0:T(1024)}, u32[]{:S(2)}) copy-start(f32[768]{0:T(1024)} %param.34) | copy-start | bytes 9220
  0.7 9.1 %copy-start.20 = (f32[768]{0:T(1024)S(1)}, f32[768]{0:T(1024)}, u32[]{:S(2)}) copy-start(f32[768]{0:T(1024)} %param.43) | copy-start | bytes 9220
  0.8 9.7 %copy-start.25 = (f32[768]{0:T(1024)S(1)}, f32[768]{0:T(1024)}, u32[]{:S(2)}) copy-start(f32[768]{0:T(1024)} %param.37) | copy-start | bytes 9220
  0.8 9.7 %copy-start.26 = (f32[768]{0:T(1024)S(1)}, f32[768]{0:T(1024)}, u32[]{:S(2)}) copy-start(f32[768]{0:T(1024)} %param.41) | copy-start | bytes 9220
  0.8 9.7 %copy-start.19 = (s32[4,1,512]{2,1,0:T(1,128)S(1)}, s32[4,1,512]{2,1,0:T(1,128)}, u32[]{:S(2)}) copy-start(s32[4,1,512]{2,1,0:T(1,128)} %param.29) | copy-start | bytes 24580
  0.8 9.8 %copy-start.7 = (bf16[4,1,512,768]{3,2,1,0:T(8,128)(2,1)S(1)}, bf16[4,1,512,768]{3,2,1,0:T(8,128)(2,1)}, u32[]{:S(2)}) copy-start(bf16[4,1,512,768]{3,2,1,0:T(8,128)(2,1)} %param.30) | copy-start | bytes 9437188
  3.6 29.2 %collective-permute-start = (bf16[1,512,768]{2,1,0:T(8,128)(2,1)}, bf16[1,512,768]{2,1,0:T(8,128)(2,1)}, u32[]{:S(2)}, u32[]{:S(2)}) collective-permute-start(bf16[1,512,768]{2,1,0:T(8,128)(2,1)} %get-tuple-element.372), channel_id=1, source_target_pairs={{0,1},{1,0},{2,3},{3,2},{4,5},{5,4},{6,7},{7,6},{8,9},{9,8},{10,11... | collective-permute-start | bytes 2359304 | tf_op jit(solution)/shard_map/ppermute | solution.py:1272
  11.2 1.7 copy-start.6
  12.9 1.3 copy-start.27
  12.9 1.3 copy-start.28
  12.9 1.3 copy-start.29
  12.9 1.3 copy-start.30
  23.5 9.3 %copy-start.15 = (bf16[1,512,768]{2,1,0:T(8,128)(2,1)S(1)}, bf16[1,512,768]{2,1,0:T(8,128)(2,1)}, u32[]{:S(2)}) copy-start(bf16[1,512,768]{2,1,0:T(8,128)(2,1)} %get-tuple-element.199) | copy-start | bytes 2359300
  32.8 25.0 %collective-permute-start.1 = (bf16[1,512,768]{2,1,0:T(8,128)(2,1)S(1)}, bf16[1,512,768]{2,1,0:T(8,128)(2,1)S(1)}, u32[]{:S(2)}, u32[]{:S(2)}) collective-permute-start(bf16[1,512,768]{2,1,0:T(8,128)(2,1)S(1)} %copy-done.15), channel_id=1, source_target_pairs={{0,1},{1,0},{2,3},{3,2},{4,5},{5,4},{6,7},{7,6},{8,9},{9,8},{10,11... | collective-permute-start | bytes 2359304 | tf_op jit(solution)/shard_map/ppermute | solution.py:1272
  57.8 0.9 copy-start.14
  58.7 40.7 %collective-permute-start.2 = (bf16[2,512,768]{2,1,0:T(8,128)(2,1)}, bf16[2,512,768]{2,1,0:T(8,128)(2,1)S(1)}, u32[]{:S(2)}, u32[]{:S(2)}) collective-permute-start(bf16[2,512,768]{2,1,0:T(8,128)(2,1)} %dynamic-slice_bitcast_fusion.1), channel_id=1, source_target_pairs={{0,1},{1,0},{2,3},{3,2},{4,5},{5,4},{6,7},{7,6},{8,9},{9,8},{10,11... | collective-permute-start | bytes 4718600 | tf_op jit(solution)/shard_map/ppermute | solution.py:1272
  99.4 1.1 copy-start.11
  99.4 38.8 %collective-permute-start.3 = (bf16[2,512,768]{2,1,0:T(8,128)(2,1)}, bf16[2,512,768]{2,1,0:T(8,128)(2,1)}, u32[]{:S(2)}, u32[]{:S(2)}) collective-permute-start(bf16[2,512,768]{2,1,0:T(8,128)(2,1)} %constant_dynamic-slice_fusion), channel_id=1, source_target_pairs={{0,1},{1,0},{2,3},{3,2},{4,5},{5,4},{6,7},{7,6},{8,9},{9,8},{10,11... | collective-permute-start | bytes 4718600 | tf_op jit(solution)/shard_map/ppermute | solution.py:1272
  244.7 31.8 %collective-permute-start.4 = (bf16[2,2,2,432,768]{4,3,2,1,0:T(8,128)(2,1)}, bf16[2,2,2,432,768]{4,3,2,1,0:T(8,128)(2,1)}, u32[]{:S(2)}, u32[]{:S(2)}) collective-permute-start(bf16[2,2,2,432,768]{4,3,2,1,0:T(8,128)(2,1)} %bitcast.167), channel_id=1, source_target_pairs={{0,2},{2,0},{4,6},{6,4},{8,10},{10,8},{12,14},{14,12},{16,18},{18,... | collective-permute-start | bytes 15925256 | tf_op jit(solution)/shard_map/ppermute | solution.py:981
  244.9 108.6 %collective-permute-start.6 = (bf16[2,512,768]{2,1,0:T(8,128)(2,1)}, bf16[2,512,768]{2,1,0:T(8,128)(2,1)S(1)}, u32[]{:S(2)}, u32[]{:S(2)}) collective-permute-start(bf16[2,512,768]{2,1,0:T(8,128)(2,1)} %get-tuple-element.248), channel_id=1, source_target_pairs={{0,1},{1,0},{2,3},{3,2},{4,5},{5,4},{6,7},{7,6},{8,9},{9,8},{10,11... | collective-permute-start | bytes 4718600 | tf_op jit(solution)/shard_map/ppermute | solution.py:1364
  281.9 2.3 copy-start.2
  285.9 67.6 %collective-permute-start.5 = (bf16[2,2,432,768]{3,2,1,0:T(8,128)(2,1)}, bf16[2,2,432,768]{3,2,1,0:T(8,128)(2,1)}, u32[]{:S(2)}, u32[]{:S(2)}) collective-permute-start(bf16[2,2,432,768]{3,2,1,0:T(8,128)(2,1)} %dynamic-slice_bitcast_fusion), channel_id=1, source_target_pairs={{0,4},{2,6},{4,0},{6,2},{8,12},{10,14},{12,8},{14,10},{16,20},{18,... | collective-permute-start | bytes 7962632 | tf_op jit(solution)/shard_map/ppermute | solution.py:981
  356.7 1.5 copy-start.3
  359.3 34.4 %collective-permute-start.7 = (bf16[2,432,768]{2,1,0:T(8,128)(2,1)}, bf16[2,432,768]{2,1,0:T(8,128)(2,1)}, u32[]{:S(2)}, u32[]{:S(2)}) collective-permute-start(bf16[2,432,768]{2,1,0:T(8,128)(2,1)} %dynamic-slice_bitcast_fusion.2), channel_id=1, source_target_pairs={{0,8},{2,10},{4,12},{6,14},{8,0},{10,2},{12,4},{14,6},{16,24},{18,... | collective-permute-start | bytes 3981320 | tf_op jit(solution)/shard_map/ppermute | solution.py:981
  360.5 33.3 %collective-permute-start.8 = (bf16[2,2,2,192,768]{4,3,2,1,0:T(8,128)(2,1)}, bf16[2,2,2,192,768]{4,3,2,1,0:T(8,128)(2,1)}, u32[]{:S(2)}, u32[]{:S(2)}) collective-permute-start(bf16[2,2,2,192,768]{4,3,2,1,0:T(8,128)(2,1)} %bitcast.31), channel_id=1, source_target_pairs={{0,2},{2,0},{4,6},{6,4},{8,10},{10,8},{12,14},{14,12},{16,18},{18,... | collective-permute-start | bytes 7077896 | tf_op jit(solution)/shard_map/ppermute | solution.py:981
  360.5 88.6 %collective-permute-start.12 = (bf16[2,512,768]{2,1,0:T(8,128)(2,1)}, bf16[2,512,768]{2,1,0:T(8,128)(2,1)}, u32[]{:S(2)}, u32[]{:S(2)}) collective-permute-start(bf16[2,512,768]{2,1,0:T(8,128)(2,1)} %get-tuple-element.273), channel_id=1, source_target_pairs={{0,1},{1,0},{2,3},{3,2},{4,5},{5,4},{6,7},{7,6},{8,9},{9,8},{10,11... | collective-permute-start | bytes 4718600 | tf_op jit(solution)/shard_map/ppermute | solution.py:1392
  392.5 2.3 copy-start.4
  393.7 6.0 %copy-start.9 = (bf16[8,192,768]{2,1,0:T(8,128)(2,1)S(1)}, bf16[8,192,768]{2,1,0:T(8,128)(2,1)}, u32[]{:S(2)}) copy-start(bf16[8,192,768]{2,1,0:T(8,128)(2,1)} %get-tuple-element.259) | copy-start | bytes 7077892
  396.6 52.5 %collective-permute-start.9 = (bf16[432,768]{1,0:T(8,128)(2,1)S(1)}, bf16[432,768]{1,0:T(8,128)(2,1)}, u32[]{:S(2)}, u32[]{:S(2)}) collective-permute-start(bf16[432,768]{1,0:T(8,128)(2,1)S(1)} %dynamic-slice_bitcast_fusion.6), channel_id=1, source_target_pairs={{0,16},{2,18},{4,20},{6,22},{8,24},{10,26},{12,28},{14,30},{16,0},... | collective-permute-start | bytes 1990664 | tf_op jit(solution)/shard_map/ppermute | solution.py:981
  402.0 1.5 copy-start.5
  404.6 44.6 %collective-permute-start.10 = (bf16[2,2,192,768]{3,2,1,0:T(8,128)(2,1)}, bf16[2,2,192,768]{3,2,1,0:T(8,128)(2,1)}, u32[]{:S(2)}, u32[]{:S(2)}) collective-permute-start(bf16[2,2,192,768]{3,2,1,0:T(8,128)(2,1)} %dynamic-slice_bitcast_fusion.3), channel_id=1, source_target_pairs={{0,4},{2,6},{4,0},{6,2},{8,12},{10,14},{12,8},{14,10},{16,20},{18,... | collective-permute-start | bytes 3538952 | tf_op jit(solution)/shard_map/ppermute | solution.py:981
  417.4 31.7 %collective-permute-start.11 = (bf16[512,768]{1,0:T(8,128)(2,1)}, bf16[512,768]{1,0:T(8,128)(2,1)}, u32[]{:S(2)}, u32[]{:S(2)}) collective-permute-start(bf16[512,768]{1,0:T(8,128)(2,1)} %get-tuple-element.272), channel_id=1, source_target_pairs={{0,1},{1,0},{2,3},{3,2},{4,5},{5,4},{6,7},{7,6},{8,9},{9,8},{10,11... | collective-permute-start | bytes 2359304 | tf_op jit(solution)/shard_map/ppermute | solution.py:1408
  459.8 27.4 %collective-permute-start.18 = (bf16[512,768]{1,0:T(8,128)(2,1)}, bf16[512,768]{1,0:T(8,128)(2,1)}, u32[]{:S(2)}, u32[]{:S(2)}) collective-permute-start(bf16[512,768]{1,0:T(8,128)(2,1)} %get-tuple-element.284), channel_id=1, source_target_pairs={{0,1},{1,0},{2,3},{3,2},{4,5},{5,4},{6,7},{7,6},{8,9},{9,8},{10,11... | collective-permute-start | bytes 2359304 | tf_op jit(solution)/shard_map/ppermute | solution.py:1419
  462.1 18.5 %copy-start.8 = (bf16[432,768]{1,0:T(8,128)(2,1)}, bf16[432,768]{1,0:T(8,128)(2,1)S(1)}, u32[]{:S(2)}) copy-start(bf16[432,768]{1,0:T(8,128)(2,1)S(1)} %fusion.8.kept_ref) | copy-start | bytes 1990660
  462.1 39.3 %collective-permute-start.13 = (bf16[432,768]{1,0:T(8,128)(2,1)S(1)}, bf16[432,768]{1,0:T(8,128)(2,1)S(1)}, u32[]{:S(2)}, u32[]{:S(2)}) collective-permute-start(bf16[432,768]{1,0:T(8,128)(2,1)S(1)} %fusion.8.kept_ref), channel_id=1, source_target_pairs={{0,1},{1,0},{2,3},{3,2},{4,5},{5,4},{6,7},{7,6},{8,9},{9,8},{10,11... | collective-permute-start | bytes 1990664 | tf_op jit(solution)/shard_map/ppermute | solution.py:983
  463.1 17.5 %collective-permute-start.14 = (bf16[2,192,768]{2,1,0:T(8,128)(2,1)}, bf16[2,192,768]{2,1,0:T(8,128)(2,1)S(1)}, u32[]{:S(2)}, u32[]{:S(2)}) collective-permute-start(bf16[2,192,768]{2,1,0:T(8,128)(2,1)} %get-tuple-element.280), channel_id=1, source_target_pairs={{0,8},{2,10},{4,12},{6,14},{8,0},{10,2},{12,4},{14,6},{16,24},{18,... | collective-permute-start | bytes 1769480 | tf_op jit(solution)/shard_map/ppermute | solution.py:981
  480.6 6.6 %collective-permute-start.16 = (bf16[2,2,2,48,1152]{4,3,2,1,0:T(8,128)(2,1)}, bf16[2,2,2,48,1152]{4,3,2,1,0:T(8,128)(2,1)S(1)}, u32[]{:S(2)}, u32[]{:S(2)}) collective-permute-start(bf16[2,2,2,48,1152]{4,3,2,1,0:T(8,128)(2,1)} %bitcast.171), channel_id=1, source_target_pairs={{0,2},{2,0},{4,6},{6,4},{8,10},{10,8},{12,14},{14,12},{16,18},{18,... | collective-permute-start | bytes 2654216 | tf_op jit(solution)/shard_map/ppermute | solution.py:981
  480.7 6.3 %copy-start.10 = (bf16[2,192,768]{2,1,0:T(8,128)(2,1)S(1)}, bf16[2,192,768]{2,1,0:T(8,128)(2,1)}, u32[]{:S(2)}) copy-start(bf16[2,192,768]{2,1,0:T(8,128)(2,1)} %get-tuple-element.279) | copy-start | bytes 1769476
  480.7 6.5 %collective-permute-start.17 = (bf16[2,2,2,48,1152]{4,3,2,1,0:T(8,128)(2,1)}, bf16[2,2,2,48,1152]{4,3,2,1,0:T(8,128)(2,1)S(1)}, u32[]{:S(2)}, u32[]{:S(2)}) collective-permute-start(bf16[2,2,2,48,1152]{4,3,2,1,0:T(8,128)(2,1)} %bitcast.170), channel_id=1, source_target_pairs={{0,2},{2,0},{4,6},{6,4},{8,10},{10,8},{12,14},{14,12},{16,18},{18,... | collective-permute-start | bytes 2654216 | tf_op jit(solution)/shard_map/ppermute | solution.py:981
  483.6 3.6 copy-start.12
  483.6 3.6 copy-start.13
  488.5 20.9 %collective-permute-start.19 = (bf16[2,2,48,1152]{3,2,1,0:T(8,128)(2,1)S(1)}, bf16[2,2,48,1152]{3,2,1,0:T(8,128)(2,1)}, u32[]{:S(2)}, u32[]{:S(2)}) collective-permute-start(bf16[2,2,48,1152]{3,2,1,0:T(8,128)(2,1)S(1)} %get-tuple-element.379), channel_id=1, source_target_pairs={{0,4},{2,6},{4,0},{6,2},{8,12},{10,14},{12,8},{14,10},{16,20},{18,... | collective-permute-start | bytes 1327112 | tf_op jit(solution)/shard_map/ppermute | solution.py:981
  490.5 18.9 %collective-permute-start.20 = (bf16[2,2,48,1152]{3,2,1,0:T(8,128)(2,1)}, bf16[2,2,48,1152]{3,2,1,0:T(8,128)(2,1)}, u32[]{:S(2)}, u32[]{:S(2)}) collective-permute-start(bf16[2,2,48,1152]{3,2,1,0:T(8,128)(2,1)} %get-tuple-element.377), channel_id=1, source_target_pairs={{0,8},{2,10},{4,12},{6,14},{8,0},{10,2},{12,4},{14,6},{16,24},{18,... | collective-permute-start | bytes 1327112 | tf_op jit(solution)/shard_map/ppermute | solution.py:981
  493.3 16.1 %collective-permute-start.15 = (bf16[192,768]{1,0:T(8,128)(2,1)}, bf16[192,768]{1,0:T(8,128)(2,1)}, u32[]{:S(2)}, u32[]{:S(2)}) collective-permute-start(bf16[192,768]{1,0:T(8,128)(2,1)} %get-tuple-element.381), channel_id=1, source_target_pairs={{0,16},{2,18},{4,20},{6,22},{8,24},{10,26},{12,28},{14,30},{16,0},... | collective-permute-start | bytes 884744 | tf_op jit(solution)/shard_map/ppermute | solution.py:981
  493.4 18.4 %copy-start.17 = (f32[8,768]{1,0:T(8,128)S(1)}, f32[8,768]{1,0:T(8,128)}, u32[]{:S(2)}) copy-start(f32[8,768]{1,0:T(8,128)} %get-tuple-element.317) | copy-start | bytes 73732
  493.4 18.4 %copy-start.18 = (f32[8,768]{1,0:T(8,128)S(1)}, f32[8,768]{1,0:T(8,128)}, u32[]{:S(2)}) copy-start(f32[8,768]{1,0:T(8,128)} %get-tuple-element.318) | copy-start | bytes 73732
  501.4 47.6 %copy-start.16 = (bf16[432,768]{1,0:T(8,128)(2,1)}, bf16[432,768]{1,0:T(8,128)(2,1)S(1)}, u32[]{:S(2)}) copy-start(bf16[432,768]{1,0:T(8,128)(2,1)S(1)} %collective-permute-done.13.got_ref) | copy-start | bytes 1990660
  513.2 39.5 %copy-start.1 = (s32[4,1]{0,1:T(1,128)S(1)}, s32[4,1]{0,1:T(1,128)}, u32[]{:S(2)}) copy-start(s32[4,1]{0,1:T(1,128)} %param.28) | copy-start | bytes 52

commit v13 on v12

--- a/solution.py
+++ b/solution.py
@@ -917,15 +917,15 @@
     )
     unit, inverse = normal_parts(x_ref[...].astype(jnp.float32))
     dx = dx_ref[...] + normal_back(unit, inverse, vec_ref[0:1, :], upstream)
+    vsum_ref[0:1, :] += column_sum(upstream * unit)
+    vsum_ref[1:2, :] += column_sum(upstream)
+    vsum_ref[2:3, :] += column_sum(dq.astype(jnp.float32))
+    vsum_ref[3:4, :] += column_sum(dv.astype(jnp.float32))
     if len(halves) == 2:
         put_rows(step, dx, own_ref, got_ref)
     else:
         out_ref = got_ref if own_ref is None else own_ref
         out_ref[...] = dx.astype(out_ref.dtype)
-    vsum_ref[0:1, :] += column_sum(upstream * unit)
-    vsum_ref[1:2, :] += column_sum(upstream)
-    vsum_ref[2:3, :] += column_sum(dq.astype(jnp.float32))
-    vsum_ref[3:4, :] += column_sum(dv.astype(jnp.float32))
 
 
 def leave(info, at, halves, previous, grads, x, dx1, weight, vectors, own, micros):

time: 559 us -> 559 us (level)
  no operation moved by 1% of the time
where the time goes in v13:
time: 559 us; the launch traced here: 553 us
  Pallas kernels  466 us (83%)
  local copies, waits for them, and re-layouts  28.4 us (5%)
  other arithmetic  27.7 us (5%)
  starting transfers between devices  20.7 us (4%)
  waiting for transfers between devices  8.17 us (1%)
    pallas_call x13, Pallas kernels, kernel_call(): pl.pallas_call(kernel, grid_spec=pltpu.PrefetchScalarGridSpec(num_scalar_...  239 us
    pallas_call x4, Pallas kernels, attend_back(): pl.pallas_call(kernel, grid=size, in_specs=[pl.BlockSpec(memory_space=pl....  123 us
    pallas_call x3, Pallas kernels, attend(): pl.pallas_call(functools.partial(attend_kernel, use_mask=use_mask, start=...  69 us
    pallas_call x1, Pallas kernels, tail(): pl.pallas_call(functools.partial(tail_kernel, orders=orders, groups=group...  35.3 us
    convert_element_type x8, other arithmetic, add(): total = total.astype(jnp.bfloat16)  16.3 us
  transfers between devices with their start and end apart: 21, of which 1 were waited for; matrix products, arithmetic and copies ran while one was open for 6% of the time, Pallas kernels for 57%

profile of v13, /device:TPU:0, one launch (start us, length us, event | category | flops | bytes accessed | tf_op | source)
XLA Modules:
  0.0 552.8 jit_solution(9879939238487377094)
XLA Ops:
  0.8 2.8 dynamic-slice_bitcast_fusion.4
  3.6 3.0 collective-permute-start
  6.5 2.7 dynamic-slice_bitcast_fusion.1
  11.2 1.7 copy-done.6
  12.9 1.3 constant_dynamic-slice_fusion
  15.0 0.6 concatenate.25.vec_ref
  16.3 0.7 maximum_maximum_fusion.1
  17.0 6.6 %enter.6 = (bf16[2048,768]{1,0:T(8,128)(2,1)}, bf16[2048,1536]{1,0:T(8,128)(2,1)}) custom-call(s32[5]{0:T(128)} %pad_add_fusion.info_ref, bf16[4,512,768]{2,1,0:T(8,128)(2,1)} %bitcast.163, bf16[768,1536]{1,0:T(8,128)(2,1)} %wi_ref.3, f32[8,768]{1,0:T(8,128)} %get-tuple-element.383.vec_ref, f32[1,1536]{1,0:T(1,128)} %broadcast_in_dim.45.bias_ref), custom_call_target="tpu_custom_call" | custom-call | flops 2415919104 | bytes 6291456 | tf_op jit(solution)/shard_map/enter/pallas_call | solution.py:510
  23.5 9.3 %enter.5 = (bf16[2048,768]{1,0:T(8,128)(2,1)}, bf16[2048,2304]{1,0:T(8,128)(2,1)}) custom-call(s32[5]{0:T(128)} %pad_add_fusion.info_ref, bf16[4,512,768]{2,1,0:T(8,128)(2,1)} %bitcast.162, bf16[768,2304]{1,0:T(8,128)(2,1)} %w_ref.15, f32[8,768]{1,0:T(8,128)} %get-tuple-element.383.vec_ref, f32[1,2304]{1,0:T(1,128)} %broadcast_in_dim.44.bias_ref), custom_call_target="tpu_custom_call" | custom-call | flops 3623878656 | bytes 7864320 | tf_op jit(solution)/shard_map/enter/pallas_call | solution.py:510
  32.9 6.6 %enter.7 = (bf16[2048,768]{1,0:T(8,128)(2,1)}, bf16[2048,2304]{1,0:T(8,128)(2,1)}) custom-call(s32[5]{0:T(128)} %pad_add_fusion.info_ref, bf16[1,512,768]{2,1,0:T(8,128)(2,1)} %collective-permute-done.source_ref, bf16[768,2304]{1,0:T(8,128)(2,1)} %w_ref.15, f32[8,768]{1,0:T(8,128)} %get-tuple-element.383.vec_ref, ...), custom_call_target="tpu_custom_call", output_to_operand_aliasing={{0}: (5, {}), {1}: (6, {})} | custom-call | flops 1811939328 | bytes 3932160 | tf_op jit(solution)/shard_map/enter/pallas_call | solution.py:510
  39.5 18.8 %attend.3 = (bf16[2,1024,768]{2,1,0:T(8,128)(2,1)}, bf16[2,12,1024,1024]{3,2,1,0:T(8,128)(2,1)}, f32[2,6,2,1024]{3,2,1,0:T(2,128)}) custom-call(s32[5]{0:T(128)} %pad_add_fusion.info_ref, bf16[2,1024,2304]{2,1,0:T(8,128)(2,1)} %bitcast.124, bf16[2,1024,2304]{2,1,0:T(8,128)(2,1)} %bitcast.125, bf16[2,1024,2304]{2,1,0:T(8,128)(2,1)} %bitcast.126), custom_call_target="tpu_custom_call" | custom-call | flops 12884901888 | bytes 25165824 | tf_op jit(solution)/shard_map/attend/pallas_call | solution.py:343
  58.3 0.9 copy-done.14
  59.2 2.0 collective-permute-start.2
  61.2 6.7 %enter.8 = (bf16[2048,768]{1,0:T(8,128)(2,1)}, bf16[2048,2304]{1,0:T(8,128)(2,1)}) custom-call(s32[5]{0:T(128)} %pad_add_fusion.info_ref, bf16[1,512,768]{2,1,0:T(8,128)(2,1)} %copy-done.14, bf16[768,2304]{1,0:T(8,128)(2,1)} %w_ref.15, f32[8,768]{1,0:T(8,128)} %get-tuple-element.383.vec_ref, ...), custom_call_target="tpu_custom_call", output_to_operand_aliasing={{0}: (5, {}), {1}: (6, {})} | custom-call | flops 1811939328 | bytes 3932160 | tf_op jit(solution)/shard_map/enter/pallas_call | solution.py:510
  67.9 19.0 %attend.4 = (bf16[2,1024,768]{2,1,0:T(8,128)(2,1)}, bf16[2,12,1024,1024]{3,2,1,0:T(8,128)(2,1)}, f32[2,6,2,1024]{3,2,1,0:T(2,128)}) custom-call(s32[5]{0:T(128)} %pad_add_fusion.info_ref, bf16[2,1024,2304]{2,1,0:T(8,128)(2,1)} %bitcast.127, bf16[2,1024,2304]{2,1,0:T(8,128)(2,1)} %bitcast.128, ...), custom_call_target="tpu_custom_call", output_to_operand_aliasing={{0}: (4, {}), {1}: (5, {}), {2}: (6, {})} | custom-call | flops 12884901888 | bytes 25165824 | tf_op jit(solution)/shard_map/attend/pallas_call | solution.py:343
  86.9 12.5 %middle.1 = (f32[2048,768]{1,0:T(8,128)}, bf16[2048,768]{1,0:T(8,128)(2,1)}) custom-call(s32[5]{0:T(128)} %pad_add_fusion.info_ref, bf16[2048,768]{1,0:T(8,128)(2,1)} %get-tuple-element.204.x_ref, bf16[2048,768]{1,0:T(8,128)(2,1)} %bitcast.157, bf16[768,768]{1,0:T(8,128)(2,1)} %wo_ref.5, bf16[768,768]{1,0:T(8,128)(2,1)} %wq_ref.3, f32[8,768]{1,0:T(8,128)} %concatenate.25.vec_ref), custom_call_target="tpu_custom_call" | custom-call | flops 4831838208 | bytes 15728640 | tf_op jit(solution)/shard_map/middle/pallas_call | solution.py:510
  99.5 1.1 copy-done.11
  100.6 6.6 %enter.9 = (bf16[2048,768]{1,0:T(8,128)(2,1)}, bf16[2048,1536]{1,0:T(8,128)(2,1)}) custom-call(s32[5]{0:T(128)} %pad_add_fusion.info_ref, bf16[2,512,768]{2,1,0:T(8,128)(2,1)} %copy-done.11, bf16[768,1536]{1,0:T(8,128)(2,1)} %wi_ref.3, f32[8,768]{1,0:T(8,128)} %get-tuple-element.383.vec_ref, ...), custom_call_target="tpu_custom_call", output_to_operand_aliasing={{0}: (5, {}), {1}: (6, {})} | custom-call | flops 2415919104 | bytes 6291456 | tf_op jit(solution)/shard_map/enter/pallas_call | solution.py:510
  107.1 31.1 %attend.5 = (bf16[2,1024,768]{2,1,0:T(8,128)(2,1)}, bf16[2,12,1024,1024]{3,2,1,0:T(8,128)(2,1)}, f32[2,6,2,1024]{3,2,1,0:T(2,128)}) custom-call(s32[5]{0:T(128)} %pad_add_fusion.info_ref, bf16[2,1024,768]{2,1,0:T(8,128)(2,1)} %bitcast.187, bf16[2,1024,1536]{2,1,0:T(8,128)(2,1)} %bitcast.148, bf16[2,1024,1536]{2,1,0:T(8,128)(2,1)} %bitcast.149), custom_call_target="tpu_custom_call" | custom-call | flops 25769803776 | bytes 50331648 | tf_op jit(solution)/shard_map/attend/pallas_call | solution.py:343
  138.2 106.4 %feed.1 = (bf16[4,512,768]{2,1,0:T(8,128)(2,1)}, bf16[2,512,768]{2,1,0:T(8,128)(2,1)}, f32[2048,768]{1,0:T(8,128)}, bf16[2048,768]{1,0:T(8,128)(2,1)}, f32[8,768...) custom-call(s32[5]{0:T(128)} %pad_add_fusion.info_ref, ...), custom_call_target="tpu_custom_call" | custom-call | flops 65229815808 | bytes 62914560 | tf_op jit(solution)/shard_map/feed/pallas_call | solution.py:510
  244.9 1.0 collective-permute-start.6
  245.9 30.6 %attend_back.4 = (bf16[2,1024,768]{2,1,0:T(8,128)(2,1)}, bf16[2,1024,768]{2,1,0:T(8,128)(2,1)}, bf16[2,1024,768]{2,1,0:T(8,128)(2,1)}) custom-call(bf16[2,1024,768]{2,1,0:T(8,128)(2,1)} %bitcast.188, bf16[2,1024,1536]{2,1,0:T(8,128)(2,1)} %bitcast.150, bf16[2,1024,1536]{2,1,0:T(8,128)(2,1)} %bitcast.151, ...), custom_call_target="tpu_custom_call" | custom-call | flops 25769803776 | bytes 25165824 | tf_op jit(solution)/shard_map/attend_back/pallas_call | solution.py:419
  276.5 5.3 fusion
  281.9 2.3 copy-done.2
  284.2 1.7 dynamic-slice_bitcast_fusion
  286.4 30.7 %attend_back.5 = (bf16[2,1024,768]{2,1,0:T(8,128)(2,1)}, bf16[2,1024,768]{2,1,0:T(8,128)(2,1)}, bf16[2,1024,768]{2,1,0:T(8,128)(2,1)}) custom-call(bf16[2,1024,768]{2,1,0:T(8,128)(2,1)} %get-tuple-element.233.refs_0_, bf16[2,1024,768]{2,1,0:T(8,128)(2,1)} %get-tuple-element.234.refs_1_, ...), custom_call_target="tpu_custom_call", output_to_operand_aliasing={{0}: (0, {}), {1}: (1, {}), {2}: (2, {})} | custom-call | flops 25769803776 | bytes 25165824 | tf_op jit(solution)/shard_map/attend_back/pallas_call | solution.py:419
  317.1 35.9 %return_rows.1 = (f32[4,512,768]{2,1,0:T(8,128)}, bf16[2,512,768]{2,1,0:T(8,128)(2,1)}, f32[2048,768]{1,0:T(8,128)}, bf16[2048,768]{1,0:T(8,128)(2,1)}, f32[8,76...) custom-call(s32[5]{0:T(128)} %pad_add_fusion.info_ref, bf16[2048,768]{1,0:T(8,128)(2,1)} %bitcast.195, ...), custom_call_target="tpu_custom_call" | custom-call | flops 19327352832 | bytes 41943040 | tf_op jit(solution)/shard_map/return_rows/pallas_call | solution.py:510
  353.0 3.2 fusion.2
  356.2 1.5 copy-done.3
  357.7 1.2 dynamic-slice_bitcast_fusion.2
  358.9 2.0 collective-permute-start.7
  360.9 1.1 collective-permute-start.12
  362.0 31.0 %attend_back.6 = (bf16[2,1024,768]{2,1,0:T(8,128)(2,1)}, bf16[2,1024,768]{2,1,0:T(8,128)(2,1)}, bf16[2,1024,768]{2,1,0:T(8,128)(2,1)}) custom-call(bf16[2,1024,2304]{2,1,0:T(8,128)(2,1)} %bitcast.130, bf16[2,1024,2304]{2,1,0:T(8,128)(2,1)} %bitcast.131, bf16[2,1024,2304]{2,1,0:T(8,128)(2,1)} %bitcast.132, ...), custom_call_target="tpu_custom_call" | custom-call | flops 25769803776 | bytes 25165824 | tf_op jit(solution)/shard_map/attend_back/pallas_call | solution.py:419
  393.0 1.2 bitcast_dynamic-update-slice_fusion
  394.2 1.0 copy-done.4
  395.3 1.7 fusion.4
  397.1 3.1 collective-permute-start.9
  400.2 2.3 fusion.3
  402.5 1.5 copy-done.5
  404.0 1.1 dynamic-slice_bitcast_fusion.3
  405.1 11.6 %leave.3 = (f32[4,512,768]{2,1,0:T(8,128)}, bf16[512,768]{1,0:T(8,128)(2,1)}, f32[8,768]{1,0:T(8,128)}) custom-call(s32[5]{0:T(128)} %pad_add_fusion.info_ref, bf16[2048,768]{1,0:T(8,128)(2,1)} %bitcast.136, bf16[2048,768]{1,0:T(8,128)(2,1)} %bitcast.140, bf16[2048,768]{1,0:T(8,128)(2,1)} %bitcast.144, bf16[2048,768]{1,0:T(8,128)(2,1)} %get-tuple-element.204.x_ref, ...), custom_call_target="tpu_custom_call" | custom-call | flops 7247757312 | bytes 16777216 | tf_op jit(solution)/shard_map/leave/pallas_call | solution.py:510
  416.7 1.0 collective-permute-start.11
  417.6 30.7 %attend_back.7 = (bf16[2,1024,768]{2,1,0:T(8,128)(2,1)}, bf16[2,1024,768]{2,1,0:T(8,128)(2,1)}, bf16[2,1024,768]{2,1,0:T(8,128)(2,1)}) custom-call(bf16[2,1024,768]{2,1,0:T(8,128)(2,1)} %get-tuple-element.266.refs_0_, bf16[2,1024,768]{2,1,0:T(8,128)(2,1)} %get-tuple-element.267.refs_1_, ...), custom_call_target="tpu_custom_call", output_to_operand_aliasing={{0}: (0, {}), {1}: (1, {}), {2}: (2, {})} | custom-call | flops 25769803776 | bytes 25165824 | tf_op jit(solution)/shard_map/attend_back/pallas_call | solution.py:419
  448.4 1.9 fusion.5
  450.3 1.1 dynamic-slice_bitcast_fusion.7
  451.4 7.6 %leave.4 = (bf16[512,768]{1,0:T(8,128)(2,1)}, f32[8,768]{1,0:T(8,128)}) custom-call(s32[5]{0:T(128)} %pad_add_fusion.info_ref, bf16[2048,768]{1,0:T(8,128)(2,1)} %bitcast.137, bf16[2048,768]{1,0:T(8,128)(2,1)} %bitcast.141, bf16[2048,768]{1,0:T(8,128)(2,1)} %bitcast.145, bf16[2048,768]{1,0:T(8,128)(2,1)} %get-tuple-element.204.x_ref, ...), custom_call_target="tpu_custom_call" | custom-call | flops 3623878656 | bytes 8388608 | tf_op jit(solution)/shard_map/leave/pallas_call | solution.py:510
  459.0 1.1 collective-permute-start.18
  460.1 1.2 fusion.8.kept_ref
  461.4 1.0 collective-permute-start.13
  462.4 0.9 collective-permute-start.14
  463.3 17.5 %last_weight.1 = (bf16[8,48,1152]{2,1,0:T(8,128)(2,1)}, bf16[8,48,1152]{2,1,0:T(8,128)(2,1)}, bf16[8,48,1152]{2,1,0:T(8,128)(2,1)}, bf16[8,48,1152]{2,1,0:T(8,128)(2,1)}) custom-call(s32[5]{0:T(128)} %pad_add_fusion.info_ref, bf16[2048,768]{1,0:T(8,128)(2,1)} %bitcast.138, bf16[2048,768]{1,0:T(8,128)(2,1)} %bitcast.142, bf16[2048,768]{1,0:T(8,128)(2,1)} %bitcast.146, ...), custom_call_target="tpu_custom_call" | custom-call | flops 28991029248 | bytes 20971520 | tf_op jit(solution)/shard_map/last_weight/pallas_call | solution.py:510
  481.4 2.4 convert_dynamic-update-slice_fusion.2.refs_0_
  483.8 3.4 convert_dynamic-update-slice_fusion
  487.9 0.8 dynamic-slice_bitcast_fusion.10
  488.7 1.5 collective-permute-start.19
  490.2 1.0 dynamic-slice_bitcast_fusion.9
  491.2 1.6 collective-permute-start.20
  492.7 0.8 dynamic-slice_bitcast_fusion.13
  493.6 8.0 %leave.5 = (f32[4,512,768]{2,1,0:T(8,128)}, f32[8,768]{1,0:T(8,128)}) custom-call(s32[5]{0:T(128)} %pad_add_fusion.info_ref, bf16[2048,768]{1,0:T(8,128)(2,1)} %bitcast.139, bf16[2048,768]{1,0:T(8,128)(2,1)} %bitcast.143, bf16[2048,768]{1,0:T(8,128)(2,1)} %bitcast.147, bf16[2048,768]{1,0:T(8,128)(2,1)} %get-tuple-element.204.x_ref, ...), custom_call_target="tpu_custom_call", output_to_operand_aliasing={{0}: (8, {})} | custom-call | flops 3623878656 | bytes 8388608 | tf_op jit(solution)/shard_map/leave/pallas_call | solution.py:510
  501.6 8.1 %collective-permute-done.15.refs_1_ = bf16[192,768]{1,0:T(8,128)(2,1)} collective-permute-done((bf16[192,768]{1,0:T(8,128)(2,1)}, bf16[192,768]{1,0:T(8,128)(2,1)}, u32[]{:S(2)}, u32[]{:S(2)}) %collective-permute-start.15) | collective-permute-done | bytes 294944 | tf_op jit(solution)/shard_map/ppermute | solution.py:981
  509.7 2.4 convert_dynamic-update-slice_fusion.1
  512.1 1.4 add_add_fusion.refs_6_
  513.5 35.3 %tail.1 = (f32[192,768]{1,0:T(8,128)}, f32[48,1152]{1,0:T(8,128)}, f32[48,1152]{1,0:T(8,128)}, f32[32,768]{1,0:T(8,128)}) custom-call(bf16[192,768]{1,0:T(8,128)(2,1)} %get-tuple-element.380.refs_0_, bf16[192,768]{1,0:T(8,128)(2,1)} %collective-permute-done.15.refs_1_, bf16[2,2,48,1152]{3,2,1,0:T(8,128)(2,1)} %get-tuple-element.378.refs_2_, ...), custom_call_target="tpu_custom_call" | custom-call | flops 20000000000 | bytes 10000000 | tf_op jit(solution)/shard_map/tail/pallas_call | solution.py:1150
  548.9 3.8 final.1
  (115 shorter events, 5.5 us)
Async XLA Ops:
  0.7 13.6 %copy-start = (s32[4,1]{0,1:T(1,128)S(1)}, s32[4,1]{0,1:T(1,128)}, u32[]{:S(2)}) copy-start(s32[4,1]{0,1:T(1,128)} %param.28) | copy-start | bytes 52
  0.7 8.5 %copy-start.21 = (f32[768]{0:T(1024)S(1)}, f32[768]{0:T(1024)}, u32[]{:S(2)}) copy-start(f32[768]{0:T(1024)} %param.39) | copy-start | bytes 9220
  0.7 8.5 %copy-start.22 = (f32[768]{0:T(1024)S(1)}, f32[768]{0:T(1024)}, u32[]{:S(2)}) copy-start(f32[768]{0:T(1024)} %param.38) | copy-start | bytes 9220
  0.7 8.5 %copy-start.23 = (f32[768]{0:T(1024)S(1)}, f32[768]{0:T(1024)}, u32[]{:S(2)}) copy-start(f32[768]{0:T(1024)} %param.32) | copy-start | bytes 9220
  0.7 8.5 %copy-start.24 = (f32[768]{0:T(1024)S(1)}, f32[768]{0:T(1024)}, u32[]{:S(2)}) copy-start(f32[768]{0:T(1024)} %param.31) | copy-start | bytes 9220
  0.7 8.5 %copy-start.31 = (f32[768]{0:T(1024)S(1)}, f32[768]{0:T(1024)}, u32[]{:S(2)}) copy-start(f32[768]{0:T(1024)} %param.35) | copy-start | bytes 9220
  0.7 8.5 %copy-start.32 = (f32[768]{0:T(1024)S(1)}, f32[768]{0:T(1024)}, u32[]{:S(2)}) copy-start(f32[768]{0:T(1024)} %param.34) | copy-start | bytes 9220
  0.7 9.1 %copy-start.20 = (f32[768]{0:T(1024)S(1)}, f32[768]{0:T(1024)}, u32[]{:S(2)}) copy-start(f32[768]{0:T(1024)} %param.43) | copy-start | bytes 9220
  0.8 9.7 %copy-start.25 = (f32[768]{0:T(1024)S(1)}, f32[768]{0:T(1024)}, u32[]{:S(2)}) copy-start(f32[768]{0:T(1024)} %param.37) | copy-start | bytes 9220
  0.8 9.7 %copy-start.26 = (f32[768]{0:T(1024)S(1)}, f32[768]{0:T(1024)}, u32[]{:S(2)}) copy-start(f32[768]{0:T(1024)} %param.41) | copy-start | bytes 9220
  0.8 9.7 %copy-start.19 = (s32[4,1,512]{2,1,0:T(1,128)S(1)}, s32[4,1,512]{2,1,0:T(1,128)}, u32[]{:S(2)}) copy-start(s32[4,1,512]{2,1,0:T(1,128)} %param.29) | copy-start | bytes 24580
  0.8 9.8 %copy-start.7 = (bf16[4,1,512,768]{3,2,1,0:T(8,128)(2,1)S(1)}, bf16[4,1,512,768]{3,2,1,0:T(8,128)(2,1)}, u32[]{:S(2)}) copy-start(bf16[4,1,512,768]{3,2,1,0:T(8,128)(2,1)} %param.30) | copy-start | bytes 9437188
  3.6 29.2 %collective-permute-start = (bf16[1,512,768]{2,1,0:T(8,128)(2,1)}, bf16[1,512,768]{2,1,0:T(8,128)(2,1)}, u32[]{:S(2)}, u32[]{:S(2)}) collective-permute-start(bf16[1,512,768]{2,1,0:T(8,128)(2,1)} %get-tuple-element.372), channel_id=1, source_target_pairs={{0,1},{1,0},{2,3},{3,2},{4,5},{5,4},{6,7},{7,6},{8,9},{9,8},{10,11... | collective-permute-start | bytes 2359304 | tf_op jit(solution)/shard_map/ppermute | solution.py:1272
  11.2 1.7 copy-start.6
  12.9 1.3 copy-start.27
  12.9 1.3 copy-start.28
  12.9 1.3 copy-start.29
  12.9 1.3 copy-start.30
  23.5 9.3 %copy-start.15 = (bf16[1,512,768]{2,1,0:T(8,128)(2,1)S(1)}, bf16[1,512,768]{2,1,0:T(8,128)(2,1)}, u32[]{:S(2)}) copy-start(bf16[1,512,768]{2,1,0:T(8,128)(2,1)} %get-tuple-element.199) | copy-start | bytes 2359300
  32.8 25.5 %collective-permute-start.1 = (bf16[1,512,768]{2,1,0:T(8,128)(2,1)S(1)}, bf16[1,512,768]{2,1,0:T(8,128)(2,1)S(1)}, u32[]{:S(2)}, u32[]{:S(2)}) collective-permute-start(bf16[1,512,768]{2,1,0:T(8,128)(2,1)S(1)} %copy-done.15), channel_id=1, source_target_pairs={{0,1},{1,0},{2,3},{3,2},{4,5},{5,4},{6,7},{7,6},{8,9},{9,8},{10,11... | collective-permute-start | bytes 2359304 | tf_op jit(solution)/shard_map/ppermute | solution.py:1272
  58.3 0.9 copy-start.14
  59.2 40.2 %collective-permute-start.2 = (bf16[2,512,768]{2,1,0:T(8,128)(2,1)}, bf16[2,512,768]{2,1,0:T(8,128)(2,1)S(1)}, u32[]{:S(2)}, u32[]{:S(2)}) collective-permute-start(bf16[2,512,768]{2,1,0:T(8,128)(2,1)} %dynamic-slice_bitcast_fusion.1), channel_id=1, source_target_pairs={{0,1},{1,0},{2,3},{3,2},{4,5},{5,4},{6,7},{7,6},{8,9},{9,8},{10,11... | collective-permute-start | bytes 4718600 | tf_op jit(solution)/shard_map/ppermute | solution.py:1272
  99.4 1.1 copy-start.11
  99.4 38.8 %collective-permute-start.3 = (bf16[2,512,768]{2,1,0:T(8,128)(2,1)}, bf16[2,512,768]{2,1,0:T(8,128)(2,1)}, u32[]{:S(2)}, u32[]{:S(2)}) collective-permute-start(bf16[2,512,768]{2,1,0:T(8,128)(2,1)} %constant_dynamic-slice_fusion), channel_id=1, source_target_pairs={{0,1},{1,0},{2,3},{3,2},{4,5},{5,4},{6,7},{7,6},{8,9},{9,8},{10,11... | collective-permute-start | bytes 4718600 | tf_op jit(solution)/shard_map/ppermute | solution.py:1272
  244.7 31.8 %collective-permute-start.4 = (bf16[2,2,2,432,768]{4,3,2,1,0:T(8,128)(2,1)}, bf16[2,2,2,432,768]{4,3,2,1,0:T(8,128)(2,1)}, u32[]{:S(2)}, u32[]{:S(2)}) collective-permute-start(bf16[2,2,2,432,768]{4,3,2,1,0:T(8,128)(2,1)} %bitcast.167), channel_id=1, source_target_pairs={{0,2},{2,0},{4,6},{6,4},{8,10},{10,8},{12,14},{14,12},{16,18},{18,... | collective-permute-start | bytes 15925256 | tf_op jit(solution)/shard_map/ppermute | solution.py:981
  244.9 108.1 %collective-permute-start.6 = (bf16[2,512,768]{2,1,0:T(8,128)(2,1)}, bf16[2,512,768]{2,1,0:T(8,128)(2,1)S(1)}, u32[]{:S(2)}, u32[]{:S(2)}) collective-permute-start(bf16[2,512,768]{2,1,0:T(8,128)(2,1)} %get-tuple-element.248), channel_id=1, source_target_pairs={{0,1},{1,0},{2,3},{3,2},{4,5},{5,4},{6,7},{7,6},{8,9},{9,8},{10,11... | collective-permute-start | bytes 4718600 | tf_op jit(solution)/shard_map/ppermute | solution.py:1364
  281.9 2.3 copy-start.2
  285.9 67.2 %collective-permute-start.5 = (bf16[2,2,432,768]{3,2,1,0:T(8,128)(2,1)}, bf16[2,2,432,768]{3,2,1,0:T(8,128)(2,1)}, u32[]{:S(2)}, u32[]{:S(2)}) collective-permute-start(bf16[2,2,432,768]{3,2,1,0:T(8,128)(2,1)} %dynamic-slice_bitcast_fusion), channel_id=1, source_target_pairs={{0,4},{2,6},{4,0},{6,2},{8,12},{10,14},{12,8},{14,10},{16,20},{18,... | collective-permute-start | bytes 7962632 | tf_op jit(solution)/shard_map/ppermute | solution.py:981
  356.2 1.5 copy-start.3
  358.9 35.4 %collective-permute-start.7 = (bf16[2,432,768]{2,1,0:T(8,128)(2,1)}, bf16[2,432,768]{2,1,0:T(8,128)(2,1)}, u32[]{:S(2)}, u32[]{:S(2)}) collective-permute-start(bf16[2,432,768]{2,1,0:T(8,128)(2,1)} %dynamic-slice_bitcast_fusion.2), channel_id=1, source_target_pairs={{0,8},{2,10},{4,12},{6,14},{8,0},{10,2},{12,4},{14,6},{16,24},{18,... | collective-permute-start | bytes 3981320 | tf_op jit(solution)/shard_map/ppermute | solution.py:981
  360.9 33.3 %collective-permute-start.8 = (bf16[2,2,2,192,768]{4,3,2,1,0:T(8,128)(2,1)}, bf16[2,2,2,192,768]{4,3,2,1,0:T(8,128)(2,1)}, u32[]{:S(2)}, u32[]{:S(2)}) collective-permute-start(bf16[2,2,2,192,768]{4,3,2,1,0:T(8,128)(2,1)} %bitcast.31), channel_id=1, source_target_pairs={{0,2},{2,0},{4,6},{6,4},{8,10},{10,8},{12,14},{14,12},{16,18},{18,... | collective-permute-start | bytes 7077896 | tf_op jit(solution)/shard_map/ppermute | solution.py:981
  360.9 87.4 %collective-permute-start.12 = (bf16[2,512,768]{2,1,0:T(8,128)(2,1)}, bf16[2,512,768]{2,1,0:T(8,128)(2,1)}, u32[]{:S(2)}, u32[]{:S(2)}) collective-permute-start(bf16[2,512,768]{2,1,0:T(8,128)(2,1)} %get-tuple-element.273), channel_id=1, source_target_pairs={{0,1},{1,0},{2,3},{3,2},{4,5},{5,4},{6,7},{7,6},{8,9},{9,8},{10,11... | collective-permute-start | bytes 4718600 | tf_op jit(solution)/shard_map/ppermute | solution.py:1392
  393.0 2.3 copy-start.4
  394.2 6.0 %copy-start.9 = (bf16[8,192,768]{2,1,0:T(8,128)(2,1)S(1)}, bf16[8,192,768]{2,1,0:T(8,128)(2,1)}, u32[]{:S(2)}) copy-start(bf16[8,192,768]{2,1,0:T(8,128)(2,1)} %get-tuple-element.259) | copy-start | bytes 7077892
  397.1 51.3 %collective-permute-start.9 = (bf16[432,768]{1,0:T(8,128)(2,1)S(1)}, bf16[432,768]{1,0:T(8,128)(2,1)}, u32[]{:S(2)}, u32[]{:S(2)}) collective-permute-start(bf16[432,768]{1,0:T(8,128)(2,1)S(1)} %dynamic-slice_bitcast_fusion.6), channel_id=1, source_target_pairs={{0,16},{2,18},{4,20},{6,22},{8,24},{10,26},{12,28},{14,30},{16,0},... | collective-permute-start | bytes 1990664 | tf_op jit(solution)/shard_map/ppermute | solution.py:981
  402.5 1.5 copy-start.5
  405.1 43.3 %collective-permute-start.10 = (bf16[2,2,192,768]{3,2,1,0:T(8,128)(2,1)}, bf16[2,2,192,768]{3,2,1,0:T(8,128)(2,1)}, u32[]{:S(2)}, u32[]{:S(2)}) collective-permute-start(bf16[2,2,192,768]{3,2,1,0:T(8,128)(2,1)} %dynamic-slice_bitcast_fusion.3), channel_id=1, source_target_pairs={{0,4},{2,6},{4,0},{6,2},{8,12},{10,14},{12,8},{14,10},{16,20},{18,... | collective-permute-start | bytes 3538952 | tf_op jit(solution)/shard_map/ppermute | solution.py:981
  416.7 31.7 %collective-permute-start.11 = (bf16[512,768]{1,0:T(8,128)(2,1)}, bf16[512,768]{1,0:T(8,128)(2,1)}, u32[]{:S(2)}, u32[]{:S(2)}) collective-permute-start(bf16[512,768]{1,0:T(8,128)(2,1)} %get-tuple-element.272), channel_id=1, source_target_pairs={{0,1},{1,0},{2,3},{3,2},{4,5},{5,4},{6,7},{7,6},{8,9},{9,8},{10,11... | collective-permute-start | bytes 2359304 | tf_op jit(solution)/shard_map/ppermute | solution.py:1408
  459.0 28.3 %collective-permute-start.18 = (bf16[512,768]{1,0:T(8,128)(2,1)}, bf16[512,768]{1,0:T(8,128)(2,1)}, u32[]{:S(2)}, u32[]{:S(2)}) collective-permute-start(bf16[512,768]{1,0:T(8,128)(2,1)} %get-tuple-element.284), channel_id=1, source_target_pairs={{0,1},{1,0},{2,3},{3,2},{4,5},{5,4},{6,7},{7,6},{8,9},{9,8},{10,11... | collective-permute-start | bytes 2359304 | tf_op jit(solution)/shard_map/ppermute | solution.py:1419
  461.4 19.4 %copy-start.8 = (bf16[432,768]{1,0:T(8,128)(2,1)}, bf16[432,768]{1,0:T(8,128)(2,1)S(1)}, u32[]{:S(2)}) copy-start(bf16[432,768]{1,0:T(8,128)(2,1)S(1)} %fusion.8.kept_ref) | copy-start | bytes 1990660
  461.4 40.3 %collective-permute-start.13 = (bf16[432,768]{1,0:T(8,128)(2,1)S(1)}, bf16[432,768]{1,0:T(8,128)(2,1)S(1)}, u32[]{:S(2)}, u32[]{:S(2)}) collective-permute-start(bf16[432,768]{1,0:T(8,128)(2,1)S(1)} %fusion.8.kept_ref), channel_id=1, source_target_pairs={{0,1},{1,0},{2,3},{3,2},{4,5},{5,4},{6,7},{7,6},{8,9},{9,8},{10,11... | collective-permute-start | bytes 1990664 | tf_op jit(solution)/shard_map/ppermute | solution.py:983
  462.4 18.4 %collective-permute-start.14 = (bf16[2,192,768]{2,1,0:T(8,128)(2,1)}, bf16[2,192,768]{2,1,0:T(8,128)(2,1)S(1)}, u32[]{:S(2)}, u32[]{:S(2)}) collective-permute-start(bf16[2,192,768]{2,1,0:T(8,128)(2,1)} %get-tuple-element.280), channel_id=1, source_target_pairs={{0,8},{2,10},{4,12},{6,14},{8,0},{10,2},{12,4},{14,6},{16,24},{18,... | collective-permute-start | bytes 1769480 | tf_op jit(solution)/shard_map/ppermute | solution.py:981
  480.8 6.6 %collective-permute-start.16 = (bf16[2,2,2,48,1152]{4,3,2,1,0:T(8,128)(2,1)}, bf16[2,2,2,48,1152]{4,3,2,1,0:T(8,128)(2,1)S(1)}, u32[]{:S(2)}, u32[]{:S(2)}) collective-permute-start(bf16[2,2,2,48,1152]{4,3,2,1,0:T(8,128)(2,1)} %bitcast.171), channel_id=1, source_target_pairs={{0,2},{2,0},{4,6},{6,4},{8,10},{10,8},{12,14},{14,12},{16,18},{18,... | collective-permute-start | bytes 2654216 | tf_op jit(solution)/shard_map/ppermute | solution.py:981
  480.9 6.3 %copy-start.10 = (bf16[2,192,768]{2,1,0:T(8,128)(2,1)S(1)}, bf16[2,192,768]{2,1,0:T(8,128)(2,1)}, u32[]{:S(2)}) copy-start(bf16[2,192,768]{2,1,0:T(8,128)(2,1)} %get-tuple-element.279) | copy-start | bytes 1769476
  480.9 6.5 %collective-permute-start.17 = (bf16[2,2,2,48,1152]{4,3,2,1,0:T(8,128)(2,1)}, bf16[2,2,2,48,1152]{4,3,2,1,0:T(8,128)(2,1)S(1)}, u32[]{:S(2)}, u32[]{:S(2)}) collective-permute-start(bf16[2,2,2,48,1152]{4,3,2,1,0:T(8,128)(2,1)} %bitcast.170), channel_id=1, source_target_pairs={{0,2},{2,0},{4,6},{6,4},{8,10},{10,8},{12,14},{14,12},{16,18},{18,... | collective-permute-start | bytes 2654216 | tf_op jit(solution)/shard_map/ppermute | solution.py:981
  483.7 3.6 copy-start.12
  483.8 3.6 copy-start.13
  488.7 21.0 %collective-permute-start.19 = (bf16[2,2,48,1152]{3,2,1,0:T(8,128)(2,1)S(1)}, bf16[2,2,48,1152]{3,2,1,0:T(8,128)(2,1)}, u32[]{:S(2)}, u32[]{:S(2)}) collective-permute-start(bf16[2,2,48,1152]{3,2,1,0:T(8,128)(2,1)S(1)} %get-tuple-element.379), channel_id=1, source_target_pairs={{0,4},{2,6},{4,0},{6,2},{8,12},{10,14},{12,8},{14,10},{16,20},{18,... | collective-permute-start | bytes 1327112 | tf_op jit(solution)/shard_map/ppermute | solution.py:981
  491.2 18.6 %collective-permute-start.20 = (bf16[2,2,48,1152]{3,2,1,0:T(8,128)(2,1)}, bf16[2,2,48,1152]{3,2,1,0:T(8,128)(2,1)}, u32[]{:S(2)}, u32[]{:S(2)}) collective-permute-start(bf16[2,2,48,1152]{3,2,1,0:T(8,128)(2,1)} %get-tuple-element.377), channel_id=1, source_target_pairs={{0,8},{2,10},{4,12},{6,14},{8,0},{10,2},{12,4},{14,6},{16,24},{18,... | collective-permute-start | bytes 1327112 | tf_op jit(solution)/shard_map/ppermute | solution.py:981
  493.6 16.1 %collective-permute-start.15 = (bf16[192,768]{1,0:T(8,128)(2,1)}, bf16[192,768]{1,0:T(8,128)(2,1)}, u32[]{:S(2)}, u32[]{:S(2)}) collective-permute-start(bf16[192,768]{1,0:T(8,128)(2,1)} %get-tuple-element.381), channel_id=1, source_target_pairs={{0,16},{2,18},{4,20},{6,22},{8,24},{10,26},{12,28},{14,30},{16,0},... | collective-permute-start | bytes 884744 | tf_op jit(solution)/shard_map/ppermute | solution.py:981
  493.6 18.5 %copy-start.17 = (f32[8,768]{1,0:T(8,128)S(1)}, f32[8,768]{1,0:T(8,128)}, u32[]{:S(2)}) copy-start(f32[8,768]{1,0:T(8,128)} %get-tuple-element.317) | copy-start | bytes 73732
  493.6 18.5 %copy-start.18 = (f32[8,768]{1,0:T(8,128)S(1)}, f32[8,768]{1,0:T(8,128)}, u32[]{:S(2)}) copy-start(f32[8,768]{1,0:T(8,128)} %get-tuple-element.318) | copy-start | bytes 73732
  501.6 47.2 %copy-start.16 = (bf16[432,768]{1,0:T(8,128)(2,1)}, bf16[432,768]{1,0:T(8,128)(2,1)S(1)}, u32[]{:S(2)}) copy-start(bf16[432,768]{1,0:T(8,128)(2,1)S(1)} %collective-permute-done.13.got_ref) | copy-start | bytes 1990660
  513.5 39.1 %copy-start.1 = (s32[4,1]{0,1:T(1,128)S(1)}, s32[4,1]{0,1:T(1,128)}, u32[]{:S(2)}) copy-start(s32[4,1]{0,1:T(1,128)} %param.28) | copy-start | bytes 52
